TPU v7x, 32 devices: a whole 2x2x4 slice. The times are simulated.
32 devices in a mesh: fsdp: 8 (over z, x), seq: 4 (over y, core).
Axes of the slice: x: 2, y: 2, z: 4, core: 2. Of those that a mesh axis runs over, the one named last changes fastest.
Arguments:
- layer_input: bfloat16 [8, 1024, 1536], P('fsdp', 'seq'), may hold values from -6 to 6
- attention_gain: bfloat16 [1536], P(('fsdp', 'seq')), may hold values from 0.099609375 to 1.8984375
- query_weight: bfloat16 [1536, 1536], P(('fsdp', 'seq')), may hold values from -0.15625 to 0.15625
- key_weight: bfloat16 [1536, 512], P(('fsdp', 'seq')), may hold values from -0.15625 to 0.15625
- value_weight: bfloat16 [1536, 512], P(('fsdp', 'seq')), may hold values from -0.15625 to 0.15625
- output_weight: bfloat16 [1536, 1536], P(('fsdp', 'seq')), may hold values from -1.25 to 1.25
- head_gains: bfloat16 [128], P(('fsdp', 'seq')), may hold values from 0.099609375 to 1.8984375
- feedforward_gain: bfloat16 [1536], P(('fsdp', 'seq')), may hold values from 0.099609375 to 1.8984375
- gate_weight: bfloat16 [1536, 6912], P(('fsdp', 'seq')), may hold values from -0.15625 to 0.15625
- up_weight: bfloat16 [1536, 6912], P(('fsdp', 'seq')), may hold values from -0.15625 to 0.15625
- down_weight: bfloat16 [1536, 6912], P(('fsdp', 'seq')), may hold values from -0.078125 to 0.078125
- upstream: bfloat16 [8, 1024, 1536], P('fsdp', 'seq'), may hold values from -6 to 6
Outputs:
- layer_output: bfloat16 [8, 1024, 1536], P('fsdp', 'seq')
- input_grad: float32 [8, 1024, 1536], P('fsdp', 'seq')
- attention_gain_grad: float32 [1536], P(('fsdp', 'seq'))
- query_weight_grad: float32 [1536, 1536], P('fsdp', 'seq')
- key_weight_grad: float32 [1536, 512], P('fsdp', 'seq')
- value_weight_grad: float32 [1536, 512], P('fsdp', 'seq')
- output_weight_grad: float32 [1536, 1536], P('fsdp', 'seq')
- head_gains_grad: float32 [128], P(('fsdp', 'seq'))
- feedforward_gain_grad: float32 [1536], P(('fsdp', 'seq'))
- gate_weight_grad: float32 [1536, 6912], P('fsdp', 'seq')
- up_weight_grad: float32 [1536, 6912], P('fsdp', 'seq')
- down_weight_grad: float32 [1536, 6912], P('fsdp', 'seq')
All inputs are finite; a program needn't handle non-finite values.
Results may differ from a plain program's by a relative error of at most 0.02.
Values may be sent and summed in bfloat16 or wider, within the bound.
No kernel may reach another device: no remote copies, remote signals or barrier semaphores. Data moves between devices by JAX's collectives and lax.ppermute only.
A program may use at most 384 MiB of HBM per device.

v0:
```python
from functools import partial

import jax
import jax.numpy as jnp
from jax import lax
from jax.sharding import PartitionSpec as P

HEADS = 24
KV_HEADS = 8
HEAD_DIM = 64
FF = 6912


EPSILON = 1e-05
ROPE_BASE = 1000000.0


def scaled_norm(values, gain_row):
    mean_square = jnp.mean(values * values, axis=-1, keepdims=True)
    return values * lax.rsqrt(mean_square + EPSILON) * gain_row


def rotary_tables(positions, head_size):
    half_dim = head_size // 2
    exponent = jnp.arange(half_dim).astype(jnp.float32) * (2.0 / head_size)
    frequency = jnp.power(jnp.float32(ROPE_BASE), -exponent)
    angles = positions.astype(jnp.float32)[:, None] * frequency[None, :]
    angles = jnp.concatenate([angles, angles], axis=-1)
    return (jnp.cos(angles)[:, None, :], jnp.sin(angles)[:, None, :])


def head_prepare(raw_heads, head_gain, cosine_table, sine_table):
    normed = scaled_norm(raw_heads, head_gain)
    half_dim = raw_heads.shape[-1] // 2
    turned = jnp.concatenate([-normed[..., half_dim:], normed[..., :half_dim]], axis=-1)
    return normed * cosine_table + turned * sine_table


def gating(gate_act, up_act):
    return gate_act * jax.nn.sigmoid(gate_act) * up_act


def project(left_side, right_side):
    return jnp.dot(left_side, right_side, preferred_element_type=jnp.float32)


def contract_rows(left_side, right_side):
    return lax.dot_general(
        left_side, right_side, (((0,), (0,)), ((), ())), preferred_element_type=jnp.float32
    )


def contract_last(left_side, right_side):
    return lax.dot_general(
        left_side, right_side, (((1,), (1,)), ((), ())), preferred_element_type=jnp.float32
    )


def tiled(values, copies):
    return jnp.broadcast_to(values[:, None, :], (values.shape[0], copies, values.shape[1]))


def attention_forward(queries, key_rows, value_rows):
    length = queries.shape[0]
    block_rows = min(512, length)
    score_scale = queries.shape[-1] ** (-0.5)
    per_head = []
    log_totals = []
    for head_index in range(queries.shape[1]):
        head_blocks = []
        head_totals = []
        for block_index in range(length // block_rows):
            first_row = block_index * block_rows
            finish = first_row + block_rows
            query_block = queries[first_row:finish, head_index]
            scores = (
                jnp.einsum(
                    "qgd,td->gqt",
                    query_block,
                    key_rows[:finish, head_index],
                    preferred_element_type=jnp.float32,
                )
                * score_scale
            )
            causal = (first_row + jnp.arange(block_rows))[:, None] >= jnp.arange(finish)[None, :]
            scores = jnp.where(causal, scores, -1e30)
            row_top = jnp.max(scores, axis=-1, keepdims=True)
            weights = jnp.exp(scores - row_top)
            row_total = jnp.sum(weights, axis=-1, keepdims=True)
            attention = (weights / row_total).astype(jnp.bfloat16)
            head_blocks.append(
                jnp.einsum(
                    "gqt,td->qgd",
                    attention,
                    value_rows[:finish, head_index],
                    preferred_element_type=jnp.float32,
                )
            )
            head_totals.append(row_top + jnp.log(row_total))
        per_head.append(jnp.concatenate(head_blocks, axis=0))
        log_totals.append(head_totals)
    return (jnp.stack(per_head, axis=1), log_totals)


def attention_backward(queries, key_rows, value_rows, grad_heads, log_totals):
    length = queries.shape[0]
    block_rows = min(512, length)
    score_scale = queries.shape[-1] ** (-0.5)
    query_parts = []
    key_parts = []
    value_parts = []
    for head_index in range(queries.shape[1]):
        head_queries = []
        key_total = jnp.zeros((length, queries.shape[-1]), jnp.float32)
        value_total = jnp.zeros((length, queries.shape[-1]), jnp.float32)
        for block_index in range(length // block_rows):
            first_row = block_index * block_rows
            finish = first_row + block_rows
            query_block = queries[first_row:finish, head_index]
            grad_block = grad_heads[first_row:finish, head_index]
            key_slice = key_rows[:finish, head_index]
            value_slice = value_rows[:finish, head_index]
            scores = (
                jnp.einsum(
                    "qgd,td->gqt", query_block, key_slice, preferred_element_type=jnp.float32
                )
                * score_scale
            )
            causal = (first_row + jnp.arange(block_rows))[:, None] >= jnp.arange(finish)[None, :]
            scores = jnp.where(causal, scores, -1e30)
            attention = jnp.exp(scores - log_totals[head_index][block_index])
            prob_grad = jnp.einsum(
                "qgd,td->gqt", grad_block, value_slice, preferred_element_type=jnp.float32
            )
            row_dot = jnp.sum(attention * prob_grad, axis=-1, keepdims=True)
            score_grad = (attention * (prob_grad - row_dot)).astype(jnp.bfloat16)
            head_queries.append(
                jnp.einsum("gqt,td->qgd", score_grad, key_slice, preferred_element_type=jnp.float32)
                * score_scale
            )
            key_total = key_total.at[:finish].add(
                jnp.einsum(
                    "gqt,qgd->td", score_grad, query_block, preferred_element_type=jnp.float32
                )
                * score_scale
            )
            value_total = value_total.at[:finish].add(
                jnp.einsum(
                    "gqt,qgd->td",
                    attention.astype(jnp.bfloat16),
                    grad_block,
                    preferred_element_type=jnp.float32,
                )
            )
        query_parts.append(jnp.concatenate(head_queries, axis=0))
        key_parts.append(key_total)
        value_parts.append(value_total)
    return (
        jnp.stack(query_parts, axis=1),
        jnp.stack(key_parts, axis=1),
        jnp.stack(value_parts, axis=1),
    )


def on_device(
    layer_input,
    attention_gain,
    query_weight,
    key_weight,
    value_weight,
    output_weight,
    head_gains,
    feedforward_gain,
    gate_weight,
    up_weight,
    down_weight,
    upstream,
):
    seq_count = lax.axis_size("seq")
    gathered = (
        lax.all_gather(attention_gain, ("fsdp", "seq"), axis=0, tiled=True),
        lax.all_gather(feedforward_gain, ("fsdp", "seq"), axis=0, tiled=True),
        lax.all_gather(query_weight, ("fsdp", "seq"), axis=0, tiled=True),
        lax.all_gather(key_weight, ("fsdp", "seq"), axis=0, tiled=True),
        lax.all_gather(value_weight, ("fsdp", "seq"), axis=0, tiled=True),
        lax.all_gather(output_weight, ("fsdp", "seq"), axis=0, tiled=True),
        lax.all_gather(head_gains, ("fsdp", "seq"), axis=0, tiled=True),
    )
    attention_scale = gathered[0].astype(jnp.float32)
    feedforward_scale = gathered[1].astype(jnp.float32)
    query_full = gathered[2]
    key_full = gathered[3]
    value_full = gathered[4]
    output_full = gathered[5]
    query_scale = gathered[6][:HEAD_DIM].astype(jnp.float32)
    key_scale = gathered[6][HEAD_DIM:].astype(jnp.float32)
    hidden = layer_input[0].astype(jnp.float32)
    tok_rows = hidden.shape[0]
    model_width = hidden.shape[1]
    normed_float, attention_pull = jax.vjp(scaled_norm, hidden, attention_scale)
    normed = normed_float.astype(jnp.bfloat16)
    query_raw = project(normed, query_full).astype(jnp.bfloat16)
    key_raw = project(normed, key_full).astype(jnp.bfloat16)
    value_local = project(normed, value_full).astype(jnp.bfloat16)
    query_width = HEADS * HEAD_DIM // seq_count
    kv_width = KV_HEADS * HEAD_DIM // seq_count
    query_heads_raw, key_heads_raw, value_heads, normed_whole = (
        lax.all_to_all(
            query_raw.reshape(tok_rows, seq_count, query_width),
            "seq",
            split_axis=1,
            concat_axis=0,
            tiled=True,
        ),
        lax.all_to_all(
            key_raw.reshape(tok_rows, seq_count, kv_width),
            "seq",
            split_axis=1,
            concat_axis=0,
            tiled=True,
        ),
        lax.all_to_all(
            value_local.reshape(tok_rows, seq_count, kv_width),
            "seq",
            split_axis=1,
            concat_axis=0,
            tiled=True,
        ),
        lax.all_to_all(tiled(normed, seq_count), "seq", split_axis=1, concat_axis=0, tiled=True),
    )
    length = query_heads_raw.shape[0]
    kv_local = KV_HEADS // seq_count
    group_size = HEADS // KV_HEADS
    normed_whole = normed_whole.reshape(length, model_width)
    cosine_table, sine_table = rotary_tables(jnp.arange(length), HEAD_DIM)
    prepare = partial(head_prepare, cosine_table=cosine_table, sine_table=sine_table)
    queries_float, query_pull = jax.vjp(
        prepare,
        query_heads_raw.reshape(length, kv_local * group_size, HEAD_DIM).astype(jnp.float32),
        query_scale,
    )
    keys_float, key_pull = jax.vjp(
        prepare, key_heads_raw.reshape(length, kv_local, HEAD_DIM).astype(jnp.float32), key_scale
    )
    query_heads = queries_float.astype(jnp.bfloat16).reshape(length, kv_local, group_size, HEAD_DIM)
    key_heads = keys_float.astype(jnp.bfloat16)
    value_heads = value_heads.reshape(length, kv_local, HEAD_DIM)
    mixed_heads, log_totals = attention_forward(query_heads, key_heads, value_heads)
    mixed_heads_low = mixed_heads.astype(jnp.bfloat16).reshape(length, query_width)
    mixed = lax.all_to_all(
        mixed_heads_low.reshape(length, 1, query_width),
        "seq",
        split_axis=0,
        concat_axis=1,
        tiled=True,
    )
    mixed = mixed.reshape(tok_rows, HEADS * HEAD_DIM)
    middle = hidden + contract_last(mixed, output_full)
    post_float, feedforward_pull = jax.vjp(scaled_norm, middle, feedforward_scale)
    post_normed = post_float.astype(jnp.bfloat16)
    pieces = (
        lax.all_gather(gate_weight, ("fsdp", "seq"), axis=0, tiled=True),
        lax.all_gather(up_weight, ("fsdp", "seq"), axis=0, tiled=True),
    )
    gate_act = project(post_normed, pieces[0])
    up_act = project(post_normed, pieces[1])
    activated_float, gating_pull = jax.vjp(gating, gate_act, up_act)
    activated = activated_float.astype(jnp.bfloat16)
    upstream_rows = upstream[0]
    branch_out = contract_last(
        activated, lax.all_gather(down_weight, ("fsdp", "seq"), axis=0, tiled=True)
    )
    layer_output = (middle + branch_out).astype(jnp.bfloat16)
    grad_columns = upstream_rows
    activated_grad = project(
        grad_columns, lax.all_gather(down_weight, ("fsdp", "seq"), axis=0, tiled=True)
    )
    gate_float, up_float = gating_pull(activated_grad)
    gate_grad = gate_float.astype(jnp.bfloat16)
    up_grad = up_float.astype(jnp.bfloat16)
    wide_local = FF // seq_count
    gate_cols, up_cols, act_cols, post_whole, upstream_whole = (
        lax.all_to_all(
            gate_grad.reshape(tok_rows, seq_count, wide_local),
            "seq",
            split_axis=1,
            concat_axis=0,
            tiled=True,
        ),
        lax.all_to_all(
            up_grad.reshape(tok_rows, seq_count, wide_local),
            "seq",
            split_axis=1,
            concat_axis=0,
            tiled=True,
        ),
        lax.all_to_all(
            activated.reshape(tok_rows, seq_count, wide_local),
            "seq",
            split_axis=1,
            concat_axis=0,
            tiled=True,
        ),
        lax.all_to_all(
            tiled(post_normed, seq_count), "seq", split_axis=1, concat_axis=0, tiled=True
        ),
        lax.all_to_all(
            tiled(upstream_rows, seq_count), "seq", split_axis=1, concat_axis=0, tiled=True
        ),
    )
    gate_cols = gate_cols.reshape(length, wide_local)
    up_cols = up_cols.reshape(length, wide_local)
    act_cols = act_cols.reshape(length, wide_local)
    post_whole = post_whole.reshape(length, model_width)
    upstream_whole = upstream_whole.reshape(length, model_width)
    grad_columns = upstream_whole
    ffn_sums = lax.psum_scatter(
        jnp.concatenate(
            [
                contract_rows(post_whole, gate_cols),
                contract_rows(post_whole, up_cols),
                contract_rows(grad_columns, act_cols),
            ],
            axis=1,
        ).astype(jnp.bfloat16),
        "fsdp",
        scatter_dimension=0,
        tiled=True,
    ).astype(jnp.float32)
    gate_weight_grad = ffn_sums[:, :wide_local]
    up_weight_grad = ffn_sums[:, wide_local : 2 * wide_local]
    down_weight_grad = ffn_sums[:, 2 * wide_local :]
    pieces = (
        lax.all_gather(gate_weight, ("fsdp", "seq"), axis=0, tiled=True),
        lax.all_gather(up_weight, ("fsdp", "seq"), axis=0, tiled=True),
    )
    part_grad = contract_last(gate_grad, pieces[0]) + contract_last(up_grad, pieces[1])
    middle_part, feedforward_gain_grad = feedforward_pull(part_grad)
    middle_grad = upstream_rows.astype(jnp.float32) + middle_part
    middle_low = middle_grad.astype(jnp.bfloat16)
    mixed_grad = project(middle_low, output_full).astype(jnp.bfloat16)
    grad_heads, middle_whole = (
        lax.all_to_all(
            mixed_grad.reshape(tok_rows, seq_count, query_width),
            "seq",
            split_axis=1,
            concat_axis=0,
            tiled=True,
        ),
        lax.all_to_all(
            tiled(middle_low, seq_count), "seq", split_axis=1, concat_axis=0, tiled=True
        ),
    )
    grad_heads = grad_heads.reshape(length, kv_local, group_size, HEAD_DIM)
    middle_whole = middle_whole.reshape(length, model_width)
    output_term = contract_rows(middle_whole, mixed_heads_low)
    query_grad, key_grad, value_grad = attention_backward(
        query_heads, key_heads, value_heads, grad_heads, log_totals
    )
    query_grad_low = (
        query_grad.astype(jnp.bfloat16)
        .astype(jnp.float32)
        .reshape(length, kv_local * group_size, HEAD_DIM)
    )
    key_grad_low = key_grad.astype(jnp.bfloat16).astype(jnp.float32)
    query_raw_grad, query_gain_grad = query_pull(query_grad_low)
    key_raw_grad, key_gain_grad = key_pull(key_grad_low)
    query_low = query_raw_grad.reshape(length, query_width).astype(jnp.bfloat16)
    key_low = key_raw_grad.reshape(length, kv_width).astype(jnp.bfloat16)
    value_low = value_grad.astype(jnp.bfloat16).reshape(length, kv_width)
    query_back, key_back, value_back = (
        lax.all_to_all(
            query_low.reshape(length, 1, query_width),
            "seq",
            split_axis=0,
            concat_axis=1,
            tiled=True,
        ),
        lax.all_to_all(
            key_low.reshape(length, 1, kv_width), "seq", split_axis=0, concat_axis=1, tiled=True
        ),
        lax.all_to_all(
            value_low.reshape(length, 1, kv_width), "seq", split_axis=0, concat_axis=1, tiled=True
        ),
    )
    query_tokens = query_back.reshape(tok_rows, HEADS * HEAD_DIM)
    key_tokens = key_back.reshape(tok_rows, KV_HEADS * HEAD_DIM)
    value_tokens = value_back.reshape(tok_rows, KV_HEADS * HEAD_DIM)
    normed_grad = (
        contract_last(query_tokens, query_full)
        + contract_last(key_tokens, key_full)
        + contract_last(value_tokens, value_full)
    )
    input_part, attention_gain_grad = attention_pull(normed_grad)
    input_grad = (middle_grad + input_part)[None]
    attention_sums = (
        lax.psum_scatter(
            contract_rows(normed_whole, query_low).astype(jnp.bfloat16),
            "fsdp",
            scatter_dimension=0,
            tiled=True,
        ).astype(jnp.float32),
        lax.psum_scatter(
            contract_rows(normed_whole, key_low).astype(jnp.bfloat16),
            "fsdp",
            scatter_dimension=0,
            tiled=True,
        ).astype(jnp.float32),
        lax.psum_scatter(
            contract_rows(normed_whole, value_low).astype(jnp.bfloat16),
            "fsdp",
            scatter_dimension=0,
            tiled=True,
        ).astype(jnp.float32),
        lax.psum_scatter(
            output_term.astype(jnp.bfloat16), "fsdp", scatter_dimension=0, tiled=True
        ).astype(jnp.float32),
    )
    gain_sums = (
        lax.psum_scatter(attention_gain_grad, ("fsdp", "seq"), scatter_dimension=0, tiled=True),
        lax.psum_scatter(feedforward_gain_grad, ("fsdp", "seq"), scatter_dimension=0, tiled=True),
        lax.psum_scatter(
            jnp.concatenate([query_gain_grad, key_gain_grad]),
            ("fsdp", "seq"),
            scatter_dimension=0,
            tiled=True,
        ),
    )
    return (
        layer_output[None],
        input_grad,
        gain_sums[0],
        attention_sums[0],
        attention_sums[1],
        attention_sums[2],
        attention_sums[3],
        gain_sums[2],
        gain_sums[1],
        gate_weight_grad,
        up_weight_grad,
        down_weight_grad,
    )


def solution(mesh):
    return jax.shard_map(
        on_device,
        mesh=mesh,
        in_specs=(
            P("fsdp", "seq", None),
            P(("fsdp", "seq")),
            P(("fsdp", "seq"), None),
            P(("fsdp", "seq"), None),
            P(("fsdp", "seq"), None),
            P(("fsdp", "seq"), None),
            P(("fsdp", "seq")),
            P(("fsdp", "seq")),
            P(("fsdp", "seq"), None),
            P(("fsdp", "seq"), None),
            P(("fsdp", "seq"), None),
            P("fsdp", "seq", None),
        ),
        out_specs=(
            P("fsdp", "seq", None),
            P("fsdp", "seq", None),
            P(("fsdp", "seq")),
            P("fsdp", "seq"),
            P("fsdp", "seq"),
            P("fsdp", "seq"),
            P("fsdp", "seq"),
            P(("fsdp", "seq")),
            P(("fsdp", "seq")),
            P("fsdp", "seq"),
            P("fsdp", "seq"),
            P("fsdp", "seq"),
        ),
        check_vma=False,
    )
```

profile of v0, /device:TPU:0, one launch (start us, length us, event | category | flops | bytes accessed | tf_op | source)
XLA Modules:
  0.0 1430.2 jit_solution(18243125961999543507)
XLA Ops:
  14.5 42.3 %all-reduce.15 = (bf16[1536]{0:T(1024)(128)(2,1)S(1)}, bf16[128]{0:T(256)(128)(2,1)S(1)}, bf16[1536]{0:T(1024)(128)(2,1)S(1)}) all-reduce(bf16[1536]{0:T(1024)(128)(2,1)S(1)} %dynamic-update-slice.20, bf16[128]{0:T(256)(128)(2,1)S(1)} %dynamic-update-slice.21, ...), channel_id=1, replica_groups=mesh['fsdp'=8,'seq'=4] {'fsdp','seq'}, use_global_device_ids=true, to_apply=%add.8 | all-reduce | flops 3200 | bytes 12800
  60.5 8.2 all-gather.10.cloned.1.call-done
  71.4 3.4 all-to-all-start.1
  74.8 50.7 %all-gather.8.cloned.1.call-done = bf16[1536,512]{1,0:T(8,128)(2,1)} async-done(((bf16[48,512]{1,0:T(8,128)(2,1)}), bf16[1536,512]{1,0:T(8,128)(2,1)}) %all-gather.8.cloned.1.call-update) | async-done | bytes 1572880 | tf_op jit(solution)/shard_map/all_gather | solution.py:185
  128.3 3.4 all-to-all-start
  132.4 58.6 %all-gather.12.cloned.1.call-done = bf16[1536,1536]{1,0:T(8,128)(2,1)} async-done(((bf16[48,1536]{1,0:T(8,128)(2,1)}), bf16[1536,1536]{1,0:T(8,128)(2,1)}) %all-gather.12.cloned.1.call-update) | async-done | bytes 4718608 | tf_op jit(solution)/shard_map/all_gather | solution.py:183
  190.9 4.6 convolution_convert_fusion.3
  197.8 3.7 all-to-all-start.2
  203.7 9.8 all-to-all-done.2
  240.5 4.2 all-to-all-start.3
  244.7 11.7 all-to-all-done.3
  256.4 3.7 reshape.677
  264.8 4.8 multiply_reduce_fusion.4
  271.8 121.8 %all-gather.16.cloned.1.call-done = bf16[1536,6912]{1,0:T(8,128)(2,1)} async-done(((bf16[48,6912]{1,0:T(8,128)(2,1)}), bf16[1536,6912]{1,0:T(8,128)(2,1)}) %all-gather.16.cloned.1.call-update) | async-done | bytes 21233680 | tf_op jit(solution)/shard_map/all_gather | solution.py:262
  393.6 14.9 %fusion.136 = f32[256,6912]{1,0:T(8,128)} fusion(bf16[256,1536]{1,0:T(8,128)(2,1)} %multiply_convert_fusion.2, bf16[1536,6912]{1,0:T(8,128)(2,1)} %all-gather.16.cloned.1.call-done), kind=kOutput, calls=%fused_computation.250 | convolution fusion | flops 5435817984 | bytes 29097984 | tf_op jit(solution)/shard_map/dot_general | solution.py:44
  408.5 122.0 %all-gather.18.cloned.1.call-done = bf16[1536,6912]{1,0:T(8,128)(2,1)} async-done(((bf16[48,6912]{1,0:T(8,128)(2,1)}), bf16[1536,6912]{1,0:T(8,128)(2,1)}) %all-gather.18.cloned.1.call-update) | async-done | bytes 21233680 | tf_op jit(solution)/shard_map/all_gather | solution.py:263
  530.4 14.8 %fusion.137 = f32[256,6912]{1,0:T(8,128)} fusion(bf16[256,1536]{1,0:T(8,128)(2,1)} %multiply_convert_fusion.2, bf16[1536,6912]{1,0:T(8,128)(2,1)} %all-gather.18.cloned.1.call-done), kind=kOutput, calls=%fused_computation.251 | convolution fusion | flops 5435817984 | bytes 29097984 | tf_op jit(solution)/shard_map/dot_general | solution.py:44
  545.3 122.1 %all-gather.20.cloned.1.call-done = bf16[1536,6912]{1,0:T(8,128)(2,1)} async-done(((bf16[48,6912]{1,0:T(8,128)(2,1)}), bf16[1536,6912]{1,0:T(8,128)(2,1)}) %all-gather.20.cloned.1.call-update) | async-done | bytes 21233680 | tf_op jit(solution)/shard_map/all_gather | solution.py:271
  667.4 17.6 %multiply_convert_fusion = (bf16[256,6912]{1,0:T(8,128)(2,1)}, bf16[256,6912]{1,0:T(8,128)(2,1)}, bf16[256,6912]{1,0:T(8,128)(2,1)}) fusion(f32[256,6912]{1,0:T(8,128)} %fusion.136, f32[256,6912]{1,0:T(8,128)} %fusion.137, bf16[1536,6912]{1,0:T(8,128)(2,1)} %all-gather.20.cloned.1.call-done, bf16[1,256,1536]{2,1,0:T(8,128)(2,1)} %param.47), kind=kOutput, calls=%fused_computation.8 | convolution fusion | flops 5464129536 | bytes 46792704 | tf_op jit(solution)/shard_map/dot_general | solution.py:44
  685.0 12.4 fusion.138
  697.4 12.9 multiply_reduce_fusion
  712.5 4.0 convolution_convert_fusion.2
  716.6 14.9 %all_to_all.213 = bf16[256,4,384]{2,0,1:T(8,128)(2,1)} all-to-all(bf16[256,4,384]{2,0,1:T(8,128)(2,1)S(1)} %bitcast.442), channel_id=1, replica_groups=mesh['fsdp'=8,'seq'=4] {'seq'}, dimensions={1} | all-to-all | bytes 1572864 | tf_op jit(solution)/shard_map/all_to_all | solution.py:343
  733.4 4.7 all-to-all-start.8
  738.7 6.0 copy.144
  744.7 5.8 copy.143
  755.2 4.3 fusion.25
  759.5 15.5 %all-to-all-done.8 = bf16[256,4,1536]{2,0,1:T(8,128)(2,1)} async-done(((bf16[256,4,1536]{2,0,1:T(8,128)(2,1)}), bf16[256,4,1536]{2,0,1:T(8,128)(2,1)}, u32[]{:S(2)}, u32[]{:S(2)}) %all-to-all-start.8) | async-done | bytes 3145760 | tf_op jit(solution)/shard_map/all_to_all | solution.py:229
  778.1 4.8 all-to-all-start.14
  782.9 3.8 fusion.27
  793.3 3.4 fusion.7
  796.8 23.1 %all-to-all-done.14 = bf16[256,4,1536]{2,0,1:T(8,128)(2,1)} async-done(((bf16[256,4,1536]{2,0,1:T(8,128)(2,1)}), bf16[256,4,1536]{2,0,1:T(8,128)(2,1)}, u32[]{:S(2)}, u32[]{:S(2)}) %all-to-all-start.14) | async-done | bytes 3145760 | tf_op jit(solution)/shard_map/all_to_all | solution.py:307
  821.8 4.9 all-to-all-start.10
  837.5 26.2 %all-to-all-done.10 = bf16[256,4,1536]{2,0,1:T(8,128)(2,1)} async-done(((bf16[256,4,1536]{2,0,1:T(8,128)(2,1)}), bf16[256,4,1536]{2,0,1:T(8,128)(2,1)}, u32[]{:S(2)}, u32[]{:S(2)}) %all-to-all-start.10) | async-done | bytes 3145760 | tf_op jit(solution)/shard_map/all_to_all | solution.py:304
  865.6 4.8 all-to-all-start.9
  872.4 3.7 convolution_convert_fusion.5
  880.8 3.9 fusion.86
  887.5 19.9 %all-to-all-done.9 = bf16[256,4,1536]{2,0,1:T(8,128)(2,1)} async-done(((bf16[256,4,1536]{2,0,1:T(8,128)(2,1)}), bf16[256,4,1536]{2,0,1:T(8,128)(2,1)}, u32[]{:S(2)}, u32[]{:S(2)}) %all-to-all-start.9) | async-done | bytes 3145760 | tf_op jit(solution)/shard_map/all_to_all | solution.py:350
  907.4 4.7 all-to-all-start.12
  912.2 3.9 convolution_convert_fusion.4
  923.4 30.0 %all-to-all-done.12 = bf16[256,4,1728]{0,2,1:T(8,128)(2,1)} async-done(((bf16[256,4,1728]{0,2,1:T(8,128)(2,1)}), bf16[256,4,1728]{0,2,1:T(8,128)(2,1)}, u32[]{:S(2)}, u32[]{:S(2)}) %all-to-all-start.12) | async-done | bytes 3538976 | tf_op jit(solution)/shard_map/all_to_all | solution.py:290
  953.3 4.8 all-to-all-start.11
  960.8 4.9 convolution_convert_fusion.1
  965.7 3.7 copy.145
  969.4 29.9 %all-to-all-done.11 = bf16[256,4,1728]{0,2,1:T(8,128)(2,1)} async-done(((bf16[256,4,1728]{0,2,1:T(8,128)(2,1)}), bf16[256,4,1728]{0,2,1:T(8,128)(2,1)}, u32[]{:S(2)}, u32[]{:S(2)}) %all-to-all-start.11) | async-done | bytes 3538976 | tf_op jit(solution)/shard_map/all_to_all | solution.py:283
  999.3 3.7 all-to-all-start.13
  1003.5 4.9 convolution_convert_fusion
  1008.5 10.0 bitcast_convert_fusion.1
  1018.5 10.0 bitcast_convert_fusion.2
  1028.5 15.7 %all-to-all-done.13 = bf16[256,4,1728]{0,2,1:T(8,128)(2,1)S(1)} async-done(((bf16[256,4,1728]{0,2,1:T(8,128)(2,1)}), bf16[256,4,1728]{0,2,1:T(8,128)(2,1)S(1)}, u32[]{:S(2)}, u32[]{:S(2)}) %all-to-all-start.13) | async-done | bytes 3538976 | tf_op jit(solution)/shard_map/all_to_all | solution.py:297
  1044.2 7.9 fusion.4
  1052.1 45.1 %pad_maximum_fusion = bf16[1536,5184]{0,1:T(8,128)(2,1)} fusion(bf16[1536,1728]{0,1:T(8,128)(2,1)S(1)} %fusion.4, bf16[1536,1728]{0,1:T(8,128)(2,1)S(1)} %copy-done.31, bf16[1536,1728]{0,1:T(8,128)(2,1)S(1)} %copy-done.32), kind=kLoop, calls=%fused_computation | loop fusion | flops 47775744 | bytes 31850496 | tf_op jit(solution)/shard_map/concatenate | solution.py:318
  1097.1 20.4 %copy.166 = bf16[1536,5184]{1,0:T(8,128)(2,1)} copy(bf16[1536,5184]{0,1:T(8,128)(2,1)} %pad_maximum_fusion) | data formatting | bytes 31850496
  1120.3 3.4 all-to-all-start.6
  1125.4 4.3 all-to-all-done.6
  1129.7 4.0 all-to-all-start.7
  1136.5 3.4 all-to-all-done.7
  1139.8 4.4 all-to-all-start.5
  1144.3 12.2 fusion.38
  1163.9 4.0 fusion.139
  1171.6 44.4 %all-reduce.14 = (f32[1536]{0:T(1024)S(1)}, f32[128]{0:T(128)S(1)}, f32[1536]{0:T(1024)S(1)}) all-reduce(f32[1536]{0:T(1024)S(1)} %get-tuple-element.192, f32[128]{0:T(128)S(1)} %pad_maximum_fusion.4, f32[1536]{0:T(1024)S(1)} %copy-done.82), channel_id=2, replica_groups=mesh['fsdp'=8,'seq'=4] {'fsdp','seq'}, use_global_device_ids=true, to_apply=%region_21.22.clone | all-reduce | flops 3200 | bytes 25600
  1217.8 3.9 fusion.50
  1227.9 182.4 %reduce-scatter.16.cloned.1.call-done = bf16[192,5184]{1,0:T(8,128)(2,1)} async-done(((bf16[1536,5184]{1,0:T(8,128)(2,1)}), bf16[192,5184]{1,0:T(8,128)(2,1)}) %reduce-scatter.16.cloned.1.call-update) | async-done | bytes 1990672
  1410.3 3.8 copy.167
  (357 shorter events, 143.2 us)
Async XLA Ops:
  7.2 51.5 %copy-start.19 = (bf16[1,256,1536]{2,1,0:T(8,128)(2,1)S(1)}, bf16[1,256,1536]{2,1,0:T(8,128)(2,1)}, u32[]{:S(2)}) copy-start(bf16[1,256,1536]{2,1,0:T(8,128)(2,1)} %param.36) | copy-start | bytes 2359300
  7.2 61.5 %all-gather.10.cloned.1.call-start = ((), (), s32[]{:S(2)}) async-start(), calls=%async_computation.21 | async-start | bytes 1622016 | tf_op jit(solution)/shard_map/all_gather | solution.py:184
  7.9 117.6 %all-gather.8.cloned.1.call-start = ((), (), s32[]{:S(2)}) async-start(), calls=%async_computation.20 | async-start | bytes 1622016 | tf_op jit(solution)/shard_map/all_gather | solution.py:185
  8.7 182.3 %all-gather.12.cloned.1.call-start = ((), (), s32[]{:S(2)}) async-start(), calls=%async_computation.22 | async-start | bytes 4866048 | tf_op jit(solution)/shard_map/all_gather | solution.py:183
  9.4 255.4 %all-gather.14.cloned.1.call-start = ((), (), s32[]{:S(2)}) async-start(), calls=%async_computation.23 | async-start | bytes 4866048 | tf_op jit(solution)/shard_map/all_gather | solution.py:186
  10.0 383.6 %all-gather.16.cloned.1.call-start = ((), (), s32[]{:S(2)}) async-start(), calls=%async_computation.24 | async-start | bytes 21897216 | tf_op jit(solution)/shard_map/all_gather | solution.py:262
  10.6 519.8 %all-gather.18.cloned.1.call-start = ((), (), s32[]{:S(2)}) async-start(), calls=%async_computation.25 | async-start | bytes 21897216 | tf_op jit(solution)/shard_map/all_gather | solution.py:263
  11.1 656.2 %all-gather.20.cloned.1.call-start = ((), (), s32[]{:S(2)}) async-start(), calls=%async_computation.26 | async-start | bytes 21897216 | tf_op jit(solution)/shard_map/all_gather | solution.py:271
  58.6 144.1 %copy-start.26 = (f32[1024,64]{0,1:T(8,128)}, f32[1024,64]{0,1:T(8,128)S(1)}, u32[]{:S(2)}) copy-start(f32[1024,64]{0,1:T(8,128)S(1)} %get-tuple-element.217) | copy-start | bytes 786436
  58.7 160.1 %copy-start.17 = (f32[1024,64]{0,1:T(8,128)}, f32[1024,64]{0,1:T(8,128)S(1)}, u32[]{:S(2)}) copy-start(f32[1024,64]{0,1:T(8,128)S(1)} %get-tuple-element.216) | copy-start | bytes 786436
  58.9 68.6 %copy-start.80 = (f32[256]{0:T(256)}, f32[256]{0:T(256)S(1)}, u32[]{:S(2)}) copy-start(f32[256]{0:T(256)S(1)} %fusion.55) | copy-start | bytes 3076
  59.0 143.8 %copy-start.74 = (f32[64]{0:T(128)}, f32[64]{0:T(128)S(1)}, u32[]{:S(2)}) copy-start(f32[64]{0:T(128)S(1)} %get-tuple-element.218) | copy-start | bytes 772
  59.0 159.8 %copy-start.76 = (f32[64]{0:T(128)}, f32[64]{0:T(128)S(1)}, u32[]{:S(2)}) copy-start(f32[64]{0:T(128)S(1)} %get-tuple-element.219) | copy-start | bytes 772
  60.4 130.5 %copy-start.38 = (bf16[256,1536]{1,0:T(8,128)(2,1)}, bf16[256,1536]{1,0:T(8,128)(2,1)S(1)}, u32[]{:S(2)}) copy-start(bf16[256,1536]{1,0:T(8,128)(2,1)S(1)} %fusion.43) | copy-start | bytes 2359300
  71.4 56.8 %all-to-all-start.1 = ((bf16[256,4,128]{2,0,1:T(8,128)(2,1)}), bf16[256,4,128]{2,0,1:T(8,128)(2,1)S(1)}, u32[]{:S(2)}, u32[]{:S(2)}) async-start(bf16[256,4,128]{2,0,1:T(8,128)(2,1)} %bitcast.427), calls=%async_computation.1 | async-start | bytes 524288 | tf_op jit(solution)/shard_map/all_to_all | solution.py:215
  128.3 69.6 %all-to-all-start = ((bf16[256,4,128]{2,0,1:T(8,128)(2,1)}), bf16[256,4,128]{2,0,1:T(8,128)(2,1)S(1)}, u32[]{:S(2)}, u32[]{:S(2)}) async-start(bf16[256,4,128]{2,0,1:T(8,128)(2,1)} %bitcast.428), calls=%async_computation | async-start | bytes 524288 | tf_op jit(solution)/shard_map/all_to_all | solution.py:222
  132.2 70.5 %copy-start.10 = (f32[1024,2,64]{0,2,1:T(8,128)}, f32[1024,2,64]{0,2,1:T(8,128)S(1)}, u32[]{:S(2)}) copy-start(f32[1024,2,64]{0,2,1:T(8,128)S(1)} %reshape.642) | copy-start | bytes 1572868
  132.3 63.2 %copy-start.68 = (f32[1024,2]{0,1:T(2,128)}, f32[1024,2]{0,1:T(2,128)S(1)}, u32[]{:S(2)}) copy-start(f32[1024,2]{0,1:T(2,128)S(1)} %multiply_reduce_fusion.8) | copy-start | bytes 24580
  132.4 70.4 %copy-start.58 = (f32[1024,2]{0,1:T(2,128)}, f32[1024,2]{0,1:T(2,128)S(1)}, u32[]{:S(2)}) copy-start(f32[1024,2]{0,1:T(2,128)S(1)} %fusion.123) | copy-start | bytes 24580
  197.8 15.6 %all-to-all-start.2 = ((bf16[256,4,384]{0,2,1:T(8,128)(2,1)}), bf16[256,4,384]{0,2,1:T(8,128)(2,1)S(1)}, u32[]{:S(2)}, u32[]{:S(2)}) async-start(bf16[256,4,384]{0,2,1:T(8,128)(2,1)} %bitcast.10), calls=%async_computation.2 | async-start | bytes 1572864 | tf_op jit(solution)/shard_map/all_to_all | solution.py:208
  221.0 568.2 %copy-start.2 = (f32[3,512,512]{1,2,0:T(8,128)}, f32[3,512,512]{1,2,0:T(8,128)S(1)}, u32[]{:S(2)}) copy-start(f32[3,512,512]{1,2,0:T(8,128)S(1)} %get-tuple-element.227) | copy-start | bytes 9437188
  222.2 6.0 copy-start.4
  240.5 15.9 %all-to-all-start.3 = ((bf16[4,2,49152]{2,1,0:T(2,128)(2,1)}), bf16[4,2,49152]{2,1,0:T(2,128)(2,1)}, u32[]{:S(2)}, u32[]{:S(2)}) async-start(bf16[4,2,49152]{2,1,0:T(2,128)(2,1)} %reshape.676), calls=%async_computation.3 | async-start | bytes 1572864 | tf_op jit(solution)/shard_map/all_to_all | solution.py:250
  244.7 465.7 %copy-start.62 = (f32[1536]{0:T(1024)}, f32[1536]{0:T(1024)S(1)}, u32[]{:S(2)}) copy-start(f32[1536]{0:T(1024)S(1)} %convert_element_type.312) | copy-start | bytes 18436
  269.6 440.8 %copy-start.70 = (f32[256]{0:T(256)}, f32[256]{0:T(256)S(1)}, u32[]{:S(2)}) copy-start(f32[256]{0:T(256)S(1)} %fusion.125) | copy-start | bytes 3076
  685.0 12.4 copy-start.13
  710.4 6.1 copy-start.78
  716.5 15.0 %copy-start.39 = (bf16[256,1536]{1,0:T(8,128)(2,1)S(1)}, bf16[256,1536]{1,0:T(8,128)(2,1)}, u32[]{:S(2)}) copy-start(bf16[256,1536]{1,0:T(8,128)(2,1)} %copy-done.38) | copy-start | bytes 2359300
  733.4 41.7 %all-to-all-start.8 = ((bf16[256,4,1536]{2,0,1:T(8,128)(2,1)}), bf16[256,4,1536]{2,0,1:T(8,128)(2,1)}, u32[]{:S(2)}, u32[]{:S(2)}) async-start(bf16[256,4,1536]{2,0,1:T(8,128)(2,1)} %broadcast_in_dim.62), calls=%async_computation.8 | async-start | bytes 6291456 | tf_op jit(solution)/shard_map/all_to_all | solution.py:229
  738.1 44.8 %copy-start.64 = (f32[3,512]{1,0:T(4,128)}, f32[3,512]{1,0:T(4,128)S(1)}, u32[]{:S(2)}) copy-start(f32[3,512]{1,0:T(4,128)S(1)} %log_add_fusion.1) | copy-start | bytes 18436
  778.1 41.8 %all-to-all-start.14 = ((bf16[256,4,1536]{2,0,1:T(8,128)(2,1)}), bf16[256,4,1536]{2,0,1:T(8,128)(2,1)}, u32[]{:S(2)}, u32[]{:S(2)}) async-start(bf16[256,4,1536]{2,0,1:T(8,128)(2,1)} %broadcast_in_dim.65), calls=%async_computation.18 | async-start | bytes 6291456 | tf_op jit(solution)/shard_map/all_to_all | solution.py:307
  782.9 5.5 copy-start.21
  782.9 5.5 copy-start.66
  793.3 26.6 %copy-start.40 = (bf16[256,1536]{1,0:T(8,128)(2,1)S(1)}, bf16[256,1536]{1,0:T(8,128)(2,1)}, u32[]{:S(2)}) copy-start(bf16[256,1536]{1,0:T(8,128)(2,1)} %multiply_convert_fusion.2) | copy-start | bytes 2359300
  821.8 10.0 slice-start
  821.8 41.9 %all-to-all-start.10 = ((bf16[256,4,1536]{2,0,1:T(8,128)(2,1)}), bf16[256,4,1536]{2,0,1:T(8,128)(2,1)}, u32[]{:S(2)}, u32[]{:S(2)}) async-start(bf16[256,4,1536]{2,0,1:T(8,128)(2,1)} %broadcast_in_dim.64), calls=%async_computation.14 | async-start | bytes 6291456 | tf_op jit(solution)/shard_map/all_to_all | solution.py:304
  835.9 27.9 %copy-start.42 = (bf16[256,1536]{1,0:T(8,128)(2,1)S(1)}, bf16[256,1536]{1,0:T(8,128)(2,1)}, u32[]{:S(2)}) copy-start(bf16[256,1536]{1,0:T(8,128)(2,1)} %copy-done.41) | copy-start | bytes 2359300
  865.6 5.8 copy-start.69
  865.6 41.8 %all-to-all-start.9 = ((bf16[256,4,1536]{2,0,1:T(8,128)(2,1)}), bf16[256,4,1536]{2,0,1:T(8,128)(2,1)}, u32[]{:S(2)}, u32[]{:S(2)}) async-start(bf16[256,4,1536]{2,0,1:T(8,128)(2,1)} %broadcast_in_dim.63), calls=%async_computation.12 | async-start | bytes 6291456 | tf_op jit(solution)/shard_map/all_to_all | solution.py:350
  870.4 351.3 %reduce-scatter.10.cloned.1.call-start = ((), (), s32[]{:S(2)}) async-start(), calls=%async_computation.28 | async-start | bytes 442368 | tf_op jit(solution)/shard_map/reduce_scatter | solution.py:403
  876.1 8.6 slice-start.2
  879.0 5.7 slice-start.3
  907.4 45.9 %all-to-all-start.12 = ((bf16[256,4,1728]{0,2,1:T(8,128)(2,1)}), bf16[256,4,1728]{0,2,1:T(8,128)(2,1)}, u32[]{:S(2)}, u32[]{:S(2)}) async-start(bf16[256,4,1728]{0,2,1:T(8,128)(2,1)} %bitcast.109), calls=%async_computation.16 | async-start | bytes 7077888 | tf_op jit(solution)/shard_map/all_to_all | solution.py:290
  912.1 311.0 %reduce-scatter.12.cloned.1.call-start = ((), (), s32[]{:S(2)}) async-start(), calls=%async_computation.29 | async-start | bytes 442368 | tf_op jit(solution)/shard_map/reduce_scatter | solution.py:409
  912.2 5.9 copy-start.5
  953.3 46.0 %all-to-all-start.11 = ((bf16[256,4,1728]{0,2,1:T(8,128)(2,1)}), bf16[256,4,1728]{0,2,1:T(8,128)(2,1)}, u32[]{:S(2)}, u32[]{:S(2)}) async-start(bf16[256,4,1728]{0,2,1:T(8,128)(2,1)} %bitcast.435), calls=%async_computation.15 | async-start | bytes 7077888 | tf_op jit(solution)/shard_map/all_to_all | solution.py:283
  958.1 266.5 %reduce-scatter.8.cloned.1.call-start = ((), (), s32[]{:S(2)}) async-start(), calls=%async_computation.27 | async-start | bytes 1327104 | tf_op jit(solution)/shard_map/reduce_scatter | solution.py:397
  999.3 44.9 %all-to-all-start.13 = ((bf16[256,4,1728]{0,2,1:T(8,128)(2,1)}), bf16[256,4,1728]{0,2,1:T(8,128)(2,1)S(1)}, u32[]{:S(2)}, u32[]{:S(2)}) async-start(bf16[256,4,1728]{0,2,1:T(8,128)(2,1)} %bitcast.114), calls=%async_computation.17 | async-start | bytes 7077888 | tf_op jit(solution)/shard_map/all_to_all | solution.py:297
  1003.1 223.2 %reduce-scatter.14.cloned.1.call-start = ((), (), s32[]{:S(2)}) async-start(), calls=%async_computation.30 | async-start | bytes 1327104 | tf_op jit(solution)/shard_map/reduce_scatter | solution.py:415
  1008.5 401.8 %reduce-scatter.16.cloned.1.call-start = ((), (), s32[]{:S(2)}) async-start(), calls=%async_computation.31 | async-start | bytes 18137088
  1044.2 7.9 copy-start.31
  1044.2 7.9 copy-start.32
  1117.6 6.1 copy-start.45
  1117.6 16.1 %copy-start.37 = (bf16[1024,6,64]{0,2,1:T(8,128)(2,1)S(1)}, bf16[1024,6,64]{0,2,1:T(8,128)(2,1)}, u32[]{:S(2)}) copy-start(bf16[1024,6,64]{0,2,1:T(8,128)(2,1)} %copy-done.36) | copy-start | bytes 2359300
  1120.3 9.4 all-to-all-start.6
  1129.7 10.2 all-to-all-start.7
  1133.7 10.5 copy-start.14
  1139.8 19.2 %all-to-all-start.5 = ((bf16[4,2,49152]{2,1,0:T(2,128)(2,1)}), bf16[4,2,49152]{2,1,0:T(2,128)(2,1)}, u32[]{:S(2)}, u32[]{:S(2)}) async-start(bf16[4,2,49152]{2,1,0:T(2,128)(2,1)} %reshape.678), calls=%async_computation.5 | async-start | bytes 1572864 | tf_op jit(solution)/shard_map/all_to_all | solution.py:372
  1144.3 12.2 copy-start.83
  1168.6 49.2 %copy-start.81 = (f32[256]{0:T(256)S(1)}, f32[256]{0:T(256)}, u32[]{:S(2)}) copy-start(f32[256]{0:T(256)} %copy-done.80) | copy-start | bytes 3076
  1168.6 49.2 %copy-start.25 = (bf16[1,256,1536]{2,1,0:T(8,128)(2,1)S(1)}, bf16[1,256,1536]{2,1,0:T(8,128)(2,1)}, u32[]{:S(2)}) copy-start(bf16[1,256,1536]{2,1,0:T(8,128)(2,1)} %param.47) | copy-start | bytes 2359300
  1168.6 49.2 %copy-start.63 = (f32[1536]{0:T(1024)S(1)}, f32[1536]{0:T(1024)}, u32[]{:S(2)}) copy-start(f32[1536]{0:T(1024)} %copy-done.62) | copy-start | bytes 18436
  1168.6 49.2 %copy-start.71 = (f32[256]{0:T(256)S(1)}, f32[256]{0:T(256)}, u32[]{:S(2)}) copy-start(f32[256]{0:T(256)} %copy-done.70) | copy-start | bytes 3076
  1168.7 49.2 %copy-start.79 = (f32[256]{0:T(256)S(1)}, f32[256]{0:T(256)}, u32[]{:S(2)}) copy-start(f32[256]{0:T(256)} %copy-done.78) | copy-start | bytes 3076
  (52 other events, 136.1 us)
Sparse Core Ops, SparseCore 0:
  10.9 57.7 all-gather.9
  71.6 53.9 all-gather.7
  128.4 62.4 all-gather.11
  193.7 62.3 all-gather.13
  258.9 134.6 all-gather.15
  396.4 134.0 all-gather.17
  533.3 134.0 all-gather.19
  876.2 60.8 reduce-scatter.9
  940.4 60.4 reduce-scatter.11
  1004.7 63.0 reduce-scatter.7
  1071.7 63.0 reduce-scatter.13
  1138.6 271.6 reduce-scatter.15
where the time goes:
time: 1440 us; the launch traced here: 1430 us
  waiting for transfers between devices  860 us (60%)
  matrix products  193 us (13%)
  local copies, waits for them, and re-layouts  109 us (8%)
  blocking collectives  102 us (7%)
  other arithmetic  90.5 us (6%)
  starting transfers between devices  60 us (4%)
  between operations  16.1 us (1%)
    unnamed x13, waiting for transfers between devices  187 us
    all_gather x1, waiting for transfers between devices, on_device(): lax.all_gather(down_weight, ('fsdp', 'seq'), axis=0, tiled=True)  122 us
    all_gather x1, waiting for transfers between devices, on_device(): lax.all_gather(up_weight, ('fsdp', 'seq'), axis=0, tiled=True)  122 us
    all_gather x1, waiting for transfers between devices, on_device(): lax.all_gather(gate_weight, ('fsdp', 'seq'), axis=0, tiled=True)  122 us
    unnamed x2, blocking collectives  86.7 us
    unnamed x210, local copies, waits for them, and re-layouts  63.3 us
    dot_general x7, matrix products, project(): return jnp.dot(left_side, right_side, preferred_element_type=jnp.float32)  59.9 us
    all_gather x1, waiting for transfers between devices, on_device(): lax.all_gather(query_weight, ('fsdp', 'seq'), axis=0, tiled=True)  58.6 us
  transfers between devices with their start and end apart: 26, of which 18 were waited for; matrix products, arithmetic and copies ran while one was open for 22% of the time, Pallas kernels for 0%

commit v1 on v0

v1 whole, which is shorter than its diff:
```python
from functools import partial

import jax
import jax.numpy as jnp
from jax import lax
from jax.sharding import Mesh
from jax.sharding import PartitionSpec as P

HEADS = 24
KV_HEADS = 8
HEAD_DIM = 64
GROUP = HEADS // KV_HEADS

EPSILON = 1e-05
ROPE_BASE = 1000000.0
PLANE = ("x", "y", "c")
SWAP = ((0, 1), (1, 0))
F32 = jnp.float32
BF16 = jnp.bfloat16


def scaled_norm(values, gain_row):
    mean_square = jnp.mean(values * values, axis=-1, keepdims=True)
    return values * lax.rsqrt(mean_square + EPSILON) * gain_row


def rotary_tables(positions, head_size):
    half_dim = head_size // 2
    exponent = jnp.arange(half_dim).astype(F32) * (2.0 / head_size)
    frequency = jnp.power(F32(ROPE_BASE), -exponent)
    angles = positions.astype(F32)[:, None] * frequency[None, :]
    angles = jnp.concatenate([angles, angles], axis=-1)
    return (jnp.cos(angles)[:, None, :], jnp.sin(angles)[:, None, :])


def head_prepare(raw_heads, head_gain, cosine_table, sine_table):
    normed = scaled_norm(raw_heads, head_gain)
    half_dim = raw_heads.shape[-1] // 2
    turned = jnp.concatenate([-normed[..., half_dim:], normed[..., :half_dim]], axis=-1)
    return normed * cosine_table + turned * sine_table


def gating(gate_act, up_act):
    return gate_act * jax.nn.sigmoid(gate_act) * up_act


def project(left_side, right_side):
    return jnp.dot(left_side, right_side, preferred_element_type=F32)


def contract_rows(left_side, right_side):
    return lax.dot_general(
        left_side, right_side, (((0,), (0,)), ((), ())), preferred_element_type=F32
    )


def contract_last(left_side, right_side):
    return lax.dot_general(
        left_side, right_side, (((1,), (1,)), ((), ())), preferred_element_type=F32
    )


def attention_forward(queries, key_rows, value_rows):
    length = queries.shape[0]
    block_rows = min(512, length)
    score_scale = queries.shape[-1] ** (-0.5)
    per_head = []
    log_totals = []
    for head_index in range(queries.shape[1]):
        head_blocks = []
        head_totals = []
        for block_index in range(length // block_rows):
            first_row = block_index * block_rows
            finish = first_row + block_rows
            query_block = queries[first_row:finish, head_index]
            scores = (
                jnp.einsum(
                    "qgd,td->gqt",
                    query_block,
                    key_rows[:finish, head_index],
                    preferred_element_type=F32,
                )
                * score_scale
            )
            causal = (first_row + jnp.arange(block_rows))[:, None] >= jnp.arange(finish)[None, :]
            scores = jnp.where(causal, scores, -1e30)
            row_top = jnp.max(scores, axis=-1, keepdims=True)
            weights = jnp.exp(scores - row_top)
            row_total = jnp.sum(weights, axis=-1, keepdims=True)
            attention = (weights / row_total).astype(BF16)
            head_blocks.append(
                jnp.einsum(
                    "gqt,td->qgd",
                    attention,
                    value_rows[:finish, head_index],
                    preferred_element_type=F32,
                )
            )
            head_totals.append(row_top + jnp.log(row_total))
        per_head.append(jnp.concatenate(head_blocks, axis=0))
        log_totals.append(head_totals)
    return (jnp.stack(per_head, axis=1), log_totals)


def attention_backward(queries, key_rows, value_rows, grad_heads, log_totals):
    length = queries.shape[0]
    block_rows = min(512, length)
    score_scale = queries.shape[-1] ** (-0.5)
    query_parts = []
    key_parts = []
    value_parts = []
    for head_index in range(queries.shape[1]):
        head_queries = []
        key_total = jnp.zeros((length, queries.shape[-1]), F32)
        value_total = jnp.zeros((length, queries.shape[-1]), F32)
        for block_index in range(length // block_rows):
            first_row = block_index * block_rows
            finish = first_row + block_rows
            query_block = queries[first_row:finish, head_index]
            grad_block = grad_heads[first_row:finish, head_index]
            key_slice = key_rows[:finish, head_index]
            value_slice = value_rows[:finish, head_index]
            scores = (
                jnp.einsum("qgd,td->gqt", query_block, key_slice, preferred_element_type=F32)
                * score_scale
            )
            causal = (first_row + jnp.arange(block_rows))[:, None] >= jnp.arange(finish)[None, :]
            scores = jnp.where(causal, scores, -1e30)
            attention = jnp.exp(scores - log_totals[head_index][block_index])
            prob_grad = jnp.einsum(
                "qgd,td->gqt", grad_block, value_slice, preferred_element_type=F32
            )
            row_dot = jnp.sum(attention * prob_grad, axis=-1, keepdims=True)
            score_grad = (attention * (prob_grad - row_dot)).astype(BF16)
            head_queries.append(
                jnp.einsum("gqt,td->qgd", score_grad, key_slice, preferred_element_type=F32)
                * score_scale
            )
            key_total = key_total.at[:finish].add(
                jnp.einsum("gqt,qgd->td", score_grad, query_block, preferred_element_type=F32)
                * score_scale
            )
            value_total = value_total.at[:finish].add(
                jnp.einsum(
                    "gqt,qgd->td",
                    attention.astype(BF16),
                    grad_block,
                    preferred_element_type=F32,
                )
            )
        query_parts.append(jnp.concatenate(head_queries, axis=0))
        key_parts.append(key_total)
        value_parts.append(value_total)
    return (
        jnp.stack(query_parts, axis=1),
        jnp.stack(key_parts, axis=1),
        jnp.stack(value_parts, axis=1),
    )


def swap(values, axis):
    return lax.ppermute(values, axis, SWAP)


def plane_gather(rows):
    half = rows.shape[0] // 2
    from_y = swap(rows, "y")
    from_x = swap(rows, "x")
    corner = jnp.concatenate([swap(from_y[:half], "x"), swap(from_x[half:], "y")], axis=0)
    mine = jnp.stack([rows, from_y, from_x, corner])
    both = jnp.stack([mine, swap(mine, "c")], axis=1)
    return both.reshape((2, 2, 2) + rows.shape)


def plane_scatter(parts):
    half = parts.shape[3] // 2
    halves = parts[:, :, 0].astype(F32) + swap(parts[:, :, 1], "c").astype(F32)
    mine, other = halves[0, 0], halves.astype(BF16)
    for_x, for_y = other[1, 0], other[0, 1]
    corner = other[1, 1]
    by_x = swap(corner[:half], "x")
    by_y = swap(corner[half:], "y")
    for_y = jnp.concatenate(
        [(for_y[:half].astype(F32) + by_x.astype(F32)).astype(BF16), for_y[half:]], axis=0
    )
    for_x = jnp.concatenate(
        [for_x[:half], (for_x[half:].astype(F32) + by_y.astype(F32)).astype(BF16)], axis=0
    )
    return mine + swap(for_y, "y").astype(F32) + swap(for_x, "x").astype(F32)


def line_gather(block):
    count = lax.axis_size("dp")
    place = lax.axis_index("dp")
    up, down = [block], [block]
    for step in range(1, count):
        up.append(
            lax.ppermute(up[-1], "dp", [(i, i + 1) for i in range(step - 1, count - 1)])
        )
        down.append(
            lax.ppermute(down[-1], "dp", [(i + 1, i) for i in range(count - step)])
        )
    rows = block.shape[0]
    whole = jnp.zeros((count * rows, block.shape[1]), block.dtype)
    whole = lax.dynamic_update_slice_in_dim(whole, block, place * rows, 0)
    for step in range(1, count):
        source = lax.rem(place - step + count, count)
        piece = jnp.where(place >= step, up[step], down[count - step])
        whole = lax.dynamic_update_slice_in_dim(whole, piece, source * rows, 0)
    return whole


def line_scatter(parts):
    count = lax.axis_size("dp")
    place = lax.axis_index("dp")
    rows = parts.shape[0] // count

    def own(index):
        return lax.dynamic_slice_in_dim(parts, jnp.clip(index, 0, count - 1) * rows, rows, 0)

    up = down = None
    for step in range(1, count):
        for_up = own(count - step + place)
        for_down = own(step - count + place)
        if step > 1:
            for_up = (for_up.astype(F32) + up.astype(F32)).astype(BF16)
            for_down = (for_down.astype(F32) + down.astype(F32)).astype(BF16)
        up = lax.ppermute(for_up, "dp", [(i, i + 1) for i in range(step)])
        down = lax.ppermute(for_down, "dp", [(i + 1, i) for i in range(count - 1 - step, count - 1)])
    return own(place).astype(F32) + up.astype(F32) + down.astype(F32)


def to_columns(weight, groups):
    rows = weight.shape[0]
    return (
        weight.reshape(rows, groups, 2, -1).transpose(2, 1, 0, 3).reshape(2 * groups, rows, -1)
    )


def plane_columns(payload):
    out = lax.all_to_all(payload, PLANE, split_axis=0, concat_axis=0, tiled=True)
    return out.reshape(-1, payload.shape[2])


def flip_blocks(values):
    values = jnp.where(lax.axis_index("y") == 1, jnp.flip(values, 1), values)
    return jnp.where(lax.axis_index("c") == 1, jnp.flip(values, 2), values)


def to_sequences(rows, batch, tokens):
    width = rows.shape[-1]
    blocks = flip_blocks(rows.reshape(2, 2, 2, batch, tokens, width))
    return blocks.transpose(0, 3, 1, 2, 4, 5).reshape(2 * batch, 4 * tokens, width)


def from_sequences(rows, batch, tokens):
    width = rows.shape[-1]
    blocks = rows.reshape(2, batch, 2, 2, tokens, width).transpose(0, 2, 3, 1, 4, 5)
    return flip_blocks(blocks).reshape(8 * batch * tokens, width)


def spread_columns(own, other):
    first = lax.axis_index("x") == 0
    return jnp.concatenate(
        [jnp.where(first, own, other), jnp.where(first, other, own)], axis=1
    )


def settle(sums):
    rows = sums.shape[0] // 2
    x = lax.axis_index("x")
    own = lax.dynamic_slice_in_dim(sums, x * rows, rows, 0)
    send = lax.dynamic_slice_in_dim(sums, (1 - x) * rows, rows, 0).astype(BF16)
    return own, swap(send, "x").astype(F32)


def on_device(
    layer_input,
    attention_gain,
    query_weight,
    key_weight,
    value_weight,
    output_weight,
    head_gains,
    feedforward_gain,
    gate_weight,
    up_weight,
    down_weight,
    upstream,
):
    batch, tokens, model_width = layer_input.shape
    groups = 4
    rows = query_weight.shape[0]
    own_rows = batch * tokens

    gain_rows = jnp.stack(
        [attention_gain, feedforward_gain, jnp.pad(head_gains, (0, rows - head_gains.shape[0]))],
        axis=1,
    )
    gain_rows = jnp.pad(gain_rows, ((0, 0), (0, 61)))
    qkv_payload = jnp.concatenate(
        [
            to_columns(query_weight, groups),
            to_columns(key_weight, groups),
            to_columns(value_weight, groups),
            jnp.broadcast_to(gain_rows[None], (2 * groups,) + gain_rows.shape),
        ],
        axis=2,
    )
    query_cols = query_weight.shape[1] // 8
    kv_cols = key_weight.shape[1] // 8
    qkv_cols = query_cols + 2 * kv_cols
    qkv_full = line_gather(plane_columns(qkv_payload))
    out_full = line_gather(plane_columns(to_columns(output_weight, groups)))
    gate_cols = to_columns(gate_weight, groups)
    up_cols = to_columns(up_weight, groups)
    down_cols = to_columns(down_weight, groups)
    wide = gate_cols.shape[2]
    cuts = [0, 256, 512, wide]
    ffn_full = []
    for first, last in zip(cuts[:-1], cuts[1:]):
        chunk = jnp.concatenate(
            [gate_cols[:, :, first:last], up_cols[:, :, first:last], down_cols[:, :, first:last]],
            axis=2,
        )
        ffn_full.append(line_gather(plane_columns(chunk)))

    own_hidden = layer_input.reshape(own_rows, model_width)
    own_upstream = upstream.reshape(own_rows, model_width)
    plane_rows = 8 * own_rows
    hidden_whole = plane_gather(own_hidden).reshape(plane_rows, model_width)
    upstream_whole = plane_gather(own_upstream).reshape(plane_rows, model_width)
    gains = qkv_full[:, qkv_cols : qkv_cols + 3].astype(F32)
    attention_scale = gains[:, 0]
    feedforward_scale = gains[:, 1]
    head_scale = gains[:, 2].reshape(-1, rows)[:, : head_gains.shape[0]].reshape(-1)
    query_scale = head_scale[:HEAD_DIM]
    key_scale = head_scale[HEAD_DIM:]
    normed_whole = scaled_norm(hidden_whole.astype(F32), attention_scale).astype(BF16)
    qkv_weight = qkv_full[:, :qkv_cols]
    qkv = project(normed_whole, qkv_weight).astype(BF16)
    qkv = to_sequences(qkv, batch, tokens)
    sequences, length = qkv.shape[:2]
    qkv = qkv.transpose(1, 0, 2)
    cosine_table, sine_table = rotary_tables(jnp.arange(length), HEAD_DIM)
    prepare = partial(head_prepare, cosine_table=cosine_table, sine_table=sine_table)
    queries_float, query_pull = jax.vjp(
        prepare,
        qkv[:, :, :query_cols].reshape(length, sequences * GROUP, HEAD_DIM).astype(F32),
        query_scale,
    )
    keys_float, key_pull = jax.vjp(
        prepare,
        qkv[:, :, query_cols : query_cols + kv_cols].astype(F32),
        key_scale,
    )
    query_heads = queries_float.astype(BF16).reshape(length, sequences, GROUP, HEAD_DIM)
    key_heads = keys_float.astype(BF16)
    value_heads = qkv[:, :, query_cols + kv_cols :]
    mixed_heads, log_totals = attention_forward(query_heads, key_heads, value_heads)
    mixed = mixed_heads.astype(BF16).reshape(length, sequences, query_cols).transpose(1, 0, 2)
    mixed = from_sequences(mixed, batch, tokens)
    parts = contract_last(mixed, out_full).astype(BF16)
    middle = own_hidden.astype(F32) + plane_scatter(
        parts.reshape(2, 2, 2, own_rows, model_width)
    )

    post_float, feedforward_pull = jax.vjp(scaled_norm, middle, feedforward_scale)
    post_whole = plane_gather(post_float.astype(BF16)).reshape(plane_rows, model_width)
    branch = post_grad = None
    ffn_sums = []
    for chunk in ffn_full:
        width = chunk.shape[1] // 3
        activated_grad = project(upstream_whole, chunk[:, 2 * width :])
        both = project(post_whole, chunk[:, : 2 * width])
        activated_float, gating_pull = jax.vjp(gating, both[:, :width], both[:, width:])
        activated = activated_float.astype(BF16)
        gate_float, up_float = gating_pull(activated_grad)
        both_grad = jnp.concatenate([gate_float.astype(BF16), up_float.astype(BF16)], axis=1)
        post_part = contract_last(both_grad, chunk[:, : 2 * width])
        post_grad = post_part if post_grad is None else post_grad + post_part
        branch_part = contract_last(activated, chunk[:, 2 * width :])
        branch = branch_part if branch is None else branch + branch_part
        weight_parts = jnp.concatenate(
            [
                contract_rows(post_whole, both_grad).astype(BF16),
                contract_rows(upstream_whole, activated).astype(BF16),
            ],
            axis=1,
        )
        ffn_sums.append(settle(line_scatter(weight_parts)))
    post_grad = plane_scatter(post_grad.astype(BF16).reshape(2, 2, 2, own_rows, model_width))
    branch = plane_scatter(branch.astype(BF16).reshape(2, 2, 2, own_rows, model_width))
    layer_output = (middle + branch).astype(BF16)
    ffn_grads = []
    for index in range(3):
        own, other = [], []
        for mine, theirs in ffn_sums:
            width = mine.shape[1] // 3
            own.append(mine[:, index * width : (index + 1) * width])
            other.append(theirs[:, index * width : (index + 1) * width])
        ffn_grads.append(
            spread_columns(jnp.concatenate(own, axis=1), jnp.concatenate(other, axis=1))
        )
    middle_part, feedforward_gain_grad = feedforward_pull(post_grad)
    middle_grad = own_upstream.astype(F32) + middle_part
    middle_low = middle_grad.astype(BF16)

    middle_whole = plane_gather(middle_low).reshape(plane_rows, model_width)
    mixed_grad = project(middle_whole, out_full).astype(BF16)
    out_own, out_other = settle(line_scatter(contract_rows(middle_whole, mixed).astype(BF16)))
    output_weight_grad = spread_columns(out_own, out_other)
    grad_heads = (
        to_sequences(mixed_grad, batch, tokens)
        .transpose(1, 0, 2)
        .reshape(length, sequences, GROUP, HEAD_DIM)
    )
    query_grad, key_grad, value_grad = attention_backward(
        query_heads, key_heads, value_heads, grad_heads, log_totals
    )
    query_raw_grad, query_gain_grad = query_pull(
        query_grad.astype(BF16).astype(F32).reshape(length, sequences * GROUP, HEAD_DIM)
    )
    key_raw_grad, key_gain_grad = key_pull(key_grad.astype(BF16).astype(F32))
    qkv_grad = jnp.concatenate(
        [
            query_raw_grad.astype(BF16).reshape(length, sequences, query_cols),
            key_raw_grad.astype(BF16),
            value_grad.astype(BF16),
        ],
        axis=2,
    )
    qkv_grad = from_sequences(qkv_grad.transpose(1, 0, 2), batch, tokens)
    weight_parts = contract_rows(normed_whole, qkv_grad)
    gain_part = jnp.sum(weight_parts * qkv_weight.astype(F32), axis=1) / attention_scale
    head_part = jnp.concatenate([query_gain_grad, key_gain_grad]).reshape(-1, head_gains.shape[0])
    head_part = jnp.pad(head_part, ((0, 0), (0, rows - head_gains.shape[0]))).reshape(-1)
    gain_parts = jnp.stack([gain_part, feedforward_gain_grad, head_part], axis=1)
    weight_parts = jnp.concatenate(
        [weight_parts.astype(BF16), jnp.pad(gain_parts, ((0, 0), (0, 61))).astype(BF16)], axis=1
    )
    own, other = settle(line_scatter(weight_parts))
    query_weight_grad = spread_columns(own[:, :query_cols], other[:, :query_cols])
    key_weight_grad = spread_columns(
        own[:, query_cols : query_cols + kv_cols], other[:, query_cols : query_cols + kv_cols]
    )
    value_weight_grad = spread_columns(
        own[:, query_cols + kv_cols : qkv_cols], other[:, query_cols + kv_cols : qkv_cols]
    )
    gain_sums = (own[:, qkv_cols : qkv_cols + 3] + other[:, qkv_cols : qkv_cols + 3]).T
    for axis in ("y", "c"):
        half = gain_sums.shape[1] // 2
        place = lax.axis_index(axis)
        keep = lax.dynamic_slice_in_dim(gain_sums, place * half, half, 1)
        send = lax.dynamic_slice_in_dim(gain_sums, (1 - place) * half, half, 1)
        gain_sums = keep + swap(send, axis)

    parts = contract_last(qkv_grad, qkv_weight).astype(BF16)
    normed_grad = plane_scatter(parts.reshape(2, 2, 2, own_rows, model_width))
    _, attention_pull = jax.vjp(
        lambda v: scaled_norm(v, attention_scale), own_hidden.astype(F32)
    )
    input_grad = middle_grad + attention_pull(normed_grad)[0]
    return (
        layer_output.reshape(layer_input.shape),
        input_grad.reshape(layer_input.shape),
        gain_sums[0],
        query_weight_grad,
        key_weight_grad,
        value_weight_grad,
        output_weight_grad,
        gain_sums[2, : head_gains.shape[0]],
        gain_sums[1],
        ffn_grads[0],
        ffn_grads[1],
        ffn_grads[2],
    )


def solution(mesh):
    fsdp, seq = mesh.shape["fsdp"], mesh.shape["seq"]
    plane_mesh = Mesh(mesh.devices.reshape(fsdp // 2, 2, seq // 2, 2), ("dp", "x", "y", "c"))
    batch = ("dp", "x")
    split = ("y", "c")
    rows = ("dp", "x", "y", "c")
    return jax.shard_map(
        on_device,
        mesh=plane_mesh,
        in_specs=(
            P(batch, split, None),
            P(rows),
            P(rows, None),
            P(rows, None),
            P(rows, None),
            P(rows, None),
            P(rows),
            P(rows),
            P(rows, None),
            P(rows, None),
            P(rows, None),
            P(batch, split, None),
        ),
        out_specs=(
            P(batch, split, None),
            P(batch, split, None),
            P(rows),
            P(batch, split),
            P(batch, split),
            P(batch, split),
            P(batch, split),
            P(rows),
            P(rows),
            P(batch, split),
            P(batch, split),
            P(batch, split),
        ),
        check_vma=False,
    )
```

time: 1440 us -> 945 us (0.66)
  waiting for transfers between devices: 860 us -> 191 us
  starting transfers between devices: 60 us -> 242 us
  blocking collectives: 102 us -> 0 us
  other arithmetic: 90.5 us -> 180 us
  local copies, waits for them, and re-layouts: 109 us -> 155 us
  matrix products: 193 us -> 162 us
    all_gather x7 -> x0, waiting for transfers between devices: 483 us -> none  [the longest x1 122 us: on_device(): lax.all_gather(down_weight, ('fsdp', 'seq'), axis=0, tiled=True)]
    ppermute x0 -> x107, starting transfers between devices: none -> 224 us  [the longest x15 96.2 us: line_scatter(): up = lax.ppermute(for_up, 'dp', [(i, i + 1) for i in range(step)])]
    unnamed x13 -> x0, waiting for transfers between devices: 187 us -> none
    ppermute x0 -> x107, waiting for transfers between devices: none -> 174 us  [the longest x47 95.7 us: swap(): return lax.ppermute(values, axis, SWAP)]
    all_to_all x14 -> x5, waiting for transfers between devices: 189 us -> 16.7 us  [plane_columns(): lax.all_to_all(payload, PLANE, split_axis=0, concat_axis=0, tiled=True)]
    unnamed x2 -> x0, blocking collectives: 86.7 us -> none
    rev x0 -> x4, local copies, waits for them, and re-layouts: none -> 41 us  [flip_blocks(): return jnp.where(lax.axis_index('c') == 1, jnp.flip(values, 2), values)]
    all_to_all x14 -> x5, starting transfers between devices: 58.9 us -> 18.1 us  [plane_columns(): lax.all_to_all(payload, PLANE, split_axis=0, concat_axis=0, tiled=True)]
  transfers between devices with their start and end apart: 26 -> 112, of which waited for: 18 -> 37; matrix products, arithmetic and copies ran while one was open for 22% -> 32% of each run, Pallas kernels for 0% -> 0%
where the time goes in v1:
time: 945 us; the launch traced here: 935 us
  starting transfers between devices  242 us (26%)
  waiting for transfers between devices  191 us (20%)
  other arithmetic  180 us (19%)
  matrix products  162 us (17%)
  local copies, waits for them, and re-layouts  155 us (16%)
    ppermute x15, starting transfers between devices, line_scatter(): up = lax.ppermute(for_up, 'dp', [(i, i + 1) for i in range(step)])  96.2 us
    ppermute x47, waiting for transfers between devices, swap(): return lax.ppermute(values, axis, SWAP)  95.7 us
    dot_general x8, matrix products, contract_last(): lax.dot_general(left_side, right_side, (((1,), (1,)), ((), ())), preferre...  64.7 us
    ppermute x15, waiting for transfers between devices, line_gather(): lax.ppermute(down[-1], 'dp', [(i + 1, i) for i in range(count - step)])  64.2 us
    ppermute x47, starting transfers between devices, swap(): return lax.ppermute(values, axis, SWAP)  52.9 us
    rev x4, local copies, waits for them, and re-layouts, flip_blocks(): return jnp.where(lax.axis_index('c') == 1, jnp.flip(values, 2), values)  41 us
    ppermute x15, starting transfers between devices, line_gather(): lax.ppermute(up[-1], 'dp', [(i, i + 1) for i in range(step - 1, count - 1)])  38.3 us
    dot_general x8, matrix products, project(): return jnp.dot(left_side, right_side, preferred_element_type=F32)  34.8 us
  transfers between devices with their start and end apart: 112, of which 37 were waited for; matrix products, arithmetic and copies ran while one was open for 32% of the time, Pallas kernels for 0%

profile of v1, /device:TPU:0, one launch (start us, length us, event | category | flops | bytes accessed | tf_op | source)
XLA Modules:
  0.0 934.9 jit_solution(6238759378483263073)
XLA Ops:
  11.1 10.9 %collective-permute-done = bf16[256,1536]{1,0:T(8,128)(2,1)S(1)} collective-permute-done((bf16[256,1536]{1,0:T(8,128)(2,1)}, bf16[256,1536]{1,0:T(8,128)(2,1)S(1)}, u32[]{:S(2)}, u32[]{:S(2)}) %collective-permute-start) | collective-permute-done | bytes 786464 | tf_op jit(solution)/shard_map/ppermute | solution.py:162
  28.5 5.1 collective-permute-done.2
  44.2 5.2 collective-permute-start.11
  55.4 5.9 collective-permute-start.5
  74.1 5.9 collective-permute-done.7
  95.7 7.2 maximum_convert_fusion
  102.9 8.5 fusion.1
  111.4 5.1 convolution_convert_fusion.6
  119.9 13.8 %rev.29 = bf16[2,2,2,1,256,320]{4,2,1,0,5,3:T(2,128)(2,1)S(1)} reverse(bf16[2,2,2,1,256,320]{4,2,1,0,5,3:T(2,128)(2,1)} %broadcast_select_fusion.1), dimensions={2} | reverse | bytes 2621440 | tf_op jit(solution)/shard_map/jit(_flip)/rev | solution.py:247
  136.7 4.7 reshape.730
  160.5 5.8 rev.31
  179.6 4.2 all-to-all-start.2
  184.6 8.7 all-to-all-done.2
  198.3 8.0 all-to-all-done.3
  215.4 5.4 collective-permute-start.27
  227.4 12.8 %collective-permute-done.50 = bf16[256,1536]{1,0:T(8,128)(2,1)} collective-permute-done((bf16[256,1536]{1,0:T(8,128)(2,1)}, bf16[256,1536]{1,0:T(8,128)(2,1)}, u32[]{:S(2)}, u32[]{:S(2)}) %collective-permute-start.50) | collective-permute-done | bytes 786464 | tf_op jit(solution)/shard_map/ppermute | solution.py:162
  256.4 4.3 collective-permute-start.33
  263.9 6.0 collective-permute-done.29
  273.5 10.1 %collective-permute-start.39 = (bf16[384,1056]{0,1:T(8,128)(2,1)S(1)}, bf16[384,1056]{0,1:T(8,128)(2,1)S(1)}, u32[]{:S(2)}, u32[]{:S(2)}) collective-permute-start(bf16[384,1056]{0,1:T(8,128)(2,1)S(1)} %copy-done.47), channel_id=1, source_target_pairs={{0,8},{8,16},{16,24},{1,9},{9,17},{17,25},{2,10},{10,18},{18,26},{... | collective-permute-start | bytes 2433032 | tf_op jit(solution)/shard_map/ppermute | solution.py:198
  283.6 18.3 %collective-permute-done.35 = bf16[384,768]{1,0:T(8,128)(2,1)S(1)} collective-permute-done((bf16[384,768]{1,0:T(8,128)(2,1)S(1)}, bf16[384,768]{1,0:T(8,128)(2,1)S(1)}, u32[]{:S(2)}, u32[]{:S(2)}) %collective-permute-start.35) | collective-permute-done | bytes 589856 | tf_op jit(solution)/shard_map/ppermute | solution.py:201
  305.5 9.1 collective-permute-done.30
  316.8 10.4 %collective-permute-done.36 = bf16[384,768]{1,0:T(8,128)(2,1)S(1)} collective-permute-done((bf16[384,768]{1,0:T(8,128)(2,1)S(1)}, bf16[384,768]{1,0:T(8,128)(2,1)S(1)}, u32[]{:S(2)}, u32[]{:S(2)}) %collective-permute-start.36) | collective-permute-done | bytes 589856 | tf_op jit(solution)/shard_map/ppermute | solution.py:201
  336.5 5.8 collective-permute-done.41
  371.2 5.6 multiply_convert_fusion
  379.6 4.9 fusion.79
  390.5 7.8 fusion.167
  406.7 6.4 fusion.171
  416.6 8.5 fusion.77
  428.6 6.5 fusion.81
  443.5 4.7 fusion.44
  448.2 6.3 fusion.28
  456.0 5.4 convolution_convert_fusion.2
  461.4 13.4 %add_convert_fusion = bf16[2048,1536]{1,0:T(8,128)(2,1)} fusion(f32[2048,1536]{1,0:T(8,128)} %fusion.81, f32[2048,1536]{1,0:T(8,128)} %fusion.77, bf16[1536,1056]{0,1:T(8,128)(2,1)S(1)} %copy-done.42, bf16[2048,352]{0,1:T(8,128)(2,1)} %copy-done.130, bf16[2048,352]{0,1:T(8,128)(2,1)} %copy-done.129), kind=kOutput, calls=%fused_computation.4 | convolution fusion | flops 4444389376 | bytes 36503552 | tf_op jit(solution)/shard_map/dot_general | solution.py:58
  478.7 13.2 %add_convert_fusion.1 = bf16[2048,1536]{1,0:T(8,128)(2,1)} fusion(f32[2048,1536]{1,0:T(8,128)} %fusion.171, f32[2048,1536]{1,0:T(8,128)} %fusion.167, bf16[2048,352]{0,1:T(8,128)(2,1)S(1)} %copy-done.63, bf16[1536,1056]{0,1:T(8,128)(2,1)S(1)} %copy-done.42), kind=kOutput, calls=%fused_computation.5 | convolution fusion | flops 2224029696 | bytes 33980416 | tf_op jit(solution)/shard_map/dot_general | solution.py:58
  491.9 6.4 convolution_convert_fusion.5
  520.2 7.3 collective-permute-done.98
  531.2 29.8 %collective-permute-start.93 = (bf16[384,768]{1,0:T(8,128)(2,1)}, bf16[384,768]{1,0:T(8,128)(2,1)}, u32[]{:S(2)}, u32[]{:S(2)}) collective-permute-start(bf16[384,768]{1,0:T(8,128)(2,1)} %get-tuple-element.290), channel_id=1, source_target_pairs={{0,8},{8,16},{1,9},{9,17},{2,10},{10,18},{3,11},{11,19},{4,12},{12... | collective-permute-start | bytes 1769480 | tf_op jit(solution)/shard_map/ppermute | solution.py:228
  570.9 4.1 convert_add_fusion.1
  576.8 4.1 convert_add_fusion.2
  588.2 4.7 collective-permute-done.46
  602.4 11.1 %collective-permute-done.57 = bf16[256,1536]{1,0:T(8,128)(2,1)S(1)} collective-permute-done((bf16[256,1536]{1,0:T(8,128)(2,1)S(1)}, bf16[256,1536]{1,0:T(8,128)(2,1)S(1)}, u32[]{:S(2)}, u32[]{:S(2)}) %collective-permute-start.57) | collective-permute-done | bytes 786464 | tf_op jit(solution)/shard_map/ppermute | solution.py:162
  616.7 11.5 %collective-permute-start.99 = (bf16[384,1056]{0,1:T(8,128)(2,1)S(1)}, bf16[384,1056]{0,1:T(8,128)(2,1)S(1)}, u32[]{:S(2)}, u32[]{:S(2)}) collective-permute-start(bf16[384,1056]{0,1:T(8,128)(2,1)S(1)} %copy-done.72), channel_id=1, source_target_pairs={{0,8},{8,16},{1,9},{9,17},{2,10},{10,18},{3,11},{11,19},{4,12},{12... | collective-permute-start | bytes 2433032 | tf_op jit(solution)/shard_map/ppermute | solution.py:228
  630.5 10.4 %collective-permute-start.88 = (bf16[384,768]{1,0:T(8,128)(2,1)}, bf16[384,768]{1,0:T(8,128)(2,1)}, u32[]{:S(2)}, u32[]{:S(2)}) collective-permute-start(bf16[384,768]{1,0:T(8,128)(2,1)} %get-tuple-element.282), channel_id=1, source_target_pairs={{0,8},{8,16},{16,24},{1,9},{9,17},{17,25},{2,10},{10,18},{18,26},{... | collective-permute-start | bytes 1769480 | tf_op jit(solution)/shard_map/ppermute | solution.py:228
  654.2 7.6 collective-permute-start.94
  674.2 5.5 collective-permute-start.100
  686.7 5.6 collective-permute-done.62
  695.4 4.2 fusion.241
  715.0 7.5 collective-permute-done.106
  738.8 7.7 rev.33
  767.4 5.2 collective-permute-start.79
  774.0 4.8 fusion.5
  778.8 4.7 fusion.7
  784.9 4.9 fusion.2
  789.7 4.5 fusion.4
  809.0 4.9 maximum_bitcast_fusion
  817.2 13.8 %rev.35 = bf16[2,2,2,1,256,320]{4,2,1,0,5,3:T(2,128)(2,1)S(1)} reverse(bf16[2,2,2,1,256,320]{4,2,1,0,5,3:T(2,128)(2,1)} %broadcast_select_fusion), dimensions={2} | reverse | bytes 2621440 | tf_op jit(solution)/shard_map/jit(_flip)/rev | solution.py:247
  837.6 5.5 convolution_convert_fusion
  843.1 5.0 multiply_reduce_fusion.1
  865.5 4.7 collective-permute-start.81
  871.9 6.5 collective-permute-start.72
  883.6 4.1 collective-permute-done.75
  895.3 6.7 convert_add_fusion
  905.5 4.5 collective-permute-done.66
  919.7 8.9 collective-permute-done.67
  (758 shorter events, 450.7 us)
Async XLA Ops:
  0.7 21.3 %collective-permute-start = (bf16[256,1536]{1,0:T(8,128)(2,1)}, bf16[256,1536]{1,0:T(8,128)(2,1)S(1)}, u32[]{:S(2)}, u32[]{:S(2)}) collective-permute-start(bf16[256,1536]{1,0:T(8,128)(2,1)} %bitcast.589), channel_id=1, source_target_pairs={{0,2},{2,0},{1,3},{3,1},{4,6},{6,4},{5,7},{7,5},{8,10},{10,8},{9,1... | collective-permute-start | bytes 2359304 | tf_op jit(solution)/shard_map/ppermute | solution.py:162
  3.7 20.7 %collective-permute-start.1 = (bf16[256,1536]{1,0:T(8,128)(2,1)}, bf16[256,1536]{1,0:T(8,128)(2,1)S(1)}, u32[]{:S(2)}, u32[]{:S(2)}) collective-permute-start(bf16[256,1536]{1,0:T(8,128)(2,1)} %bitcast.590), channel_id=1, source_target_pairs={{0,4},{4,0},{1,5},{5,1},{2,6},{6,2},{3,7},{7,3},{8,12},{12,8},{9,1... | collective-permute-start | bytes 2359304 | tf_op jit(solution)/shard_map/ppermute | solution.py:162
  7.1 30.9 %all-to-all-start.1 = ((bf16[8,48,192]{2,1,0:T(8,128)(2,1)}), bf16[8,48,192]{2,1,0:T(8,128)(2,1)S(1)}, u32[]{:S(2)}, u32[]{:S(2)}) async-start(bf16[8,48,192]{2,1,0:T(8,128)(2,1)} %bitcast.55), calls=%async_computation.1 | async-start | bytes 393216 | tf_op jit(solution)/shard_map/all_to_all | solution.py:241
  37.9 54.3 %collective-permute-start.4 = (bf16[4,256,1536]{2,1,0:T(8,128)(2,1)}, bf16[4,256,1536]{2,1,0:T(8,128)(2,1)}, u32[]{:S(2)}, u32[]{:S(2)}) collective-permute-start(bf16[4,256,1536]{2,1,0:T(8,128)(2,1)} %get-tuple-element.281), channel_id=1, source_target_pairs={{0,1},{1,0},{2,3},{3,2},{4,5},{5,4},{6,7},{7,6},{8,9},{9,8},{10,11... | collective-permute-start | bytes 9437192 | tf_op jit(solution)/shard_map/ppermute | solution.py:162
  44.2 17.9 %collective-permute-start.11 = (bf16[384,192]{1,0:T(8,128)(2,1)}, bf16[384,192]{1,0:T(8,128)(2,1)}, u32[]{:S(2)}, u32[]{:S(2)}) collective-permute-start(bf16[384,192]{1,0:T(8,128)(2,1)} %bitcast.657), channel_id=1, source_target_pairs={{0,8},{8,16},{16,24},{1,9},{9,17},{17,25},{2,10},{10,18},{18,26},{... | collective-permute-start | bytes 442376 | tf_op jit(solution)/shard_map/ppermute | solution.py:198
  50.3 19.1 %collective-permute-start.6 = (bf16[384,384]{0,1:T(8,128)(2,1)}, bf16[384,384]{0,1:T(8,128)(2,1)}, u32[]{:S(2)}, u32[]{:S(2)}) collective-permute-start(bf16[384,384]{0,1:T(8,128)(2,1)} %copy.295), channel_id=1, source_target_pairs={{8,0},{16,8},{24,16},{9,1},{17,9},{25,17},{10,2},{18,10},{26,18},{... | collective-permute-start | bytes 884744 | tf_op jit(solution)/shard_map/ppermute | solution.py:201
  55.4 16.1 %collective-permute-start.5 = (bf16[384,384]{0,1:T(8,128)(2,1)}, bf16[384,384]{0,1:T(8,128)(2,1)}, u32[]{:S(2)}, u32[]{:S(2)}) collective-permute-start(bf16[384,384]{0,1:T(8,128)(2,1)} %copy.295), channel_id=1, source_target_pairs={{0,8},{8,16},{16,24},{1,9},{9,17},{17,25},{2,10},{10,18},{18,26},{... | collective-permute-start | bytes 884744 | tf_op jit(solution)/shard_map/ppermute | solution.py:198
  175.0 70.8 %collective-permute-start.17 = (bf16[2,2,256,1536]{3,2,1,0:T(8,128)(2,1)}, bf16[2,2,256,1536]{3,2,1,0:T(8,128)(2,1)}, u32[]{:S(2)}, u32[]{:S(2)}) collective-permute-start(bf16[2,2,256,1536]{3,2,1,0:T(8,128)(2,1)} %slice_bitcast_fusion.6), channel_id=1, source_target_pairs={{0,1},{1,0},{2,3},{3,2},{4,5},{5,4},{6,7},{7,6},{8,9},{9,8},{10,11... | collective-permute-start | bytes 9437192 | tf_op jit(solution)/shard_map/ppermute | solution.py:162
  207.1 17.5 %all-to-all-start.4 = ((bf16[8,48,1056]{2,1,0:T(8,128)(2,1)}), bf16[8,48,1056]{2,1,0:T(8,128)(2,1)S(1)}, u32[]{:S(2)}, u32[]{:S(2)}) async-start(bf16[8,48,1056]{2,1,0:T(8,128)(2,1)} %concatenate.194), calls=%async_computation.4 | async-start | bytes 1769472 | tf_op jit(solution)/shard_map/all_to_all | solution.py:241
  210.7 29.6 %collective-permute-start.50 = (bf16[256,1536]{1,0:T(8,128)(2,1)}, bf16[256,1536]{1,0:T(8,128)(2,1)}, u32[]{:S(2)}, u32[]{:S(2)}) collective-permute-start(bf16[256,1536]{1,0:T(8,128)(2,1)} %bitcast.94), channel_id=1, source_target_pairs={{0,2},{2,0},{1,3},{3,1},{4,6},{6,4},{5,7},{7,5},{8,10},{10,8},{9,1... | collective-permute-start | bytes 2359304 | tf_op jit(solution)/shard_map/ppermute | solution.py:162
  212.6 30.0 %collective-permute-start.51 = (bf16[256,1536]{1,0:T(8,128)(2,1)}, bf16[256,1536]{1,0:T(8,128)(2,1)}, u32[]{:S(2)}, u32[]{:S(2)}) collective-permute-start(bf16[256,1536]{1,0:T(8,128)(2,1)} %bitcast.94), channel_id=1, source_target_pairs={{0,4},{4,0},{1,5},{5,1},{2,6},{6,2},{3,7},{7,3},{8,12},{12,8},{9,1... | collective-permute-start | bytes 2359304 | tf_op jit(solution)/shard_map/ppermute | solution.py:162
  214.1 31.1 %collective-permute-start.28 = (bf16[384,768]{1,0:T(8,128)(2,1)}, bf16[384,768]{1,0:T(8,128)(2,1)}, u32[]{:S(2)}, u32[]{:S(2)}) collective-permute-start(bf16[384,768]{1,0:T(8,128)(2,1)} %bitcast.80), channel_id=1, source_target_pairs={{8,0},{16,8},{24,16},{9,1},{17,9},{25,17},{10,2},{18,10},{26,18},{... | collective-permute-start | bytes 1769480 | tf_op jit(solution)/shard_map/ppermute | solution.py:201
  215.4 41.0 %collective-permute-start.27 = (bf16[384,768]{1,0:T(8,128)(2,1)}, bf16[384,768]{1,0:T(8,128)(2,1)}, u32[]{:S(2)}, u32[]{:S(2)}) collective-permute-start(bf16[384,768]{1,0:T(8,128)(2,1)} %bitcast.80), channel_id=1, source_target_pairs={{0,8},{8,16},{16,24},{1,9},{9,17},{17,25},{2,10},{10,18},{18,26},{... | collective-permute-start | bytes 1769480 | tf_op jit(solution)/shard_map/ppermute | solution.py:198
  240.2 22.4 %collective-permute-start.34 = (bf16[384,768]{1,0:T(8,128)(2,1)S(1)}, bf16[384,768]{1,0:T(8,128)(2,1)S(1)}, u32[]{:S(2)}, u32[]{:S(2)}) collective-permute-start(bf16[384,768]{1,0:T(8,128)(2,1)S(1)} %bitcast.647), channel_id=1, source_target_pairs={{8,0},{16,8},{24,16},{9,1},{17,9},{25,17},{10,2},{18,10},{26,18},{... | collective-permute-start | bytes 1769480 | tf_op jit(solution)/shard_map/ppermute | solution.py:201
  245.8 24.2 %collective-permute-start.29 = (bf16[384,768]{1,0:T(8,128)(2,1)}, bf16[384,768]{1,0:T(8,128)(2,1)S(1)}, u32[]{:S(2)}, u32[]{:S(2)}) collective-permute-start(bf16[384,768]{1,0:T(8,128)(2,1)} %collective-permute-done.28), channel_id=1, source_target_pairs={{8,0},{16,8},{9,1},{17,9},{10,2},{18,10},{11,3},{19,11},{12,4},{20... | collective-permute-start | bytes 1769480 | tf_op jit(solution)/shard_map/ppermute | solution.py:201
  253.3 17.4 %collective-permute-start.18 = (bf16[128,1536]{1,0:T(8,128)(2,1)S(1)}, bf16[128,1536]{1,0:T(8,128)(2,1)S(1)}, u32[]{:S(2)}, u32[]{:S(2)}) collective-permute-start(bf16[128,1536]{1,0:T(8,128)(2,1)S(1)} %get-tuple-element.276), channel_id=1, source_target_pairs={{0,4},{4,0},{1,5},{5,1},{2,6},{6,2},{3,7},{7,3},{8,12},{12,8},{9,1... | collective-permute-start | bytes 1179656 | tf_op jit(solution)/shard_map/ppermute | solution.py:162
  255.6 16.3 %collective-permute-start.20 = (bf16[128,1536]{1,0:T(8,128)(2,1)S(1)}, bf16[128,1536]{1,0:T(8,128)(2,1)S(1)}, u32[]{:S(2)}, u32[]{:S(2)}) collective-permute-start(bf16[128,1536]{1,0:T(8,128)(2,1)S(1)} %get-tuple-element.277), channel_id=1, source_target_pairs={{0,2},{2,0},{1,3},{3,1},{4,6},{6,4},{5,7},{7,5},{8,10},{10,8},{9,1... | collective-permute-start | bytes 1179656 | tf_op jit(solution)/shard_map/ppermute | solution.py:162
  256.4 17.1 %collective-permute-start.33 = (bf16[384,768]{1,0:T(8,128)(2,1)S(1)}, bf16[384,768]{1,0:T(8,128)(2,1)S(1)}, u32[]{:S(2)}, u32[]{:S(2)}) collective-permute-start(bf16[384,768]{1,0:T(8,128)(2,1)S(1)} %bitcast.648), channel_id=1, source_target_pairs={{0,8},{8,16},{16,24},{1,9},{9,17},{17,25},{2,10},{10,18},{18,26},{... | collective-permute-start | bytes 1769480 | tf_op jit(solution)/shard_map/ppermute | solution.py:198
  262.6 40.7 %collective-permute-start.40 = (bf16[384,1056]{0,1:T(8,128)(2,1)S(1)}, bf16[384,1056]{0,1:T(8,128)(2,1)S(1)}, u32[]{:S(2)}, u32[]{:S(2)}) collective-permute-start(bf16[384,1056]{0,1:T(8,128)(2,1)S(1)} %copy-done.47), channel_id=1, source_target_pairs={{8,0},{16,8},{24,16},{9,1},{17,9},{25,17},{10,2},{18,10},{26,18},{... | collective-permute-start | bytes 2433032 | tf_op jit(solution)/shard_map/ppermute | solution.py:201
  270.0 34.2 %collective-permute-start.31 = (bf16[384,768]{1,0:T(8,128)(2,1)}, bf16[384,768]{1,0:T(8,128)(2,1)S(1)}, u32[]{:S(2)}, u32[]{:S(2)}) collective-permute-start(bf16[384,768]{1,0:T(8,128)(2,1)} %collective-permute-done.27), channel_id=1, source_target_pairs={{8,16},{16,24},{9,17},{17,25},{10,18},{18,26},{11,19},{19,27},{12,... | collective-permute-start | bytes 1769480 | tf_op jit(solution)/shard_map/ppermute | solution.py:198
  270.7 31.3 %collective-permute-start.35 = (bf16[384,768]{1,0:T(8,128)(2,1)S(1)}, bf16[384,768]{1,0:T(8,128)(2,1)S(1)}, u32[]{:S(2)}, u32[]{:S(2)}) collective-permute-start(bf16[384,768]{1,0:T(8,128)(2,1)S(1)} %collective-permute-done.34), channel_id=1, source_target_pairs={{8,0},{16,8},{9,1},{17,9},{10,2},{18,10},{11,3},{19,11},{12,4},{20... | collective-permute-start | bytes 1769480 | tf_op jit(solution)/shard_map/ppermute | solution.py:201
  272.0 42.6 %collective-permute-start.30 = (bf16[384,768]{1,0:T(8,128)(2,1)S(1)}, bf16[384,768]{1,0:T(8,128)(2,1)S(1)}, u32[]{:S(2)}, u32[]{:S(2)}) collective-permute-start(bf16[384,768]{1,0:T(8,128)(2,1)S(1)} %collective-permute-done.29), channel_id=1, source_target_pairs={{8,0},{9,1},{10,2},{11,3},{12,4},{13,5},{14,6},{15,7}} | collective-permute-start | bytes 1769480 | tf_op jit(solution)/shard_map/ppermute | solution.py:201
  273.5 42.0 %collective-permute-start.39 = (bf16[384,1056]{0,1:T(8,128)(2,1)S(1)}, bf16[384,1056]{0,1:T(8,128)(2,1)S(1)}, u32[]{:S(2)}, u32[]{:S(2)}) collective-permute-start(bf16[384,1056]{0,1:T(8,128)(2,1)S(1)} %copy-done.47), channel_id=1, source_target_pairs={{0,8},{8,16},{16,24},{1,9},{9,17},{17,25},{2,10},{10,18},{18,26},{... | collective-permute-start | bytes 2433032 | tf_op jit(solution)/shard_map/ppermute | solution.py:198
  301.9 25.3 %collective-permute-start.36 = (bf16[384,768]{1,0:T(8,128)(2,1)S(1)}, bf16[384,768]{1,0:T(8,128)(2,1)S(1)}, u32[]{:S(2)}, u32[]{:S(2)}) collective-permute-start(bf16[384,768]{1,0:T(8,128)(2,1)S(1)} %collective-permute-done.35), channel_id=1, source_target_pairs={{8,0},{9,1},{10,2},{11,3},{12,4},{13,5},{14,6},{15,7}} | collective-permute-start | bytes 1769480 | tf_op jit(solution)/shard_map/ppermute | solution.py:201
  303.3 25.6 %collective-permute-start.37 = (bf16[384,768]{1,0:T(8,128)(2,1)S(1)}, bf16[384,768]{1,0:T(8,128)(2,1)S(1)}, u32[]{:S(2)}, u32[]{:S(2)}) collective-permute-start(bf16[384,768]{1,0:T(8,128)(2,1)S(1)} %collective-permute-done.33), channel_id=1, source_target_pairs={{8,16},{16,24},{9,17},{17,25},{10,18},{18,26},{11,19},{19,27},{12,... | collective-permute-start | bytes 1769480 | tf_op jit(solution)/shard_map/ppermute | solution.py:198
  304.2 25.5 %collective-permute-start.19 = (bf16[256,1536]{1,0:T(8,128)(2,1)S(1)}, bf16[256,1536]{1,0:T(8,128)(2,1)S(1)}, u32[]{:S(2)}, u32[]{:S(2)}) collective-permute-start(bf16[256,1536]{1,0:T(8,128)(2,1)S(1)} %pad_maximum_fusion.19), channel_id=1, source_target_pairs={{0,2},{2,0},{1,3},{3,1},{4,6},{6,4},{5,7},{7,5},{8,10},{10,8},{9,1... | collective-permute-start | bytes 2359304 | tf_op jit(solution)/shard_map/ppermute | solution.py:162
  314.6 15.8 %collective-permute-start.21 = (bf16[256,1536]{1,0:T(8,128)(2,1)S(1)}, bf16[256,1536]{1,0:T(8,128)(2,1)S(1)}, u32[]{:S(2)}, u32[]{:S(2)}) collective-permute-start(bf16[256,1536]{1,0:T(8,128)(2,1)S(1)} %pad_maximum_fusion.20), channel_id=1, source_target_pairs={{0,4},{4,0},{1,5},{5,1},{2,6},{6,2},{3,7},{7,3},{8,12},{12,8},{9,1... | collective-permute-start | bytes 2359304 | tf_op jit(solution)/shard_map/ppermute | solution.py:162
  315.5 26.8 %collective-permute-start.41 = (bf16[384,1056]{0,1:T(8,128)(2,1)S(1)}, bf16[384,1056]{0,1:T(8,128)(2,1)S(1)}, u32[]{:S(2)}, u32[]{:S(2)}) collective-permute-start(bf16[384,1056]{0,1:T(8,128)(2,1)S(1)} %collective-permute-done.40), channel_id=1, source_target_pairs={{8,0},{16,8},{9,1},{17,9},{10,2},{18,10},{11,3},{19,11},{12,4},{20... | collective-permute-start | bytes 2433032 | tf_op jit(solution)/shard_map/ppermute | solution.py:201
  327.2 16.4 %collective-permute-start.43 = (bf16[384,1056]{0,1:T(8,128)(2,1)S(1)}, bf16[384,1056]{0,1:T(8,128)(2,1)S(1)}, u32[]{:S(2)}, u32[]{:S(2)}) collective-permute-start(bf16[384,1056]{0,1:T(8,128)(2,1)S(1)} %collective-permute-done.39), channel_id=1, source_target_pairs={{8,16},{16,24},{9,17},{17,25},{10,18},{18,26},{11,19},{19,27},{12,... | collective-permute-start | bytes 2433032 | tf_op jit(solution)/shard_map/ppermute | solution.py:198
  331.2 15.2 %collective-permute-start.22 = (bf16[256,1536]{1,0:T(8,128)(2,1)S(1)}, bf16[256,1536]{1,0:T(8,128)(2,1)S(1)}, u32[]{:S(2)}, u32[]{:S(2)}) collective-permute-start(bf16[256,1536]{1,0:T(8,128)(2,1)S(1)} %multiply_convert_fusion.7), channel_id=1, source_target_pairs={{0,2},{2,0},{1,3},{3,1},{4,6},{6,4},{5,7},{7,5},{8,10},{10,8},{9,1... | collective-permute-start | bytes 2359304 | tf_op jit(solution)/shard_map/ppermute | solution.py:162
  332.5 17.7 %collective-permute-start.23 = (bf16[256,1536]{1,0:T(8,128)(2,1)S(1)}, bf16[256,1536]{1,0:T(8,128)(2,1)S(1)}, u32[]{:S(2)}, u32[]{:S(2)}) collective-permute-start(bf16[256,1536]{1,0:T(8,128)(2,1)S(1)} %multiply_convert_fusion.7), channel_id=1, source_target_pairs={{0,4},{4,0},{1,5},{5,1},{2,6},{6,2},{3,7},{7,3},{8,12},{12,8},{9,1... | collective-permute-start | bytes 2359304 | tf_op jit(solution)/shard_map/ppermute | solution.py:162
  334.1 28.7 %collective-permute-start.54 = (bf16[4,256,1536]{2,1,0:T(8,128)(2,1)S(1)}, bf16[4,256,1536]{2,1,0:T(8,128)(2,1)S(1)}, u32[]{:S(2)}, u32[]{:S(2)}) collective-permute-start(bf16[4,256,1536]{2,1,0:T(8,128)(2,1)S(1)} %get-tuple-element.265), channel_id=1, source_target_pairs={{0,1},{1,0},{2,3},{3,2},{4,5},{5,4},{6,7},{7,6},{8,9},{9,8},{10,11... | collective-permute-start | bytes 9437192 | tf_op jit(solution)/shard_map/ppermute | solution.py:162
  342.3 19.7 %collective-permute-start.42 = (bf16[384,1056]{0,1:T(8,128)(2,1)S(1)}, bf16[384,1056]{0,1:T(8,128)(2,1)S(1)}, u32[]{:S(2)}, u32[]{:S(2)}) collective-permute-start(bf16[384,1056]{0,1:T(8,128)(2,1)S(1)} %collective-permute-done.41), channel_id=1, source_target_pairs={{8,0},{9,1},{10,2},{11,3},{12,4},{13,5},{14,6},{15,7}} | collective-permute-start | bytes 2433032 | tf_op jit(solution)/shard_map/ppermute | solution.py:201
  343.6 18.9 %collective-permute-start.44 = (bf16[384,1056]{0,1:T(8,128)(2,1)S(1)}, bf16[384,1056]{0,1:T(8,128)(2,1)S(1)}, u32[]{:S(2)}, u32[]{:S(2)}) collective-permute-start(bf16[384,1056]{0,1:T(8,128)(2,1)S(1)} %collective-permute-done.43), channel_id=1, source_target_pairs={{16,24},{17,25},{18,26},{19,27},{20,28},{21,29},{22,30},{23,31}} | collective-permute-start | bytes 2433032 | tf_op jit(solution)/shard_map/ppermute | solution.py:198
  360.5 16.3 %collective-permute-start.26 = (bf16[4,256,1536]{2,1,0:T(8,128)(2,1)}, bf16[4,256,1536]{2,1,0:T(8,128)(2,1)}, u32[]{:S(2)}, u32[]{:S(2)}) collective-permute-start(bf16[4,256,1536]{2,1,0:T(8,128)(2,1)} %get-tuple-element.273), channel_id=1, source_target_pairs={{0,1},{1,0},{2,3},{3,2},{4,5},{5,4},{6,7},{7,6},{8,9},{9,8},{10,11... | collective-permute-start | bytes 9437192 | tf_op jit(solution)/shard_map/ppermute | solution.py:162
  436.3 70.5 %collective-permute-start.86 = (bf16[384,768]{1,0:T(8,128)(2,1)}, bf16[384,768]{1,0:T(8,128)(2,1)}, u32[]{:S(2)}, u32[]{:S(2)}) collective-permute-start(bf16[384,768]{1,0:T(8,128)(2,1)} %get-tuple-element.286), channel_id=1, source_target_pairs={{0,8},{1,9},{2,10},{3,11},{4,12},{5,13},{6,14},{7,15}} | collective-permute-start | bytes 1769480 | tf_op jit(solution)/shard_map/ppermute | solution.py:228
  438.8 68.7 %collective-permute-start.89 = (bf16[384,768]{1,0:T(8,128)(2,1)}, bf16[384,768]{1,0:T(8,128)(2,1)}, u32[]{:S(2)}, u32[]{:S(2)}) collective-permute-start(bf16[384,768]{1,0:T(8,128)(2,1)} %get-tuple-element.287), channel_id=1, source_target_pairs={{24,16},{25,17},{26,18},{27,19},{28,20},{29,21},{30,22},{31,23}} | collective-permute-start | bytes 1769480 | tf_op jit(solution)/shard_map/ppermute | solution.py:229
  441.4 68.3 %collective-permute-start.92 = (bf16[384,768]{1,0:T(8,128)(2,1)}, bf16[384,768]{1,0:T(8,128)(2,1)}, u32[]{:S(2)}, u32[]{:S(2)}) collective-permute-start(bf16[384,768]{1,0:T(8,128)(2,1)} %get-tuple-element.292), channel_id=1, source_target_pairs={{0,8},{1,9},{2,10},{3,11},{4,12},{5,13},{6,14},{7,15}} | collective-permute-start | bytes 1769480 | tf_op jit(solution)/shard_map/ppermute | solution.py:228
  478.7 92.2 %collective-permute-start.55 = (bf16[2,2,256,1536]{3,2,1,0:T(8,128)(2,1)}, bf16[2,2,256,1536]{3,2,1,0:T(8,128)(2,1)}, u32[]{:S(2)}, u32[]{:S(2)}) collective-permute-start(bf16[2,2,256,1536]{3,2,1,0:T(8,128)(2,1)} %slice_bitcast_fusion.2), channel_id=1, source_target_pairs={{0,1},{1,0},{2,3},{3,2},{4,5},{5,4},{6,7},{7,6},{8,9},{9,8},{10,11... | collective-permute-start | bytes 9437192 | tf_op jit(solution)/shard_map/ppermute | solution.py:162
  500.2 75.4 %collective-permute-start.45 = (bf16[2,2,256,1536]{3,2,1,0:T(8,128)(2,1)}, bf16[2,2,256,1536]{3,2,1,0:T(8,128)(2,1)}, u32[]{:S(2)}, u32[]{:S(2)}) collective-permute-start(bf16[2,2,256,1536]{3,2,1,0:T(8,128)(2,1)} %slice_bitcast_fusion.4), channel_id=1, source_target_pairs={{0,1},{1,0},{2,3},{3,2},{4,5},{5,4},{6,7},{7,6},{8,9},{9,8},{10,11... | collective-permute-start | bytes 9437192 | tf_op jit(solution)/shard_map/ppermute | solution.py:162
  507.5 20.0 %collective-permute-start.98 = (bf16[384,1056]{0,1:T(8,128)(2,1)}, bf16[384,1056]{0,1:T(8,128)(2,1)}, u32[]{:S(2)}, u32[]{:S(2)}) collective-permute-start(bf16[384,1056]{0,1:T(8,128)(2,1)} %copy.348), channel_id=1, source_target_pairs={{0,8},{1,9},{2,10},{3,11},{4,12},{5,13},{6,14},{7,15}} | collective-permute-start | bytes 2433032 | tf_op jit(solution)/shard_map/ppermute | solution.py:228
  509.7 21.5 %collective-permute-start.101 = (bf16[384,1056]{0,1:T(8,128)(2,1)}, bf16[384,1056]{0,1:T(8,128)(2,1)}, u32[]{:S(2)}, u32[]{:S(2)}) collective-permute-start(bf16[384,1056]{0,1:T(8,128)(2,1)} %copy.354), channel_id=1, source_target_pairs={{24,16},{25,17},{26,18},{27,19},{28,20},{29,21},{30,22},{31,23}} | collective-permute-start | bytes 2433032 | tf_op jit(solution)/shard_map/ppermute | solution.py:229
  515.6 83.0 %collective-permute-start.87 = (bf16[384,768]{1,0:T(8,128)(2,1)}, bf16[384,768]{1,0:T(8,128)(2,1)}, u32[]{:S(2)}, u32[]{:S(2)}) collective-permute-start(bf16[384,768]{1,0:T(8,128)(2,1)} %get-tuple-element.284), channel_id=1, source_target_pairs={{0,8},{8,16},{1,9},{9,17},{2,10},{10,18},{3,11},{11,19},{4,12},{12... | collective-permute-start | bytes 1769480 | tf_op jit(solution)/shard_map/ppermute | solution.py:228
  527.5 72.3 %collective-permute-start.90 = (bf16[384,768]{1,0:T(8,128)(2,1)}, bf16[384,768]{1,0:T(8,128)(2,1)}, u32[]{:S(2)}, u32[]{:S(2)}) collective-permute-start(bf16[384,768]{1,0:T(8,128)(2,1)} %get-tuple-element.285), channel_id=1, source_target_pairs={{16,8},{24,16},{17,9},{25,17},{18,10},{26,18},{19,11},{27,19},{20,... | collective-permute-start | bytes 1769480 | tf_op jit(solution)/shard_map/ppermute | solution.py:229
  531.2 113.5 %collective-permute-start.93 = (bf16[384,768]{1,0:T(8,128)(2,1)}, bf16[384,768]{1,0:T(8,128)(2,1)}, u32[]{:S(2)}, u32[]{:S(2)}) collective-permute-start(bf16[384,768]{1,0:T(8,128)(2,1)} %get-tuple-element.290), channel_id=1, source_target_pairs={{0,8},{8,16},{1,9},{9,17},{2,10},{10,18},{3,11},{11,19},{4,12},{12... | collective-permute-start | bytes 1769480 | tf_op jit(solution)/shard_map/ppermute | solution.py:228
  593.0 20.5 %collective-permute-start.57 = (bf16[256,1536]{1,0:T(8,128)(2,1)S(1)}, bf16[256,1536]{1,0:T(8,128)(2,1)S(1)}, u32[]{:S(2)}, u32[]{:S(2)}) collective-permute-start(bf16[256,1536]{1,0:T(8,128)(2,1)S(1)} %pad_maximum_fusion.23), channel_id=1, source_target_pairs={{0,2},{2,0},{1,3},{3,1},{4,6},{6,4},{5,7},{7,5},{8,10},{10,8},{9,1... | collective-permute-start | bytes 2359304 | tf_op jit(solution)/shard_map/ppermute | solution.py:162
  595.5 21.2 %collective-permute-start.59 = (bf16[256,1536]{1,0:T(8,128)(2,1)S(1)}, bf16[256,1536]{1,0:T(8,128)(2,1)S(1)}, u32[]{:S(2)}, u32[]{:S(2)}) collective-permute-start(bf16[256,1536]{1,0:T(8,128)(2,1)S(1)} %pad_maximum_fusion.24), channel_id=1, source_target_pairs={{0,4},{4,0},{1,5},{5,1},{2,6},{6,2},{3,7},{7,3},{8,12},{12,8},{9,1... | collective-permute-start | bytes 2359304 | tf_op jit(solution)/shard_map/ppermute | solution.py:162
  598.7 30.3 %collective-permute-start.47 = (bf16[256,1536]{1,0:T(8,128)(2,1)S(1)}, bf16[256,1536]{1,0:T(8,128)(2,1)S(1)}, u32[]{:S(2)}, u32[]{:S(2)}) collective-permute-start(bf16[256,1536]{1,0:T(8,128)(2,1)S(1)} %pad_maximum_fusion.21), channel_id=1, source_target_pairs={{0,2},{2,0},{1,3},{3,1},{4,6},{6,4},{5,7},{7,5},{8,10},{10,8},{9,1... | collective-permute-start | bytes 2359304 | tf_op jit(solution)/shard_map/ppermute | solution.py:162
  599.8 30.8 %collective-permute-start.49 = (bf16[256,1536]{1,0:T(8,128)(2,1)S(1)}, bf16[256,1536]{1,0:T(8,128)(2,1)S(1)}, u32[]{:S(2)}, u32[]{:S(2)}) collective-permute-start(bf16[256,1536]{1,0:T(8,128)(2,1)S(1)} %pad_maximum_fusion.22), channel_id=1, source_target_pairs={{0,4},{4,0},{1,5},{5,1},{2,6},{6,2},{3,7},{7,3},{8,12},{12,8},{9,1... | collective-permute-start | bytes 2359304 | tf_op jit(solution)/shard_map/ppermute | solution.py:162
  613.4 32.4 %collective-permute-start.96 = (bf16[384,768]{1,0:T(8,128)(2,1)S(1)}, bf16[384,768]{1,0:T(8,128)(2,1)S(1)}, u32[]{:S(2)}, u32[]{:S(2)}) collective-permute-start(bf16[384,768]{1,0:T(8,128)(2,1)S(1)} %copy-done.87), channel_id=1, source_target_pairs={{16,8},{24,16},{17,9},{25,17},{18,10},{26,18},{19,11},{27,19},{20,... | collective-permute-start | bytes 1769480 | tf_op jit(solution)/shard_map/ppermute | solution.py:229
  616.7 33.1 %collective-permute-start.99 = (bf16[384,1056]{0,1:T(8,128)(2,1)S(1)}, bf16[384,1056]{0,1:T(8,128)(2,1)S(1)}, u32[]{:S(2)}, u32[]{:S(2)}) collective-permute-start(bf16[384,1056]{0,1:T(8,128)(2,1)S(1)} %copy-done.72), channel_id=1, source_target_pairs={{0,8},{8,16},{1,9},{9,17},{2,10},{10,18},{3,11},{11,19},{4,12},{12... | collective-permute-start | bytes 2433032 | tf_op jit(solution)/shard_map/ppermute | solution.py:228
  629.0 25.3 %collective-permute-start.102 = (bf16[384,1056]{0,1:T(8,128)(2,1)}, bf16[384,1056]{0,1:T(8,128)(2,1)}, u32[]{:S(2)}, u32[]{:S(2)}) collective-permute-start(bf16[384,1056]{0,1:T(8,128)(2,1)} %copy.356), channel_id=1, source_target_pairs={{16,8},{24,16},{17,9},{25,17},{18,10},{26,18},{19,11},{27,19},{20,... | collective-permute-start | bytes 2433032 | tf_op jit(solution)/shard_map/ppermute | solution.py:229
  630.5 50.2 %collective-permute-start.88 = (bf16[384,768]{1,0:T(8,128)(2,1)}, bf16[384,768]{1,0:T(8,128)(2,1)}, u32[]{:S(2)}, u32[]{:S(2)}) collective-permute-start(bf16[384,768]{1,0:T(8,128)(2,1)} %get-tuple-element.282), channel_id=1, source_target_pairs={{0,8},{8,16},{16,24},{1,9},{9,17},{17,25},{2,10},{10,18},{18,26},{... | collective-permute-start | bytes 1769480 | tf_op jit(solution)/shard_map/ppermute | solution.py:228
  644.7 27.0 %collective-permute-start.60 = (bf16[256,1536]{1,0:T(8,128)(2,1)}, bf16[256,1536]{1,0:T(8,128)(2,1)}, u32[]{:S(2)}, u32[]{:S(2)}) collective-permute-start(bf16[256,1536]{1,0:T(8,128)(2,1)} %get-tuple-element.223), channel_id=1, source_target_pairs={{0,2},{2,0},{1,3},{3,1},{4,6},{6,4},{5,7},{7,5},{8,10},{10,8},{9,1... | collective-permute-start | bytes 2359304 | tf_op jit(solution)/shard_map/ppermute | solution.py:162
  645.9 28.3 %collective-permute-start.61 = (bf16[256,1536]{1,0:T(8,128)(2,1)}, bf16[256,1536]{1,0:T(8,128)(2,1)}, u32[]{:S(2)}, u32[]{:S(2)}) collective-permute-start(bf16[256,1536]{1,0:T(8,128)(2,1)} %get-tuple-element.223), channel_id=1, source_target_pairs={{0,4},{4,0},{1,5},{5,1},{2,6},{6,2},{3,7},{7,3},{8,12},{12,8},{9,1... | collective-permute-start | bytes 2359304 | tf_op jit(solution)/shard_map/ppermute | solution.py:162
  650.7 32.7 %collective-permute-start.91 = (bf16[384,768]{1,0:T(8,128)(2,1)}, bf16[384,768]{1,0:T(8,128)(2,1)}, u32[]{:S(2)}, u32[]{:S(2)}) collective-permute-start(bf16[384,768]{1,0:T(8,128)(2,1)} %get-tuple-element.283), channel_id=1, source_target_pairs={{8,0},{16,8},{24,16},{9,1},{17,9},{25,17},{10,2},{18,10},{26,18},{... | collective-permute-start | bytes 1769480 | tf_op jit(solution)/shard_map/ppermute | solution.py:229
  654.2 45.4 %collective-permute-start.94 = (bf16[384,768]{1,0:T(8,128)(2,1)}, bf16[384,768]{1,0:T(8,128)(2,1)}, u32[]{:S(2)}, u32[]{:S(2)}) collective-permute-start(bf16[384,768]{1,0:T(8,128)(2,1)} %get-tuple-element.288), channel_id=1, source_target_pairs={{0,8},{8,16},{16,24},{1,9},{9,17},{17,25},{2,10},{10,18},{18,26},{... | collective-permute-start | bytes 1769480 | tf_op jit(solution)/shard_map/ppermute | solution.py:228
  671.7 27.9 %collective-permute-start.97 = (bf16[384,768]{1,0:T(8,128)(2,1)}, bf16[384,768]{1,0:T(8,128)(2,1)S(1)}, u32[]{:S(2)}, u32[]{:S(2)}) collective-permute-start(bf16[384,768]{1,0:T(8,128)(2,1)} %get-tuple-element.289), channel_id=1, source_target_pairs={{8,0},{16,8},{24,16},{9,1},{17,9},{25,17},{10,2},{18,10},{26,18},{... | collective-permute-start | bytes 1769480 | tf_op jit(solution)/shard_map/ppermute | solution.py:229
  674.2 29.6 %collective-permute-start.100 = (bf16[384,1056]{0,1:T(8,128)(2,1)}, bf16[384,1056]{0,1:T(8,128)(2,1)}, u32[]{:S(2)}, u32[]{:S(2)}) collective-permute-start(bf16[384,1056]{0,1:T(8,128)(2,1)} %copy.352), channel_id=1, source_target_pairs={{0,8},{8,16},{16,24},{1,9},{9,17},{17,25},{2,10},{10,18},{18,26},{... | collective-permute-start | bytes 2433032 | tf_op jit(solution)/shard_map/ppermute | solution.py:228
  693.6 19.0 %collective-permute-start.104 = (bf16[192,768]{1,0:T(8,128)(2,1)}, bf16[192,768]{1,0:T(8,128)(2,1)}, u32[]{:S(2)}, u32[]{:S(2)}) collective-permute-start(bf16[192,768]{1,0:T(8,128)(2,1)} %dynamic-slice_convert_fusion.2), channel_id=1, source_target_pairs={{0,4},{4,0},{1,5},{5,1},{2,6},{6,2},{3,7},{7,3},{8,12},{12,8},{9,1... | collective-permute-start | bytes 884744 | tf_op jit(solution)/shard_map/ppermute | solution.py:162
  699.6 28.6 %collective-permute-start.64 = (bf16[4,256,1536]{2,1,0:T(8,128)(2,1)}, bf16[4,256,1536]{2,1,0:T(8,128)(2,1)}, u32[]{:S(2)}, u32[]{:S(2)}) collective-permute-start(bf16[4,256,1536]{2,1,0:T(8,128)(2,1)} %get-tuple-element.257), channel_id=1, source_target_pairs={{0,1},{1,0},{2,3},{3,2},{4,5},{5,4},{6,7},{7,6},{8,9},{9,8},{10,11... | collective-permute-start | bytes 9437192 | tf_op jit(solution)/shard_map/ppermute | solution.py:162
  767.4 88.2 %collective-permute-start.79 = (bf16[384,192]{0,1:T(8,128)(2,1)}, bf16[384,192]{0,1:T(8,128)(2,1)}, u32[]{:S(2)}, u32[]{:S(2)}) collective-permute-start(bf16[384,192]{0,1:T(8,128)(2,1)} %get-tuple-element.336), channel_id=1, source_target_pairs={{0,8},{1,9},{2,10},{3,11},{4,12},{5,13},{6,14},{7,15}} | collective-permute-start | bytes 442376 | tf_op jit(solution)/shard_map/ppermute | solution.py:228
  772.6 89.9 %collective-permute-start.82 = (bf16[384,192]{0,1:T(8,128)(2,1)}, bf16[384,192]{0,1:T(8,128)(2,1)}, u32[]{:S(2)}, u32[]{:S(2)}) collective-permute-start(bf16[384,192]{0,1:T(8,128)(2,1)} %get-tuple-element.337), channel_id=1, source_target_pairs={{24,16},{25,17},{26,18},{27,19},{28,20},{29,21},{30,22},{31,23}} | collective-permute-start | bytes 442376 | tf_op jit(solution)/shard_map/ppermute | solution.py:229
  855.6 39.7 %collective-permute-start.65 = (bf16[2,2,256,1536]{3,2,1,0:T(8,128)(2,1)}, bf16[2,2,256,1536]{3,2,1,0:T(8,128)(2,1)}, u32[]{:S(2)}, u32[]{:S(2)}) collective-permute-start(bf16[2,2,256,1536]{3,2,1,0:T(8,128)(2,1)} %slice_bitcast_fusion), channel_id=1, source_target_pairs={{0,1},{1,0},{2,3},{3,2},{4,5},{5,4},{6,7},{7,6},{8,9},{9,8},{10,11... | collective-permute-start | bytes 9437192 | tf_op jit(solution)/shard_map/ppermute | solution.py:162
  (183 other events, 2319.7 us)

commit v2 on v1

v2 whole, which is shorter than its diff:
```python
import jax
import jax.numpy as jnp
from jax import lax
from jax.experimental import pallas as pl
from jax.experimental.pallas import tpu as pltpu
from jax.sharding import Mesh
from jax.sharding import PartitionSpec as P

HEADS = 24
KV_HEADS = 8
HEAD_DIM = 64
GROUP = HEADS // KV_HEADS

EPSILON = 1e-05
ROPE_BASE = 1000000.0
PLANE = ("x", "y", "c")
SWAP = ((0, 1), (1, 0))
F32 = jnp.float32
BF16 = jnp.bfloat16
QK = (GROUP + 1) * HEAD_DIM
AUG = 2 * HEAD_DIM
GAIN_LANES = 64
ANY = pl.BlockSpec(memory_space=pl.ANY)


def scaled_norm(values, gain_row):
    mean_square = jnp.mean(values * values, axis=-1, keepdims=True)
    return values * lax.rsqrt(mean_square + EPSILON) * gain_row


def gating(gate_act, up_act):
    return gate_act * jax.nn.sigmoid(gate_act) * up_act


def dot(left, right, left_dim=1, right_dim=0):
    return lax.dot_general(
        left, right, (((left_dim,), (right_dim,)), ((), ())), preferred_element_type=F32
    )


def head_means(values):
    row = lax.broadcasted_iota(jnp.int32, (QK, QK), 0) // HEAD_DIM
    column = lax.broadcasted_iota(jnp.int32, (QK, QK), 1) // HEAD_DIM
    ones = jnp.where(row == column, 1.0 / HEAD_DIM, 0.0).astype(BF16)
    high = values.astype(BF16)
    rest = (values - high.astype(F32)).astype(BF16)
    return dot(high, ones) + dot(rest, ones)


def half_swap(values):
    lane = lax.broadcasted_iota(jnp.int32, values.shape, 1)
    ahead = pltpu.roll(values, QK - HEAD_DIM // 2, 1)
    behind = pltpu.roll(values, HEAD_DIM // 2, 1)
    return jnp.where(lane % HEAD_DIM < HEAD_DIM // 2, ahead, behind)


def unit_heads(raw):
    scale = lax.rsqrt(head_means(raw * raw) + EPSILON)
    return raw * scale, scale


def rotated(unit, gain, cosine, sine):
    normed = unit * gain
    return normed * cosine + half_swap(normed) * sine


def in_lanes(values, extras):
    rows = values.shape[0]
    lane = lax.broadcasted_iota(jnp.int32, (rows, HEAD_DIM), 1)
    tail = jnp.zeros((rows, HEAD_DIM), F32)
    rest = extras
    for part in range(3):
        high = rest.astype(BF16).astype(F32)
        tail = jnp.where(lane == part, high, tail)
        rest = rest - high
    return jnp.concatenate([values.astype(F32), tail], axis=1).astype(BF16)


def with_ones(values, count):
    rows = values.shape[0]
    lane = lax.broadcasted_iota(jnp.int32, (rows, HEAD_DIM), 1)
    return jnp.concatenate(
        [values.astype(F32), jnp.where(lane < count, 1.0, 0.0)], axis=1
    ).astype(BF16)


def block_at(place, block):
    away = jnp.bitwise_xor(place, block)
    return (jnp.bitwise_and(away, 1), 0, lax.shift_right_logical(away, 1), 0)


def attend_forward(place_ref, qkv_ref, gain_ref, cos_ref, sin_ref, mixed_ref, stat_ref, keys, values):
    place = place_ref[0]
    tokens = qkv_ref.shape[4]
    gain = gain_ref[...]
    row = lax.broadcasted_iota(jnp.int32, (tokens, tokens), 0)
    column = lax.broadcasted_iota(jnp.int32, (tokens, tokens), 1)
    causal = row >= column
    lane = lax.broadcasted_iota(jnp.int32, (tokens, AUG), 1)
    for block in range(4):
        source = block_at(place, block)
        here = pl.ds(block * tokens, tokens)
        raw = qkv_ref[source]
        unit, _ = unit_heads(raw[:, :QK].astype(F32))
        turned = rotated(unit, gain, cos_ref[here], sin_ref[here])
        keys[here] = turned[:, GROUP * HEAD_DIM :].astype(BF16)
        values[here] = with_ones(raw[:, QK:], 1)
        outs = []
        stats = jnp.zeros((tokens, AUG), F32)
        for head in range(GROUP):
            query = turned[:, head * HEAD_DIM : (head + 1) * HEAD_DIM].astype(BF16) * BF16(
                HEAD_DIM**-0.5
            )
            weights = jnp.exp(dot(query, keys[here], 1, 1))
            total = dot(jnp.where(causal, weights, 0.0).astype(BF16), values[here])
            if block:
                before = pl.ds(0, block * tokens)
                weights = jnp.exp(dot(query, keys[before], 1, 1))
                total = total + dot(weights.astype(BF16), values[before])
            rows_total = total[:, HEAD_DIM : HEAD_DIM + 1]
            outs.append(total[:, :HEAD_DIM] / rows_total)
            stats = jnp.where(lane == head, jnp.log(rows_total), stats)
        mixed_ref[source] = jnp.concatenate(outs, axis=1).astype(BF16)
        stat_ref[source] = stats


def attend_backward(
    place_ref,
    qkv_ref,
    mixed_ref,
    grad_ref,
    stat_ref,
    gain_ref,
    cos_ref,
    sin_ref,
    out_ref,
    gain_grad_ref,
    keys,
    values,
    key_grads,
    value_grads,
    query_grads,
):
    place = place_ref[0]
    tokens = qkv_ref.shape[4]
    gain = gain_ref[...]
    key_row = lax.broadcasted_iota(jnp.int32, (tokens, tokens), 0)
    query_row = lax.broadcasted_iota(jnp.int32, (tokens, tokens), 1)
    causal = query_row >= key_row
    key_grads[...] = jnp.zeros_like(key_grads)
    value_grads[...] = jnp.zeros_like(value_grads)
    for block in range(4):
        source = block_at(place, block)
        here = pl.ds(block * tokens, tokens)
        raw = qkv_ref[source]
        unit, _ = unit_heads(raw[:, :QK].astype(F32))
        turned = rotated(unit, gain, cos_ref[here], sin_ref[here])
        keys[here] = with_ones(turned[:, GROUP * HEAD_DIM :].astype(BF16), 3)
        values[here] = with_ones(raw[:, QK:], 3)
        grads = grad_ref[source].astype(F32)
        product = mixed_ref[source].astype(F32) * grads
        stats = stat_ref[source]
        for head in range(GROUP):
            lanes = slice(head * HEAD_DIM, (head + 1) * HEAD_DIM)
            query = in_lanes(
                turned[:, lanes].astype(BF16).astype(F32) * HEAD_DIM**-0.5,
                -stats[:, head : head + 1],
            )
            grad = in_lanes(grads[:, lanes], -jnp.sum(product[:, lanes], axis=1, keepdims=True))
            query_total = jnp.zeros((tokens, AUG), F32)
            for span, masked in ((pl.ds(0, block * tokens), False), (here, True)):
                if span.size == 0:
                    continue
                probs = jnp.exp(dot(keys[span], query, 1, 1))
                if masked:
                    probs = jnp.where(causal, probs, 0.0)
                score_grad = (probs * dot(values[span], grad, 1, 1)).astype(BF16)
                value_grads[span] += dot(probs.astype(BF16), grad)
                key_grads[span] += dot(score_grad, query)
                query_total = query_total + dot(score_grad, keys[span], 0, 0)
            query_grads[here, lanes] = query_total[:, :HEAD_DIM] * HEAD_DIM**-0.5
    gain_total = jnp.zeros((1, QK), F32)
    for block in range(4):
        source = block_at(place, block)
        here = pl.ds(block * tokens, tokens)
        raw = qkv_ref[source]
        unit, scale = unit_heads(raw[:, :QK].astype(F32))
        grads = jnp.concatenate(
            [query_grads[here, : GROUP * HEAD_DIM], key_grads[here, :HEAD_DIM]], axis=1
        )
        grads = grads.astype(BF16).astype(F32)
        back = grads * cos_ref[here] + half_swap(grads * sin_ref[here])
        gain_total = gain_total + jnp.sum(back * unit, axis=0, keepdims=True)
        scaled = back * gain
        raw_grad = scale * (scaled - unit * head_means(scaled * unit))
        out_ref[source] = jnp.concatenate(
            [raw_grad, value_grads[here, :HEAD_DIM]], axis=1
        ).astype(BF16)
    gain_grad_ref[...] = jnp.broadcast_to(gain_total[None], gain_grad_ref.shape)


def attention_call(kernel, name, place, blocked, whole, outs, scratch, deps):
    batch = blocked[0].shape[3]

    def spec(shape):
        if len(shape) == 6:
            return pl.BlockSpec(
                (2, 1, 2, 1) + tuple(shape[4:]), lambda i, *_: (0, i // batch, 0, i % batch, 0, 0)
            )
        return pl.BlockSpec((1,) + tuple(shape[1:]), lambda i, *_: (i, 0, 0))

    inputs = len(blocked) + len(whole)

    def body(place_ref, *refs):
        kernel(place_ref, *refs[:inputs], *refs[inputs + len(deps) :])

    return pl.pallas_call(
        body,
        grid_spec=pltpu.PrefetchScalarGridSpec(
            num_scalar_prefetch=1,
            grid=(2 * batch,),
            in_specs=[spec(a.shape) for a in blocked]
            + [pl.BlockSpec(a.shape, lambda i, *_: (0, 0)) for a in whole]
            + [ANY] * len(deps),
            out_specs=[spec(o.shape) for o in outs],
            scratch_shapes=scratch,
        ),
        out_shape=outs,
        name=name,
        compiler_params=pltpu.CompilerParams(vmem_limit_bytes=48 << 20),
    )(place, *blocked, *whole, *deps)


def forward_attention(place, qkv, gain, cosine, sine, deps=()):
    lead = qkv.shape[:5]
    length = 4 * qkv.shape[4]
    return attention_call(
        attend_forward,
        "attend_forward",
        place,
        [qkv],
        [gain, cosine, sine],
        [
            jax.ShapeDtypeStruct(lead + (GROUP * HEAD_DIM,), BF16),
            jax.ShapeDtypeStruct(lead + (AUG,), F32),
        ],
        [pltpu.VMEM((length, HEAD_DIM), BF16), pltpu.VMEM((length, AUG), BF16)],
        deps,
    )


def backward_attention(place, qkv, mixed, grads, stats, gain, cosine, sine, deps=()):
    length = 4 * qkv.shape[4]
    return attention_call(
        attend_backward,
        "attend_backward",
        place,
        [qkv, mixed, grads, stats],
        [gain, cosine, sine],
        [
            jax.ShapeDtypeStruct(qkv.shape, BF16),
            jax.ShapeDtypeStruct((2 * qkv.shape[3], 8, QK), F32),
        ],
        [
            pltpu.VMEM((length, AUG), BF16),
            pltpu.VMEM((length, AUG), BF16),
            pltpu.VMEM((length, AUG), F32),
            pltpu.VMEM((length, AUG), F32),
            pltpu.VMEM((length, GROUP * HEAD_DIM), F32),
        ],
        deps,
    )


def rotary_rows(length):
    half = HEAD_DIM // 2
    exponent = jnp.arange(half).astype(F32) * (2.0 / HEAD_DIM)
    frequency = jnp.power(F32(ROPE_BASE), -exponent)
    angles = jnp.arange(length).astype(F32)[:, None] * frequency[None, :]
    cosine, sine = jnp.cos(angles), jnp.sin(angles)
    heads = QK // HEAD_DIM
    return (
        jnp.tile(jnp.concatenate([cosine, cosine], axis=1), (1, heads)),
        jnp.tile(jnp.concatenate([-sine, sine], axis=1), (1, heads)),
    )


def norm_project(near, far, gain, weight, width, deps=()):
    rows, depth = near.shape
    tile = 256
    steps = rows // tile

    def body(near_ref, far_ref, gain_ref, weight_ref, *refs):
        normed_ref, out_ref = refs[len(deps) :]

        def run(ref):
            normed = scaled_norm(ref[...].astype(F32), gain_ref[...]).astype(BF16)
            normed_ref[...] = normed
            out_ref[...] = dot(normed, weight_ref[...])[:, :width].astype(BF16)

        pl.when(pl.program_id(0) < steps)(lambda: run(near_ref))
        pl.when(pl.program_id(0) >= steps)(lambda: run(far_ref))

    return pl.pallas_call(
        body,
        grid=(2 * steps,),
        in_specs=[
            pl.BlockSpec((tile, depth), lambda i: (jnp.minimum(i, steps - 1), 0)),
            pl.BlockSpec((tile, depth), lambda i: (jnp.maximum(i - steps, 0), 0)),
            pl.BlockSpec((1, depth), lambda i: (0, 0)),
            pl.BlockSpec(weight.shape, lambda i: (0, 0)),
        ]
        + [ANY] * len(deps),
        out_specs=[
            pl.BlockSpec((tile, depth), lambda i: (i, 0)),
            pl.BlockSpec((tile, width), lambda i: (i, 0)),
        ],
        out_shape=[
            jax.ShapeDtypeStruct((2 * rows, depth), BF16),
            jax.ShapeDtypeStruct((2 * rows, width), BF16),
        ],
        name="norm_project",
        compiler_params=pltpu.CompilerParams(vmem_limit_bytes=48 << 20),
    )(near, far, gain, weight, *deps)


def pack_columns(weights, widths, extra=None):
    rows = weights[0].shape[0]
    count = len(weights)
    spans = [w.shape[1] // 8 for w in weights]

    def body(*refs):
        outs = refs[count + (extra is not None) :]
        for place in range(8):
            x, s = place // 4, place % 4
            pieces = []
            for ref, span in zip(refs[:count], spans):
                first = (2 * s + x) * span
                pieces.append(ref[:, first : first + span].astype(F32))
            for out, parts in zip(outs, widths):
                line = [
                    pieces[index][:, first:last] for index, first, last in parts
                ]
                if extra is not None:
                    line.append(refs[count][...].astype(F32))
                out[place] = jnp.concatenate(line, axis=1).astype(BF16)

    extras = [] if extra is None else [extra]
    sizes = [
        sum(last - first for _, first, last in parts) + sum(e.shape[1] for e in extras)
        for parts in widths
    ]
    return pl.pallas_call(
        body,
        out_shape=[jax.ShapeDtypeStruct((8, rows, size), BF16) for size in sizes],
        name="pack_columns",
        compiler_params=pltpu.CompilerParams(vmem_limit_bytes=48 << 20),
    )(*weights, *extras)


def swap(values, axis):
    return lax.ppermute(values, axis, SWAP)


def plane_gather(rows):
    half = rows.shape[0] // 2
    from_y = swap(rows, "y")
    from_x = swap(rows, "x")
    corner = jnp.concatenate([swap(from_y[:half], "x"), swap(from_x[half:], "y")], axis=0)
    near = jnp.concatenate([rows, from_y, from_x, corner])
    return near, swap(near, "c")


def plane_scatter(near, far):
    half = near.shape[1] // 2
    halves = near.astype(F32) + swap(far, "c").astype(F32)
    mine, other = halves[0], halves.astype(BF16)
    for_y, for_x, corner = other[1], other[2], other[3]
    by_x = swap(corner[:half], "x")
    by_y = swap(corner[half:], "y")
    for_y = jnp.concatenate(
        [(for_y[:half].astype(F32) + by_x.astype(F32)).astype(BF16), for_y[half:]], axis=0
    )
    for_x = jnp.concatenate(
        [for_x[:half], (for_x[half:].astype(F32) + by_y.astype(F32)).astype(BF16)], axis=0
    )
    return mine + swap(for_y, "y").astype(F32) + swap(for_x, "x").astype(F32)


def line_gather(block):
    return lax.all_gather(block, "dp", axis=0, tiled=True)


def line_scatter(parts):
    return lax.psum_scatter(parts, "dp", scatter_dimension=0, tiled=True).astype(F32)


def plane_columns(payload):
    out = lax.all_to_all(payload, PLANE, split_axis=0, concat_axis=0, tiled=True)
    return out.reshape(-1, payload.shape[2])


def spread_columns(own, other):
    first = lax.axis_index("x") == 0
    return jnp.concatenate([jnp.where(first, own, other), jnp.where(first, other, own)], axis=1)


def settle(sums):
    rows = sums.shape[0] // 2
    x = lax.axis_index("x")
    own = lax.dynamic_slice_in_dim(sums, x * rows, rows, 0)
    send = lax.dynamic_slice_in_dim(sums, (1 - x) * rows, rows, 0).astype(BF16)
    return own, swap(send, "x").astype(F32)


def on_device(
    layer_input,
    attention_gain,
    query_weight,
    key_weight,
    value_weight,
    output_weight,
    head_gains,
    feedforward_gain,
    gate_weight,
    up_weight,
    down_weight,
    upstream,
):
    batch, tokens, model_width = layer_input.shape
    rows = query_weight.shape[0]
    own_rows = batch * tokens
    head_rows = head_gains.shape[0]
    query_cols = query_weight.shape[1] // 8
    kv_cols = key_weight.shape[1] // 8
    qkv_cols = query_cols + 2 * kv_cols
    wide = gate_weight.shape[1] // 8
    lead = (2, 2, 2, batch, tokens)
    place = (2 * lax.axis_index("y") + lax.axis_index("c")).astype(jnp.int32).reshape(1)

    gain_rows = jnp.stack(
        [attention_gain, feedforward_gain, jnp.pad(head_gains, (0, rows - head_rows))], axis=1
    )
    gain_rows = jnp.pad(gain_rows, ((0, 0), (0, 2 * GAIN_LANES - 3)))
    (first_payload,) = pack_columns(
        [query_weight, key_weight, value_weight, output_weight],
        [[(0, 0, query_cols), (1, 0, kv_cols), (2, 0, kv_cols), (3, 0, query_cols)]],
        gain_rows,
    )
    cuts = [0, 512, wide]
    spans = list(zip(cuts[:-1], cuts[1:]))
    payloads = pack_columns(
        [gate_weight, up_weight, down_weight],
        [[(index, first, last) for index in range(3)] for first, last in spans],
    )
    first_full = line_gather(plane_columns(first_payload))
    ffn_blocks = [plane_columns(payload) for payload in payloads]
    ffn_full = [line_gather(block) for block in ffn_blocks]

    own_hidden = layer_input.reshape(own_rows, model_width)
    own_upstream = upstream.reshape(own_rows, model_width)
    plane_rows = 8 * own_rows
    hidden_near, hidden_far = plane_gather(own_hidden)
    cosine, sine = rotary_rows(4 * tokens)
    gains = first_full[:, qkv_cols + query_cols : qkv_cols + query_cols + 3].astype(F32)
    attention_scale = gains[:, 0]
    feedforward_scale = gains[:, 1]
    head_scale = gains[:, 2].reshape(-1, rows)[:, :head_rows].reshape(-1)
    head_scale = jnp.concatenate(
        [jnp.tile(head_scale[:HEAD_DIM], GROUP), head_scale[HEAD_DIM:]]
    ).reshape(1, QK)
    normed_whole, qkv = norm_project(
        hidden_near, hidden_far, attention_scale[None], first_full, qkv_cols, deps=ffn_blocks
    )
    qkv_weight = first_full[:, :qkv_cols]
    out_weight = first_full[:, qkv_cols : qkv_cols + query_cols]
    upstream_near, upstream_far = plane_gather(own_upstream)
    qkv = qkv.reshape(lead + (qkv_cols,))
    mixed, stats = forward_attention(place, qkv, head_scale, cosine, sine)
    mixed_rows = mixed.reshape(2, 4 * own_rows, query_cols)
    part_shape = (4, own_rows, model_width)
    far = dot(mixed_rows[1], out_weight, 1, 1).astype(BF16).reshape(part_shape)
    near = dot(mixed_rows[0], out_weight, 1, 1).astype(BF16).reshape(part_shape)
    middle = own_hidden.astype(F32) + plane_scatter(near, far)

    post_float, feedforward_pull = jax.vjp(scaled_norm, middle, feedforward_scale)
    post_whole = jnp.concatenate(plane_gather(post_float.astype(BF16)))
    upstream_whole = jnp.concatenate([upstream_near, upstream_far])
    branch = post_grad = None
    ffn_sums = []
    for chunk in ffn_full:
        width = chunk.shape[1] // 3
        activated_grad = dot(upstream_whole, chunk[:, 2 * width :])
        both = dot(post_whole, chunk[:, : 2 * width])
        activated_float, gating_pull = jax.vjp(gating, both[:, :width], both[:, width:])
        activated = activated_float.astype(BF16)
        gate_float, up_float = gating_pull(activated_grad)
        both_grad = jnp.concatenate([gate_float.astype(BF16), up_float.astype(BF16)], axis=1)
        post_part = dot(both_grad, chunk[:, : 2 * width], 1, 1)
        post_grad = post_part if post_grad is None else post_grad + post_part
        branch_part = dot(activated, chunk[:, 2 * width :], 1, 1)
        branch = branch_part if branch is None else branch + branch_part
        weight_parts = jnp.concatenate(
            [
                dot(post_whole, both_grad, 0, 0).astype(BF16),
                dot(upstream_whole, activated, 0, 0).astype(BF16),
            ],
            axis=1,
        )
        ffn_sums.append(settle(line_scatter(weight_parts)))
    post_grad = plane_scatter(*post_grad.astype(BF16).reshape((2,) + part_shape))
    branch = plane_scatter(*branch.astype(BF16).reshape((2,) + part_shape))
    layer_output = (middle + branch).astype(BF16)
    ffn_grads = []
    for index in range(3):
        own, other = [], []
        for mine, theirs in ffn_sums:
            width = mine.shape[1] // 3
            own.append(mine[:, index * width : (index + 1) * width])
            other.append(theirs[:, index * width : (index + 1) * width])
        ffn_grads.append(
            spread_columns(jnp.concatenate(own, axis=1), jnp.concatenate(other, axis=1))
        )
    middle_part, feedforward_gain_grad = feedforward_pull(post_grad)
    middle_grad = own_upstream.astype(F32) + middle_part
    middle_low = middle_grad.astype(BF16)

    middle_whole = jnp.concatenate(plane_gather(middle_low))
    mixed_grad = dot(middle_whole, out_weight).astype(BF16)
    out_parts = dot(middle_whole, mixed.reshape(plane_rows, query_cols), 0, 0)
    out_own, out_other = settle(line_scatter(out_parts.astype(BF16)))
    output_weight_grad = spread_columns(out_own, out_other)
    qkv_grad, head_part = backward_attention(
        place, qkv, mixed, mixed_grad.reshape(mixed.shape), stats, head_scale, cosine, sine
    )
    qkv_grad = qkv_grad.reshape(plane_rows, qkv_cols)
    weight_parts = dot(normed_whole, qkv_grad, 0, 0)
    gain_part = jnp.sum(weight_parts * qkv_weight.astype(F32), axis=1) / attention_scale
    head_part = jnp.sum(head_part[:, 0], axis=0).reshape(GROUP + 1, HEAD_DIM)
    head_part = jnp.concatenate([jnp.sum(head_part[:GROUP], axis=0), head_part[GROUP]])
    head_part = jnp.pad(head_part.reshape(-1, head_rows), ((0, 0), (0, rows - head_rows)))
    gain_parts = jnp.stack([gain_part, feedforward_gain_grad, head_part.reshape(-1)], axis=1)
    gain_parts = jnp.pad(gain_parts, ((0, 0), (0, GAIN_LANES - 3)))
    weight_parts = jnp.concatenate([weight_parts.astype(BF16), gain_parts.astype(BF16)], axis=1)
    own, other = settle(line_scatter(weight_parts))
    query_weight_grad = spread_columns(own[:, :query_cols], other[:, :query_cols])
    key_weight_grad = spread_columns(
        own[:, query_cols : query_cols + kv_cols], other[:, query_cols : query_cols + kv_cols]
    )
    value_weight_grad = spread_columns(
        own[:, query_cols + kv_cols : qkv_cols], other[:, query_cols + kv_cols : qkv_cols]
    )
    gain_sums = (own[:, qkv_cols : qkv_cols + 3] + other[:, qkv_cols : qkv_cols + 3]).T
    for axis in ("y", "c"):
        half = gain_sums.shape[1] // 2
        index = lax.axis_index(axis)
        keep = lax.dynamic_slice_in_dim(gain_sums, index * half, half, 1)
        send = lax.dynamic_slice_in_dim(gain_sums, (1 - index) * half, half, 1)
        gain_sums = keep + swap(send, axis)

    grad_rows = qkv_grad.reshape(2, 4 * own_rows, qkv_cols)
    far = dot(grad_rows[1], qkv_weight, 1, 1).astype(BF16).reshape(part_shape)
    near = dot(grad_rows[0], qkv_weight, 1, 1).astype(BF16).reshape(part_shape)
    normed_grad = plane_scatter(near, far)
    _, attention_pull = jax.vjp(lambda v: scaled_norm(v, attention_scale), own_hidden.astype(F32))
    input_grad = middle_grad + attention_pull(normed_grad)[0]
    return (
        layer_output.reshape(layer_input.shape),
        input_grad.reshape(layer_input.shape),
        gain_sums[0],
        query_weight_grad,
        key_weight_grad,
        value_weight_grad,
        output_weight_grad,
        gain_sums[2, :head_rows],
        gain_sums[1],
        ffn_grads[0],
        ffn_grads[1],
        ffn_grads[2],
    )


def solution(mesh):
    fsdp, seq = mesh.shape["fsdp"], mesh.shape["seq"]
    plane_mesh = Mesh(mesh.devices.reshape(fsdp // 2, 2, seq // 2, 2), ("dp", "x", "y", "c"))
    batch = ("dp", "x")
    split = ("y", "c")
    rows = ("dp", "x", "y", "c")
    return jax.shard_map(
        on_device,
        mesh=plane_mesh,
        in_specs=(
            P(batch, split, None),
            P(rows),
            P(rows, None),
            P(rows, None),
            P(rows, None),
            P(rows, None),
            P(rows),
            P(rows),
            P(rows, None),
            P(rows, None),
            P(rows, None),
            P(batch, split, None),
        ),
        out_specs=(
            P(batch, split, None),
            P(batch, split, None),
            P(rows),
            P(batch, split),
            P(batch, split),
            P(batch, split),
            P(batch, split),
            P(rows),
            P(rows),
            P(batch, split),
            P(batch, split),
            P(batch, split),
        ),
        check_vma=False,
    )
```

time: 945 us -> 651 us (0.69)
  starting transfers between devices: 242 us -> 51.6 us
  other arithmetic: 180 us -> 67.7 us
  local copies, waits for them, and re-layouts: 155 us -> 100 us
  waiting for transfers between devices: 191 us -> 246 us
  Pallas kernels: 0 us -> 47.5 us
  matrix products: 162 us -> 118 us
  between operations: 4.09 us -> 15.4 us
    ppermute x60 -> x0, starting transfers between devices: 171 us -> none  [the longest x15 96.2 us: line_scatter(): up = lax.ppermute(for_up, 'dp', [(i, i + 1) for i in range(step)])]
    ppermute x60 -> x0, waiting for transfers between devices: 78.5 us -> none  [the longest x15 64.2 us: line_gather(): lax.ppermute(down[-1], 'dp', [(i + 1, i) for i in range(count - step)])]
    convert_element_type x27 -> x6, other arithmetic: 58.5 us -> 4.28 us  [the longest x4 3.08 us: line_scatter(): lax.psum_scatter(parts, 'dp', scatter_dimension=0, tiled=True).astype(F32)]
    ppermute x47 -> x46, waiting for transfers between devices: 95.7 us -> 149 us  [swap(): return lax.ppermute(values, axis, SWAP)]
    all_gather x0 -> x3, waiting for transfers between devices: none -> 51.8 us  [line_gather(): return lax.all_gather(block, 'dp', axis=0, tiled=True)]
    pallas_call x0 -> x5, Pallas kernels: none -> 47.5 us  [the longest x2 34.2 us: attention_call(): pl.pallas_call(body, grid_spec=pltpu.PrefetchScalarGridSpec(num_scalar_pr...]
    dot_general x48 -> x19, matrix products: 162 us -> 118 us  [dot(): lax.dot_general(left, right, (((left_dim,), (right_dim,)), ((), ())), pre...]
    rev x4 -> x0, local copies, waits for them, and re-layouts: 41 us -> none  [flip_blocks(): return jnp.where(lax.axis_index('c') == 1, jnp.flip(values, 2), values)]
  transfers between devices with their start and end apart: 112 -> 56, of which waited for: 37 -> 32; matrix products, arithmetic and copies ran while one was open for 32% -> 40% of each run, Pallas kernels for 0% -> 4%
where the time goes in v2:
time: 651 us; the launch traced here: 646 us
  waiting for transfers between devices  246 us (38%)
  matrix products  118 us (18%)
  local copies, waits for them, and re-layouts  100 us (15%)
  other arithmetic  67.7 us (10%)
  starting transfers between devices  51.6 us (8%)
  Pallas kernels  47.5 us (7%)
  between operations  15.4 us (2%)
    ppermute x46, waiting for transfers between devices, swap(): return lax.ppermute(values, axis, SWAP)  149 us
    dot_general x19, matrix products, dot(): lax.dot_general(left, right, (((left_dim,), (right_dim,)), ((), ())), pre...  118 us
    unnamed x149, local copies, waits for them, and re-layouts  60.4 us
    all_gather x3, waiting for transfers between devices, line_gather(): return lax.all_gather(block, 'dp', axis=0, tiled=True)  51.8 us
    ppermute x46, starting transfers between devices, swap(): return lax.ppermute(values, axis, SWAP)  39.4 us
    pallas_call x2, Pallas kernels, attention_call(): pl.pallas_call(body, grid_spec=pltpu.PrefetchScalarGridSpec(num_scalar_pr...  34.2 us
    all_to_all x3, waiting for transfers between devices, plane_columns(): lax.all_to_all(payload, PLANE, split_axis=0, concat_axis=0, tiled=True)  25.9 us
    add x4, other arithmetic, plane_scatter(): halves = near.astype(F32) + swap(far, 'c').astype(F32)  19.2 us
  transfers between devices with their start and end apart: 56, of which 32 were waited for; matrix products, arithmetic and copies ran while one was open for 40% of the time, Pallas kernels for 4%

profile of v2, /device:TPU:0, one launch (start us, length us, event | category | flops | bytes accessed | tf_op | source)
XLA Modules:
  0.0 646.2 jit_solution(16461375917758641608)
XLA Ops:
  7.2 3.0 collective-permute-start
  17.5 3.5 all-to-all-start
  23.2 11.6 %all-to-all-done = bf16[8,48,640]{2,1,0:T(8,128)(2,1)S(1)} async-done(((bf16[8,48,640]{2,1,0:T(8,128)(2,1)}), bf16[8,48,640]{2,1,0:T(8,128)(2,1)S(1)}, u32[]{:S(2)}, u32[]{:S(2)}) %all-to-all-start) | async-done | bytes 491552 | tf_op jit(solution)/shard_map/all_to_all | solution.py:399
  39.6 6.2 collective-permute-done.2
  49.8 3.6 all-to-all-start.2
  53.9 12.1 %all-to-all-done.2 = bf16[8,48,1056]{2,1,0:T(8,128)(2,1)S(1)} async-done(((bf16[8,48,1056]{2,1,0:T(8,128)(2,1)}), bf16[8,48,1056]{2,1,0:T(8,128)(2,1)S(1)}, u32[]{:S(2)}, u32[]{:S(2)}) %all-to-all-start.2) | async-done | bytes 811040 | tf_op jit(solution)/shard_map/all_to_all | solution.py:399
  66.0 3.6 all-to-all-start.1
  74.4 5.2 all-gather.4.cloned.1.call-done.weight_ref
  83.1 2.3 all-to-all-done.1
  87.0 10.5 %norm_project.1 = (bf16[2048,1536]{1,0:T(8,128)(2,1)}, bf16[2048,320]{1,0:T(8,128)(2,1)S(1)}) custom-call(bf16[1024,1536]{1,0:T(8,128)(2,1)} %constant_dynamic-update-slice_fusion.near_ref, bf16[1024,1536]{1,0:T(8,128)(2,1)} %collective-permute-done.4.far_ref, f32[1,1536]{1,0:T(1,128)S(1)} %broadcast_in_dim_squeeze.2.gain_ref, ...), custom_call_target="tpu_custom_call" | custom-call | tf_op jit(solution)/shard_map/norm_project/pallas_call | solution.py:304
  97.5 9.7 %attend_forward.1 = (bf16[2,2,2,1,256,192]{5,4,3,2,1,0:T(8,128)(2,1)S(1)}, f32[2,2,2,1,256,128]{5,4,3,2,1,0:T(8,128)S(1)}) custom-call(s32[1]{0:T(128)} %bitcast.1.place_ref, bf16[2,2,2,1,256,320]{5,4,3,2,1,0:T(8,128)(2,1)S(1)} %bitcast.207, f32[1,256]{1,0:T(1,128)S(1)} %bitcast.211, f32[1024,256]{1,0:T(8,128)S(1)} %copy-done.3, f32[1024,256]{1,0:T(8,128)S(1)} %copy-done.5), custom_call_target="tpu_custom_call" | custom-call | tf_op jit(solution)/shard_map/attend_forward/pallas_call | solution.py:217
  109.6 4.6 collective-permute-done.5
  114.2 3.8 convert_add_fusion.3
  123.4 7.9 %collective-permute-done.6 = bf16[128,1536]{1,0:T(8,128)(2,1)} collective-permute-done((bf16[128,1536]{1,0:T(8,128)(2,1)}, bf16[128,1536]{1,0:T(8,128)(2,1)}, u32[]{:S(2)}, u32[]{:S(2)}) %collective-permute-start.6) | collective-permute-done | bytes 393248 | tf_op jit(solution)/shard_map/ppermute | solution.py:362
  139.6 10.1 %collective-permute-done.20 = bf16[256,1536]{1,0:T(8,128)(2,1)} collective-permute-done((bf16[256,1536]{1,0:T(8,128)(2,1)}, bf16[256,1536]{1,0:T(8,128)(2,1)}, u32[]{:S(2)}, u32[]{:S(2)}) %collective-permute-start.20) | collective-permute-done | bytes 786464 | tf_op jit(solution)/shard_map/ppermute | solution.py:362
  156.1 10.4 %collective-permute-done.7 = bf16[256,1536]{1,0:T(8,128)(2,1)S(1)} collective-permute-done((bf16[256,1536]{1,0:T(8,128)(2,1)S(1)}, bf16[256,1536]{1,0:T(8,128)(2,1)S(1)}, u32[]{:S(2)}, u32[]{:S(2)}) %collective-permute-start.7) | collective-permute-done | bytes 786464 | tf_op jit(solution)/shard_map/ppermute | solution.py:362
  176.7 13.9 %collective-permute-done.10 = bf16[256,1536]{1,0:T(8,128)(2,1)S(1)} collective-permute-done((bf16[256,1536]{1,0:T(8,128)(2,1)S(1)}, bf16[256,1536]{1,0:T(8,128)(2,1)S(1)}, u32[]{:S(2)}, u32[]{:S(2)}) %collective-permute-start.10) | collective-permute-done | bytes 786464 | tf_op jit(solution)/shard_map/ppermute | solution.py:362
  195.3 5.5 collective-permute-done.12
  204.7 4.0 collective-permute-done.14
  208.7 4.0 constant_dynamic-update-slice_fusion.10
  212.7 8.0 %fusion.13 = f32[2048,704]{0,1:T(8,128)S(1)} fusion(bf16[2048,1536]{1,0:T(8,128)(2,1)} %constant_dynamic-update-slice_fusion.10, bf16[1536,1056]{1,0:T(8,128)(2,1)} %all-gather.8.cloned.1.call-done), kind=kOutput, calls=%fused_computation.48 | convolution fusion | flops 4429185024 | bytes 14417920 | tf_op jit(solution)/shard_map/dot_general | solution.py:36
  220.8 6.4 fusion.6
  227.2 2.4 convolution_convert_fusion.7
  229.6 8.6 %convolution_convert_fusion.5 = bf16[1536,704]{0,1:T(8,128)(2,1)S(1)} fusion(bf16[2048,1536]{1,0:T(8,128)(2,1)} %constant_dynamic-update-slice_fusion.10, bf16[2048,352]{0,1:T(8,128)(2,1)S(1)} %get-tuple-element.105, bf16[2048,352]{0,1:T(8,128)(2,1)S(1)} %get-tuple-element.104), kind=kOutput, calls=%fused_computation.22 | convolution fusion | flops 4436033536 | bytes 11337728 | tf_op jit(solution)/shard_map/dot_general | solution.py:36
  240.2 5.5 copy.127
  246.1 46.6 %all-gather.6.cloned.1.call-done = bf16[1536,1536]{1,0:T(8,128)(2,1)} async-done(((bf16[384,1536]{1,0:T(8,128)(2,1)}), bf16[1536,1536]{1,0:T(8,128)(2,1)}) %all-gather.6.cloned.1.call-update) | async-done | bytes 4718608 | tf_op jit(solution)/shard_map/all_gather | solution.py:391
  292.7 10.3 %fusion.9 = f32[2048,1024]{0,1:T(8,128)S(1)} fusion(bf16[2048,1536]{1,0:T(8,128)(2,1)} %constant_dynamic-update-slice_fusion.10, bf16[1536,1536]{1,0:T(8,128)(2,1)} %all-gather.6.cloned.1.call-done), kind=kOutput, calls=%fused_computation.34 | convolution fusion | flops 6442450944 | bytes 17825792 | tf_op jit(solution)/shard_map/dot_general | solution.py:36
  303.0 9.9 %fusion.2 = (bf16[2048,512]{0,1:T(8,128)(2,1)}, bf16[2048,512]{0,1:T(8,128)(2,1)}, bf16[2048,512]{0,1:T(8,128)(2,1)S(1)}) fusion(f32[2048,1024]{0,1:T(8,128)S(1)} %fusion.9, bf16[2048,1536]{1,0:T(8,128)(2,1)} %constant_dynamic-update-slice_fusion.21, bf16[1536,1536]{1,0:T(8,128)(2,1)S(1)} %copy-done.53), kind=kOutput, calls=%fused_computation.11 | convolution fusion | flops 3238002688 | bytes 22544384 | tf_op jit(solution)/shard_map/dot_general | solution.py:36
  314.3 3.5 fusion.33
  317.9 5.8 add_convert_fusion.1
  326.6 8.3 %fusion.11 = f32[2048,1536]{1,0:T(8,128)} fusion(bf16[1536,1056]{1,0:T(8,128)(2,1)S(1)} %copy-done.41, bf16[2048,352]{0,1:T(8,128)(2,1)S(1)} %copy-done.59, bf16[2048,352]{0,1:T(8,128)(2,1)S(1)} %copy-done.57), kind=kOutput, calls=%fused_computation.46 | convolution fusion | flops 4434952192 | bytes 17825792 | tf_op jit(solution)/shard_map/dot_general | solution.py:36
  334.9 12.1 %add_convert_fusion = bf16[2048,1536]{1,0:T(8,128)(2,1)S(1)} fusion(f32[2048,1536]{1,0:T(8,128)} %fusion.11, bf16[1536,1536]{1,0:T(8,128)(2,1)} %all-gather.6.cloned.1.call-done, bf16[2048,512]{0,1:T(8,128)(2,1)} %get-tuple-element.103, bf16[2048,512]{0,1:T(8,128)(2,1)} %get-tuple-element.102), kind=kOutput, calls=%fused_computation | convolution fusion | flops 6457131008 | bytes 26214400 | tf_op jit(solution)/shard_map/dot_general | solution.py:36
  348.6 9.7 %convolution_convert_fusion = bf16[1536,1024]{0,1:T(8,128)(2,1)S(1)} fusion(bf16[2048,1536]{1,0:T(8,128)(2,1)} %constant_dynamic-update-slice_fusion.10, bf16[2048,512]{0,1:T(8,128)(2,1)} %get-tuple-element.103, bf16[2048,512]{0,1:T(8,128)(2,1)S(1)} %copy-done.60), kind=kOutput, calls=%fused_computation.17 | convolution fusion | flops 6452412416 | bytes 13631488 | tf_op jit(solution)/shard_map/dot_general | solution.py:36
  358.4 5.9 convert_add_fusion.2
  367.4 3.8 convert_add_fusion.1
  372.5 3.9 collective-permute-done.16
  382.2 2.7 collective-permute-done.26
  390.5 6.2 convolution_convert_fusion.6
  396.7 2.6 pad_maximum_fusion
  399.3 6.7 %copy.125 = bf16[1536,1536]{1,0:T(8,128)(2,1)} copy(bf16[1536,1536]{0,1:T(8,128)(2,1)} %pad_maximum_fusion) | data formatting | bytes 9437184
  406.5 12.2 %collective-permute-done.27 = bf16[256,1536]{1,0:T(8,128)(2,1)S(1)} collective-permute-done((bf16[256,1536]{1,0:T(8,128)(2,1)}, bf16[256,1536]{1,0:T(8,128)(2,1)S(1)}, u32[]{:S(2)}, u32[]{:S(2)}) %collective-permute-start.27) | collective-permute-done | bytes 786464 | tf_op jit(solution)/shard_map/ppermute | solution.py:362
  418.8 4.2 multiply_reduce_fusion.1
  423.0 3.6 constant_dynamic-update-slice_fusion.31
  428.6 16.2 %collective-permute-done.30 = bf16[256,1536]{1,0:T(8,128)(2,1)S(1)} collective-permute-done((bf16[256,1536]{1,0:T(8,128)(2,1)S(1)}, bf16[256,1536]{1,0:T(8,128)(2,1)S(1)}, u32[]{:S(2)}, u32[]{:S(2)}) %collective-permute-start.30) | collective-permute-done | bytes 786464 | tf_op jit(solution)/shard_map/ppermute | solution.py:362
  449.1 5.4 collective-permute-done.32
  456.1 2.6 copy-done.46
  463.2 10.5 %collective-permute-done.45 = bf16[192,1056]{1,0:T(8,128)(2,1)S(1)} collective-permute-done((bf16[192,1056]{1,0:T(8,128)(2,1)}, bf16[192,1056]{1,0:T(8,128)(2,1)S(1)}, u32[]{:S(2)}, u32[]{:S(2)}) %collective-permute-start.45) | collective-permute-done | bytes 405536 | tf_op jit(solution)/shard_map/ppermute | solution.py:362
  474.8 3.9 constant_dynamic-update-slice_fusion.32
  478.7 4.4 convolution_convert_fusion.8
  484.2 6.1 convolution_convert_fusion.9
  490.3 2.4 copy.106
  497.6 24.6 %attend_backward.1 = (bf16[2,2,2,1,256,320]{5,4,3,2,1,0:T(8,128)(2,1)}, f32[2,8,256]{2,1,0:T(8,128)S(1)}) custom-call(s32[1]{0:T(128)} %bitcast.1.place_ref, bf16[2,2,2,1,256,320]{5,4,3,2,1,0:T(8,128)(2,1)} %bitcast.208, bf16[2,2,2,1,256,192]{5,4,3,2,1,0:T(8,128)(2,1)S(1)} %copy-done.13, bf16[2,2,2,1,256,192]{5,4,3,2,1,0:T(8,128)(2,1)S(1)} %bitcast.209, ...), custom_call_target="tpu_custom_call" | custom-call | tf_op jit(solution)/shard_map/attend_backward/pallas_call | solution.py:217
  522.2 7.0 %fusion.89 = (bf16[1536,320]{0,1:T(8,128)(2,1)}, f32[1536,320]{0,1:T(8,128)}) fusion(bf16[2048,1536]{1,0:T(8,128)(2,1)} %get-tuple-element.26, bf16[2048,320]{1,0:T(8,128)(2,1)} %bitcast.227), kind=kOutput, calls=%fused_computation.266 | convolution fusion | flops 2013757440 | bytes 10551296 | tf_op jit(solution)/shard_map/dot_general | solution.py:36
  529.3 3.1 copy.109
  540.0 3.5 convolution_convert_fusion.3
  543.6 3.5 convolution_convert_fusion.4
  550.9 5.3 reduce-scatter.15.cloned.1.call-done
  559.8 7.9 %collective-permute-done.43 = bf16[192,192]{0,1:T(8,128)(2,1)S(1)} collective-permute-done((bf16[192,192]{0,1:T(8,128)(2,1)S(1)}, bf16[192,192]{0,1:T(8,128)(2,1)S(1)}, u32[]{:S(2)}, u32[]{:S(2)}) %collective-permute-start.43) | collective-permute-done | bytes 73760 | tf_op jit(solution)/shard_map/ppermute | solution.py:362
  574.0 13.7 %reduce-scatter.13.cloned.1.call-done = bf16[384,384]{1,0:T(8,128)(2,1)} async-done(((bf16[1536,384]{1,0:T(8,128)(2,1)}), bf16[384,384]{1,0:T(8,128)(2,1)}) %reduce-scatter.13.cloned.1.call-update) | async-done | bytes 294928
  591.9 3.6 collective-permute-done.40
  597.5 5.7 convert_add_fusion
  606.8 6.1 collective-permute-done.36
  623.2 9.0 %collective-permute-done.37 = bf16[256,1536]{1,0:T(8,128)(2,1)S(1)} collective-permute-done((bf16[256,1536]{1,0:T(8,128)(2,1)}, bf16[256,1536]{1,0:T(8,128)(2,1)S(1)}, u32[]{:S(2)}, u32[]{:S(2)}) %collective-permute-start.37) | collective-permute-done | bytes 786464 | tf_op jit(solution)/shard_map/ppermute | solution.py:362
  635.8 3.4 fusion.17
  (355 shorter events, 158.7 us)
Async XLA Ops:
  7.2 28.4 %collective-permute-start = (bf16[256,1536]{1,0:T(8,128)(2,1)}, bf16[256,1536]{1,0:T(8,128)(2,1)S(1)}, u32[]{:S(2)}, u32[]{:S(2)}) collective-permute-start(bf16[256,1536]{1,0:T(8,128)(2,1)} %bitcast.213), channel_id=1, source_target_pairs={{0,2},{2,0},{1,3},{3,1},{4,6},{6,4},{5,7},{7,5},{8,10},{10,8},{9,1... | collective-permute-start | bytes 2359304 | tf_op jit(solution)/shard_map/ppermute | solution.py:362
  10.2 27.0 %collective-permute-start.1 = (bf16[256,1536]{1,0:T(8,128)(2,1)}, bf16[256,1536]{1,0:T(8,128)(2,1)S(1)}, u32[]{:S(2)}, u32[]{:S(2)}) collective-permute-start(bf16[256,1536]{1,0:T(8,128)(2,1)} %bitcast.214), channel_id=1, source_target_pairs={{0,4},{4,0},{1,5},{5,1},{2,6},{6,2},{3,7},{7,3},{8,12},{12,8},{9,1... | collective-permute-start | bytes 2359304 | tf_op jit(solution)/shard_map/ppermute | solution.py:362
  17.5 17.2 %all-to-all-start = ((bf16[8,48,640]{2,1,0:T(8,128)(2,1)}), bf16[8,48,640]{2,1,0:T(8,128)(2,1)S(1)}, u32[]{:S(2)}, u32[]{:S(2)}) async-start(bf16[8,48,640]{2,1,0:T(8,128)(2,1)} %pack_columns.2), calls=%async_computation | async-start | bytes 983040 | tf_op jit(solution)/shard_map/all_to_all | solution.py:399
  21.0 58.5 %all-gather.4.cloned.1.call-start = ((), (), s32[]{:S(2)}) async-start(), calls=%async_computation.7 | async-start | bytes 2457600 | tf_op jit(solution)/shard_map/all_gather | solution.py:391
  35.6 10.2 %collective-permute-start.2 = (bf16[128,1536]{1,0:T(8,128)(2,1)S(1)}, bf16[128,1536]{1,0:T(8,128)(2,1)S(1)}, u32[]{:S(2)}, u32[]{:S(2)}) collective-permute-start(bf16[128,1536]{1,0:T(8,128)(2,1)S(1)} %slice.476), channel_id=1, source_target_pairs={{0,4},{4,0},{1,5},{5,1},{2,6},{6,2},{3,7},{7,3},{8,12},{12,8},{9,1... | collective-permute-start | bytes 1179656 | tf_op jit(solution)/shard_map/ppermute | solution.py:362
  37.2 10.0 %collective-permute-start.3 = (bf16[128,1536]{1,0:T(8,128)(2,1)S(1)}, bf16[128,1536]{1,0:T(8,128)(2,1)S(1)}, u32[]{:S(2)}, u32[]{:S(2)}) collective-permute-start(bf16[128,1536]{1,0:T(8,128)(2,1)S(1)} %slice.477), channel_id=1, source_target_pairs={{0,2},{2,0},{1,3},{3,1},{4,6},{6,4},{5,7},{7,5},{8,10},{10,8},{9,1... | collective-permute-start | bytes 1179656 | tf_op jit(solution)/shard_map/ppermute | solution.py:362
  48.0 37.4 %collective-permute-start.4 = (bf16[1024,1536]{1,0:T(8,128)(2,1)}, bf16[1024,1536]{1,0:T(8,128)(2,1)}, u32[]{:S(2)}, u32[]{:S(2)}) collective-permute-start(bf16[1024,1536]{1,0:T(8,128)(2,1)} %constant_dynamic-update-slice_fusion.near_ref), channel_id=1, source_target_pairs={{0,1},{1,0},{2,3},{3,2},{4,5},{5,4},{6,7},{7,6},{8,9},{9,8},{10,11... | collective-permute-start | bytes 9437192 | tf_op jit(solution)/shard_map/ppermute | solution.py:362
  49.8 16.2 %all-to-all-start.2 = ((bf16[8,48,1056]{2,1,0:T(8,128)(2,1)}), bf16[8,48,1056]{2,1,0:T(8,128)(2,1)S(1)}, u32[]{:S(2)}, u32[]{:S(2)}) async-start(bf16[8,48,1056]{2,1,0:T(8,128)(2,1)} %get-tuple-element.21), calls=%async_computation.2 | async-start | bytes 1769472 | tf_op jit(solution)/shard_map/all_to_all | solution.py:399
  66.0 19.4 %all-to-all-start.1 = ((bf16[8,48,1536]{2,1,0:T(8,128)(2,1)}), bf16[8,48,1536]{2,1,0:T(8,128)(2,1)S(1)}, u32[]{:S(2)}, u32[]{:S(2)}) async-start(bf16[8,48,1536]{2,1,0:T(8,128)(2,1)} %get-tuple-element.20), calls=%async_computation.1 | async-start | bytes 2359296 | tf_op jit(solution)/shard_map/all_to_all | solution.py:399
  69.6 143.2 %all-gather.8.cloned.1.call-start = ((), (), s32[]{:S(2)}) async-start(), calls=%async_computation.9 | async-start | bytes 4423680 | tf_op jit(solution)/shard_map/all_gather | solution.py:391
  108.5 5.7 collective-permute-start.5
  119.1 12.3 %collective-permute-start.6 = (bf16[128,1536]{1,0:T(8,128)(2,1)}, bf16[128,1536]{1,0:T(8,128)(2,1)}, u32[]{:S(2)}, u32[]{:S(2)}) collective-permute-start(bf16[128,1536]{1,0:T(8,128)(2,1)} %get-tuple-element.140), channel_id=1, source_target_pairs={{0,4},{4,0},{1,5},{5,1},{2,6},{6,2},{3,7},{7,3},{8,12},{12,8},{9,1... | collective-permute-start | bytes 1179656 | tf_op jit(solution)/shard_map/ppermute | solution.py:362
  120.5 12.3 %collective-permute-start.8 = (bf16[128,1536]{1,0:T(8,128)(2,1)}, bf16[128,1536]{1,0:T(8,128)(2,1)}, u32[]{:S(2)}, u32[]{:S(2)}) collective-permute-start(bf16[128,1536]{1,0:T(8,128)(2,1)} %get-tuple-element.141), channel_id=1, source_target_pairs={{0,2},{2,0},{1,3},{3,1},{4,6},{6,4},{5,7},{7,5},{8,10},{10,8},{9,1... | collective-permute-start | bytes 1179656 | tf_op jit(solution)/shard_map/ppermute | solution.py:362
  121.1 28.6 %collective-permute-start.20 = (bf16[256,1536]{1,0:T(8,128)(2,1)}, bf16[256,1536]{1,0:T(8,128)(2,1)}, u32[]{:S(2)}, u32[]{:S(2)}) collective-permute-start(bf16[256,1536]{1,0:T(8,128)(2,1)} %bitcast.33), channel_id=1, source_target_pairs={{0,2},{2,0},{1,3},{3,1},{4,6},{6,4},{5,7},{7,5},{8,10},{10,8},{9,1... | collective-permute-start | bytes 2359304 | tf_op jit(solution)/shard_map/ppermute | solution.py:362
  122.6 28.8 %collective-permute-start.21 = (bf16[256,1536]{1,0:T(8,128)(2,1)}, bf16[256,1536]{1,0:T(8,128)(2,1)}, u32[]{:S(2)}, u32[]{:S(2)}) collective-permute-start(bf16[256,1536]{1,0:T(8,128)(2,1)} %bitcast.33), channel_id=1, source_target_pairs={{0,4},{4,0},{1,5},{5,1},{2,6},{6,2},{3,7},{7,3},{8,12},{12,8},{9,1... | collective-permute-start | bytes 2359304 | tf_op jit(solution)/shard_map/ppermute | solution.py:362
  123.1 169.6 %all-gather.6.cloned.1.call-start = ((), (), s32[]{:S(2)}) async-start(), calls=%async_computation.8 | async-start | bytes 5898240 | tf_op jit(solution)/shard_map/all_gather | solution.py:391
  135.3 31.2 %collective-permute-start.7 = (bf16[256,1536]{1,0:T(8,128)(2,1)S(1)}, bf16[256,1536]{1,0:T(8,128)(2,1)S(1)}, u32[]{:S(2)}, u32[]{:S(2)}) collective-permute-start(bf16[256,1536]{1,0:T(8,128)(2,1)S(1)} %pad_maximum_fusion.12), channel_id=1, source_target_pairs={{0,2},{2,0},{1,3},{3,1},{4,6},{6,4},{5,7},{7,5},{8,10},{10,8},{9,1... | collective-permute-start | bytes 2359304 | tf_op jit(solution)/shard_map/ppermute | solution.py:362
  135.9 30.5 %copy-start.27 = (bf16[1,256,1536]{2,1,0:T(8,128)(2,1)S(1)}, bf16[1,256,1536]{2,1,0:T(8,128)(2,1)}, u32[]{:S(2)}) copy-start(bf16[1,256,1536]{2,1,0:T(8,128)(2,1)} %param.12) | copy-start | bytes 2359300
  136.0 30.5 %collective-permute-start.9 = (bf16[256,1536]{1,0:T(8,128)(2,1)S(1)}, bf16[256,1536]{1,0:T(8,128)(2,1)S(1)}, u32[]{:S(2)}, u32[]{:S(2)}) collective-permute-start(bf16[256,1536]{1,0:T(8,128)(2,1)S(1)} %pad_maximum_fusion.13), channel_id=1, source_target_pairs={{0,4},{4,0},{1,5},{5,1},{2,6},{6,2},{3,7},{7,3},{8,12},{12,8},{9,1... | collective-permute-start | bytes 2359304 | tf_op jit(solution)/shard_map/ppermute | solution.py:362
  150.7 23.3 %collective-permute-start.22 = (bf16[128,1536]{1,0:T(8,128)(2,1)S(1)}, bf16[128,1536]{1,0:T(8,128)(2,1)S(1)}, u32[]{:S(2)}, u32[]{:S(2)}) collective-permute-start(bf16[128,1536]{1,0:T(8,128)(2,1)S(1)} %slice.509), channel_id=1, source_target_pairs={{0,4},{4,0},{1,5},{5,1},{2,6},{6,2},{3,7},{7,3},{8,12},{12,8},{9,1... | collective-permute-start | bytes 1179656 | tf_op jit(solution)/shard_map/ppermute | solution.py:362
  152.4 22.5 %collective-permute-start.23 = (bf16[128,1536]{1,0:T(8,128)(2,1)S(1)}, bf16[128,1536]{1,0:T(8,128)(2,1)S(1)}, u32[]{:S(2)}, u32[]{:S(2)}) collective-permute-start(bf16[128,1536]{1,0:T(8,128)(2,1)S(1)} %slice.510), channel_id=1, source_target_pairs={{0,2},{2,0},{1,3},{3,1},{4,6},{6,4},{5,7},{7,5},{8,10},{10,8},{9,1... | collective-permute-start | bytes 1179656 | tf_op jit(solution)/shard_map/ppermute | solution.py:362
  169.8 20.8 %collective-permute-start.10 = (bf16[256,1536]{1,0:T(8,128)(2,1)S(1)}, bf16[256,1536]{1,0:T(8,128)(2,1)S(1)}, u32[]{:S(2)}, u32[]{:S(2)}) collective-permute-start(bf16[256,1536]{1,0:T(8,128)(2,1)S(1)} %get-tuple-element.99), channel_id=1, source_target_pairs={{0,2},{2,0},{1,3},{3,1},{4,6},{6,4},{5,7},{7,5},{8,10},{10,8},{9,1... | collective-permute-start | bytes 2359304 | tf_op jit(solution)/shard_map/ppermute | solution.py:362
  170.4 20.9 %collective-permute-start.11 = (bf16[256,1536]{1,0:T(8,128)(2,1)S(1)}, bf16[256,1536]{1,0:T(8,128)(2,1)S(1)}, u32[]{:S(2)}, u32[]{:S(2)}) collective-permute-start(bf16[256,1536]{1,0:T(8,128)(2,1)S(1)} %get-tuple-element.99), channel_id=1, source_target_pairs={{0,4},{4,0},{1,5},{5,1},{2,6},{6,2},{3,7},{7,3},{8,12},{12,8},{9,1... | collective-permute-start | bytes 2359304 | tf_op jit(solution)/shard_map/ppermute | solution.py:362
  175.7 19.6 %copy-start.47 = (bf16[2048,1536]{1,0:T(8,128)(2,1)}, bf16[2048,1536]{1,0:T(8,128)(2,1)S(1)}, u32[]{:S(2)}) copy-start(bf16[2048,1536]{1,0:T(8,128)(2,1)S(1)} %get-tuple-element.192) | copy-start | bytes 18874372
  175.7 27.1 %collective-permute-start.24 = (bf16[1024,1536]{1,0:T(8,128)(2,1)}, bf16[1024,1536]{1,0:T(8,128)(2,1)S(1)}, u32[]{:S(2)}, u32[]{:S(2)}) collective-permute-start(bf16[1024,1536]{1,0:T(8,128)(2,1)} %get-tuple-element.191), channel_id=1, source_target_pairs={{0,1},{1,0},{2,3},{3,2},{4,5},{5,4},{6,7},{7,6},{8,9},{9,8},{10,11... | collective-permute-start | bytes 9437192 | tf_op jit(solution)/shard_map/ppermute | solution.py:362
  190.6 10.2 %collective-permute-start.12 = (bf16[128,1536]{1,0:T(8,128)(2,1)S(1)}, bf16[128,1536]{1,0:T(8,128)(2,1)S(1)}, u32[]{:S(2)}, u32[]{:S(2)}) collective-permute-start(bf16[128,1536]{1,0:T(8,128)(2,1)S(1)} %slice.492), channel_id=1, source_target_pairs={{0,4},{4,0},{1,5},{5,1},{2,6},{6,2},{3,7},{7,3},{8,12},{12,8},{9,1... | collective-permute-start | bytes 1179656 | tf_op jit(solution)/shard_map/ppermute | solution.py:362
  191.3 10.5 %collective-permute-start.13 = (bf16[128,1536]{1,0:T(8,128)(2,1)S(1)}, bf16[128,1536]{1,0:T(8,128)(2,1)S(1)}, u32[]{:S(2)}, u32[]{:S(2)}) collective-permute-start(bf16[128,1536]{1,0:T(8,128)(2,1)S(1)} %slice.493), channel_id=1, source_target_pairs={{0,2},{2,0},{1,3},{3,1},{4,6},{6,4},{5,7},{7,5},{8,10},{10,8},{9,1... | collective-permute-start | bytes 1179656 | tf_op jit(solution)/shard_map/ppermute | solution.py:362
  202.7 6.0 collective-permute-start.14
  202.7 256.0 %reduce-scatter.19.cloned.1.call-start = ((), (), s32[]{:S(2)}) async-start(), calls=%async_computation.13 | async-start | bytes 4423680 | tf_op jit(solution)/shard_map/reduce_scatter | solution.py:395
  245.7 301.4 %reduce-scatter.17.cloned.1.call-start = ((), (), s32[]{:S(2)}) async-start(), calls=%async_computation.12 | async-start | bytes 5898240 | tf_op jit(solution)/shard_map/reduce_scatter | solution.py:395
  324.1 34.3 %collective-permute-start.15 = (bf16[4,256,1536]{2,1,0:T(8,128)(2,1)S(1)}, bf16[4,256,1536]{2,1,0:T(8,128)(2,1)}, u32[]{:S(2)}, u32[]{:S(2)}) collective-permute-start(bf16[4,256,1536]{2,1,0:T(8,128)(2,1)S(1)} %bitcast.222), channel_id=1, source_target_pairs={{0,1},{1,0},{2,3},{3,2},{4,5},{5,4},{6,7},{7,6},{8,9},{9,8},{10,11... | collective-permute-start | bytes 9437192 | tf_op jit(solution)/shard_map/ppermute | solution.py:362
  347.5 20.0 %collective-permute-start.25 = (bf16[4,256,1536]{2,1,0:T(8,128)(2,1)S(1)}, bf16[4,256,1536]{2,1,0:T(8,128)(2,1)S(1)}, u32[]{:S(2)}, u32[]{:S(2)}) collective-permute-start(bf16[4,256,1536]{2,1,0:T(8,128)(2,1)S(1)} %bitcast.221), channel_id=1, source_target_pairs={{0,1},{1,0},{2,3},{3,2},{4,5},{5,4},{6,7},{7,6},{8,9},{9,8},{10,11... | collective-permute-start | bytes 9437192 | tf_op jit(solution)/shard_map/ppermute | solution.py:362
  364.4 12.1 %collective-permute-start.16 = (bf16[128,1536]{1,0:T(8,128)(2,1)S(1)}, bf16[128,1536]{1,0:T(8,128)(2,1)S(1)}, u32[]{:S(2)}, u32[]{:S(2)}) collective-permute-start(bf16[128,1536]{1,0:T(8,128)(2,1)S(1)} %get-tuple-element.134), channel_id=1, source_target_pairs={{0,4},{4,0},{1,5},{5,1},{2,6},{6,2},{3,7},{7,3},{8,12},{12,8},{9,1... | collective-permute-start | bytes 1179656 | tf_op jit(solution)/shard_map/ppermute | solution.py:362
  366.0 12.0 %collective-permute-start.18 = (bf16[128,1536]{1,0:T(8,128)(2,1)S(1)}, bf16[128,1536]{1,0:T(8,128)(2,1)S(1)}, u32[]{:S(2)}, u32[]{:S(2)}) collective-permute-start(bf16[128,1536]{1,0:T(8,128)(2,1)S(1)} %get-tuple-element.135), channel_id=1, source_target_pairs={{0,2},{2,0},{1,3},{3,1},{4,6},{6,4},{5,7},{7,5},{8,10},{10,8},{9,1... | collective-permute-start | bytes 1179656 | tf_op jit(solution)/shard_map/ppermute | solution.py:362
  371.4 13.5 %collective-permute-start.26 = (bf16[128,1536]{1,0:T(8,128)(2,1)S(1)}, bf16[128,1536]{1,0:T(8,128)(2,1)S(1)}, u32[]{:S(2)}, u32[]{:S(2)}) collective-permute-start(bf16[128,1536]{1,0:T(8,128)(2,1)S(1)} %get-tuple-element.128), channel_id=1, source_target_pairs={{0,4},{4,0},{1,5},{5,1},{2,6},{6,2},{3,7},{7,3},{8,12},{12,8},{9,1... | collective-permute-start | bytes 1179656 | tf_op jit(solution)/shard_map/ppermute | solution.py:362
  372.0 14.4 %collective-permute-start.28 = (bf16[128,1536]{1,0:T(8,128)(2,1)S(1)}, bf16[128,1536]{1,0:T(8,128)(2,1)S(1)}, u32[]{:S(2)}, u32[]{:S(2)}) collective-permute-start(bf16[128,1536]{1,0:T(8,128)(2,1)S(1)} %get-tuple-element.129), channel_id=1, source_target_pairs={{0,2},{2,0},{1,3},{3,1},{4,6},{6,4},{5,7},{7,5},{8,10},{10,8},{9,1... | collective-permute-start | bytes 1179656 | tf_op jit(solution)/shard_map/ppermute | solution.py:362
  379.2 27.3 %collective-permute-start.17 = (bf16[256,1536]{1,0:T(8,128)(2,1)}, bf16[256,1536]{1,0:T(8,128)(2,1)}, u32[]{:S(2)}, u32[]{:S(2)}) collective-permute-start(bf16[256,1536]{1,0:T(8,128)(2,1)} %pad_maximum_fusion.14), channel_id=1, source_target_pairs={{0,2},{2,0},{1,3},{3,1},{4,6},{6,4},{5,7},{7,5},{8,10},{10,8},{9,1... | collective-permute-start | bytes 2359304 | tf_op jit(solution)/shard_map/ppermute | solution.py:362
  381.6 24.9 %collective-permute-start.19 = (bf16[256,1536]{1,0:T(8,128)(2,1)}, bf16[256,1536]{1,0:T(8,128)(2,1)}, u32[]{:S(2)}, u32[]{:S(2)}) collective-permute-start(bf16[256,1536]{1,0:T(8,128)(2,1)} %pad_maximum_fusion.15), channel_id=1, source_target_pairs={{0,4},{4,0},{1,5},{5,1},{2,6},{6,2},{3,7},{7,3},{8,12},{12,8},{9,1... | collective-permute-start | bytes 2359304 | tf_op jit(solution)/shard_map/ppermute | solution.py:362
  387.6 31.2 %collective-permute-start.27 = (bf16[256,1536]{1,0:T(8,128)(2,1)}, bf16[256,1536]{1,0:T(8,128)(2,1)S(1)}, u32[]{:S(2)}, u32[]{:S(2)}) collective-permute-start(bf16[256,1536]{1,0:T(8,128)(2,1)} %pad_maximum_fusion.16), channel_id=1, source_target_pairs={{0,2},{2,0},{1,3},{3,1},{4,6},{6,4},{5,7},{7,5},{8,10},{10,8},{9,1... | collective-permute-start | bytes 2359304 | tf_op jit(solution)/shard_map/ppermute | solution.py:362
  389.9 28.8 %collective-permute-start.29 = (bf16[256,1536]{1,0:T(8,128)(2,1)}, bf16[256,1536]{1,0:T(8,128)(2,1)S(1)}, u32[]{:S(2)}, u32[]{:S(2)}) collective-permute-start(bf16[256,1536]{1,0:T(8,128)(2,1)} %pad_maximum_fusion.17), channel_id=1, source_target_pairs={{0,4},{4,0},{1,5},{5,1},{2,6},{6,2},{3,7},{7,3},{8,12},{12,8},{9,1... | collective-permute-start | bytes 2359304 | tf_op jit(solution)/shard_map/ppermute | solution.py:362
  406.0 12.8 %copy-start.24 = (f32[256,1536]{1,0:T(8,128)S(1)}, f32[256,1536]{1,0:T(8,128)}, u32[]{:S(2)}) copy-start(f32[256,1536]{1,0:T(8,128)} %copy-done.23) | copy-start | bytes 4718596
  406.0 12.8 %copy-start.45 = (f32[1536]{0:T(1024)S(1)}, f32[1536]{0:T(1024)}, u32[]{:S(2)}) copy-start(f32[1536]{0:T(1024)} %get-tuple-element.92) | copy-start | bytes 18436
  406.0 12.8 %copy-start.50 = (f32[256]{0:T(256)S(1)}, f32[256]{0:T(256)}, u32[]{:S(2)}) copy-start(f32[256]{0:T(256)} %copy-done.49) | copy-start | bytes 3076
  406.0 150.3 %reduce-scatter.15.cloned.1.call-start = ((), (), s32[]{:S(2)}) async-start(), calls=%async_computation.11 | async-start | bytes 983040
  426.6 18.3 %collective-permute-start.30 = (bf16[256,1536]{1,0:T(8,128)(2,1)S(1)}, bf16[256,1536]{1,0:T(8,128)(2,1)S(1)}, u32[]{:S(2)}, u32[]{:S(2)}) collective-permute-start(bf16[256,1536]{1,0:T(8,128)(2,1)S(1)} %get-tuple-element.96), channel_id=1, source_target_pairs={{0,2},{2,0},{1,3},{3,1},{4,6},{6,4},{5,7},{7,5},{8,10},{10,8},{9,1... | collective-permute-start | bytes 2359304 | tf_op jit(solution)/shard_map/ppermute | solution.py:362
  428.1 18.4 %collective-permute-start.31 = (bf16[256,1536]{1,0:T(8,128)(2,1)S(1)}, bf16[256,1536]{1,0:T(8,128)(2,1)S(1)}, u32[]{:S(2)}, u32[]{:S(2)}) collective-permute-start(bf16[256,1536]{1,0:T(8,128)(2,1)S(1)} %get-tuple-element.96), channel_id=1, source_target_pairs={{0,4},{4,0},{1,5},{5,1},{2,6},{6,2},{3,7},{7,3},{8,12},{12,8},{9,1... | collective-permute-start | bytes 2359304 | tf_op jit(solution)/shard_map/ppermute | solution.py:362
  444.9 9.6 %collective-permute-start.32 = (bf16[128,1536]{1,0:T(8,128)(2,1)S(1)}, bf16[128,1536]{1,0:T(8,128)(2,1)S(1)}, u32[]{:S(2)}, u32[]{:S(2)}) collective-permute-start(bf16[128,1536]{1,0:T(8,128)(2,1)S(1)} %slice.518), channel_id=1, source_target_pairs={{0,4},{4,0},{1,5},{5,1},{2,6},{6,2},{3,7},{7,3},{8,12},{12,8},{9,1... | collective-permute-start | bytes 1179656 | tf_op jit(solution)/shard_map/ppermute | solution.py:362
  446.5 8.8 %collective-permute-start.33 = (bf16[128,1536]{1,0:T(8,128)(2,1)S(1)}, bf16[128,1536]{1,0:T(8,128)(2,1)S(1)}, u32[]{:S(2)}, u32[]{:S(2)}) collective-permute-start(bf16[128,1536]{1,0:T(8,128)(2,1)S(1)} %slice.519), channel_id=1, source_target_pairs={{0,2},{2,0},{1,3},{3,1},{4,6},{6,4},{5,7},{7,5},{8,10},{10,8},{9,1... | collective-permute-start | bytes 1179656 | tf_op jit(solution)/shard_map/ppermute | solution.py:362
  458.7 16.0 %collective-permute-start.34 = (bf16[1024,1536]{1,0:T(8,128)(2,1)}, bf16[1024,1536]{1,0:T(8,128)(2,1)}, u32[]{:S(2)}, u32[]{:S(2)}) collective-permute-start(bf16[1024,1536]{1,0:T(8,128)(2,1)} %get-tuple-element.187), channel_id=1, source_target_pairs={{0,1},{1,0},{2,3},{3,2},{4,5},{5,4},{6,7},{7,6},{8,9},{9,8},{10,11... | collective-permute-start | bytes 9437192 | tf_op jit(solution)/shard_map/ppermute | solution.py:362
  460.9 12.8 %collective-permute-start.45 = (bf16[192,1056]{1,0:T(8,128)(2,1)}, bf16[192,1056]{1,0:T(8,128)(2,1)S(1)}, u32[]{:S(2)}, u32[]{:S(2)}) collective-permute-start(bf16[192,1056]{1,0:T(8,128)(2,1)} %dynamic-slice_convert_fusion.1), channel_id=1, source_target_pairs={{0,4},{4,0},{1,5},{5,1},{2,6},{6,2},{3,7},{7,3},{8,12},{12,8},{9,1... | collective-permute-start | bytes 1216520 | tf_op jit(solution)/shard_map/ppermute | solution.py:362
  535.2 52.4 %reduce-scatter.13.cloned.1.call-start = ((), (), s32[]{:S(2)}) async-start(), calls=%async_computation.10 | async-start | bytes 1474560
  543.6 54.0 %collective-permute-start.35 = (bf16[4,256,1536]{2,1,0:T(8,128)(2,1)}, bf16[4,256,1536]{2,1,0:T(8,128)(2,1)}, u32[]{:S(2)}, u32[]{:S(2)}) collective-permute-start(bf16[4,256,1536]{2,1,0:T(8,128)(2,1)} %bitcast.47), channel_id=1, source_target_pairs={{0,1},{1,0},{2,3},{3,2},{4,5},{5,4},{6,7},{7,6},{8,9},{9,8},{10,11... | collective-permute-start | bytes 9437192 | tf_op jit(solution)/shard_map/ppermute | solution.py:362
  549.6 19.1 %collective-permute-start.44 = (bf16[192,1536]{1,0:T(8,128)(2,1)}, bf16[192,1536]{1,0:T(8,128)(2,1)S(1)}, u32[]{:S(2)}, u32[]{:S(2)}) collective-permute-start(bf16[192,1536]{1,0:T(8,128)(2,1)} %dynamic-slice_convert_fusion), channel_id=1, source_target_pairs={{0,4},{4,0},{1,5},{5,1},{2,6},{6,2},{3,7},{7,3},{8,12},{12,8},{9,1... | collective-permute-start | bytes 1769480 | tf_op jit(solution)/shard_map/ppermute | solution.py:362
  557.5 10.2 %collective-permute-start.43 = (bf16[192,192]{0,1:T(8,128)(2,1)S(1)}, bf16[192,192]{0,1:T(8,128)(2,1)S(1)}, u32[]{:S(2)}, u32[]{:S(2)}) collective-permute-start(bf16[192,192]{0,1:T(8,128)(2,1)S(1)} %dynamic-slice_convert_fusion.3), channel_id=1, source_target_pairs={{0,4},{4,0},{1,5},{5,1},{2,6},{6,2},{3,7},{7,3},{8,12},{12,8},{9,1... | collective-permute-start | bytes 221192 | tf_op jit(solution)/shard_map/ppermute | solution.py:362
  589.0 6.5 %collective-permute-start.40 = (bf16[192,384]{0,1:T(8,128)(2,1)S(1)}, bf16[192,384]{0,1:T(8,128)(2,1)S(1)}, u32[]{:S(2)}, u32[]{:S(2)}) collective-permute-start(bf16[192,384]{0,1:T(8,128)(2,1)S(1)} %dynamic-slice_convert_fusion.2), channel_id=1, source_target_pairs={{0,4},{4,0},{1,5},{5,1},{2,6},{6,2},{3,7},{7,3},{8,12},{12,8},{9,1... | collective-permute-start | bytes 442376 | tf_op jit(solution)/shard_map/ppermute | solution.py:362
  595.7 10.4 %collective-permute-start.41 = (f32[3,96]{1,0:T(4,128)S(1)}, f32[3,96]{1,0:T(4,128)S(1)}, u32[]{:S(2)}, u32[]{:S(2)}) collective-permute-start(f32[3,96]{1,0:T(4,128)S(1)} %fusion.67), channel_id=1, source_target_pairs={{0,2},{2,0},{1,3},{3,1},{4,6},{6,4},{5,7},{7,5},{8,10},{10,8},{9,1... | collective-permute-start | bytes 3464 | tf_op jit(solution)/shard_map/ppermute | solution.py:362
  603.3 9.6 %collective-permute-start.36 = (bf16[128,1536]{1,0:T(8,128)(2,1)S(1)}, bf16[128,1536]{1,0:T(8,128)(2,1)S(1)}, u32[]{:S(2)}, u32[]{:S(2)}) collective-permute-start(bf16[128,1536]{1,0:T(8,128)(2,1)S(1)} %get-tuple-element.122), channel_id=1, source_target_pairs={{0,4},{4,0},{1,5},{5,1},{2,6},{6,2},{3,7},{7,3},{8,12},{12,8},{9,1... | collective-permute-start | bytes 1179656 | tf_op jit(solution)/shard_map/ppermute | solution.py:362
  604.8 9.2 %collective-permute-start.38 = (bf16[128,1536]{1,0:T(8,128)(2,1)S(1)}, bf16[128,1536]{1,0:T(8,128)(2,1)S(1)}, u32[]{:S(2)}, u32[]{:S(2)}) collective-permute-start(bf16[128,1536]{1,0:T(8,128)(2,1)S(1)} %get-tuple-element.123), channel_id=1, source_target_pairs={{0,2},{2,0},{1,3},{3,1},{4,6},{6,4},{5,7},{7,5},{8,10},{10,8},{9,1... | collective-permute-start | bytes 1179656 | tf_op jit(solution)/shard_map/ppermute | solution.py:362
  606.8 26.8 %copy-start.28 = (bf16[1,256,1536]{2,1,0:T(8,128)(2,1)S(1)}, bf16[1,256,1536]{2,1,0:T(8,128)(2,1)}, u32[]{:S(2)}) copy-start(bf16[1,256,1536]{2,1,0:T(8,128)(2,1)} %param.12) | copy-start | bytes 2359300
  606.8 26.8 %copy-start.43 = (f32[1536]{0:T(1024)S(1)}, f32[1536]{0:T(1024)}, u32[]{:S(2)}) copy-start(f32[1536]{0:T(1024)} %copy-done.42) | copy-start | bytes 18436
  606.8 15.3 %collective-permute-start.42 = (f32[3,48]{1,0:T(4,128)}, f32[3,48]{1,0:T(4,128)S(1)}, u32[]{:S(2)}, u32[]{:S(2)}) collective-permute-start(f32[3,48]{1,0:T(4,128)} %constant_dynamic-slice_fusion.2), channel_id=1, source_target_pairs={{0,1},{1,0},{2,3},{3,2},{4,5},{5,4},{6,7},{7,6},{8,9},{9,8},{10,11... | collective-permute-start | bytes 1736 | tf_op jit(solution)/shard_map/ppermute | solution.py:362
  615.2 16.9 %collective-permute-start.37 = (bf16[256,1536]{1,0:T(8,128)(2,1)}, bf16[256,1536]{1,0:T(8,128)(2,1)S(1)}, u32[]{:S(2)}, u32[]{:S(2)}) collective-permute-start(bf16[256,1536]{1,0:T(8,128)(2,1)} %pad_maximum_fusion.18), channel_id=1, source_target_pairs={{0,2},{2,0},{1,3},{3,1},{4,6},{6,4},{5,7},{7,5},{8,10},{10,8},{9,1... | collective-permute-start | bytes 2359304 | tf_op jit(solution)/shard_map/ppermute | solution.py:362
  615.8 20.0 %copy-start.29 = (f32[256,1536]{1,0:T(8,128)S(1)}, f32[256,1536]{1,0:T(8,128)}, u32[]{:S(2)}) copy-start(f32[256,1536]{1,0:T(8,128)} %get-tuple-element.97) | copy-start | bytes 4718596
  616.7 16.8 %collective-permute-start.39 = (bf16[256,1536]{1,0:T(8,128)(2,1)}, bf16[256,1536]{1,0:T(8,128)(2,1)}, u32[]{:S(2)}, u32[]{:S(2)}) collective-permute-start(bf16[256,1536]{1,0:T(8,128)(2,1)} %pad_maximum_fusion.19), channel_id=1, source_target_pairs={{0,4},{4,0},{1,5},{5,1},{2,6},{6,2},{3,7},{7,3},{8,12},{12,8},{9,1... | collective-permute-start | bytes 2359304 | tf_op jit(solution)/shard_map/ppermute | solution.py:362
  (53 other events, 258.7 us)
Sparse Core Ops, SparseCore 0:
  35.7 43.8 all-gather.3
  123.3 70.2 all-gather.7
  202.9 89.8 all-gather.5
  294.9 64.8 reduce-scatter.18
  406.1 82.6 reduce-scatter.16
  535.3 20.8 reduce-scatter.14
  559.2 28.4 reduce-scatter.12

commit v3 on v2

v3 whole, which is shorter than its diff:
```python
import jax
import jax.numpy as jnp
from jax import lax
from jax.experimental import pallas as pl
from jax.experimental.pallas import tpu as pltpu
from jax.sharding import Mesh
from jax.sharding import PartitionSpec as P

HEADS = 24
KV_HEADS = 8
HEAD_DIM = 64
GROUP = HEADS // KV_HEADS

EPSILON = 1e-05
ROPE_BASE = 1000000.0
PLANE = ("x", "y", "c")
SWAP = ((0, 1), (1, 0))
F32 = jnp.float32
BF16 = jnp.bfloat16
QK = (GROUP + 1) * HEAD_DIM
AUG = 2 * HEAD_DIM
GAIN_LANES = 64
ANY = pl.BlockSpec(memory_space=pl.ANY)


def scaled_norm(values, gain_row):
    mean_square = jnp.mean(values * values, axis=-1, keepdims=True)
    return values * lax.rsqrt(mean_square + EPSILON) * gain_row


def gating(gate_act, up_act):
    return gate_act * jax.nn.sigmoid(gate_act) * up_act


def dot(left, right, left_dim=1, right_dim=0):
    return lax.dot_general(
        left, right, (((left_dim,), (right_dim,)), ((), ())), preferred_element_type=F32
    )


def head_means(values):
    row = lax.broadcasted_iota(jnp.int32, (QK, QK), 0) // HEAD_DIM
    column = lax.broadcasted_iota(jnp.int32, (QK, QK), 1) // HEAD_DIM
    ones = jnp.where(row == column, 1.0 / HEAD_DIM, 0.0).astype(BF16)
    high = values.astype(BF16)
    rest = (values - high.astype(F32)).astype(BF16)
    return dot(high, ones) + dot(rest, ones)


def half_swap(values):
    lane = lax.broadcasted_iota(jnp.int32, values.shape, 1)
    ahead = pltpu.roll(values, QK - HEAD_DIM // 2, 1)
    behind = pltpu.roll(values, HEAD_DIM // 2, 1)
    return jnp.where(lane % HEAD_DIM < HEAD_DIM // 2, ahead, behind)


def unit_heads(raw):
    scale = lax.rsqrt(head_means(raw * raw) + EPSILON)
    return raw * scale, scale


def rotated(unit, gain, cosine, sine):
    normed = unit * gain
    return normed * cosine + half_swap(normed) * sine


def in_lanes(values, extras):
    rows = values.shape[0]
    lane = lax.broadcasted_iota(jnp.int32, (rows, HEAD_DIM), 1)
    tail = jnp.zeros((rows, HEAD_DIM), F32)
    rest = extras
    for part in range(3):
        high = rest.astype(BF16).astype(F32)
        tail = jnp.where(lane == part, high, tail)
        rest = rest - high
    return jnp.concatenate([values.astype(F32), tail], axis=1).astype(BF16)


def with_ones(values, count):
    rows = values.shape[0]
    lane = lax.broadcasted_iota(jnp.int32, (rows, HEAD_DIM), 1)
    return jnp.concatenate(
        [values.astype(F32), jnp.where(lane < count, 1.0, 0.0)], axis=1
    ).astype(BF16)


def block_at(place, block):
    away = jnp.bitwise_xor(place, block)
    core, y = jnp.bitwise_and(away, 1), lax.shift_right_logical(away, 1)
    pair = 2 * pl.program_id(1) + y
    return (4 * core + pair, 0), pair, core


def store_pair(refs, pair, core, values):
    for k, ref in enumerate(refs):

        @pl.when(pair == k)
        def _(ref=ref):
            ref[core, 0] = values


def load_pair(refs, pair, core):
    values = refs[0][core, 0]
    for k in range(1, 4):
        values = jnp.where(pair == k, refs[k][core, 0], values)
    return values


def attend_forward(place_ref, qkv_ref, gain_ref, cos_ref, sin_ref, *refs):
    *mixed_refs, stat_ref, keys, values = refs
    place = place_ref[0]
    tokens = qkv_ref.shape[2]
    gain = gain_ref[...]
    row = lax.broadcasted_iota(jnp.int32, (tokens, tokens), 0)
    column = lax.broadcasted_iota(jnp.int32, (tokens, tokens), 1)
    causal = row >= column
    lane = lax.broadcasted_iota(jnp.int32, (tokens, AUG), 1)
    for block in range(4):
        source, pair, core = block_at(place, block)
        here = pl.ds(block * tokens, tokens)
        raw = qkv_ref[source]
        unit, _ = unit_heads(raw[:, :QK].astype(F32))
        turned = rotated(unit, gain, cos_ref[here], sin_ref[here])
        keys[here] = turned[:, GROUP * HEAD_DIM :].astype(BF16)
        values[here] = with_ones(raw[:, QK:], 1)
        outs = []
        stats = jnp.zeros((tokens, AUG), F32)
        for head in range(GROUP):
            query = turned[:, head * HEAD_DIM : (head + 1) * HEAD_DIM].astype(BF16) * BF16(
                HEAD_DIM**-0.5
            )
            weights = jnp.exp(dot(query, keys[here], 1, 1))
            total = dot(jnp.where(causal, weights, 0.0).astype(BF16), values[here])
            if block:
                before = pl.ds(0, block * tokens)
                weights = jnp.exp(dot(query, keys[before], 1, 1))
                total = total + dot(weights.astype(BF16), values[before])
            rows_total = total[:, HEAD_DIM : HEAD_DIM + 1]
            outs.append(total[:, :HEAD_DIM] / rows_total)
            stats = jnp.where(lane == head, jnp.log(rows_total), stats)
        store_pair(mixed_refs, pair, core, jnp.concatenate(outs, axis=1).astype(BF16))
        stat_ref[source] = stats


def attend_backward(place_ref, qkv_ref, grad_ref, stat_ref, *refs):
    *mixed_refs, gain_ref, cos_ref, sin_ref = refs[:7]
    *out_refs, gain_grad_ref, keys, values, key_grads, value_grads, query_grads = refs[7:]
    place = place_ref[0]
    tokens = qkv_ref.shape[2]
    gain = gain_ref[...]
    key_row = lax.broadcasted_iota(jnp.int32, (tokens, tokens), 0)
    query_row = lax.broadcasted_iota(jnp.int32, (tokens, tokens), 1)
    causal = query_row >= key_row
    key_grads[...] = jnp.zeros_like(key_grads)
    value_grads[...] = jnp.zeros_like(value_grads)
    for block in range(4):
        source, pair, core = block_at(place, block)
        here = pl.ds(block * tokens, tokens)
        raw = qkv_ref[source]
        unit, _ = unit_heads(raw[:, :QK].astype(F32))
        turned = rotated(unit, gain, cos_ref[here], sin_ref[here])
        keys[here] = with_ones(turned[:, GROUP * HEAD_DIM :].astype(BF16), 3)
        values[here] = with_ones(raw[:, QK:], 3)
        grads = grad_ref[source].astype(F32)
        product = load_pair(mixed_refs, pair, core).astype(F32) * grads
        stats = stat_ref[source]
        for head in range(GROUP):
            lanes = slice(head * HEAD_DIM, (head + 1) * HEAD_DIM)
            query = in_lanes(
                turned[:, lanes].astype(BF16).astype(F32) * HEAD_DIM**-0.5,
                -stats[:, head : head + 1],
            )
            grad = in_lanes(grads[:, lanes], -jnp.sum(product[:, lanes], axis=1, keepdims=True))
            query_total = jnp.zeros((tokens, AUG), F32)
            for span, masked in ((pl.ds(0, block * tokens), False), (here, True)):
                if span.size == 0:
                    continue
                probs = jnp.exp(dot(keys[span], query, 1, 1))
                if masked:
                    probs = jnp.where(causal, probs, 0.0)
                score_grad = (probs * dot(values[span], grad, 1, 1)).astype(BF16)
                value_grads[span] += dot(probs.astype(BF16), grad)
                key_grads[span] += dot(score_grad, query)
                query_total = query_total + dot(score_grad, keys[span], 0, 0)
            query_grads[here, lanes] = query_total[:, :HEAD_DIM] * HEAD_DIM**-0.5
    gain_total = jnp.zeros((1, QK), F32)
    for block in range(4):
        source, pair, core = block_at(place, block)
        here = pl.ds(block * tokens, tokens)
        raw = qkv_ref[source]
        unit, scale = unit_heads(raw[:, :QK].astype(F32))
        grads = jnp.concatenate(
            [query_grads[here, : GROUP * HEAD_DIM], key_grads[here, :HEAD_DIM]], axis=1
        )
        grads = grads.astype(BF16).astype(F32)
        back = grads * cos_ref[here] + half_swap(grads * sin_ref[here])
        gain_total = gain_total + jnp.sum(back * unit, axis=0, keepdims=True)
        scaled = back * gain
        raw_grad = scale * (scaled - unit * head_means(scaled * unit))
        grads = jnp.concatenate([raw_grad, value_grads[here, :HEAD_DIM]], axis=1)
        store_pair(out_refs, pair, core, grads.astype(BF16))
    gain_grad_ref[...] = jnp.broadcast_to(gain_total[None], gain_grad_ref.shape)


def attention_call(kernel, name, place, blocked, whole, outs, scratch, deps, passes, share):
    batch = blocked[0].shape[1]

    def spec(shape):
        if len(shape) == 4:
            return pl.BlockSpec(
                (shape[0], 1) + tuple(shape[2:]), lambda i, j, *_: (0, i, 0, 0)
            )
        return pl.BlockSpec((1,) + tuple(shape[1:]), lambda i, j, *_: (2 * i + j, 0, 0))

    inputs = len(blocked) + len(whole)
    tokens = blocked[0].shape[2]
    flops = passes * 2 * batch * GROUP * (4 * tokens) ** 2 * AUG

    def body(place_ref, *refs):
        kernel(place_ref, *refs[:inputs], *refs[inputs + len(deps) :])

    return pl.pallas_call(
        body,
        grid_spec=pltpu.PrefetchScalarGridSpec(
            num_scalar_prefetch=1,
            grid=(batch, 2),
            in_specs=[spec(a.shape) for a in blocked]
            + [pl.BlockSpec(a.shape, lambda i, j, *_: (0, 0)) for a in whole]
            + [ANY] * len(deps),
            out_specs=[spec(o.shape) for o in outs],
            scratch_shapes=scratch,
        ),
        out_shape=outs,
        name=name,
        cost_estimate=cost(flops, share),
        compiler_params=pltpu.CompilerParams(vmem_limit_bytes=48 << 20),
    )(place, *blocked, *whole, *deps)


def forward_attention(place, qkv, gain, cosine, sine, deps=()):
    batch, tokens = qkv.shape[1:3]
    length = 4 * tokens
    *mixed, stats = attention_call(
        attend_forward,
        "attend_forward",
        place,
        [qkv],
        [gain, cosine, sine],
        [jax.ShapeDtypeStruct((2, batch, tokens, GROUP * HEAD_DIM), BF16)] * 4
        + [jax.ShapeDtypeStruct((8, batch, tokens, AUG), F32)],
        [pltpu.VMEM((length, HEAD_DIM), BF16), pltpu.VMEM((length, AUG), BF16)],
        deps,
        14,
        0.0,
    )
    return mixed, stats


def backward_attention(place, qkv, mixed, grads, stats, gain, cosine, sine, deps=()):
    batch, tokens = qkv.shape[1:3]
    length = 4 * tokens
    *qkv_grads, head_part = attention_call(
        attend_backward,
        "attend_backward",
        place,
        [qkv, grads, stats, *mixed],
        [gain, cosine, sine],
        [jax.ShapeDtypeStruct((2,) + qkv.shape[1:], BF16)] * 4
        + [jax.ShapeDtypeStruct((2 * batch, 8, QK), F32)],
        [
            pltpu.VMEM((length, AUG), BF16),
            pltpu.VMEM((length, AUG), BF16),
            pltpu.VMEM((length, AUG), F32),
            pltpu.VMEM((length, AUG), F32),
            pltpu.VMEM((length, GROUP * HEAD_DIM), F32),
        ],
        deps,
        34,
        0.0,
    )
    return qkv_grads, head_part


def rotary_rows(length):
    half = HEAD_DIM // 2
    exponent = jnp.arange(half).astype(F32) * (2.0 / HEAD_DIM)
    frequency = jnp.power(F32(ROPE_BASE), -exponent)
    angles = jnp.arange(length).astype(F32)[:, None] * frequency[None, :]

    def body(cos_ref, sin_ref, cos_out, sin_out):
        cosine, sine = cos_ref[...], sin_ref[...]
        heads = QK // HEAD_DIM
        cos_out[...] = jnp.concatenate([cosine, cosine] * heads, axis=1)
        sin_out[...] = jnp.concatenate([-sine, sine] * heads, axis=1)

    return pl.pallas_call(
        body,
        out_shape=[jax.ShapeDtypeStruct((length, QK), F32)] * 2,
        name="rotary_rows",
        cost_estimate=cost(0),
    )(jnp.cos(angles), jnp.sin(angles))


TILE = 256


def cost(flops, share=0.0):
    return pl.CostEstimate(flops=int(flops * share) + 1, bytes_accessed=1, transcendentals=0)


def rows_of(sides):
    return sum(side.shape[0] for side in sides)


def side_specs(counts, width, tile=TILE):
    specs, bounds, first = [], [], 0
    for count in counts:

        def index(i, first=first, count=count):
            return (jnp.clip(i - first, 0, count - 1), 0)

        specs.append(pl.BlockSpec((tile, width), index))
        bounds.append((first, first + count))
        first += count
    return specs, bounds


def tiles_of(sides, tile=TILE):
    return [side.shape[0] // tile for side in sides]


def on_side(bounds, run):
    step = pl.program_id(0)
    for k, (first, last) in enumerate(bounds):
        pl.when(jnp.logical_and(step >= first, step < last))(lambda k=k: run(k))


def norm_project(sides, gains, weight, width, deps=()):
    depth = sides[0].shape[1]
    rows = rows_of(sides)
    specs, bounds = side_specs(tiles_of(sides), depth)
    lanes = -(-width // 128) * 128
    count = len(sides)

    def body(*refs):
        gain_ref, weight_ref = refs[count : count + 2]
        normed_ref, out_ref = refs[count + 2 + len(deps) :]

        def run(k):
            normed = scaled_norm(refs[k][...].astype(F32), gain_ref[:1].astype(F32)).astype(BF16)
            normed_ref[...] = normed
            out_ref[...] = dot(normed, weight_ref[...])[:, :width].astype(BF16)

        on_side(bounds, run)

    return pl.pallas_call(
        body,
        grid=(rows // TILE,),
        in_specs=specs
        + [
            pl.BlockSpec(gains.shape, lambda i: (0, 0)),
            pl.BlockSpec((depth, lanes), lambda i: (0, 0)),
        ]
        + [ANY] * len(deps),
        out_specs=[
            pl.BlockSpec((TILE, depth), lambda i: (i, 0)),
            pl.BlockSpec((TILE, width), lambda i: (i, 0)),
        ],
        out_shape=[
            jax.ShapeDtypeStruct((rows, depth), BF16),
            jax.ShapeDtypeStruct((rows, width), BF16),
        ],
        name="norm_project",
        cost_estimate=cost(0),
        compiler_params=pltpu.CompilerParams(vmem_limit_bytes=48 << 20),
    )(*sides, gains, weight, *deps)


def feed_forward(post, grads, weight, total=None, deps=()):
    depth = post[0].shape[1]
    rows = rows_of(post)
    width = weight.shape[1] // 3
    count = len(post)
    totals = [] if total is None else [total]
    specs, bounds = side_specs(tiles_of(post), depth)

    def body(*refs):
        weight_ref = refs[2 * count]
        both_ref, act_ref, out_ref = refs[2 * count + 1 + len(totals) + len(deps) :]

        def run(k):
            hidden = dot(refs[k][...], weight_ref[:, : 2 * width])
            act_grad = dot(refs[count + k][...], weight_ref[:, 2 * width :])
            gate, up = hidden[:, :width], hidden[:, width:]
            sig = 1.0 / (1.0 + jnp.exp(-gate))
            silu = gate * sig
            act_ref[...] = (silu * up).astype(BF16)
            both = jnp.concatenate(
                [act_grad * up * (sig + silu * (1.0 - sig)), act_grad * silu], axis=1
            ).astype(BF16)
            both_ref[...] = both
            part = dot(both, weight_ref[:, : 2 * width], 1, 1)
            if totals:
                part = refs[2 * count + 1][...].astype(F32) + part
            out_ref[...] = part.astype(BF16)

        on_side(bounds, run)

    widths = (2 * width, width, depth)
    tile = [pl.BlockSpec((TILE, w), lambda i: (i, 0)) for w in widths]
    return pl.pallas_call(
        body,
        grid=(rows // TILE,),
        in_specs=specs * 2 + [entire(weight)] + tile[2:] * len(totals) + [ANY] * len(deps),
        out_specs=tile,
        out_shape=[jax.ShapeDtypeStruct((rows, w), BF16) for w in widths],
        name="feed_forward",
        cost_estimate=cost(0),
        compiler_params=pltpu.CompilerParams(vmem_limit_bytes=56 << 20),
    )(*post, *grads, weight, *totals, *deps)


def matches(lefts, rights, paired):
    def cuts(arrays):
        places, total = [], 0
        for k, array in enumerate(arrays):
            places.append((total, total + array.shape[0], k))
            total += array.shape[0]
        return places

    if paired:
        rows = rights[0].shape[0] // 2
        others = [
            ((4 * core + pair) * rows, (4 * core + pair + 1) * rows, pair, core * rows)
            for core in range(2)
            for pair in range(4)
        ]
    else:
        others = [(first, last, k, 0) for first, last, k in cuts(rights)]
    spans = []
    for first, last, l in cuts(lefts):
        for start, stop, r, offset in others:
            low, high = max(first, start), min(last, stop)
            if low < high:
                spans.append(((l, low - first), (r, low - start + offset), high - low))
    return spans


def weight_grads(pairs, deps=(), tile=256, gains=None, paired=False):
    depth = pairs[0][0][0].shape[1]
    widths = [rights[0].shape[1] for _, rights in pairs]
    others = 0 if gains is None else gains[1].shape[1]
    lanes = -(-(sum(widths) + others) // 128) * 128

    def head_column(sums, held, depth):
        parts = [sums[:, k * HEAD_DIM : (k + 1) * HEAD_DIM] for k in range(GROUP + 1)]
        sums = jnp.concatenate([sum(parts[1:GROUP], parts[0]), parts[GROUP]], axis=1)
        span = depth * held // sums.shape[1]
        row = lax.broadcasted_iota(jnp.int32, (tile, sums.shape[1]), 0) + pl.program_id(0) * tile
        column = lax.broadcasted_iota(jnp.int32, (tile, sums.shape[1]), 1)
        here = jnp.logical_and(row // span == column // held, row % span == column % held)
        return jnp.sum(jnp.where(here, sums, 0.0), axis=1, keepdims=True)

    def body(*refs):
        out = refs[-1]
        line = []
        at = 0
        for index, (lefts, rights) in enumerate(pairs):
            value = None
            left_refs = refs[at : at + len(lefts)]
            at += len(lefts)
            right_refs = refs[at : at + len(rights)]
            at += len(rights)
            for (l, left_first), (r, right_first), count in matches(lefts, rights, paired):
                left = left_refs[l][left_first : left_first + count]
                right = right_refs[r][right_first : right_first + count]
                part = dot(left, right, 0, 0)
                value = part if value is None else value + part
            line.append(value)
            if index == 0 and gains is not None:
                weight, rest, heads = refs[spec_count : spec_count + 3]
                width = widths[0]
                scaled = jnp.sum(weight[:, :width].astype(F32) * value, axis=1, keepdims=True)
                scaled = scaled / weight[:, width : width + 1].astype(F32)
                lane = lax.broadcasted_iota(jnp.int32, rest.shape, 1)
                column = head_column(jnp.sum(heads[...], axis=0)[:1], gains[3], depth)
                values = jnp.where(lane == 2, column, rest[...])
                line.append(jnp.where(lane == 0, scaled, values))
        if lanes > sum(widths) + others:
            line.append(jnp.zeros((tile, lanes - sum(widths) - others), F32))
        out[...] = jnp.concatenate(line, axis=1).astype(BF16)

    specs, args, flops = [], [], 0
    for lefts, rights in pairs:
        specs += [pl.BlockSpec((left.shape[0], tile), lambda i: (0, i)) for left in lefts]
        specs += [pl.BlockSpec(right.shape, lambda i: (0, 0)) for right in rights]
        args += [*lefts, *rights]
        flops += 4 * rows_of(lefts) * depth * rights[0].shape[1]
    spec_count = len(specs)
    if gains is not None:
        for array in gains[:2]:
            specs.append(pl.BlockSpec((tile, array.shape[1]), lambda i: (i, 0)))
            args.append(array)
        specs.append(pl.BlockSpec(gains[2].shape, lambda i: (0, 0, 0)))
        args.append(gains[2])
    return pl.pallas_call(
        body,
        grid=(depth // tile,),
        in_specs=specs + [ANY] * len(deps),
        out_specs=pl.BlockSpec((tile, lanes), lambda i: (i, 0)),
        out_shape=jax.ShapeDtypeStruct((depth, lanes), BF16),
        name="weight_grads",
        cost_estimate=cost(0),
        compiler_params=pltpu.CompilerParams(vmem_limit_bytes=56 << 20),
    )(*args, *deps)


def project_back(lefts, weights, turns, deps=()):
    number = len(weights)
    sides = lefts[0]
    count = len(sides)
    tile = 2 * TILE
    counts = tiles_of(sides, tile)
    depth = weights[0].shape[1] if len(turns[0]) == 2 else weights[0].shape[0]
    _, bounds = side_specs(counts, depth, tile)

    def body(*refs):
        weight_refs = refs[number * count : number * count + number]
        outs = refs[number * count + number + len(deps) :]

        def run(k):
            total = None
            for i, turn in enumerate(turns):
                left = refs[i * count + k][...]
                if len(turn) == 2:
                    part = dot(left, weight_refs[i][turn[0] : turn[1]])
                else:
                    part = dot(left, weight_refs[i][:, turn[0] : turn[1]], 1, 1)
                total = part if total is None else total + part
            outs[k][...] = total.astype(BF16)

        on_side(bounds, run)

    widths = [left[0].shape[1] for left in lefts]
    return pl.pallas_call(
        body,
        grid=(sum(counts),),
        in_specs=[spec for w in widths for spec in side_specs(counts, w, tile)[0]]
        + [pl.BlockSpec(w.shape, lambda i: (0, 0)) for w in weights]
        + [ANY] * len(deps),
        out_specs=side_specs(counts, depth, tile)[0],
        out_shape=[jax.ShapeDtypeStruct((side.shape[0], depth), BF16) for side in sides],
        name="project_back",
        cost_estimate=cost(0),
        compiler_params=pltpu.CompilerParams(vmem_limit_bytes=56 << 20),
    )(*[side for left in lefts for side in left], *weights, *deps)


def row_tiles(array, first=0, tile=TILE):
    return pl.BlockSpec((tile, array.shape[1]), lambda i: (first // tile + i, 0))


def entire(array):
    return pl.BlockSpec(array.shape, lambda i: (0,) * len(array.shape))


def from_pairs(refs, weights):
    total = None
    for ref, weight in zip(refs, weights):
        part = dot(ref[...], weight[...])
        total = part if total is None else total + part
    return total


def pair_specs(pairs):
    near, far = pairs
    rows = far.shape[0] // 4
    return [row_tiles(pair) for pair in near] + [row_tiles(far, k * rows) for k in range(4)]


def pair_args(pairs):
    return [*pairs[0], *[pairs[1]] * 4]


def attend_out(pairs, weights, hidden, gains):
    rows, depth = hidden.shape

    def body(*refs):
        hidden_ref, gain_ref, middle_ref, post_ref = refs[16:]
        middle = hidden_ref[...].astype(F32) + from_pairs(refs[:8], refs[8:16])
        middle_ref[...] = middle
        post_ref[...] = scaled_norm(middle, gain_ref[1:2].astype(F32)).astype(BF16)

    return pl.pallas_call(
        body,
        grid=(rows // TILE,),
        in_specs=pair_specs(pairs)
        + [entire(w) for w in weights]
        + [row_tiles(hidden), entire(gains)],
        out_specs=[row_tiles(hidden)] * 2,
        out_shape=[
            jax.ShapeDtypeStruct((rows, depth), F32),
            jax.ShapeDtypeStruct((rows, depth), BF16),
        ],
        name="attend_out",
        cost_estimate=cost(0),
        compiler_params=pltpu.CompilerParams(vmem_limit_bytes=48 << 20),
    )(*pair_args(pairs), *weights, hidden, gains)


def norm_back(values, gain, grads):
    scale = lax.rsqrt(jnp.mean(values * values, axis=-1, keepdims=True) + EPSILON)
    unit = values * scale
    scaled = grads * gain
    return scale * (scaled - unit * jnp.mean(scaled * unit, axis=-1, keepdims=True)), unit


def middle_back(mine, others, middle, upstream, weights, gains, deps=()):
    rows, depth = middle.shape
    width = weights[0].shape[0]

    def body(*refs):
        mine_ref, first, second, third, middle_ref, up_ref = refs[:6]
        weight_refs, gain_ref = refs[6:14], refs[14]
        grad_ref, low_ref, *pair_refs, sum_ref = refs[15 + len(deps) :]
        post_grad = mine_ref[...]
        for ref in (first, second, third):
            post_grad = post_grad + ref[...].astype(F32)
        back, unit = norm_back(middle_ref[...], gain_ref[1:2].astype(F32), post_grad)
        grad = up_ref[...].astype(F32) + back
        grad_ref[...] = grad
        low = grad.astype(BF16)
        low_ref[...] = low
        for k in range(4):
            pair_refs[k][0] = dot(low, weight_refs[k][...], 1, 1).astype(BF16)
            pair_refs[k][1] = dot(low, weight_refs[4 + k][...], 1, 1).astype(BF16)
        total = jnp.sum(post_grad * unit, axis=0, keepdims=True)

        @pl.when(pl.program_id(0) == 0)
        def _():
            sum_ref[...] = jnp.zeros_like(sum_ref)

        sum_ref[...] += jnp.broadcast_to(total, sum_ref.shape)

    side = pl.BlockSpec((2, TILE, width), lambda i: (0, i, 0))
    return pl.pallas_call(
        body,
        grid=(rows // TILE,),
        in_specs=[row_tiles(a) for a in (mine, *others, middle, upstream)]
        + [entire(w) for w in weights]
        + [entire(gains)]
        + [ANY] * len(deps),
        out_specs=[row_tiles(middle)] * 2
        + [side] * 4
        + [pl.BlockSpec((8, depth), lambda i: (0, 0))],
        out_shape=[
            jax.ShapeDtypeStruct((rows, depth), F32),
            jax.ShapeDtypeStruct((rows, depth), BF16),
            *[jax.ShapeDtypeStruct((2, rows, width), BF16)] * 4,
            jax.ShapeDtypeStruct((8, depth), F32),
        ],
        name="middle_back",
        cost_estimate=cost(0),
        compiler_params=pltpu.CompilerParams(vmem_limit_bytes=48 << 20),
    )(mine, *others, middle, upstream, *weights, gains, *deps)


def input_back(pairs, weights, hidden, grads, gains, deps=()):
    rows, depth = hidden.shape

    def body(*refs):
        hidden_ref, grad_ref, gain_ref = refs[16:19]
        product = from_pairs(refs[:8], refs[8:16])
        gain = gain_ref[:1].astype(F32)
        refs[-1][...] = grad_ref[...] + norm_back(hidden_ref[...].astype(F32), gain, product)[0]

    return pl.pallas_call(
        body,
        grid=(rows // TILE,),
        in_specs=pair_specs(pairs)
        + [entire(w) for w in weights]
        + [row_tiles(hidden), row_tiles(grads), entire(gains)]
        + [ANY] * len(deps),
        out_specs=row_tiles(grads),
        out_shape=jax.ShapeDtypeStruct((rows, depth), F32),
        name="input_back",
        cost_estimate=cost(0),
        compiler_params=pltpu.CompilerParams(vmem_limit_bytes=48 << 20),
    )(*pair_args(pairs), *weights, hidden, grads, gains, *deps)


def core_sum(near, far):
    rows, width = near.shape[0] // 4, near.shape[1]

    def body(near_ref, far_ref, *outs):
        for part, out in enumerate(outs):

            @pl.when(pl.program_id(0) == part)
            def _(out=out):
                out[...] = (near_ref[...].astype(F32) + far_ref[...].astype(F32)).astype(out.dtype)

    tile = pl.BlockSpec((rows, width), lambda i: (i, 0))
    return pl.pallas_call(
        body,
        grid=(4,),
        in_specs=[tile, tile],
        out_specs=[pl.BlockSpec((rows, width), lambda i: (0, 0))] * 4,
        out_shape=[
            jax.ShapeDtypeStruct((rows, width), dtype) for dtype in (F32, BF16, BF16, BF16)
        ],
        name="core_sum",
        cost_estimate=cost(0),
        compiler_params=pltpu.CompilerParams(vmem_limit_bytes=48 << 20),
    )(near, far)


def turn(weight, spans):
    def body(ref, *outs):
        turned = ref[...].T
        for (first, last), out in zip(spans, outs):
            out[...] = turned[first:last]

    return pl.pallas_call(
        body,
        out_shape=[
            jax.ShapeDtypeStruct((last - first, weight.shape[0]), weight.dtype)
            for first, last in spans
        ],
        name="turn",
        cost_estimate=cost(0),
        compiler_params=pltpu.CompilerParams(vmem_limit_bytes=48 << 20),
    )(weight)


def pack_columns(weights, layouts, extra=None):
    rows = weights[0].shape[0]
    count = len(weights)
    spans = [w.shape[1] // 8 for w in weights]
    extras = [] if extra is None else [extra]

    def body(*refs):
        outs = refs[count + len(extras) :]
        for place in range(8):
            x, s = place // 4, place % 4
            for out, layout in zip(outs, layouts):
                line = []
                for entry in layout:
                    if entry is None:
                        line.append(refs[count][...].astype(F32))
                    elif isinstance(entry, int):
                        line.append(jnp.zeros((rows, entry), F32))
                    else:
                        index, first, last = entry
                        start = (2 * s + x) * spans[index]
                        line.append(refs[index][:, start + first : start + last].astype(F32))
                out[place] = jnp.concatenate(line, axis=1).astype(BF16)

    def lanes(entry):
        if entry is None:
            return extra.shape[1]
        return entry if isinstance(entry, int) else entry[2] - entry[1]

    return pl.pallas_call(
        body,
        out_shape=[
            jax.ShapeDtypeStruct((8, rows, sum(lanes(e) for e in layout)), BF16)
            for layout in layouts
        ],
        name="pack_columns",
        compiler_params=pltpu.CompilerParams(vmem_limit_bytes=48 << 20),
    )(*weights, *extras)


def unpack_columns(x, sums, others, outputs, dtype=F32):
    rows = others[0].shape[0]
    count = len(sums)
    *pairs, summed = outputs

    def body(x_ref, *refs):
        own, other, outs = refs[:count], refs[count : 2 * count], refs[2 * count :]

        def write(left, right):
            for out, entries in zip(outs, pairs):
                line = [left[i][:, first:last].astype(F32) for i, first, last in entries]
                line += [right[i][:, first:last].astype(F32) for i, first, last in entries]
                out[...] = jnp.concatenate(line, axis=1)

        pl.when(x_ref[0] == 0)(lambda: write(own, other))
        pl.when(x_ref[0] != 0)(lambda: write(other, own))
        if summed is not None:
            i, first, last = summed
            outs[-1][...] = own[i][:, first:last].astype(F32) + other[i][:, first:last].astype(F32)

    widths = [2 * sum(last - first for _, first, last in entries) for entries in pairs]
    if summed is not None:
        widths.append(summed[2] - summed[1])
    return pl.pallas_call(
        body,
        grid_spec=pltpu.PrefetchScalarGridSpec(
            num_scalar_prefetch=1,
            grid=(1,),
            in_specs=[
                pl.BlockSpec((rows, a.shape[1]), lambda i, x_ref: (x_ref[0], 0)) for a in sums
            ]
            + [pl.BlockSpec(a.shape, lambda i, x_ref: (0, 0)) for a in others],
            out_specs=[pl.BlockSpec((rows, w), lambda i, x_ref: (0, 0)) for w in widths],
        ),
        out_shape=[jax.ShapeDtypeStruct((rows, w), F32) for w in widths],
        name="unpack_columns",
        compiler_params=pltpu.CompilerParams(vmem_limit_bytes=48 << 20),
    )(x, *sums, *others)


def after(values, *deps):
    def body(*refs):
        pass

    return pl.pallas_call(
        body,
        in_specs=[ANY] * (1 + len(deps)),
        out_specs=ANY,
        out_shape=jax.ShapeDtypeStruct(values.shape, values.dtype),
        input_output_aliases={0: 0},
        name="after",
    )(values, *deps)


def swap(values, axis):
    return lax.ppermute(values, axis, SWAP)


def plane_near(rows):
    return [rows, *diamond(rows, rows, rows)], swap(rows, "c")


def plane_all(gathered):
    near, first = gathered
    return near + [first] + [swap(piece, "c") for piece in near[1:]]


def staged_gather(rows, between=()):
    half = rows.shape[0] // 2
    from_y = swap(rows, "y")
    if between:
        from_y = after(from_y, *between)
    from_x = swap(rows, "x")
    corner = jnp.concatenate([swap(from_y[:half], "x"), swap(from_x[half:], "y")])
    near = [rows, from_y, from_x, corner]
    return near + [swap(piece, "c") for piece in near]


def diamond(for_y, for_x, for_both):
    across = lax.ppermute(for_both, ("x", "y"), ((0, 3), (1, 2), (2, 1), (3, 0)))
    return swap(for_y, "y"), swap(for_x, "x"), across


def exchange_near(pairs):
    return [pairs[0], *diamond(*pairs[1:])]


def exchange_all(came):
    rows = came[0].shape[0] // 2
    return came, swap(jnp.concatenate([pair[rows:] for pair in came]), "c")


def scatter_end(mine, others):
    for other in others:
        mine = mine + other.astype(F32)
    return mine


def line_gather(block):
    return lax.all_gather(block, "dp", axis=0, tiled=True)


def line_scatter(parts):
    return lax.psum_scatter(parts, "dp", scatter_dimension=0, tiled=True)


def together(work, *operands):
    shapes = jax.eval_shape(work, *operands)

    def skip(*_):
        return jax.tree.map(lambda shape: jnp.zeros(shape.shape, shape.dtype), shapes)

    return lax.cond(lax.axis_index("x") < 2, work, skip, *operands)


def plane_columns(payload):
    out = lax.all_to_all(payload, PLANE, split_axis=0, concat_axis=0, tiled=True)
    return out.reshape(-1, payload.shape[2])


def from_x(sums):
    rows = sums.shape[0] // 2
    place = lax.axis_index("x")
    return swap(lax.dynamic_slice_in_dim(sums, (1 - place) * rows, rows, 0), "x")


def on_device(
    layer_input,
    attention_gain,
    query_weight,
    key_weight,
    value_weight,
    output_weight,
    head_gains,
    feedforward_gain,
    gate_weight,
    up_weight,
    down_weight,
    upstream,
):
    batch, tokens, model_width = layer_input.shape
    rows = query_weight.shape[0]
    own_rows = batch * tokens
    head_rows = head_gains.shape[0]
    query_cols = query_weight.shape[1] // 8
    kv_cols = key_weight.shape[1] // 8
    qkv_cols = query_cols + 2 * kv_cols
    wide = gate_weight.shape[1] // 8
    place = (2 * lax.axis_index("y") + lax.axis_index("c")).astype(jnp.int32).reshape(1)

    gain_rows = jnp.stack(
        [attention_gain, feedforward_gain, jnp.pad(head_gains, (0, rows - head_rows))], axis=1
    )
    gain_rows = jnp.pad(gain_rows, ((0, 0), (0, GAIN_LANES - 3)))
    own_hidden = layer_input.reshape(own_rows, model_width)
    own_upstream = upstream.reshape(own_rows, model_width)
    cut = 640
    rest = -(wide - cut) % 128
    (first_payload,) = pack_columns(
        [query_weight, key_weight, value_weight, output_weight],
        [
            [(0, 0, query_cols), (1, 0, kv_cols), (2, 0, kv_cols), None, (3, 0, query_cols)]
            + [GAIN_LANES]
        ],
        gain_rows,
    )
    first_block = plane_columns(first_payload)
    first_full = line_gather(first_block)
    (second_payload,) = pack_columns(
        [gate_weight, up_weight, down_weight],
        [
            [(0, 0, cut), (1, 0, cut), (2, 0, cut)]
            + [(0, cut, wide), rest, (1, cut, wide), rest, (2, cut, wide), rest],
        ],
    )

    second_block = plane_columns(after(second_payload, first_block))
    ffn_blocks = [second_block[:, : 3 * cut], second_block[:, 3 * cut :]]
    ffn_full = [line_gather(block) for block in ffn_blocks]

    def begin(own_hidden):
        tables = rotary_rows(4 * tokens)
        return staged_gather(own_hidden, tables), tables

    hidden, (cosine, sine) = together(begin, after(own_hidden, *ffn_blocks))

    out_first = qkv_cols + GAIN_LANES
    qkv_rows, gain_turned, out_rows = turn(
        first_full,
        [(0, qkv_cols), (qkv_cols, qkv_cols + 16), (out_first, out_first + query_cols)],
    )
    head_scale = gain_turned[2].astype(F32).reshape(-1, rows)[:, :head_rows].reshape(-1)
    head_scale = jnp.concatenate(
        [jnp.tile(head_scale[:HEAD_DIM], GROUP), head_scale[HEAD_DIM:]]
    ).reshape(1, QK)

    def attend(hidden, gain_turned, first_full, out_rows, head_scale, cosine, sine):
        out_near, out_first = plane_near(out_rows)
        normed, qkv = norm_project(hidden, gain_turned, first_full, qkv_cols)
        qkv = qkv.reshape(8, batch, tokens, qkv_cols)
        mixed, stats = forward_attention(place, qkv, head_scale, cosine, sine)
        return out_near[1:], out_first, normed, qkv, mixed, stats

    out_near, out_own, normed, qkv, mixed, stats = together(
        attend,
        hidden,
        gain_turned,
        first_full,
        out_rows,
        head_scale,
        cosine,
        sine,
    )

    out_weights = [out_rows, *out_near], out_own

    def attended(mixed, out_weights, own_hidden, own_upstream, gain_turned):
        came = exchange_near([pair.reshape(-1, query_cols) for pair in mixed])
        grads = staged_gather(own_upstream)
        out_weights = plane_all(out_weights)
        middle, post = attend_out(exchange_all(came), out_weights, own_hidden, gain_turned)
        return middle, staged_gather(post)[1:], grads[1:], post, out_weights[5:]

    middle, post, grads, post_own, out_far = together(
        attended, mixed, out_weights, own_hidden, own_upstream, gain_turned
    )
    post, grads = [post_own] + post, [own_upstream] + grads
    out_weights = [*out_weights[0], out_weights[1], *out_far]

    def first_chunk(post, grads, weight, qkv_rows):
        qkv_near, qkv_first = plane_near(qkv_rows)
        near = feed_forward(post[:4], grads[:4], weight)
        far = feed_forward(post[4:], grads[4:], weight)
        both, act, total = zip(near, far)
        return both, act, total, weight_grads([(post, both), (grads, act)]), (
            qkv_near[1:],
            qkv_first,
        )

    both_0, act_0, total, parts_0, (qkv_near, qkv_first) = together(
        first_chunk, post, grads, ffn_full[0], qkv_rows
    )
    sums_0 = line_scatter(parts_0)
    far = feed_forward(post[4:], grads[4:], ffn_full[1], total[1], deps=[parts_0])
    near = feed_forward(post[:4], grads[:4], ffn_full[1], total[0], deps=far[2:])
    both_1, act_1, (near, far) = zip(near, far)
    mine, *parts = core_sum(near, swap(far, "c"))

    def behind(parts, post, grads, act_0, act_1, both_1, weights):
        others = diamond(*parts)
        columns = [(2 * weight.shape[1] // 3, weight.shape[1], True) for weight in weights]
        branch = project_back([act_0, act_1], weights, columns)
        parts_1 = weight_grads([(post, both_1), (grads, act_1)])
        return others, parts_1, branch

    others, parts_1, branch = together(
        behind, parts, post, grads, act_0, act_1, both_1, ffn_full
    )
    middle_grad, middle_low, *pairs, feedforward_part = middle_back(
        mine, others, middle, own_upstream, out_weights, gain_turned
    )

    near, far = exchange_all(exchange_near([pair.reshape(-1, query_cols) for pair in pairs]))
    mixed_grad = jnp.concatenate([*[pair[:own_rows] for pair in near], far])

    def back(middle_low, qkv, mixed, mixed_grad, stats, head_scale, cosine, sine, branch):
        middle_near, middle_first = plane_near(middle_low)
        branch_far = swap(branch[1], "c")
        qkv_grad, head_part = backward_attention(
            place, qkv, mixed, mixed_grad, stats, head_scale, cosine, sine
        )
        return middle_near[1:], middle_first, qkv_grad, head_part, branch_far

    mixed_grad = mixed_grad.reshape(8, batch, tokens, query_cols)
    middle_near, middle_first, qkv_grad, head_part, branch_far = together(
        back, middle_low, qkv, mixed, mixed_grad, stats, head_scale, cosine, sine, branch
    )
    middle_whole = plane_all(([middle_low, *middle_near], middle_first))
    sums_1 = line_scatter(parts_1)
    gain_parts = after(feedforward_part, sums_0)
    gain_parts = jnp.pad(gain_parts[0][:, None], ((0, 0), (1, GAIN_LANES - 2)))

    def attention_grads(qkv_grad, normed, middle_whole, mixed, first_full, gain_parts, head_part):
        qkv_grad = [pair.reshape(-1, qkv_cols) for pair in qkv_grad]
        mixed = [pair.reshape(-1, query_cols) for pair in mixed]
        came = exchange_near(qkv_grad)
        parts = weight_grads(
            [([normed], qkv_grad), (middle_whole, mixed)],
            gains=(first_full, gain_parts, head_part, head_rows),
            paired=True,
        )
        return came[1:], parts

    came, attention_parts = together(
        attention_grads,
        qkv_grad,
        normed,
        middle_whole,
        mixed,
        first_full,
        gain_parts,
        head_part,
    )
    attention_sums = line_scatter(after(attention_parts, sums_1))
    x = lax.axis_index("x").astype(jnp.int32).reshape(1)

    branch_mine, *branch_parts = core_sum(branch[0], branch_far)
    qkv_pairs = exchange_all([qkv_grad[0].reshape(-1, qkv_cols), *came])
    qkv_weights = plane_all(([qkv_rows, *qkv_near], qkv_first))

    def finish(branch_parts, sums_0, sums_1, qkv_pairs, qkv_weights, own_hidden, middle_grad, gain_turned):
        branch_others = diamond(*branch_parts)
        others = from_x(sums_0), from_x(sums_1)
        input_grad = input_back(qkv_pairs, qkv_weights, own_hidden, middle_grad, gain_turned)
        return branch_others, others, input_grad

    branch_others, others, input_grad = together(
        finish,
        branch_parts,
        sums_0,
        sums_1,
        qkv_pairs,
        qkv_weights,
        own_hidden,
        middle_grad,
        gain_turned,
    )
    layer_output = (middle + scatter_end(branch_mine, branch_others)).astype(BF16)
    x = lax.axis_index("x").astype(jnp.int32).reshape(1)
    ffn_grads = unpack_columns(
        x,
        [sums_0, sums_1],
        others,
        [
            [
                (0, index * cut, (index + 1) * cut),
                (1, index * (wide - cut + rest), (index + 1) * (wide - cut + rest) - rest),
            ]
            for index in range(3)
        ]
        + [None],
    )

    attention_sums = after(attention_sums, layer_output, ffn_grads[0])
    key_first, value_first = query_cols, query_cols + kv_cols
    (
        query_weight_grad,
        key_weight_grad,
        value_weight_grad,
        output_weight_grad,
        gain_sums,
    ) = unpack_columns(
        x,
        [attention_sums],
        [from_x(attention_sums)],
        [
            [(0, 0, query_cols)],
            [(0, key_first, value_first)],
            [(0, value_first, qkv_cols)],
            [(0, out_first, out_first + query_cols)],
            (0, qkv_cols, qkv_cols + GAIN_LANES),
        ],
    )
    for axis in ("y", "c"):
        count = gain_sums.shape[0] // 2
        index = lax.axis_index(axis)
        keep = lax.dynamic_slice_in_dim(gain_sums, index * count, count, 0)
        send = lax.dynamic_slice_in_dim(gain_sums, (1 - index) * count, count, 0)
        gain_sums = keep + swap(send, axis)
    gain_sums = gain_sums[:, :3].T
    return (
        layer_output.reshape(layer_input.shape),
        input_grad.reshape(layer_input.shape),
        gain_sums[0],
        query_weight_grad,
        key_weight_grad,
        value_weight_grad,
        output_weight_grad,
        gain_sums[2, :head_rows],
        gain_sums[1],
        ffn_grads[0],
        ffn_grads[1],
        ffn_grads[2],
    )


def solution(mesh):
    fsdp, seq = mesh.shape["fsdp"], mesh.shape["seq"]
    plane_mesh = Mesh(mesh.devices.reshape(fsdp // 2, 2, seq // 2, 2), ("dp", "x", "y", "c"))
    batch = ("dp", "x")
    split = ("y", "c")
    rows = ("dp", "x", "y", "c")
    return jax.shard_map(
        on_device,
        mesh=plane_mesh,
        in_specs=(
            P(batch, split, None),
            P(rows),
            P(rows, None),
            P(rows, None),
            P(rows, None),
            P(rows, None),
            P(rows),
            P(rows),
            P(rows, None),
            P(rows, None),
            P(rows, None),
            P(batch, split, None),
        ),
        out_specs=(
            P(batch, split, None),
            P(batch, split, None),
            P(rows),
            P(batch, split),
            P(batch, split),
            P(batch, split),
            P(batch, split),
            P(rows),
            P(rows),
            P(batch, split),
            P(batch, split),
            P(batch, split),
        ),
        check_vma=False,
    )
```

time: 651 us -> 540 us (0.83)
  Pallas kernels: 47.5 us -> 204 us
  matrix products: 118 us -> 0 us
  waiting for transfers between devices: 246 us -> 160 us
  local copies, waits for them, and re-layouts: 100 us -> 41.5 us
  other arithmetic: 67.7 us -> 17.8 us
  blocking collectives: 0 us -> 43.1 us
    pallas_call x3 -> x26, Pallas kernels: 13.3 us -> 163 us  [the longest x4 55.8 us: feed_forward(): pl.pallas_call(body, grid=(rows // TILE,), in_specs=specs * 2 + [entire(w...]
    dot_general x19 -> x0, matrix products: 118 us -> none  [dot(): lax.dot_general(left, right, (((left_dim,), (right_dim,)), ((), ())), pre...]
    all_gather x3, waiting for transfers between devices: 51.8 us -> 0.04 us  [line_gather(): return lax.all_gather(block, 'dp', axis=0, tiled=True)]
    unnamed x149 -> x62, local copies, waits for them, and re-layouts: 60.4 us -> 12.5 us
    ppermute x0 -> x8, waiting for transfers between devices: none -> 45.4 us  [diamond(): lax.ppermute(for_both, ('x', 'y'), ((0, 3), (1, 2), (2, 1), (3, 0)))]
    all_to_all x0 -> x2, blocking collectives: none -> 43.1 us  [plane_columns(): lax.all_to_all(payload, PLANE, split_axis=0, concat_axis=0, tiled=True)]
    ppermute x46 -> x62, waiting for transfers between devices: 149 us -> 114 us  [swap(): return lax.ppermute(values, axis, SWAP)]
    all_to_all x3 -> x0, waiting for transfers between devices: 25.9 us -> none  [plane_columns(): lax.all_to_all(payload, PLANE, split_axis=0, concat_axis=0, tiled=True)]
  transfers between devices with their start and end apart: 56 -> 76, of which waited for: 32 -> 32; matrix products, arithmetic and copies ran while one was open for 40% -> 8% of each run, Pallas kernels for 4% -> 38%
where the time goes in v3:
time: 540 us; the launch traced here: 531 us
  Pallas kernels  204 us (38%)
  waiting for transfers between devices  160 us (30%)
  starting transfers between devices  49.3 us (9%)
  blocking collectives  43.1 us (8%)
  local copies, waits for them, and re-layouts  41.5 us (8%)
  other arithmetic  17.8 us (3%)
  between operations  14.7 us (3%)
    ppermute x62, waiting for transfers between devices, swap(): return lax.ppermute(values, axis, SWAP)  114 us
    pallas_call x4, Pallas kernels, feed_forward(): pl.pallas_call(body, grid=(rows // TILE,), in_specs=specs * 2 + [entire(w...  55.8 us
    ppermute x8, waiting for transfers between devices, diamond(): lax.ppermute(for_both, ('x', 'y'), ((0, 3), (1, 2), (2, 1), (3, 0)))  45.4 us
    all_to_all x2, blocking collectives, plane_columns(): lax.all_to_all(payload, PLANE, split_axis=0, concat_axis=0, tiled=True)  43.1 us
    pallas_call x2, Pallas kernels, attention_call(): pl.pallas_call(body, grid_spec=pltpu.PrefetchScalarGridSpec(num_scalar_pr...  41.4 us
    pallas_call x3, Pallas kernels, weight_grads(): pl.pallas_call(body, grid=(depth // tile,), in_specs=specs + [ANY] * len(...  41.1 us
    ppermute x62, starting transfers between devices, swap(): return lax.ppermute(values, axis, SWAP)  38.4 us
    unnamed x62, local copies, waits for them, and re-layouts  12.5 us
  transfers between devices with their start and end apart: 76, of which 32 were waited for; matrix products, arithmetic and copies ran while one was open for 8% of the time, Pallas kernels for 38%

profile of v3, /device:TPU:0, one launch (start us, length us, event | category | flops | bytes accessed | tf_op | source)
XLA Modules:
  0.0 530.8 jit_solution(4262796315264406440)
XLA Ops:
  12.5 13.8 %all_to_all.10 = bf16[8,48,640]{2,1,0:T(8,128)(2,1)} all-to-all(bf16[8,48,640]{2,1,0:T(8,128)(2,1)S(1)} %pack_columns.2), channel_id=1, replica_groups=mesh['dp'=4,'x'=2,'y'=2,'c'=2] {'x','y','c'}, dimensions={0} | all-to-all | bytes 983040 | tf_op jit(solution)/shard_map/all_to_all | solution.py:890
  28.2 29.3 %all_to_all.11 = bf16[8,48,2688]{2,1,0:T(8,128)(2,1)S(1)} all-to-all(bf16[8,48,2688]{2,1,0:T(8,128)(2,1)} %after.7), channel_id=1, replica_groups=mesh['dp'=4,'x'=2,'y'=2,'c'=2] {'x','y','c'}, dimensions={0} | all-to-all | bytes 4128768 | tf_op jit(solution)/shard_map/all_to_all | solution.py:890
  60.2 36.0 %conditional.8 = (bf16[256,1536]{1,0:T(8,128)(2,1)}, bf16[256,1536]{1,0:T(8,128)(2,1)}, bf16[256,1536]{1,0:T(8,128)(2,1)}, bf16[256,1536]{1,0:T(8,128)(2,1)}, bf...) conditional(s32[]{:T(128)} %convert_element_type.60, () %tuple.92, ...), branch_computations={%region_0.1_spmd, %region_1.2_spmd} | conditional | flops 33889 | bytes 43787008 | solution.py:886
  62.1 3.0 multiply_sine_fusion
  65.2 2.1 rotary_rows.1
  67.3 12.3 %collective-permute-done.11.refs_0_ = bf16[256,1536]{1,0:T(8,128)(2,1)} collective-permute-done((bf16[256,1536]{1,0:T(8,128)(2,1)S(1)}, bf16[256,1536]{1,0:T(8,128)(2,1)}, u32[]{:S(2)}, u32[]{:S(2)}) %collective-permute-start.11) | collective-permute-done | bytes 786464 | tf_op jit(solution)/shard_map/cond/branch_1_fun/ppermute | solution.py:829
  84.4 6.2 %collective-permute-done.13 = bf16[128,1536]{1,0:T(8,128)(2,1)S(1)} collective-permute-done((bf16[128,1536]{1,0:T(8,128)(2,1)S(1)}, bf16[128,1536]{1,0:T(8,128)(2,1)S(1)}, u32[]{:S(2)}, u32[]{:S(2)}) %collective-permute-start.13) | collective-permute-done | bytes 393248 | tf_op jit(solution)/shard_map/cond/branch_1_fun/ppermute | solution.py:829
  94.5 1.7 collective-permute-done.18
  96.2 3.6 turn.1
  100.3 29.5 %conditional.9 = (bf16[192,1536]{1,0:T(8,128)(2,1)}, bf16[192,1536]{1,0:T(8,128)(2,1)}, bf16[192,1536]{1,0:T(8,128)(2,1)}, bf16[192,1536]{1,0:T(8,128)(2,1)}, bf...) conditional(s32[]{:T(128)} %convert_element_type.60, () %tuple.91, ...), branch_computations={%region_2.3_spmd, %region_3.4_spmd} | conditional | flops 2 | bytes 11796592 | solution.py:886
  103.9 10.9 %norm_project.1 = (bf16[2048,1536]{1,0:T(8,128)(2,1)}, bf16[2048,320]{1,0:T(8,128)(2,1)}) custom-call(bf16[256,1536]{1,0:T(8,128)(2,1)} %get-tuple-element.270.refs_0_, bf16[256,1536]{1,0:T(8,128)(2,1)} %get-tuple-element.271.refs_1_, bf16[256,1536]{1,0:T(8,128)(2,1)} %get-tuple-element.272.refs_2_, bf16[256,1536]{1,0:T(8,128)(2,1)} %get-tuple-element.273.refs_3_, ...), custom_call_target="tpu_custom_call" | custom-call | flops 1 | bytes 1 | tf_op jit(solution)/shard_map/cond/branch_1_fun/norm_project/pallas_call | solution.py:356
  114.7 14.8 %attend_forward.1 = (bf16[2,1,256,192]{3,2,1,0:T(8,128)(2,1)S(1)}, bf16[2,1,256,192]{3,2,1,0:T(8,128)(2,1)S(1)}, bf16[2,1,256,192]{3,2,1,0:T(8,128)(2,1)}, bf16[...) custom-call(s32[1]{0:T(128)} %get-tuple-element.282.place_ref, bf16[8,1,256,320]{3,2,1,0:T(8,128)(2,1)} %bitcast.refs_0_, ...), custom_call_target="tpu_custom_call" | custom-call | flops 1 | bytes 1 | tf_op jit(solution)/shard_map/cond/branch_1_fun/attend_forward/pallas_call | solution.py:222
  130.7 82.9 %conditional.10 = (f32[256,1536]{1,0:T(8,128)}, bf16[256,1536]{1,0:T(8,128)(2,1)}, bf16[256,1536]{1,0:T(8,128)(2,1)}, bf16[256,1536]{1,0:T(8,128)(2,1)}, bf16[25...) conditional(s32[]{:T(128)} %convert_element_type.60, () %tuple.90, ...), branch_computations={%region_4.5_spmd, %region_5.6_spmd} | conditional | flops 1572865 | bytes 68420712 | solution.py:886
  134.7 11.3 %collective-permute-done.21.refs_3_ = bf16[512,192]{1,0:T(8,128)(2,1)S(1)} collective-permute-done((bf16[512,192]{1,0:T(8,128)(2,1)}, bf16[512,192]{1,0:T(8,128)(2,1)S(1)}, u32[]{:S(2)}, u32[]{:S(2)}) %collective-permute-start.21) | collective-permute-done | bytes 196640 | tf_op jit(solution)/shard_map/cond/branch_1_fun/ppermute | solution.py:853
  149.6 5.4 %attend_out.1 = (f32[256,1536]{1,0:T(8,128)}, bf16[256,1536]{1,0:T(8,128)(2,1)}) custom-call(bf16[512,192]{1,0:T(8,128)(2,1)S(1)} %bitcast.80, bf16[512,192]{1,0:T(8,128)(2,1)S(1)} %collective-permute-done.19.refs_1_, bf16[512,192]{1,0:T(8,128)(2,1)S(1)} %collective-permute-done.20.refs_2_, bf16[512,192]{1,0:T(8,128)(2,1)S(1)} %collective-permute-done.21.refs_3_, ...), custom_call_target="tpu_custom_call" | custom-call | flops 1 | bytes 1 | tf_op jit(solution)/shard_map/cond/branch_1_fun/attend_out/pallas_call | solution.py:594
  154.9 1.6 collective-permute-start.26
  157.1 10.2 %collective-permute-done.34 = bf16[256,1536]{1,0:T(8,128)(2,1)} collective-permute-done((bf16[256,1536]{1,0:T(8,128)(2,1)S(1)}, bf16[256,1536]{1,0:T(8,128)(2,1)}, u32[]{:S(2)}, u32[]{:S(2)}) %collective-permute-start.34) | collective-permute-done | bytes 786464 | tf_op jit(solution)/shard_map/cond/branch_1_fun/ppermute | solution.py:829
  171.8 12.3 %collective-permute-done.26 = bf16[256,1536]{1,0:T(8,128)(2,1)} collective-permute-done((bf16[256,1536]{1,0:T(8,128)(2,1)}, bf16[256,1536]{1,0:T(8,128)(2,1)}, u32[]{:S(2)}, u32[]{:S(2)}) %collective-permute-start.26) | collective-permute-done | bytes 786464 | tf_op jit(solution)/shard_map/cond/branch_1_fun/ppermute | solution.py:829
  185.2 8.5 %collective-permute-done.36 = bf16[128,1536]{1,0:T(8,128)(2,1)S(1)} collective-permute-done((bf16[128,1536]{1,0:T(8,128)(2,1)S(1)}, bf16[128,1536]{1,0:T(8,128)(2,1)S(1)}, u32[]{:S(2)}, u32[]{:S(2)}) %collective-permute-start.36) | collective-permute-done | bytes 393248 | tf_op jit(solution)/shard_map/cond/branch_1_fun/ppermute | solution.py:829
  196.2 1.7 collective-permute-start.29
  198.7 6.5 %collective-permute-done.28 = bf16[128,1536]{1,0:T(8,128)(2,1)S(1)} collective-permute-done((bf16[128,1536]{1,0:T(8,128)(2,1)S(1)}, bf16[128,1536]{1,0:T(8,128)(2,1)S(1)}, u32[]{:S(2)}, u32[]{:S(2)}) %collective-permute-start.28) | collective-permute-done | bytes 393248 | tf_op jit(solution)/shard_map/cond/branch_1_fun/ppermute | solution.py:829
  206.0 1.6 collective-permute-done.29
  213.6 57.2 %conditional.11 = (bf16[1024,640]{1,0:T(8,128)(2,1)}, bf16[1024,640]{1,0:T(8,128)(2,1)}, bf16[1024,1536]{1,0:T(8,128)(2,1)}, bf16[1024,1536]{1,0:T(8,128)(2,1)},...) conditional(s32[]{:T(128)} %convert_element_type.60, () %tuple.96, ...), branch_computations={%region_6.7_spmd, %region_7.8_spmd} | conditional | flops 3 | bytes 33423640 | solution.py:886
  213.6 1.6 collective-permute-start.4
  217.1 17.7 %feed_forward.4 = (bf16[1024,1280]{1,0:T(8,128)(2,1)}, bf16[1024,640]{1,0:T(8,128)(2,1)}, bf16[1024,1536]{1,0:T(8,128)(2,1)}) custom-call(bf16[256,1536]{1,0:T(8,128)(2,1)} %get-tuple-element.305.refs_0_, bf16[256,1536]{1,0:T(8,128)(2,1)} %get-tuple-element.306.refs_1_, bf16[256,1536]{1,0:T(8,128)(2,1)} %get-tuple-element.307.refs_2_, ...), custom_call_target="tpu_custom_call" | custom-call | flops 1 | bytes 1 | tf_op jit(solution)/shard_map/cond/branch_1_fun/feed_forward/pallas_call | solution.py:411
  234.8 16.3 %feed_forward.5 = (bf16[1024,1280]{1,0:T(8,128)(2,1)}, bf16[1024,640]{1,0:T(8,128)(2,1)}, bf16[1024,1536]{1,0:T(8,128)(2,1)}) custom-call(bf16[256,1536]{1,0:T(8,128)(2,1)} %get-tuple-element.315.refs_0_.refs_4_, bf16[256,1536]{1,0:T(8,128)(2,1)} %get-tuple-element.316.refs_1_.refs_5_, bf16[256,1536]{1,0:T(8,128)(2,1)} %get-tuple-element.317.refs_2_.refs_6_, ...), custom_call_target="tpu_custom_call" | custom-call | flops 1 | bytes 1 | tf_op jit(solution)/shard_map/cond/branch_1_fun/feed_forward/pallas_call | solution.py:411
  251.1 19.6 %weight_grads.3 = bf16[1536,1920]{1,0:T(8,128)(2,1)} custom-call(bf16[256,1536]{1,0:T(8,128)(2,1)} %get-tuple-element.305.refs_0_, bf16[256,1536]{1,0:T(8,128)(2,1)} %get-tuple-element.306.refs_1_, bf16[256,1536]{1,0:T(8,128)(2,1)} %get-tuple-element.307.refs_2_, bf16[256,1536]{1,0:T(8,128)(2,1)} %get-tuple-element.308.refs_3_, ...), custom_call_target="tpu_custom_call" | custom-call | flops 1 | bytes 1 | tf_op jit(solution)/shard_map/cond/branch_1_fun/weight_grads/pallas_call | solution.py:506
  270.8 11.6 %feed_forward.6 = (bf16[1024,512]{1,0:T(8,128)(2,1)}, bf16[1024,256]{1,0:T(8,128)(2,1)}, bf16[1024,1536]{1,0:T(8,128)(2,1)}) custom-call(bf16[256,1536]{1,0:T(8,128)(2,1)} %get-tuple-element.569.refs_0_, bf16[256,1536]{1,0:T(8,128)(2,1)} %get-tuple-element.570.refs_1_, bf16[256,1536]{1,0:T(8,128)(2,1)} %get-tuple-element.571.refs_2_, ...), custom_call_target="tpu_custom_call" | custom-call | flops 1 | bytes 1 | tf_op jit(solution)/shard_map/feed_forward/pallas_call | solution.py:411
  282.9 10.3 %feed_forward.7 = (bf16[1024,512]{1,0:T(8,128)(2,1)}, bf16[1024,256]{1,0:T(8,128)(2,1)}, bf16[1024,1536]{1,0:T(8,128)(2,1)}) custom-call(bf16[256,1536]{1,0:T(8,128)(2,1)} %get-tuple-element.562.refs_0_, bf16[256,1536]{1,0:T(8,128)(2,1)} %get-tuple-element.563.refs_1_, bf16[256,1536]{1,0:T(8,128)(2,1)} %get-tuple-element.564.refs_2_, ...), custom_call_target="tpu_custom_call" | custom-call | flops 1 | bytes 1 | tf_op jit(solution)/shard_map/feed_forward/pallas_call | solution.py:411
  293.2 1.7 copy-done.27
  294.9 1.9 copy-done.1
  296.8 4.6 core_sum.2
  301.4 37.9 %conditional.12 = (bf16[256,1536]{1,0:T(8,128)(2,1)}, bf16[256,1536]{1,0:T(8,128)(2,1)}, bf16[256,1536]{1,0:T(8,128)(2,1)}, bf16[1536,768]{1,0:T(8,128)(2,1)}, b...) conditional(s32[]{:T(128)} %convert_element_type.60, () %tuple.95, (bf16[256,1536]{1,0:T(8,128)(2,1)}, ...), branch_computations={%region_8.9_spmd, %region_9.10_spmd} | conditional | flops 2 | bytes 11010108 | solution.py:886
  301.4 1.7 collective-permute-start.8
  304.9 12.3 %project_back.1 = (bf16[1024,1536]{1,0:T(8,128)(2,1)}, bf16[1024,1536]{1,0:T(8,128)(2,1)}) custom-call(bf16[1024,640]{1,0:T(8,128)(2,1)} %get-tuple-element.352.refs_0_, bf16[1024,640]{1,0:T(8,128)(2,1)} %get-tuple-element.353.refs_1_, bf16[1024,256]{1,0:T(8,128)(2,1)S(1)} %get-tuple-element.350.refs_18_.refs_2_, ...), custom_call_target="tpu_custom_call" | custom-call | flops 1 | bytes 1 | tf_op jit(solution)/shard_map/cond/branch_1_fun/project_back/pallas_call | solution.py:545
  317.2 10.5 %weight_grads.4 = bf16[1536,768]{1,0:T(8,128)(2,1)} custom-call(bf16[256,1536]{1,0:T(8,128)(2,1)} %get-tuple-element.332.refs_0_, bf16[256,1536]{1,0:T(8,128)(2,1)} %get-tuple-element.333.refs_1_, bf16[256,1536]{1,0:T(8,128)(2,1)} %get-tuple-element.334.refs_2_, bf16[256,1536]{1,0:T(8,128)(2,1)} %get-tuple-element.335.refs_3_, ...), custom_call_target="tpu_custom_call" | custom-call | flops 1 | bytes 1 | tf_op jit(solution)/shard_map/cond/branch_1_fun/weight_grads/pallas_call | solution.py:506
  327.8 11.5 %collective-permute-done.10 = bf16[256,1536]{1,0:T(8,128)(2,1)} collective-permute-done((bf16[256,1536]{1,0:T(8,128)(2,1)}, bf16[256,1536]{1,0:T(8,128)(2,1)}, u32[]{:S(2)}, u32[]{:S(2)}) %collective-permute-start.10) | collective-permute-done | bytes 786464 | tf_op jit(solution)/shard_map/cond/branch_1_fun/ppermute | solution.py:853
  339.3 7.1 %middle_back.1 = (f32[256,1536]{1,0:T(8,128)}, bf16[256,1536]{1,0:T(8,128)(2,1)}, bf16[2,256,192]{2,1,0:T(8,128)(2,1)S(1)}, bf16[2,256,192]{2,1,0:T(8,128)(2,1)S...) custom-call(f32[256,1536]{1,0:T(8,128)S(1)} %get-tuple-element.593.refs_0_, ...), custom_call_target="tpu_custom_call" | custom-call | flops 1 | bytes 1 | tf_op jit(solution)/shard_map/middle_back/pallas_call | solution.py:646
  346.4 1.5 collective-permute-start.58
  349.9 9.9 %collective-permute-done.56 = bf16[512,192]{1,0:T(8,128)(2,1)S(1)} collective-permute-done((bf16[512,192]{1,0:T(8,128)(2,1)S(1)}, bf16[512,192]{1,0:T(8,128)(2,1)S(1)}, u32[]{:S(2)}, u32[]{:S(2)}) %collective-permute-start.56) | collective-permute-done | bytes 196640 | tf_op jit(solution)/shard_map/ppermute | solution.py:829
  360.4 1.9 collective-permute-done.59
  362.4 38.4 %conditional.13 = (bf16[256,1536]{1,0:T(8,128)(2,1)}, bf16[256,1536]{1,0:T(8,128)(2,1)}, bf16[256,1536]{1,0:T(8,128)(2,1)}, bf16[256,1536]{1,0:T(8,128)(2,1)}, b...) conditional(s32[]{:T(128)} %convert_element_type.60, () %tuple.99, ...), branch_computations={%region_10.11_spmd, %region_11.12_spmd} | conditional | flops 1 | bytes 26476840 | solution.py:886
  366.1 26.6 %attend_backward.1 = (bf16[2,1,256,320]{3,2,1,0:T(8,128)(2,1)}, bf16[2,1,256,320]{3,2,1,0:T(8,128)(2,1)}, bf16[2,1,256,320]{3,2,1,0:T(8,128)(2,1)}, bf16[2,1,256,320]{3,2,1,0:T(8,128)(2,1)}, f32[2,8,256]{2,1,0:T(8,128)S(1)}) custom-call(s32[1]{0:T(128)} %get-tuple-element.359.place_ref, bf16[8,1,256,320]{3,2,1,0:T(8,128)(2,1)} %get-tuple-element.360.refs_0_, ...), custom_call_target="tpu_custom_call" | custom-call | flops 1 | bytes 1 | tf_op jit(solution)/shard_map/cond/branch_1_fun/attend_backward/pallas_call | solution.py:222
  392.7 1.8 copy.246
  395.6 5.1 collective-permute-done.44
  401.9 2.0 collective-permute-done.60
  403.9 2.2 collective-permute-done.61
  406.3 22.9 %conditional.14 = (bf16[512,320]{1,0:T(8,128)(2,1)}, bf16[512,320]{1,0:T(8,128)(2,1)}, bf16[512,320]{1,0:T(8,128)(2,1)}, bf16[1536,640]{1,0:T(8,128)(2,1)S(1)}, ...) conditional(s32[]{:T(128)} %convert_element_type.60, () %tuple.102, ...), branch_computations={%region_14.15_spmd, %region_15.16_spmd} | conditional | flops 1 | bytes 14973249 | solution.py:886
  411.4 11.0 %weight_grads.5 = bf16[1536,640]{1,0:T(8,128)(2,1)S(1)} custom-call(bf16[2048,1536]{1,0:T(8,128)(2,1)} %get-tuple-element.379.refs_0_, bf16[512,320]{1,0:T(8,128)(2,1)} %bitcast.22.refs_1_, bf16[512,320]{1,0:T(8,128)(2,1)} %bitcast.16.refs_2_, bf16[512,320]{1,0:T(8,128)(2,1)} %bitcast.18.refs_3_, bf16[512,320]{1,0:T(8,128)(2,1)} %bitcast.20.refs_4_, ...), custom_call_target="tpu_custom_call" | custom-call | flops 1 | bytes 1 | tf_op jit(solution)/shard_map/cond/branch_1_fun/weight_grads/pallas_call | solution.py:506
  424.5 2.9 collective-permute-done.49
  431.2 1.8 pad_maximum_fusion.1
  433.4 5.3 core_sum.3
  438.7 60.1 %conditional.15 = (bf16[192,1920]{1,0:T(8,128)(2,1)}, bf16[192,768]{1,0:T(8,128)(2,1)}, f32[256,1536]{1,0:T(8,128)}, f32[256,1536]{1,0:T(8,128)}, f32[256,1536]{1,0:T(8,128)}, /*index=5*/f32[1,256,1536]{2,1,0:T(8,128)}) conditional(s32[]{:T(128)} %convert_element_type.60, () %tuple.101, (bf16[384,1920]{1,0:T(8,128)(2,1)S(1)}, ...), branch_computations={%region_16.17_spmd, %region_17.18_spmd} | conditional | flops 1179657 | bytes 29524372 | solution.py:886
  447.5 8.9 %input_back.1 = f32[256,1536]{1,0:T(8,128)} custom-call(bf16[512,320]{1,0:T(8,128)(2,1)} %get-tuple-element.401.refs_0_, bf16[512,320]{1,0:T(8,128)(2,1)} %get-tuple-element.402.refs_1_, bf16[512,320]{1,0:T(8,128)(2,1)} %get-tuple-element.403.refs_2_, bf16[512,320]{1,0:T(8,128)(2,1)} %get-tuple-element.404.refs_3_, ...), custom_call_target="tpu_custom_call" | custom-call | flops 1 | bytes 1 | tf_op jit(solution)/shard_map/cond/branch_1_fun/input_back/pallas_call | solution.py:677
  456.4 2.3 collective-permute-done.52
  458.7 2.5 convert_element_type.53
  461.2 2.5 convert_element_type.54
  463.7 14.2 %collective-permute-done.54 = bf16[256,1536]{1,0:T(8,128)(2,1)} collective-permute-done((bf16[256,1536]{1,0:T(8,128)(2,1)}, bf16[256,1536]{1,0:T(8,128)(2,1)}, u32[]{:S(2)}, u32[]{:S(2)}) %collective-permute-start.54) | collective-permute-done | bytes 786464 | tf_op jit(solution)/shard_map/cond/branch_1_fun/ppermute | solution.py:853
  477.9 2.6 convert_element_type.55
  480.5 18.3 %collective-permute-done.51 = bf16[192,768]{1,0:T(8,128)(2,1)} collective-permute-done((bf16[192,768]{1,0:T(8,128)(2,1)}, bf16[192,768]{1,0:T(8,128)(2,1)}, u32[]{:S(2)}, u32[]{:S(2)}) %collective-permute-start.51) | collective-permute-done | bytes 294944 | tf_op jit(solution)/shard_map/cond/branch_1_fun/ppermute | solution.py:829
  498.8 3.9 unpack_columns.2
  502.7 4.4 add_convert_fusion.refs_1_
  508.7 6.2 %collective-permute-done.67.refs_1_ = bf16[192,640]{1,0:T(8,128)(2,1)S(1)} collective-permute-done((bf16[192,640]{1,0:T(8,128)(2,1)S(1)}, bf16[192,640]{1,0:T(8,128)(2,1)S(1)}, u32[]{:S(2)}, u32[]{:S(2)}) %collective-permute-start.67) | collective-permute-done | bytes 245792 | tf_op jit(solution)/shard_map/ppermute | solution.py:829
  517.4 3.6 collective-permute-done.68
  (293 shorter events, 89.1 us)
Async XLA Ops:
  7.2 89.0 %all-gather.4.cloned.1.call-start = ((), (), s32[]{:S(2)}) async-start(), calls=%async_computation.5 | async-start | bytes 2457600 | tf_op jit(solution)/shard_map/all_gather | solution.py:873
  26.2 187.3 %all-gather.8.cloned.1.call-start = ((), (), s32[]{:S(2)}) async-start(), calls=%async_computation.7 | async-start | bytes 7372800 | tf_op jit(solution)/shard_map/all_gather | solution.py:873
  58.8 212.1 %all-gather.6.cloned.1.call-start = ((), (), s32[]{:S(2)}) async-start(), calls=%async_computation.6 | async-start | bytes 2949120 | tf_op jit(solution)/shard_map/all_gather | solution.py:873
  59.7 342.2 %reduce-scatter.4.cloned.1.call-start = ((), (), s32[]{:S(2)}) async-start(), calls=%async_computation.8 | async-start | bytes 7372800 | tf_op jit(solution)/shard_map/reduce_scatter | solution.py:877
  60.2 19.4 %collective-permute-start.11 = (bf16[256,1536]{1,0:T(8,128)(2,1)S(1)}, bf16[256,1536]{1,0:T(8,128)(2,1)}, u32[]{:S(2)}, u32[]{:S(2)}) collective-permute-start(bf16[256,1536]{1,0:T(8,128)(2,1)S(1)} %param.1), channel_id=1, source_target_pairs={{0,2},{2,0},{1,3},{3,1},{4,6},{6,4},{5,7},{7,5},{8,10},{10,8},{9,1... | collective-permute-start | bytes 2359304 | tf_op jit(solution)/shard_map/cond/branch_1_fun/ppermute | solution.py:829
  61.6 20.3 %collective-permute-start.12 = (bf16[256,1536]{1,0:T(8,128)(2,1)S(1)}, bf16[256,1536]{1,0:T(8,128)(2,1)}, u32[]{:S(2)}, u32[]{:S(2)}) collective-permute-start(bf16[256,1536]{1,0:T(8,128)(2,1)S(1)} %param.1), channel_id=1, source_target_pairs={{0,4},{4,0},{1,5},{5,1},{2,6},{6,2},{3,7},{7,3},{8,12},{12,8},{9,1... | collective-permute-start | bytes 2359304 | tf_op jit(solution)/shard_map/cond/branch_1_fun/ppermute | solution.py:829
  80.6 10.0 %collective-permute-start.13 = (bf16[128,1536]{1,0:T(8,128)(2,1)S(1)}, bf16[128,1536]{1,0:T(8,128)(2,1)S(1)}, u32[]{:S(2)}, u32[]{:S(2)}) collective-permute-start(bf16[128,1536]{1,0:T(8,128)(2,1)S(1)} %slice.148), channel_id=1, source_target_pairs={{0,4},{4,0},{1,5},{5,1},{2,6},{6,2},{3,7},{7,3},{8,12},{12,8},{9,1... | collective-permute-start | bytes 1179656 | tf_op jit(solution)/shard_map/cond/branch_1_fun/ppermute | solution.py:829
  82.9 9.9 %collective-permute-start.14 = (bf16[128,1536]{1,0:T(8,128)(2,1)S(1)}, bf16[128,1536]{1,0:T(8,128)(2,1)S(1)}, u32[]{:S(2)}, u32[]{:S(2)}) collective-permute-start(bf16[128,1536]{1,0:T(8,128)(2,1)S(1)} %slice.149), channel_id=1, source_target_pairs={{0,2},{2,0},{1,3},{3,1},{4,6},{6,4},{5,7},{7,5},{8,10},{10,8},{9,1... | collective-permute-start | bytes 1179656 | tf_op jit(solution)/shard_map/cond/branch_1_fun/ppermute | solution.py:829
  83.9 10.6 %collective-permute-start.15 = (bf16[256,1536]{1,0:T(8,128)(2,1)S(1)}, bf16[256,1536]{1,0:T(8,128)(2,1)}, u32[]{:S(2)}, u32[]{:S(2)}) collective-permute-start(bf16[256,1536]{1,0:T(8,128)(2,1)S(1)} %param.1), channel_id=1, source_target_pairs={{0,1},{1,0},{2,3},{3,2},{4,5},{5,4},{6,7},{7,6},{8,9},{9,8},{10,11... | collective-permute-start | bytes 2359304 | tf_op jit(solution)/shard_map/cond/branch_1_fun/ppermute | solution.py:829
  83.9 10.6 %collective-permute-start.16 = (bf16[256,1536]{1,0:T(8,128)(2,1)}, bf16[256,1536]{1,0:T(8,128)(2,1)}, u32[]{:S(2)}, u32[]{:S(2)}) collective-permute-start(bf16[256,1536]{1,0:T(8,128)(2,1)} %after.6), channel_id=1, source_target_pairs={{0,1},{1,0},{2,3},{3,2},{4,5},{5,4},{6,7},{7,6},{8,9},{9,8},{10,11... | collective-permute-start | bytes 2359304 | tf_op jit(solution)/shard_map/cond/branch_1_fun/ppermute | solution.py:829
  84.4 10.1 %collective-permute-start.17 = (bf16[256,1536]{1,0:T(8,128)(2,1)}, bf16[256,1536]{1,0:T(8,128)(2,1)}, u32[]{:S(2)}, u32[]{:S(2)}) collective-permute-start(bf16[256,1536]{1,0:T(8,128)(2,1)} %collective-permute-done.12), channel_id=1, source_target_pairs={{0,1},{1,0},{2,3},{3,2},{4,5},{5,4},{6,7},{7,6},{8,9},{9,8},{10,11... | collective-permute-start | bytes 2359304 | tf_op jit(solution)/shard_map/cond/branch_1_fun/ppermute | solution.py:829
  100.3 29.2 %collective-permute-start = (bf16[192,1536]{1,0:T(8,128)(2,1)}, bf16[192,1536]{1,0:T(8,128)(2,1)}, u32[]{:S(2)}, u32[]{:S(2)}) collective-permute-start(bf16[192,1536]{1,0:T(8,128)(2,1)} %get-tuple-element.269), channel_id=1, source_target_pairs={{0,2},{2,0},{1,3},{3,1},{4,6},{6,4},{5,7},{7,5},{8,10},{10,8},{9,1... | collective-permute-start | bytes 1769480 | tf_op jit(solution)/shard_map/cond/branch_1_fun/ppermute | solution.py:829
  101.2 28.3 %collective-permute-start.1 = (bf16[192,1536]{1,0:T(8,128)(2,1)}, bf16[192,1536]{1,0:T(8,128)(2,1)}, u32[]{:S(2)}, u32[]{:S(2)}) collective-permute-start(bf16[192,1536]{1,0:T(8,128)(2,1)} %get-tuple-element.269), channel_id=1, source_target_pairs={{0,4},{4,0},{1,5},{5,1},{2,6},{6,2},{3,7},{7,3},{8,12},{12,8},{9,1... | collective-permute-start | bytes 1769480 | tf_op jit(solution)/shard_map/cond/branch_1_fun/ppermute | solution.py:829
  102.7 27.2 %collective-permute-start.2 = (bf16[192,1536]{1,0:T(8,128)(2,1)}, bf16[192,1536]{1,0:T(8,128)(2,1)}, u32[]{:S(2)}, u32[]{:S(2)}) collective-permute-start(bf16[192,1536]{1,0:T(8,128)(2,1)} %get-tuple-element.269), channel_id=1, source_target_pairs={{0,6},{2,4},{4,2},{6,0},{1,7},{3,5},{5,3},{7,1},{8,14},{10,12},{12... | collective-permute-start | bytes 1769480 | tf_op jit(solution)/shard_map/cond/branch_1_fun/ppermute | solution.py:853
  103.9 26.0 %collective-permute-start.3 = (bf16[192,1536]{1,0:T(8,128)(2,1)}, bf16[192,1536]{1,0:T(8,128)(2,1)}, u32[]{:S(2)}, u32[]{:S(2)}) collective-permute-start(bf16[192,1536]{1,0:T(8,128)(2,1)} %get-tuple-element.269), channel_id=1, source_target_pairs={{0,1},{1,0},{2,3},{3,2},{4,5},{5,4},{6,7},{7,6},{8,9},{9,8},{10,11... | collective-permute-start | bytes 1769480 | tf_op jit(solution)/shard_map/cond/branch_1_fun/ppermute | solution.py:829
  130.7 15.4 %collective-permute-start.19 = (bf16[512,192]{1,0:T(8,128)(2,1)S(1)}, bf16[512,192]{1,0:T(8,128)(2,1)S(1)}, u32[]{:S(2)}, u32[]{:S(2)}) collective-permute-start(bf16[512,192]{1,0:T(8,128)(2,1)S(1)} %bitcast.85), channel_id=1, source_target_pairs={{0,2},{2,0},{1,3},{3,1},{4,6},{6,4},{5,7},{7,5},{8,10},{10,8},{9,1... | collective-permute-start | bytes 589832 | tf_op jit(solution)/shard_map/cond/branch_1_fun/ppermute | solution.py:829
  131.5 14.5 %collective-permute-start.20 = (bf16[512,192]{1,0:T(8,128)(2,1)}, bf16[512,192]{1,0:T(8,128)(2,1)S(1)}, u32[]{:S(2)}, u32[]{:S(2)}) collective-permute-start(bf16[512,192]{1,0:T(8,128)(2,1)} %bitcast.87), channel_id=1, source_target_pairs={{0,4},{4,0},{1,5},{5,1},{2,6},{6,2},{3,7},{7,3},{8,12},{12,8},{9,1... | collective-permute-start | bytes 589832 | tf_op jit(solution)/shard_map/cond/branch_1_fun/ppermute | solution.py:829
  133.0 13.0 %collective-permute-start.21 = (bf16[512,192]{1,0:T(8,128)(2,1)}, bf16[512,192]{1,0:T(8,128)(2,1)S(1)}, u32[]{:S(2)}, u32[]{:S(2)}) collective-permute-start(bf16[512,192]{1,0:T(8,128)(2,1)} %bitcast.89), channel_id=1, source_target_pairs={{0,6},{2,4},{4,2},{6,0},{1,7},{3,5},{5,3},{7,1},{8,14},{10,12},{12... | collective-permute-start | bytes 589832 | tf_op jit(solution)/shard_map/cond/branch_1_fun/ppermute | solution.py:853
  134.2 15.4 %collective-permute-start.23 = (bf16[192,1536]{1,0:T(8,128)(2,1)}, bf16[192,1536]{1,0:T(8,128)(2,1)}, u32[]{:S(2)}, u32[]{:S(2)}) collective-permute-start(bf16[192,1536]{1,0:T(8,128)(2,1)} %get-tuple-element.296.refs_9_), channel_id=1, source_target_pairs={{0,1},{1,0},{2,3},{3,2},{4,5},{5,4},{6,7},{7,6},{8,9},{9,8},{10,11... | collective-permute-start | bytes 1769480 | tf_op jit(solution)/shard_map/cond/branch_1_fun/ppermute | solution.py:829
  134.2 15.4 %collective-permute-start.24 = (bf16[192,1536]{1,0:T(8,128)(2,1)}, bf16[192,1536]{1,0:T(8,128)(2,1)}, u32[]{:S(2)}, u32[]{:S(2)}) collective-permute-start(bf16[192,1536]{1,0:T(8,128)(2,1)} %get-tuple-element.297.refs_10_), channel_id=1, source_target_pairs={{0,1},{1,0},{2,3},{3,2},{4,5},{5,4},{6,7},{7,6},{8,9},{9,8},{10,11... | collective-permute-start | bytes 1769480 | tf_op jit(solution)/shard_map/cond/branch_1_fun/ppermute | solution.py:829
  146.8 20.5 %collective-permute-start.34 = (bf16[256,1536]{1,0:T(8,128)(2,1)S(1)}, bf16[256,1536]{1,0:T(8,128)(2,1)}, u32[]{:S(2)}, u32[]{:S(2)}) collective-permute-start(bf16[256,1536]{1,0:T(8,128)(2,1)S(1)} %get-tuple-element.304), channel_id=1, source_target_pairs={{0,2},{2,0},{1,3},{3,1},{4,6},{6,4},{5,7},{7,5},{8,10},{10,8},{9,1... | collective-permute-start | bytes 2359304 | tf_op jit(solution)/shard_map/cond/branch_1_fun/ppermute | solution.py:829
  148.8 20.5 %collective-permute-start.35 = (bf16[256,1536]{1,0:T(8,128)(2,1)S(1)}, bf16[256,1536]{1,0:T(8,128)(2,1)}, u32[]{:S(2)}, u32[]{:S(2)}) collective-permute-start(bf16[256,1536]{1,0:T(8,128)(2,1)S(1)} %get-tuple-element.304), channel_id=1, source_target_pairs={{0,4},{4,0},{1,5},{5,1},{2,6},{6,2},{3,7},{7,3},{8,12},{12,8},{9,1... | collective-permute-start | bytes 2359304 | tf_op jit(solution)/shard_map/cond/branch_1_fun/ppermute | solution.py:829
  154.9 29.2 %collective-permute-start.26 = (bf16[256,1536]{1,0:T(8,128)(2,1)}, bf16[256,1536]{1,0:T(8,128)(2,1)}, u32[]{:S(2)}, u32[]{:S(2)}) collective-permute-start(bf16[256,1536]{1,0:T(8,128)(2,1)} %get-tuple-element.915), channel_id=1, source_target_pairs={{0,2},{2,0},{1,3},{3,1},{4,6},{6,4},{5,7},{7,5},{8,10},{10,8},{9,1... | collective-permute-start | bytes 2359304 | tf_op jit(solution)/shard_map/cond/branch_1_fun/ppermute | solution.py:829
  156.5 37.1 %collective-permute-start.27 = (bf16[256,1536]{1,0:T(8,128)(2,1)}, bf16[256,1536]{1,0:T(8,128)(2,1)}, u32[]{:S(2)}, u32[]{:S(2)}) collective-permute-start(bf16[256,1536]{1,0:T(8,128)(2,1)} %get-tuple-element.915), channel_id=1, source_target_pairs={{0,4},{4,0},{1,5},{5,1},{2,6},{6,2},{3,7},{7,3},{8,12},{12,8},{9,1... | collective-permute-start | bytes 2359304 | tf_op jit(solution)/shard_map/cond/branch_1_fun/ppermute | solution.py:829
  168.3 25.3 %collective-permute-start.36 = (bf16[128,1536]{1,0:T(8,128)(2,1)S(1)}, bf16[128,1536]{1,0:T(8,128)(2,1)S(1)}, u32[]{:S(2)}, u32[]{:S(2)}) collective-permute-start(bf16[128,1536]{1,0:T(8,128)(2,1)S(1)} %slice.155), channel_id=1, source_target_pairs={{0,4},{4,0},{1,5},{5,1},{2,6},{6,2},{3,7},{7,3},{8,12},{12,8},{9,1... | collective-permute-start | bytes 1179656 | tf_op jit(solution)/shard_map/cond/branch_1_fun/ppermute | solution.py:829
  170.3 25.9 %collective-permute-start.37 = (bf16[128,1536]{1,0:T(8,128)(2,1)S(1)}, bf16[128,1536]{1,0:T(8,128)(2,1)S(1)}, u32[]{:S(2)}, u32[]{:S(2)}) collective-permute-start(bf16[128,1536]{1,0:T(8,128)(2,1)S(1)} %slice.156), channel_id=1, source_target_pairs={{0,2},{2,0},{1,3},{3,1},{4,6},{6,4},{5,7},{7,5},{8,10},{10,8},{9,1... | collective-permute-start | bytes 1179656 | tf_op jit(solution)/shard_map/cond/branch_1_fun/ppermute | solution.py:829
  171.8 36.5 %collective-permute-start.38 = (bf16[256,1536]{1,0:T(8,128)(2,1)S(1)}, bf16[256,1536]{1,0:T(8,128)(2,1)}, u32[]{:S(2)}, u32[]{:S(2)}) collective-permute-start(bf16[256,1536]{1,0:T(8,128)(2,1)S(1)} %get-tuple-element.304), channel_id=1, source_target_pairs={{0,1},{1,0},{2,3},{3,2},{4,5},{5,4},{6,7},{7,6},{8,9},{9,8},{10,11... | collective-permute-start | bytes 2359304 | tf_op jit(solution)/shard_map/cond/branch_1_fun/ppermute | solution.py:829
  184.1 24.7 %collective-permute-start.30 = (bf16[256,1536]{1,0:T(8,128)(2,1)}, bf16[256,1536]{1,0:T(8,128)(2,1)}, u32[]{:S(2)}, u32[]{:S(2)}) collective-permute-start(bf16[256,1536]{1,0:T(8,128)(2,1)} %get-tuple-element.915), channel_id=1, source_target_pairs={{0,1},{1,0},{2,3},{3,2},{4,5},{5,4},{6,7},{7,6},{8,9},{9,8},{10,11... | collective-permute-start | bytes 2359304 | tf_op jit(solution)/shard_map/cond/branch_1_fun/ppermute | solution.py:829
  193.7 15.3 %collective-permute-start.39 = (bf16[256,1536]{1,0:T(8,128)(2,1)}, bf16[256,1536]{1,0:T(8,128)(2,1)}, u32[]{:S(2)}, u32[]{:S(2)}) collective-permute-start(bf16[256,1536]{1,0:T(8,128)(2,1)} %collective-permute-done.34), channel_id=1, source_target_pairs={{0,1},{1,0},{2,3},{3,2},{4,5},{5,4},{6,7},{7,6},{8,9},{9,8},{10,11... | collective-permute-start | bytes 2359304 | tf_op jit(solution)/shard_map/cond/branch_1_fun/ppermute | solution.py:829
  193.7 11.5 %collective-permute-start.28 = (bf16[128,1536]{1,0:T(8,128)(2,1)S(1)}, bf16[128,1536]{1,0:T(8,128)(2,1)S(1)}, u32[]{:S(2)}, u32[]{:S(2)}) collective-permute-start(bf16[128,1536]{1,0:T(8,128)(2,1)S(1)} %slice.153), channel_id=1, source_target_pairs={{0,4},{4,0},{1,5},{5,1},{2,6},{6,2},{3,7},{7,3},{8,12},{12,8},{9,1... | collective-permute-start | bytes 1179656 | tf_op jit(solution)/shard_map/cond/branch_1_fun/ppermute | solution.py:829
  196.2 11.3 %collective-permute-start.29 = (bf16[128,1536]{1,0:T(8,128)(2,1)S(1)}, bf16[128,1536]{1,0:T(8,128)(2,1)S(1)}, u32[]{:S(2)}, u32[]{:S(2)}) collective-permute-start(bf16[128,1536]{1,0:T(8,128)(2,1)S(1)} %slice.154), channel_id=1, source_target_pairs={{0,2},{2,0},{1,3},{3,1},{4,6},{6,4},{5,7},{7,5},{8,10},{10,8},{9,1... | collective-permute-start | bytes 1179656 | tf_op jit(solution)/shard_map/cond/branch_1_fun/ppermute | solution.py:829
  208.9 4.6 collective-permute-start.33
  213.6 57.1 %collective-permute-start.4 = (bf16[320,1536]{1,0:T(8,128)(2,1)}, bf16[320,1536]{1,0:T(8,128)(2,1)}, u32[]{:S(2)}, u32[]{:S(2)}) collective-permute-start(bf16[320,1536]{1,0:T(8,128)(2,1)} %get-tuple-element.328), channel_id=1, source_target_pairs={{0,2},{2,0},{1,3},{3,1},{4,6},{6,4},{5,7},{7,5},{8,10},{10,8},{9,1... | collective-permute-start | bytes 2949128 | tf_op jit(solution)/shard_map/cond/branch_1_fun/ppermute | solution.py:829
  215.2 55.5 %collective-permute-start.5 = (bf16[320,1536]{1,0:T(8,128)(2,1)}, bf16[320,1536]{1,0:T(8,128)(2,1)}, u32[]{:S(2)}, u32[]{:S(2)}) collective-permute-start(bf16[320,1536]{1,0:T(8,128)(2,1)} %get-tuple-element.328), channel_id=1, source_target_pairs={{0,4},{4,0},{1,5},{5,1},{2,6},{6,2},{3,7},{7,3},{8,12},{12,8},{9,1... | collective-permute-start | bytes 2949128 | tf_op jit(solution)/shard_map/cond/branch_1_fun/ppermute | solution.py:829
  215.7 55.0 %collective-permute-start.6 = (bf16[320,1536]{1,0:T(8,128)(2,1)}, bf16[320,1536]{1,0:T(8,128)(2,1)}, u32[]{:S(2)}, u32[]{:S(2)}) collective-permute-start(bf16[320,1536]{1,0:T(8,128)(2,1)} %get-tuple-element.328), channel_id=1, source_target_pairs={{0,6},{2,4},{4,2},{6,0},{1,7},{3,5},{5,3},{7,1},{8,14},{10,12},{12... | collective-permute-start | bytes 2949128 | tf_op jit(solution)/shard_map/cond/branch_1_fun/ppermute | solution.py:853
  217.0 53.7 %collective-permute-start.7 = (bf16[320,1536]{1,0:T(8,128)(2,1)}, bf16[320,1536]{1,0:T(8,128)(2,1)}, u32[]{:S(2)}, u32[]{:S(2)}) collective-permute-start(bf16[320,1536]{1,0:T(8,128)(2,1)} %get-tuple-element.328), channel_id=1, source_target_pairs={{0,1},{1,0},{2,3},{3,2},{4,5},{5,4},{6,7},{7,6},{8,9},{9,8},{10,11... | collective-permute-start | bytes 2949128 | tf_op jit(solution)/shard_map/cond/branch_1_fun/ppermute | solution.py:829
  270.8 158.5 %reduce-scatter.6.cloned.1.call-start = ((), (), s32[]{:S(2)}) async-start(), calls=%async_computation.9 | async-start | bytes 2949120 | tf_op jit(solution)/shard_map/reduce_scatter | solution.py:877
  282.4 10.8 %collective-permute-start.55 = (bf16[1024,1536]{1,0:T(8,128)(2,1)}, bf16[1024,1536]{1,0:T(8,128)(2,1)S(1)}, u32[]{:S(2)}, u32[]{:S(2)}) collective-permute-start(bf16[1024,1536]{1,0:T(8,128)(2,1)} %get-tuple-element.581.refs_10_), channel_id=1, source_target_pairs={{0,1},{1,0},{2,3},{3,2},{4,5},{5,4},{6,7},{7,6},{8,9},{9,8},{10,11... | collective-permute-start | bytes 9437192 | tf_op jit(solution)/shard_map/ppermute | solution.py:829
  301.4 26.4 %collective-permute-start.8 = (bf16[256,1536]{1,0:T(8,128)(2,1)}, bf16[256,1536]{1,0:T(8,128)(2,1)}, u32[]{:S(2)}, u32[]{:S(2)}) collective-permute-start(bf16[256,1536]{1,0:T(8,128)(2,1)} %get-tuple-element.329), channel_id=1, source_target_pairs={{0,2},{2,0},{1,3},{3,1},{4,6},{6,4},{5,7},{7,5},{8,10},{10,8},{9,1... | collective-permute-start | bytes 2359304 | tf_op jit(solution)/shard_map/cond/branch_1_fun/ppermute | solution.py:829
  303.0 24.7 %collective-permute-start.9 = (bf16[256,1536]{1,0:T(8,128)(2,1)}, bf16[256,1536]{1,0:T(8,128)(2,1)}, u32[]{:S(2)}, u32[]{:S(2)}) collective-permute-start(bf16[256,1536]{1,0:T(8,128)(2,1)} %get-tuple-element.330), channel_id=1, source_target_pairs={{0,4},{4,0},{1,5},{5,1},{2,6},{6,2},{3,7},{7,3},{8,12},{12,8},{9,1... | collective-permute-start | bytes 2359304 | tf_op jit(solution)/shard_map/cond/branch_1_fun/ppermute | solution.py:829
  303.6 35.6 %collective-permute-start.10 = (bf16[256,1536]{1,0:T(8,128)(2,1)}, bf16[256,1536]{1,0:T(8,128)(2,1)}, u32[]{:S(2)}, u32[]{:S(2)}) collective-permute-start(bf16[256,1536]{1,0:T(8,128)(2,1)} %get-tuple-element.331), channel_id=1, source_target_pairs={{0,6},{2,4},{4,2},{6,0},{1,7},{3,5},{5,3},{7,1},{8,14},{10,12},{12... | collective-permute-start | bytes 2359304 | tf_op jit(solution)/shard_map/cond/branch_1_fun/ppermute | solution.py:853
  339.3 167.8 %reduce-scatter.8.cloned.1.call-start = ((), (), s32[]{:S(2)}) async-start(), calls=%async_computation.10 | async-start | bytes 2457600 | tf_op jit(solution)/shard_map/reduce_scatter | solution.py:877
  346.4 13.8 %collective-permute-start.58 = (bf16[512,192]{1,0:T(8,128)(2,1)S(1)}, bf16[512,192]{1,0:T(8,128)(2,1)S(1)}, u32[]{:S(2)}, u32[]{:S(2)}) collective-permute-start(bf16[512,192]{1,0:T(8,128)(2,1)S(1)} %bitcast.65), channel_id=1, source_target_pairs={{0,6},{2,4},{4,2},{6,0},{1,7},{3,5},{5,3},{7,1},{8,14},{10,12},{12... | collective-permute-start | bytes 589832 | tf_op jit(solution)/shard_map/ppermute | solution.py:853
  348.0 12.1 %collective-permute-start.57 = (bf16[512,192]{1,0:T(8,128)(2,1)S(1)}, bf16[512,192]{1,0:T(8,128)(2,1)S(1)}, u32[]{:S(2)}, u32[]{:S(2)}) collective-permute-start(bf16[512,192]{1,0:T(8,128)(2,1)S(1)} %bitcast.66), channel_id=1, source_target_pairs={{0,4},{4,0},{1,5},{5,1},{2,6},{6,2},{3,7},{7,3},{8,12},{12,8},{9,1... | collective-permute-start | bytes 589832 | tf_op jit(solution)/shard_map/ppermute | solution.py:829
  349.5 10.4 %collective-permute-start.56 = (bf16[512,192]{1,0:T(8,128)(2,1)S(1)}, bf16[512,192]{1,0:T(8,128)(2,1)S(1)}, u32[]{:S(2)}, u32[]{:S(2)}) collective-permute-start(bf16[512,192]{1,0:T(8,128)(2,1)S(1)} %bitcast.67), channel_id=1, source_target_pairs={{0,2},{2,0},{1,3},{3,1},{4,6},{6,4},{5,7},{7,5},{8,10},{10,8},{9,1... | collective-permute-start | bytes 589832 | tf_op jit(solution)/shard_map/ppermute | solution.py:829
  362.4 38.4 %collective-permute-start.46 = (bf16[1024,1536]{1,0:T(8,128)(2,1)}, bf16[1024,1536]{1,0:T(8,128)(2,1)}, u32[]{:S(2)}, u32[]{:S(2)}) collective-permute-start(bf16[1024,1536]{1,0:T(8,128)(2,1)} %get-tuple-element.375), channel_id=1, source_target_pairs={{0,1},{1,0},{2,3},{3,2},{4,5},{5,4},{6,7},{7,6},{8,9},{9,8},{10,11... | collective-permute-start | bytes 9437192 | tf_op jit(solution)/shard_map/cond/branch_1_fun/ppermute | solution.py:829
  362.6 33.0 %collective-permute-start.42 = (bf16[256,1536]{1,0:T(8,128)(2,1)}, bf16[256,1536]{1,0:T(8,128)(2,1)}, u32[]{:S(2)}, u32[]{:S(2)}) collective-permute-start(bf16[256,1536]{1,0:T(8,128)(2,1)} %get-tuple-element.358), channel_id=1, source_target_pairs={{0,2},{2,0},{1,3},{3,1},{4,6},{6,4},{5,7},{7,5},{8,10},{10,8},{9,1... | collective-permute-start | bytes 2359304 | tf_op jit(solution)/shard_map/cond/branch_1_fun/ppermute | solution.py:829
  364.1 31.6 %collective-permute-start.43 = (bf16[256,1536]{1,0:T(8,128)(2,1)}, bf16[256,1536]{1,0:T(8,128)(2,1)}, u32[]{:S(2)}, u32[]{:S(2)}) collective-permute-start(bf16[256,1536]{1,0:T(8,128)(2,1)} %get-tuple-element.358), channel_id=1, source_target_pairs={{0,4},{4,0},{1,5},{5,1},{2,6},{6,2},{3,7},{7,3},{8,12},{12,8},{9,1... | collective-permute-start | bytes 2359304 | tf_op jit(solution)/shard_map/cond/branch_1_fun/ppermute | solution.py:829
  364.7 36.1 %collective-permute-start.44 = (bf16[256,1536]{1,0:T(8,128)(2,1)}, bf16[256,1536]{1,0:T(8,128)(2,1)}, u32[]{:S(2)}, u32[]{:S(2)}) collective-permute-start(bf16[256,1536]{1,0:T(8,128)(2,1)} %get-tuple-element.358), channel_id=1, source_target_pairs={{0,6},{2,4},{4,2},{6,0},{1,7},{3,5},{5,3},{7,1},{8,14},{10,12},{12... | collective-permute-start | bytes 2359304 | tf_op jit(solution)/shard_map/cond/branch_1_fun/ppermute | solution.py:853
  366.1 34.7 %collective-permute-start.45 = (bf16[256,1536]{1,0:T(8,128)(2,1)}, bf16[256,1536]{1,0:T(8,128)(2,1)}, u32[]{:S(2)}, u32[]{:S(2)}) collective-permute-start(bf16[256,1536]{1,0:T(8,128)(2,1)} %get-tuple-element.358), channel_id=1, source_target_pairs={{0,1},{1,0},{2,3},{3,2},{4,5},{5,4},{6,7},{7,6},{8,9},{9,8},{10,11... | collective-permute-start | bytes 2359304 | tf_op jit(solution)/shard_map/cond/branch_1_fun/ppermute | solution.py:829
  401.4 4.7 collective-permute-start.61
  406.3 16.0 %collective-permute-start.47 = (bf16[512,320]{1,0:T(8,128)(2,1)}, bf16[512,320]{1,0:T(8,128)(2,1)}, u32[]{:S(2)}, u32[]{:S(2)}) collective-permute-start(bf16[512,320]{1,0:T(8,128)(2,1)} %bitcast.16.refs_2_), channel_id=1, source_target_pairs={{0,2},{2,0},{1,3},{3,1},{4,6},{6,4},{5,7},{7,5},{8,10},{10,8},{9,1... | collective-permute-start | bytes 983048 | tf_op jit(solution)/shard_map/cond/branch_1_fun/ppermute | solution.py:829
  407.9 15.6 %collective-permute-start.48 = (bf16[512,320]{1,0:T(8,128)(2,1)}, bf16[512,320]{1,0:T(8,128)(2,1)}, u32[]{:S(2)}, u32[]{:S(2)}) collective-permute-start(bf16[512,320]{1,0:T(8,128)(2,1)} %bitcast.18.refs_3_), channel_id=1, source_target_pairs={{0,4},{4,0},{1,5},{5,1},{2,6},{6,2},{3,7},{7,3},{8,12},{12,8},{9,1... | collective-permute-start | bytes 983048 | tf_op jit(solution)/shard_map/cond/branch_1_fun/ppermute | solution.py:829
  408.5 19.0 %collective-permute-start.49 = (bf16[512,320]{1,0:T(8,128)(2,1)}, bf16[512,320]{1,0:T(8,128)(2,1)}, u32[]{:S(2)}, u32[]{:S(2)}) collective-permute-start(bf16[512,320]{1,0:T(8,128)(2,1)} %bitcast.20.refs_4_), channel_id=1, source_target_pairs={{0,6},{2,4},{4,2},{6,0},{1,7},{3,5},{5,3},{7,1},{8,14},{10,12},{12... | collective-permute-start | bytes 983048 | tf_op jit(solution)/shard_map/cond/branch_1_fun/ppermute | solution.py:853
  430.5 8.2 %collective-permute-start.64 = (bf16[320,1536]{1,0:T(8,128)(2,1)}, bf16[320,1536]{1,0:T(8,128)(2,1)}, u32[]{:S(2)}, u32[]{:S(2)}) collective-permute-start(bf16[320,1536]{1,0:T(8,128)(2,1)} %get-tuple-element.633), channel_id=1, source_target_pairs={{0,1},{1,0},{2,3},{3,2},{4,5},{5,4},{6,7},{7,6},{8,9},{9,8},{10,11... | collective-permute-start | bytes 2949128 | tf_op jit(solution)/shard_map/ppermute | solution.py:829
  430.6 8.1 %collective-permute-start.65 = (bf16[320,1536]{1,0:T(8,128)(2,1)}, bf16[320,1536]{1,0:T(8,128)(2,1)}, u32[]{:S(2)}, u32[]{:S(2)}) collective-permute-start(bf16[320,1536]{1,0:T(8,128)(2,1)} %get-tuple-element.634), channel_id=1, source_target_pairs={{0,1},{1,0},{2,3},{3,2},{4,5},{5,4},{6,7},{7,6},{8,9},{9,8},{10,11... | collective-permute-start | bytes 2949128 | tf_op jit(solution)/shard_map/ppermute | solution.py:829
  431.1 7.6 %collective-permute-start.66 = (bf16[320,1536]{1,0:T(8,128)(2,1)}, bf16[320,1536]{1,0:T(8,128)(2,1)}, u32[]{:S(2)}, u32[]{:S(2)}) collective-permute-start(bf16[320,1536]{1,0:T(8,128)(2,1)} %get-tuple-element.635), channel_id=1, source_target_pairs={{0,1},{1,0},{2,3},{3,2},{4,5},{5,4},{6,7},{7,6},{8,9},{9,8},{10,11... | collective-permute-start | bytes 2949128 | tf_op jit(solution)/shard_map/ppermute | solution.py:829
  433.0 5.7 %collective-permute-start.63 = (bf16[1024,320]{0,1:T(8,128)(2,1)}, bf16[1024,320]{0,1:T(8,128)(2,1)}, u32[]{:S(2)}, u32[]{:S(2)}) collective-permute-start(bf16[1024,320]{0,1:T(8,128)(2,1)} %pad_maximum_fusion.1), channel_id=1, source_target_pairs={{0,1},{1,0},{2,3},{3,2},{4,5},{5,4},{6,7},{7,6},{8,9},{9,8},{10,11... | collective-permute-start | bytes 1966088 | tf_op jit(solution)/shard_map/ppermute | solution.py:829
  438.7 19.9 %collective-permute-start.52 = (bf16[256,1536]{1,0:T(8,128)(2,1)}, bf16[256,1536]{1,0:T(8,128)(2,1)}, u32[]{:S(2)}, u32[]{:S(2)}) collective-permute-start(bf16[256,1536]{1,0:T(8,128)(2,1)} %get-tuple-element.398), channel_id=1, source_target_pairs={{0,2},{2,0},{1,3},{3,1},{4,6},{6,4},{5,7},{7,5},{8,10},{10,8},{9,1... | collective-permute-start | bytes 2359304 | tf_op jit(solution)/shard_map/cond/branch_1_fun/ppermute | solution.py:829
  440.3 20.9 %collective-permute-start.53 = (bf16[256,1536]{1,0:T(8,128)(2,1)}, bf16[256,1536]{1,0:T(8,128)(2,1)}, u32[]{:S(2)}, u32[]{:S(2)}) collective-permute-start(bf16[256,1536]{1,0:T(8,128)(2,1)} %get-tuple-element.399), channel_id=1, source_target_pairs={{0,4},{4,0},{1,5},{5,1},{2,6},{6,2},{3,7},{7,3},{8,12},{12,8},{9,1... | collective-permute-start | bytes 2359304 | tf_op jit(solution)/shard_map/cond/branch_1_fun/ppermute | solution.py:829
  440.9 37.0 %collective-permute-start.54 = (bf16[256,1536]{1,0:T(8,128)(2,1)}, bf16[256,1536]{1,0:T(8,128)(2,1)}, u32[]{:S(2)}, u32[]{:S(2)}) collective-permute-start(bf16[256,1536]{1,0:T(8,128)(2,1)} %get-tuple-element.400), channel_id=1, source_target_pairs={{0,6},{2,4},{4,2},{6,0},{1,7},{3,5},{5,3},{7,1},{8,14},{10,12},{12... | collective-permute-start | bytes 2359304 | tf_op jit(solution)/shard_map/cond/branch_1_fun/ppermute | solution.py:853
  443.2 55.6 %collective-permute-start.50 = (bf16[192,1920]{1,0:T(8,128)(2,1)}, bf16[192,1920]{1,0:T(8,128)(2,1)}, u32[]{:S(2)}, u32[]{:S(2)}) collective-permute-start(bf16[192,1920]{1,0:T(8,128)(2,1)} %constant_dynamic-slice_fusion.1), channel_id=1, source_target_pairs={{0,4},{4,0},{1,5},{5,1},{2,6},{6,2},{3,7},{7,3},{8,12},{12,8},{9,1... | collective-permute-start | bytes 2211848 | tf_op jit(solution)/shard_map/cond/branch_1_fun/ppermute | solution.py:829
  445.0 53.8 %collective-permute-start.51 = (bf16[192,768]{1,0:T(8,128)(2,1)}, bf16[192,768]{1,0:T(8,128)(2,1)}, u32[]{:S(2)}, u32[]{:S(2)}) collective-permute-start(bf16[192,768]{1,0:T(8,128)(2,1)} %constant_dynamic-slice_fusion), channel_id=1, source_target_pairs={{0,4},{4,0},{1,5},{5,1},{2,6},{6,2},{3,7},{7,3},{8,12},{12,8},{9,1... | collective-permute-start | bytes 884744 | tf_op jit(solution)/shard_map/cond/branch_1_fun/ppermute | solution.py:829
  508.0 6.8 %collective-permute-start.67 = (bf16[192,640]{1,0:T(8,128)(2,1)S(1)}, bf16[192,640]{1,0:T(8,128)(2,1)S(1)}, u32[]{:S(2)}, u32[]{:S(2)}) collective-permute-start(bf16[192,640]{1,0:T(8,128)(2,1)S(1)} %constant_dynamic-slice_fusion.4), channel_id=1, source_target_pairs={{0,4},{4,0},{1,5},{5,1},{2,6},{6,2},{3,7},{7,3},{8,12},{12,8},{9,1... | collective-permute-start | bytes 737288 | tf_op jit(solution)/shard_map/ppermute | solution.py:829
  (57 other events, 338.3 us)
Sparse Core Ops, SparseCore 0:
  26.4 43.6 all-gather.3
  71.6 107.6 all-gather.7
  181.0 48.7 all-gather.5
  270.9 104.9 reduce-scatter.3
  378.0 48.5 reduce-scatter.5
  430.6 41.7 reduce-scatter.7

commit v4 on v3

--- a/solution.py
+++ b/solution.py
@@ -329,6 +329,21 @@
     return [side.shape[0] // tile for side in sides]
 
 
+def shared(bounds, others):
+    spans = []
+    for k, (first, last) in enumerate(bounds):
+        for m, (start, stop) in enumerate(others):
+            if max(first, start) < min(last, stop):
+                spans.append((k, m, max(first, start), min(last, stop)))
+    return spans
+
+
+def on_shared(bounds, others, run):
+    step = pl.program_id(0)
+    for k, m, first, last in shared(bounds, others):
+        pl.when(jnp.logical_and(step >= first, step < last))(lambda k=k, m=m: run(k, m))
+
+
 def on_side(bounds, run):
     step = pl.program_id(0)
     for k, (first, last) in enumerate(bounds):
@@ -376,19 +391,21 @@
     )(*sides, gains, weight, *deps)
 
 
-def feed_forward(post, grads, weight, total=None, deps=()):
+def feed_forward(post, grads, weight, cut, totals=(), deps=()):
     depth = post[0].shape[1]
     rows = rows_of(post)
     width = weight.shape[1] // 3
     count = len(post)
-    totals = [] if total is None else [total]
+    unit = post[0].shape[0]
     specs, bounds = side_specs(tiles_of(post), depth)
+    total_specs, total_bounds = side_specs([unit * c // TILE for c in cut], depth)
 
     def body(*refs):
         weight_ref = refs[2 * count]
-        both_ref, act_ref, out_ref = refs[2 * count + 1 + len(totals) + len(deps) :]
-
-        def run(k):
+        total_refs = refs[2 * count + 1 :]
+        both_ref, act_ref, *outs = refs[2 * count + 1 + len(totals) + len(deps) :]
+
+        def run(k, m):
             hidden = dot(refs[k][...], weight_ref[:, : 2 * width])
             act_grad = dot(refs[count + k][...], weight_ref[:, 2 * width :])
             gate, up = hidden[:, :width], hidden[:, width:]
@@ -401,23 +418,27 @@
             both_ref[...] = both
             part = dot(both, weight_ref[:, : 2 * width], 1, 1)
             if totals:
-                part = refs[2 * count + 1][...].astype(F32) + part
-            out_ref[...] = part.astype(BF16)
-
-        on_side(bounds, run)
-
-    widths = (2 * width, width, depth)
-    tile = [pl.BlockSpec((TILE, w), lambda i: (i, 0)) for w in widths]
-    return pl.pallas_call(
+                part = total_refs[m][...].astype(F32) + part
+            outs[m][...] = part.astype(BF16)
+
+        on_shared(bounds, total_bounds, run)
+
+    widths = (2 * width, width)
+    both, act, *outs = pl.pallas_call(
         body,
         grid=(rows // TILE,),
-        in_specs=specs * 2 + [entire(weight)] + tile[2:] * len(totals) + [ANY] * len(deps),
-        out_specs=tile,
-        out_shape=[jax.ShapeDtypeStruct((rows, w), BF16) for w in widths],
+        in_specs=specs * 2
+        + [entire(weight)]
+        + (total_specs if totals else [])
+        + [ANY] * len(deps),
+        out_specs=[pl.BlockSpec((TILE, w), lambda i: (i, 0)) for w in widths] + total_specs,
+        out_shape=[jax.ShapeDtypeStruct((rows, w), BF16) for w in widths]
+        + [jax.ShapeDtypeStruct((unit * c, depth), BF16) for c in cut],
         name="feed_forward",
         cost_estimate=cost(0),
         compiler_params=pltpu.CompilerParams(vmem_limit_bytes=56 << 20),
     )(*post, *grads, weight, *totals, *deps)
+    return both, act, outs
 
 
 def matches(lefts, rights, paired):
@@ -515,45 +536,39 @@
     )(*args, *deps)
 
 
-def project_back(lefts, weights, turns, deps=()):
+def project_back(lefts, weights, turns, cut, unit):
     number = len(weights)
     sides = lefts[0]
     count = len(sides)
-    tile = 2 * TILE
-    counts = tiles_of(sides, tile)
-    depth = weights[0].shape[1] if len(turns[0]) == 2 else weights[0].shape[0]
-    _, bounds = side_specs(counts, depth, tile)
+    depth = weights[0].shape[0]
+    _, bounds = side_specs(tiles_of(sides), depth)
+    out_specs, out_bounds = side_specs([unit * c // TILE for c in cut], depth)
 
     def body(*refs):
         weight_refs = refs[number * count : number * count + number]
-        outs = refs[number * count + number + len(deps) :]
-
-        def run(k):
+        outs = refs[number * count + number :]
+
+        def run(k, m):
             total = None
-            for i, turn in enumerate(turns):
-                left = refs[i * count + k][...]
-                if len(turn) == 2:
-                    part = dot(left, weight_refs[i][turn[0] : turn[1]])
-                else:
-                    part = dot(left, weight_refs[i][:, turn[0] : turn[1]], 1, 1)
+            for i, (first, last) in enumerate(turns):
+                part = dot(refs[i * count + k][...], weight_refs[i][:, first:last], 1, 1)
                 total = part if total is None else total + part
-            outs[k][...] = total.astype(BF16)
-
-        on_side(bounds, run)
+            outs[m][...] = total.astype(BF16)
+
+        on_shared(bounds, out_bounds, run)
 
     widths = [left[0].shape[1] for left in lefts]
     return pl.pallas_call(
         body,
-        grid=(sum(counts),),
-        in_specs=[spec for w in widths for spec in side_specs(counts, w, tile)[0]]
-        + [pl.BlockSpec(w.shape, lambda i: (0, 0)) for w in weights]
-        + [ANY] * len(deps),
-        out_specs=side_specs(counts, depth, tile)[0],
-        out_shape=[jax.ShapeDtypeStruct((side.shape[0], depth), BF16) for side in sides],
+        grid=(rows_of(sides) // TILE,),
+        in_specs=[spec for w in widths for spec in side_specs(tiles_of(sides), w)[0]]
+        + [entire(w) for w in weights],
+        out_specs=out_specs,
+        out_shape=[jax.ShapeDtypeStruct((unit * c, depth), BF16) for c in cut],
         name="project_back",
         cost_estimate=cost(0),
         compiler_params=pltpu.CompilerParams(vmem_limit_bytes=56 << 20),
-    )(*[side for left in lefts for side in left], *weights, *deps)
+    )(*[side for left in lefts for side in left], *weights)
 
 
 def row_tiles(array, first=0, tile=TILE):
@@ -690,42 +705,74 @@
 
 
 def core_sum(near, far):
-    rows, width = near.shape[0] // 4, near.shape[1]
-
-    def body(near_ref, far_ref, *outs):
+    rows, width = far.shape[0] // 4, far.shape[1]
+
+    def body(three_ref, one_ref, far_ref, *outs):
         for part, out in enumerate(outs):
 
             @pl.when(pl.program_id(0) == part)
-            def _(out=out):
+            def _(out=out, near_ref=three_ref if part < 3 else one_ref):
                 out[...] = (near_ref[...].astype(F32) + far_ref[...].astype(F32)).astype(out.dtype)
 
-    tile = pl.BlockSpec((rows, width), lambda i: (i, 0))
+    def tile(last):
+        return pl.BlockSpec((rows, width), lambda i: (jnp.minimum(i, last), 0))
+
     return pl.pallas_call(
         body,
         grid=(4,),
-        in_specs=[tile, tile],
-        out_specs=[pl.BlockSpec((rows, width), lambda i: (0, 0))] * 4,
+        in_specs=[tile(2), tile(0), tile(3)],
+        out_specs=[tile(0)] * 4,
         out_shape=[
             jax.ShapeDtypeStruct((rows, width), dtype) for dtype in (F32, BF16, BF16, BF16)
         ],
         name="core_sum",
         cost_estimate=cost(0),
-        compiler_params=pltpu.CompilerParams(vmem_limit_bytes=48 << 20),
-    )(near, far)
-
-
-def turn(weight, spans):
+        compiler_params=pltpu.CompilerParams(vmem_limit_bytes=60 << 20),
+    )(*near, far)
+
+
+def corner_sum(for_y, for_x, by_x, by_y):
+    half = by_x.shape[0]
+
+    def body(y_ref, x_ref, by_x_ref, by_y_ref, y_out, x_out):
+        def total(left, right):
+            return (left.astype(F32) + right.astype(F32)).astype(BF16)
+
+        y_out[:half] = total(y_ref[:half], by_x_ref[...])
+        y_out[half:] = y_ref[half:]
+        x_out[:half] = x_ref[:half]
+        x_out[half:] = total(x_ref[half:], by_y_ref[...])
+
+    return pl.pallas_call(
+        body,
+        out_shape=[jax.ShapeDtypeStruct(for_y.shape, BF16)] * 2,
+        name="corner_sum",
+        cost_estimate=cost(0),
+        compiler_params=pltpu.CompilerParams(vmem_limit_bytes=60 << 20),
+    )(for_y, for_x, by_x, by_y)
+
+
+def turn(weight, spans, held, span):
+    rows = weight.shape[0]
+
     def body(ref, *outs):
         turned = ref[...].T
         for (first, last), out in zip(spans, outs):
             out[...] = turned[first:last]
+        count = rows // span * held
+        row = lax.broadcasted_iota(jnp.int32, (rows, count), 0)
+        column = lax.broadcasted_iota(jnp.int32, (rows, count), 1)
+        here = jnp.logical_and(row // span == column // held, row % span == column % held)
+        gains = dot(turned[spans[1][0] : spans[1][0] + 8], jnp.where(here, 1.0, 0.0).astype(BF16))
+        query, key = gains[2:3, :HEAD_DIM], gains[2:3, HEAD_DIM:]
+        outs[-1][...] = jnp.concatenate([query] * GROUP + [key], axis=1)
 
     return pl.pallas_call(
         body,
         out_shape=[
-            jax.ShapeDtypeStruct((last - first, weight.shape[0]), weight.dtype)
-            for first, last in spans
-        ],
+            jax.ShapeDtypeStruct((last - first, rows), weight.dtype) for first, last in spans
+        ]
+        + [jax.ShapeDtypeStruct((1, QK), F32)],
         name="turn",
         cost_estimate=cost(0),
         compiler_params=pltpu.CompilerParams(vmem_limit_bytes=48 << 20),
@@ -838,20 +885,26 @@
     return near + [first] + [swap(piece, "c") for piece in near[1:]]
 
 
-def staged_gather(rows, between=()):
-    half = rows.shape[0] // 2
-    from_y = swap(rows, "y")
-    if between:
-        from_y = after(from_y, *between)
-    from_x = swap(rows, "x")
-    corner = jnp.concatenate([swap(from_y[:half], "x"), swap(from_x[half:], "y")])
-    near = [rows, from_y, from_x, corner]
-    return near + [swap(piece, "c") for piece in near]
+def sides_come(rows):
+    return swap(rows, "y"), swap(rows, "x")
+
+
+def corner_comes(from_y, from_x):
+    half = from_y.shape[0] // 2
+    return swap(from_y[:half], "x"), swap(from_x[half:], "y")
+
+
+def across(pieces):
+    return [swap(piece, "c") for piece in pieces]
+
+
+def opposite(rows):
+    return lax.ppermute(rows, ("x", "y"), ((0, 3), (1, 2), (2, 1), (3, 0)))
 
 
 def diamond(for_y, for_x, for_both):
-    across = lax.ppermute(for_both, ("x", "y"), ((0, 3), (1, 2), (2, 1), (3, 0)))
-    return swap(for_y, "y"), swap(for_x, "x"), across
+    both = opposite(for_both)
+    return swap(for_y, "y"), swap(for_x, "x"), both
 
 
 def exchange_near(pairs):
@@ -891,10 +944,9 @@
     return out.reshape(-1, payload.shape[2])
 
 
-def from_x(sums):
+def for_x_side(sums):
     rows = sums.shape[0] // 2
-    place = lax.axis_index("x")
-    return swap(lax.dynamic_slice_in_dim(sums, (1 - place) * rows, rows, 0), "x")
+    return lax.dynamic_slice_in_dim(sums, (1 - lax.axis_index("x")) * rows, rows, 0)
 
 
 def on_device(
@@ -927,7 +979,7 @@
     gain_rows = jnp.pad(gain_rows, ((0, 0), (0, GAIN_LANES - 3)))
     own_hidden = layer_input.reshape(own_rows, model_width)
     own_upstream = upstream.reshape(own_rows, model_width)
-    cut = 640
+    cut = 512
     rest = -(wide - cut) % 128
     (first_payload,) = pack_columns(
         [query_weight, key_weight, value_weight, output_weight],
@@ -937,35 +989,39 @@
         ],
         gain_rows,
     )
-    first_block = plane_columns(first_payload)
+
+    def start(payload, own_hidden):
+        return plane_columns(payload), sides_come(own_hidden)
+
+    first_block, hidden_sides = together(start, first_payload, own_hidden)
     first_full = line_gather(first_block)
-    (second_payload,) = pack_columns(
+    payloads = pack_columns(
         [gate_weight, up_weight, down_weight],
         [
-            [(0, 0, cut), (1, 0, cut), (2, 0, cut)]
-            + [(0, cut, wide), rest, (1, cut, wide), rest, (2, cut, wide), rest],
+            [(0, 0, cut), (1, 0, cut), (2, 0, cut)],
+            [(0, cut, wide), rest, (1, cut, wide), rest, (2, cut, wide), rest],
         ],
     )
 
-    second_block = plane_columns(after(second_payload, first_block))
-    ffn_blocks = [second_block[:, : 3 * cut], second_block[:, 3 * cut :]]
+    def begin(own_hidden, hidden_sides, payloads):
+        corner = corner_comes(*hidden_sides)
+        far = across([own_hidden, *hidden_sides])
+        blocks = [plane_columns(payload) for payload in payloads]
+        return corner, far, blocks, rotary_rows(4 * tokens)
+
+    corner, far, ffn_blocks, (cosine, sine) = together(
+        begin, own_hidden, hidden_sides, [after(payload, first_block) for payload in payloads]
+    )
+    corner = jnp.concatenate(corner)
+    hidden = [own_hidden, *hidden_sides, corner, *far, swap(corner, "c")]
     ffn_full = [line_gather(block) for block in ffn_blocks]
-
-    def begin(own_hidden):
-        tables = rotary_rows(4 * tokens)
-        return staged_gather(own_hidden, tables), tables
-
-    hidden, (cosine, sine) = together(begin, after(own_hidden, *ffn_blocks))
-
     out_first = qkv_cols + GAIN_LANES
-    qkv_rows, gain_turned, out_rows = turn(
+    qkv_rows, gain_turned, out_rows, head_scale = turn(
         first_full,
         [(0, qkv_cols), (qkv_cols, qkv_cols + 16), (out_first, out_first + query_cols)],
-    )
-    head_scale = gain_turned[2].astype(F32).reshape(-1, rows)[:, :head_rows].reshape(-1)
-    head_scale = jnp.concatenate(
-        [jnp.tile(head_scale[:HEAD_DIM], GROUP), head_scale[HEAD_DIM:]]
-    ).reshape(1, QK)
+        head_rows,
+        rows,
+    )
 
     def attend(hidden, gain_turned, first_full, out_rows, head_scale, cosine, sine):
         out_near, out_first = plane_near(out_rows)
@@ -989,40 +1045,62 @@
 
     def attended(mixed, out_weights, own_hidden, own_upstream, gain_turned):
         came = exchange_near([pair.reshape(-1, query_cols) for pair in mixed])
-        grads = staged_gather(own_upstream)
+        grad_sides = sides_come(after(own_upstream, *came[1:]))
         out_weights = plane_all(out_weights)
         middle, post = attend_out(exchange_all(came), out_weights, own_hidden, gain_turned)
-        return middle, staged_gather(post)[1:], grads[1:], post, out_weights[5:]
-
-    middle, post, grads, post_own, out_far = together(
+        grad_far = across([own_upstream, *grad_sides])
+        post_far = across([post])
+        return middle, post, sides_come(post), post_far, grad_sides, grad_far, out_weights[5:]
+
+    middle, post_own, post_sides, post_far, grad_sides, grad_far, out_far = together(
         attended, mixed, out_weights, own_hidden, own_upstream, gain_turned
     )
-    post, grads = [post_own] + post, [own_upstream] + grads
+    post = [post_own, *post_sides]
+    grads = [own_upstream, *grad_sides]
     out_weights = [*out_weights[0], out_weights[1], *out_far]
 
-    def first_chunk(post, grads, weight, qkv_rows):
-        qkv_near, qkv_first = plane_near(qkv_rows)
-        near = feed_forward(post[:4], grads[:4], weight)
-        far = feed_forward(post[4:], grads[4:], weight)
-        both, act, total = zip(near, far)
-        return both, act, total, weight_grads([(post, both), (grads, act)]), (
-            qkv_near[1:],
-            qkv_first,
-        )
-
-    both_0, act_0, total, parts_0, (qkv_near, qkv_first) = together(
-        first_chunk, post, grads, ffn_full[0], qkv_rows
-    )
+    def first_blocks(post, grads, weight):
+        corner = corner_comes(*post[1:])
+        grad_corner = corner_comes(*grads[1:])
+        far = across(post[1:])
+        return corner, grad_corner, far, feed_forward(post, grads, weight, [3])
+
+    corner, grad_corner, far, early = together(first_blocks, post, grads, ffn_full[0])
+    corner, grad_corner = jnp.concatenate(corner), jnp.concatenate(grad_corner)
+    post = [*post, corner, *post_far, *far, swap(corner, "c")]
+    grads = [*grads, grad_corner, *grad_far, swap(grad_corner, "c")]
+
+    def first_chunk(post, grads, weight, qkv_rows, early):
+        qkv_sides = sides_come(qkv_rows)
+        late = feed_forward(post[3:], grads[3:], weight, [1, 4])
+        both, act = [early[0], late[0]], [early[1], late[1]]
+        parts = weight_grads([(post, both), (grads, act)])
+        return late, parts, qkv_sides
+
+    late, parts_0, qkv_sides = together(
+        first_chunk, post, grads, ffn_full[0], qkv_rows, early
+    )
+    both_0, act_0, total = [early[0], late[0]], [early[1], late[1]], early[2] + late[2]
     sums_0 = line_scatter(parts_0)
-    far = feed_forward(post[4:], grads[4:], ffn_full[1], total[1], deps=[parts_0])
-    near = feed_forward(post[:4], grads[:4], ffn_full[1], total[0], deps=far[2:])
-    both_1, act_1, (near, far) = zip(near, far)
-    mine, *parts = core_sum(near, swap(far, "c"))
+
+    def second_chunk(post, grads, weight, total, qkv_sides):
+        qkv_corner = corner_comes(*qkv_sides)
+        return qkv_corner, feed_forward(post, grads, weight, [1, 4], total)
+
+    qkv_corner, late = together(
+        second_chunk, post[3:], grads[3:], ffn_full[1], total[1:], qkv_sides
+    )
+    far = swap(late[2][1], "c")
+    early = feed_forward(post[:3], grads[:3], ffn_full[1], [3], total[:1], late[2][1:])
+    both_1, act_1 = [early[0], late[0]], [early[1], late[1]]
+    qkv_corner = jnp.concatenate(qkv_corner)
+    mine, *parts = core_sum(early[2] + late[2][:1], far)
+    qkv_weights = [qkv_rows, *qkv_sides, qkv_corner]
 
     def behind(parts, post, grads, act_0, act_1, both_1, weights):
         others = diamond(*parts)
-        columns = [(2 * weight.shape[1] // 3, weight.shape[1], True) for weight in weights]
-        branch = project_back([act_0, act_1], weights, columns)
+        columns = [(2 * weight.shape[1] // 3, weight.shape[1]) for weight in weights]
+        branch = project_back([act_0, act_1], weights, columns, [3, 1, 4], own_rows)
         parts_1 = weight_grads([(post, both_1), (grads, act_1)])
         return others, parts_1, branch
 
@@ -1033,27 +1111,35 @@
         mine, others, middle, own_upstream, out_weights, gain_turned
     )
 
+    branch_far = swap(branch[2], "c")
+
     near, far = exchange_all(exchange_near([pair.reshape(-1, query_cols) for pair in pairs]))
     mixed_grad = jnp.concatenate([*[pair[:own_rows] for pair in near], far])
 
-    def back(middle_low, qkv, mixed, mixed_grad, stats, head_scale, cosine, sine, branch):
+    def back(middle_low, qkv, mixed, mixed_grad, stats, head_scale, cosine, sine):
         middle_near, middle_first = plane_near(middle_low)
-        branch_far = swap(branch[1], "c")
         qkv_grad, head_part = backward_attention(
             place, qkv, mixed, mixed_grad, stats, head_scale, cosine, sine
         )
-        return middle_near[1:], middle_first, qkv_grad, head_part, branch_far
+        return middle_near[1:], middle_first, qkv_grad, head_part
 
     mixed_grad = mixed_grad.reshape(8, batch, tokens, query_cols)
-    middle_near, middle_first, qkv_grad, head_part, branch_far = together(
-        back, middle_low, qkv, mixed, mixed_grad, stats, head_scale, cosine, sine, branch
+    middle_near, middle_first, qkv_grad, head_part = together(
+        back,
+        middle_low,
+        qkv,
+        mixed,
+        mixed_grad,
+        stats,
+        head_scale,
+        cosine,
+        sine,
     )
     middle_whole = plane_all(([middle_low, *middle_near], middle_first))
     sums_1 = line_scatter(parts_1)
-    gain_parts = after(feedforward_part, sums_0)
-    gain_parts = jnp.pad(gain_parts[0][:, None], ((0, 0), (1, GAIN_LANES - 2)))
-
-    def attention_grads(qkv_grad, normed, middle_whole, mixed, first_full, gain_parts, head_part):
+    gain_parts = jnp.pad(feedforward_part[0][:, None], ((0, 0), (1, GAIN_LANES - 2)))
+
+    def attention_grads(branch, sums_0, qkv_grad, normed, middle_whole, mixed, first_full, gain_parts, head_part):
         qkv_grad = [pair.reshape(-1, qkv_cols) for pair in qkv_grad]
         mixed = [pair.reshape(-1, query_cols) for pair in mixed]
         came = exchange_near(qkv_grad)
@@ -1062,10 +1148,12 @@
             gains=(first_full, gain_parts, head_part, head_rows),
             paired=True,
         )
-        return came[1:], parts
-
-    came, attention_parts = together(
+        return came[1:], parts, core_sum(*branch), for_x_side(sums_0)
+
+    came, attention_parts, branch, send_0 = together(
         attention_grads,
+        (branch[:2], branch_far),
+        sums_0,
         qkv_grad,
         normed,
         middle_whole,
@@ -1077,44 +1165,60 @@
     attention_sums = line_scatter(after(attention_parts, sums_1))
     x = lax.axis_index("x").astype(jnp.int32).reshape(1)
 
-    branch_mine, *branch_parts = core_sum(branch[0], branch_far)
-    qkv_pairs = exchange_all([qkv_grad[0].reshape(-1, qkv_cols), *came])
-    qkv_weights = plane_all(([qkv_rows, *qkv_near], qkv_first))
-
-    def finish(branch_parts, sums_0, sums_1, qkv_pairs, qkv_weights, own_hidden, middle_grad, gain_turned):
-        branch_others = diamond(*branch_parts)
-        others = from_x(sums_0), from_x(sums_1)
+    branch_mine, for_y, for_x, corner = branch
+    middle_rows = own_rows // 2
+
+    def corners(corner, send_0, qkv_pair, came, qkv_weights):
+        by_x, by_y = swap(corner[:middle_rows], "x"), swap(corner[middle_rows:], "y")
+        other_0 = swap(send_0, "x")
+        return by_x, by_y, other_0, exchange_all([qkv_pair, *came])[1], across(qkv_weights)
+
+    by_x, by_y, other_0, pairs_far, qkv_far = together(
+        corners, corner, send_0, qkv_grad[0].reshape(-1, qkv_cols), came, qkv_weights
+    )
+    qkv_weights = qkv_weights + qkv_far
+    for_y, for_x = corner_sum(for_y, for_x, by_x, by_y)
+    qkv_pairs = [qkv_grad[0].reshape(-1, qkv_cols), *came], pairs_far
+
+    def sides(for_y, for_x, sums_1, qkv_pairs, qkv_weights, own_hidden, middle_grad, gain_turned):
+        others = swap(for_y, "y"), swap(for_x, "x"), swap(for_x_side(sums_1), "x")
         input_grad = input_back(qkv_pairs, qkv_weights, own_hidden, middle_grad, gain_turned)
-        return branch_others, others, input_grad
-
-    branch_others, others, input_grad = together(
-        finish,
-        branch_parts,
+        return *others, input_grad
+
+    *branch_others, other_1, input_grad = together(
+        sides, for_y, for_x, sums_1, qkv_pairs, qkv_weights, own_hidden, middle_grad, gain_turned
+    )
+    x = lax.axis_index("x").astype(jnp.int32).reshape(1)
+
+    def last(attention_sums, sums_0, sums_1, other_0, other_1, middle, branch_mine, branch_others):
+        ffn_grads = unpack_columns(
+            x,
+            [sums_0, sums_1],
+            [other_0, other_1],
+            [
+                [
+                    (0, index * cut, (index + 1) * cut),
+                    (1, index * (wide - cut + rest), (index + 1) * (wide - cut + rest) - rest),
+                ]
+                for index in range(3)
+            ]
+            + [None],
+        )
+        layer_output = (middle + scatter_end(branch_mine, branch_others)).astype(BF16)
+        return swap(for_x_side(attention_sums), "x"), ffn_grads, layer_output
+
+    attention_other, ffn_grads, layer_output = together(
+        last,
+        attention_sums,
         sums_0,
         sums_1,
-        qkv_pairs,
-        qkv_weights,
-        own_hidden,
-        middle_grad,
-        gain_turned,
-    )
-    layer_output = (middle + scatter_end(branch_mine, branch_others)).astype(BF16)
-    x = lax.axis_index("x").astype(jnp.int32).reshape(1)
-    ffn_grads = unpack_columns(
-        x,
-        [sums_0, sums_1],
-        others,
-        [
-            [
-                (0, index * cut, (index + 1) * cut),
-                (1, index * (wide - cut + rest), (index + 1) * (wide - cut + rest) - rest),
-            ]
-            for index in range(3)
-        ]
-        + [None],
-    )
-
-    attention_sums = after(attention_sums, layer_output, ffn_grads[0])
+        other_0,
+        after(other_1, attention_sums),
+        middle,
+        branch_mine,
+        branch_others,
+    )
+
     key_first, value_first = query_cols, query_cols + kv_cols
     (
         query_weight_grad,
@@ -1125,7 +1229,7 @@
     ) = unpack_columns(
         x,
         [attention_sums],
-        [from_x(attention_sums)],
+        [attention_other],
         [
             [(0, 0, query_cols)],
             [(0, key_first, value_first)],
@@ -1134,12 +1238,19 @@
             (0, qkv_cols, qkv_cols + GAIN_LANES),
         ],
     )
-    for axis in ("y", "c"):
-        count = gain_sums.shape[0] // 2
-        index = lax.axis_index(axis)
-        keep = lax.dynamic_slice_in_dim(gain_sums, index * count, count, 0)
-        send = lax.dynamic_slice_in_dim(gain_sums, (1 - index) * count, count, 0)
-        gain_sums = keep + swap(send, axis)
+    size = gain_sums.shape[0] // 4
+    index = place[0]
+
+    def quarter(k):
+        return lax.dynamic_slice_in_dim(gain_sums, jnp.bitwise_xor(index, k) * size, size, 0)
+
+    facing = ((0, 3), (1, 2), (2, 1), (3, 0))
+    gain_sums = (
+        quarter(0)
+        + swap(quarter(1), "c")
+        + swap(quarter(2), "y")
+        + lax.ppermute(quarter(3), ("y", "c"), facing)
+    )
     gain_sums = gain_sums[:, :3].T
     return (
         layer_output.reshape(layer_input.shape),

time: 540 us -> 511 us (0.946)
  waiting for transfers between devices: 160 us -> 119 us
  local copies, waits for them, and re-layouts: 41.5 us -> 53.5 us
  starting transfers between devices: 49.3 us -> 60.6 us
  other arithmetic: 17.8 us -> 8.23 us
  Pallas kernels: 204 us -> 210 us
    ppermute x8 -> x7, waiting for transfers between devices: 45.4 us -> 15 us  [the longest x6 13.8 us: opposite(): return lax.ppermute(rows, ('x', 'y'), ((0, 3), (1, 2), (2, 1), (3, 0)))]
    convert_element_type x5 -> x0, other arithmetic: 12 us -> none  [the longest x3 7.57 us: scatter_end(): mine = mine + other.astype(F32)]
    ppermute x62 -> x66, waiting for transfers between devices: 114 us -> 103 us  [swap(): return lax.ppermute(values, axis, SWAP)]
    ppermute x62 -> x66, starting transfers between devices: 38.4 us -> 44.4 us  [swap(): return lax.ppermute(values, axis, SWAP)]
    pallas_call x4 -> x5, Pallas kernels: 25.8 us -> 31 us  [the longest x1 13.2 us: project_back(): pl.pallas_call(body, grid=(rows_of(sides) // TILE,), in_specs=[spec for w...]
    unnamed x62 -> x95, local copies, waits for them, and re-layouts: 12.5 us -> 17.4 us
    ppermute x8 -> x7, starting transfers between devices: 10.7 us -> 11.7 us  [the longest x6 10.4 us: opposite(): return lax.ppermute(rows, ('x', 'y'), ((0, 3), (1, 2), (2, 1), (3, 0)))]
  transfers between devices with their start and end apart: 76 -> 80, of which waited for: 32 -> 28; matrix products, arithmetic and copies ran while one was open for 8% -> 8% of each run, Pallas kernels for 38% -> 41%
where the time goes in v4:
time: 511 us; the launch traced here: 505 us
  Pallas kernels  210 us (41%)
  waiting for transfers between devices  119 us (23%)
  starting transfers between devices  60.6 us (12%)
  local copies, waits for them, and re-layouts  53.5 us (10%)
  blocking collectives  39 us (8%)
  between operations  15 us (3%)
  other arithmetic  8.23 us (2%)
    ppermute x66, waiting for transfers between devices, swap(): return lax.ppermute(values, axis, SWAP)  103 us
    pallas_call x4, Pallas kernels, feed_forward(): pl.pallas_call(body, grid=(rows // TILE,), in_specs=specs * 2 + [entire(w...  55.3 us
    ppermute x66, starting transfers between devices, swap(): return lax.ppermute(values, axis, SWAP)  44.4 us
    pallas_call x2, Pallas kernels, attention_call(): pl.pallas_call(body, grid_spec=pltpu.PrefetchScalarGridSpec(num_scalar_pr...  41.1 us
    pallas_call x3, Pallas kernels, weight_grads(): pl.pallas_call(body, grid=(depth // tile,), in_specs=specs + [ANY] * len(...  39.5 us
    all_to_all x2, blocking collectives, plane_columns(): lax.all_to_all(payload, PLANE, split_axis=0, concat_axis=0, tiled=True)  39 us
    unnamed x95, local copies, waits for them, and re-layouts  17.4 us
    ppermute x6, waiting for transfers between devices, opposite(): return lax.ppermute(rows, ('x', 'y'), ((0, 3), (1, 2), (2, 1), (3, 0)))  13.8 us
  transfers between devices with their start and end apart: 80, of which 28 were waited for; matrix products, arithmetic and copies ran while one was open for 8% of the time, Pallas kernels for 41%

profile of v4, /device:TPU:0, one launch (start us, length us, event | category | flops | bytes accessed | tf_op | source)
XLA Modules:
  0.0 505.3 jit_solution(12656968135697586516)
XLA Ops:
  12.3 27.5 %conditional.13 = (bf16[384,640]{1,0:T(8,128)(2,1)S(1)}, bf16[256,1536]{1,0:T(8,128)(2,1)}, bf16[256,1536]{1,0:T(8,128)(2,1)}) conditional(s32[]{:T(128)} %convert_element_type.48, () %tuple.123, (bf16[8,48,640]{2,1,0:T(8,128)(2,1)S(1)}, bf16[256,1536]{1,0:T(8,128)(2,1)}) %tuple.217), branch_computations={%region_0.1_spmd, %region_1.2_spmd} | conditional | bytes 7274600 | solution.py:939
  12.3 3.0 collective-permute-start.1
  16.9 23.0 %all_to_all.12 = bf16[8,48,640]{2,1,0:T(8,128)(2,1)S(1)} all-to-all(bf16[8,48,640]{2,1,0:T(8,128)(2,1)S(1)} %get-tuple-element.363), channel_id=1, replica_groups=mesh['dp'=4,'x'=2,'y'=2,'c'=2] {'x','y','c'}, dimensions={0} | all-to-all | bytes 983040 | tf_op jit(solution)/shard_map/cond/branch_1_fun/all_to_all | solution.py:943
  40.7 1.9 pack_columns.3
  44.0 44.6 %conditional.14 = (bf16[128,1536]{1,0:T(8,128)(2,1)}, bf16[128,1536]{1,0:T(8,128)(2,1)}, bf16[256,1536]{1,0:T(8,128)(2,1)}, bf16[256,1536]{1,0:T(8,128)(2,1)}, b...) conditional(s32[]{:T(128)} %convert_element_type.48, () %tuple.125, ...), branch_computations={%region_2.3_spmd, %region_3.4_spmd} | conditional | flops 33889 | bytes 19735088 | solution.py:939
  44.0 16.1 %all_to_all.13 = bf16[8,48,1152]{2,1,0:T(8,128)(2,1)S(1)} all-to-all(bf16[8,48,1152]{2,1,0:T(8,128)(2,1)S(1)} %get-tuple-element.369), channel_id=1, replica_groups=mesh['dp'=4,'x'=2,'y'=2,'c'=2] {'x','y','c'}, dimensions={0} | all-to-all | bytes 1769472 | tf_op jit(solution)/shard_map/cond/branch_1_fun/all_to_all | solution.py:943
  60.0 4.3 all-to-all-start.1
  70.6 3.0 multiply_sine_fusion
  73.6 3.1 rotary_rows.1
  76.7 11.9 %collective-permute-done.24 = bf16[128,1536]{1,0:T(8,128)(2,1)} collective-permute-done((bf16[128,1536]{1,0:T(8,128)(2,1)S(1)}, bf16[128,1536]{1,0:T(8,128)(2,1)}, u32[]{:S(2)}, u32[]{:S(2)}) %collective-permute-start.24) | collective-permute-done | bytes 393248 | tf_op jit(solution)/shard_map/cond/branch_1_fun/ppermute | solution.py:876
  91.8 3.5 turn.1
  96.1 29.4 %conditional.15 = (bf16[192,1536]{1,0:T(8,128)(2,1)}, bf16[192,1536]{1,0:T(8,128)(2,1)}, bf16[192,1536]{1,0:T(8,128)(2,1)}, bf16[192,1536]{1,0:T(8,128)(2,1)}, b...) conditional(s32[]{:T(128)} %convert_element_type.48, () %tuple.122, ...), branch_computations={%region_4.5_spmd, %region_5.6_spmd} | conditional | flops 2 | bytes 17826096 | solution.py:939
  100.0 10.5 %norm_project.1 = (bf16[2048,1536]{1,0:T(8,128)(2,1)}, bf16[2048,320]{1,0:T(8,128)(2,1)}) custom-call(bf16[256,1536]{1,0:T(8,128)(2,1)S(1)} %get-tuple-element.373.refs_0_, bf16[256,1536]{1,0:T(8,128)(2,1)} %get-tuple-element.374.refs_1_, bf16[256,1536]{1,0:T(8,128)(2,1)} %get-tuple-element.375.refs_2_, bf16[256,1536]{1,0:T(8,128)(2,1)} %get-tuple-element.376.refs_3_, ...), custom_call_target="tpu_custom_call" | custom-call | flops 1 | bytes 1 | tf_op jit(solution)/shard_map/cond/branch_1_fun/norm_project/pallas_call | solution.py:371
  110.6 14.4 %attend_forward.1 = (bf16[2,1,256,192]{3,2,1,0:T(8,128)(2,1)}, bf16[2,1,256,192]{3,2,1,0:T(8,128)(2,1)S(1)}, bf16[2,1,256,192]{3,2,1,0:T(8,128)(2,1)S(1)}, bf16[...) custom-call(s32[1]{0:T(128)} %get-tuple-element.385.place_ref, bf16[8,1,256,320]{3,2,1,0:T(8,128)(2,1)} %bitcast.3.refs_0_, ...), custom_call_target="tpu_custom_call" | custom-call | flops 1 | bytes 1 | tf_op jit(solution)/shard_map/cond/branch_1_fun/attend_forward/pallas_call | solution.py:222
  126.5 55.0 %conditional.16 = (f32[256,1536]{1,0:T(8,128)}, bf16[256,1536]{1,0:T(8,128)(2,1)}, bf16[256,1536]{1,0:T(8,128)(2,1)}, bf16[256,1536]{1,0:T(8,128)(2,1)}, bf16[25...) conditional(s32[]{:T(128)} %convert_element_type.48, () %tuple.121, ...), branch_computations={%region_6.7_spmd, %region_7.8_spmd} | conditional | flops 1572865 | bytes 45024160 | solution.py:939
  130.9 5.7 %collective-permute-done.30.refs_3_ = bf16[512,192]{1,0:T(8,128)(2,1)S(1)} collective-permute-done((bf16[512,192]{1,0:T(8,128)(2,1)S(1)}, bf16[512,192]{1,0:T(8,128)(2,1)S(1)}, u32[]{:S(2)}, u32[]{:S(2)}) %collective-permute-start.30) | collective-permute-done | bytes 196640 | tf_op jit(solution)/shard_map/cond/branch_1_fun/ppermute | solution.py:902
  136.6 4.6 collective-permute-done.29.refs_2_
  146.2 1.8 collective-permute-done.33.refs_14_
  151.8 5.5 %attend_out.1 = (f32[256,1536]{1,0:T(8,128)}, bf16[256,1536]{1,0:T(8,128)(2,1)}) custom-call(bf16[512,192]{1,0:T(8,128)(2,1)S(1)} %bitcast.79, bf16[512,192]{1,0:T(8,128)(2,1)S(1)} %copy-done.5, bf16[512,192]{1,0:T(8,128)(2,1)S(1)} %copy-done.3, bf16[512,192]{1,0:T(8,128)(2,1)S(1)} %copy-done.1, ...), custom_call_target="tpu_custom_call" | custom-call | flops 1 | bytes 1 | tf_op jit(solution)/shard_map/cond/branch_1_fun/attend_out/pallas_call | solution.py:609
  159.5 4.9 collective-permute-done.39
  165.8 14.5 %collective-permute-done.36 = bf16[256,1536]{1,0:T(8,128)(2,1)} collective-permute-done((bf16[256,1536]{1,0:T(8,128)(2,1)}, bf16[256,1536]{1,0:T(8,128)(2,1)}, u32[]{:S(2)}, u32[]{:S(2)}) %collective-permute-start.36) | collective-permute-done | bytes 786464 | tf_op jit(solution)/shard_map/cond/branch_1_fun/ppermute | solution.py:876
  181.5 23.8 %conditional.17 = (bf16[128,1536]{1,0:T(8,128)(2,1)}, bf16[128,1536]{1,0:T(8,128)(2,1)}, bf16[128,1536]{1,0:T(8,128)(2,1)}, bf16[128,1536]{1,0:T(8,128)(2,1)}, b...) conditional(s32[]{:T(128)} %convert_element_type.48, () %tuple.129, ...), branch_computations={%region_8.9_spmd, %region_9.10_spmd} | conditional | flops 1 | bytes 15728953 | solution.py:939
  189.0 3.7 collective-permute-done.7
  193.3 11.9 %feed_forward.4 = (bf16[768,1024]{1,0:T(8,128)(2,1)}, bf16[768,512]{1,0:T(8,128)(2,1)}, bf16[768,1536]{1,0:T(8,128)(2,1)}) custom-call(bf16[256,1536]{1,0:T(8,128)(2,1)} %get-tuple-element.412.refs_0_, bf16[256,1536]{1,0:T(8,128)(2,1)} %get-tuple-element.408.refs_1_, bf16[256,1536]{1,0:T(8,128)(2,1)} %get-tuple-element.409.refs_2_, ...), custom_call_target="tpu_custom_call" | custom-call | flops 1 | bytes 1 | tf_op jit(solution)/shard_map/cond/branch_1_fun/feed_forward/pallas_call | solution.py:427
  210.2 2.0 collective-permute-done.59
  213.1 34.9 %conditional.18 = (bf16[1280,512]{1,0:T(8,128)(2,1)}, bf16[256,1536]{1,0:T(8,128)(2,1)}, bf16[1024,1536]{1,0:T(8,128)(2,1)}, bf16[1536,1536]{1,0:T(8,128)(2,1)},...) conditional(s32[]{:T(128)} %convert_element_type.48, () %tuple.132, (bf16[256,1536]{1,0:T(8,128)(2,1)S(1)}, ...), branch_computations={%region_10.11_spmd, %region_11.12_spmd} | conditional | flops 2 | bytes 11927612 | solution.py:939
  215.2 17.8 %feed_forward.5 = (bf16[1280,1024]{1,0:T(8,128)(2,1)}, bf16[1280,512]{1,0:T(8,128)(2,1)}, bf16[256,1536]{1,0:T(8,128)(2,1)}, bf16[1024,1536]{1,0:T(8,128)(2,1)}) custom-call(bf16[256,1536]{1,0:T(8,128)(2,1)S(1)} %get-tuple-element.418.refs_0_.refs_3_, bf16[256,1536]{1,0:T(8,128)(2,1)} %get-tuple-element.419.refs_1_.refs_4_, ...), custom_call_target="tpu_custom_call" | custom-call | flops 1 | bytes 1 | tf_op jit(solution)/shard_map/cond/branch_1_fun/feed_forward/pallas_call | solution.py:427
  233.0 15.0 %weight_grads.3 = bf16[1536,1536]{1,0:T(8,128)(2,1)} custom-call(bf16[256,1536]{1,0:T(8,128)(2,1)} %get-tuple-element.432.refs_0_, bf16[256,1536]{1,0:T(8,128)(2,1)} %get-tuple-element.433.refs_1_, bf16[256,1536]{1,0:T(8,128)(2,1)} %get-tuple-element.434.refs_2_, bf16[256,1536]{1,0:T(8,128)(2,1)S(1)} %get-tuple-element.418.refs_0_.refs_3_, ...), custom_call_target="tpu_custom_call" | custom-call | flops 1 | bytes 1 | tf_op jit(solution)/shard_map/cond/branch_1_fun/weight_grads/pallas_call | solution.py:527
  249.2 21.3 %conditional.19 = (bf16[160,1536]{1,0:T(8,128)(2,1)}, bf16[160,1536]{1,0:T(8,128)(2,1)}, bf16[1280,768]{1,0:T(8,128)(2,1)}, bf16[1280,384]{1,0:T(8,128)(2,1)}, b...) conditional(s32[]{:T(128)} %convert_element_type.48, () %tuple.131, (bf16[320,1536]{1,0:T(8,128)(2,1)}, ...), branch_computations={%region_13.14_spmd, %region_14.15_spmd} | conditional | flops 1 | bytes 9044125 | solution.py:939
  251.8 1.8 slice.80
  255.2 15.3 %feed_forward.6 = (bf16[1280,768]{1,0:T(8,128)(2,1)}, bf16[1280,384]{1,0:T(8,128)(2,1)}, bf16[256,1536]{1,0:T(8,128)(2,1)}, bf16[1024,1536]{1,0:T(8,128)(2,1)S(1)}) custom-call(bf16[256,1536]{1,0:T(8,128)(2,1)S(1)} %get-tuple-element.444.refs_0_, bf16[256,1536]{1,0:T(8,128)(2,1)} %get-tuple-element.445.refs_1_, ...), custom_call_target="tpu_custom_call" | custom-call | flops 1 | bytes 1 | tf_op jit(solution)/shard_map/cond/branch_1_fun/feed_forward/pallas_call | solution.py:427
  270.5 10.2 %feed_forward.7 = (bf16[768,768]{1,0:T(8,128)(2,1)}, bf16[768,384]{1,0:T(8,128)(2,1)S(1)}, bf16[768,1536]{1,0:T(8,128)(2,1)}) custom-call(bf16[256,1536]{1,0:T(8,128)(2,1)} %get-tuple-element.739.refs_0_, bf16[256,1536]{1,0:T(8,128)(2,1)} %get-tuple-element.740.refs_1_, bf16[256,1536]{1,0:T(8,128)(2,1)} %get-tuple-element.741.refs_2_, ...), custom_call_target="tpu_custom_call" | custom-call | flops 1 | bytes 1 | tf_op jit(solution)/shard_map/feed_forward/pallas_call | solution.py:427
  280.8 6.2 %core_sum.3 = (f32[256,1536]{1,0:T(8,128)}, bf16[256,1536]{1,0:T(8,128)(2,1)}, bf16[256,1536]{1,0:T(8,128)(2,1)}, bf16[256,1536]{1,0:T(8,128)(2,1)}) custom-call(bf16[768,1536]{1,0:T(8,128)(2,1)} %get-tuple-element.765.three_ref, bf16[256,1536]{1,0:T(8,128)(2,1)} %get-tuple-element.766.one_ref, bf16[1024,1536]{1,0:T(8,128)(2,1)} %collective-permute-done.61.far_ref), custom_call_target="tpu_custom_call" | custom-call | flops 1 | bytes 1 | tf_op jit(solution)/shard_map/core_sum/pallas_call | solution.py:720
  287.0 38.3 %conditional.20 = (bf16[256,1536]{1,0:T(8,128)(2,1)}, bf16[256,1536]{1,0:T(8,128)(2,1)}, bf16[256,1536]{1,0:T(8,128)(2,1)}, bf16[1536,1152]{1,0:T(8,128)(2,1)}, ...) conditional(s32[]{:T(128)} %convert_element_type.48, () %tuple.135, ...), branch_computations={%region_15.16_spmd, %region_16.17_spmd} | conditional | flops 2 | bytes 25166140 | solution.py:939
  288.3 2.2 collective-permute-start.18
  290.6 13.2 %project_back.1 = (bf16[768,1536]{1,0:T(8,128)(2,1)}, bf16[256,1536]{1,0:T(8,128)(2,1)}, bf16[1024,1536]{1,0:T(8,128)(2,1)}) custom-call(bf16[768,512]{1,0:T(8,128)(2,1)} %get-tuple-element.484.refs_0_, bf16[1280,512]{1,0:T(8,128)(2,1)} %get-tuple-element.485.refs_1_, bf16[768,384]{1,0:T(8,128)(2,1)S(1)} %get-tuple-element.482.refs_18_.refs_2_, ...), custom_call_target="tpu_custom_call" | custom-call | flops 1 | bytes 1 | tf_op jit(solution)/shard_map/cond/branch_1_fun/project_back/pallas_call | solution.py:561
  303.8 13.5 %weight_grads.4 = bf16[1536,1152]{1,0:T(8,128)(2,1)} custom-call(bf16[256,1536]{1,0:T(8,128)(2,1)} %get-tuple-element.464.refs_0_, bf16[256,1536]{1,0:T(8,128)(2,1)} %get-tuple-element.465.refs_1_, bf16[256,1536]{1,0:T(8,128)(2,1)} %get-tuple-element.466.refs_2_, bf16[256,1536]{1,0:T(8,128)(2,1)S(1)} %copy-done.23, ...), custom_call_target="tpu_custom_call" | custom-call | flops 1 | bytes 1 | tf_op jit(solution)/shard_map/cond/branch_1_fun/weight_grads/pallas_call | solution.py:527
  317.2 8.1 %collective-permute-done.18 = bf16[256,1536]{1,0:T(8,128)(2,1)} collective-permute-done((bf16[256,1536]{1,0:T(8,128)(2,1)}, bf16[256,1536]{1,0:T(8,128)(2,1)}, u32[]{:S(2)}, u32[]{:S(2)}) %collective-permute-start.18) | collective-permute-done | bytes 786464 | tf_op jit(solution)/shard_map/cond/branch_1_fun/ppermute | solution.py:902
  327.1 6.9 %middle_back.1 = (f32[256,1536]{1,0:T(8,128)}, bf16[256,1536]{1,0:T(8,128)(2,1)S(1)}, bf16[2,256,192]{2,1,0:T(8,128)(2,1)S(1)}, bf16[2,256,192]{2,1,0:T(8,128)(2...) custom-call(f32[256,1536]{1,0:T(8,128)S(1)} %copy-done.6, ...), custom_call_target="tpu_custom_call" | custom-call | flops 1 | bytes 1 | tf_op jit(solution)/shard_map/middle_back/pallas_call | solution.py:661
  335.2 2.2 collective-permute-start.64
  337.5 10.2 %collective-permute-done.62 = bf16[512,192]{1,0:T(8,128)(2,1)S(1)} collective-permute-done((bf16[512,192]{1,0:T(8,128)(2,1)S(1)}, bf16[512,192]{1,0:T(8,128)(2,1)S(1)}, u32[]{:S(2)}, u32[]{:S(2)}) %collective-permute-start.62) | collective-permute-done | bytes 196640 | tf_op jit(solution)/shard_map/ppermute | solution.py:876
  348.0 1.9 collective-permute-done.65
  350.0 37.9 %conditional.21 = (bf16[256,1536]{1,0:T(8,128)(2,1)}, bf16[256,1536]{1,0:T(8,128)(2,1)}, bf16[256,1536]{1,0:T(8,128)(2,1)}, bf16[256,1536]{1,0:T(8,128)(2,1)}, b...) conditional(s32[]{:T(128)} %convert_element_type.48, () %tuple.120, ...), branch_computations={%region_18.19_spmd, %region_19.20_spmd} | conditional | flops 1 | bytes 12583145 | solution.py:939
  353.8 26.7 %attend_backward.1 = (bf16[2,1,256,320]{3,2,1,0:T(8,128)(2,1)}, bf16[2,1,256,320]{3,2,1,0:T(8,128)(2,1)}, bf16[2,1,256,320]{3,2,1,0:T(8,128)(2,1)}, bf16[2,1,256,320]{3,2,1,0:T(8,128)(2,1)}, f32[2,8,256]{2,1,0:T(8,128)S(1)}) custom-call(s32[1]{0:T(128)} %get-tuple-element.492.place_ref, bf16[8,1,256,320]{3,2,1,0:T(8,128)(2,1)} %get-tuple-element.493.refs_0_, ...), custom_call_target="tpu_custom_call" | custom-call | flops 1 | bytes 1 | tf_op jit(solution)/shard_map/cond/branch_1_fun/attend_backward/pallas_call | solution.py:222
  380.5 6.8 %collective-permute-done.20 = bf16[256,1536]{1,0:T(8,128)(2,1)} collective-permute-done((bf16[256,1536]{1,0:T(8,128)(2,1)S(1)}, bf16[256,1536]{1,0:T(8,128)(2,1)}, u32[]{:S(2)}, u32[]{:S(2)}) %collective-permute-start.20) | collective-permute-done | bytes 786464 | tf_op jit(solution)/shard_map/cond/branch_1_fun/ppermute | solution.py:876
  388.5 2.1 collective-permute-done.66
  392.8 24.2 %conditional.22 = (bf16[512,320]{1,0:T(8,128)(2,1)}, bf16[512,320]{1,0:T(8,128)(2,1)}, bf16[512,320]{1,0:T(8,128)(2,1)}, bf16[1536,640]{1,0:T(8,128)(2,1)S(1)}, ...) conditional(s32[]{:T(128)} %convert_element_type.48, () %tuple.119, ...), branch_computations={%region_20.21_spmd, %region_21.22_spmd} | conditional | flops 10 | bytes 9468336 | solution.py:939
  397.2 5.3 %core_sum.2 = (f32[256,1536]{1,0:T(8,128)S(1)}, bf16[256,1536]{1,0:T(8,128)(2,1)}, bf16[256,1536]{1,0:T(8,128)(2,1)}, bf16[256,1536]{1,0:T(8,128)(2,1)}) custom-call(bf16[768,1536]{1,0:T(8,128)(2,1)} %get-tuple-element.528.three_ref, bf16[256,1536]{1,0:T(8,128)(2,1)} %get-tuple-element.529.one_ref, bf16[1024,1536]{1,0:T(8,128)(2,1)} %get-tuple-element.530.far_ref), custom_call_target="tpu_custom_call" | custom-call | flops 1 | bytes 1 | tf_op jit(solution)/shard_map/cond/branch_1_fun/core_sum/pallas_call | solution.py:720
  404.0 11.1 %weight_grads.5 = bf16[1536,640]{1,0:T(8,128)(2,1)S(1)} custom-call(bf16[2048,1536]{1,0:T(8,128)(2,1)} %get-tuple-element.511.refs_0_, bf16[512,320]{1,0:T(8,128)(2,1)} %bitcast.23.refs_1_, bf16[512,320]{1,0:T(8,128)(2,1)} %bitcast.17.refs_2_, bf16[512,320]{1,0:T(8,128)(2,1)} %bitcast.19.refs_3_, bf16[512,320]{1,0:T(8,128)(2,1)} %bitcast.21.refs_4_, ...), custom_call_target="tpu_custom_call" | custom-call | flops 1 | bytes 1 | tf_op jit(solution)/shard_map/cond/branch_1_fun/weight_grads/pallas_call | solution.py:527
  415.1 1.9 constant_dynamic-slice_fusion
  421.5 27.1 %conditional.23 = (bf16[128,1536]{1,0:T(8,128)(2,1)}, bf16[128,1536]{1,0:T(8,128)(2,1)S(1)}, bf16[192,1536]{1,0:T(8,128)(2,1)}, bf16[1024,320]{0,1:T(8,128)(2,1)...) conditional(s32[]{:T(128)} %convert_element_type.48, () %tuple.139, ...), branch_computations={%region_22.23_spmd, %region_23.24_spmd} | conditional | flops 2621440 | bytes 33817016 | solution.py:939
  426.2 6.9 %collective-permute-done.51 = bf16[128,1536]{1,0:T(8,128)(2,1)S(1)} collective-permute-done((bf16[128,1536]{1,0:T(8,128)(2,1)S(1)}, bf16[128,1536]{1,0:T(8,128)(2,1)S(1)}, u32[]{:S(2)}, u32[]{:S(2)}) %collective-permute-start.51) | collective-permute-done | bytes 393248 | tf_op jit(solution)/shard_map/cond/branch_1_fun/ppermute | solution.py:876
  433.1 2.7 collective-permute-done.50
  443.0 3.4 collective-permute-done.52
  446.4 2.2 collective-permute-done.53
  448.7 2.8 corner_sum.1
  451.5 29.4 %conditional.24 = (bf16[256,1536]{1,0:T(8,128)(2,1)}, bf16[256,1536]{1,0:T(8,128)(2,1)}, bf16[192,1152]{1,0:T(8,128)(2,1)}, f32[1,256,1536]{2,1,0:T(8,128)}) conditional(s32[]{:T(128)} %convert_element_type.48, () %tuple.141, (bf16[256,1536]{1,0:T(8,128)(2,1)}, bf16[256,1536]{1,0:T(8,128)(2,1)}, bf16[384,1152]{1,0:T(8,128)(2,1)}, ...), branch_computations={%region_24.25_spmd, %region_25.26_spmd} | conditional | flops 9 | bytes 10453267 | solution.py:939
  458.0 8.9 %input_back.1 = f32[256,1536]{1,0:T(8,128)} custom-call(bf16[512,320]{1,0:T(8,128)(2,1)} %get-tuple-element.549.refs_0_, bf16[512,320]{1,0:T(8,128)(2,1)} %get-tuple-element.550.refs_1_, bf16[512,320]{1,0:T(8,128)(2,1)} %get-tuple-element.551.refs_2_, bf16[512,320]{1,0:T(8,128)(2,1)} %get-tuple-element.552.refs_3_, ...), custom_call_target="tpu_custom_call" | custom-call | flops 1 | bytes 1 | tf_op jit(solution)/shard_map/cond/branch_1_fun/input_back/pallas_call | solution.py:692
  466.9 14.0 %collective-permute-done.48 = bf16[192,1152]{1,0:T(8,128)(2,1)} collective-permute-done((bf16[192,1152]{1,0:T(8,128)(2,1)}, bf16[192,1152]{1,0:T(8,128)(2,1)}, u32[]{:S(2)}, u32[]{:S(2)}) %collective-permute-start.48) | collective-permute-done | bytes 442400 | tf_op jit(solution)/shard_map/cond/branch_1_fun/ppermute | solution.py:876
  480.9 8.4 %conditional.25 = (bf16[192,640]{1,0:T(8,128)(2,1)}, f32[192,1728]{1,0:T(8,128)}, f32[192,1728]{1,0:T(8,128)}, f32[192,1728]{1,0:T(8,128)}, bf16[1,256,1536]{2,1,0:T(8,128)(2,1)S(1)}) conditional(s32[]{:T(128)} %convert_element_type.48, () %tuple.118, (bf16[384,640]{1,0:T(8,128)(2,1)}, s32[1]{0:T(128)}, bf16[384,1536]{1,0:T(8,128)(2,1)}, ...), branch_computations={%region_27.28_spmd, %region_28.29_spmd} | conditional | flops 2359304 | bytes 15237350 | solution.py:939
  483.2 2.4 fusion
  485.7 3.6 unpack_columns.2
  489.3 2.4 unpack_columns.3
  495.1 1.8 collective-permute-done.71
  (345 shorter events, 111.0 us)
Async XLA Ops:
  7.2 84.6 %all-gather.4.cloned.1.call-start = ((), (), s32[]{:S(2)}) async-start(), calls=%async_computation.6 | async-start | bytes 2457600 | tf_op jit(solution)/shard_map/all_gather | solution.py:926
  12.3 27.5 %collective-permute-start.1 = (bf16[256,1536]{1,0:T(8,128)(2,1)}, bf16[256,1536]{1,0:T(8,128)(2,1)}, u32[]{:S(2)}, u32[]{:S(2)}) collective-permute-start(bf16[256,1536]{1,0:T(8,128)(2,1)} %get-tuple-element.364), channel_id=1, source_target_pairs={{0,4},{4,0},{1,5},{5,1},{2,6},{6,2},{3,7},{7,3},{8,12},{12,8},{9,1... | collective-permute-start | bytes 2359304 | tf_op jit(solution)/shard_map/cond/branch_1_fun/ppermute | solution.py:876
  15.3 24.5 %collective-permute-start = (bf16[256,1536]{1,0:T(8,128)(2,1)}, bf16[256,1536]{1,0:T(8,128)(2,1)}, u32[]{:S(2)}, u32[]{:S(2)}) collective-permute-start(bf16[256,1536]{1,0:T(8,128)(2,1)} %get-tuple-element.364), channel_id=1, source_target_pairs={{0,2},{2,0},{1,3},{3,1},{4,6},{6,4},{5,7},{7,5},{8,10},{10,8},{9,1... | collective-permute-start | bytes 2359304 | tf_op jit(solution)/shard_map/cond/branch_1_fun/ppermute | solution.py:876
  40.6 140.9 %all-gather.8.cloned.1.call-start = ((), (), s32[]{:S(2)}) async-start(), calls=%async_computation.8 | async-start | bytes 5898240 | tf_op jit(solution)/shard_map/all_gather | solution.py:926
  60.0 28.6 %all-to-all-start.1 = ((bf16[8,48,1536]{2,1,0:T(8,128)(2,1)}), bf16[8,48,1536]{2,1,0:T(8,128)(2,1)}, u32[]{:S(2)}, u32[]{:S(2)}) async-start(bf16[8,48,1536]{2,1,0:T(8,128)(2,1)} %get-tuple-element.368), calls=%async_computation.1 | async-start | bytes 2359296 | tf_op jit(solution)/shard_map/cond/branch_1_fun/all_to_all | solution.py:943
  64.3 24.3 %collective-permute-start.25 = (bf16[256,1536]{1,0:T(8,128)(2,1)S(1)}, bf16[256,1536]{1,0:T(8,128)(2,1)}, u32[]{:S(2)}, u32[]{:S(2)}) collective-permute-start(bf16[256,1536]{1,0:T(8,128)(2,1)S(1)} %get-tuple-element.367), channel_id=1, source_target_pairs={{0,1},{1,0},{2,3},{3,2},{4,5},{5,4},{6,7},{7,6},{8,9},{9,8},{10,11... | collective-permute-start | bytes 2359304 | tf_op jit(solution)/shard_map/cond/branch_1_fun/ppermute | solution.py:876
  64.7 23.9 %collective-permute-start.26 = (bf16[256,1536]{1,0:T(8,128)(2,1)}, bf16[256,1536]{1,0:T(8,128)(2,1)}, u32[]{:S(2)}, u32[]{:S(2)}) collective-permute-start(bf16[256,1536]{1,0:T(8,128)(2,1)} %get-tuple-element.365), channel_id=1, source_target_pairs={{0,1},{1,0},{2,3},{3,2},{4,5},{5,4},{6,7},{7,6},{8,9},{9,8},{10,11... | collective-permute-start | bytes 2359304 | tf_op jit(solution)/shard_map/cond/branch_1_fun/ppermute | solution.py:876
  64.9 23.7 %collective-permute-start.27 = (bf16[256,1536]{1,0:T(8,128)(2,1)}, bf16[256,1536]{1,0:T(8,128)(2,1)}, u32[]{:S(2)}, u32[]{:S(2)}) collective-permute-start(bf16[256,1536]{1,0:T(8,128)(2,1)} %get-tuple-element.366), channel_id=1, source_target_pairs={{0,1},{1,0},{2,3},{3,2},{4,5},{5,4},{6,7},{7,6},{8,9},{9,8},{10,11... | collective-permute-start | bytes 2359304 | tf_op jit(solution)/shard_map/cond/branch_1_fun/ppermute | solution.py:876
  66.2 22.4 %collective-permute-start.24 = (bf16[128,1536]{1,0:T(8,128)(2,1)S(1)}, bf16[128,1536]{1,0:T(8,128)(2,1)}, u32[]{:S(2)}, u32[]{:S(2)}) collective-permute-start(bf16[128,1536]{1,0:T(8,128)(2,1)S(1)} %slice.70), channel_id=1, source_target_pairs={{0,2},{2,0},{1,3},{3,1},{4,6},{6,4},{5,7},{7,5},{8,10},{10,8},{9,1... | collective-permute-start | bytes 1179656 | tf_op jit(solution)/shard_map/cond/branch_1_fun/ppermute | solution.py:876
  69.0 19.6 %collective-permute-start.23 = (bf16[128,1536]{1,0:T(8,128)(2,1)S(1)}, bf16[128,1536]{1,0:T(8,128)(2,1)}, u32[]{:S(2)}, u32[]{:S(2)}) collective-permute-start(bf16[128,1536]{1,0:T(8,128)(2,1)S(1)} %slice.69), channel_id=1, source_target_pairs={{0,4},{4,0},{1,5},{5,1},{2,6},{6,2},{3,7},{7,3},{8,12},{12,8},{9,1... | collective-permute-start | bytes 1179656 | tf_op jit(solution)/shard_map/cond/branch_1_fun/ppermute | solution.py:876
  88.7 160.5 %all-gather.6.cloned.1.call-start = ((), (), s32[]{:S(2)}) async-start(), calls=%async_computation.7 | async-start | bytes 4423680 | tf_op jit(solution)/shard_map/all_gather | solution.py:926
  89.6 303.3 %reduce-scatter.4.cloned.1.call-start = ((), (), s32[]{:S(2)}) async-start(), calls=%async_computation.9 | async-start | bytes 5898240 | tf_op jit(solution)/shard_map/reduce_scatter | solution.py:930
  96.1 28.8 %collective-permute-start.5 = (bf16[192,1536]{1,0:T(8,128)(2,1)S(1)}, bf16[192,1536]{1,0:T(8,128)(2,1)}, u32[]{:S(2)}, u32[]{:S(2)}) collective-permute-start(bf16[192,1536]{1,0:T(8,128)(2,1)S(1)} %get-tuple-element.372), channel_id=1, source_target_pairs={{0,1},{1,0},{2,3},{3,2},{4,5},{5,4},{6,7},{7,6},{8,9},{9,8},{10,11... | collective-permute-start | bytes 1769480 | tf_op jit(solution)/shard_map/cond/branch_1_fun/ppermute | solution.py:876
  96.5 28.5 %collective-permute-start.4 = (bf16[192,1536]{1,0:T(8,128)(2,1)S(1)}, bf16[192,1536]{1,0:T(8,128)(2,1)}, u32[]{:S(2)}, u32[]{:S(2)}) collective-permute-start(bf16[192,1536]{1,0:T(8,128)(2,1)S(1)} %get-tuple-element.372), channel_id=1, source_target_pairs={{0,6},{2,4},{4,2},{6,0},{1,7},{3,5},{5,3},{7,1},{8,14},{10,12},{12... | collective-permute-start | bytes 1769480 | tf_op jit(solution)/shard_map/cond/branch_1_fun/ppermute | solution.py:902
  98.0 27.6 %collective-permute-start.3 = (bf16[192,1536]{1,0:T(8,128)(2,1)S(1)}, bf16[192,1536]{1,0:T(8,128)(2,1)}, u32[]{:S(2)}, u32[]{:S(2)}) collective-permute-start(bf16[192,1536]{1,0:T(8,128)(2,1)S(1)} %get-tuple-element.372), channel_id=1, source_target_pairs={{0,4},{4,0},{1,5},{5,1},{2,6},{6,2},{3,7},{7,3},{8,12},{12,8},{9,1... | collective-permute-start | bytes 1769480 | tf_op jit(solution)/shard_map/cond/branch_1_fun/ppermute | solution.py:876
  99.5 26.1 %collective-permute-start.2 = (bf16[192,1536]{1,0:T(8,128)(2,1)S(1)}, bf16[192,1536]{1,0:T(8,128)(2,1)}, u32[]{:S(2)}, u32[]{:S(2)}) collective-permute-start(bf16[192,1536]{1,0:T(8,128)(2,1)S(1)} %get-tuple-element.372), channel_id=1, source_target_pairs={{0,2},{2,0},{1,3},{3,1},{4,6},{6,4},{5,7},{7,5},{8,10},{10,8},{9,1... | collective-permute-start | bytes 1769480 | tf_op jit(solution)/shard_map/cond/branch_1_fun/ppermute | solution.py:876
  126.5 10.1 %collective-permute-start.30 = (bf16[512,192]{1,0:T(8,128)(2,1)S(1)}, bf16[512,192]{1,0:T(8,128)(2,1)S(1)}, u32[]{:S(2)}, u32[]{:S(2)}) collective-permute-start(bf16[512,192]{1,0:T(8,128)(2,1)S(1)} %bitcast.82), channel_id=1, source_target_pairs={{0,6},{2,4},{4,2},{6,0},{1,7},{3,5},{5,3},{7,1},{8,14},{10,12},{12... | collective-permute-start | bytes 589832 | tf_op jit(solution)/shard_map/cond/branch_1_fun/ppermute | solution.py:902
  127.9 13.3 %collective-permute-start.29 = (bf16[512,192]{1,0:T(8,128)(2,1)S(1)}, bf16[512,192]{1,0:T(8,128)(2,1)S(1)}, u32[]{:S(2)}, u32[]{:S(2)}) collective-permute-start(bf16[512,192]{1,0:T(8,128)(2,1)S(1)} %bitcast.84), channel_id=1, source_target_pairs={{0,4},{4,0},{1,5},{5,1},{2,6},{6,2},{3,7},{7,3},{8,12},{12,8},{9,1... | collective-permute-start | bytes 589832 | tf_op jit(solution)/shard_map/cond/branch_1_fun/ppermute | solution.py:876
  129.3 11.9 %collective-permute-start.28 = (bf16[512,192]{1,0:T(8,128)(2,1)S(1)}, bf16[512,192]{1,0:T(8,128)(2,1)S(1)}, u32[]{:S(2)}, u32[]{:S(2)}) collective-permute-start(bf16[512,192]{1,0:T(8,128)(2,1)S(1)} %bitcast.86), channel_id=1, source_target_pairs={{0,2},{2,0},{1,3},{3,1},{4,6},{6,4},{5,7},{7,5},{8,10},{10,8},{9,1... | collective-permute-start | bytes 589832 | tf_op jit(solution)/shard_map/cond/branch_1_fun/ppermute | solution.py:876
  130.0 15.8 %collective-permute-start.34 = (bf16[192,1536]{1,0:T(8,128)(2,1)}, bf16[192,1536]{1,0:T(8,128)(2,1)}, u32[]{:S(2)}, u32[]{:S(2)}) collective-permute-start(bf16[192,1536]{1,0:T(8,128)(2,1)} %get-tuple-element.401.refs_11_), channel_id=1, source_target_pairs={{0,1},{1,0},{2,3},{3,2},{4,5},{5,4},{6,7},{7,6},{8,9},{9,8},{10,11... | collective-permute-start | bytes 1769480 | tf_op jit(solution)/shard_map/cond/branch_1_fun/ppermute | solution.py:876
  142.2 16.6 %collective-permute-start.40 = (bf16[256,1536]{1,0:T(8,128)(2,1)S(1)}, bf16[256,1536]{1,0:T(8,128)(2,1)}, u32[]{:S(2)}, u32[]{:S(2)}) collective-permute-start(bf16[256,1536]{1,0:T(8,128)(2,1)S(1)} %get-tuple-element.407), channel_id=1, source_target_pairs={{0,1},{1,0},{2,3},{3,2},{4,5},{5,4},{6,7},{7,6},{8,9},{9,8},{10,11... | collective-permute-start | bytes 2359304 | tf_op jit(solution)/shard_map/cond/branch_1_fun/ppermute | solution.py:876
  143.6 20.8 %collective-permute-start.39 = (bf16[256,1536]{1,0:T(8,128)(2,1)}, bf16[256,1536]{1,0:T(8,128)(2,1)}, u32[]{:S(2)}, u32[]{:S(2)}) collective-permute-start(bf16[256,1536]{1,0:T(8,128)(2,1)} %after.5), channel_id=1, source_target_pairs={{0,4},{4,0},{1,5},{5,1},{2,6},{6,2},{3,7},{7,3},{8,12},{12,8},{9,1... | collective-permute-start | bytes 2359304 | tf_op jit(solution)/shard_map/cond/branch_1_fun/ppermute | solution.py:876
  145.0 20.7 %collective-permute-start.38 = (bf16[256,1536]{1,0:T(8,128)(2,1)}, bf16[256,1536]{1,0:T(8,128)(2,1)}, u32[]{:S(2)}, u32[]{:S(2)}) collective-permute-start(bf16[256,1536]{1,0:T(8,128)(2,1)} %after.5), channel_id=1, source_target_pairs={{0,2},{2,0},{1,3},{3,1},{4,6},{6,4},{5,7},{7,5},{8,10},{10,8},{9,1... | collective-permute-start | bytes 2359304 | tf_op jit(solution)/shard_map/cond/branch_1_fun/ppermute | solution.py:876
  157.4 22.9 %collective-permute-start.36 = (bf16[256,1536]{1,0:T(8,128)(2,1)}, bf16[256,1536]{1,0:T(8,128)(2,1)}, u32[]{:S(2)}, u32[]{:S(2)}) collective-permute-start(bf16[256,1536]{1,0:T(8,128)(2,1)} %get-tuple-element.1119), channel_id=1, source_target_pairs={{0,4},{4,0},{1,5},{5,1},{2,6},{6,2},{3,7},{7,3},{8,12},{12,8},{9,1... | collective-permute-start | bytes 2359304 | tf_op jit(solution)/shard_map/cond/branch_1_fun/ppermute | solution.py:876
  158.8 22.7 %collective-permute-start.35 = (bf16[256,1536]{1,0:T(8,128)(2,1)}, bf16[256,1536]{1,0:T(8,128)(2,1)}, u32[]{:S(2)}, u32[]{:S(2)}) collective-permute-start(bf16[256,1536]{1,0:T(8,128)(2,1)} %get-tuple-element.1119), channel_id=1, source_target_pairs={{0,2},{2,0},{1,3},{3,1},{4,6},{6,4},{5,7},{7,5},{8,10},{10,8},{9,1... | collective-permute-start | bytes 2359304 | tf_op jit(solution)/shard_map/cond/branch_1_fun/ppermute | solution.py:876
  164.4 17.1 %collective-permute-start.42 = (bf16[256,1536]{1,0:T(8,128)(2,1)}, bf16[256,1536]{1,0:T(8,128)(2,1)}, u32[]{:S(2)}, u32[]{:S(2)}) collective-permute-start(bf16[256,1536]{1,0:T(8,128)(2,1)} %collective-permute-done.39), channel_id=1, source_target_pairs={{0,1},{1,0},{2,3},{3,2},{4,5},{5,4},{6,7},{7,6},{8,9},{9,8},{10,11... | collective-permute-start | bytes 2359304 | tf_op jit(solution)/shard_map/cond/branch_1_fun/ppermute | solution.py:876
  165.8 15.7 %collective-permute-start.41 = (bf16[256,1536]{1,0:T(8,128)(2,1)}, bf16[256,1536]{1,0:T(8,128)(2,1)}, u32[]{:S(2)}, u32[]{:S(2)}) collective-permute-start(bf16[256,1536]{1,0:T(8,128)(2,1)} %collective-permute-done.38), channel_id=1, source_target_pairs={{0,1},{1,0},{2,3},{3,2},{4,5},{5,4},{6,7},{7,6},{8,9},{9,8},{10,11... | collective-permute-start | bytes 2359304 | tf_op jit(solution)/shard_map/cond/branch_1_fun/ppermute | solution.py:876
  182.5 10.2 %collective-permute-start.7 = (bf16[128,1536]{1,0:T(8,128)(2,1)S(1)}, bf16[128,1536]{1,0:T(8,128)(2,1)}, u32[]{:S(2)}, u32[]{:S(2)}) collective-permute-start(bf16[128,1536]{1,0:T(8,128)(2,1)S(1)} %slice.77), channel_id=1, source_target_pairs={{0,2},{2,0},{1,3},{3,1},{4,6},{6,4},{5,7},{7,5},{8,10},{10,8},{9,1... | collective-permute-start | bytes 1179656 | tf_op jit(solution)/shard_map/cond/branch_1_fun/ppermute | solution.py:876
  183.2 22.1 %collective-permute-start.10 = (bf16[256,1536]{1,0:T(8,128)(2,1)}, bf16[256,1536]{1,0:T(8,128)(2,1)}, u32[]{:S(2)}, u32[]{:S(2)}) collective-permute-start(bf16[256,1536]{1,0:T(8,128)(2,1)} %get-tuple-element.408.refs_1_), channel_id=1, source_target_pairs={{0,1},{1,0},{2,3},{3,2},{4,5},{5,4},{6,7},{7,6},{8,9},{9,8},{10,11... | collective-permute-start | bytes 2359304 | tf_op jit(solution)/shard_map/cond/branch_1_fun/ppermute | solution.py:876
  183.2 22.1 %collective-permute-start.11 = (bf16[256,1536]{1,0:T(8,128)(2,1)}, bf16[256,1536]{1,0:T(8,128)(2,1)}, u32[]{:S(2)}, u32[]{:S(2)}) collective-permute-start(bf16[256,1536]{1,0:T(8,128)(2,1)} %get-tuple-element.409.refs_2_), channel_id=1, source_target_pairs={{0,1},{1,0},{2,3},{3,2},{4,5},{5,4},{6,7},{7,6},{8,9},{9,8},{10,11... | collective-permute-start | bytes 2359304 | tf_op jit(solution)/shard_map/cond/branch_1_fun/ppermute | solution.py:876
  184.7 20.5 %collective-permute-start.6 = (bf16[128,1536]{1,0:T(8,128)(2,1)S(1)}, bf16[128,1536]{1,0:T(8,128)(2,1)}, u32[]{:S(2)}, u32[]{:S(2)}) collective-permute-start(bf16[128,1536]{1,0:T(8,128)(2,1)S(1)} %slice.76), channel_id=1, source_target_pairs={{0,4},{4,0},{1,5},{5,1},{2,6},{6,2},{3,7},{7,3},{8,12},{12,8},{9,1... | collective-permute-start | bytes 1179656 | tf_op jit(solution)/shard_map/cond/branch_1_fun/ppermute | solution.py:876
  187.3 17.9 %collective-permute-start.8 = (bf16[128,1536]{1,0:T(8,128)(2,1)S(1)}, bf16[128,1536]{1,0:T(8,128)(2,1)}, u32[]{:S(2)}, u32[]{:S(2)}) collective-permute-start(bf16[128,1536]{1,0:T(8,128)(2,1)S(1)} %slice.78), channel_id=1, source_target_pairs={{0,4},{4,0},{1,5},{5,1},{2,6},{6,2},{3,7},{7,3},{8,12},{12,8},{9,1... | collective-permute-start | bytes 1179656 | tf_op jit(solution)/shard_map/cond/branch_1_fun/ppermute | solution.py:876
  192.7 12.6 %collective-permute-start.9 = (bf16[128,1536]{1,0:T(8,128)(2,1)S(1)}, bf16[128,1536]{1,0:T(8,128)(2,1)}, u32[]{:S(2)}, u32[]{:S(2)}) collective-permute-start(bf16[128,1536]{1,0:T(8,128)(2,1)S(1)} %slice.79), channel_id=1, source_target_pairs={{0,2},{2,0},{1,3},{3,1},{4,6},{6,4},{5,7},{7,5},{8,10},{10,8},{9,1... | collective-permute-start | bytes 1179656 | tf_op jit(solution)/shard_map/cond/branch_1_fun/ppermute | solution.py:876
  213.1 34.9 %collective-permute-start.13 = (bf16[320,1536]{1,0:T(8,128)(2,1)}, bf16[320,1536]{1,0:T(8,128)(2,1)}, u32[]{:S(2)}, u32[]{:S(2)}) collective-permute-start(bf16[320,1536]{1,0:T(8,128)(2,1)} %get-tuple-element.441), channel_id=1, source_target_pairs={{0,4},{4,0},{1,5},{5,1},{2,6},{6,2},{3,7},{7,3},{8,12},{12,8},{9,1... | collective-permute-start | bytes 2949128 | tf_op jit(solution)/shard_map/cond/branch_1_fun/ppermute | solution.py:876
  214.5 33.4 %collective-permute-start.12 = (bf16[320,1536]{1,0:T(8,128)(2,1)}, bf16[320,1536]{1,0:T(8,128)(2,1)}, u32[]{:S(2)}, u32[]{:S(2)}) collective-permute-start(bf16[320,1536]{1,0:T(8,128)(2,1)} %get-tuple-element.441), channel_id=1, source_target_pairs={{0,2},{2,0},{1,3},{3,1},{4,6},{6,4},{5,7},{7,5},{8,10},{10,8},{9,1... | collective-permute-start | bytes 2949128 | tf_op jit(solution)/shard_map/cond/branch_1_fun/ppermute | solution.py:876
  248.0 169.1 %reduce-scatter.6.cloned.1.call-start = ((), (), s32[]{:S(2)}) async-start(), calls=%async_computation.10 | async-start | bytes 4423680 | tf_op jit(solution)/shard_map/reduce_scatter | solution.py:930
  250.3 20.1 %collective-permute-start.15 = (bf16[160,1536]{1,0:T(8,128)(2,1)S(1)}, bf16[160,1536]{1,0:T(8,128)(2,1)}, u32[]{:S(2)}, u32[]{:S(2)}) collective-permute-start(bf16[160,1536]{1,0:T(8,128)(2,1)S(1)} %slice.81), channel_id=1, source_target_pairs={{0,2},{2,0},{1,3},{3,1},{4,6},{6,4},{5,7},{7,5},{8,10},{10,8},{9,1... | collective-permute-start | bytes 1474568 | tf_op jit(solution)/shard_map/cond/branch_1_fun/ppermute | solution.py:876
  253.7 16.8 %collective-permute-start.14 = (bf16[160,1536]{1,0:T(8,128)(2,1)}, bf16[160,1536]{1,0:T(8,128)(2,1)}, u32[]{:S(2)}, u32[]{:S(2)}) collective-permute-start(bf16[160,1536]{1,0:T(8,128)(2,1)} %slice.80), channel_id=1, source_target_pairs={{0,4},{4,0},{1,5},{5,1},{2,6},{6,2},{3,7},{7,3},{8,12},{12,8},{9,1... | collective-permute-start | bytes 1474568 | tf_op jit(solution)/shard_map/cond/branch_1_fun/ppermute | solution.py:876
  270.5 10.3 %collective-permute-start.61 = (bf16[1024,1536]{1,0:T(8,128)(2,1)S(1)}, bf16[1024,1536]{1,0:T(8,128)(2,1)}, u32[]{:S(2)}, u32[]{:S(2)}) collective-permute-start(bf16[1024,1536]{1,0:T(8,128)(2,1)S(1)} %get-tuple-element.764.refs_8_), channel_id=1, source_target_pairs={{0,1},{1,0},{2,3},{3,2},{4,5},{5,4},{6,7},{7,6},{8,9},{9,8},{10,11... | collective-permute-start | bytes 9437192 | tf_op jit(solution)/shard_map/ppermute | solution.py:876
  287.0 30.2 %collective-permute-start.16 = (bf16[256,1536]{1,0:T(8,128)(2,1)}, bf16[256,1536]{1,0:T(8,128)(2,1)}, u32[]{:S(2)}, u32[]{:S(2)}) collective-permute-start(bf16[256,1536]{1,0:T(8,128)(2,1)} %get-tuple-element.461), channel_id=1, source_target_pairs={{0,2},{2,0},{1,3},{3,1},{4,6},{6,4},{5,7},{7,5},{8,10},{10,8},{9,1... | collective-permute-start | bytes 2359304 | tf_op jit(solution)/shard_map/cond/branch_1_fun/ppermute | solution.py:876
  287.9 29.3 %collective-permute-start.17 = (bf16[256,1536]{1,0:T(8,128)(2,1)}, bf16[256,1536]{1,0:T(8,128)(2,1)}, u32[]{:S(2)}, u32[]{:S(2)}) collective-permute-start(bf16[256,1536]{1,0:T(8,128)(2,1)} %get-tuple-element.462), channel_id=1, source_target_pairs={{0,4},{4,0},{1,5},{5,1},{2,6},{6,2},{3,7},{7,3},{8,12},{12,8},{9,1... | collective-permute-start | bytes 2359304 | tf_op jit(solution)/shard_map/cond/branch_1_fun/ppermute | solution.py:876
  288.3 37.0 %collective-permute-start.18 = (bf16[256,1536]{1,0:T(8,128)(2,1)}, bf16[256,1536]{1,0:T(8,128)(2,1)}, u32[]{:S(2)}, u32[]{:S(2)}) collective-permute-start(bf16[256,1536]{1,0:T(8,128)(2,1)} %get-tuple-element.463), channel_id=1, source_target_pairs={{0,6},{2,4},{4,2},{6,0},{1,7},{3,5},{5,3},{7,1},{8,14},{10,12},{12... | collective-permute-start | bytes 2359304 | tf_op jit(solution)/shard_map/cond/branch_1_fun/ppermute | solution.py:902
  325.4 155.5 %reduce-scatter.8.cloned.1.call-start = ((), (), s32[]{:S(2)}) async-start(), calls=%async_computation.11 | async-start | bytes 2457600 | tf_op jit(solution)/shard_map/reduce_scatter | solution.py:930
  325.4 67.4 %collective-permute-start.69 = (bf16[1024,1536]{1,0:T(8,128)(2,1)}, bf16[1024,1536]{1,0:T(8,128)(2,1)}, u32[]{:S(2)}, u32[]{:S(2)}) collective-permute-start(bf16[1024,1536]{1,0:T(8,128)(2,1)} %get-tuple-element.803), channel_id=1, source_target_pairs={{0,1},{1,0},{2,3},{3,2},{4,5},{5,4},{6,7},{7,6},{8,9},{9,8},{10,11... | collective-permute-start | bytes 9437192 | tf_op jit(solution)/shard_map/ppermute | solution.py:876
  334.0 13.8 %collective-permute-start.63 = (bf16[512,192]{1,0:T(8,128)(2,1)S(1)}, bf16[512,192]{1,0:T(8,128)(2,1)S(1)}, u32[]{:S(2)}, u32[]{:S(2)}) collective-permute-start(bf16[512,192]{1,0:T(8,128)(2,1)S(1)} %bitcast.65), channel_id=1, source_target_pairs={{0,4},{4,0},{1,5},{5,1},{2,6},{6,2},{3,7},{7,3},{8,12},{12,8},{9,1... | collective-permute-start | bytes 589832 | tf_op jit(solution)/shard_map/ppermute | solution.py:876
  334.8 12.9 %collective-permute-start.62 = (bf16[512,192]{1,0:T(8,128)(2,1)S(1)}, bf16[512,192]{1,0:T(8,128)(2,1)S(1)}, u32[]{:S(2)}, u32[]{:S(2)}) collective-permute-start(bf16[512,192]{1,0:T(8,128)(2,1)S(1)} %bitcast.66), channel_id=1, source_target_pairs={{0,2},{2,0},{1,3},{3,1},{4,6},{6,4},{5,7},{7,5},{8,10},{10,8},{9,1... | collective-permute-start | bytes 589832 | tf_op jit(solution)/shard_map/ppermute | solution.py:876
  335.2 12.6 %collective-permute-start.64 = (bf16[512,192]{1,0:T(8,128)(2,1)S(1)}, bf16[512,192]{1,0:T(8,128)(2,1)S(1)}, u32[]{:S(2)}, u32[]{:S(2)}) collective-permute-start(bf16[512,192]{1,0:T(8,128)(2,1)S(1)} %bitcast.64), channel_id=1, source_target_pairs={{0,6},{2,4},{4,2},{6,0},{1,7},{3,5},{5,3},{7,1},{8,14},{10,12},{12... | collective-permute-start | bytes 589832 | tf_op jit(solution)/shard_map/ppermute | solution.py:902
  350.1 30.4 %collective-permute-start.22 = (bf16[256,1536]{1,0:T(8,128)(2,1)S(1)}, bf16[256,1536]{1,0:T(8,128)(2,1)}, u32[]{:S(2)}, u32[]{:S(2)}) collective-permute-start(bf16[256,1536]{1,0:T(8,128)(2,1)S(1)} %get-tuple-element.491), channel_id=1, source_target_pairs={{0,1},{1,0},{2,3},{3,2},{4,5},{5,4},{6,7},{7,6},{8,9},{9,8},{10,11... | collective-permute-start | bytes 2359304 | tf_op jit(solution)/shard_map/cond/branch_1_fun/ppermute | solution.py:876
  350.3 30.2 %collective-permute-start.21 = (bf16[256,1536]{1,0:T(8,128)(2,1)S(1)}, bf16[256,1536]{1,0:T(8,128)(2,1)}, u32[]{:S(2)}, u32[]{:S(2)}) collective-permute-start(bf16[256,1536]{1,0:T(8,128)(2,1)S(1)} %get-tuple-element.491), channel_id=1, source_target_pairs={{0,6},{2,4},{4,2},{6,0},{1,7},{3,5},{5,3},{7,1},{8,14},{10,12},{12... | collective-permute-start | bytes 2359304 | tf_op jit(solution)/shard_map/cond/branch_1_fun/ppermute | solution.py:902
  351.7 35.6 %collective-permute-start.20 = (bf16[256,1536]{1,0:T(8,128)(2,1)S(1)}, bf16[256,1536]{1,0:T(8,128)(2,1)}, u32[]{:S(2)}, u32[]{:S(2)}) collective-permute-start(bf16[256,1536]{1,0:T(8,128)(2,1)S(1)} %get-tuple-element.491), channel_id=1, source_target_pairs={{0,4},{4,0},{1,5},{5,1},{2,6},{6,2},{3,7},{7,3},{8,12},{12,8},{9,1... | collective-permute-start | bytes 2359304 | tf_op jit(solution)/shard_map/cond/branch_1_fun/ppermute | solution.py:876
  352.5 35.4 %collective-permute-start.19 = (bf16[256,1536]{1,0:T(8,128)(2,1)S(1)}, bf16[256,1536]{1,0:T(8,128)(2,1)}, u32[]{:S(2)}, u32[]{:S(2)}) collective-permute-start(bf16[256,1536]{1,0:T(8,128)(2,1)S(1)} %get-tuple-element.491), channel_id=1, source_target_pairs={{0,2},{2,0},{1,3},{3,1},{4,6},{6,4},{5,7},{7,5},{8,10},{10,8},{9,1... | collective-permute-start | bytes 2359304 | tf_op jit(solution)/shard_map/cond/branch_1_fun/ppermute | solution.py:876
  392.8 24.2 %collective-permute-start.45 = (bf16[512,320]{1,0:T(8,128)(2,1)}, bf16[512,320]{1,0:T(8,128)(2,1)}, u32[]{:S(2)}, u32[]{:S(2)}) collective-permute-start(bf16[512,320]{1,0:T(8,128)(2,1)} %bitcast.21.refs_4_), channel_id=1, source_target_pairs={{0,6},{2,4},{4,2},{6,0},{1,7},{3,5},{5,3},{7,1},{8,14},{10,12},{12... | collective-permute-start | bytes 983048 | tf_op jit(solution)/shard_map/cond/branch_1_fun/ppermute | solution.py:902
  394.3 22.7 %collective-permute-start.44 = (bf16[512,320]{1,0:T(8,128)(2,1)}, bf16[512,320]{1,0:T(8,128)(2,1)}, u32[]{:S(2)}, u32[]{:S(2)}) collective-permute-start(bf16[512,320]{1,0:T(8,128)(2,1)} %bitcast.19.refs_3_), channel_id=1, source_target_pairs={{0,4},{4,0},{1,5},{5,1},{2,6},{6,2},{3,7},{7,3},{8,12},{12,8},{9,1... | collective-permute-start | bytes 983048 | tf_op jit(solution)/shard_map/cond/branch_1_fun/ppermute | solution.py:876
  395.1 21.9 %collective-permute-start.43 = (bf16[512,320]{1,0:T(8,128)(2,1)}, bf16[512,320]{1,0:T(8,128)(2,1)}, u32[]{:S(2)}, u32[]{:S(2)}) collective-permute-start(bf16[512,320]{1,0:T(8,128)(2,1)} %bitcast.17.refs_2_), channel_id=1, source_target_pairs={{0,2},{2,0},{1,3},{3,1},{4,6},{6,4},{5,7},{7,5},{8,10},{10,8},{9,1... | collective-permute-start | bytes 983048 | tf_op jit(solution)/shard_map/cond/branch_1_fun/ppermute | solution.py:876
  422.7 10.4 %collective-permute-start.51 = (bf16[128,1536]{1,0:T(8,128)(2,1)S(1)}, bf16[128,1536]{1,0:T(8,128)(2,1)S(1)}, u32[]{:S(2)}, u32[]{:S(2)}) collective-permute-start(bf16[128,1536]{1,0:T(8,128)(2,1)S(1)} %get-tuple-element.1048), channel_id=1, source_target_pairs={{0,2},{2,0},{1,3},{3,1},{4,6},{6,4},{5,7},{7,5},{8,10},{10,8},{9,1... | collective-permute-start | bytes 1179656 | tf_op jit(solution)/shard_map/cond/branch_1_fun/ppermute | solution.py:876
  423.6 12.2 %collective-permute-start.50 = (bf16[128,1536]{1,0:T(8,128)(2,1)S(1)}, bf16[128,1536]{1,0:T(8,128)(2,1)}, u32[]{:S(2)}, u32[]{:S(2)}) collective-permute-start(bf16[128,1536]{1,0:T(8,128)(2,1)S(1)} %get-tuple-element.1049), channel_id=1, source_target_pairs={{0,4},{4,0},{1,5},{5,1},{2,6},{6,2},{3,7},{7,3},{8,12},{12,8},{9,1... | collective-permute-start | bytes 1179656 | tf_op jit(solution)/shard_map/cond/branch_1_fun/ppermute | solution.py:876
  424.9 21.5 %collective-permute-start.52 = (bf16[192,1536]{1,0:T(8,128)(2,1)}, bf16[192,1536]{1,0:T(8,128)(2,1)}, u32[]{:S(2)}, u32[]{:S(2)}) collective-permute-start(bf16[192,1536]{1,0:T(8,128)(2,1)} %get-tuple-element.537), channel_id=1, source_target_pairs={{0,4},{4,0},{1,5},{5,1},{2,6},{6,2},{3,7},{7,3},{8,12},{12,8},{9,1... | collective-permute-start | bytes 1769480 | tf_op jit(solution)/shard_map/cond/branch_1_fun/ppermute | solution.py:876
  425.7 22.9 %collective-permute-start.57 = (bf16[320,1536]{1,0:T(8,128)(2,1)S(1)}, bf16[320,1536]{1,0:T(8,128)(2,1)}, u32[]{:S(2)}, u32[]{:S(2)}) collective-permute-start(bf16[320,1536]{1,0:T(8,128)(2,1)S(1)} %get-tuple-element.545), channel_id=1, source_target_pairs={{0,1},{1,0},{2,3},{3,2},{4,5},{5,4},{6,7},{7,6},{8,9},{9,8},{10,11... | collective-permute-start | bytes 2949128 | tf_op jit(solution)/shard_map/cond/branch_1_fun/ppermute | solution.py:876
  425.7 22.9 %collective-permute-start.56 = (bf16[320,1536]{1,0:T(8,128)(2,1)}, bf16[320,1536]{1,0:T(8,128)(2,1)}, u32[]{:S(2)}, u32[]{:S(2)}) collective-permute-start(bf16[320,1536]{1,0:T(8,128)(2,1)} %get-tuple-element.544), channel_id=1, source_target_pairs={{0,1},{1,0},{2,3},{3,2},{4,5},{5,4},{6,7},{7,6},{8,9},{9,8},{10,11... | collective-permute-start | bytes 2949128 | tf_op jit(solution)/shard_map/cond/branch_1_fun/ppermute | solution.py:876
  433.1 15.5 %collective-permute-start.55 = (bf16[320,1536]{1,0:T(8,128)(2,1)}, bf16[320,1536]{1,0:T(8,128)(2,1)}, u32[]{:S(2)}, u32[]{:S(2)}) collective-permute-start(bf16[320,1536]{1,0:T(8,128)(2,1)} %get-tuple-element.543), channel_id=1, source_target_pairs={{0,1},{1,0},{2,3},{3,2},{4,5},{5,4},{6,7},{7,6},{8,9},{9,8},{10,11... | collective-permute-start | bytes 2949128 | tf_op jit(solution)/shard_map/cond/branch_1_fun/ppermute | solution.py:876
  435.8 12.8 %collective-permute-start.54 = (bf16[320,1536]{1,0:T(8,128)(2,1)}, bf16[320,1536]{1,0:T(8,128)(2,1)}, u32[]{:S(2)}, u32[]{:S(2)}) collective-permute-start(bf16[320,1536]{1,0:T(8,128)(2,1)} %get-tuple-element.542), channel_id=1, source_target_pairs={{0,1},{1,0},{2,3},{3,2},{4,5},{5,4},{6,7},{7,6},{8,9},{9,8},{10,11... | collective-permute-start | bytes 2949128 | tf_op jit(solution)/shard_map/cond/branch_1_fun/ppermute | solution.py:876
  451.5 29.4 %collective-permute-start.47 = (bf16[256,1536]{1,0:T(8,128)(2,1)}, bf16[256,1536]{1,0:T(8,128)(2,1)}, u32[]{:S(2)}, u32[]{:S(2)}) collective-permute-start(bf16[256,1536]{1,0:T(8,128)(2,1)} %get-tuple-element.547), channel_id=1, source_target_pairs={{0,4},{4,0},{1,5},{5,1},{2,6},{6,2},{3,7},{7,3},{8,12},{12,8},{9,1... | collective-permute-start | bytes 2359304 | tf_op jit(solution)/shard_map/cond/branch_1_fun/ppermute | solution.py:876
  452.7 28.2 %collective-permute-start.46 = (bf16[256,1536]{1,0:T(8,128)(2,1)}, bf16[256,1536]{1,0:T(8,128)(2,1)}, u32[]{:S(2)}, u32[]{:S(2)}) collective-permute-start(bf16[256,1536]{1,0:T(8,128)(2,1)} %get-tuple-element.546), channel_id=1, source_target_pairs={{0,2},{2,0},{1,3},{3,1},{4,6},{6,4},{5,7},{7,5},{8,10},{10,8},{9,1... | collective-permute-start | bytes 2359304 | tf_op jit(solution)/shard_map/cond/branch_1_fun/ppermute | solution.py:876
  455.7 25.1 %collective-permute-start.48 = (bf16[192,1152]{1,0:T(8,128)(2,1)}, bf16[192,1152]{1,0:T(8,128)(2,1)}, u32[]{:S(2)}, u32[]{:S(2)}) collective-permute-start(bf16[192,1152]{1,0:T(8,128)(2,1)} %constant_dynamic-slice_fusion.1), channel_id=1, source_target_pairs={{0,4},{4,0},{1,5},{5,1},{2,6},{6,2},{3,7},{7,3},{8,12},{12,8},{9,1... | collective-permute-start | bytes 1327112 | tf_op jit(solution)/shard_map/cond/branch_1_fun/ppermute | solution.py:876
  (87 other events, 565.6 us)
Sparse Core Ops, SparseCore 0:
  40.8 43.8 all-gather.3
  88.8 89.6 all-gather.7
  180.7 68.4 all-gather.5
  251.3 83.8 reduce-scatter.3
  337.3 66.8 reduce-scatter.5
  418.5 40.6 reduce-scatter.7

commit v5 on v4

--- a/solution.py
+++ b/solution.py
@@ -101,8 +101,8 @@
 
 def load_pair(refs, pair, core):
     values = refs[0][core, 0]
-    for k in range(1, 4):
-        values = jnp.where(pair == k, refs[k][core, 0], values)
+    for k, ref in enumerate(refs[1:], 1):
+        values = jnp.where(pair == k, ref[core, 0], values)
     return values
 
 
@@ -142,11 +142,18 @@
         stat_ref[source] = stats
 
 
-def attend_backward(place_ref, qkv_ref, grad_ref, stat_ref, *refs):
-    *mixed_refs, gain_ref, cos_ref, sin_ref = refs[:7]
-    *out_refs, gain_grad_ref, keys, values, key_grads, value_grads, query_grads = refs[7:]
+def place_in_sequence(place, block):
+    away = jnp.bitwise_xor(place, block)
+    core, y = jnp.bitwise_and(away, 1), lax.shift_right_logical(away, 1)
+    return (core, 0, y, 0), y, core
+
+
+def attend_backward(place_ref, qkv_ref, stat_ref, far_ref, *refs):
+    near_refs, mixed_refs = refs[:2], refs[2:4]
+    gain_ref, cos_ref, sin_ref, *out_refs = refs[4:9]
+    gain_grad_ref, keys, values, key_grads, value_grads, query_grads = refs[9:]
     place = place_ref[0]
-    tokens = qkv_ref.shape[2]
+    tokens = qkv_ref.shape[4]
     gain = gain_ref[...]
     key_row = lax.broadcasted_iota(jnp.int32, (tokens, tokens), 0)
     query_row = lax.broadcasted_iota(jnp.int32, (tokens, tokens), 1)
@@ -154,14 +161,15 @@
     key_grads[...] = jnp.zeros_like(key_grads)
     value_grads[...] = jnp.zeros_like(value_grads)
     for block in range(4):
-        source, pair, core = block_at(place, block)
+        source, pair, core = place_in_sequence(place, block)
         here = pl.ds(block * tokens, tokens)
         raw = qkv_ref[source]
         unit, _ = unit_heads(raw[:, :QK].astype(F32))
         turned = rotated(unit, gain, cos_ref[here], sin_ref[here])
         keys[here] = with_ones(turned[:, GROUP * HEAD_DIM :].astype(BF16), 3)
         values[here] = with_ones(raw[:, QK:], 3)
-        grads = grad_ref[source].astype(F32)
+        near = jnp.where(pair == 0, near_refs[0][0, 0], near_refs[1][0, 0])
+        grads = jnp.where(core == 0, near, far_ref[pair, 0]).astype(F32)
         product = load_pair(mixed_refs, pair, core).astype(F32) * grads
         stats = stat_ref[source]
         for head in range(GROUP):
@@ -185,7 +193,7 @@
             query_grads[here, lanes] = query_total[:, :HEAD_DIM] * HEAD_DIM**-0.5
     gain_total = jnp.zeros((1, QK), F32)
     for block in range(4):
-        source, pair, core = block_at(place, block)
+        source, pair, core = place_in_sequence(place, block)
         here = pl.ds(block * tokens, tokens)
         raw = qkv_ref[source]
         unit, scale = unit_heads(raw[:, :QK].astype(F32))
@@ -256,28 +264,55 @@
     return mixed, stats
 
 
-def backward_attention(place, qkv, mixed, grads, stats, gain, cosine, sine, deps=()):
+def backward_attention(place, sequence, qkv, mixed, grads, stats, gain, cosine, sine):
     batch, tokens = qkv.shape[1:3]
     length = 4 * tokens
-    *qkv_grads, head_part = attention_call(
+
+    def spread(array):
+        return array.reshape((2, 2, 2) + array.shape[1:])
+
+    def spec(array):
+        tail = tuple(array.shape[4:])
+        return pl.BlockSpec((2, 1, 2, 1) + tail, lambda i, *_: (0, sequence, 0, i, 0, 0))
+
+    def pair_spec(width):
+        return pl.BlockSpec((2, 1, tokens, width), lambda i, *_: (0, i, 0, 0))
+
+    def own_half(array):
+        return pl.BlockSpec((1, 1) + array.shape[2:], lambda i, *_: (0, i, 0, 0))
+
+    blocked = [spread(array) for array in (qkv, stats)]
+    here = slice(2 * sequence, 2 * sequence + 2)
+    near = [pair.reshape(2, batch, tokens, -1) for pair in grads[0][here]]
+    far = grads[1].reshape(4, batch, tokens, -1)
+    mixed = mixed[here]
+    whole = [gain, cosine, sine]
+    width = qkv.shape[3]
+    *qkv_grads, head_part = pl.pallas_call(
         attend_backward,
-        "attend_backward",
-        place,
-        [qkv, grads, stats, *mixed],
-        [gain, cosine, sine],
-        [jax.ShapeDtypeStruct((2,) + qkv.shape[1:], BF16)] * 4
-        + [jax.ShapeDtypeStruct((2 * batch, 8, QK), F32)],
-        [
-            pltpu.VMEM((length, AUG), BF16),
-            pltpu.VMEM((length, AUG), BF16),
-            pltpu.VMEM((length, AUG), F32),
-            pltpu.VMEM((length, AUG), F32),
-            pltpu.VMEM((length, GROUP * HEAD_DIM), F32),
-        ],
-        deps,
-        34,
-        0.0,
-    )
+        grid_spec=pltpu.PrefetchScalarGridSpec(
+            num_scalar_prefetch=1,
+            grid=(batch,),
+            in_specs=[spec(a) for a in blocked]
+            + [pl.BlockSpec((2, 1) + far.shape[2:], lambda i, *_: (sequence, i, 0, 0))]
+            + [own_half(pair) for pair in near]
+            + [pair_spec(GROUP * HEAD_DIM)] * 2
+            + [pl.BlockSpec(a.shape, lambda i, *_: (0, 0)) for a in whole],
+            out_specs=[pair_spec(width)] * 2 + [pl.BlockSpec((1, 8, QK), lambda i, *_: (i, 0, 0))],
+            scratch_shapes=[
+                pltpu.VMEM((length, AUG), BF16),
+                pltpu.VMEM((length, AUG), BF16),
+                pltpu.VMEM((length, AUG), F32),
+                pltpu.VMEM((length, AUG), F32),
+                pltpu.VMEM((length, GROUP * HEAD_DIM), F32),
+            ],
+        ),
+        out_shape=[jax.ShapeDtypeStruct((2, batch, tokens, width), BF16)] * 2
+        + [jax.ShapeDtypeStruct((batch, 8, QK), F32)],
+        name="attend_backward",
+        cost_estimate=cost(0),
+        compiler_params=pltpu.CompilerParams(vmem_limit_bytes=60 << 20),
+    )(place, *blocked, far, *near, *mixed, *whole)
     return qkv_grads, head_part
 
 
@@ -499,12 +534,13 @@
                 value = part if value is None else value + part
             line.append(value)
             if index == 0 and gains is not None:
-                weight, rest, heads = refs[spec_count : spec_count + 3]
+                weight, rest, *heads = refs[spec_count : spec_count + 2 + len(gains[2])]
                 width = widths[0]
                 scaled = jnp.sum(weight[:, :width].astype(F32) * value, axis=1, keepdims=True)
                 scaled = scaled / weight[:, width : width + 1].astype(F32)
                 lane = lax.broadcasted_iota(jnp.int32, rest.shape, 1)
-                column = head_column(jnp.sum(heads[...], axis=0)[:1], gains[3], depth)
+                sums = sum(jnp.sum(ref[...], axis=0)[:1] for ref in heads)
+                column = head_column(sums, gains[3], depth)
                 values = jnp.where(lane == 2, column, rest[...])
                 line.append(jnp.where(lane == 0, scaled, values))
         if lanes > sum(widths) + others:
@@ -522,8 +558,8 @@
         for array in gains[:2]:
             specs.append(pl.BlockSpec((tile, array.shape[1]), lambda i: (i, 0)))
             args.append(array)
-        specs.append(pl.BlockSpec(gains[2].shape, lambda i: (0, 0, 0)))
-        args.append(gains[2])
+        specs += [entire(heads) for heads in gains[2]]
+        args += gains[2]
     return pl.pallas_call(
         body,
         grid=(depth // tile,),
@@ -637,7 +673,7 @@
     def body(*refs):
         mine_ref, first, second, third, middle_ref, up_ref = refs[:6]
         weight_refs, gain_ref = refs[6:14], refs[14]
-        grad_ref, low_ref, *pair_refs, sum_ref = refs[15 + len(deps) :]
+        grad_ref, low_ref, *pair_refs, sum_ref, sums = refs[15 + len(deps) :]
         post_grad = mine_ref[...]
         for ref in (first, second, third):
             post_grad = post_grad + ref[...].astype(F32)
@@ -653,9 +689,15 @@
 
         @pl.when(pl.program_id(0) == 0)
         def _():
-            sum_ref[...] = jnp.zeros_like(sum_ref)
-
-        sum_ref[...] += jnp.broadcast_to(total, sum_ref.shape)
+            sums[...] = jnp.zeros_like(sums)
+
+        sums[...] += jnp.broadcast_to(total, sums.shape)
+
+        @pl.when(pl.program_id(0) == rows // TILE - 1)
+        def _():
+            column = jnp.concatenate([sums[...].T] * (GAIN_LANES // 8), axis=1)
+            lane = lax.broadcasted_iota(jnp.int32, column.shape, 1)
+            sum_ref[...] = jnp.where(lane == 1, column, 0.0)
 
     side = pl.BlockSpec((2, TILE, width), lambda i: (0, i, 0))
     return pl.pallas_call(
@@ -667,13 +709,14 @@
         + [ANY] * len(deps),
         out_specs=[row_tiles(middle)] * 2
         + [side] * 4
-        + [pl.BlockSpec((8, depth), lambda i: (0, 0))],
+        + [pl.BlockSpec((depth, GAIN_LANES), lambda i: (0, 0))],
         out_shape=[
             jax.ShapeDtypeStruct((rows, depth), F32),
             jax.ShapeDtypeStruct((rows, depth), BF16),
             *[jax.ShapeDtypeStruct((2, rows, width), BF16)] * 4,
-            jax.ShapeDtypeStruct((8, depth), F32),
+            jax.ShapeDtypeStruct((depth, GAIN_LANES), F32),
         ],
+        scratch_shapes=[pltpu.VMEM((8, depth), F32)],
         name="middle_back",
         cost_estimate=cost(0),
         compiler_params=pltpu.CompilerParams(vmem_limit_bytes=48 << 20),
@@ -752,6 +795,65 @@
     )(for_y, for_x, by_x, by_y)
 
 
+def halves(sides):
+    count = len(sides)
+    rows, width = sides[0][0].shape[0] // 2, sides[0][0].shape[1]
+
+    def body(*refs):
+        for k in range(count):
+            here = slice(k * rows, (k + 1) * rows)
+            refs[2 * count][here] = refs[2 * k][...]
+            refs[2 * count + 1][here] = refs[2 * k + 1][...]
+
+    block = [pl.BlockSpec((rows, width), lambda i, k=k: (k, 0)) for k in range(2)]
+    return pl.pallas_call(
+        body,
+        grid=(1,),
+        in_specs=block * count,
+        out_specs=[pl.BlockSpec((count * rows, width), lambda i: (0, 0))] * 2,
+        out_shape=[jax.ShapeDtypeStruct((count * rows, width), sides[0][0].dtype)] * 2,
+        name="halves",
+        cost_estimate=cost(0),
+        compiler_params=pltpu.CompilerParams(vmem_limit_bytes=60 << 20),
+    )(*[side for pair in sides for side in pair])
+
+
+def joined(first, second, count):
+    rows, width = first.shape[0] // count, first.shape[1]
+
+    def body(first_ref, second_ref, *outs):
+        for k, out in enumerate(outs):
+            out[:rows] = first_ref[k * rows : (k + 1) * rows]
+            out[rows:] = second_ref[k * rows : (k + 1) * rows]
+
+    return pl.pallas_call(
+        body,
+        out_shape=[jax.ShapeDtypeStruct((2 * rows, width), first.dtype)] * count,
+        name="joined",
+        cost_estimate=cost(0),
+        compiler_params=pltpu.CompilerParams(vmem_limit_bytes=60 << 20),
+    )(first, second)
+
+
+def far_parts(pairs):
+    rows, width = pairs[0].shape[0] // 2, pairs[0].shape[1]
+
+    def body(*refs):
+        for k in range(4):
+            refs[4][k * rows : (k + 1) * rows] = refs[k][...]
+
+    return pl.pallas_call(
+        body,
+        grid=(1,),
+        in_specs=[pl.BlockSpec((rows, width), lambda i: (1, 0))] * 4,
+        out_specs=pl.BlockSpec((4 * rows, width), lambda i: (0, 0)),
+        out_shape=jax.ShapeDtypeStruct((4 * rows, width), pairs[0].dtype),
+        name="far_parts",
+        cost_estimate=cost(0),
+        compiler_params=pltpu.CompilerParams(vmem_limit_bytes=60 << 20),
+    )(*pairs)
+
+
 def turn(weight, spans, held, span):
     rows = weight.shape[0]
 
@@ -779,21 +881,30 @@
     )(weight)
 
 
-def pack_columns(weights, layouts, extra=None):
+def pack_columns(weights, layouts, gains=()):
     rows = weights[0].shape[0]
     count = len(weights)
     spans = [w.shape[1] // 8 for w in weights]
-    extras = [] if extra is None else [extra]
 
     def body(*refs):
-        outs = refs[count + len(extras) :]
+        outs = refs[count + len(gains) :]
+        columns = None
+        if gains:
+            lane = lax.broadcasted_iota(jnp.int32, (rows, GAIN_LANES), 1)
+            columns = jnp.zeros((rows, GAIN_LANES), F32)
+            for k, ref in enumerate(refs[count : count + len(gains)]):
+                size = ref.shape[1]
+                here = lax.broadcasted_iota(jnp.int32, (rows, size), 0)
+                here = here == lax.broadcasted_iota(jnp.int32, (rows, size), 1)
+                column = jnp.sum(jnp.where(here, ref[...].astype(F32), 0.0), axis=1, keepdims=True)
+                columns = jnp.where(lane == k, column, columns)
         for place in range(8):
             x, s = place // 4, place % 4
             for out, layout in zip(outs, layouts):
                 line = []
                 for entry in layout:
                     if entry is None:
-                        line.append(refs[count][...].astype(F32))
+                        line.append(columns)
                     elif isinstance(entry, int):
                         line.append(jnp.zeros((rows, entry), F32))
                     else:
@@ -804,7 +915,7 @@
 
     def lanes(entry):
         if entry is None:
-            return extra.shape[1]
+            return GAIN_LANES
         return entry if isinstance(entry, int) else entry[2] - entry[1]
 
     return pl.pallas_call(
@@ -814,8 +925,8 @@
             for layout in layouts
         ],
         name="pack_columns",
-        compiler_params=pltpu.CompilerParams(vmem_limit_bytes=48 << 20),
-    )(*weights, *extras)
+        compiler_params=pltpu.CompilerParams(vmem_limit_bytes=60 << 20),
+    )(*weights, *gains)
 
 
 def unpack_columns(x, sums, others, outputs, dtype=F32):
@@ -889,9 +1000,9 @@
     return swap(rows, "y"), swap(rows, "x")
 
 
-def corner_comes(from_y, from_x):
-    half = from_y.shape[0] // 2
-    return swap(from_y[:half], "x"), swap(from_x[half:], "y")
+def corners_come(*sides):
+    by_x, by_y = halves(sides)
+    return swap(by_x, "x"), swap(by_y, "y")
 
 
 def across(pieces):
@@ -912,8 +1023,7 @@
 
 
 def exchange_all(came):
-    rows = came[0].shape[0] // 2
-    return came, swap(jnp.concatenate([pair[rows:] for pair in came]), "c")
+    return came, swap(far_parts(came), "c")
 
 
 def scatter_end(mine, others):
@@ -973,10 +1083,7 @@
     wide = gate_weight.shape[1] // 8
     place = (2 * lax.axis_index("y") + lax.axis_index("c")).astype(jnp.int32).reshape(1)
 
-    gain_rows = jnp.stack(
-        [attention_gain, feedforward_gain, jnp.pad(head_gains, (0, rows - head_rows))], axis=1
-    )
-    gain_rows = jnp.pad(gain_rows, ((0, 0), (0, GAIN_LANES - 3)))
+    gain_rows = [gain.reshape(1, -1) for gain in (attention_gain, feedforward_gain, head_gains)]
     own_hidden = layer_input.reshape(own_rows, model_width)
     own_upstream = upstream.reshape(own_rows, model_width)
     cut = 512
@@ -990,10 +1097,7 @@
         gain_rows,
     )
 
-    def start(payload, own_hidden):
-        return plane_columns(payload), sides_come(own_hidden)
-
-    first_block, hidden_sides = together(start, first_payload, own_hidden)
+    first_block = plane_columns(first_payload)
     first_full = line_gather(first_block)
     payloads = pack_columns(
         [gate_weight, up_weight, down_weight],
@@ -1003,25 +1107,32 @@
         ],
     )
 
-    def begin(own_hidden, hidden_sides, payloads):
-        corner = corner_comes(*hidden_sides)
-        far = across([own_hidden, *hidden_sides])
-        blocks = [plane_columns(payload) for payload in payloads]
-        return corner, far, blocks, rotary_rows(4 * tokens)
-
-    corner, far, ffn_blocks, (cosine, sine) = together(
-        begin, own_hidden, hidden_sides, [after(payload, first_block) for payload in payloads]
-    )
-    corner = jnp.concatenate(corner)
+    early_block = plane_columns(after(payloads[0], first_block))
+    out_first = qkv_cols + GAIN_LANES
+
+    def hidden_comes(own_hidden, payload):
+        return sides_come(own_hidden), plane_columns(payload)
+
+    hidden_sides, late_block = together(
+        hidden_comes, after(own_hidden, early_block), payloads[1]
+    )
+    ffn_full = [line_gather(block) for block in (early_block, late_block)]
+
+    def hidden_corner(own_hidden, hidden_sides, first_full):
+        turned = turn(
+            first_full,
+            [(0, qkv_cols), (qkv_cols, qkv_cols + 16), (out_first, out_first + query_cols)],
+            head_rows,
+            rows,
+        )
+        come = corners_come(hidden_sides), across([own_hidden, *hidden_sides])
+        return *come, turned, rotary_rows(4 * tokens)
+
+    corner, far, (qkv_rows, gain_turned, out_rows, head_scale), (cosine, sine) = together(
+        hidden_corner, own_hidden, hidden_sides, first_full
+    )
+    (corner,) = joined(*corner, 1)
     hidden = [own_hidden, *hidden_sides, corner, *far, swap(corner, "c")]
-    ffn_full = [line_gather(block) for block in ffn_blocks]
-    out_first = qkv_cols + GAIN_LANES
-    qkv_rows, gain_turned, out_rows, head_scale = turn(
-        first_full,
-        [(0, qkv_cols), (qkv_cols, qkv_cols + 16), (out_first, out_first + query_cols)],
-        head_rows,
-        rows,
-    )
 
     def attend(hidden, gain_turned, first_full, out_rows, head_scale, cosine, sine):
         out_near, out_first = plane_near(out_rows)
@@ -1045,7 +1156,7 @@
 
     def attended(mixed, out_weights, own_hidden, own_upstream, gain_turned):
         came = exchange_near([pair.reshape(-1, query_cols) for pair in mixed])
-        grad_sides = sides_come(after(own_upstream, *came[1:]))
+        grad_sides = sides_come(after(own_upstream, came[1]))
         out_weights = plane_all(out_weights)
         middle, post = attend_out(exchange_all(came), out_weights, own_hidden, gain_turned)
         grad_far = across([own_upstream, *grad_sides])
@@ -1060,13 +1171,12 @@
     out_weights = [*out_weights[0], out_weights[1], *out_far]
 
     def first_blocks(post, grads, weight):
-        corner = corner_comes(*post[1:])
-        grad_corner = corner_comes(*grads[1:])
+        corners = corners_come(post[1:], grads[1:])
         far = across(post[1:])
-        return corner, grad_corner, far, feed_forward(post, grads, weight, [3])
-
-    corner, grad_corner, far, early = together(first_blocks, post, grads, ffn_full[0])
-    corner, grad_corner = jnp.concatenate(corner), jnp.concatenate(grad_corner)
+        return corners, far, feed_forward(post, grads, weight, [3])
+
+    corners, far, early = together(first_blocks, post, grads, ffn_full[0])
+    corner, grad_corner = joined(*corners, 2)
     post = [*post, corner, *post_far, *far, swap(corner, "c")]
     grads = [*grads, grad_corner, *grad_far, swap(grad_corner, "c")]
 
@@ -1084,7 +1194,7 @@
     sums_0 = line_scatter(parts_0)
 
     def second_chunk(post, grads, weight, total, qkv_sides):
-        qkv_corner = corner_comes(*qkv_sides)
+        qkv_corner = corners_come(qkv_sides)
         return qkv_corner, feed_forward(post, grads, weight, [1, 4], total)
 
     qkv_corner, late = together(
@@ -1093,9 +1203,7 @@
     far = swap(late[2][1], "c")
     early = feed_forward(post[:3], grads[:3], ffn_full[1], [3], total[:1], late[2][1:])
     both_1, act_1 = [early[0], late[0]], [early[1], late[1]]
-    qkv_corner = jnp.concatenate(qkv_corner)
     mine, *parts = core_sum(early[2] + late[2][:1], far)
-    qkv_weights = [qkv_rows, *qkv_sides, qkv_corner]
 
     def behind(parts, post, grads, act_0, act_1, both_1, weights):
         others = diamond(*parts)
@@ -1113,33 +1221,46 @@
 
     branch_far = swap(branch[2], "c")
 
-    near, far = exchange_all(exchange_near([pair.reshape(-1, query_cols) for pair in pairs]))
-    mixed_grad = jnp.concatenate([*[pair[:own_rows] for pair in near], far])
-
-    def back(middle_low, qkv, mixed, mixed_grad, stats, head_scale, cosine, sine):
-        middle_near, middle_first = plane_near(middle_low)
-        qkv_grad, head_part = backward_attention(
-            place, qkv, mixed, mixed_grad, stats, head_scale, cosine, sine
-        )
-        return middle_near[1:], middle_first, qkv_grad, head_part
-
-    mixed_grad = mixed_grad.reshape(8, batch, tokens, query_cols)
-    middle_near, middle_first, qkv_grad, head_part = together(
-        back,
+    mixed_grad = exchange_all(exchange_near([pair.reshape(-1, query_cols) for pair in pairs]))
+
+    tables = head_scale, cosine, sine
+
+    def back_first(middle_low, qkv, mixed, mixed_grad, stats, tables, sums_0):
+        middle_sides = sides_come(middle_low)
+        middle_first = swap(middle_low, "c")
+        grads = backward_attention(place, 0, qkv, mixed, mixed_grad, stats, *tables)
+        send_0 = for_x_side(sums_0)
+        return middle_sides, middle_first, grads, send_0
+
+    middle_sides, middle_first, first_grads, send_0 = together(
+        back_first,
         middle_low,
         qkv,
         mixed,
         mixed_grad,
         stats,
-        head_scale,
-        cosine,
-        sine,
-    )
-    middle_whole = plane_all(([middle_low, *middle_near], middle_first))
+        tables,
+        sums_0,
+    )
+
+    def back_second(middle_sides, qkv, mixed, mixed_grad, stats, tables, send_0):
+        corner = swap(middle_sides[1], "y")
+        other_0 = swap(send_0, "x")
+        far = across(middle_sides)
+        grads = backward_attention(place, 1, qkv, mixed, mixed_grad, stats, *tables)
+        return corner, other_0, far, grads
+
+    corner, other_0, far, second_grads = together(
+        back_second, middle_sides, qkv, mixed, mixed_grad, stats, tables, send_0
+    )
+    middle_whole = [middle_low, *middle_sides, corner, middle_first, *far, swap(corner, "c")]
+    qkv_grad = first_grads[0] + second_grads[0]
+    head_part = [first_grads[1], second_grads[1]]
     sums_1 = line_scatter(parts_1)
-    gain_parts = jnp.pad(feedforward_part[0][:, None], ((0, 0), (1, GAIN_LANES - 2)))
-
-    def attention_grads(branch, sums_0, qkv_grad, normed, middle_whole, mixed, first_full, gain_parts, head_part):
+    gain_parts = feedforward_part
+
+
+    def attention_grads(branch, qkv_grad, normed, middle_whole, mixed, first_full, gain_parts, head_part):
         qkv_grad = [pair.reshape(-1, qkv_cols) for pair in qkv_grad]
         mixed = [pair.reshape(-1, query_cols) for pair in mixed]
         came = exchange_near(qkv_grad)
@@ -1148,12 +1269,11 @@
             gains=(first_full, gain_parts, head_part, head_rows),
             paired=True,
         )
-        return came[1:], parts, core_sum(*branch), for_x_side(sums_0)
-
-    came, attention_parts, branch, send_0 = together(
+        return came[1:], parts, core_sum(*branch)
+
+    came, attention_parts, branch = together(
         attention_grads,
         (branch[:2], branch_far),
-        sums_0,
         qkv_grad,
         normed,
         middle_whole,
@@ -1163,30 +1283,37 @@
         head_part,
     )
     attention_sums = line_scatter(after(attention_parts, sums_1))
-    x = lax.axis_index("x").astype(jnp.int32).reshape(1)
-
-    branch_mine, for_y, for_x, corner = branch
+    branch_mine, for_y, for_x, branch_corner = branch
     middle_rows = own_rows // 2
 
-    def corners(corner, send_0, qkv_pair, came, qkv_weights):
+    def corners(corner, qkv_pair, came, qkv_corner):
         by_x, by_y = swap(corner[:middle_rows], "x"), swap(corner[middle_rows:], "y")
-        other_0 = swap(send_0, "x")
-        return by_x, by_y, other_0, exchange_all([qkv_pair, *came])[1], across(qkv_weights)
-
-    by_x, by_y, other_0, pairs_far, qkv_far = together(
-        corners, corner, send_0, qkv_grad[0].reshape(-1, qkv_cols), came, qkv_weights
-    )
-    qkv_weights = qkv_weights + qkv_far
+        return by_x, by_y, exchange_all([qkv_pair, *came])[1], joined(*qkv_corner, 1)
+
+    by_x, by_y, pairs_far, qkv_corner = together(
+        corners, branch_corner, qkv_grad[0].reshape(-1, qkv_cols), came, qkv_corner
+    )
+    qkv_weights = [qkv_rows, *qkv_sides, *qkv_corner]
+    qkv_pairs = [qkv_grad[0].reshape(-1, qkv_cols), *came], pairs_far
     for_y, for_x = corner_sum(for_y, for_x, by_x, by_y)
-    qkv_pairs = [qkv_grad[0].reshape(-1, qkv_cols), *came], pairs_far
 
     def sides(for_y, for_x, sums_1, qkv_pairs, qkv_weights, own_hidden, middle_grad, gain_turned):
-        others = swap(for_y, "y"), swap(for_x, "x"), swap(for_x_side(sums_1), "x")
-        input_grad = input_back(qkv_pairs, qkv_weights, own_hidden, middle_grad, gain_turned)
-        return *others, input_grad
+        others = swap(for_y, "y"), swap(for_x, "x")
+        weights = qkv_weights + across(qkv_weights)
+        input_grad = input_back(qkv_pairs, weights, own_hidden, middle_grad, gain_turned)
+        other_1 = swap(after(for_x_side(sums_1), input_grad), "x")
+        return *others, other_1, input_grad
 
     *branch_others, other_1, input_grad = together(
-        sides, for_y, for_x, sums_1, qkv_pairs, qkv_weights, own_hidden, middle_grad, gain_turned
+        sides,
+        for_y,
+        for_x,
+        sums_1,
+        qkv_pairs,
+        qkv_weights,
+        own_hidden,
+        middle_grad,
+        gain_turned,
     )
     x = lax.axis_index("x").astype(jnp.int32).reshape(1)
 

time: 511 us -> 500 us (0.978)
  local copies, waits for them, and re-layouts: 53.5 us -> 19.1 us
  blocking collectives: 39 us -> 62.7 us
  Pallas kernels: 210 us -> 232 us
  starting transfers between devices: 60.6 us -> 48.6 us
  waiting for transfers between devices: 119 us -> 108 us
    pallas_call x0 -> x11, Pallas kernels: none -> 45.5 us  [the longest x2 28.4 us: backward_attention(): pl.pallas_call(attend_backward, grid_spec=pltpu.PrefetchScalarGridSpec(nu...]
    pallas_call x2 -> x1, Pallas kernels: 41.1 us -> 14.3 us  [attention_call(): pl.pallas_call(body, grid_spec=pltpu.PrefetchScalarGridSpec(num_scalar_pr...]
    all_to_all x2 -> x3, blocking collectives: 39 us -> 62.7 us  [plane_columns(): lax.all_to_all(payload, PLANE, split_axis=0, concat_axis=0, tiled=True)]
    ppermute x66 -> x65, waiting for transfers between devices: 103 us -> 87.6 us  [swap(): return lax.ppermute(values, axis, SWAP)]
    slice x20 -> x0, local copies, waits for them, and re-layouts: 11.6 us -> none  [the longest x8 9.2 us: corner_comes(): return (swap(from_y[:half], 'x'), swap(from_x[half:], 'y'))]
    unnamed x95 -> x75, local copies, waits for them, and re-layouts: 17.4 us -> 8.41 us
    another operation x9 -> x1, local copies, waits for them, and re-layouts: 7.95 us -> 1.45 us
    ppermute x66 -> x65, starting transfers between devices: 44.4 us -> 38.8 us  [swap(): return lax.ppermute(values, axis, SWAP)]
  transfers between devices with their start and end apart: 80 -> 77, of which waited for: 28 -> 38; matrix products, arithmetic and copies ran while one was open for 8% -> 3% of each run, Pallas kernels for 41% -> 46%
where the time goes in v5:
time: 500 us; the launch traced here: 491 us
  Pallas kernels  232 us (46%)
  waiting for transfers between devices  108 us (22%)
  blocking collectives  62.7 us (13%)
  starting transfers between devices  48.6 us (10%)
  local copies, waits for them, and re-layouts  19.1 us (4%)
  between operations  14.8 us (3%)
  other arithmetic  5.93 us (1%)
    ppermute x65, waiting for transfers between devices, swap(): return lax.ppermute(values, axis, SWAP)  87.6 us
    all_to_all x3, blocking collectives, plane_columns(): lax.all_to_all(payload, PLANE, split_axis=0, concat_axis=0, tiled=True)  62.7 us
    pallas_call x4, Pallas kernels, feed_forward(): pl.pallas_call(body, grid=(rows // TILE,), in_specs=specs * 2 + [entire(w...  56.1 us
    pallas_call x3, Pallas kernels, weight_grads(): pl.pallas_call(body, grid=(depth // tile,), in_specs=specs + [ANY] * len(...  39.5 us
    ppermute x65, starting transfers between devices, swap(): return lax.ppermute(values, axis, SWAP)  38.8 us
    pallas_call x2, Pallas kernels, backward_attention(): pl.pallas_call(attend_backward, grid_spec=pltpu.PrefetchScalarGridSpec(nu...  28.4 us
    ppermute x5, waiting for transfers between devices, opposite(): return lax.ppermute(rows, ('x', 'y'), ((0, 3), (1, 2), (2, 1), (3, 0)))  18.8 us
    pallas_call x1, Pallas kernels, attention_call(): pl.pallas_call(body, grid_spec=pltpu.PrefetchScalarGridSpec(num_scalar_pr...  14.3 us
  transfers between devices with their start and end apart: 77, of which 38 were waited for; matrix products, arithmetic and copies ran while one was open for 3% of the time, Pallas kernels for 46%

profile of v5, /device:TPU:0, one launch (start us, length us, event | category | flops | bytes accessed | tf_op | source)
XLA Modules:
  0.0 490.9 jit_solution(11157053673327320376)
XLA Ops:
  9.2 14.0 %all_to_all.15 = bf16[8,48,640]{2,1,0:T(8,128)(2,1)} all-to-all(bf16[8,48,640]{2,1,0:T(8,128)(2,1)} %pack_columns.3), channel_id=1, replica_groups=mesh['dp'=4,'x'=2,'y'=2,'c'=2] {'x','y','c'}, dimensions={0} | all-to-all | bytes 983040 | tf_op jit(solution)/shard_map/all_to_all | solution.py:1053
  23.3 3.1 pack_columns.2
  26.4 21.0 %all_to_all.16 = bf16[8,48,1536]{2,1,0:T(8,128)(2,1)} all-to-all(bf16[8,48,1536]{2,1,0:T(8,128)(2,1)} %after.8), channel_id=1, replica_groups=mesh['dp'=4,'x'=2,'y'=2,'c'=2] {'x','y','c'}, dimensions={0} | all-to-all | bytes 2359296 | tf_op jit(solution)/shard_map/all_to_all | solution.py:1053
  47.5 29.4 %conditional.14 = (bf16[256,1536]{1,0:T(8,128)(2,1)}, bf16[256,1536]{1,0:T(8,128)(2,1)}, bf16[384,1152]{1,0:T(8,128)(2,1)S(1)}) conditional(s32[]{:T(128)} %convert_element_type.43, () %tuple.130, (bf16[256,1536]{1,0:T(8,128)(2,1)S(1)}, bf16[8,48,1152]{2,1,0:T(8,128)(2,1)S(1)}) %tuple.131), branch_computations={%region_0.0_spmd, %region_1.0_spmd} | conditional | bytes 8061032 | solution.py:1049
  49.0 27.8 %all_to_all.14 = bf16[8,48,1152]{2,1,0:T(8,128)(2,1)S(1)} all-to-all(bf16[8,48,1152]{2,1,0:T(8,128)(2,1)S(1)} %get-tuple-element.373), channel_id=1, replica_groups=mesh['dp'=4,'x'=2,'y'=2,'c'=2] {'x','y','c'}, dimensions={0} | all-to-all | bytes 1769472 | tf_op jit(solution)/shard_map/cond/branch_1_fun/all_to_all | solution.py:1053
  77.9 15.5 %conditional.15 = (bf16[128,1536]{1,0:T(8,128)(2,1)}, bf16[128,1536]{1,0:T(8,128)(2,1)}, bf16[256,1536]{1,0:T(8,128)(2,1)}, bf16[256,1536]{1,0:T(8,128)(2,1)}, b...) conditional(s32[]{:T(128)} %convert_element_type.43, () %tuple.129, ...), branch_computations={%region_2.0_spmd, %region_3.0_spmd} | conditional | flops 33891 | bytes 12853795 | solution.py:1049
  78.6 2.0 halves.3
  82.9 3.5 turn.1
  86.4 3.0 multiply_sine_fusion
  89.4 2.1 rotary_rows.1
  95.3 2.4 collective-permute-done.58
  97.7 29.7 %conditional.16 = (bf16[192,1536]{1,0:T(8,128)(2,1)}, bf16[192,1536]{1,0:T(8,128)(2,1)}, bf16[192,1536]{1,0:T(8,128)(2,1)}, bf16[192,1536]{1,0:T(8,128)(2,1)}, b...) conditional(s32[]{:T(128)} %convert_element_type.43, () %tuple.128, ...), branch_computations={%region_4.0_spmd, %region_5.0_spmd} | conditional | flops 2 | bytes 11796592 | solution.py:1049
  101.4 10.9 %norm_project.1 = (bf16[2048,1536]{1,0:T(8,128)(2,1)}, bf16[2048,320]{1,0:T(8,128)(2,1)}) custom-call(bf16[256,1536]{1,0:T(8,128)(2,1)} %get-tuple-element.387.refs_0_, bf16[256,1536]{1,0:T(8,128)(2,1)} %get-tuple-element.388.refs_1_, bf16[256,1536]{1,0:T(8,128)(2,1)} %get-tuple-element.389.refs_2_, bf16[256,1536]{1,0:T(8,128)(2,1)} %get-tuple-element.390.refs_3_, ...), custom_call_target="tpu_custom_call" | custom-call | flops 1 | bytes 1 | tf_op jit(solution)/shard_map/cond/branch_1_fun/norm_project/pallas_call | solution.py:406
  112.3 14.3 %attend_forward.1 = (bf16[2,1,256,192]{3,2,1,0:T(8,128)(2,1)S(1)}, bf16[2,1,256,192]{3,2,1,0:T(8,128)(2,1)S(1)}, bf16[2,1,256,192]{3,2,1,0:T(8,128)(2,1)S(1)}, b...) custom-call(s32[1]{0:T(128)} %get-tuple-element.399.place_ref, bf16[8,1,256,320]{3,2,1,0:T(8,128)(2,1)} %bitcast.1.refs_0_, ...), custom_call_target="tpu_custom_call" | custom-call | flops 1 | bytes 1 | tf_op jit(solution)/shard_map/cond/branch_1_fun/attend_forward/pallas_call | solution.py:230
  128.4 56.0 %conditional.17 = (f32[256,1536]{1,0:T(8,128)}, bf16[256,1536]{1,0:T(8,128)(2,1)}, bf16[256,1536]{1,0:T(8,128)(2,1)}, bf16[256,1536]{1,0:T(8,128)(2,1)}, bf16[25...) conditional(s32[]{:T(128)} %convert_element_type.43, () %tuple.127, ...), branch_computations={%region_6.0_spmd, %region_7.0_spmd} | conditional | flops 2 | bytes 45613956 | solution.py:1049
  131.9 6.6 %collective-permute-done.8.refs_3_ = bf16[512,192]{1,0:T(8,128)(2,1)S(1)} collective-permute-done((bf16[512,192]{1,0:T(8,128)(2,1)S(1)}, bf16[512,192]{1,0:T(8,128)(2,1)S(1)}, u32[]{:S(2)}, u32[]{:S(2)}) %collective-permute-start.8) | collective-permute-done | bytes 196640 | tf_op jit(solution)/shard_map/cond/branch_1_fun/ppermute | solution.py:1013
  138.5 4.2 collective-permute-done.7.refs_2_
  151.9 5.5 %attend_out.1 = (f32[256,1536]{1,0:T(8,128)}, bf16[256,1536]{1,0:T(8,128)(2,1)}) custom-call(bf16[512,192]{1,0:T(8,128)(2,1)S(1)} %bitcast.94, bf16[512,192]{1,0:T(8,128)(2,1)S(1)} %copy-done.1, bf16[512,192]{1,0:T(8,128)(2,1)S(1)} %copy-done.6, bf16[512,192]{1,0:T(8,128)(2,1)S(1)} %copy-done.4, ...), custom_call_target="tpu_custom_call" | custom-call | flops 1 | bytes 1 | tf_op jit(solution)/shard_map/cond/branch_1_fun/attend_out/pallas_call | solution.py:645
  160.1 7.7 %collective-permute-done.17 = bf16[256,1536]{1,0:T(8,128)(2,1)} collective-permute-done((bf16[256,1536]{1,0:T(8,128)(2,1)}, bf16[256,1536]{1,0:T(8,128)(2,1)}, u32[]{:S(2)}, u32[]{:S(2)}) %collective-permute-start.17) | collective-permute-done | bytes 786464 | tf_op jit(solution)/shard_map/cond/branch_1_fun/ppermute | solution.py:987
  168.6 15.2 %collective-permute-done.14 = bf16[256,1536]{1,0:T(8,128)(2,1)} collective-permute-done((bf16[256,1536]{1,0:T(8,128)(2,1)}, bf16[256,1536]{1,0:T(8,128)(2,1)}, u32[]{:S(2)}, u32[]{:S(2)}) %collective-permute-start.14) | collective-permute-done | bytes 786464 | tf_op jit(solution)/shard_map/cond/branch_1_fun/ppermute | solution.py:987
  184.4 22.3 %conditional.18 = (bf16[256,1536]{1,0:T(8,128)(2,1)}, bf16[256,1536]{1,0:T(8,128)(2,1)}, bf16[256,1536]{1,0:T(8,128)(2,1)}, bf16[256,1536]{1,0:T(8,128)(2,1)}, b...) conditional(s32[]{:T(128)} %convert_element_type.43, () %tuple.135, ...), branch_computations={%region_8.0_spmd, %region_9.0_spmd} | conditional | flops 2 | bytes 12583130 | solution.py:1049
  184.4 2.6 halves.4
  189.8 12.0 %feed_forward.4 = (bf16[768,1024]{1,0:T(8,128)(2,1)}, bf16[768,512]{1,0:T(8,128)(2,1)}, bf16[768,1536]{1,0:T(8,128)(2,1)}) custom-call(bf16[256,1536]{1,0:T(8,128)(2,1)} %get-tuple-element.428.refs_0_, bf16[256,1536]{1,0:T(8,128)(2,1)} %get-tuple-element.422.refs_0_.refs_1_, bf16[256,1536]{1,0:T(8,128)(2,1)} %get-tuple-element.423.refs_1_.refs_2_, ...), custom_call_target="tpu_custom_call" | custom-call | flops 1 | bytes 1 | tf_op jit(solution)/shard_map/cond/branch_1_fun/feed_forward/pallas_call | solution.py:462
  201.7 4.0 collective-permute-done.21
  212.6 34.5 %conditional.19 = (bf16[1280,512]{1,0:T(8,128)(2,1)}, bf16[256,1536]{1,0:T(8,128)(2,1)}, bf16[1024,1536]{1,0:T(8,128)(2,1)}, bf16[1536,1536]{1,0:T(8,128)(2,1)},...) conditional(s32[]{:T(128)} %convert_element_type.43, () %tuple.138, (bf16[256,1536]{1,0:T(8,128)(2,1)S(1)}, ...), branch_computations={%region_10.0_spmd, %region_11.0_spmd} | conditional | flops 2 | bytes 17301690 | solution.py:1049
  214.2 17.8 %feed_forward.5 = (bf16[1280,1024]{1,0:T(8,128)(2,1)}, bf16[1280,512]{1,0:T(8,128)(2,1)}, bf16[256,1536]{1,0:T(8,128)(2,1)}, bf16[1024,1536]{1,0:T(8,128)(2,1)}) custom-call(bf16[256,1536]{1,0:T(8,128)(2,1)S(1)} %get-tuple-element.434.refs_0_.refs_3_, bf16[256,1536]{1,0:T(8,128)(2,1)} %get-tuple-element.435.refs_1_.refs_4_, ...), custom_call_target="tpu_custom_call" | custom-call | flops 1 | bytes 1 | tf_op jit(solution)/shard_map/cond/branch_1_fun/feed_forward/pallas_call | solution.py:462
  232.1 15.0 %weight_grads.3 = bf16[1536,1536]{1,0:T(8,128)(2,1)} custom-call(bf16[256,1536]{1,0:T(8,128)(2,1)} %get-tuple-element.448.refs_0_, bf16[256,1536]{1,0:T(8,128)(2,1)} %get-tuple-element.449.refs_1_, bf16[256,1536]{1,0:T(8,128)(2,1)} %get-tuple-element.450.refs_2_, bf16[256,1536]{1,0:T(8,128)(2,1)S(1)} %get-tuple-element.434.refs_0_.refs_3_, ...), custom_call_target="tpu_custom_call" | custom-call | flops 1 | bytes 1 | tf_op jit(solution)/shard_map/cond/branch_1_fun/weight_grads/pallas_call | solution.py:563
  247.3 20.7 %conditional.20 = (bf16[160,1536]{1,0:T(8,128)(2,1)}, bf16[160,1536]{1,0:T(8,128)(2,1)}, bf16[1280,768]{1,0:T(8,128)(2,1)}, bf16[1280,384]{1,0:T(8,128)(2,1)}, b...) conditional(s32[]{:T(128)} %convert_element_type.43, () %tuple.137, (bf16[320,1536]{1,0:T(8,128)(2,1)}, ...), branch_computations={%region_13.0_spmd, %region_14.0_spmd} | conditional | flops 2 | bytes 7864380 | solution.py:1049
  247.3 2.2 halves.5
  251.8 16.1 %feed_forward.6 = (bf16[1280,768]{1,0:T(8,128)(2,1)}, bf16[1280,384]{1,0:T(8,128)(2,1)}, bf16[256,1536]{1,0:T(8,128)(2,1)}, bf16[1024,1536]{1,0:T(8,128)(2,1)}) custom-call(bf16[256,1536]{1,0:T(8,128)(2,1)S(1)} %get-tuple-element.462.refs_0_, bf16[256,1536]{1,0:T(8,128)(2,1)} %get-tuple-element.463.refs_1_, bf16[256,1536]{1,0:T(8,128)(2,1)} %get-tuple-element.464.refs_2_, ...), custom_call_target="tpu_custom_call" | custom-call | flops 1 | bytes 1 | tf_op jit(solution)/shard_map/cond/branch_1_fun/feed_forward/pallas_call | solution.py:462
  268.0 10.2 %feed_forward.7 = (bf16[768,768]{1,0:T(8,128)(2,1)}, bf16[768,384]{1,0:T(8,128)(2,1)S(1)}, bf16[768,1536]{1,0:T(8,128)(2,1)}) custom-call(bf16[256,1536]{1,0:T(8,128)(2,1)} %get-tuple-element.763.refs_0_, bf16[256,1536]{1,0:T(8,128)(2,1)} %get-tuple-element.764.refs_1_, bf16[256,1536]{1,0:T(8,128)(2,1)} %get-tuple-element.765.refs_2_, ...), custom_call_target="tpu_custom_call" | custom-call | flops 1 | bytes 1 | tf_op jit(solution)/shard_map/feed_forward/pallas_call | solution.py:462
  279.9 6.0 %core_sum.3 = (f32[256,1536]{1,0:T(8,128)}, bf16[256,1536]{1,0:T(8,128)(2,1)}, bf16[256,1536]{1,0:T(8,128)(2,1)}, bf16[256,1536]{1,0:T(8,128)(2,1)}) custom-call(bf16[768,1536]{1,0:T(8,128)(2,1)} %get-tuple-element.788.three_ref, bf16[256,1536]{1,0:T(8,128)(2,1)} %get-tuple-element.789.one_ref, bf16[1024,1536]{1,0:T(8,128)(2,1)} %copy-done.36), custom_call_target="tpu_custom_call" | custom-call | flops 1 | bytes 1 | tf_op jit(solution)/shard_map/core_sum/pallas_call | solution.py:763
  285.9 38.3 %conditional.21 = (bf16[256,1536]{1,0:T(8,128)(2,1)}, bf16[256,1536]{1,0:T(8,128)(2,1)}, bf16[256,1536]{1,0:T(8,128)(2,1)}, bf16[1536,1152]{1,0:T(8,128)(2,1)}, ...) conditional(s32[]{:T(128)} %convert_element_type.43, () %tuple.141, ...), branch_computations={%region_15.0_spmd, %region_16.0_spmd} | conditional | flops 2 | bytes 25166140 | solution.py:1049
  286.9 2.5 collective-permute-start.31
  289.5 13.2 %project_back.1 = (bf16[768,1536]{1,0:T(8,128)(2,1)}, bf16[256,1536]{1,0:T(8,128)(2,1)}, bf16[1024,1536]{1,0:T(8,128)(2,1)}) custom-call(bf16[768,512]{1,0:T(8,128)(2,1)} %get-tuple-element.502.refs_0_, bf16[1280,512]{1,0:T(8,128)(2,1)} %get-tuple-element.503.refs_1_, bf16[768,384]{1,0:T(8,128)(2,1)S(1)} %get-tuple-element.500.refs_18_.refs_2_, ...), custom_call_target="tpu_custom_call" | custom-call | flops 1 | bytes 1 | tf_op jit(solution)/shard_map/cond/branch_1_fun/project_back/pallas_call | solution.py:597
  302.7 13.5 %weight_grads.4 = bf16[1536,1152]{1,0:T(8,128)(2,1)} custom-call(bf16[256,1536]{1,0:T(8,128)(2,1)} %get-tuple-element.482.refs_0_, bf16[256,1536]{1,0:T(8,128)(2,1)} %get-tuple-element.483.refs_1_, bf16[256,1536]{1,0:T(8,128)(2,1)} %get-tuple-element.484.refs_2_, bf16[256,1536]{1,0:T(8,128)(2,1)S(1)} %copy-done.17, ...), custom_call_target="tpu_custom_call" | custom-call | flops 1 | bytes 1 | tf_op jit(solution)/shard_map/cond/branch_1_fun/weight_grads/pallas_call | solution.py:563
  316.1 8.1 %collective-permute-done.31 = bf16[256,1536]{1,0:T(8,128)(2,1)} collective-permute-done((bf16[256,1536]{1,0:T(8,128)(2,1)}, bf16[256,1536]{1,0:T(8,128)(2,1)}, u32[]{:S(2)}, u32[]{:S(2)}) %collective-permute-start.31) | collective-permute-done | bytes 786464 | tf_op jit(solution)/shard_map/cond/branch_1_fun/ppermute | solution.py:1013
  325.9 7.3 %middle_back.1 = (f32[256,1536]{1,0:T(8,128)}, bf16[256,1536]{1,0:T(8,128)(2,1)}, bf16[2,256,192]{2,1,0:T(8,128)(2,1)S(1)}, bf16[2,256,192]{2,1,0:T(8,128)(2,1)S...) custom-call(f32[256,1536]{1,0:T(8,128)S(1)} %copy-done.2, ...), custom_call_target="tpu_custom_call" | custom-call | flops 1 | bytes 1 | tf_op jit(solution)/shard_map/middle_back/pallas_call | solution.py:703
  334.5 2.2 collective-permute-start.64
  336.8 5.8 %collective-permute-done.63.refs_2_ = bf16[512,192]{1,0:T(8,128)(2,1)S(1)} collective-permute-done((bf16[512,192]{1,0:T(8,128)(2,1)S(1)}, bf16[512,192]{1,0:T(8,128)(2,1)S(1)}, u32[]{:S(2)}, u32[]{:S(2)}) %collective-permute-start.63) | collective-permute-done | bytes 196640 | tf_op jit(solution)/shard_map/ppermute | solution.py:987
  342.9 4.1 collective-permute-done.64.refs_3_
  348.5 2.1 collective-permute-done.65
  351.5 21.0 %conditional.22 = (bf16[256,1536]{1,0:T(8,128)(2,1)}, bf16[256,1536]{1,0:T(8,128)(2,1)}, bf16[256,1536]{1,0:T(8,128)(2,1)}, bf16[2,1,256,320]{3,2,1,0:T(8,128)(2...) conditional(s32[]{:T(128)} %convert_element_type.43, () %tuple.126, ...), branch_computations={%region_18.0_spmd, %region_19.0_spmd} | conditional | flops 9 | bytes 10617103 | solution.py:1049
  353.9 14.2 %attend_backward.2 = (bf16[2,1,256,320]{3,2,1,0:T(8,128)(2,1)}, bf16[2,1,256,320]{3,2,1,0:T(8,128)(2,1)}, f32[1,8,256]{2,1,0:T(8,128)S(1)}) custom-call(s32[1]{0:T(128)} %get-tuple-element.510.place_ref, bf16[2,2,2,1,256,320]{5,4,3,2,1,0:T(8,128)(2,1)} %bitcast.15.qkv_ref, f32[2,2,2,1,256,128]{5,4,3,2,1,0:T(8,128)} %bitcast.91, ...), custom_call_target="tpu_custom_call" | custom-call | flops 1 | bytes 1 | tf_op jit(solution)/shard_map/cond/branch_1_fun/attend_backward/pallas_call | solution.py:291
  372.5 20.4 %conditional.23 = (bf16[256,1536]{1,0:T(8,128)(2,1)}, bf16[192,1536]{1,0:T(8,128)(2,1)}, bf16[256,1536]{1,0:T(8,128)(2,1)}, bf16[256,1536]{1,0:T(8,128)(2,1)}, b...) conditional(s32[]{:T(128)} %convert_element_type.43, () %tuple.144, ...), branch_computations={%region_20.0_spmd, %region_21.0_spmd} | conditional | flops 1 | bytes 11796697 | solution.py:1049
  374.6 14.1 %attend_backward.3 = (bf16[2,1,256,320]{3,2,1,0:T(8,128)(2,1)}, bf16[2,1,256,320]{3,2,1,0:T(8,128)(2,1)S(1)}, f32[1,8,256]{2,1,0:T(8,128)S(1)}) custom-call(s32[1]{0:T(128)} %get-tuple-element.528.place_ref, bf16[2,2,2,1,256,320]{5,4,3,2,1,0:T(8,128)(2,1)} %bitcast.24.qkv_ref, f32[2,2,2,1,256,128]{5,4,3,2,1,0:T(8,128)} %bitcast.92, ...), custom_call_target="tpu_custom_call" | custom-call | flops 1 | bytes 1 | tf_op jit(solution)/shard_map/cond/branch_1_fun/attend_backward/pallas_call | solution.py:291
  389.8 3.1 collective-permute-done.32
  392.9 2.5 collective-permute-done.66
  395.4 20.7 %conditional.24 = (bf16[512,320]{1,0:T(8,128)(2,1)}, bf16[512,320]{1,0:T(8,128)(2,1)}, bf16[512,320]{1,0:T(8,128)(2,1)}, bf16[1536,640]{1,0:T(8,128)(2,1)S(1)}, ...) conditional(s32[]{:T(128)} %convert_element_type.43, () %tuple.125, ...), branch_computations={%region_22.0_spmd, %region_23.0_spmd} | conditional | flops 2 | bytes 10748230 | solution.py:1049
  399.0 5.4 %core_sum.2 = (f32[256,1536]{1,0:T(8,128)}, bf16[256,1536]{1,0:T(8,128)(2,1)}, bf16[256,1536]{1,0:T(8,128)(2,1)}, bf16[256,1536]{1,0:T(8,128)(2,1)S(1)}) custom-call(bf16[768,1536]{1,0:T(8,128)(2,1)} %get-tuple-element.563.three_ref, bf16[256,1536]{1,0:T(8,128)(2,1)} %get-tuple-element.564.one_ref, bf16[1024,1536]{1,0:T(8,128)(2,1)} %get-tuple-element.565.far_ref), custom_call_target="tpu_custom_call" | custom-call | flops 1 | bytes 1 | tf_op jit(solution)/shard_map/cond/branch_1_fun/core_sum/pallas_call | solution.py:763
  404.4 11.0 %weight_grads.5 = bf16[1536,640]{1,0:T(8,128)(2,1)S(1)} custom-call(bf16[2048,1536]{1,0:T(8,128)(2,1)} %get-tuple-element.545.refs_0_, bf16[512,320]{1,0:T(8,128)(2,1)S(1)} %bitcast.98, bf16[512,320]{1,0:T(8,128)(2,1)} %bitcast.33.refs_2_, bf16[512,320]{1,0:T(8,128)(2,1)} %bitcast.35.refs_3_, bf16[512,320]{1,0:T(8,128)(2,1)S(1)} %bitcast.111, ...), custom_call_target="tpu_custom_call" | custom-call | flops 1 | bytes 1 | tf_op jit(solution)/shard_map/cond/branch_1_fun/weight_grads/pallas_call | solution.py:563
  417.4 16.0 %conditional.25 = (bf16[128,1536]{1,0:T(8,128)(2,1)}, bf16[128,1536]{1,0:T(8,128)(2,1)}, bf16[1024,320]{0,1:T(8,128)(2,1)}, bf16[320,1536]{1,0:T(8,128)(2,1)}) conditional(s32[]{:T(128)} %convert_element_type.43, () %tuple.148, (bf16[256,1536]{1,0:T(8,128)(2,1)S(1)}, bf16[512,320]{1,0:T(8,128)(2,1)S(1)}, bf16[512,320]{1,0:T(8,128)(2,1)}, ...), branch_computations={%region_24.0_spmd, %region_25.0_spmd} | conditional | flops 2 | bytes 8650906 | solution.py:1049
  417.4 2.1 far_parts.4
  422.8 2.4 joined.3
  425.2 7.5 %collective-permute-done.56 = bf16[128,1536]{1,0:T(8,128)(2,1)} collective-permute-done((bf16[128,1536]{1,0:T(8,128)(2,1)S(1)}, bf16[128,1536]{1,0:T(8,128)(2,1)}, u32[]{:S(2)}, u32[]{:S(2)}) %collective-permute-start.56) | collective-permute-done | bytes 393248 | tf_op jit(solution)/shard_map/cond/branch_1_fun/ppermute | solution.py:987
  433.4 2.9 corner_sum.1
  436.3 30.3 %conditional.26 = (bf16[256,1536]{1,0:T(8,128)(2,1)}, bf16[256,1536]{1,0:T(8,128)(2,1)}, bf16[192,1152]{1,0:T(8,128)(2,1)}, f32[1,256,1536]{2,1,0:T(8,128)}) conditional(s32[]{:T(128)} %convert_element_type.43, () %tuple.147, (bf16[256,1536]{1,0:T(8,128)(2,1)}, bf16[256,1536]{1,0:T(8,128)(2,1)}, bf16[384,1152]{1,0:T(8,128)(2,1)}, ...), branch_computations={%region_26.0_spmd, %region_27.0_spmd} | conditional | flops 9 | bytes 27296180 | solution.py:1049
  443.5 8.3 %input_back.1.refs_1_ = f32[256,1536]{1,0:T(8,128)} custom-call(bf16[512,320]{1,0:T(8,128)(2,1)} %copy-done.33, bf16[512,320]{1,0:T(8,128)(2,1)} %get-tuple-element.581.refs_1_, bf16[512,320]{1,0:T(8,128)(2,1)} %get-tuple-element.582.refs_2_, bf16[512,320]{1,0:T(8,128)(2,1)} %get-tuple-element.583.refs_3_, ...), custom_call_target="tpu_custom_call" | custom-call | flops 1 | bytes 1 | tf_op jit(solution)/shard_map/cond/branch_1_fun/input_back/pallas_call | solution.py:735
  452.5 5.6 %collective-permute-done.48 = bf16[256,1536]{1,0:T(8,128)(2,1)} collective-permute-done((bf16[256,1536]{1,0:T(8,128)(2,1)}, bf16[256,1536]{1,0:T(8,128)(2,1)}, u32[]{:S(2)}, u32[]{:S(2)}) %collective-permute-start.48) | collective-permute-done | bytes 786464 | tf_op jit(solution)/shard_map/cond/branch_1_fun/ppermute | solution.py:987
  459.0 7.7 %collective-permute-done.53 = bf16[192,1152]{1,0:T(8,128)(2,1)} collective-permute-done((bf16[192,1152]{1,0:T(8,128)(2,1)}, bf16[192,1152]{1,0:T(8,128)(2,1)}, u32[]{:S(2)}, u32[]{:S(2)}) %collective-permute-start.53) | collective-permute-done | bytes 442400 | tf_op jit(solution)/shard_map/cond/branch_1_fun/ppermute | solution.py:987
  466.7 8.3 %conditional.27 = (bf16[192,640]{1,0:T(8,128)(2,1)}, f32[192,1728]{1,0:T(8,128)}, f32[192,1728]{1,0:T(8,128)}, f32[192,1728]{1,0:T(8,128)}, bf16[1,256,1536]{2,1,0:T(8,128)(2,1)S(1)}) conditional(s32[]{:T(128)} %convert_element_type.43, () %tuple.124, (bf16[384,640]{1,0:T(8,128)(2,1)}, s32[1]{0:T(128)}, bf16[384,1536]{1,0:T(8,128)(2,1)}, ...), branch_computations={%region_29.0_spmd, %region_30.0_spmd} | conditional | flops 2359304 | bytes 15237350 | solution.py:1049
  468.4 2.9 fusion
  471.4 3.6 unpack_columns.2
  475.0 2.4 unpack_columns.3
  (286 shorter events, 92.0 us)
Async XLA Ops:
  7.2 70.7 %all-gather.4.cloned.1.call-start = ((), (), s32[]{:S(2)}) async-start(), calls=%async_computation.6 | async-start | bytes 2457600 | tf_op jit(solution)/shard_map/all_gather | solution.py:1036
  23.2 161.2 %all-gather.8.cloned.1.call-start = ((), (), s32[]{:S(2)}) async-start(), calls=%async_computation.8 | async-start | bytes 5898240 | tf_op jit(solution)/shard_map/all_gather | solution.py:1036
  47.4 199.8 %all-gather.6.cloned.1.call-start = ((), (), s32[]{:S(2)}) async-start(), calls=%async_computation.7 | async-start | bytes 4423680 | tf_op jit(solution)/shard_map/all_gather | solution.py:1036
  47.5 29.4 %collective-permute-start.1 = (bf16[256,1536]{1,0:T(8,128)(2,1)S(1)}, bf16[256,1536]{1,0:T(8,128)(2,1)}, u32[]{:S(2)}, u32[]{:S(2)}) collective-permute-start(bf16[256,1536]{1,0:T(8,128)(2,1)S(1)} %get-tuple-element.372), channel_id=1, source_target_pairs={{0,4},{4,0},{1,5},{5,1},{2,6},{6,2},{3,7},{7,3},{8,12},{12,8},{9,1... | collective-permute-start | bytes 2359304 | tf_op jit(solution)/shard_map/cond/branch_1_fun/ppermute | solution.py:987
  48.3 28.6 %collective-permute-start = (bf16[256,1536]{1,0:T(8,128)(2,1)S(1)}, bf16[256,1536]{1,0:T(8,128)(2,1)}, u32[]{:S(2)}, u32[]{:S(2)}) collective-permute-start(bf16[256,1536]{1,0:T(8,128)(2,1)S(1)} %get-tuple-element.372), channel_id=1, source_target_pairs={{0,2},{2,0},{1,3},{3,1},{4,6},{6,4},{5,7},{7,5},{8,10},{10,8},{9,1... | collective-permute-start | bytes 2359304 | tf_op jit(solution)/shard_map/cond/branch_1_fun/ppermute | solution.py:987
  77.8 272.8 %reduce-scatter.4.cloned.1.call-start = ((), (), s32[]{:S(2)}) async-start(), calls=%async_computation.9 | async-start | bytes 5898240 | tf_op jit(solution)/shard_map/reduce_scatter | solution.py:1040
  77.9 15.5 %collective-permute-start.41 = (bf16[256,1536]{1,0:T(8,128)(2,1)S(1)}, bf16[256,1536]{1,0:T(8,128)(2,1)}, u32[]{:S(2)}, u32[]{:S(2)}) collective-permute-start(bf16[256,1536]{1,0:T(8,128)(2,1)S(1)} %get-tuple-element.378), channel_id=1, source_target_pairs={{0,1},{1,0},{2,3},{3,2},{4,5},{5,4},{6,7},{7,6},{8,9},{9,8},{10,11... | collective-permute-start | bytes 2359304 | tf_op jit(solution)/shard_map/cond/branch_1_fun/ppermute | solution.py:987
  78.0 15.4 %collective-permute-start.42 = (bf16[256,1536]{1,0:T(8,128)(2,1)}, bf16[256,1536]{1,0:T(8,128)(2,1)}, u32[]{:S(2)}, u32[]{:S(2)}) collective-permute-start(bf16[256,1536]{1,0:T(8,128)(2,1)} %get-tuple-element.374.refs_0_), channel_id=1, source_target_pairs={{0,1},{1,0},{2,3},{3,2},{4,5},{5,4},{6,7},{7,6},{8,9},{9,8},{10,11... | collective-permute-start | bytes 2359304 | tf_op jit(solution)/shard_map/cond/branch_1_fun/ppermute | solution.py:987
  78.5 14.9 %collective-permute-start.43 = (bf16[256,1536]{1,0:T(8,128)(2,1)}, bf16[256,1536]{1,0:T(8,128)(2,1)}, u32[]{:S(2)}, u32[]{:S(2)}) collective-permute-start(bf16[256,1536]{1,0:T(8,128)(2,1)} %get-tuple-element.375.refs_1_), channel_id=1, source_target_pairs={{0,1},{1,0},{2,3},{3,2},{4,5},{5,4},{6,7},{7,6},{8,9},{9,8},{10,11... | collective-permute-start | bytes 2359304 | tf_op jit(solution)/shard_map/cond/branch_1_fun/ppermute | solution.py:987
  80.6 11.8 %collective-permute-start.39 = (bf16[128,1536]{1,0:T(8,128)(2,1)}, bf16[128,1536]{1,0:T(8,128)(2,1)}, u32[]{:S(2)}, u32[]{:S(2)}) collective-permute-start(bf16[128,1536]{1,0:T(8,128)(2,1)} %get-tuple-element.376), channel_id=1, source_target_pairs={{0,4},{4,0},{1,5},{5,1},{2,6},{6,2},{3,7},{7,3},{8,12},{12,8},{9,1... | collective-permute-start | bytes 1179656 | tf_op jit(solution)/shard_map/cond/branch_1_fun/ppermute | solution.py:987
  81.9 11.4 %collective-permute-start.40 = (bf16[128,1536]{1,0:T(8,128)(2,1)}, bf16[128,1536]{1,0:T(8,128)(2,1)}, u32[]{:S(2)}, u32[]{:S(2)}) collective-permute-start(bf16[128,1536]{1,0:T(8,128)(2,1)} %get-tuple-element.377), channel_id=1, source_target_pairs={{0,2},{2,0},{1,3},{3,1},{4,6},{6,4},{5,7},{7,5},{8,10},{10,8},{9,1... | collective-permute-start | bytes 1179656 | tf_op jit(solution)/shard_map/cond/branch_1_fun/ppermute | solution.py:987
  97.7 28.9 %collective-permute-start.5 = (bf16[192,1536]{1,0:T(8,128)(2,1)}, bf16[192,1536]{1,0:T(8,128)(2,1)}, u32[]{:S(2)}, u32[]{:S(2)}) collective-permute-start(bf16[192,1536]{1,0:T(8,128)(2,1)} %get-tuple-element.386), channel_id=1, source_target_pairs={{0,1},{1,0},{2,3},{3,2},{4,5},{5,4},{6,7},{7,6},{8,9},{9,8},{10,11... | collective-permute-start | bytes 1769480 | tf_op jit(solution)/shard_map/cond/branch_1_fun/ppermute | solution.py:987
  97.9 28.7 %collective-permute-start.4 = (bf16[192,1536]{1,0:T(8,128)(2,1)}, bf16[192,1536]{1,0:T(8,128)(2,1)}, u32[]{:S(2)}, u32[]{:S(2)}) collective-permute-start(bf16[192,1536]{1,0:T(8,128)(2,1)} %get-tuple-element.386), channel_id=1, source_target_pairs={{0,6},{2,4},{4,2},{6,0},{1,7},{3,5},{5,3},{7,1},{8,14},{10,12},{12... | collective-permute-start | bytes 1769480 | tf_op jit(solution)/shard_map/cond/branch_1_fun/ppermute | solution.py:1013
  98.9 28.0 %collective-permute-start.3 = (bf16[192,1536]{1,0:T(8,128)(2,1)}, bf16[192,1536]{1,0:T(8,128)(2,1)}, u32[]{:S(2)}, u32[]{:S(2)}) collective-permute-start(bf16[192,1536]{1,0:T(8,128)(2,1)} %get-tuple-element.386), channel_id=1, source_target_pairs={{0,4},{4,0},{1,5},{5,1},{2,6},{6,2},{3,7},{7,3},{8,12},{12,8},{9,1... | collective-permute-start | bytes 1769480 | tf_op jit(solution)/shard_map/cond/branch_1_fun/ppermute | solution.py:987
  100.4 27.0 %collective-permute-start.2 = (bf16[192,1536]{1,0:T(8,128)(2,1)}, bf16[192,1536]{1,0:T(8,128)(2,1)}, u32[]{:S(2)}, u32[]{:S(2)}) collective-permute-start(bf16[192,1536]{1,0:T(8,128)(2,1)} %get-tuple-element.386), channel_id=1, source_target_pairs={{0,2},{2,0},{1,3},{3,1},{4,6},{6,4},{5,7},{7,5},{8,10},{10,8},{9,1... | collective-permute-start | bytes 1769480 | tf_op jit(solution)/shard_map/cond/branch_1_fun/ppermute | solution.py:987
  128.4 10.1 %collective-permute-start.8 = (bf16[512,192]{1,0:T(8,128)(2,1)S(1)}, bf16[512,192]{1,0:T(8,128)(2,1)S(1)}, u32[]{:S(2)}, u32[]{:S(2)}) collective-permute-start(bf16[512,192]{1,0:T(8,128)(2,1)S(1)} %bitcast.102), channel_id=1, source_target_pairs={{0,6},{2,4},{4,2},{6,0},{1,7},{3,5},{5,3},{7,1},{8,14},{10,12},{12... | collective-permute-start | bytes 589832 | tf_op jit(solution)/shard_map/cond/branch_1_fun/ppermute | solution.py:1013
  129.4 13.3 %collective-permute-start.7 = (bf16[512,192]{1,0:T(8,128)(2,1)S(1)}, bf16[512,192]{1,0:T(8,128)(2,1)S(1)}, u32[]{:S(2)}, u32[]{:S(2)}) collective-permute-start(bf16[512,192]{1,0:T(8,128)(2,1)S(1)} %bitcast.104), channel_id=1, source_target_pairs={{0,4},{4,0},{1,5},{5,1},{2,6},{6,2},{3,7},{7,3},{8,12},{12,8},{9,1... | collective-permute-start | bytes 589832 | tf_op jit(solution)/shard_map/cond/branch_1_fun/ppermute | solution.py:987
  130.9 12.3 %collective-permute-start.6 = (bf16[512,192]{1,0:T(8,128)(2,1)S(1)}, bf16[512,192]{1,0:T(8,128)(2,1)S(1)}, u32[]{:S(2)}, u32[]{:S(2)}) collective-permute-start(bf16[512,192]{1,0:T(8,128)(2,1)S(1)} %bitcast.106), channel_id=1, source_target_pairs={{0,2},{2,0},{1,3},{3,1},{4,6},{6,4},{5,7},{7,5},{8,10},{10,8},{9,1... | collective-permute-start | bytes 589832 | tf_op jit(solution)/shard_map/cond/branch_1_fun/ppermute | solution.py:987
  131.9 16.9 %collective-permute-start.12 = (bf16[192,1536]{1,0:T(8,128)(2,1)}, bf16[192,1536]{1,0:T(8,128)(2,1)}, u32[]{:S(2)}, u32[]{:S(2)}) collective-permute-start(bf16[192,1536]{1,0:T(8,128)(2,1)} %get-tuple-element.415.refs_11_), channel_id=1, source_target_pairs={{0,1},{1,0},{2,3},{3,2},{4,5},{5,4},{6,7},{7,6},{8,9},{9,8},{10,11... | collective-permute-start | bytes 1769480 | tf_op jit(solution)/shard_map/cond/branch_1_fun/ppermute | solution.py:987
  145.8 13.3 %collective-permute-start.18 = (bf16[256,1536]{1,0:T(8,128)(2,1)S(1)}, bf16[256,1536]{1,0:T(8,128)(2,1)}, u32[]{:S(2)}, u32[]{:S(2)}) collective-permute-start(bf16[256,1536]{1,0:T(8,128)(2,1)S(1)} %get-tuple-element.421), channel_id=1, source_target_pairs={{0,1},{1,0},{2,3},{3,2},{4,5},{5,4},{6,7},{7,6},{8,9},{9,8},{10,11... | collective-permute-start | bytes 2359304 | tf_op jit(solution)/shard_map/cond/branch_1_fun/ppermute | solution.py:987
  147.1 20.7 %collective-permute-start.17 = (bf16[256,1536]{1,0:T(8,128)(2,1)}, bf16[256,1536]{1,0:T(8,128)(2,1)}, u32[]{:S(2)}, u32[]{:S(2)}) collective-permute-start(bf16[256,1536]{1,0:T(8,128)(2,1)} %after.6), channel_id=1, source_target_pairs={{0,4},{4,0},{1,5},{5,1},{2,6},{6,2},{3,7},{7,3},{8,12},{12,8},{9,1... | collective-permute-start | bytes 2359304 | tf_op jit(solution)/shard_map/cond/branch_1_fun/ppermute | solution.py:987
  147.9 20.7 %collective-permute-start.16 = (bf16[256,1536]{1,0:T(8,128)(2,1)}, bf16[256,1536]{1,0:T(8,128)(2,1)}, u32[]{:S(2)}, u32[]{:S(2)}) collective-permute-start(bf16[256,1536]{1,0:T(8,128)(2,1)} %after.6), channel_id=1, source_target_pairs={{0,2},{2,0},{1,3},{3,1},{4,6},{6,4},{5,7},{7,5},{8,10},{10,8},{9,1... | collective-permute-start | bytes 2359304 | tf_op jit(solution)/shard_map/cond/branch_1_fun/ppermute | solution.py:987
  157.5 11.2 %collective-permute-start.15 = (bf16[256,1536]{1,0:T(8,128)(2,1)}, bf16[256,1536]{1,0:T(8,128)(2,1)}, u32[]{:S(2)}, u32[]{:S(2)}) collective-permute-start(bf16[256,1536]{1,0:T(8,128)(2,1)} %get-tuple-element.1220), channel_id=1, source_target_pairs={{0,1},{1,0},{2,3},{3,2},{4,5},{5,4},{6,7},{7,6},{8,9},{9,8},{10,11... | collective-permute-start | bytes 2359304 | tf_op jit(solution)/shard_map/cond/branch_1_fun/ppermute | solution.py:987
  157.6 26.3 %collective-permute-start.14 = (bf16[256,1536]{1,0:T(8,128)(2,1)}, bf16[256,1536]{1,0:T(8,128)(2,1)}, u32[]{:S(2)}, u32[]{:S(2)}) collective-permute-start(bf16[256,1536]{1,0:T(8,128)(2,1)} %get-tuple-element.1220), channel_id=1, source_target_pairs={{0,4},{4,0},{1,5},{5,1},{2,6},{6,2},{3,7},{7,3},{8,12},{12,8},{9,1... | collective-permute-start | bytes 2359304 | tf_op jit(solution)/shard_map/cond/branch_1_fun/ppermute | solution.py:987
  159.1 25.2 %collective-permute-start.13 = (bf16[256,1536]{1,0:T(8,128)(2,1)}, bf16[256,1536]{1,0:T(8,128)(2,1)}, u32[]{:S(2)}, u32[]{:S(2)}) collective-permute-start(bf16[256,1536]{1,0:T(8,128)(2,1)} %get-tuple-element.1220), channel_id=1, source_target_pairs={{0,2},{2,0},{1,3},{3,1},{4,6},{6,4},{5,7},{7,5},{8,10},{10,8},{9,1... | collective-permute-start | bytes 2359304 | tf_op jit(solution)/shard_map/cond/branch_1_fun/ppermute | solution.py:987
  167.9 16.5 %collective-permute-start.20 = (bf16[256,1536]{1,0:T(8,128)(2,1)}, bf16[256,1536]{1,0:T(8,128)(2,1)}, u32[]{:S(2)}, u32[]{:S(2)}) collective-permute-start(bf16[256,1536]{1,0:T(8,128)(2,1)} %collective-permute-done.17), channel_id=1, source_target_pairs={{0,1},{1,0},{2,3},{3,2},{4,5},{5,4},{6,7},{7,6},{8,9},{9,8},{10,11... | collective-permute-start | bytes 2359304 | tf_op jit(solution)/shard_map/cond/branch_1_fun/ppermute | solution.py:987
  168.6 15.7 %collective-permute-start.19 = (bf16[256,1536]{1,0:T(8,128)(2,1)}, bf16[256,1536]{1,0:T(8,128)(2,1)}, u32[]{:S(2)}, u32[]{:S(2)}) collective-permute-start(bf16[256,1536]{1,0:T(8,128)(2,1)} %collective-permute-done.16), channel_id=1, source_target_pairs={{0,1},{1,0},{2,3},{3,2},{4,5},{5,4},{6,7},{7,6},{8,9},{9,8},{10,11... | collective-permute-start | bytes 2359304 | tf_op jit(solution)/shard_map/cond/branch_1_fun/ppermute | solution.py:987
  186.9 18.7 %collective-permute-start.21 = (bf16[256,1536]{1,0:T(8,128)(2,1)}, bf16[256,1536]{1,0:T(8,128)(2,1)}, u32[]{:S(2)}, u32[]{:S(2)}) collective-permute-start(bf16[256,1536]{1,0:T(8,128)(2,1)} %get-tuple-element.426), channel_id=1, source_target_pairs={{0,4},{4,0},{1,5},{5,1},{2,6},{6,2},{3,7},{7,3},{8,12},{12,8},{9,1... | collective-permute-start | bytes 2359304 | tf_op jit(solution)/shard_map/cond/branch_1_fun/ppermute | solution.py:987
  188.2 18.5 %collective-permute-start.22 = (bf16[256,1536]{1,0:T(8,128)(2,1)}, bf16[256,1536]{1,0:T(8,128)(2,1)}, u32[]{:S(2)}, u32[]{:S(2)}) collective-permute-start(bf16[256,1536]{1,0:T(8,128)(2,1)} %get-tuple-element.427), channel_id=1, source_target_pairs={{0,2},{2,0},{1,3},{3,1},{4,6},{6,4},{5,7},{7,5},{8,10},{10,8},{9,1... | collective-permute-start | bytes 2359304 | tf_op jit(solution)/shard_map/cond/branch_1_fun/ppermute | solution.py:987
  189.2 17.4 %collective-permute-start.23 = (bf16[256,1536]{1,0:T(8,128)(2,1)}, bf16[256,1536]{1,0:T(8,128)(2,1)}, u32[]{:S(2)}, u32[]{:S(2)}) collective-permute-start(bf16[256,1536]{1,0:T(8,128)(2,1)} %get-tuple-element.422.refs_0_.refs_1_), channel_id=1, source_target_pairs={{0,1},{1,0},{2,3},{3,2},{4,5},{5,4},{6,7},{7,6},{8,9},{9,8},{10,11... | collective-permute-start | bytes 2359304 | tf_op jit(solution)/shard_map/cond/branch_1_fun/ppermute | solution.py:987
  189.2 17.4 %collective-permute-start.24 = (bf16[256,1536]{1,0:T(8,128)(2,1)}, bf16[256,1536]{1,0:T(8,128)(2,1)}, u32[]{:S(2)}, u32[]{:S(2)}) collective-permute-start(bf16[256,1536]{1,0:T(8,128)(2,1)} %get-tuple-element.423.refs_1_.refs_2_), channel_id=1, source_target_pairs={{0,1},{1,0},{2,3},{3,2},{4,5},{5,4},{6,7},{7,6},{8,9},{9,8},{10,11... | collective-permute-start | bytes 2359304 | tf_op jit(solution)/shard_map/cond/branch_1_fun/ppermute | solution.py:987
  212.6 34.5 %collective-permute-start.26 = (bf16[320,1536]{1,0:T(8,128)(2,1)}, bf16[320,1536]{1,0:T(8,128)(2,1)}, u32[]{:S(2)}, u32[]{:S(2)}) collective-permute-start(bf16[320,1536]{1,0:T(8,128)(2,1)} %get-tuple-element.457), channel_id=1, source_target_pairs={{0,4},{4,0},{1,5},{5,1},{2,6},{6,2},{3,7},{7,3},{8,12},{12,8},{9,1... | collective-permute-start | bytes 2949128 | tf_op jit(solution)/shard_map/cond/branch_1_fun/ppermute | solution.py:987
  213.3 33.8 %collective-permute-start.25 = (bf16[320,1536]{1,0:T(8,128)(2,1)}, bf16[320,1536]{1,0:T(8,128)(2,1)}, u32[]{:S(2)}, u32[]{:S(2)}) collective-permute-start(bf16[320,1536]{1,0:T(8,128)(2,1)} %get-tuple-element.457), channel_id=1, source_target_pairs={{0,2},{2,0},{1,3},{3,1},{4,6},{6,4},{5,7},{7,5},{8,10},{10,8},{9,1... | collective-permute-start | bytes 2949128 | tf_op jit(solution)/shard_map/cond/branch_1_fun/ppermute | solution.py:987
  247.1 168.9 %reduce-scatter.6.cloned.1.call-start = ((), (), s32[]{:S(2)}) async-start(), calls=%async_computation.10 | async-start | bytes 4423680 | tf_op jit(solution)/shard_map/reduce_scatter | solution.py:1040
  249.4 18.5 %collective-permute-start.27 = (bf16[160,1536]{1,0:T(8,128)(2,1)}, bf16[160,1536]{1,0:T(8,128)(2,1)}, u32[]{:S(2)}, u32[]{:S(2)}) collective-permute-start(bf16[160,1536]{1,0:T(8,128)(2,1)} %get-tuple-element.460), channel_id=1, source_target_pairs={{0,4},{4,0},{1,5},{5,1},{2,6},{6,2},{3,7},{7,3},{8,12},{12,8},{9,1... | collective-permute-start | bytes 1474568 | tf_op jit(solution)/shard_map/cond/branch_1_fun/ppermute | solution.py:987
  250.8 17.1 %collective-permute-start.28 = (bf16[160,1536]{1,0:T(8,128)(2,1)}, bf16[160,1536]{1,0:T(8,128)(2,1)}, u32[]{:S(2)}, u32[]{:S(2)}) collective-permute-start(bf16[160,1536]{1,0:T(8,128)(2,1)} %get-tuple-element.461), channel_id=1, source_target_pairs={{0,2},{2,0},{1,3},{3,1},{4,6},{6,4},{5,7},{7,5},{8,10},{10,8},{9,1... | collective-permute-start | bytes 1474568 | tf_op jit(solution)/shard_map/cond/branch_1_fun/ppermute | solution.py:987
  268.0 10.3 %collective-permute-start.61 = (bf16[1024,1536]{1,0:T(8,128)(2,1)}, bf16[1024,1536]{1,0:T(8,128)(2,1)S(1)}, u32[]{:S(2)}, u32[]{:S(2)}) collective-permute-start(bf16[1024,1536]{1,0:T(8,128)(2,1)} %get-tuple-element.787.refs_8_), channel_id=1, source_target_pairs={{0,1},{1,0},{2,3},{3,2},{4,5},{5,4},{6,7},{7,6},{8,9},{9,8},{10,11... | collective-permute-start | bytes 9437192 | tf_op jit(solution)/shard_map/ppermute | solution.py:987
  285.9 30.2 %collective-permute-start.29 = (bf16[256,1536]{1,0:T(8,128)(2,1)}, bf16[256,1536]{1,0:T(8,128)(2,1)}, u32[]{:S(2)}, u32[]{:S(2)}) collective-permute-start(bf16[256,1536]{1,0:T(8,128)(2,1)} %get-tuple-element.479), channel_id=1, source_target_pairs={{0,2},{2,0},{1,3},{3,1},{4,6},{6,4},{5,7},{7,5},{8,10},{10,8},{9,1... | collective-permute-start | bytes 2359304 | tf_op jit(solution)/shard_map/cond/branch_1_fun/ppermute | solution.py:987
  286.9 29.2 %collective-permute-start.30 = (bf16[256,1536]{1,0:T(8,128)(2,1)}, bf16[256,1536]{1,0:T(8,128)(2,1)}, u32[]{:S(2)}, u32[]{:S(2)}) collective-permute-start(bf16[256,1536]{1,0:T(8,128)(2,1)} %get-tuple-element.480), channel_id=1, source_target_pairs={{0,4},{4,0},{1,5},{5,1},{2,6},{6,2},{3,7},{7,3},{8,12},{12,8},{9,1... | collective-permute-start | bytes 2359304 | tf_op jit(solution)/shard_map/cond/branch_1_fun/ppermute | solution.py:987
  286.9 37.3 %collective-permute-start.31 = (bf16[256,1536]{1,0:T(8,128)(2,1)}, bf16[256,1536]{1,0:T(8,128)(2,1)}, u32[]{:S(2)}, u32[]{:S(2)}) collective-permute-start(bf16[256,1536]{1,0:T(8,128)(2,1)} %get-tuple-element.481), channel_id=1, source_target_pairs={{0,6},{2,4},{4,2},{6,0},{1,7},{3,5},{5,3},{7,1},{8,14},{10,12},{12... | collective-permute-start | bytes 2359304 | tf_op jit(solution)/shard_map/cond/branch_1_fun/ppermute | solution.py:1013
  324.3 142.4 %reduce-scatter.8.cloned.1.call-start = ((), (), s32[]{:S(2)}) async-start(), calls=%async_computation.11 | async-start | bytes 2457600 | tf_op jit(solution)/shard_map/reduce_scatter | solution.py:1040
  324.7 68.2 %collective-permute-start.67 = (bf16[1024,1536]{1,0:T(8,128)(2,1)}, bf16[1024,1536]{1,0:T(8,128)(2,1)}, u32[]{:S(2)}, u32[]{:S(2)}) collective-permute-start(bf16[1024,1536]{1,0:T(8,128)(2,1)} %get-tuple-element.831), channel_id=1, source_target_pairs={{0,1},{1,0},{2,3},{3,2},{4,5},{5,4},{6,7},{7,6},{8,9},{9,8},{10,11... | collective-permute-start | bytes 9437192 | tf_op jit(solution)/shard_map/ppermute | solution.py:987
  333.2 9.3 %collective-permute-start.63 = (bf16[512,192]{1,0:T(8,128)(2,1)S(1)}, bf16[512,192]{1,0:T(8,128)(2,1)S(1)}, u32[]{:S(2)}, u32[]{:S(2)}) collective-permute-start(bf16[512,192]{1,0:T(8,128)(2,1)S(1)} %bitcast.77), channel_id=1, source_target_pairs={{0,4},{4,0},{1,5},{5,1},{2,6},{6,2},{3,7},{7,3},{8,12},{12,8},{9,1... | collective-permute-start | bytes 589832 | tf_op jit(solution)/shard_map/ppermute | solution.py:987
  333.9 9.0 %collective-permute-start.62 = (bf16[512,192]{1,0:T(8,128)(2,1)S(1)}, bf16[512,192]{1,0:T(8,128)(2,1)S(1)}, u32[]{:S(2)}, u32[]{:S(2)}) collective-permute-start(bf16[512,192]{1,0:T(8,128)(2,1)S(1)} %bitcast.76), channel_id=1, source_target_pairs={{0,2},{2,0},{1,3},{3,1},{4,6},{6,4},{5,7},{7,5},{8,10},{10,8},{9,1... | collective-permute-start | bytes 589832 | tf_op jit(solution)/shard_map/ppermute | solution.py:987
  334.5 12.5 %collective-permute-start.64 = (bf16[512,192]{1,0:T(8,128)(2,1)S(1)}, bf16[512,192]{1,0:T(8,128)(2,1)S(1)}, u32[]{:S(2)}, u32[]{:S(2)}) collective-permute-start(bf16[512,192]{1,0:T(8,128)(2,1)S(1)} %bitcast.75), channel_id=1, source_target_pairs={{0,6},{2,4},{4,2},{6,0},{1,7},{3,5},{5,3},{7,1},{8,14},{10,12},{12... | collective-permute-start | bytes 589832 | tf_op jit(solution)/shard_map/ppermute | solution.py:1013
  351.5 20.0 %collective-permute-start.45 = (bf16[256,1536]{1,0:T(8,128)(2,1)}, bf16[256,1536]{1,0:T(8,128)(2,1)}, u32[]{:S(2)}, u32[]{:S(2)}) collective-permute-start(bf16[256,1536]{1,0:T(8,128)(2,1)} %get-tuple-element.509), channel_id=1, source_target_pairs={{0,4},{4,0},{1,5},{5,1},{2,6},{6,2},{3,7},{7,3},{8,12},{12,8},{9,1... | collective-permute-start | bytes 2359304 | tf_op jit(solution)/shard_map/cond/branch_1_fun/ppermute | solution.py:987
  352.9 19.6 %collective-permute-start.44 = (bf16[256,1536]{1,0:T(8,128)(2,1)}, bf16[256,1536]{1,0:T(8,128)(2,1)}, u32[]{:S(2)}, u32[]{:S(2)}) collective-permute-start(bf16[256,1536]{1,0:T(8,128)(2,1)} %get-tuple-element.509), channel_id=1, source_target_pairs={{0,2},{2,0},{1,3},{3,1},{4,6},{6,4},{5,7},{7,5},{8,10},{10,8},{9,1... | collective-permute-start | bytes 2359304 | tf_op jit(solution)/shard_map/cond/branch_1_fun/ppermute | solution.py:987
  353.9 18.6 %collective-permute-start.46 = (bf16[256,1536]{1,0:T(8,128)(2,1)}, bf16[256,1536]{1,0:T(8,128)(2,1)}, u32[]{:S(2)}, u32[]{:S(2)}) collective-permute-start(bf16[256,1536]{1,0:T(8,128)(2,1)} %get-tuple-element.509), channel_id=1, source_target_pairs={{0,1},{1,0},{2,3},{3,2},{4,5},{5,4},{6,7},{7,6},{8,9},{9,8},{10,11... | collective-permute-start | bytes 2359304 | tf_op jit(solution)/shard_map/cond/branch_1_fun/ppermute | solution.py:987
  372.5 17.2 %collective-permute-start.34 = (bf16[256,1536]{1,0:T(8,128)(2,1)}, bf16[256,1536]{1,0:T(8,128)(2,1)}, u32[]{:S(2)}, u32[]{:S(2)}) collective-permute-start(bf16[256,1536]{1,0:T(8,128)(2,1)} %get-tuple-element.527), channel_id=1, source_target_pairs={{0,1},{1,0},{2,3},{3,2},{4,5},{5,4},{6,7},{7,6},{8,9},{9,8},{10,11... | collective-permute-start | bytes 2359304 | tf_op jit(solution)/shard_map/cond/branch_1_fun/ppermute | solution.py:987
  372.6 20.3 %collective-permute-start.32 = (bf16[256,1536]{1,0:T(8,128)(2,1)}, bf16[256,1536]{1,0:T(8,128)(2,1)}, u32[]{:S(2)}, u32[]{:S(2)}) collective-permute-start(bf16[256,1536]{1,0:T(8,128)(2,1)} %get-tuple-element.525), channel_id=1, source_target_pairs={{0,2},{2,0},{1,3},{3,1},{4,6},{6,4},{5,7},{7,5},{8,10},{10,8},{9,1... | collective-permute-start | bytes 2359304 | tf_op jit(solution)/shard_map/cond/branch_1_fun/ppermute | solution.py:987
  373.7 19.2 %collective-permute-start.35 = (bf16[256,1536]{1,0:T(8,128)(2,1)}, bf16[256,1536]{1,0:T(8,128)(2,1)}, u32[]{:S(2)}, u32[]{:S(2)}) collective-permute-start(bf16[256,1536]{1,0:T(8,128)(2,1)} %get-tuple-element.525), channel_id=1, source_target_pairs={{0,1},{1,0},{2,3},{3,2},{4,5},{5,4},{6,7},{7,6},{8,9},{9,8},{10,11... | collective-permute-start | bytes 2359304 | tf_op jit(solution)/shard_map/cond/branch_1_fun/ppermute | solution.py:987
  373.9 15.9 %collective-permute-start.33 = (bf16[192,1536]{1,0:T(8,128)(2,1)}, bf16[192,1536]{1,0:T(8,128)(2,1)}, u32[]{:S(2)}, u32[]{:S(2)}) collective-permute-start(bf16[192,1536]{1,0:T(8,128)(2,1)} %get-tuple-element.526), channel_id=1, source_target_pairs={{0,4},{4,0},{1,5},{5,1},{2,6},{6,2},{3,7},{7,3},{8,12},{12,8},{9,1... | collective-permute-start | bytes 1769480 | tf_op jit(solution)/shard_map/cond/branch_1_fun/ppermute | solution.py:987
  395.4 20.1 %collective-permute-start.38 = (bf16[512,320]{1,0:T(8,128)(2,1)S(1)}, bf16[512,320]{1,0:T(8,128)(2,1)}, u32[]{:S(2)}, u32[]{:S(2)}) collective-permute-start(bf16[512,320]{1,0:T(8,128)(2,1)S(1)} %bitcast.110), channel_id=1, source_target_pairs={{0,6},{2,4},{4,2},{6,0},{1,7},{3,5},{5,3},{7,1},{8,14},{10,12},{12... | collective-permute-start | bytes 983048 | tf_op jit(solution)/shard_map/cond/branch_1_fun/ppermute | solution.py:1013
  396.6 19.0 %collective-permute-start.37 = (bf16[512,320]{1,0:T(8,128)(2,1)}, bf16[512,320]{1,0:T(8,128)(2,1)}, u32[]{:S(2)}, u32[]{:S(2)}) collective-permute-start(bf16[512,320]{1,0:T(8,128)(2,1)} %bitcast.35.refs_3_), channel_id=1, source_target_pairs={{0,4},{4,0},{1,5},{5,1},{2,6},{6,2},{3,7},{7,3},{8,12},{12,8},{9,1... | collective-permute-start | bytes 983048 | tf_op jit(solution)/shard_map/cond/branch_1_fun/ppermute | solution.py:987
  397.9 18.1 %collective-permute-start.36 = (bf16[512,320]{1,0:T(8,128)(2,1)}, bf16[512,320]{1,0:T(8,128)(2,1)}, u32[]{:S(2)}, u32[]{:S(2)}) collective-permute-start(bf16[512,320]{1,0:T(8,128)(2,1)} %bitcast.33.refs_2_), channel_id=1, source_target_pairs={{0,2},{2,0},{1,3},{3,1},{4,6},{6,4},{5,7},{7,5},{8,10},{10,8},{9,1... | collective-permute-start | bytes 983048 | tf_op jit(solution)/shard_map/cond/branch_1_fun/ppermute | solution.py:987
  420.9 12.5 %collective-permute-start.57 = (bf16[1024,320]{0,1:T(8,128)(2,1)S(1)}, bf16[1024,320]{0,1:T(8,128)(2,1)}, u32[]{:S(2)}, u32[]{:S(2)}) collective-permute-start(bf16[1024,320]{0,1:T(8,128)(2,1)S(1)} %copy.81), channel_id=1, source_target_pairs={{0,1},{1,0},{2,3},{3,2},{4,5},{5,4},{6,7},{7,6},{8,9},{9,8},{10,11... | collective-permute-start | bytes 1966088 | tf_op jit(solution)/shard_map/cond/branch_1_fun/ppermute | solution.py:987
  421.0 11.7 %collective-permute-start.56 = (bf16[128,1536]{1,0:T(8,128)(2,1)S(1)}, bf16[128,1536]{1,0:T(8,128)(2,1)}, u32[]{:S(2)}, u32[]{:S(2)}) collective-permute-start(bf16[128,1536]{1,0:T(8,128)(2,1)S(1)} %get-tuple-element.1149), channel_id=1, source_target_pairs={{0,2},{2,0},{1,3},{3,1},{4,6},{6,4},{5,7},{7,5},{8,10},{10,8},{9,1... | collective-permute-start | bytes 1179656 | tf_op jit(solution)/shard_map/cond/branch_1_fun/ppermute | solution.py:987
  422.1 11.3 %collective-permute-start.55 = (bf16[128,1536]{1,0:T(8,128)(2,1)S(1)}, bf16[128,1536]{1,0:T(8,128)(2,1)}, u32[]{:S(2)}, u32[]{:S(2)}) collective-permute-start(bf16[128,1536]{1,0:T(8,128)(2,1)S(1)} %get-tuple-element.1150), channel_id=1, source_target_pairs={{0,4},{4,0},{1,5},{5,1},{2,6},{6,2},{3,7},{7,3},{8,12},{12,8},{9,1... | collective-permute-start | bytes 1179656 | tf_op jit(solution)/shard_map/cond/branch_1_fun/ppermute | solution.py:987
  436.4 7.1 %collective-permute-start.51 = (bf16[320,1536]{1,0:T(8,128)(2,1)}, bf16[320,1536]{1,0:T(8,128)(2,1)S(1)}, u32[]{:S(2)}, u32[]{:S(2)}) collective-permute-start(bf16[320,1536]{1,0:T(8,128)(2,1)} %get-tuple-element.587.refs_10_), channel_id=1, source_target_pairs={{0,1},{1,0},{2,3},{3,2},{4,5},{5,4},{6,7},{7,6},{8,9},{9,8},{10,11... | collective-permute-start | bytes 2949128 | tf_op jit(solution)/shard_map/cond/branch_1_fun/ppermute | solution.py:987
  436.9 6.6 %collective-permute-start.50 = (bf16[320,1536]{1,0:T(8,128)(2,1)}, bf16[320,1536]{1,0:T(8,128)(2,1)}, u32[]{:S(2)}, u32[]{:S(2)}) collective-permute-start(bf16[320,1536]{1,0:T(8,128)(2,1)} %get-tuple-element.586.refs_9_), channel_id=1, source_target_pairs={{0,1},{1,0},{2,3},{3,2},{4,5},{5,4},{6,7},{7,6},{8,9},{9,8},{10,11... | collective-permute-start | bytes 2949128 | tf_op jit(solution)/shard_map/cond/branch_1_fun/ppermute | solution.py:987
  437.4 20.7 %collective-permute-start.48 = (bf16[256,1536]{1,0:T(8,128)(2,1)}, bf16[256,1536]{1,0:T(8,128)(2,1)}, u32[]{:S(2)}, u32[]{:S(2)}) collective-permute-start(bf16[256,1536]{1,0:T(8,128)(2,1)} %get-tuple-element.578), channel_id=1, source_target_pairs={{0,4},{4,0},{1,5},{5,1},{2,6},{6,2},{3,7},{7,3},{8,12},{12,8},{9,1... | collective-permute-start | bytes 2359304 | tf_op jit(solution)/shard_map/cond/branch_1_fun/ppermute | solution.py:987
  439.1 19.9 %collective-permute-start.47 = (bf16[256,1536]{1,0:T(8,128)(2,1)}, bf16[256,1536]{1,0:T(8,128)(2,1)}, u32[]{:S(2)}, u32[]{:S(2)}) collective-permute-start(bf16[256,1536]{1,0:T(8,128)(2,1)} %get-tuple-element.577), channel_id=1, source_target_pairs={{0,2},{2,0},{1,3},{3,1},{4,6},{6,4},{5,7},{7,5},{8,10},{10,8},{9,1... | collective-permute-start | bytes 2359304 | tf_op jit(solution)/shard_map/cond/branch_1_fun/ppermute | solution.py:987
  451.8 14.9 %collective-permute-start.53 = (bf16[192,1152]{1,0:T(8,128)(2,1)}, bf16[192,1152]{1,0:T(8,128)(2,1)}, u32[]{:S(2)}, u32[]{:S(2)}) collective-permute-start(bf16[192,1152]{1,0:T(8,128)(2,1)} %after.7), channel_id=1, source_target_pairs={{0,4},{4,0},{1,5},{5,1},{2,6},{6,2},{3,7},{7,3},{8,12},{12,8},{9,1... | collective-permute-start | bytes 1327112 | tf_op jit(solution)/shard_map/cond/branch_1_fun/ppermute | solution.py:987
  467.7 7.3 %collective-permute-start.54 = (bf16[192,640]{1,0:T(8,128)(2,1)S(1)}, bf16[192,640]{1,0:T(8,128)(2,1)}, u32[]{:S(2)}, u32[]{:S(2)}) collective-permute-start(bf16[192,640]{1,0:T(8,128)(2,1)S(1)} %constant_dynamic-slice_fusion.2), channel_id=1, source_target_pairs={{0,4},{4,0},{1,5},{5,1},{2,6},{6,2},{3,7},{7,3},{8,12},{12,8},{9,1... | collective-permute-start | bytes 737288 | tf_op jit(solution)/shard_map/cond/branch_1_fun/ppermute | solution.py:987
  (72 other events, 638.0 us)
Sparse Core Ops, SparseCore 0:
  23.3 43.9 all-gather.3
  68.9 88.2 all-gather.7
  159.4 68.4 all-gather.5
  247.3 86.1 reduce-scatter.3
  335.7 66.8 reduce-scatter.5
  417.5 41.5 reduce-scatter.7

commit v6 on v5

--- a/solution.py
+++ b/solution.py
@@ -91,6 +91,28 @@
     return (4 * core + pair, 0), pair, core
 
 
+def packed(values):
+    rows, width = values.shape
+    quarter = rows // 4
+    lines = []
+    for first in range(0, width, HEAD_DIM):
+        head = values[:, first : first + HEAD_DIM]
+        lines.append(
+            jnp.concatenate([head[q * quarter : (q + 1) * quarter] for q in range(4)], axis=1)
+        )
+    return jnp.concatenate(lines, axis=0)
+
+
+def unpacked(values, heads):
+    quarter = values.shape[0] // heads
+    columns = []
+    for head in range(heads):
+        line = values[head * quarter : (head + 1) * quarter]
+        parts = [line[:, q * HEAD_DIM : (q + 1) * HEAD_DIM] for q in range(4)]
+        columns.append(jnp.concatenate(parts, axis=0))
+    return jnp.concatenate(columns, axis=1)
+
+
 def store_pair(refs, pair, core, values):
     for k, ref in enumerate(refs):
 
@@ -107,7 +129,7 @@
 
 
 def attend_forward(place_ref, qkv_ref, gain_ref, cos_ref, sin_ref, *refs):
-    *mixed_refs, stat_ref, keys, values = refs
+    mixed_refs, packed_refs, (stat_ref, keys, values) = refs[:4], refs[4:8], refs[8:]
     place = place_ref[0]
     tokens = qkv_ref.shape[2]
     gain = gain_ref[...]
@@ -138,7 +160,9 @@
             rows_total = total[:, HEAD_DIM : HEAD_DIM + 1]
             outs.append(total[:, :HEAD_DIM] / rows_total)
             stats = jnp.where(lane == head, jnp.log(rows_total), stats)
-        store_pair(mixed_refs, pair, core, jnp.concatenate(outs, axis=1).astype(BF16))
+        mixed = jnp.concatenate(outs, axis=1)
+        store_pair(mixed_refs, pair, core, mixed.astype(BF16))
+        store_pair(packed_refs, pair, core, packed(mixed).astype(BF16))
         stat_ref[source] = stats
 
 
@@ -150,8 +174,9 @@
 
 def attend_backward(place_ref, qkv_ref, stat_ref, far_ref, *refs):
     near_refs, mixed_refs = refs[:2], refs[2:4]
-    gain_ref, cos_ref, sin_ref, *out_refs = refs[4:9]
-    gain_grad_ref, keys, values, key_grads, value_grads, query_grads = refs[9:]
+    gain_ref, cos_ref, sin_ref = refs[4:7]
+    out_refs, packed_refs = refs[7:9], refs[9:11]
+    gain_grad_ref, keys, values, key_grads, value_grads, query_grads = refs[11:]
     place = place_ref[0]
     tokens = qkv_ref.shape[4]
     gain = gain_ref[...]
@@ -169,7 +194,7 @@
         keys[here] = with_ones(turned[:, GROUP * HEAD_DIM :].astype(BF16), 3)
         values[here] = with_ones(raw[:, QK:], 3)
         near = jnp.where(pair == 0, near_refs[0][0, 0], near_refs[1][0, 0])
-        grads = jnp.where(core == 0, near, far_ref[pair, 0]).astype(F32)
+        grads = unpacked(jnp.where(core == 0, near, far_ref[pair, 0]).astype(F32), GROUP)
         product = load_pair(mixed_refs, pair, core).astype(F32) * grads
         stats = stat_ref[source]
         for head in range(GROUP):
@@ -207,6 +232,7 @@
         raw_grad = scale * (scaled - unit * head_means(scaled * unit))
         grads = jnp.concatenate([raw_grad, value_grads[here, :HEAD_DIM]], axis=1)
         store_pair(out_refs, pair, core, grads.astype(BF16))
+        store_pair(packed_refs, pair, core, packed(grads).astype(BF16))
     gain_grad_ref[...] = jnp.broadcast_to(gain_total[None], gain_grad_ref.shape)
 
 
@@ -248,20 +274,22 @@
 def forward_attention(place, qkv, gain, cosine, sine, deps=()):
     batch, tokens = qkv.shape[1:3]
     length = 4 * tokens
-    *mixed, stats = attention_call(
+    width = GROUP * HEAD_DIM
+    outs = attention_call(
         attend_forward,
         "attend_forward",
         place,
         [qkv],
         [gain, cosine, sine],
-        [jax.ShapeDtypeStruct((2, batch, tokens, GROUP * HEAD_DIM), BF16)] * 4
+        [jax.ShapeDtypeStruct((2, batch, tokens, width), BF16)] * 4
+        + [jax.ShapeDtypeStruct((2, batch, GROUP * tokens // 4, 4 * HEAD_DIM), BF16)] * 4
         + [jax.ShapeDtypeStruct((8, batch, tokens, AUG), F32)],
         [pltpu.VMEM((length, HEAD_DIM), BF16), pltpu.VMEM((length, AUG), BF16)],
         deps,
         14,
         0.0,
     )
-    return mixed, stats
+    return outs[:4], outs[4:8], outs[8]
 
 
 def backward_attention(place, sequence, qkv, mixed, grads, stats, gain, cosine, sine):
@@ -283,11 +311,12 @@
 
     blocked = [spread(array) for array in (qkv, stats)]
     here = slice(2 * sequence, 2 * sequence + 2)
-    near = [pair.reshape(2, batch, tokens, -1) for pair in grads[0][here]]
-    far = grads[1].reshape(4, batch, tokens, -1)
+    near = [pair.reshape(2, batch, -1, 4 * HEAD_DIM) for pair in grads[0][here]]
+    far = grads[1].reshape(4, batch, -1, 4 * HEAD_DIM)
     mixed = mixed[here]
     whole = [gain, cosine, sine]
     width = qkv.shape[3]
+    pack = (2, batch, width // HEAD_DIM * tokens // 4, 4 * HEAD_DIM)
     *qkv_grads, head_part = pl.pallas_call(
         attend_backward,
         grid_spec=pltpu.PrefetchScalarGridSpec(
@@ -298,7 +327,9 @@
             + [own_half(pair) for pair in near]
             + [pair_spec(GROUP * HEAD_DIM)] * 2
             + [pl.BlockSpec(a.shape, lambda i, *_: (0, 0)) for a in whole],
-            out_specs=[pair_spec(width)] * 2 + [pl.BlockSpec((1, 8, QK), lambda i, *_: (i, 0, 0))],
+            out_specs=[pair_spec(width)] * 2
+            + [pl.BlockSpec((2, 1) + pack[2:], lambda i, *_: (0, i, 0, 0))] * 2
+            + [pl.BlockSpec((1, 8, QK), lambda i, *_: (i, 0, 0))],
             scratch_shapes=[
                 pltpu.VMEM((length, AUG), BF16),
                 pltpu.VMEM((length, AUG), BF16),
@@ -308,12 +339,13 @@
             ],
         ),
         out_shape=[jax.ShapeDtypeStruct((2, batch, tokens, width), BF16)] * 2
+        + [jax.ShapeDtypeStruct(pack, BF16)] * 2
         + [jax.ShapeDtypeStruct((batch, 8, QK), F32)],
         name="attend_backward",
         cost_estimate=cost(0),
         compiler_params=pltpu.CompilerParams(vmem_limit_bytes=60 << 20),
     )(place, *blocked, far, *near, *mixed, *whole)
-    return qkv_grads, head_part
+    return qkv_grads[:2], qkv_grads[2:], head_part
 
 
 def rotary_rows(length):
@@ -618,15 +650,19 @@
 def from_pairs(refs, weights):
     total = None
     for ref, weight in zip(refs, weights):
-        part = dot(ref[...], weight[...])
+        values = unpacked(ref[...].astype(F32), weight.shape[0] // HEAD_DIM).astype(BF16)
+        part = dot(values, weight[...])
         total = part if total is None else total + part
     return total
 
 
-def pair_specs(pairs):
+def pair_specs(pairs, rows):
     near, far = pairs
-    rows = far.shape[0] // 4
-    return [row_tiles(pair) for pair in near] + [row_tiles(far, k * rows) for k in range(4)]
+    size = far.shape[0] // 4
+    tile = size * TILE // rows
+    return [row_tiles(pair, 0, tile) for pair in near] + [
+        row_tiles(far, k * size, tile) for k in range(4)
+    ]
 
 
 def pair_args(pairs):
@@ -645,7 +681,7 @@
     return pl.pallas_call(
         body,
         grid=(rows // TILE,),
-        in_specs=pair_specs(pairs)
+        in_specs=pair_specs(pairs, rows)
         + [entire(w) for w in weights]
         + [row_tiles(hidden), entire(gains)],
         out_specs=[row_tiles(hidden)] * 2,
@@ -674,7 +710,7 @@
         mine_ref, first, second, third, middle_ref, up_ref = refs[:6]
         weight_refs, gain_ref = refs[6:14], refs[14]
         grad_ref, low_ref, *pair_refs, sum_ref, sums = refs[15 + len(deps) :]
-        post_grad = mine_ref[...]
+        post_grad = mine_ref[...].astype(F32)
         for ref in (first, second, third):
             post_grad = post_grad + ref[...].astype(F32)
         back, unit = norm_back(middle_ref[...], gain_ref[1:2].astype(F32), post_grad)
@@ -683,8 +719,8 @@
         low = grad.astype(BF16)
         low_ref[...] = low
         for k in range(4):
-            pair_refs[k][0] = dot(low, weight_refs[k][...], 1, 1).astype(BF16)
-            pair_refs[k][1] = dot(low, weight_refs[4 + k][...], 1, 1).astype(BF16)
+            pair_refs[k][0] = packed(dot(low, weight_refs[k][...], 1, 1)).astype(BF16)
+            pair_refs[k][1] = packed(dot(low, weight_refs[4 + k][...], 1, 1)).astype(BF16)
         total = jnp.sum(post_grad * unit, axis=0, keepdims=True)
 
         @pl.when(pl.program_id(0) == 0)
@@ -699,7 +735,8 @@
             lane = lax.broadcasted_iota(jnp.int32, column.shape, 1)
             sum_ref[...] = jnp.where(lane == 1, column, 0.0)
 
-    side = pl.BlockSpec((2, TILE, width), lambda i: (0, i, 0))
+    size = width // HEAD_DIM * TILE // 4
+    side = pl.BlockSpec((2, size, 4 * HEAD_DIM), lambda i: (0, i, 0))
     return pl.pallas_call(
         body,
         grid=(rows // TILE,),
@@ -713,7 +750,7 @@
         out_shape=[
             jax.ShapeDtypeStruct((rows, depth), F32),
             jax.ShapeDtypeStruct((rows, depth), BF16),
-            *[jax.ShapeDtypeStruct((2, rows, width), BF16)] * 4,
+            *[jax.ShapeDtypeStruct((2, size * rows // TILE, 4 * HEAD_DIM), BF16)] * 4,
             jax.ShapeDtypeStruct((depth, GAIN_LANES), F32),
         ],
         scratch_shapes=[pltpu.VMEM((8, depth), F32)],
@@ -735,7 +772,7 @@
     return pl.pallas_call(
         body,
         grid=(rows // TILE,),
-        in_specs=pair_specs(pairs)
+        in_specs=pair_specs(pairs, rows)
         + [entire(w) for w in weights]
         + [row_tiles(hidden), row_tiles(grads), entire(gains)]
         + [ANY] * len(deps),
@@ -766,7 +803,7 @@
         in_specs=[tile(2), tile(0), tile(3)],
         out_specs=[tile(0)] * 4,
         out_shape=[
-            jax.ShapeDtypeStruct((rows, width), dtype) for dtype in (F32, BF16, BF16, BF16)
+            jax.ShapeDtypeStruct((rows, width), BF16) for _ in range(4)
         ],
         name="core_sum",
         cost_estimate=cost(0),
@@ -1027,6 +1064,7 @@
 
 
 def scatter_end(mine, others):
+    mine = mine.astype(F32)
     for other in others:
         mine = mine + other.astype(F32)
     return mine
@@ -1097,51 +1135,49 @@
         gain_rows,
     )
 
-    first_block = plane_columns(first_payload)
+
+    def start(payload, own_hidden, weights):
+        payloads = pack_columns(
+            weights,
+            [
+                [(0, 0, cut), (1, 0, cut), (2, 0, cut)],
+                [(0, cut, wide), rest, (1, cut, wide), rest, (2, cut, wide), rest],
+            ],
+        )
+        return plane_columns(payload), sides_come(own_hidden), payloads
+
+    first_block, hidden_sides, payloads = together(
+        start, first_payload, own_hidden, [gate_weight, up_weight, down_weight]
+    )
     first_full = line_gather(first_block)
-    payloads = pack_columns(
-        [gate_weight, up_weight, down_weight],
-        [
-            [(0, 0, cut), (1, 0, cut), (2, 0, cut)],
-            [(0, cut, wide), rest, (1, cut, wide), rest, (2, cut, wide), rest],
-        ],
-    )
-
-    early_block = plane_columns(after(payloads[0], first_block))
     out_first = qkv_cols + GAIN_LANES
 
-    def hidden_comes(own_hidden, payload):
-        return sides_come(own_hidden), plane_columns(payload)
-
-    hidden_sides, late_block = together(
-        hidden_comes, after(own_hidden, early_block), payloads[1]
+    def hidden_corner(own_hidden, hidden_sides, payload):
+        come = corners_come(hidden_sides), across([own_hidden, *hidden_sides])
+        return *come, rotary_rows(4 * tokens), plane_columns(payload)
+
+    corner, far, (cosine, sine), early_block = together(
+        hidden_corner, own_hidden, hidden_sides, payloads[0]
+    )
+    (corner,) = joined(*corner, 1)
+    late_block = plane_columns(after(payloads[1], early_block, corner))
+    qkv_rows, gain_turned, out_rows, head_scale = turn(
+        first_full,
+        [(0, qkv_cols), (qkv_cols, qkv_cols + 16), (out_first, out_first + query_cols)],
+        head_rows,
+        rows,
     )
     ffn_full = [line_gather(block) for block in (early_block, late_block)]
-
-    def hidden_corner(own_hidden, hidden_sides, first_full):
-        turned = turn(
-            first_full,
-            [(0, qkv_cols), (qkv_cols, qkv_cols + 16), (out_first, out_first + query_cols)],
-            head_rows,
-            rows,
-        )
-        come = corners_come(hidden_sides), across([own_hidden, *hidden_sides])
-        return *come, turned, rotary_rows(4 * tokens)
-
-    corner, far, (qkv_rows, gain_turned, out_rows, head_scale), (cosine, sine) = together(
-        hidden_corner, own_hidden, hidden_sides, first_full
-    )
-    (corner,) = joined(*corner, 1)
     hidden = [own_hidden, *hidden_sides, corner, *far, swap(corner, "c")]
 
     def attend(hidden, gain_turned, first_full, out_rows, head_scale, cosine, sine):
         out_near, out_first = plane_near(out_rows)
         normed, qkv = norm_project(hidden, gain_turned, first_full, qkv_cols)
         qkv = qkv.reshape(8, batch, tokens, qkv_cols)
-        mixed, stats = forward_attention(place, qkv, head_scale, cosine, sine)
-        return out_near[1:], out_first, normed, qkv, mixed, stats
-
-    out_near, out_own, normed, qkv, mixed, stats = together(
+        mixed, packs, stats = forward_attention(place, qkv, head_scale, cosine, sine)
+        return out_near[1:], out_first, normed, qkv, mixed, packs, stats
+
+    out_near, out_own, normed, qkv, mixed, packs, stats = together(
         attend,
         hidden,
         gain_turned,
@@ -1154,8 +1190,8 @@
 
     out_weights = [out_rows, *out_near], out_own
 
-    def attended(mixed, out_weights, own_hidden, own_upstream, gain_turned):
-        came = exchange_near([pair.reshape(-1, query_cols) for pair in mixed])
+    def attended(packs, out_weights, own_hidden, own_upstream, gain_turned):
+        came = exchange_near([pair.reshape(-1, 4 * HEAD_DIM) for pair in packs])
         grad_sides = sides_come(after(own_upstream, came[1]))
         out_weights = plane_all(out_weights)
         middle, post = attend_out(exchange_all(came), out_weights, own_hidden, gain_turned)
@@ -1164,7 +1200,7 @@
         return middle, post, sides_come(post), post_far, grad_sides, grad_far, out_weights[5:]
 
     middle, post_own, post_sides, post_far, grad_sides, grad_far, out_far = together(
-        attended, mixed, out_weights, own_hidden, own_upstream, gain_turned
+        attended, packs, out_weights, own_hidden, own_upstream, gain_turned
     )
     post = [post_own, *post_sides]
     grads = [own_upstream, *grad_sides]
@@ -1221,7 +1257,7 @@
 
     branch_far = swap(branch[2], "c")
 
-    mixed_grad = exchange_all(exchange_near([pair.reshape(-1, query_cols) for pair in pairs]))
+    mixed_grad = exchange_all(exchange_near([pair.reshape(-1, 4 * HEAD_DIM) for pair in pairs]))
 
     tables = head_scale, cosine, sine
 
@@ -1229,8 +1265,7 @@
         middle_sides = sides_come(middle_low)
         middle_first = swap(middle_low, "c")
         grads = backward_attention(place, 0, qkv, mixed, mixed_grad, stats, *tables)
-        send_0 = for_x_side(sums_0)
-        return middle_sides, middle_first, grads, send_0
+        return middle_sides, middle_first, grads, for_x_side(sums_0)
 
     middle_sides, middle_first, first_grads, send_0 = together(
         back_first,
@@ -1255,15 +1290,16 @@
     )
     middle_whole = [middle_low, *middle_sides, corner, middle_first, *far, swap(corner, "c")]
     qkv_grad = first_grads[0] + second_grads[0]
-    head_part = [first_grads[1], second_grads[1]]
+    qkv_packs = [pack.reshape(-1, 4 * HEAD_DIM) for pack in first_grads[1] + second_grads[1]]
+    head_part = [first_grads[2], second_grads[2]]
     sums_1 = line_scatter(parts_1)
     gain_parts = feedforward_part
 
 
-    def attention_grads(branch, qkv_grad, normed, middle_whole, mixed, first_full, gain_parts, head_part):
+    def attention_grads(branch, qkv_packs, qkv_grad, normed, middle_whole, mixed, first_full, gain_parts, head_part):
         qkv_grad = [pair.reshape(-1, qkv_cols) for pair in qkv_grad]
         mixed = [pair.reshape(-1, query_cols) for pair in mixed]
-        came = exchange_near(qkv_grad)
+        came = exchange_near(qkv_packs)
         parts = weight_grads(
             [([normed], qkv_grad), (middle_whole, mixed)],
             gains=(first_full, gain_parts, head_part, head_rows),
@@ -1274,6 +1310,7 @@
     came, attention_parts, branch = together(
         attention_grads,
         (branch[:2], branch_far),
+        qkv_packs,
         qkv_grad,
         normed,
         middle_whole,
@@ -1286,42 +1323,28 @@
     branch_mine, for_y, for_x, branch_corner = branch
     middle_rows = own_rows // 2
 
-    def corners(corner, qkv_pair, came, qkv_corner):
+    def corners(corner, sums_1, qkv_pair, came, qkv_corner):
         by_x, by_y = swap(corner[:middle_rows], "x"), swap(corner[middle_rows:], "y")
-        return by_x, by_y, exchange_all([qkv_pair, *came])[1], joined(*qkv_corner, 1)
-
-    by_x, by_y, pairs_far, qkv_corner = together(
-        corners, branch_corner, qkv_grad[0].reshape(-1, qkv_cols), came, qkv_corner
+        far = exchange_all([qkv_pair, *came])[1]
+        return by_x, by_y, swap(for_x_side(sums_1), "x"), far, joined(*qkv_corner, 1)
+
+    by_x, by_y, other_1, pairs_far, qkv_corner = together(
+        corners, branch_corner, sums_1, qkv_packs[0], came, qkv_corner
     )
     qkv_weights = [qkv_rows, *qkv_sides, *qkv_corner]
-    qkv_pairs = [qkv_grad[0].reshape(-1, qkv_cols), *came], pairs_far
+    qkv_pairs = [qkv_packs[0], *came], pairs_far
     for_y, for_x = corner_sum(for_y, for_x, by_x, by_y)
 
-    def sides(for_y, for_x, sums_1, qkv_pairs, qkv_weights, own_hidden, middle_grad, gain_turned):
-        others = swap(for_y, "y"), swap(for_x, "x")
+    x = lax.axis_index("x").astype(jnp.int32).reshape(1)
+
+    def sides(for_y, for_x, ffn_sums, others, qkv_pairs, qkv_weights, own_hidden, middle_grad, gain_turned):
+        branch_others = swap(for_y, "y"), swap(for_x, "x")
         weights = qkv_weights + across(qkv_weights)
         input_grad = input_back(qkv_pairs, weights, own_hidden, middle_grad, gain_turned)
-        other_1 = swap(after(for_x_side(sums_1), input_grad), "x")
-        return *others, other_1, input_grad
-
-    *branch_others, other_1, input_grad = together(
-        sides,
-        for_y,
-        for_x,
-        sums_1,
-        qkv_pairs,
-        qkv_weights,
-        own_hidden,
-        middle_grad,
-        gain_turned,
-    )
-    x = lax.axis_index("x").astype(jnp.int32).reshape(1)
-
-    def last(attention_sums, sums_0, sums_1, other_0, other_1, middle, branch_mine, branch_others):
         ffn_grads = unpack_columns(
             x,
-            [sums_0, sums_1],
-            [other_0, other_1],
+            ffn_sums,
+            others,
             [
                 [
                     (0, index * cut, (index + 1) * cut),
@@ -1331,19 +1354,27 @@
             ]
             + [None],
         )
+        return branch_others, input_grad, ffn_grads
+
+    branch_others, input_grad, ffn_grads = together(
+        sides,
+        for_y,
+        for_x,
+        [sums_0, sums_1],
+        [other_0, other_1],
+        qkv_pairs,
+        qkv_weights,
+        own_hidden,
+        middle_grad,
+        gain_turned,
+    )
+
+    def last(attention_sums, middle, branch_mine, branch_others):
         layer_output = (middle + scatter_end(branch_mine, branch_others)).astype(BF16)
-        return swap(for_x_side(attention_sums), "x"), ffn_grads, layer_output
-
-    attention_other, ffn_grads, layer_output = together(
-        last,
-        attention_sums,
-        sums_0,
-        sums_1,
-        other_0,
-        after(other_1, attention_sums),
-        middle,
-        branch_mine,
-        branch_others,
+        return swap(for_x_side(attention_sums), "x"), layer_output
+
+    attention_other, layer_output = together(
+        last, attention_sums, middle, branch_mine, branch_others
     )
 
     key_first, value_first = query_cols, query_cols + kv_cols

time: 500 us -> 482 us (0.964)
  blocking collectives: 62.7 us -> 16.6 us
  waiting for transfers between devices: 108 us -> 131 us
  starting transfers between devices: 48.6 us -> 61 us
  local copies, waits for them, and re-layouts: 19.1 us -> 12.1 us
    all_to_all x3 -> x1, blocking collectives: 62.7 us -> 16.6 us  [plane_columns(): lax.all_to_all(payload, PLANE, split_axis=0, concat_axis=0, tiled=True)]
    all_to_all x0 -> x2, waiting for transfers between devices: none -> 15.9 us  [plane_columns(): lax.all_to_all(payload, PLANE, split_axis=0, concat_axis=0, tiled=True)]
    all_to_all x0 -> x2, starting transfers between devices: none -> 8.51 us  [plane_columns(): lax.all_to_all(payload, PLANE, split_axis=0, concat_axis=0, tiled=True)]
    ppermute x65, waiting for transfers between devices: 87.6 us -> 95.2 us  [swap(): return lax.ppermute(values, axis, SWAP)]
    all_gather x3, waiting for transfers between devices: 0.05 us -> 5.71 us  [line_gather(): return lax.all_gather(block, 'dp', axis=0, tiled=True)]
    ppermute x5, waiting for transfers between devices: 18.8 us -> 13.3 us  [opposite(): return lax.ppermute(rows, ('x', 'y'), ((0, 3), (1, 2), (2, 1), (3, 0)))]
  transfers between devices with their start and end apart: 77 -> 79, of which waited for: 38 -> 32; matrix products, arithmetic and copies ran while one was open for 3% -> 2% of each run, Pallas kernels for 46% -> 48%
where the time goes in v6:
time: 482 us; the launch traced here: 477 us
  Pallas kernels  236 us (49%)
  waiting for transfers between devices  131 us (27%)
  starting transfers between devices  61 us (13%)
  blocking collectives  16.6 us (3%)
  between operations  14.7 us (3%)
  local copies, waits for them, and re-layouts  12.1 us (3%)
  other arithmetic  5.05 us (1%)
    ppermute x65, waiting for transfers between devices, swap(): return lax.ppermute(values, axis, SWAP)  95.2 us
    pallas_call x4, Pallas kernels, feed_forward(): pl.pallas_call(body, grid=(rows // TILE,), in_specs=specs * 2 + [entire(w...  56.7 us
    ppermute x65, starting transfers between devices, swap(): return lax.ppermute(values, axis, SWAP)  42.8 us
    pallas_call x3, Pallas kernels, weight_grads(): pl.pallas_call(body, grid=(depth // tile,), in_specs=specs + [ANY] * len(...  39.4 us
    pallas_call x2, Pallas kernels, backward_attention(): pl.pallas_call(attend_backward, grid_spec=pltpu.PrefetchScalarGridSpec(nu...  31.2 us
    all_to_all x1, blocking collectives, plane_columns(): lax.all_to_all(payload, PLANE, split_axis=0, concat_axis=0, tiled=True)  16.6 us
    all_to_all x2, waiting for transfers between devices, plane_columns(): lax.all_to_all(payload, PLANE, split_axis=0, concat_axis=0, tiled=True)  15.9 us
    pallas_call x1, Pallas kernels, attention_call(): pl.pallas_call(body, grid_spec=pltpu.PrefetchScalarGridSpec(num_scalar_pr...  15.6 us
  transfers between devices with their start and end apart: 79, of which 32 were waited for; matrix products, arithmetic and copies ran while one was open for 2% of the time, Pallas kernels for 48%

profile of v6, /device:TPU:0, one launch (start us, length us, event | category | flops | bytes accessed | tf_op | source)
XLA Modules:
  0.0 476.8 jit_solution(12294851152988785263)
XLA Ops:
  9.2 27.5 %conditional.14 = (bf16[384,640]{1,0:T(8,128)(2,1)}, bf16[256,1536]{1,0:T(8,128)(2,1)}, bf16[256,1536]{1,0:T(8,128)(2,1)}, bf16[8,48,1536]{2,1,0:T(8,128)(2,1)}, bf16[8,48,1152]{2,1,0:T(8,128)(2,1)S(1)}) conditional(s32[]{:T(128)} %convert_element_type.46, () %tuple.137, (bf16[8,48,640]{2,1,0:T(8,128)(2,1)}, bf16[256,1536]{1,0:T(8,128)(2,1)}, ...), branch_computations={%region_0.0_spmd, %region_1.0_spmd} | conditional | bytes 7766168 | solution.py:1087
  9.2 2.9 collective-permute-start.1
  13.7 4.1 all-to-all-start
  17.8 3.1 pack_columns.2
  20.9 15.9 %all-to-all-done = bf16[8,48,640]{2,1,0:T(8,128)(2,1)} async-done(((bf16[8,48,640]{2,1,0:T(8,128)(2,1)}), bf16[8,48,640]{2,1,0:T(8,128)(2,1)}, u32[]{:S(2)}, u32[]{:S(2)}) %all-to-all-start) | async-done | bytes 491552 | tf_op jit(solution)/shard_map/cond/branch_1_fun/all_to_all | solution.py:1091
  36.8 28.7 %conditional.15 = (bf16[128,1536]{1,0:T(8,128)(2,1)}, bf16[128,1536]{1,0:T(8,128)(2,1)}, bf16[256,1536]{1,0:T(8,128)(2,1)}, bf16[256,1536]{1,0:T(8,128)(2,1)}, b...) conditional(s32[]{:T(128)} %convert_element_type.46, () %tuple.139, ...), branch_computations={%region_2.0_spmd, %region_3.0_spmd} | conditional | flops 33890 | bytes 19538502 | solution.py:1087
  36.9 4.4 all-to-all-start.1
  42.1 2.0 halves.3
  47.4 3.0 multiply_sine_fusion
  50.4 3.0 rotary_rows.1
  53.4 12.1 %collective-permute-done.45 = bf16[128,1536]{1,0:T(8,128)(2,1)} collective-permute-done((bf16[128,1536]{1,0:T(8,128)(2,1)}, bf16[128,1536]{1,0:T(8,128)(2,1)}, u32[]{:S(2)}, u32[]{:S(2)}) %collective-permute-start.45) | collective-permute-done | bytes 393248 | tf_op jit(solution)/shard_map/cond/branch_1_fun/ppermute | solution.py:1024
  65.7 2.1 joined.4.refs_2_
  67.7 16.6 %all_to_all.13 = bf16[8,48,1152]{2,1,0:T(8,128)(2,1)} all-to-all(bf16[8,48,1152]{2,1,0:T(8,128)(2,1)S(1)} %after.4), channel_id=1, replica_groups=mesh['dp'=4,'x'=2,'y'=2,'c'=2] {'x','y','c'}, dimensions={0} | all-to-all | bytes 1769472 | tf_op jit(solution)/shard_map/all_to_all | solution.py:1091
  84.5 3.5 turn.1
  89.1 30.2 %conditional.16 = (bf16[192,1536]{1,0:T(8,128)(2,1)}, bf16[192,1536]{1,0:T(8,128)(2,1)}, bf16[192,1536]{1,0:T(8,128)(2,1)}, bf16[192,1536]{1,0:T(8,128)(2,1)}, b...) conditional(s32[]{:T(128)} %convert_element_type.46, () %tuple.136, ...), branch_computations={%region_4.0_spmd, %region_5.0_spmd} | conditional | flops 2 | bytes 17826128 | solution.py:1087
  93.0 10.5 %norm_project.1 = (bf16[2048,1536]{1,0:T(8,128)(2,1)}, bf16[2048,320]{1,0:T(8,128)(2,1)}) custom-call(bf16[256,1536]{1,0:T(8,128)(2,1)S(1)} %get-tuple-element.404.refs_0_, bf16[256,1536]{1,0:T(8,128)(2,1)} %get-tuple-element.405.refs_1_, bf16[256,1536]{1,0:T(8,128)(2,1)} %get-tuple-element.406.refs_2_, bf16[256,1536]{1,0:T(8,128)(2,1)} %get-tuple-element.407.refs_3_, ...), custom_call_target="tpu_custom_call" | custom-call | flops 1 | bytes 1 | tf_op jit(solution)/shard_map/cond/branch_1_fun/norm_project/pallas_call | solution.py:438
  103.6 15.6 %attend_forward.1 = (bf16[2,1,256,192]{3,2,1,0:T(8,128)(2,1)}, bf16[2,1,256,192]{3,2,1,0:T(8,128)(2,1)}, bf16[2,1,256,192]{3,2,1,0:T(8,128)(2,1)}, bf16[2,1,256,...) custom-call(s32[1]{0:T(128)} %get-tuple-element.416.place_ref, ...), custom_call_target="tpu_custom_call" | custom-call | flops 1 | bytes 1 | tf_op jit(solution)/shard_map/cond/branch_1_fun/attend_forward/pallas_call | solution.py:256
  119.3 52.4 %conditional.17 = (f32[256,1536]{1,0:T(8,128)}, bf16[256,1536]{1,0:T(8,128)(2,1)}, bf16[256,1536]{1,0:T(8,128)(2,1)}, bf16[256,1536]{1,0:T(8,128)(2,1)}, bf16[25...) conditional(s32[]{:T(128)} %convert_element_type.46, () %tuple.135, ...), branch_computations={%region_6.0_spmd, %region_7.0_spmd} | conditional | flops 2 | bytes 45810620 | solution.py:1087
  122.9 5.2 %collective-permute-done.8.refs_3_ = bf16[384,256]{1,0:T(8,128)(2,1)S(1)} collective-permute-done((bf16[384,256]{1,0:T(8,128)(2,1)S(1)}, bf16[384,256]{1,0:T(8,128)(2,1)S(1)}, u32[]{:S(2)}, u32[]{:S(2)}) %collective-permute-start.8) | collective-permute-done | bytes 196640 | tf_op jit(solution)/shard_map/cond/branch_1_fun/ppermute | solution.py:1050
  139.4 5.5 %attend_out.1 = (f32[256,1536]{1,0:T(8,128)}, bf16[256,1536]{1,0:T(8,128)(2,1)}) custom-call(bf16[384,256]{1,0:T(8,128)(2,1)S(1)} %bitcast.101, bf16[384,256]{1,0:T(8,128)(2,1)S(1)} %copy-done.1, bf16[384,256]{1,0:T(8,128)(2,1)S(1)} %copy-done.6, bf16[384,256]{1,0:T(8,128)(2,1)S(1)} %copy-done.4, ...), custom_call_target="tpu_custom_call" | custom-call | flops 1 | bytes 1 | tf_op jit(solution)/shard_map/cond/branch_1_fun/attend_out/pallas_call | solution.py:681
  147.4 7.8 %collective-permute-done.17 = bf16[256,1536]{1,0:T(8,128)(2,1)} collective-permute-done((bf16[256,1536]{1,0:T(8,128)(2,1)}, bf16[256,1536]{1,0:T(8,128)(2,1)}, u32[]{:S(2)}, u32[]{:S(2)}) %collective-permute-start.17) | collective-permute-done | bytes 786464 | tf_op jit(solution)/shard_map/cond/branch_1_fun/ppermute | solution.py:1024
  156.1 15.0 %collective-permute-done.14 = bf16[256,1536]{1,0:T(8,128)(2,1)} collective-permute-done((bf16[256,1536]{1,0:T(8,128)(2,1)}, bf16[256,1536]{1,0:T(8,128)(2,1)}, u32[]{:S(2)}, u32[]{:S(2)}) %collective-permute-start.14) | collective-permute-done | bytes 786464 | tf_op jit(solution)/shard_map/cond/branch_1_fun/ppermute | solution.py:1024
  171.7 22.4 %conditional.18 = (bf16[256,1536]{1,0:T(8,128)(2,1)}, bf16[256,1536]{1,0:T(8,128)(2,1)}, bf16[256,1536]{1,0:T(8,128)(2,1)}, bf16[256,1536]{1,0:T(8,128)(2,1)}, b...) conditional(s32[]{:T(128)} %convert_element_type.46, () %tuple.143, ...), branch_computations={%region_8.0_spmd, %region_9.0_spmd} | conditional | flops 2 | bytes 12583130 | solution.py:1087
  171.7 2.6 halves.4
  176.9 12.5 %feed_forward.4 = (bf16[768,1024]{1,0:T(8,128)(2,1)}, bf16[768,512]{1,0:T(8,128)(2,1)}, bf16[768,1536]{1,0:T(8,128)(2,1)}) custom-call(bf16[256,1536]{1,0:T(8,128)(2,1)} %get-tuple-element.449.refs_0_, bf16[256,1536]{1,0:T(8,128)(2,1)} %get-tuple-element.443.refs_0_.refs_1_, bf16[256,1536]{1,0:T(8,128)(2,1)} %get-tuple-element.444.refs_1_.refs_2_, ...), custom_call_target="tpu_custom_call" | custom-call | flops 1 | bytes 1 | tf_op jit(solution)/shard_map/cond/branch_1_fun/feed_forward/pallas_call | solution.py:494
  189.4 3.5 collective-permute-done.21
  200.0 35.0 %conditional.19 = (bf16[1280,512]{1,0:T(8,128)(2,1)}, bf16[256,1536]{1,0:T(8,128)(2,1)}, bf16[1024,1536]{1,0:T(8,128)(2,1)}, bf16[1536,1536]{1,0:T(8,128)(2,1)},...) conditional(s32[]{:T(128)} %convert_element_type.46, () %tuple.146, (bf16[256,1536]{1,0:T(8,128)(2,1)S(1)}, ...), branch_computations={%region_10.0_spmd, %region_11.0_spmd} | conditional | flops 2 | bytes 17301690 | solution.py:1087
  202.0 17.9 %feed_forward.5 = (bf16[1280,1024]{1,0:T(8,128)(2,1)}, bf16[1280,512]{1,0:T(8,128)(2,1)}, bf16[256,1536]{1,0:T(8,128)(2,1)}, bf16[1024,1536]{1,0:T(8,128)(2,1)}) custom-call(bf16[256,1536]{1,0:T(8,128)(2,1)S(1)} %get-tuple-element.455.refs_0_.refs_3_, bf16[256,1536]{1,0:T(8,128)(2,1)} %get-tuple-element.456.refs_1_.refs_4_, ...), custom_call_target="tpu_custom_call" | custom-call | flops 1 | bytes 1 | tf_op jit(solution)/shard_map/cond/branch_1_fun/feed_forward/pallas_call | solution.py:494
  219.9 15.1 %weight_grads.3 = bf16[1536,1536]{1,0:T(8,128)(2,1)} custom-call(bf16[256,1536]{1,0:T(8,128)(2,1)} %get-tuple-element.469.refs_0_, bf16[256,1536]{1,0:T(8,128)(2,1)} %get-tuple-element.470.refs_1_, bf16[256,1536]{1,0:T(8,128)(2,1)} %get-tuple-element.471.refs_2_, bf16[256,1536]{1,0:T(8,128)(2,1)S(1)} %get-tuple-element.455.refs_0_.refs_3_, ...), custom_call_target="tpu_custom_call" | custom-call | flops 1 | bytes 1 | tf_op jit(solution)/shard_map/cond/branch_1_fun/weight_grads/pallas_call | solution.py:595
  235.1 5.7 %all-gather.6.cloned.1.call-done.refs_6_ = bf16[1536,1152]{1,0:T(8,128)(2,1)} async-done(((bf16[384,1152]{1,0:T(8,128)(2,1)}), bf16[1536,1152]{1,0:T(8,128)(2,1)}) %all-gather.6.cloned.1.call-update) | async-done | bytes 3538960 | tf_op jit(solution)/shard_map/all_gather | solution.py:1074
  240.8 21.3 %conditional.20 = (bf16[160,1536]{1,0:T(8,128)(2,1)}, bf16[160,1536]{1,0:T(8,128)(2,1)}, bf16[1280,768]{1,0:T(8,128)(2,1)}, bf16[1280,384]{1,0:T(8,128)(2,1)}, b...) conditional(s32[]{:T(128)} %convert_element_type.46, () %tuple.145, (bf16[320,1536]{1,0:T(8,128)(2,1)}, ...), branch_computations={%region_12.0_spmd, %region_13.0_spmd} | conditional | flops 2 | bytes 7864380 | solution.py:1087
  240.8 2.2 halves.5
  245.9 16.1 %feed_forward.6 = (bf16[1280,768]{1,0:T(8,128)(2,1)}, bf16[1280,384]{1,0:T(8,128)(2,1)}, bf16[256,1536]{1,0:T(8,128)(2,1)}, bf16[1024,1536]{1,0:T(8,128)(2,1)}) custom-call(bf16[256,1536]{1,0:T(8,128)(2,1)S(1)} %get-tuple-element.483.refs_0_, bf16[256,1536]{1,0:T(8,128)(2,1)} %get-tuple-element.484.refs_1_, bf16[256,1536]{1,0:T(8,128)(2,1)} %get-tuple-element.485.refs_2_, ...), custom_call_target="tpu_custom_call" | custom-call | flops 1 | bytes 1 | tf_op jit(solution)/shard_map/cond/branch_1_fun/feed_forward/pallas_call | solution.py:494
  262.1 10.2 %feed_forward.7 = (bf16[768,768]{1,0:T(8,128)(2,1)}, bf16[768,384]{1,0:T(8,128)(2,1)S(1)}, bf16[768,1536]{1,0:T(8,128)(2,1)}) custom-call(bf16[256,1536]{1,0:T(8,128)(2,1)} %get-tuple-element.800.refs_0_, bf16[256,1536]{1,0:T(8,128)(2,1)} %get-tuple-element.801.refs_1_, bf16[256,1536]{1,0:T(8,128)(2,1)} %get-tuple-element.802.refs_2_, ...), custom_call_target="tpu_custom_call" | custom-call | flops 1 | bytes 1 | tf_op jit(solution)/shard_map/feed_forward/pallas_call | solution.py:494
  274.1 5.8 %core_sum.3 = (bf16[256,1536]{1,0:T(8,128)(2,1)}, bf16[256,1536]{1,0:T(8,128)(2,1)}, bf16[256,1536]{1,0:T(8,128)(2,1)}, bf16[256,1536]{1,0:T(8,128)(2,1)}) custom-call(bf16[768,1536]{1,0:T(8,128)(2,1)} %get-tuple-element.826.three_ref, bf16[256,1536]{1,0:T(8,128)(2,1)} %get-tuple-element.827.one_ref, bf16[1024,1536]{1,0:T(8,128)(2,1)} %copy-done.33), custom_call_target="tpu_custom_call" | custom-call | flops 1 | bytes 1 | tf_op jit(solution)/shard_map/core_sum/pallas_call | solution.py:800
  279.8 38.3 %conditional.21 = (bf16[256,1536]{1,0:T(8,128)(2,1)}, bf16[256,1536]{1,0:T(8,128)(2,1)}, bf16[256,1536]{1,0:T(8,128)(2,1)}, bf16[1536,1152]{1,0:T(8,128)(2,1)}, ...) conditional(s32[]{:T(128)} %convert_element_type.46, () %tuple.149, ...), branch_computations={%region_14.0_spmd, %region_15.0_spmd} | conditional | flops 2 | bytes 25166140 | solution.py:1087
  280.5 2.9 collective-permute-start.31
  283.4 13.2 %project_back.1 = (bf16[768,1536]{1,0:T(8,128)(2,1)}, bf16[256,1536]{1,0:T(8,128)(2,1)}, bf16[1024,1536]{1,0:T(8,128)(2,1)}) custom-call(bf16[768,512]{1,0:T(8,128)(2,1)} %get-tuple-element.523.refs_0_, bf16[1280,512]{1,0:T(8,128)(2,1)} %get-tuple-element.524.refs_1_, bf16[768,384]{1,0:T(8,128)(2,1)S(1)} %get-tuple-element.521.refs_18_.refs_2_, ...), custom_call_target="tpu_custom_call" | custom-call | flops 1 | bytes 1 | tf_op jit(solution)/shard_map/cond/branch_1_fun/project_back/pallas_call | solution.py:629
  296.6 13.5 %weight_grads.4 = bf16[1536,1152]{1,0:T(8,128)(2,1)} custom-call(bf16[256,1536]{1,0:T(8,128)(2,1)} %get-tuple-element.503.refs_0_, bf16[256,1536]{1,0:T(8,128)(2,1)} %get-tuple-element.504.refs_1_, bf16[256,1536]{1,0:T(8,128)(2,1)} %get-tuple-element.505.refs_2_, bf16[256,1536]{1,0:T(8,128)(2,1)S(1)} %copy-done.18, ...), custom_call_target="tpu_custom_call" | custom-call | flops 1 | bytes 1 | tf_op jit(solution)/shard_map/cond/branch_1_fun/weight_grads/pallas_call | solution.py:595
  310.1 8.1 %collective-permute-done.31 = bf16[256,1536]{1,0:T(8,128)(2,1)} collective-permute-done((bf16[256,1536]{1,0:T(8,128)(2,1)}, bf16[256,1536]{1,0:T(8,128)(2,1)}, u32[]{:S(2)}, u32[]{:S(2)}) %collective-permute-start.31) | collective-permute-done | bytes 786464 | tf_op jit(solution)/shard_map/cond/branch_1_fun/ppermute | solution.py:1050
  319.5 7.7 %middle_back.1 = (f32[256,1536]{1,0:T(8,128)}, bf16[256,1536]{1,0:T(8,128)(2,1)}, bf16[2,192,256]{2,1,0:T(8,128)(2,1)S(1)}, bf16[2,192,256]{2,1,0:T(8,128)(2,1)S...) custom-call(bf16[256,1536]{1,0:T(8,128)(2,1)S(1)} %copy-done.2, ...), custom_call_target="tpu_custom_call" | custom-call | flops 1 | bytes 1 | tf_op jit(solution)/shard_map/middle_back/pallas_call | solution.py:740
  328.1 2.6 collective-permute-start.64
  330.7 4.3 collective-permute-done.63.refs_2_
  335.0 3.2 collective-permute-done.62.refs_1_
  341.1 21.2 %conditional.22 = (bf16[256,1536]{1,0:T(8,128)(2,1)}, bf16[256,1536]{1,0:T(8,128)(2,1)}, bf16[256,1536]{1,0:T(8,128)(2,1)}, bf16[2,1,256,320]{3,2,1,0:T(8,128)(2...) conditional(s32[]{:T(128)} %convert_element_type.46, () %tuple.134, ...), branch_computations={%region_17.0_spmd, %region_18.0_spmd} | conditional | flops 9 | bytes 16122199 | solution.py:1087
  343.2 15.6 %attend_backward.2 = (bf16[2,1,256,320]{3,2,1,0:T(8,128)(2,1)}, bf16[2,1,256,320]{3,2,1,0:T(8,128)(2,1)}, bf16[2,1,320,256]{3,2,1,0:T(8,128)(2,1)}, bf16[2,1,320,256]{3,2,1,0:T(8,128)(2,1)}, f32[1,8,256]{2,1,0:T(8,128)S(1)}) custom-call(s32[1]{0:T(128)} %get-tuple-element.531.place_ref, bf16[2,2,2,1,256,320]{5,4,3,2,1,0:T(8,128)(2,1)} %bitcast.16.qkv_ref, ...), custom_call_target="tpu_custom_call" | custom-call | flops 1 | bytes 1 | tf_op jit(solution)/shard_map/cond/branch_1_fun/attend_backward/pallas_call | solution.py:320
  362.2 20.4 %conditional.23 = (bf16[256,1536]{1,0:T(8,128)(2,1)}, bf16[192,1536]{1,0:T(8,128)(2,1)}, bf16[256,1536]{1,0:T(8,128)(2,1)}, bf16[256,1536]{1,0:T(8,128)(2,1)}, b...) conditional(s32[]{:T(128)} %convert_element_type.46, () %tuple.152, ...), branch_computations={%region_19.0_spmd, %region_20.0_spmd} | conditional | flops 1 | bytes 11796713 | solution.py:1087
  364.3 15.5 %attend_backward.3 = (bf16[2,1,256,320]{3,2,1,0:T(8,128)(2,1)}, bf16[2,1,256,320]{3,2,1,0:T(8,128)(2,1)}, bf16[2,1,320,256]{3,2,1,0:T(8,128)(2,1)}, bf16[2,1,320,256]{3,2,1,0:T(8,128)(2,1)}, f32[1,8,256]{2,1,0:T(8,128)S(1)}) custom-call(s32[1]{0:T(128)} %get-tuple-element.551.place_ref, bf16[2,2,2,1,256,320]{5,4,3,2,1,0:T(8,128)(2,1)} %bitcast.27.qkv_ref, ...), custom_call_target="tpu_custom_call" | custom-call | flops 1 | bytes 1 | tf_op jit(solution)/shard_map/cond/branch_1_fun/attend_backward/pallas_call | solution.py:320
  379.8 2.8 collective-permute-done.32
  382.6 2.5 collective-permute-done.66
  385.1 20.0 %conditional.24 = (bf16[640,256]{1,0:T(8,128)(2,1)}, bf16[640,256]{1,0:T(8,128)(2,1)}, bf16[640,256]{1,0:T(8,128)(2,1)}, bf16[1536,640]{1,0:T(8,128)(2,1)S(1)}, ...) conditional(s32[]{:T(128)} %convert_element_type.46, () %tuple.133, ...), branch_computations={%region_21.0_spmd, %region_22.0_spmd} | conditional | flops 2 | bytes 10486058 | solution.py:1087
  388.6 5.5 %core_sum.2 = (bf16[256,1536]{1,0:T(8,128)(2,1)}, bf16[256,1536]{1,0:T(8,128)(2,1)}, bf16[256,1536]{1,0:T(8,128)(2,1)}, bf16[256,1536]{1,0:T(8,128)(2,1)}) custom-call(bf16[768,1536]{1,0:T(8,128)(2,1)} %get-tuple-element.591.three_ref, bf16[256,1536]{1,0:T(8,128)(2,1)} %get-tuple-element.592.one_ref, bf16[1024,1536]{1,0:T(8,128)(2,1)} %get-tuple-element.593.far_ref), custom_call_target="tpu_custom_call" | custom-call | flops 1 | bytes 1 | tf_op jit(solution)/shard_map/cond/branch_1_fun/core_sum/pallas_call | solution.py:800
  394.1 10.9 %weight_grads.5 = bf16[1536,640]{1,0:T(8,128)(2,1)S(1)} custom-call(bf16[2048,1536]{1,0:T(8,128)(2,1)} %get-tuple-element.570.refs_0_, bf16[512,320]{1,0:T(8,128)(2,1)S(1)} %bitcast.103, bf16[512,320]{1,0:T(8,128)(2,1)S(1)} %bitcast.102, bf16[512,320]{1,0:T(8,128)(2,1)} %bitcast.105, bf16[512,320]{1,0:T(8,128)(2,1)} %bitcast.104, ...), custom_call_target="tpu_custom_call" | custom-call | flops 1 | bytes 1 | tf_op jit(solution)/shard_map/cond/branch_1_fun/weight_grads/pallas_call | solution.py:595
  407.1 20.0 %conditional.25 = (bf16[128,1536]{1,0:T(8,128)(2,1)}, bf16[128,1536]{1,0:T(8,128)(2,1)}, bf16[192,1152]{1,0:T(8,128)(2,1)}, bf16[1280,256]{1,0:T(8,128)(2,1)}, bf16[320,1536]{1,0:T(8,128)(2,1)S(1)}) conditional(s32[]{:T(128)} %convert_element_type.46, () %tuple.156, (bf16[256,1536]{1,0:T(8,128)(2,1)}, bf16[384,1152]{1,0:T(8,128)(2,1)S(1)}, ...), branch_computations={%region_24.0_spmd, %region_25.0_spmd} | conditional | flops 10 | bytes 13140292 | solution.py:1087
  413.7 8.6 %collective-permute-done.55 = bf16[128,1536]{1,0:T(8,128)(2,1)} collective-permute-done((bf16[128,1536]{1,0:T(8,128)(2,1)}, bf16[128,1536]{1,0:T(8,128)(2,1)}, u32[]{:S(2)}, u32[]{:S(2)}) %collective-permute-start.55) | collective-permute-done | bytes 393248 | tf_op jit(solution)/shard_map/cond/branch_1_fun/ppermute | solution.py:1024
  422.3 4.8 %collective-permute-done.54 = bf16[128,1536]{1,0:T(8,128)(2,1)} collective-permute-done((bf16[128,1536]{1,0:T(8,128)(2,1)S(1)}, bf16[128,1536]{1,0:T(8,128)(2,1)}, u32[]{:S(2)}, u32[]{:S(2)}) %collective-permute-start.54) | collective-permute-done | bytes 393248 | tf_op jit(solution)/shard_map/cond/branch_1_fun/ppermute | solution.py:1024
  427.1 3.2 corner_sum.1
  430.3 22.8 %conditional.26 = (bf16[256,1536]{1,0:T(8,128)(2,1)}, bf16[256,1536]{1,0:T(8,128)(2,1)}, f32[192,1728]{1,0:T(8,128)}, f32[192,1728]{1,0:T(8,128)}, f32[192,1728]{1,0:T(8,128)}, /*index=5*/f32[1,256,1536]{2,1,0:T(8,128)}) conditional(s32[]{:T(128)} %convert_element_type.46, () %tuple.155, (bf16[256,1536]{1,0:T(8,128)(2,1)}, ...), branch_computations={%region_26.0_spmd, %region_27.0_spmd} | conditional | flops 1 | bytes 32244056 | solution.py:1087
  433.7 3.8 unpack_columns.2
  437.5 7.2 %input_back.1 = f32[256,1536]{1,0:T(8,128)} custom-call(bf16[640,256]{1,0:T(8,128)(2,1)S(1)} %get-tuple-element.616.refs_0_, bf16[640,256]{1,0:T(8,128)(2,1)} %get-tuple-element.617.refs_1_, bf16[640,256]{1,0:T(8,128)(2,1)} %get-tuple-element.618.refs_2_, bf16[640,256]{1,0:T(8,128)(2,1)} %get-tuple-element.619.refs_3_, ...), custom_call_target="tpu_custom_call" | custom-call | flops 1 | bytes 1 | tf_op jit(solution)/shard_map/cond/branch_1_fun/input_back/pallas_call | solution.py:772
  444.8 6.5 %collective-permute-done.39 = bf16[256,1536]{1,0:T(8,128)(2,1)} collective-permute-done((bf16[256,1536]{1,0:T(8,128)(2,1)}, bf16[256,1536]{1,0:T(8,128)(2,1)}, u32[]{:S(2)}, u32[]{:S(2)}) %collective-permute-start.39) | collective-permute-done | bytes 786464 | tf_op jit(solution)/shard_map/cond/branch_1_fun/ppermute | solution.py:1024
  453.1 8.3 %conditional.27 = (bf16[192,640]{1,0:T(8,128)(2,1)}, bf16[1,256,1536]{2,1,0:T(8,128)(2,1)S(1)}) conditional(s32[]{:T(128)} %convert_element_type.46, () %tuple.132, (bf16[384,640]{1,0:T(8,128)(2,1)}, bf16[256,1536]{1,0:T(8,128)(2,1)}, bf16[256,1536]{1,0:T(8,128)(2,1)}, bf16[256,1536]{1,0:T(8,128)(2,1)}, f32[256,1536]{1,0:T(8,128)S(1)}) %tuple.226), branch_computations={%region_29.0_spmd, %region_30.0_spmd} | conditional | flops 2752520 | bytes 6193302 | solution.py:1087
  456.6 4.8 %collective-permute-done.53 = bf16[192,640]{1,0:T(8,128)(2,1)} collective-permute-done((bf16[192,640]{1,0:T(8,128)(2,1)S(1)}, bf16[192,640]{1,0:T(8,128)(2,1)}, u32[]{:S(2)}, u32[]{:S(2)}) %collective-permute-start.53) | collective-permute-done | bytes 245792 | tf_op jit(solution)/shard_map/cond/branch_1_fun/ppermute | solution.py:1024
  461.4 2.4 unpack_columns.3
  (284 shorter events, 88.3 us)
Async XLA Ops:
  7.2 77.3 %all-gather.4.cloned.1.call-start = ((), (), s32[]{:S(2)}) async-start(), calls=%async_computation.6 | async-start | bytes 2457600 | tf_op jit(solution)/shard_map/all_gather | solution.py:1074
  9.2 27.5 %collective-permute-start.1 = (bf16[256,1536]{1,0:T(8,128)(2,1)}, bf16[256,1536]{1,0:T(8,128)(2,1)}, u32[]{:S(2)}, u32[]{:S(2)}) collective-permute-start(bf16[256,1536]{1,0:T(8,128)(2,1)} %get-tuple-element.389), channel_id=1, source_target_pairs={{0,4},{4,0},{1,5},{5,1},{2,6},{6,2},{3,7},{7,3},{8,12},{12,8},{9,1... | collective-permute-start | bytes 2359304 | tf_op jit(solution)/shard_map/cond/branch_1_fun/ppermute | solution.py:1024
  12.2 24.6 %collective-permute-start = (bf16[256,1536]{1,0:T(8,128)(2,1)}, bf16[256,1536]{1,0:T(8,128)(2,1)}, u32[]{:S(2)}, u32[]{:S(2)}) collective-permute-start(bf16[256,1536]{1,0:T(8,128)(2,1)} %get-tuple-element.389), channel_id=1, source_target_pairs={{0,2},{2,0},{1,3},{3,1},{4,6},{6,4},{5,7},{7,5},{8,10},{10,8},{9,1... | collective-permute-start | bytes 2359304 | tf_op jit(solution)/shard_map/cond/branch_1_fun/ppermute | solution.py:1024
  13.7 23.1 %all-to-all-start = ((bf16[8,48,640]{2,1,0:T(8,128)(2,1)}), bf16[8,48,640]{2,1,0:T(8,128)(2,1)}, u32[]{:S(2)}, u32[]{:S(2)}) async-start(bf16[8,48,640]{2,1,0:T(8,128)(2,1)} %get-tuple-element.388), calls=%async_computation | async-start | bytes 983040 | tf_op jit(solution)/shard_map/cond/branch_1_fun/all_to_all | solution.py:1091
  36.8 134.9 %all-gather.8.cloned.1.call-start = ((), (), s32[]{:S(2)}) async-start(), calls=%async_computation.8 | async-start | bytes 5898240 | tf_op jit(solution)/shard_map/all_gather | solution.py:1074
  36.9 28.7 %all-to-all-start.1 = ((bf16[8,48,1536]{2,1,0:T(8,128)(2,1)}), bf16[8,48,1536]{2,1,0:T(8,128)(2,1)}, u32[]{:S(2)}, u32[]{:S(2)}) async-start(bf16[8,48,1536]{2,1,0:T(8,128)(2,1)} %get-tuple-element.402), calls=%async_computation.1 | async-start | bytes 2359296 | tf_op jit(solution)/shard_map/cond/branch_1_fun/all_to_all | solution.py:1091
  41.3 24.3 %collective-permute-start.47 = (bf16[256,1536]{1,0:T(8,128)(2,1)S(1)}, bf16[256,1536]{1,0:T(8,128)(2,1)}, u32[]{:S(2)}, u32[]{:S(2)}) collective-permute-start(bf16[256,1536]{1,0:T(8,128)(2,1)S(1)} %copy-done.28), channel_id=1, source_target_pairs={{0,1},{1,0},{2,3},{3,2},{4,5},{5,4},{6,7},{7,6},{8,9},{9,8},{10,11... | collective-permute-start | bytes 2359304 | tf_op jit(solution)/shard_map/cond/branch_1_fun/ppermute | solution.py:1024
  41.6 23.9 %collective-permute-start.48 = (bf16[256,1536]{1,0:T(8,128)(2,1)}, bf16[256,1536]{1,0:T(8,128)(2,1)}, u32[]{:S(2)}, u32[]{:S(2)}) collective-permute-start(bf16[256,1536]{1,0:T(8,128)(2,1)} %get-tuple-element.395.refs_0_), channel_id=1, source_target_pairs={{0,1},{1,0},{2,3},{3,2},{4,5},{5,4},{6,7},{7,6},{8,9},{9,8},{10,11... | collective-permute-start | bytes 2359304 | tf_op jit(solution)/shard_map/cond/branch_1_fun/ppermute | solution.py:1024
  41.8 23.7 %collective-permute-start.49 = (bf16[256,1536]{1,0:T(8,128)(2,1)}, bf16[256,1536]{1,0:T(8,128)(2,1)}, u32[]{:S(2)}, u32[]{:S(2)}) collective-permute-start(bf16[256,1536]{1,0:T(8,128)(2,1)} %get-tuple-element.396.refs_1_), channel_id=1, source_target_pairs={{0,1},{1,0},{2,3},{3,2},{4,5},{5,4},{6,7},{7,6},{8,9},{9,8},{10,11... | collective-permute-start | bytes 2359304 | tf_op jit(solution)/shard_map/cond/branch_1_fun/ppermute | solution.py:1024
  44.2 21.4 %collective-permute-start.45 = (bf16[128,1536]{1,0:T(8,128)(2,1)}, bf16[128,1536]{1,0:T(8,128)(2,1)}, u32[]{:S(2)}, u32[]{:S(2)}) collective-permute-start(bf16[128,1536]{1,0:T(8,128)(2,1)} %get-tuple-element.397), channel_id=1, source_target_pairs={{0,4},{4,0},{1,5},{5,1},{2,6},{6,2},{3,7},{7,3},{8,12},{12,8},{9,1... | collective-permute-start | bytes 1179656 | tf_op jit(solution)/shard_map/cond/branch_1_fun/ppermute | solution.py:1024
  45.9 19.7 %collective-permute-start.46 = (bf16[128,1536]{1,0:T(8,128)(2,1)}, bf16[128,1536]{1,0:T(8,128)(2,1)}, u32[]{:S(2)}, u32[]{:S(2)}) collective-permute-start(bf16[128,1536]{1,0:T(8,128)(2,1)} %get-tuple-element.398), channel_id=1, source_target_pairs={{0,2},{2,0},{1,3},{3,1},{4,6},{6,4},{5,7},{7,5},{8,10},{10,8},{9,1... | collective-permute-start | bytes 1179656 | tf_op jit(solution)/shard_map/cond/branch_1_fun/ppermute | solution.py:1024
  65.6 175.1 %all-gather.6.cloned.1.call-start = ((), (), s32[]{:S(2)}) async-start(), calls=%async_computation.7 | async-start | bytes 4423680 | tf_op jit(solution)/shard_map/all_gather | solution.py:1074
  84.3 256.7 %reduce-scatter.4.cloned.1.call-start = ((), (), s32[]{:S(2)}) async-start(), calls=%async_computation.9 | async-start | bytes 5898240 | tf_op jit(solution)/shard_map/reduce_scatter | solution.py:1078
  89.1 30.2 %collective-permute-start.5 = (bf16[192,1536]{1,0:T(8,128)(2,1)S(1)}, bf16[192,1536]{1,0:T(8,128)(2,1)}, u32[]{:S(2)}, u32[]{:S(2)}) collective-permute-start(bf16[192,1536]{1,0:T(8,128)(2,1)S(1)} %get-tuple-element.403), channel_id=1, source_target_pairs={{0,1},{1,0},{2,3},{3,2},{4,5},{5,4},{6,7},{7,6},{8,9},{9,8},{10,11... | collective-permute-start | bytes 1769480 | tf_op jit(solution)/shard_map/cond/branch_1_fun/ppermute | solution.py:1024
  89.5 29.7 %collective-permute-start.4 = (bf16[192,1536]{1,0:T(8,128)(2,1)S(1)}, bf16[192,1536]{1,0:T(8,128)(2,1)}, u32[]{:S(2)}, u32[]{:S(2)}) collective-permute-start(bf16[192,1536]{1,0:T(8,128)(2,1)S(1)} %get-tuple-element.403), channel_id=1, source_target_pairs={{0,6},{2,4},{4,2},{6,0},{1,7},{3,5},{5,3},{7,1},{8,14},{10,12},{12... | collective-permute-start | bytes 1769480 | tf_op jit(solution)/shard_map/cond/branch_1_fun/ppermute | solution.py:1050
  90.3 28.9 %collective-permute-start.3 = (bf16[192,1536]{1,0:T(8,128)(2,1)S(1)}, bf16[192,1536]{1,0:T(8,128)(2,1)}, u32[]{:S(2)}, u32[]{:S(2)}) collective-permute-start(bf16[192,1536]{1,0:T(8,128)(2,1)S(1)} %get-tuple-element.403), channel_id=1, source_target_pairs={{0,4},{4,0},{1,5},{5,1},{2,6},{6,2},{3,7},{7,3},{8,12},{12,8},{9,1... | collective-permute-start | bytes 1769480 | tf_op jit(solution)/shard_map/cond/branch_1_fun/ppermute | solution.py:1024
  91.8 27.4 %collective-permute-start.2 = (bf16[192,1536]{1,0:T(8,128)(2,1)S(1)}, bf16[192,1536]{1,0:T(8,128)(2,1)}, u32[]{:S(2)}, u32[]{:S(2)}) collective-permute-start(bf16[192,1536]{1,0:T(8,128)(2,1)S(1)} %get-tuple-element.403), channel_id=1, source_target_pairs={{0,2},{2,0},{1,3},{3,1},{4,6},{6,4},{5,7},{7,5},{8,10},{10,8},{9,1... | collective-permute-start | bytes 1769480 | tf_op jit(solution)/shard_map/cond/branch_1_fun/ppermute | solution.py:1024
  119.3 8.8 %collective-permute-start.8 = (bf16[384,256]{1,0:T(8,128)(2,1)S(1)}, bf16[384,256]{1,0:T(8,128)(2,1)S(1)}, u32[]{:S(2)}, u32[]{:S(2)}) collective-permute-start(bf16[384,256]{1,0:T(8,128)(2,1)S(1)} %bitcast.113), channel_id=1, source_target_pairs={{0,6},{2,4},{4,2},{6,0},{1,7},{3,5},{5,3},{7,1},{8,14},{10,12},{12... | collective-permute-start | bytes 589832 | tf_op jit(solution)/shard_map/cond/branch_1_fun/ppermute | solution.py:1050
  120.3 9.7 %collective-permute-start.7 = (bf16[384,256]{1,0:T(8,128)(2,1)S(1)}, bf16[384,256]{1,0:T(8,128)(2,1)S(1)}, u32[]{:S(2)}, u32[]{:S(2)}) collective-permute-start(bf16[384,256]{1,0:T(8,128)(2,1)S(1)} %bitcast.114), channel_id=1, source_target_pairs={{0,4},{4,0},{1,5},{5,1},{2,6},{6,2},{3,7},{7,3},{8,12},{12,8},{9,1... | collective-permute-start | bytes 589832 | tf_op jit(solution)/shard_map/cond/branch_1_fun/ppermute | solution.py:1024
  121.6 8.9 %collective-permute-start.6 = (bf16[384,256]{1,0:T(8,128)(2,1)S(1)}, bf16[384,256]{1,0:T(8,128)(2,1)S(1)}, u32[]{:S(2)}, u32[]{:S(2)}) collective-permute-start(bf16[384,256]{1,0:T(8,128)(2,1)S(1)} %bitcast.115), channel_id=1, source_target_pairs={{0,2},{2,0},{1,3},{3,1},{4,6},{6,4},{5,7},{7,5},{8,10},{10,8},{9,1... | collective-permute-start | bytes 589832 | tf_op jit(solution)/shard_map/cond/branch_1_fun/ppermute | solution.py:1024
  122.9 13.3 %collective-permute-start.12 = (bf16[192,1536]{1,0:T(8,128)(2,1)}, bf16[192,1536]{1,0:T(8,128)(2,1)}, u32[]{:S(2)}, u32[]{:S(2)}) collective-permute-start(bf16[192,1536]{1,0:T(8,128)(2,1)} %get-tuple-element.436.refs_11_), channel_id=1, source_target_pairs={{0,1},{1,0},{2,3},{3,2},{4,5},{5,4},{6,7},{7,6},{8,9},{9,8},{10,11... | collective-permute-start | bytes 1769480 | tf_op jit(solution)/shard_map/cond/branch_1_fun/ppermute | solution.py:1024
  133.0 13.3 %collective-permute-start.18 = (bf16[256,1536]{1,0:T(8,128)(2,1)S(1)}, bf16[256,1536]{1,0:T(8,128)(2,1)}, u32[]{:S(2)}, u32[]{:S(2)}) collective-permute-start(bf16[256,1536]{1,0:T(8,128)(2,1)S(1)} %get-tuple-element.442), channel_id=1, source_target_pairs={{0,1},{1,0},{2,3},{3,2},{4,5},{5,4},{6,7},{7,6},{8,9},{9,8},{10,11... | collective-permute-start | bytes 2359304 | tf_op jit(solution)/shard_map/cond/branch_1_fun/ppermute | solution.py:1024
  134.5 20.7 %collective-permute-start.17 = (bf16[256,1536]{1,0:T(8,128)(2,1)}, bf16[256,1536]{1,0:T(8,128)(2,1)}, u32[]{:S(2)}, u32[]{:S(2)}) collective-permute-start(bf16[256,1536]{1,0:T(8,128)(2,1)} %after.3), channel_id=1, source_target_pairs={{0,4},{4,0},{1,5},{5,1},{2,6},{6,2},{3,7},{7,3},{8,12},{12,8},{9,1... | collective-permute-start | bytes 2359304 | tf_op jit(solution)/shard_map/cond/branch_1_fun/ppermute | solution.py:1024
  135.3 20.8 %collective-permute-start.16 = (bf16[256,1536]{1,0:T(8,128)(2,1)}, bf16[256,1536]{1,0:T(8,128)(2,1)}, u32[]{:S(2)}, u32[]{:S(2)}) collective-permute-start(bf16[256,1536]{1,0:T(8,128)(2,1)} %after.3), channel_id=1, source_target_pairs={{0,2},{2,0},{1,3},{3,1},{4,6},{6,4},{5,7},{7,5},{8,10},{10,8},{9,1... | collective-permute-start | bytes 2359304 | tf_op jit(solution)/shard_map/cond/branch_1_fun/ppermute | solution.py:1024
  144.9 11.2 %collective-permute-start.15 = (bf16[256,1536]{1,0:T(8,128)(2,1)}, bf16[256,1536]{1,0:T(8,128)(2,1)}, u32[]{:S(2)}, u32[]{:S(2)}) collective-permute-start(bf16[256,1536]{1,0:T(8,128)(2,1)} %get-tuple-element.1194), channel_id=1, source_target_pairs={{0,1},{1,0},{2,3},{3,2},{4,5},{5,4},{6,7},{7,6},{8,9},{9,8},{10,11... | collective-permute-start | bytes 2359304 | tf_op jit(solution)/shard_map/cond/branch_1_fun/ppermute | solution.py:1024
  145.1 26.1 %collective-permute-start.14 = (bf16[256,1536]{1,0:T(8,128)(2,1)}, bf16[256,1536]{1,0:T(8,128)(2,1)}, u32[]{:S(2)}, u32[]{:S(2)}) collective-permute-start(bf16[256,1536]{1,0:T(8,128)(2,1)} %get-tuple-element.1194), channel_id=1, source_target_pairs={{0,4},{4,0},{1,5},{5,1},{2,6},{6,2},{3,7},{7,3},{8,12},{12,8},{9,1... | collective-permute-start | bytes 2359304 | tf_op jit(solution)/shard_map/cond/branch_1_fun/ppermute | solution.py:1024
  146.4 25.3 %collective-permute-start.13 = (bf16[256,1536]{1,0:T(8,128)(2,1)}, bf16[256,1536]{1,0:T(8,128)(2,1)}, u32[]{:S(2)}, u32[]{:S(2)}) collective-permute-start(bf16[256,1536]{1,0:T(8,128)(2,1)} %get-tuple-element.1194), channel_id=1, source_target_pairs={{0,2},{2,0},{1,3},{3,1},{4,6},{6,4},{5,7},{7,5},{8,10},{10,8},{9,1... | collective-permute-start | bytes 2359304 | tf_op jit(solution)/shard_map/cond/branch_1_fun/ppermute | solution.py:1024
  155.2 16.5 %collective-permute-start.20 = (bf16[256,1536]{1,0:T(8,128)(2,1)}, bf16[256,1536]{1,0:T(8,128)(2,1)}, u32[]{:S(2)}, u32[]{:S(2)}) collective-permute-start(bf16[256,1536]{1,0:T(8,128)(2,1)} %collective-permute-done.17), channel_id=1, source_target_pairs={{0,1},{1,0},{2,3},{3,2},{4,5},{5,4},{6,7},{7,6},{8,9},{9,8},{10,11... | collective-permute-start | bytes 2359304 | tf_op jit(solution)/shard_map/cond/branch_1_fun/ppermute | solution.py:1024
  156.1 15.6 %collective-permute-start.19 = (bf16[256,1536]{1,0:T(8,128)(2,1)}, bf16[256,1536]{1,0:T(8,128)(2,1)}, u32[]{:S(2)}, u32[]{:S(2)}) collective-permute-start(bf16[256,1536]{1,0:T(8,128)(2,1)} %collective-permute-done.16), channel_id=1, source_target_pairs={{0,1},{1,0},{2,3},{3,2},{4,5},{5,4},{6,7},{7,6},{8,9},{9,8},{10,11... | collective-permute-start | bytes 2359304 | tf_op jit(solution)/shard_map/cond/branch_1_fun/ppermute | solution.py:1024
  174.3 18.6 %collective-permute-start.21 = (bf16[256,1536]{1,0:T(8,128)(2,1)}, bf16[256,1536]{1,0:T(8,128)(2,1)}, u32[]{:S(2)}, u32[]{:S(2)}) collective-permute-start(bf16[256,1536]{1,0:T(8,128)(2,1)} %get-tuple-element.447), channel_id=1, source_target_pairs={{0,4},{4,0},{1,5},{5,1},{2,6},{6,2},{3,7},{7,3},{8,12},{12,8},{9,1... | collective-permute-start | bytes 2359304 | tf_op jit(solution)/shard_map/cond/branch_1_fun/ppermute | solution.py:1024
  175.5 18.6 %collective-permute-start.22 = (bf16[256,1536]{1,0:T(8,128)(2,1)}, bf16[256,1536]{1,0:T(8,128)(2,1)}, u32[]{:S(2)}, u32[]{:S(2)}) collective-permute-start(bf16[256,1536]{1,0:T(8,128)(2,1)} %get-tuple-element.448), channel_id=1, source_target_pairs={{0,2},{2,0},{1,3},{3,1},{4,6},{6,4},{5,7},{7,5},{8,10},{10,8},{9,1... | collective-permute-start | bytes 2359304 | tf_op jit(solution)/shard_map/cond/branch_1_fun/ppermute | solution.py:1024
  176.4 17.7 %collective-permute-start.23 = (bf16[256,1536]{1,0:T(8,128)(2,1)}, bf16[256,1536]{1,0:T(8,128)(2,1)}, u32[]{:S(2)}, u32[]{:S(2)}) collective-permute-start(bf16[256,1536]{1,0:T(8,128)(2,1)} %get-tuple-element.443.refs_0_.refs_1_), channel_id=1, source_target_pairs={{0,1},{1,0},{2,3},{3,2},{4,5},{5,4},{6,7},{7,6},{8,9},{9,8},{10,11... | collective-permute-start | bytes 2359304 | tf_op jit(solution)/shard_map/cond/branch_1_fun/ppermute | solution.py:1024
  176.4 17.7 %collective-permute-start.24 = (bf16[256,1536]{1,0:T(8,128)(2,1)}, bf16[256,1536]{1,0:T(8,128)(2,1)}, u32[]{:S(2)}, u32[]{:S(2)}) collective-permute-start(bf16[256,1536]{1,0:T(8,128)(2,1)} %get-tuple-element.444.refs_1_.refs_2_), channel_id=1, source_target_pairs={{0,1},{1,0},{2,3},{3,2},{4,5},{5,4},{6,7},{7,6},{8,9},{9,8},{10,11... | collective-permute-start | bytes 2359304 | tf_op jit(solution)/shard_map/cond/branch_1_fun/ppermute | solution.py:1024
  200.0 35.0 %collective-permute-start.26 = (bf16[320,1536]{1,0:T(8,128)(2,1)}, bf16[320,1536]{1,0:T(8,128)(2,1)}, u32[]{:S(2)}, u32[]{:S(2)}) collective-permute-start(bf16[320,1536]{1,0:T(8,128)(2,1)} %get-tuple-element.478), channel_id=1, source_target_pairs={{0,4},{4,0},{1,5},{5,1},{2,6},{6,2},{3,7},{7,3},{8,12},{12,8},{9,1... | collective-permute-start | bytes 2949128 | tf_op jit(solution)/shard_map/cond/branch_1_fun/ppermute | solution.py:1024
  200.6 34.4 %collective-permute-start.25 = (bf16[320,1536]{1,0:T(8,128)(2,1)}, bf16[320,1536]{1,0:T(8,128)(2,1)}, u32[]{:S(2)}, u32[]{:S(2)}) collective-permute-start(bf16[320,1536]{1,0:T(8,128)(2,1)} %get-tuple-element.478), channel_id=1, source_target_pairs={{0,2},{2,0},{1,3},{3,1},{4,6},{6,4},{5,7},{7,5},{8,10},{10,8},{9,1... | collective-permute-start | bytes 2949128 | tf_op jit(solution)/shard_map/cond/branch_1_fun/ppermute | solution.py:1024
  235.0 170.1 %reduce-scatter.6.cloned.1.call-start = ((), (), s32[]{:S(2)}) async-start(), calls=%async_computation.10 | async-start | bytes 4423680 | tf_op jit(solution)/shard_map/reduce_scatter | solution.py:1078
  243.0 19.1 %collective-permute-start.27 = (bf16[160,1536]{1,0:T(8,128)(2,1)}, bf16[160,1536]{1,0:T(8,128)(2,1)}, u32[]{:S(2)}, u32[]{:S(2)}) collective-permute-start(bf16[160,1536]{1,0:T(8,128)(2,1)} %get-tuple-element.481), channel_id=1, source_target_pairs={{0,4},{4,0},{1,5},{5,1},{2,6},{6,2},{3,7},{7,3},{8,12},{12,8},{9,1... | collective-permute-start | bytes 1474568 | tf_op jit(solution)/shard_map/cond/branch_1_fun/ppermute | solution.py:1024
  244.4 17.6 %collective-permute-start.28 = (bf16[160,1536]{1,0:T(8,128)(2,1)}, bf16[160,1536]{1,0:T(8,128)(2,1)}, u32[]{:S(2)}, u32[]{:S(2)}) collective-permute-start(bf16[160,1536]{1,0:T(8,128)(2,1)} %get-tuple-element.482), channel_id=1, source_target_pairs={{0,2},{2,0},{1,3},{3,1},{4,6},{6,4},{5,7},{7,5},{8,10},{10,8},{9,1... | collective-permute-start | bytes 1474568 | tf_op jit(solution)/shard_map/cond/branch_1_fun/ppermute | solution.py:1024
  262.0 10.3 %collective-permute-start.61 = (bf16[1024,1536]{1,0:T(8,128)(2,1)}, bf16[1024,1536]{1,0:T(8,128)(2,1)S(1)}, u32[]{:S(2)}, u32[]{:S(2)}) collective-permute-start(bf16[1024,1536]{1,0:T(8,128)(2,1)} %get-tuple-element.825.refs_8_), channel_id=1, source_target_pairs={{0,1},{1,0},{2,3},{3,2},{4,5},{5,4},{6,7},{7,6},{8,9},{9,8},{10,11... | collective-permute-start | bytes 9437192 | tf_op jit(solution)/shard_map/ppermute | solution.py:1024
  279.8 30.3 %collective-permute-start.29 = (bf16[256,1536]{1,0:T(8,128)(2,1)}, bf16[256,1536]{1,0:T(8,128)(2,1)}, u32[]{:S(2)}, u32[]{:S(2)}) collective-permute-start(bf16[256,1536]{1,0:T(8,128)(2,1)} %get-tuple-element.500), channel_id=1, source_target_pairs={{0,2},{2,0},{1,3},{3,1},{4,6},{6,4},{5,7},{7,5},{8,10},{10,8},{9,1... | collective-permute-start | bytes 2359304 | tf_op jit(solution)/shard_map/cond/branch_1_fun/ppermute | solution.py:1024
  280.4 29.6 %collective-permute-start.30 = (bf16[256,1536]{1,0:T(8,128)(2,1)}, bf16[256,1536]{1,0:T(8,128)(2,1)}, u32[]{:S(2)}, u32[]{:S(2)}) collective-permute-start(bf16[256,1536]{1,0:T(8,128)(2,1)} %get-tuple-element.501), channel_id=1, source_target_pairs={{0,4},{4,0},{1,5},{5,1},{2,6},{6,2},{3,7},{7,3},{8,12},{12,8},{9,1... | collective-permute-start | bytes 2359304 | tf_op jit(solution)/shard_map/cond/branch_1_fun/ppermute | solution.py:1024
  280.5 37.6 %collective-permute-start.31 = (bf16[256,1536]{1,0:T(8,128)(2,1)}, bf16[256,1536]{1,0:T(8,128)(2,1)}, u32[]{:S(2)}, u32[]{:S(2)}) collective-permute-start(bf16[256,1536]{1,0:T(8,128)(2,1)} %get-tuple-element.502), channel_id=1, source_target_pairs={{0,6},{2,4},{4,2},{6,0},{1,7},{3,5},{5,3},{7,1},{8,14},{10,12},{12... | collective-permute-start | bytes 2359304 | tf_op jit(solution)/shard_map/cond/branch_1_fun/ppermute | solution.py:1050
  318.2 134.9 %reduce-scatter.8.cloned.1.call-start = ((), (), s32[]{:S(2)}) async-start(), calls=%async_computation.11 | async-start | bytes 2457600 | tf_op jit(solution)/shard_map/reduce_scatter | solution.py:1078
  318.6 64.0 %collective-permute-start.67 = (bf16[1024,1536]{1,0:T(8,128)(2,1)}, bf16[1024,1536]{1,0:T(8,128)(2,1)}, u32[]{:S(2)}, u32[]{:S(2)}) collective-permute-start(bf16[1024,1536]{1,0:T(8,128)(2,1)} %get-tuple-element.876), channel_id=1, source_target_pairs={{0,1},{1,0},{2,3},{3,2},{4,5},{5,4},{6,7},{7,6},{8,9},{9,8},{10,11... | collective-permute-start | bytes 9437192 | tf_op jit(solution)/shard_map/ppermute | solution.py:1024
  327.2 7.8 %collective-permute-start.63 = (bf16[384,256]{1,0:T(8,128)(2,1)S(1)}, bf16[384,256]{1,0:T(8,128)(2,1)S(1)}, u32[]{:S(2)}, u32[]{:S(2)}) collective-permute-start(bf16[384,256]{1,0:T(8,128)(2,1)S(1)} %bitcast.80), channel_id=1, source_target_pairs={{0,4},{4,0},{1,5},{5,1},{2,6},{6,2},{3,7},{7,3},{8,12},{12,8},{9,1... | collective-permute-start | bytes 589832 | tf_op jit(solution)/shard_map/ppermute | solution.py:1024
  327.8 10.5 %collective-permute-start.62 = (bf16[384,256]{1,0:T(8,128)(2,1)S(1)}, bf16[384,256]{1,0:T(8,128)(2,1)S(1)}, u32[]{:S(2)}, u32[]{:S(2)}) collective-permute-start(bf16[384,256]{1,0:T(8,128)(2,1)S(1)} %bitcast.79), channel_id=1, source_target_pairs={{0,2},{2,0},{1,3},{3,1},{4,6},{6,4},{5,7},{7,5},{8,10},{10,8},{9,1... | collective-permute-start | bytes 589832 | tf_op jit(solution)/shard_map/ppermute | solution.py:1024
  328.1 10.1 %collective-permute-start.64 = (bf16[384,256]{1,0:T(8,128)(2,1)S(1)}, bf16[384,256]{1,0:T(8,128)(2,1)S(1)}, u32[]{:S(2)}, u32[]{:S(2)}) collective-permute-start(bf16[384,256]{1,0:T(8,128)(2,1)S(1)} %bitcast.78), channel_id=1, source_target_pairs={{0,6},{2,4},{4,2},{6,0},{1,7},{3,5},{5,3},{7,1},{8,14},{10,12},{12... | collective-permute-start | bytes 589832 | tf_op jit(solution)/shard_map/ppermute | solution.py:1050
  341.1 20.0 %collective-permute-start.51 = (bf16[256,1536]{1,0:T(8,128)(2,1)}, bf16[256,1536]{1,0:T(8,128)(2,1)}, u32[]{:S(2)}, u32[]{:S(2)}) collective-permute-start(bf16[256,1536]{1,0:T(8,128)(2,1)} %get-tuple-element.530), channel_id=1, source_target_pairs={{0,4},{4,0},{1,5},{5,1},{2,6},{6,2},{3,7},{7,3},{8,12},{12,8},{9,1... | collective-permute-start | bytes 2359304 | tf_op jit(solution)/shard_map/cond/branch_1_fun/ppermute | solution.py:1024
  342.6 19.6 %collective-permute-start.50 = (bf16[256,1536]{1,0:T(8,128)(2,1)}, bf16[256,1536]{1,0:T(8,128)(2,1)}, u32[]{:S(2)}, u32[]{:S(2)}) collective-permute-start(bf16[256,1536]{1,0:T(8,128)(2,1)} %get-tuple-element.530), channel_id=1, source_target_pairs={{0,2},{2,0},{1,3},{3,1},{4,6},{6,4},{5,7},{7,5},{8,10},{10,8},{9,1... | collective-permute-start | bytes 2359304 | tf_op jit(solution)/shard_map/cond/branch_1_fun/ppermute | solution.py:1024
  343.2 19.0 %collective-permute-start.52 = (bf16[256,1536]{1,0:T(8,128)(2,1)}, bf16[256,1536]{1,0:T(8,128)(2,1)}, u32[]{:S(2)}, u32[]{:S(2)}) collective-permute-start(bf16[256,1536]{1,0:T(8,128)(2,1)} %get-tuple-element.530), channel_id=1, source_target_pairs={{0,1},{1,0},{2,3},{3,2},{4,5},{5,4},{6,7},{7,6},{8,9},{9,8},{10,11... | collective-permute-start | bytes 2359304 | tf_op jit(solution)/shard_map/cond/branch_1_fun/ppermute | solution.py:1024
  362.2 17.6 %collective-permute-start.34 = (bf16[256,1536]{1,0:T(8,128)(2,1)}, bf16[256,1536]{1,0:T(8,128)(2,1)}, u32[]{:S(2)}, u32[]{:S(2)}) collective-permute-start(bf16[256,1536]{1,0:T(8,128)(2,1)} %get-tuple-element.550), channel_id=1, source_target_pairs={{0,1},{1,0},{2,3},{3,2},{4,5},{5,4},{6,7},{7,6},{8,9},{9,8},{10,11... | collective-permute-start | bytes 2359304 | tf_op jit(solution)/shard_map/cond/branch_1_fun/ppermute | solution.py:1024
  362.3 20.3 %collective-permute-start.32 = (bf16[256,1536]{1,0:T(8,128)(2,1)}, bf16[256,1536]{1,0:T(8,128)(2,1)}, u32[]{:S(2)}, u32[]{:S(2)}) collective-permute-start(bf16[256,1536]{1,0:T(8,128)(2,1)} %get-tuple-element.548), channel_id=1, source_target_pairs={{0,2},{2,0},{1,3},{3,1},{4,6},{6,4},{5,7},{7,5},{8,10},{10,8},{9,1... | collective-permute-start | bytes 2359304 | tf_op jit(solution)/shard_map/cond/branch_1_fun/ppermute | solution.py:1024
  363.0 19.6 %collective-permute-start.35 = (bf16[256,1536]{1,0:T(8,128)(2,1)}, bf16[256,1536]{1,0:T(8,128)(2,1)}, u32[]{:S(2)}, u32[]{:S(2)}) collective-permute-start(bf16[256,1536]{1,0:T(8,128)(2,1)} %get-tuple-element.548), channel_id=1, source_target_pairs={{0,1},{1,0},{2,3},{3,2},{4,5},{5,4},{6,7},{7,6},{8,9},{9,8},{10,11... | collective-permute-start | bytes 2359304 | tf_op jit(solution)/shard_map/cond/branch_1_fun/ppermute | solution.py:1024
  363.1 16.7 %collective-permute-start.33 = (bf16[192,1536]{1,0:T(8,128)(2,1)}, bf16[192,1536]{1,0:T(8,128)(2,1)}, u32[]{:S(2)}, u32[]{:S(2)}) collective-permute-start(bf16[192,1536]{1,0:T(8,128)(2,1)} %get-tuple-element.549), channel_id=1, source_target_pairs={{0,4},{4,0},{1,5},{5,1},{2,6},{6,2},{3,7},{7,3},{8,12},{12,8},{9,1... | collective-permute-start | bytes 1769480 | tf_op jit(solution)/shard_map/cond/branch_1_fun/ppermute | solution.py:1024
  385.1 20.0 %collective-permute-start.38 = (bf16[640,256]{1,0:T(8,128)(2,1)}, bf16[640,256]{1,0:T(8,128)(2,1)}, u32[]{:S(2)}, u32[]{:S(2)}) collective-permute-start(bf16[640,256]{1,0:T(8,128)(2,1)} %get-tuple-element.569), channel_id=1, source_target_pairs={{0,6},{2,4},{4,2},{6,0},{1,7},{3,5},{5,3},{7,1},{8,14},{10,12},{12... | collective-permute-start | bytes 983048 | tf_op jit(solution)/shard_map/cond/branch_1_fun/ppermute | solution.py:1050
  386.3 18.8 %collective-permute-start.37 = (bf16[640,256]{1,0:T(8,128)(2,1)}, bf16[640,256]{1,0:T(8,128)(2,1)}, u32[]{:S(2)}, u32[]{:S(2)}) collective-permute-start(bf16[640,256]{1,0:T(8,128)(2,1)} %get-tuple-element.568), channel_id=1, source_target_pairs={{0,4},{4,0},{1,5},{5,1},{2,6},{6,2},{3,7},{7,3},{8,12},{12,8},{9,1... | collective-permute-start | bytes 983048 | tf_op jit(solution)/shard_map/cond/branch_1_fun/ppermute | solution.py:1024
  387.1 17.9 %collective-permute-start.36 = (bf16[640,256]{1,0:T(8,128)(2,1)}, bf16[640,256]{1,0:T(8,128)(2,1)}, u32[]{:S(2)}, u32[]{:S(2)}) collective-permute-start(bf16[640,256]{1,0:T(8,128)(2,1)} %get-tuple-element.567), channel_id=1, source_target_pairs={{0,2},{2,0},{1,3},{3,1},{4,6},{6,4},{5,7},{7,5},{8,10},{10,8},{9,1... | collective-permute-start | bytes 983048 | tf_op jit(solution)/shard_map/cond/branch_1_fun/ppermute | solution.py:1024
  407.1 19.9 %collective-permute-start.56 = (bf16[192,1152]{1,0:T(8,128)(2,1)S(1)}, bf16[192,1152]{1,0:T(8,128)(2,1)}, u32[]{:S(2)}, u32[]{:S(2)}) collective-permute-start(bf16[192,1152]{1,0:T(8,128)(2,1)S(1)} %constant_dynamic-slice_fusion.1), channel_id=1, source_target_pairs={{0,4},{4,0},{1,5},{5,1},{2,6},{6,2},{3,7},{7,3},{8,12},{12,8},{9,1... | collective-permute-start | bytes 1327112 | tf_op jit(solution)/shard_map/cond/branch_1_fun/ppermute | solution.py:1024
  409.6 17.5 %collective-permute-start.57 = (bf16[1280,256]{1,0:T(8,128)(2,1)}, bf16[1280,256]{1,0:T(8,128)(2,1)}, u32[]{:S(2)}, u32[]{:S(2)}) collective-permute-start(bf16[1280,256]{1,0:T(8,128)(2,1)} %far_parts.4), channel_id=1, source_target_pairs={{0,1},{1,0},{2,3},{3,2},{4,5},{5,4},{6,7},{7,6},{8,9},{9,8},{10,11... | collective-permute-start | bytes 1966088 | tf_op jit(solution)/shard_map/cond/branch_1_fun/ppermute | solution.py:1024
  410.4 11.8 %collective-permute-start.55 = (bf16[128,1536]{1,0:T(8,128)(2,1)}, bf16[128,1536]{1,0:T(8,128)(2,1)}, u32[]{:S(2)}, u32[]{:S(2)}) collective-permute-start(bf16[128,1536]{1,0:T(8,128)(2,1)} %get-tuple-element.1119), channel_id=1, source_target_pairs={{0,2},{2,0},{1,3},{3,1},{4,6},{6,4},{5,7},{7,5},{8,10},{10,8},{9,1... | collective-permute-start | bytes 1179656 | tf_op jit(solution)/shard_map/cond/branch_1_fun/ppermute | solution.py:1024
  411.6 15.5 %collective-permute-start.54 = (bf16[128,1536]{1,0:T(8,128)(2,1)S(1)}, bf16[128,1536]{1,0:T(8,128)(2,1)}, u32[]{:S(2)}, u32[]{:S(2)}) collective-permute-start(bf16[128,1536]{1,0:T(8,128)(2,1)S(1)} %get-tuple-element.1120), channel_id=1, source_target_pairs={{0,4},{4,0},{1,5},{5,1},{2,6},{6,2},{3,7},{7,3},{8,12},{12,8},{9,1... | collective-permute-start | bytes 1179656 | tf_op jit(solution)/shard_map/cond/branch_1_fun/ppermute | solution.py:1024
  431.4 19.8 %collective-permute-start.39 = (bf16[256,1536]{1,0:T(8,128)(2,1)}, bf16[256,1536]{1,0:T(8,128)(2,1)}, u32[]{:S(2)}, u32[]{:S(2)}) collective-permute-start(bf16[256,1536]{1,0:T(8,128)(2,1)} %get-tuple-element.606), channel_id=1, source_target_pairs={{0,2},{2,0},{1,3},{3,1},{4,6},{6,4},{5,7},{7,5},{8,10},{10,8},{9,1... | collective-permute-start | bytes 2359304 | tf_op jit(solution)/shard_map/cond/branch_1_fun/ppermute | solution.py:1024
  433.2 19.9 %collective-permute-start.40 = (bf16[256,1536]{1,0:T(8,128)(2,1)}, bf16[256,1536]{1,0:T(8,128)(2,1)}, u32[]{:S(2)}, u32[]{:S(2)}) collective-permute-start(bf16[256,1536]{1,0:T(8,128)(2,1)} %get-tuple-element.607), channel_id=1, source_target_pairs={{0,4},{4,0},{1,5},{5,1},{2,6},{6,2},{3,7},{7,3},{8,12},{12,8},{9,1... | collective-permute-start | bytes 2359304 | tf_op jit(solution)/shard_map/cond/branch_1_fun/ppermute | solution.py:1024
  454.1 7.3 %collective-permute-start.53 = (bf16[192,640]{1,0:T(8,128)(2,1)S(1)}, bf16[192,640]{1,0:T(8,128)(2,1)}, u32[]{:S(2)}, u32[]{:S(2)}) collective-permute-start(bf16[192,640]{1,0:T(8,128)(2,1)S(1)} %constant_dynamic-slice_fusion.2), channel_id=1, source_target_pairs={{0,4},{4,0},{1,5},{5,1},{2,6},{6,2},{3,7},{7,3},{8,12},{12,8},{9,1... | collective-permute-start | bytes 737288 | tf_op jit(solution)/shard_map/cond/branch_1_fun/ppermute | solution.py:1024
  (75 other events, 641.4 us)
Sparse Core Ops, SparseCore 0:
  36.9 43.8 all-gather.3
  82.4 88.2 all-gather.7
  172.3 68.4 all-gather.5
  242.9 83.8 reduce-scatter.3
  328.9 66.8 reduce-scatter.5
  406.6 38.8 reduce-scatter.7

commit v7 on v6

--- a/solution.py
+++ b/solution.py
@@ -604,33 +604,49 @@
     )(*args, *deps)
 
 
+def segments(lists):
+    edges = sorted({edge for bounds in lists for span in bounds for edge in span})
+    spans = []
+    for first, last in zip(edges[:-1], edges[1:]):
+        at = [
+            next(k for k, (start, stop) in enumerate(bounds) if start <= first < stop)
+            for bounds in lists
+        ]
+        spans.append((first, last, at))
+    return spans
+
+
 def project_back(lefts, weights, turns, cut, unit):
     number = len(weights)
-    sides = lefts[0]
-    count = len(sides)
     depth = weights[0].shape[0]
-    _, bounds = side_specs(tiles_of(sides), depth)
+    specs, lists, starts = [], [], []
+    for left in lefts:
+        starts.append(len(specs))
+        left_specs, bounds = side_specs(tiles_of(left), left[0].shape[1])
+        specs += left_specs
+        lists.append(bounds)
     out_specs, out_bounds = side_specs([unit * c // TILE for c in cut], depth)
+    count = len(specs)
 
     def body(*refs):
-        weight_refs = refs[number * count : number * count + number]
-        outs = refs[number * count + number :]
-
-        def run(k, m):
+        weight_refs, outs = refs[count : count + number], refs[count + number :]
+        step = pl.program_id(0)
+
+        def run(at):
             total = None
             for i, (first, last) in enumerate(turns):
-                part = dot(refs[i * count + k][...], weight_refs[i][:, first:last], 1, 1)
+                left = refs[starts[i] + at[i]][...]
+                part = dot(left, weight_refs[i][:, first:last], 1, 1)
                 total = part if total is None else total + part
-            outs[m][...] = total.astype(BF16)
-
-        on_shared(bounds, out_bounds, run)
-
-    widths = [left[0].shape[1] for left in lefts]
-    return pl.pallas_call(
-        body,
-        grid=(rows_of(sides) // TILE,),
-        in_specs=[spec for w in widths for spec in side_specs(tiles_of(sides), w)[0]]
-        + [entire(w) for w in weights],
+            outs[at[-1]][...] = total.astype(BF16)
+
+        for first, last, at in segments([*lists, out_bounds]):
+            pl.when(jnp.logical_and(step >= first, step < last))(lambda at=at: run(at))
+
+    return pl.pallas_call(
+        body,
+        grid=(rows_of(lefts[0]) // TILE,),
+        in_specs=specs + [entire(w) for w in weights],
         out_specs=out_specs,
         out_shape=[jax.ShapeDtypeStruct((unit * c, depth), BF16) for c in cut],
         name="project_back",
@@ -702,16 +718,16 @@
     return scale * (scaled - unit * jnp.mean(scaled * unit, axis=-1, keepdims=True)), unit
 
 
-def middle_back(mine, others, middle, upstream, weights, gains, deps=()):
+def middle_back(mine, far, others, middle, upstream, weights, gains):
     rows, depth = middle.shape
     width = weights[0].shape[0]
 
     def body(*refs):
-        mine_ref, first, second, third, middle_ref, up_ref = refs[:6]
-        weight_refs, gain_ref = refs[6:14], refs[14]
-        grad_ref, low_ref, *pair_refs, sum_ref, sums = refs[15 + len(deps) :]
-        post_grad = mine_ref[...].astype(F32)
-        for ref in (first, second, third):
+        parts, (middle_ref, up_ref) = refs[:5], refs[5:7]
+        weight_refs, gain_ref = refs[7:15], refs[15]
+        grad_ref, low_ref, *pair_refs, sum_ref, sums = refs[16:]
+        post_grad = parts[0][...].astype(F32)
+        for ref in parts[1:]:
             post_grad = post_grad + ref[...].astype(F32)
         back, unit = norm_back(middle_ref[...], gain_ref[1:2].astype(F32), post_grad)
         grad = up_ref[...].astype(F32) + back
@@ -740,10 +756,9 @@
     return pl.pallas_call(
         body,
         grid=(rows // TILE,),
-        in_specs=[row_tiles(a) for a in (mine, *others, middle, upstream)]
+        in_specs=[row_tiles(a) for a in (mine, far, *others, middle, upstream)]
         + [entire(w) for w in weights]
-        + [entire(gains)]
-        + [ANY] * len(deps),
+        + [entire(gains)],
         out_specs=[row_tiles(middle)] * 2
         + [side] * 4
         + [pl.BlockSpec((depth, GAIN_LANES), lambda i: (0, 0))],
@@ -757,7 +772,7 @@
         name="middle_back",
         cost_estimate=cost(0),
         compiler_params=pltpu.CompilerParams(vmem_limit_bytes=48 << 20),
-    )(mine, *others, middle, upstream, *weights, gains, *deps)
+    )(mine, far, *others, middle, upstream, *weights, gains)
 
 
 def input_back(pairs, weights, hidden, grads, gains, deps=()):
@@ -784,31 +799,29 @@
     )(*pair_args(pairs), *weights, hidden, grads, gains, *deps)
 
 
-def core_sum(near, far):
-    rows, width = far.shape[0] // 4, far.shape[1]
-
-    def body(three_ref, one_ref, far_ref, *outs):
+def sent_sums(sides, corner, far):
+    rows, width = corner.shape
+
+    def body(sides_ref, corner_ref, far_ref, *outs):
         for part, out in enumerate(outs):
 
             @pl.when(pl.program_id(0) == part)
-            def _(out=out, near_ref=three_ref if part < 3 else one_ref):
+            def _(out=out, near_ref=sides_ref if part < 2 else corner_ref):
                 out[...] = (near_ref[...].astype(F32) + far_ref[...].astype(F32)).astype(out.dtype)
 
-    def tile(last):
-        return pl.BlockSpec((rows, width), lambda i: (jnp.minimum(i, last), 0))
-
-    return pl.pallas_call(
-        body,
-        grid=(4,),
-        in_specs=[tile(2), tile(0), tile(3)],
-        out_specs=[tile(0)] * 4,
-        out_shape=[
-            jax.ShapeDtypeStruct((rows, width), BF16) for _ in range(4)
-        ],
-        name="core_sum",
+    def tile(last, first=0):
+        return pl.BlockSpec((rows, width), lambda i: (first + jnp.minimum(i, last), 0))
+
+    return pl.pallas_call(
+        body,
+        grid=(3,),
+        in_specs=[tile(1), tile(0), tile(2, 1)],
+        out_specs=[tile(0)] * 3,
+        out_shape=[jax.ShapeDtypeStruct((rows, width), BF16)] * 3,
+        name="sent_sums",
         cost_estimate=cost(0),
         compiler_params=pltpu.CompilerParams(vmem_limit_bytes=60 << 20),
-    )(*near, far)
+    )(sides, corner, far)
 
 
 def corner_sum(for_y, for_x, by_x, by_y):
@@ -1209,7 +1222,7 @@
     def first_blocks(post, grads, weight):
         corners = corners_come(post[1:], grads[1:])
         far = across(post[1:])
-        return corners, far, feed_forward(post, grads, weight, [3])
+        return corners, far, feed_forward(post, grads, weight, [1, 2])
 
     corners, far, early = together(first_blocks, post, grads, ffn_full[0])
     corner, grad_corner = joined(*corners, 2)
@@ -1229,33 +1242,44 @@
     both_0, act_0, total = [early[0], late[0]], [early[1], late[1]], early[2] + late[2]
     sums_0 = line_scatter(parts_0)
 
-    def second_chunk(post, grads, weight, total, qkv_sides):
-        qkv_corner = corners_come(qkv_sides)
+    own_total, sides_total, *late_total = total
+    qkv_halves = halves([qkv_sides])
+
+    def second_chunk(post, grads, weight, total, qkv_halves):
+        qkv_corner = swap(qkv_halves[0], "x"), swap(qkv_halves[1], "y")
         return qkv_corner, feed_forward(post, grads, weight, [1, 4], total)
 
     qkv_corner, late = together(
-        second_chunk, post[3:], grads[3:], ffn_full[1], total[1:], qkv_sides
+        second_chunk, post[3:], grads[3:], ffn_full[1], late_total, qkv_halves
     )
     far = swap(late[2][1], "c")
-    early = feed_forward(post[:3], grads[:3], ffn_full[1], [3], total[:1], late[2][1:])
-    both_1, act_1 = [early[0], late[0]], [early[1], late[1]]
-    mine, *parts = core_sum(early[2] + late[2][:1], far)
-
-    def behind(parts, post, grads, act_0, act_1, both_1, weights):
+    sides = feed_forward(post[1:3], grads[1:3], ffn_full[1], [2], [sides_total], late[2][1:])
+    parts = sent_sums(sides[2][0], late[2][0], far)
+
+    def behind(parts, post, grads, weights, own_total, act_0, act_1, both_1):
         others = diamond(*parts)
+        own = feed_forward(post[:1], grads[:1], weights[1], [1], [own_total])
+        both, act = [own[0], *both_1], [own[1], *act_1]
         columns = [(2 * weight.shape[1] // 3, weight.shape[1]) for weight in weights]
-        branch = project_back([act_0, act_1], weights, columns, [3, 1, 4], own_rows)
-        parts_1 = weight_grads([(post, both_1), (grads, act_1)])
-        return others, parts_1, branch
-
-    others, parts_1, branch = together(
-        behind, parts, post, grads, act_0, act_1, both_1, ffn_full
+        branch = project_back([act_0, act], weights, columns, [1, 2, 1, 4], own_rows)
+        parts_1 = weight_grads([(post, both), (grads, act)])
+        return others, own[2][0], parts_1, branch
+
+    others, mine, parts_1, branch = together(
+        behind,
+        parts,
+        post,
+        grads,
+        ffn_full,
+        own_total,
+        act_0,
+        [sides[1], late[1]],
+        [sides[0], late[0]],
     )
     middle_grad, middle_low, *pairs, feedforward_part = middle_back(
-        mine, others, middle, own_upstream, out_weights, gain_turned
-    )
-
-    branch_far = swap(branch[2], "c")
+        mine, far, others, middle, own_upstream, out_weights, gain_turned
+    )
+    branch_far = swap(branch[3], "c")
 
     mixed_grad = exchange_all(exchange_near([pair.reshape(-1, 4 * HEAD_DIM) for pair in pairs]))
 
@@ -1305,11 +1329,11 @@
             gains=(first_full, gain_parts, head_part, head_rows),
             paired=True,
         )
-        return came[1:], parts, core_sum(*branch)
-
-    came, attention_parts, branch = together(
+        return came[1:], parts, sent_sums(*branch)
+
+    came, attention_parts, sent = together(
         attention_grads,
-        (branch[:2], branch_far),
+        (*branch[1:3], branch_far),
         qkv_packs,
         qkv_grad,
         normed,
@@ -1320,7 +1344,7 @@
         head_part,
     )
     attention_sums = line_scatter(after(attention_parts, sums_1))
-    branch_mine, for_y, for_x, branch_corner = branch
+    for_y, for_x, branch_corner = sent
     middle_rows = own_rows // 2
 
     def corners(corner, sums_1, qkv_pair, came, qkv_corner):
@@ -1369,12 +1393,13 @@
         gain_turned,
     )
 
-    def last(attention_sums, middle, branch_mine, branch_others):
-        layer_output = (middle + scatter_end(branch_mine, branch_others)).astype(BF16)
+    def last(attention_sums, middle, branch_own, branch_far, branch_others):
+        parts = branch_far[:own_rows], *branch_others
+        layer_output = (middle + scatter_end(branch_own, parts)).astype(BF16)
         return swap(for_x_side(attention_sums), "x"), layer_output
 
     attention_other, layer_output = together(
-        last, attention_sums, middle, branch_mine, branch_others
+        last, attention_sums, middle, branch[0], branch_far, branch_others
     )
 
     key_first, value_first = query_cols, query_cols + kv_cols

time: 482 us -> 475 us (0.985)
  waiting for transfers between devices: 131 us -> 122 us
    ppermute x5, waiting for transfers between devices: 13.3 us -> 7.55 us  [opposite(): return lax.ppermute(rows, ('x', 'y'), ((0, 3), (1, 2), (2, 1), (3, 0)))]
    pallas_call x4 -> x5, Pallas kernels: 56.7 us -> 59.6 us  [feed_forward(): pl.pallas_call(body, grid=(rows // TILE,), in_specs=specs * 2 + [entire(w...]
  transfers between devices with their start and end apart: 79 -> 79, of which waited for: 32 -> 32; matrix products, arithmetic and copies ran while one was open for 2% -> 2% of each run, Pallas kernels for 48% -> 49%
where the time goes in v7:
time: 475 us; the launch traced here: 470 us
  Pallas kernels  237 us (50%)
  waiting for transfers between devices  122 us (26%)
  starting transfers between devices  62.2 us (13%)
  blocking collectives  16.6 us (3%)
  between operations  14.7 us (3%)
  local copies, waits for them, and re-layouts  12.2 us (3%)
  other arithmetic  5.39 us (1%)
    ppermute x65, waiting for transfers between devices, swap(): return lax.ppermute(values, axis, SWAP)  93.9 us
    pallas_call x5, Pallas kernels, feed_forward(): pl.pallas_call(body, grid=(rows // TILE,), in_specs=specs * 2 + [entire(w...  59.6 us
    ppermute x65, starting transfers between devices, swap(): return lax.ppermute(values, axis, SWAP)  43.3 us
    pallas_call x3, Pallas kernels, weight_grads(): pl.pallas_call(body, grid=(depth // tile,), in_specs=specs + [ANY] * len(...  39.5 us
    pallas_call x2, Pallas kernels, backward_attention(): pl.pallas_call(attend_backward, grid_spec=pltpu.PrefetchScalarGridSpec(nu...  31.5 us
    all_to_all x1, blocking collectives, plane_columns(): lax.all_to_all(payload, PLANE, split_axis=0, concat_axis=0, tiled=True)  16.6 us
    all_to_all x2, waiting for transfers between devices, plane_columns(): lax.all_to_all(payload, PLANE, split_axis=0, concat_axis=0, tiled=True)  15.9 us
    pallas_call x1, Pallas kernels, attention_call(): pl.pallas_call(body, grid_spec=pltpu.PrefetchScalarGridSpec(num_scalar_pr...  15.6 us
  transfers between devices with their start and end apart: 79, of which 32 were waited for; matrix products, arithmetic and copies ran while one was open for 2% of the time, Pallas kernels for 49%

profile of v7, /device:TPU:0, one launch (start us, length us, event | category | flops | bytes accessed | tf_op | source)
XLA Modules:
  0.0 470.4 jit_solution(5687846927382718573)
XLA Ops:
  9.2 27.5 %conditional.14 = (bf16[384,640]{1,0:T(8,128)(2,1)}, bf16[256,1536]{1,0:T(8,128)(2,1)}, bf16[256,1536]{1,0:T(8,128)(2,1)}, bf16[8,48,1536]{2,1,0:T(8,128)(2,1)}, bf16[8,48,1152]{2,1,0:T(8,128)(2,1)S(1)}) conditional(s32[]{:T(128)} %convert_element_type.49, () %tuple.138, (bf16[8,48,640]{2,1,0:T(8,128)(2,1)}, bf16[256,1536]{1,0:T(8,128)(2,1)}, ...), branch_computations={%region_0.0_spmd, %region_1.0_spmd} | conditional | bytes 7766168 | solution.py:1100
  9.2 2.9 collective-permute-start.1
  13.7 4.1 all-to-all-start
  17.8 3.1 pack_columns.2
  20.9 15.9 %all-to-all-done = bf16[8,48,640]{2,1,0:T(8,128)(2,1)} async-done(((bf16[8,48,640]{2,1,0:T(8,128)(2,1)}), bf16[8,48,640]{2,1,0:T(8,128)(2,1)}, u32[]{:S(2)}, u32[]{:S(2)}) %all-to-all-start) | async-done | bytes 491552 | tf_op jit(solution)/shard_map/cond/branch_1_fun/all_to_all | solution.py:1104
  36.8 28.8 %conditional.15 = (bf16[128,1536]{1,0:T(8,128)(2,1)}, bf16[128,1536]{1,0:T(8,128)(2,1)}, bf16[256,1536]{1,0:T(8,128)(2,1)}, bf16[256,1536]{1,0:T(8,128)(2,1)}, b...) conditional(s32[]{:T(128)} %convert_element_type.49, () %tuple.140, ...), branch_computations={%region_2.0_spmd, %region_3.0_spmd} | conditional | flops 33890 | bytes 19538502 | solution.py:1100
  36.9 4.4 all-to-all-start.1
  47.4 3.0 multiply_sine_fusion
  50.5 3.1 rotary_rows.1
  53.5 12.1 %collective-permute-done.45 = bf16[128,1536]{1,0:T(8,128)(2,1)} collective-permute-done((bf16[128,1536]{1,0:T(8,128)(2,1)}, bf16[128,1536]{1,0:T(8,128)(2,1)}, u32[]{:S(2)}, u32[]{:S(2)}) %collective-permute-start.45) | collective-permute-done | bytes 393248 | tf_op jit(solution)/shard_map/cond/branch_1_fun/ppermute | solution.py:1037
  66.9 16.6 %all_to_all.13 = bf16[8,48,1152]{2,1,0:T(8,128)(2,1)} all-to-all(bf16[8,48,1152]{2,1,0:T(8,128)(2,1)S(1)} %after.4), channel_id=1, replica_groups=mesh['dp'=4,'x'=2,'y'=2,'c'=2] {'x','y','c'}, dimensions={0} | all-to-all | bytes 1769472 | tf_op jit(solution)/shard_map/all_to_all | solution.py:1104
  83.7 3.5 turn.1
  88.0 30.3 %conditional.16 = (bf16[192,1536]{1,0:T(8,128)(2,1)}, bf16[192,1536]{1,0:T(8,128)(2,1)}, bf16[192,1536]{1,0:T(8,128)(2,1)}, bf16[192,1536]{1,0:T(8,128)(2,1)}, b...) conditional(s32[]{:T(128)} %convert_element_type.49, () %tuple.137, ...), branch_computations={%region_4.0_spmd, %region_5.0_spmd} | conditional | flops 2 | bytes 17826128 | solution.py:1100
  91.9 10.7 %norm_project.1 = (bf16[2048,1536]{1,0:T(8,128)(2,1)}, bf16[2048,320]{1,0:T(8,128)(2,1)}) custom-call(bf16[256,1536]{1,0:T(8,128)(2,1)} %get-tuple-element.408.refs_0_, bf16[256,1536]{1,0:T(8,128)(2,1)} %get-tuple-element.409.refs_1_, bf16[256,1536]{1,0:T(8,128)(2,1)} %get-tuple-element.410.refs_2_, bf16[256,1536]{1,0:T(8,128)(2,1)} %get-tuple-element.411.refs_3_, ...), custom_call_target="tpu_custom_call" | custom-call | flops 1 | bytes 1 | tf_op jit(solution)/shard_map/cond/branch_1_fun/norm_project/pallas_call | solution.py:438
  102.7 15.6 %attend_forward.1 = (bf16[2,1,256,192]{3,2,1,0:T(8,128)(2,1)}, bf16[2,1,256,192]{3,2,1,0:T(8,128)(2,1)}, bf16[2,1,256,192]{3,2,1,0:T(8,128)(2,1)}, bf16[2,1,256,...) custom-call(s32[1]{0:T(128)} %get-tuple-element.420.place_ref, ...), custom_call_target="tpu_custom_call" | custom-call | flops 1 | bytes 1 | tf_op jit(solution)/shard_map/cond/branch_1_fun/attend_forward/pallas_call | solution.py:256
  118.3 52.6 %conditional.17 = (f32[256,1536]{1,0:T(8,128)}, bf16[256,1536]{1,0:T(8,128)(2,1)}, bf16[256,1536]{1,0:T(8,128)(2,1)}, bf16[256,1536]{1,0:T(8,128)(2,1)}, bf16[25...) conditional(s32[]{:T(128)} %convert_element_type.49, () %tuple.136, ...), branch_computations={%region_6.0_spmd, %region_7.0_spmd} | conditional | flops 2 | bytes 47973280 | solution.py:1100
  121.9 5.3 %collective-permute-done.8.refs_3_ = bf16[384,256]{1,0:T(8,128)(2,1)S(1)} collective-permute-done((bf16[384,256]{1,0:T(8,128)(2,1)S(1)}, bf16[384,256]{1,0:T(8,128)(2,1)S(1)}, u32[]{:S(2)}, u32[]{:S(2)}) %collective-permute-start.8) | collective-permute-done | bytes 196640 | tf_op jit(solution)/shard_map/cond/branch_1_fun/ppermute | solution.py:1063
  138.6 5.5 %attend_out.1 = (f32[256,1536]{1,0:T(8,128)}, bf16[256,1536]{1,0:T(8,128)(2,1)}) custom-call(bf16[384,256]{1,0:T(8,128)(2,1)S(1)} %bitcast.100, bf16[384,256]{1,0:T(8,128)(2,1)S(1)} %copy-done.3, bf16[384,256]{1,0:T(8,128)(2,1)S(1)} %copy-done.7, bf16[384,256]{1,0:T(8,128)(2,1)S(1)} %copy-done.5, ...), custom_call_target="tpu_custom_call" | custom-call | flops 1 | bytes 1 | tf_op jit(solution)/shard_map/cond/branch_1_fun/attend_out/pallas_call | solution.py:697
  146.5 7.8 %collective-permute-done.17 = bf16[256,1536]{1,0:T(8,128)(2,1)} collective-permute-done((bf16[256,1536]{1,0:T(8,128)(2,1)}, bf16[256,1536]{1,0:T(8,128)(2,1)}, u32[]{:S(2)}, u32[]{:S(2)}) %collective-permute-start.17) | collective-permute-done | bytes 786464 | tf_op jit(solution)/shard_map/cond/branch_1_fun/ppermute | solution.py:1037
  155.3 15.0 %collective-permute-done.14 = bf16[256,1536]{1,0:T(8,128)(2,1)} collective-permute-done((bf16[256,1536]{1,0:T(8,128)(2,1)}, bf16[256,1536]{1,0:T(8,128)(2,1)}, u32[]{:S(2)}, u32[]{:S(2)}) %collective-permute-start.14) | collective-permute-done | bytes 786464 | tf_op jit(solution)/shard_map/cond/branch_1_fun/ppermute | solution.py:1037
  170.9 23.3 %conditional.18 = (bf16[256,1536]{1,0:T(8,128)(2,1)}, bf16[256,1536]{1,0:T(8,128)(2,1)}, bf16[256,1536]{1,0:T(8,128)(2,1)}, bf16[256,1536]{1,0:T(8,128)(2,1)}, b...) conditional(s32[]{:T(128)} %convert_element_type.49, () %tuple.144, ...), branch_computations={%region_8.0_spmd, %region_9.0_spmd} | conditional | flops 2 | bytes 12583138 | solution.py:1100
  170.9 2.6 halves.4
  176.8 12.8 %feed_forward.5 = (bf16[768,1024]{1,0:T(8,128)(2,1)}, bf16[768,512]{1,0:T(8,128)(2,1)}, bf16[256,1536]{1,0:T(8,128)(2,1)}, bf16[512,1536]{1,0:T(8,128)(2,1)}) custom-call(bf16[256,1536]{1,0:T(8,128)(2,1)} %get-tuple-element.453.refs_0_, bf16[256,1536]{1,0:T(8,128)(2,1)} %get-tuple-element.447.refs_0_.refs_1_, ...), custom_call_target="tpu_custom_call" | custom-call | flops 1 | bytes 1 | tf_op jit(solution)/shard_map/cond/branch_1_fun/feed_forward/pallas_call | solution.py:494
  189.6 3.4 collective-permute-done.21
  200.1 35.0 %conditional.19 = (bf16[1280,512]{1,0:T(8,128)(2,1)}, bf16[256,1536]{1,0:T(8,128)(2,1)}, bf16[1024,1536]{1,0:T(8,128)(2,1)}, bf16[1536,1536]{1,0:T(8,128)(2,1)},...) conditional(s32[]{:T(128)} %convert_element_type.49, () %tuple.147, (bf16[256,1536]{1,0:T(8,128)(2,1)S(1)}, ...), branch_computations={%region_10.0_spmd, %region_11.0_spmd} | conditional | flops 2 | bytes 17301690 | solution.py:1100
  202.1 17.9 %feed_forward.6 = (bf16[1280,1024]{1,0:T(8,128)(2,1)}, bf16[1280,512]{1,0:T(8,128)(2,1)}, bf16[256,1536]{1,0:T(8,128)(2,1)}, bf16[1024,1536]{1,0:T(8,128)(2,1)}) custom-call(bf16[256,1536]{1,0:T(8,128)(2,1)S(1)} %get-tuple-element.460.refs_0_.refs_3_, bf16[256,1536]{1,0:T(8,128)(2,1)} %get-tuple-element.461.refs_1_.refs_4_, ...), custom_call_target="tpu_custom_call" | custom-call | flops 1 | bytes 1 | tf_op jit(solution)/shard_map/cond/branch_1_fun/feed_forward/pallas_call | solution.py:494
  220.0 15.0 %weight_grads.3 = bf16[1536,1536]{1,0:T(8,128)(2,1)} custom-call(bf16[256,1536]{1,0:T(8,128)(2,1)} %get-tuple-element.474.refs_0_, bf16[256,1536]{1,0:T(8,128)(2,1)} %get-tuple-element.475.refs_1_, bf16[256,1536]{1,0:T(8,128)(2,1)} %get-tuple-element.476.refs_2_, bf16[256,1536]{1,0:T(8,128)(2,1)S(1)} %get-tuple-element.460.refs_0_.refs_3_, ...), custom_call_target="tpu_custom_call" | custom-call | flops 1 | bytes 1 | tf_op jit(solution)/shard_map/cond/branch_1_fun/weight_grads/pallas_call | solution.py:595
  235.1 2.2 halves.5
  237.3 3.4 all-gather.6.cloned.1.call-done.refs_4_
  240.8 18.4 %conditional.20 = (bf16[160,1536]{1,0:T(8,128)(2,1)}, bf16[160,1536]{1,0:T(8,128)(2,1)}, bf16[1280,768]{1,0:T(8,128)(2,1)}, bf16[1280,384]{1,0:T(8,128)(2,1)}, b...) conditional(s32[]{:T(128)} %convert_element_type.49, () %tuple.146, (bf16[160,1536]{1,0:T(8,128)(2,1)}, ...), branch_computations={%region_12.0_spmd, %region_13.0_spmd} | conditional | flops 1 | bytes 7864380 | solution.py:1100
  243.8 15.4 %feed_forward.7 = (bf16[1280,768]{1,0:T(8,128)(2,1)}, bf16[1280,384]{1,0:T(8,128)(2,1)}, bf16[256,1536]{1,0:T(8,128)(2,1)}, bf16[1024,1536]{1,0:T(8,128)(2,1)S(1)}) custom-call(bf16[256,1536]{1,0:T(8,128)(2,1)S(1)} %get-tuple-element.486.refs_0_, bf16[256,1536]{1,0:T(8,128)(2,1)} %get-tuple-element.487.refs_1_, ...), custom_call_target="tpu_custom_call" | custom-call | flops 1 | bytes 1 | tf_op jit(solution)/shard_map/cond/branch_1_fun/feed_forward/pallas_call | solution.py:494
  259.3 8.1 %feed_forward.9 = (bf16[512,768]{1,0:T(8,128)(2,1)}, bf16[512,384]{1,0:T(8,128)(2,1)}, bf16[512,1536]{1,0:T(8,128)(2,1)}) custom-call(bf16[256,1536]{1,0:T(8,128)(2,1)} %get-tuple-element.811.refs_0_, bf16[256,1536]{1,0:T(8,128)(2,1)} %get-tuple-element.812.refs_1_, bf16[256,1536]{1,0:T(8,128)(2,1)} %get-tuple-element.813.refs_2_, ...), custom_call_target="tpu_custom_call" | custom-call | flops 1 | bytes 1 | tf_op jit(solution)/shard_map/feed_forward/pallas_call | solution.py:494
  269.0 4.7 sent_sums.3
  273.7 38.3 %conditional.21 = (bf16[256,1536]{1,0:T(8,128)(2,1)}, bf16[256,1536]{1,0:T(8,128)(2,1)}, bf16[256,1536]{1,0:T(8,128)(2,1)}, bf16[256,1536]{1,0:T(8,128)(2,1)}, b...) conditional(s32[]{:T(128)} %convert_element_type.49, () %tuple.135, ...), branch_computations={%region_14.0_spmd, %region_15.0_spmd} | conditional | flops 3 | bytes 37749096 | solution.py:1100
  274.3 2.9 collective-permute-start.31
  277.2 5.3 %feed_forward.8 = (bf16[256,768]{1,0:T(8,128)(2,1)}, bf16[256,384]{1,0:T(8,128)(2,1)}, bf16[256,1536]{1,0:T(8,128)(2,1)}) custom-call(bf16[256,1536]{1,0:T(8,128)(2,1)} %get-tuple-element.506.refs_0_, bf16[256,1536]{1,0:T(8,128)(2,1)S(1)} %get-tuple-element.507.refs_1_.refs_11_, bf16[1536,1152]{1,0:T(8,128)(2,1)} %get-tuple-element.508.refs_2_.refs_6_, ...), custom_call_target="tpu_custom_call" | custom-call | flops 1 | bytes 1 | tf_op jit(solution)/shard_map/cond/branch_1_fun/feed_forward/pallas_call | solution.py:494
  282.5 13.5 %project_back.1 = (bf16[256,1536]{1,0:T(8,128)(2,1)}, bf16[512,1536]{1,0:T(8,128)(2,1)}, bf16[256,1536]{1,0:T(8,128)(2,1)}, bf16[1024,1536]{1,0:T(8,128)(2,1)}) custom-call(bf16[768,512]{1,0:T(8,128)(2,1)} %get-tuple-element.531.refs_0_, bf16[1280,512]{1,0:T(8,128)(2,1)} %get-tuple-element.532.refs_1_, bf16[256,384]{1,0:T(8,128)(2,1)} %get-tuple-element.528.refs_19_.refs_2_, ...), custom_call_target="tpu_custom_call" | custom-call | flops 1 | bytes 1 | tf_op jit(solution)/shard_map/cond/branch_1_fun/project_back/pallas_call | solution.py:646
  296.0 13.6 %weight_grads.4 = bf16[1536,1152]{1,0:T(8,128)(2,1)} custom-call(bf16[256,1536]{1,0:T(8,128)(2,1)} %get-tuple-element.506.refs_0_, bf16[256,1536]{1,0:T(8,128)(2,1)} %get-tuple-element.511.refs_1_, bf16[256,1536]{1,0:T(8,128)(2,1)} %get-tuple-element.512.refs_2_, bf16[256,1536]{1,0:T(8,128)(2,1)S(1)} %copy-done.16, ...), custom_call_target="tpu_custom_call" | custom-call | flops 1 | bytes 1 | tf_op jit(solution)/shard_map/cond/branch_1_fun/weight_grads/pallas_call | solution.py:595
  309.6 2.3 collective-permute-done.31
  313.8 8.1 %middle_back.1 = (f32[256,1536]{1,0:T(8,128)}, bf16[256,1536]{1,0:T(8,128)(2,1)}, bf16[2,192,256]{2,1,0:T(8,128)(2,1)S(1)}, bf16[2,192,256]{2,1,0:T(8,128)(2,1)S...) custom-call(bf16[256,1536]{1,0:T(8,128)(2,1)} %get-tuple-element.850.refs_0_, ...), custom_call_target="tpu_custom_call" | custom-call | flops 1 | bytes 1 | tf_op jit(solution)/shard_map/middle_back/pallas_call | solution.py:756
  322.6 2.9 collective-permute-start.64
  325.4 4.4 collective-permute-done.63.refs_2_
  329.8 2.9 collective-permute-done.62.refs_1_
  335.4 21.1 %conditional.22 = (bf16[256,1536]{1,0:T(8,128)(2,1)}, bf16[256,1536]{1,0:T(8,128)(2,1)}, bf16[256,1536]{1,0:T(8,128)(2,1)}, bf16[2,1,256,320]{3,2,1,0:T(8,128)(2...) conditional(s32[]{:T(128)} %convert_element_type.49, () %tuple.134, ...), branch_computations={%region_17.0_spmd, %region_18.0_spmd} | conditional | flops 9 | bytes 15335739 | solution.py:1100
  337.5 15.8 %attend_backward.2 = (bf16[2,1,256,320]{3,2,1,0:T(8,128)(2,1)}, bf16[2,1,256,320]{3,2,1,0:T(8,128)(2,1)}, bf16[2,1,320,256]{3,2,1,0:T(8,128)(2,1)S(1)}, bf16[2,1,320,256]{3,2,1,0:T(8,128)(2,1)}, f32[1,8,256]{2,1,0:T(8,128)S(1)}) custom-call(s32[1]{0:T(128)} %get-tuple-element.539.place_ref, bf16[2,2,2,1,256,320]{5,4,3,2,1,0:T(8,128)(2,1)} %bitcast.16.qkv_ref, ...), custom_call_target="tpu_custom_call" | custom-call | flops 1 | bytes 1 | tf_op jit(solution)/shard_map/cond/branch_1_fun/attend_backward/pallas_call | solution.py:320
  356.5 20.4 %conditional.23 = (bf16[256,1536]{1,0:T(8,128)(2,1)}, bf16[192,1536]{1,0:T(8,128)(2,1)}, bf16[256,1536]{1,0:T(8,128)(2,1)}, bf16[256,1536]{1,0:T(8,128)(2,1)}, b...) conditional(s32[]{:T(128)} %convert_element_type.49, () %tuple.152, ...), branch_computations={%region_19.0_spmd, %region_20.0_spmd} | conditional | flops 1 | bytes 11796713 | solution.py:1100
  358.6 15.7 %attend_backward.3 = (bf16[2,1,256,320]{3,2,1,0:T(8,128)(2,1)}, bf16[2,1,256,320]{3,2,1,0:T(8,128)(2,1)}, bf16[2,1,320,256]{3,2,1,0:T(8,128)(2,1)}, bf16[2,1,320,256]{3,2,1,0:T(8,128)(2,1)}, f32[1,8,256]{2,1,0:T(8,128)S(1)}) custom-call(s32[1]{0:T(128)} %get-tuple-element.559.place_ref, bf16[2,2,2,1,256,320]{5,4,3,2,1,0:T(8,128)(2,1)} %bitcast.27.qkv_ref, ...), custom_call_target="tpu_custom_call" | custom-call | flops 1 | bytes 1 | tf_op jit(solution)/shard_map/cond/branch_1_fun/attend_backward/pallas_call | solution.py:320
  374.3 2.6 collective-permute-done.32
  376.9 2.5 collective-permute-done.66
  379.4 19.1 %conditional.24 = (bf16[640,256]{1,0:T(8,128)(2,1)}, bf16[640,256]{1,0:T(8,128)(2,1)}, bf16[640,256]{1,0:T(8,128)(2,1)}, bf16[1536,640]{1,0:T(8,128)(2,1)S(1)}, ...) conditional(s32[]{:T(128)} %convert_element_type.49, () %tuple.133, ...), branch_computations={%region_21.0_spmd, %region_22.0_spmd} | conditional | flops 2 | bytes 8388842 | solution.py:1100
  382.9 4.7 sent_sums.2
  387.6 10.9 %weight_grads.5 = bf16[1536,640]{1,0:T(8,128)(2,1)S(1)} custom-call(bf16[2048,1536]{1,0:T(8,128)(2,1)} %get-tuple-element.578.refs_0_, bf16[512,320]{1,0:T(8,128)(2,1)} %bitcast.102, bf16[512,320]{1,0:T(8,128)(2,1)S(1)} %bitcast.101, bf16[512,320]{1,0:T(8,128)(2,1)} %bitcast.104, bf16[512,320]{1,0:T(8,128)(2,1)} %bitcast.103, ...), custom_call_target="tpu_custom_call" | custom-call | flops 1 | bytes 1 | tf_op jit(solution)/shard_map/cond/branch_1_fun/weight_grads/pallas_call | solution.py:595
  400.4 20.1 %conditional.25 = (bf16[128,1536]{1,0:T(8,128)(2,1)}, bf16[128,1536]{1,0:T(8,128)(2,1)}, bf16[192,1152]{1,0:T(8,128)(2,1)}, bf16[1280,256]{1,0:T(8,128)(2,1)}, bf16[320,1536]{1,0:T(8,128)(2,1)S(1)}) conditional(s32[]{:T(128)} %convert_element_type.49, () %tuple.156, (bf16[256,1536]{1,0:T(8,128)(2,1)}, bf16[384,1152]{1,0:T(8,128)(2,1)S(1)}, ...), branch_computations={%region_24.0_spmd, %region_25.0_spmd} | conditional | flops 10 | bytes 13140292 | solution.py:1100
  407.3 8.6 %collective-permute-done.55 = bf16[128,1536]{1,0:T(8,128)(2,1)} collective-permute-done((bf16[128,1536]{1,0:T(8,128)(2,1)}, bf16[128,1536]{1,0:T(8,128)(2,1)}, u32[]{:S(2)}, u32[]{:S(2)}) %collective-permute-start.55) | collective-permute-done | bytes 393248 | tf_op jit(solution)/shard_map/cond/branch_1_fun/ppermute | solution.py:1037
  415.8 4.6 collective-permute-done.54
  420.5 3.3 corner_sum.1
  423.8 22.8 %conditional.26 = (bf16[256,1536]{1,0:T(8,128)(2,1)}, bf16[256,1536]{1,0:T(8,128)(2,1)}, f32[192,1728]{1,0:T(8,128)}, f32[192,1728]{1,0:T(8,128)}, f32[192,1728]{1,0:T(8,128)}, /*index=5*/f32[1,256,1536]{2,1,0:T(8,128)}) conditional(s32[]{:T(128)} %convert_element_type.49, () %tuple.155, (bf16[256,1536]{1,0:T(8,128)(2,1)}, ...), branch_computations={%region_26.0_spmd, %region_27.0_spmd} | conditional | flops 1 | bytes 32244056 | solution.py:1100
  427.2 3.8 unpack_columns.2
  431.1 7.3 %input_back.1 = f32[256,1536]{1,0:T(8,128)} custom-call(bf16[640,256]{1,0:T(8,128)(2,1)S(1)} %get-tuple-element.623.refs_0_, bf16[640,256]{1,0:T(8,128)(2,1)} %get-tuple-element.624.refs_1_, bf16[640,256]{1,0:T(8,128)(2,1)} %get-tuple-element.625.refs_2_, bf16[640,256]{1,0:T(8,128)(2,1)} %get-tuple-element.626.refs_3_, ...), custom_call_target="tpu_custom_call" | custom-call | flops 1 | bytes 1 | tf_op jit(solution)/shard_map/cond/branch_1_fun/input_back/pallas_call | solution.py:787
  438.3 6.4 %collective-permute-done.39 = bf16[256,1536]{1,0:T(8,128)(2,1)} collective-permute-done((bf16[256,1536]{1,0:T(8,128)(2,1)}, bf16[256,1536]{1,0:T(8,128)(2,1)}, u32[]{:S(2)}, u32[]{:S(2)}) %collective-permute-start.39) | collective-permute-done | bytes 786464 | tf_op jit(solution)/shard_map/cond/branch_1_fun/ppermute | solution.py:1037
  446.5 8.3 %conditional.27 = (bf16[192,640]{1,0:T(8,128)(2,1)}, bf16[1,256,1536]{2,1,0:T(8,128)(2,1)S(1)}) conditional(s32[]{:T(128)} %convert_element_type.49, () %tuple.132, (bf16[384,640]{1,0:T(8,128)(2,1)}, bf16[256,1536]{1,0:T(8,128)(2,1)}, bf16[1024,1536]{1,0:T(8,128)(2,1)}, bf16[256,1536]{1,0:T(8,128)(2,1)}, bf16[256,1536]{1,0:T(8,128)(2,1)}, ...), branch_computations={%region_29.0_spmd, %region_30.0_spmd} | conditional | flops 3538952 | bytes 6979734 | solution.py:1100
  448.2 2.3 fusion
  450.5 4.3 collective-permute-done.53
  454.8 2.4 unpack_columns.3
  (261 shorter events, 90.4 us)
Async XLA Ops:
  7.2 76.5 %all-gather.4.cloned.1.call-start = ((), (), s32[]{:S(2)}) async-start(), calls=%async_computation.6 | async-start | bytes 2457600 | tf_op jit(solution)/shard_map/all_gather | solution.py:1087
  9.2 27.5 %collective-permute-start.1 = (bf16[256,1536]{1,0:T(8,128)(2,1)}, bf16[256,1536]{1,0:T(8,128)(2,1)}, u32[]{:S(2)}, u32[]{:S(2)}) collective-permute-start(bf16[256,1536]{1,0:T(8,128)(2,1)} %get-tuple-element.393), channel_id=1, source_target_pairs={{0,4},{4,0},{1,5},{5,1},{2,6},{6,2},{3,7},{7,3},{8,12},{12,8},{9,1... | collective-permute-start | bytes 2359304 | tf_op jit(solution)/shard_map/cond/branch_1_fun/ppermute | solution.py:1037
  12.2 24.6 %collective-permute-start = (bf16[256,1536]{1,0:T(8,128)(2,1)}, bf16[256,1536]{1,0:T(8,128)(2,1)}, u32[]{:S(2)}, u32[]{:S(2)}) collective-permute-start(bf16[256,1536]{1,0:T(8,128)(2,1)} %get-tuple-element.393), channel_id=1, source_target_pairs={{0,2},{2,0},{1,3},{3,1},{4,6},{6,4},{5,7},{7,5},{8,10},{10,8},{9,1... | collective-permute-start | bytes 2359304 | tf_op jit(solution)/shard_map/cond/branch_1_fun/ppermute | solution.py:1037
  13.7 23.1 %all-to-all-start = ((bf16[8,48,640]{2,1,0:T(8,128)(2,1)}), bf16[8,48,640]{2,1,0:T(8,128)(2,1)}, u32[]{:S(2)}, u32[]{:S(2)}) async-start(bf16[8,48,640]{2,1,0:T(8,128)(2,1)} %get-tuple-element.392), calls=%async_computation | async-start | bytes 983040 | tf_op jit(solution)/shard_map/cond/branch_1_fun/all_to_all | solution.py:1104
  36.8 134.1 %all-gather.8.cloned.1.call-start = ((), (), s32[]{:S(2)}) async-start(), calls=%async_computation.8 | async-start | bytes 5898240 | tf_op jit(solution)/shard_map/all_gather | solution.py:1087
  36.9 28.7 %all-to-all-start.1 = ((bf16[8,48,1536]{2,1,0:T(8,128)(2,1)}), bf16[8,48,1536]{2,1,0:T(8,128)(2,1)}, u32[]{:S(2)}, u32[]{:S(2)}) async-start(bf16[8,48,1536]{2,1,0:T(8,128)(2,1)} %get-tuple-element.406), calls=%async_computation.1 | async-start | bytes 2359296 | tf_op jit(solution)/shard_map/cond/branch_1_fun/all_to_all | solution.py:1104
  41.3 24.3 %collective-permute-start.47 = (bf16[256,1536]{1,0:T(8,128)(2,1)S(1)}, bf16[256,1536]{1,0:T(8,128)(2,1)}, u32[]{:S(2)}, u32[]{:S(2)}) collective-permute-start(bf16[256,1536]{1,0:T(8,128)(2,1)S(1)} %copy-done.25), channel_id=1, source_target_pairs={{0,1},{1,0},{2,3},{3,2},{4,5},{5,4},{6,7},{7,6},{8,9},{9,8},{10,11... | collective-permute-start | bytes 2359304 | tf_op jit(solution)/shard_map/cond/branch_1_fun/ppermute | solution.py:1037
  41.7 23.9 %collective-permute-start.48 = (bf16[256,1536]{1,0:T(8,128)(2,1)}, bf16[256,1536]{1,0:T(8,128)(2,1)}, u32[]{:S(2)}, u32[]{:S(2)}) collective-permute-start(bf16[256,1536]{1,0:T(8,128)(2,1)} %get-tuple-element.399.refs_0_), channel_id=1, source_target_pairs={{0,1},{1,0},{2,3},{3,2},{4,5},{5,4},{6,7},{7,6},{8,9},{9,8},{10,11... | collective-permute-start | bytes 2359304 | tf_op jit(solution)/shard_map/cond/branch_1_fun/ppermute | solution.py:1037
  41.9 23.7 %collective-permute-start.49 = (bf16[256,1536]{1,0:T(8,128)(2,1)}, bf16[256,1536]{1,0:T(8,128)(2,1)}, u32[]{:S(2)}, u32[]{:S(2)}) collective-permute-start(bf16[256,1536]{1,0:T(8,128)(2,1)} %get-tuple-element.400.refs_1_), channel_id=1, source_target_pairs={{0,1},{1,0},{2,3},{3,2},{4,5},{5,4},{6,7},{7,6},{8,9},{9,8},{10,11... | collective-permute-start | bytes 2359304 | tf_op jit(solution)/shard_map/cond/branch_1_fun/ppermute | solution.py:1037
  44.2 21.3 %collective-permute-start.45 = (bf16[128,1536]{1,0:T(8,128)(2,1)}, bf16[128,1536]{1,0:T(8,128)(2,1)}, u32[]{:S(2)}, u32[]{:S(2)}) collective-permute-start(bf16[128,1536]{1,0:T(8,128)(2,1)} %get-tuple-element.401), channel_id=1, source_target_pairs={{0,4},{4,0},{1,5},{5,1},{2,6},{6,2},{3,7},{7,3},{8,12},{12,8},{9,1... | collective-permute-start | bytes 1179656 | tf_op jit(solution)/shard_map/cond/branch_1_fun/ppermute | solution.py:1037
  45.9 19.6 %collective-permute-start.46 = (bf16[128,1536]{1,0:T(8,128)(2,1)}, bf16[128,1536]{1,0:T(8,128)(2,1)}, u32[]{:S(2)}, u32[]{:S(2)}) collective-permute-start(bf16[128,1536]{1,0:T(8,128)(2,1)} %get-tuple-element.402), channel_id=1, source_target_pairs={{0,2},{2,0},{1,3},{3,1},{4,6},{6,4},{5,7},{7,5},{8,10},{10,8},{9,1... | collective-permute-start | bytes 1179656 | tf_op jit(solution)/shard_map/cond/branch_1_fun/ppermute | solution.py:1037
  65.6 175.1 %all-gather.6.cloned.1.call-start = ((), (), s32[]{:S(2)}) async-start(), calls=%async_computation.7 | async-start | bytes 4423680 | tf_op jit(solution)/shard_map/all_gather | solution.py:1087
  83.5 251.9 %reduce-scatter.4.cloned.1.call-start = ((), (), s32[]{:S(2)}) async-start(), calls=%async_computation.9 | async-start | bytes 5898240 | tf_op jit(solution)/shard_map/reduce_scatter | solution.py:1091
  88.0 30.3 %collective-permute-start.5 = (bf16[192,1536]{1,0:T(8,128)(2,1)S(1)}, bf16[192,1536]{1,0:T(8,128)(2,1)}, u32[]{:S(2)}, u32[]{:S(2)}) collective-permute-start(bf16[192,1536]{1,0:T(8,128)(2,1)S(1)} %get-tuple-element.407), channel_id=1, source_target_pairs={{0,1},{1,0},{2,3},{3,2},{4,5},{5,4},{6,7},{7,6},{8,9},{9,8},{10,11... | collective-permute-start | bytes 1769480 | tf_op jit(solution)/shard_map/cond/branch_1_fun/ppermute | solution.py:1037
  88.4 29.8 %collective-permute-start.4 = (bf16[192,1536]{1,0:T(8,128)(2,1)S(1)}, bf16[192,1536]{1,0:T(8,128)(2,1)}, u32[]{:S(2)}, u32[]{:S(2)}) collective-permute-start(bf16[192,1536]{1,0:T(8,128)(2,1)S(1)} %get-tuple-element.407), channel_id=1, source_target_pairs={{0,6},{2,4},{4,2},{6,0},{1,7},{3,5},{5,3},{7,1},{8,14},{10,12},{12... | collective-permute-start | bytes 1769480 | tf_op jit(solution)/shard_map/cond/branch_1_fun/ppermute | solution.py:1063
  89.3 29.0 %collective-permute-start.3 = (bf16[192,1536]{1,0:T(8,128)(2,1)S(1)}, bf16[192,1536]{1,0:T(8,128)(2,1)}, u32[]{:S(2)}, u32[]{:S(2)}) collective-permute-start(bf16[192,1536]{1,0:T(8,128)(2,1)S(1)} %get-tuple-element.407), channel_id=1, source_target_pairs={{0,4},{4,0},{1,5},{5,1},{2,6},{6,2},{3,7},{7,3},{8,12},{12,8},{9,1... | collective-permute-start | bytes 1769480 | tf_op jit(solution)/shard_map/cond/branch_1_fun/ppermute | solution.py:1037
  90.7 27.6 %collective-permute-start.2 = (bf16[192,1536]{1,0:T(8,128)(2,1)S(1)}, bf16[192,1536]{1,0:T(8,128)(2,1)}, u32[]{:S(2)}, u32[]{:S(2)}) collective-permute-start(bf16[192,1536]{1,0:T(8,128)(2,1)S(1)} %get-tuple-element.407), channel_id=1, source_target_pairs={{0,2},{2,0},{1,3},{3,1},{4,6},{6,4},{5,7},{7,5},{8,10},{10,8},{9,1... | collective-permute-start | bytes 1769480 | tf_op jit(solution)/shard_map/cond/branch_1_fun/ppermute | solution.py:1037
  118.3 8.8 %collective-permute-start.8 = (bf16[384,256]{1,0:T(8,128)(2,1)S(1)}, bf16[384,256]{1,0:T(8,128)(2,1)S(1)}, u32[]{:S(2)}, u32[]{:S(2)}) collective-permute-start(bf16[384,256]{1,0:T(8,128)(2,1)S(1)} %bitcast.112), channel_id=1, source_target_pairs={{0,6},{2,4},{4,2},{6,0},{1,7},{3,5},{5,3},{7,1},{8,14},{10,12},{12... | collective-permute-start | bytes 589832 | tf_op jit(solution)/shard_map/cond/branch_1_fun/ppermute | solution.py:1063
  119.6 9.7 %collective-permute-start.7 = (bf16[384,256]{1,0:T(8,128)(2,1)S(1)}, bf16[384,256]{1,0:T(8,128)(2,1)S(1)}, u32[]{:S(2)}, u32[]{:S(2)}) collective-permute-start(bf16[384,256]{1,0:T(8,128)(2,1)S(1)} %bitcast.113), channel_id=1, source_target_pairs={{0,4},{4,0},{1,5},{5,1},{2,6},{6,2},{3,7},{7,3},{8,12},{12,8},{9,1... | collective-permute-start | bytes 589832 | tf_op jit(solution)/shard_map/cond/branch_1_fun/ppermute | solution.py:1037
  120.9 8.9 %collective-permute-start.6 = (bf16[384,256]{1,0:T(8,128)(2,1)S(1)}, bf16[384,256]{1,0:T(8,128)(2,1)S(1)}, u32[]{:S(2)}, u32[]{:S(2)}) collective-permute-start(bf16[384,256]{1,0:T(8,128)(2,1)S(1)} %bitcast.114), channel_id=1, source_target_pairs={{0,2},{2,0},{1,3},{3,1},{4,6},{6,4},{5,7},{7,5},{8,10},{10,8},{9,1... | collective-permute-start | bytes 589832 | tf_op jit(solution)/shard_map/cond/branch_1_fun/ppermute | solution.py:1037
  121.9 13.5 %collective-permute-start.12 = (bf16[192,1536]{1,0:T(8,128)(2,1)}, bf16[192,1536]{1,0:T(8,128)(2,1)}, u32[]{:S(2)}, u32[]{:S(2)}) collective-permute-start(bf16[192,1536]{1,0:T(8,128)(2,1)} %get-tuple-element.440.refs_11_), channel_id=1, source_target_pairs={{0,1},{1,0},{2,3},{3,2},{4,5},{5,4},{6,7},{7,6},{8,9},{9,8},{10,11... | collective-permute-start | bytes 1769480 | tf_op jit(solution)/shard_map/cond/branch_1_fun/ppermute | solution.py:1037
  132.2 13.3 %collective-permute-start.18 = (bf16[256,1536]{1,0:T(8,128)(2,1)S(1)}, bf16[256,1536]{1,0:T(8,128)(2,1)}, u32[]{:S(2)}, u32[]{:S(2)}) collective-permute-start(bf16[256,1536]{1,0:T(8,128)(2,1)S(1)} %get-tuple-element.446), channel_id=1, source_target_pairs={{0,1},{1,0},{2,3},{3,2},{4,5},{5,4},{6,7},{7,6},{8,9},{9,8},{10,11... | collective-permute-start | bytes 2359304 | tf_op jit(solution)/shard_map/cond/branch_1_fun/ppermute | solution.py:1037
  133.6 20.7 %collective-permute-start.17 = (bf16[256,1536]{1,0:T(8,128)(2,1)}, bf16[256,1536]{1,0:T(8,128)(2,1)}, u32[]{:S(2)}, u32[]{:S(2)}) collective-permute-start(bf16[256,1536]{1,0:T(8,128)(2,1)} %after.3), channel_id=1, source_target_pairs={{0,4},{4,0},{1,5},{5,1},{2,6},{6,2},{3,7},{7,3},{8,12},{12,8},{9,1... | collective-permute-start | bytes 2359304 | tf_op jit(solution)/shard_map/cond/branch_1_fun/ppermute | solution.py:1037
  134.5 20.8 %collective-permute-start.16 = (bf16[256,1536]{1,0:T(8,128)(2,1)}, bf16[256,1536]{1,0:T(8,128)(2,1)}, u32[]{:S(2)}, u32[]{:S(2)}) collective-permute-start(bf16[256,1536]{1,0:T(8,128)(2,1)} %after.3), channel_id=1, source_target_pairs={{0,2},{2,0},{1,3},{3,1},{4,6},{6,4},{5,7},{7,5},{8,10},{10,8},{9,1... | collective-permute-start | bytes 2359304 | tf_op jit(solution)/shard_map/cond/branch_1_fun/ppermute | solution.py:1037
  144.1 11.2 %collective-permute-start.15 = (bf16[256,1536]{1,0:T(8,128)(2,1)}, bf16[256,1536]{1,0:T(8,128)(2,1)}, u32[]{:S(2)}, u32[]{:S(2)}) collective-permute-start(bf16[256,1536]{1,0:T(8,128)(2,1)} %get-tuple-element.1208), channel_id=1, source_target_pairs={{0,1},{1,0},{2,3},{3,2},{4,5},{5,4},{6,7},{7,6},{8,9},{9,8},{10,11... | collective-permute-start | bytes 2359304 | tf_op jit(solution)/shard_map/cond/branch_1_fun/ppermute | solution.py:1037
  144.2 26.0 %collective-permute-start.14 = (bf16[256,1536]{1,0:T(8,128)(2,1)}, bf16[256,1536]{1,0:T(8,128)(2,1)}, u32[]{:S(2)}, u32[]{:S(2)}) collective-permute-start(bf16[256,1536]{1,0:T(8,128)(2,1)} %get-tuple-element.1208), channel_id=1, source_target_pairs={{0,4},{4,0},{1,5},{5,1},{2,6},{6,2},{3,7},{7,3},{8,12},{12,8},{9,1... | collective-permute-start | bytes 2359304 | tf_op jit(solution)/shard_map/cond/branch_1_fun/ppermute | solution.py:1037
  145.5 25.3 %collective-permute-start.13 = (bf16[256,1536]{1,0:T(8,128)(2,1)}, bf16[256,1536]{1,0:T(8,128)(2,1)}, u32[]{:S(2)}, u32[]{:S(2)}) collective-permute-start(bf16[256,1536]{1,0:T(8,128)(2,1)} %get-tuple-element.1208), channel_id=1, source_target_pairs={{0,2},{2,0},{1,3},{3,1},{4,6},{6,4},{5,7},{7,5},{8,10},{10,8},{9,1... | collective-permute-start | bytes 2359304 | tf_op jit(solution)/shard_map/cond/branch_1_fun/ppermute | solution.py:1037
  154.4 16.5 %collective-permute-start.20 = (bf16[256,1536]{1,0:T(8,128)(2,1)}, bf16[256,1536]{1,0:T(8,128)(2,1)}, u32[]{:S(2)}, u32[]{:S(2)}) collective-permute-start(bf16[256,1536]{1,0:T(8,128)(2,1)} %collective-permute-done.17), channel_id=1, source_target_pairs={{0,1},{1,0},{2,3},{3,2},{4,5},{5,4},{6,7},{7,6},{8,9},{9,8},{10,11... | collective-permute-start | bytes 2359304 | tf_op jit(solution)/shard_map/cond/branch_1_fun/ppermute | solution.py:1037
  155.3 15.6 %collective-permute-start.19 = (bf16[256,1536]{1,0:T(8,128)(2,1)}, bf16[256,1536]{1,0:T(8,128)(2,1)}, u32[]{:S(2)}, u32[]{:S(2)}) collective-permute-start(bf16[256,1536]{1,0:T(8,128)(2,1)} %collective-permute-done.16), channel_id=1, source_target_pairs={{0,1},{1,0},{2,3},{3,2},{4,5},{5,4},{6,7},{7,6},{8,9},{9,8},{10,11... | collective-permute-start | bytes 2359304 | tf_op jit(solution)/shard_map/cond/branch_1_fun/ppermute | solution.py:1037
  173.5 19.5 %collective-permute-start.21 = (bf16[256,1536]{1,0:T(8,128)(2,1)}, bf16[256,1536]{1,0:T(8,128)(2,1)}, u32[]{:S(2)}, u32[]{:S(2)}) collective-permute-start(bf16[256,1536]{1,0:T(8,128)(2,1)} %get-tuple-element.451), channel_id=1, source_target_pairs={{0,4},{4,0},{1,5},{5,1},{2,6},{6,2},{3,7},{7,3},{8,12},{12,8},{9,1... | collective-permute-start | bytes 2359304 | tf_op jit(solution)/shard_map/cond/branch_1_fun/ppermute | solution.py:1037
  174.8 19.4 %collective-permute-start.22 = (bf16[256,1536]{1,0:T(8,128)(2,1)}, bf16[256,1536]{1,0:T(8,128)(2,1)}, u32[]{:S(2)}, u32[]{:S(2)}) collective-permute-start(bf16[256,1536]{1,0:T(8,128)(2,1)} %get-tuple-element.452), channel_id=1, source_target_pairs={{0,2},{2,0},{1,3},{3,1},{4,6},{6,4},{5,7},{7,5},{8,10},{10,8},{9,1... | collective-permute-start | bytes 2359304 | tf_op jit(solution)/shard_map/cond/branch_1_fun/ppermute | solution.py:1037
  176.3 17.9 %collective-permute-start.23 = (bf16[256,1536]{1,0:T(8,128)(2,1)}, bf16[256,1536]{1,0:T(8,128)(2,1)}, u32[]{:S(2)}, u32[]{:S(2)}) collective-permute-start(bf16[256,1536]{1,0:T(8,128)(2,1)} %get-tuple-element.447.refs_0_.refs_1_), channel_id=1, source_target_pairs={{0,1},{1,0},{2,3},{3,2},{4,5},{5,4},{6,7},{7,6},{8,9},{9,8},{10,11... | collective-permute-start | bytes 2359304 | tf_op jit(solution)/shard_map/cond/branch_1_fun/ppermute | solution.py:1037
  176.3 17.9 %collective-permute-start.24 = (bf16[256,1536]{1,0:T(8,128)(2,1)}, bf16[256,1536]{1,0:T(8,128)(2,1)}, u32[]{:S(2)}, u32[]{:S(2)}) collective-permute-start(bf16[256,1536]{1,0:T(8,128)(2,1)} %get-tuple-element.448.refs_1_.refs_2_), channel_id=1, source_target_pairs={{0,1},{1,0},{2,3},{3,2},{4,5},{5,4},{6,7},{7,6},{8,9},{9,8},{10,11... | collective-permute-start | bytes 2359304 | tf_op jit(solution)/shard_map/cond/branch_1_fun/ppermute | solution.py:1037
  200.1 35.0 %collective-permute-start.26 = (bf16[320,1536]{1,0:T(8,128)(2,1)}, bf16[320,1536]{1,0:T(8,128)(2,1)}, u32[]{:S(2)}, u32[]{:S(2)}) collective-permute-start(bf16[320,1536]{1,0:T(8,128)(2,1)} %get-tuple-element.483), channel_id=1, source_target_pairs={{0,4},{4,0},{1,5},{5,1},{2,6},{6,2},{3,7},{7,3},{8,12},{12,8},{9,1... | collective-permute-start | bytes 2949128 | tf_op jit(solution)/shard_map/cond/branch_1_fun/ppermute | solution.py:1037
  200.6 34.5 %collective-permute-start.25 = (bf16[320,1536]{1,0:T(8,128)(2,1)}, bf16[320,1536]{1,0:T(8,128)(2,1)}, u32[]{:S(2)}, u32[]{:S(2)}) collective-permute-start(bf16[320,1536]{1,0:T(8,128)(2,1)} %get-tuple-element.483), channel_id=1, source_target_pairs={{0,2},{2,0},{1,3},{3,1},{4,6},{6,4},{5,7},{7,5},{8,10},{10,8},{9,1... | collective-permute-start | bytes 2949128 | tf_op jit(solution)/shard_map/cond/branch_1_fun/ppermute | solution.py:1037
  235.1 163.5 %reduce-scatter.6.cloned.1.call-start = ((), (), s32[]{:S(2)}) async-start(), calls=%async_computation.10 | async-start | bytes 4423680 | tf_op jit(solution)/shard_map/reduce_scatter | solution.py:1091
  240.8 18.4 %collective-permute-start.27 = (bf16[160,1536]{1,0:T(8,128)(2,1)}, bf16[160,1536]{1,0:T(8,128)(2,1)}, u32[]{:S(2)}, u32[]{:S(2)}) collective-permute-start(bf16[160,1536]{1,0:T(8,128)(2,1)} %get-tuple-element.484), channel_id=1, source_target_pairs={{0,4},{4,0},{1,5},{5,1},{2,6},{6,2},{3,7},{7,3},{8,12},{12,8},{9,1... | collective-permute-start | bytes 1474568 | tf_op jit(solution)/shard_map/cond/branch_1_fun/ppermute | solution.py:1037
  242.3 16.9 %collective-permute-start.28 = (bf16[160,1536]{1,0:T(8,128)(2,1)}, bf16[160,1536]{1,0:T(8,128)(2,1)}, u32[]{:S(2)}, u32[]{:S(2)}) collective-permute-start(bf16[160,1536]{1,0:T(8,128)(2,1)} %get-tuple-element.485), channel_id=1, source_target_pairs={{0,2},{2,0},{1,3},{3,1},{4,6},{6,4},{5,7},{7,5},{8,10},{10,8},{9,1... | collective-permute-start | bytes 1474568 | tf_op jit(solution)/shard_map/cond/branch_1_fun/ppermute | solution.py:1037
  259.2 8.2 %collective-permute-start.61 = (bf16[1024,1536]{1,0:T(8,128)(2,1)S(1)}, bf16[1024,1536]{1,0:T(8,128)(2,1)S(1)}, u32[]{:S(2)}, u32[]{:S(2)}) collective-permute-start(bf16[1024,1536]{1,0:T(8,128)(2,1)S(1)} %get-tuple-element.838.refs_6_), channel_id=1, source_target_pairs={{0,1},{1,0},{2,3},{3,2},{4,5},{5,4},{6,7},{7,6},{8,9},{9,8},{10,11... | collective-permute-start | bytes 9437192 | tf_op jit(solution)/shard_map/ppermute | solution.py:1037
  273.7 35.9 %collective-permute-start.29 = (bf16[256,1536]{1,0:T(8,128)(2,1)}, bf16[256,1536]{1,0:T(8,128)(2,1)}, u32[]{:S(2)}, u32[]{:S(2)}) collective-permute-start(bf16[256,1536]{1,0:T(8,128)(2,1)} %get-tuple-element.503), channel_id=1, source_target_pairs={{0,2},{2,0},{1,3},{3,1},{4,6},{6,4},{5,7},{7,5},{8,10},{10,8},{9,1... | collective-permute-start | bytes 2359304 | tf_op jit(solution)/shard_map/cond/branch_1_fun/ppermute | solution.py:1037
  273.7 36.0 %collective-permute-start.30 = (bf16[256,1536]{1,0:T(8,128)(2,1)}, bf16[256,1536]{1,0:T(8,128)(2,1)}, u32[]{:S(2)}, u32[]{:S(2)}) collective-permute-start(bf16[256,1536]{1,0:T(8,128)(2,1)} %get-tuple-element.504), channel_id=1, source_target_pairs={{0,4},{4,0},{1,5},{5,1},{2,6},{6,2},{3,7},{7,3},{8,12},{12,8},{9,1... | collective-permute-start | bytes 2359304 | tf_op jit(solution)/shard_map/cond/branch_1_fun/ppermute | solution.py:1037
  274.3 37.6 %collective-permute-start.31 = (bf16[256,1536]{1,0:T(8,128)(2,1)}, bf16[256,1536]{1,0:T(8,128)(2,1)}, u32[]{:S(2)}, u32[]{:S(2)}) collective-permute-start(bf16[256,1536]{1,0:T(8,128)(2,1)} %get-tuple-element.505), channel_id=1, source_target_pairs={{0,6},{2,4},{4,2},{6,0},{1,7},{3,5},{5,3},{7,1},{8,14},{10,12},{12... | collective-permute-start | bytes 2359304 | tf_op jit(solution)/shard_map/cond/branch_1_fun/ppermute | solution.py:1063
  312.0 134.6 %reduce-scatter.8.cloned.1.call-start = ((), (), s32[]{:S(2)}) async-start(), calls=%async_computation.11 | async-start | bytes 2457600 | tf_op jit(solution)/shard_map/reduce_scatter | solution.py:1091
  312.4 64.5 %collective-permute-start.67 = (bf16[1024,1536]{1,0:T(8,128)(2,1)}, bf16[1024,1536]{1,0:T(8,128)(2,1)}, u32[]{:S(2)}, u32[]{:S(2)}) collective-permute-start(bf16[1024,1536]{1,0:T(8,128)(2,1)} %get-tuple-element.890), channel_id=1, source_target_pairs={{0,1},{1,0},{2,3},{3,2},{4,5},{5,4},{6,7},{7,6},{8,9},{9,8},{10,11... | collective-permute-start | bytes 9437192 | tf_op jit(solution)/shard_map/ppermute | solution.py:1037
  321.9 7.8 %collective-permute-start.63 = (bf16[384,256]{1,0:T(8,128)(2,1)S(1)}, bf16[384,256]{1,0:T(8,128)(2,1)S(1)}, u32[]{:S(2)}, u32[]{:S(2)}) collective-permute-start(bf16[384,256]{1,0:T(8,128)(2,1)S(1)} %bitcast.80), channel_id=1, source_target_pairs={{0,4},{4,0},{1,5},{5,1},{2,6},{6,2},{3,7},{7,3},{8,12},{12,8},{9,1... | collective-permute-start | bytes 589832 | tf_op jit(solution)/shard_map/ppermute | solution.py:1037
  322.3 10.4 %collective-permute-start.62 = (bf16[384,256]{1,0:T(8,128)(2,1)S(1)}, bf16[384,256]{1,0:T(8,128)(2,1)S(1)}, u32[]{:S(2)}, u32[]{:S(2)}) collective-permute-start(bf16[384,256]{1,0:T(8,128)(2,1)S(1)} %bitcast.79), channel_id=1, source_target_pairs={{0,2},{2,0},{1,3},{3,1},{4,6},{6,4},{5,7},{7,5},{8,10},{10,8},{9,1... | collective-permute-start | bytes 589832 | tf_op jit(solution)/shard_map/ppermute | solution.py:1037
  322.6 10.1 %collective-permute-start.64 = (bf16[384,256]{1,0:T(8,128)(2,1)S(1)}, bf16[384,256]{1,0:T(8,128)(2,1)S(1)}, u32[]{:S(2)}, u32[]{:S(2)}) collective-permute-start(bf16[384,256]{1,0:T(8,128)(2,1)S(1)} %bitcast.78), channel_id=1, source_target_pairs={{0,6},{2,4},{4,2},{6,0},{1,7},{3,5},{5,3},{7,1},{8,14},{10,12},{12... | collective-permute-start | bytes 589832 | tf_op jit(solution)/shard_map/ppermute | solution.py:1063
  335.4 20.0 %collective-permute-start.51 = (bf16[256,1536]{1,0:T(8,128)(2,1)}, bf16[256,1536]{1,0:T(8,128)(2,1)}, u32[]{:S(2)}, u32[]{:S(2)}) collective-permute-start(bf16[256,1536]{1,0:T(8,128)(2,1)} %get-tuple-element.538), channel_id=1, source_target_pairs={{0,4},{4,0},{1,5},{5,1},{2,6},{6,2},{3,7},{7,3},{8,12},{12,8},{9,1... | collective-permute-start | bytes 2359304 | tf_op jit(solution)/shard_map/cond/branch_1_fun/ppermute | solution.py:1037
  336.9 19.6 %collective-permute-start.50 = (bf16[256,1536]{1,0:T(8,128)(2,1)}, bf16[256,1536]{1,0:T(8,128)(2,1)}, u32[]{:S(2)}, u32[]{:S(2)}) collective-permute-start(bf16[256,1536]{1,0:T(8,128)(2,1)} %get-tuple-element.538), channel_id=1, source_target_pairs={{0,2},{2,0},{1,3},{3,1},{4,6},{6,4},{5,7},{7,5},{8,10},{10,8},{9,1... | collective-permute-start | bytes 2359304 | tf_op jit(solution)/shard_map/cond/branch_1_fun/ppermute | solution.py:1037
  337.5 19.0 %collective-permute-start.52 = (bf16[256,1536]{1,0:T(8,128)(2,1)}, bf16[256,1536]{1,0:T(8,128)(2,1)}, u32[]{:S(2)}, u32[]{:S(2)}) collective-permute-start(bf16[256,1536]{1,0:T(8,128)(2,1)} %get-tuple-element.538), channel_id=1, source_target_pairs={{0,1},{1,0},{2,3},{3,2},{4,5},{5,4},{6,7},{7,6},{8,9},{9,8},{10,11... | collective-permute-start | bytes 2359304 | tf_op jit(solution)/shard_map/cond/branch_1_fun/ppermute | solution.py:1037
  356.5 17.8 %collective-permute-start.34 = (bf16[256,1536]{1,0:T(8,128)(2,1)}, bf16[256,1536]{1,0:T(8,128)(2,1)}, u32[]{:S(2)}, u32[]{:S(2)}) collective-permute-start(bf16[256,1536]{1,0:T(8,128)(2,1)} %get-tuple-element.558), channel_id=1, source_target_pairs={{0,1},{1,0},{2,3},{3,2},{4,5},{5,4},{6,7},{7,6},{8,9},{9,8},{10,11... | collective-permute-start | bytes 2359304 | tf_op jit(solution)/shard_map/cond/branch_1_fun/ppermute | solution.py:1037
  356.6 20.3 %collective-permute-start.32 = (bf16[256,1536]{1,0:T(8,128)(2,1)}, bf16[256,1536]{1,0:T(8,128)(2,1)}, u32[]{:S(2)}, u32[]{:S(2)}) collective-permute-start(bf16[256,1536]{1,0:T(8,128)(2,1)} %get-tuple-element.556), channel_id=1, source_target_pairs={{0,2},{2,0},{1,3},{3,1},{4,6},{6,4},{5,7},{7,5},{8,10},{10,8},{9,1... | collective-permute-start | bytes 2359304 | tf_op jit(solution)/shard_map/cond/branch_1_fun/ppermute | solution.py:1037
  357.3 19.6 %collective-permute-start.35 = (bf16[256,1536]{1,0:T(8,128)(2,1)}, bf16[256,1536]{1,0:T(8,128)(2,1)}, u32[]{:S(2)}, u32[]{:S(2)}) collective-permute-start(bf16[256,1536]{1,0:T(8,128)(2,1)} %get-tuple-element.556), channel_id=1, source_target_pairs={{0,1},{1,0},{2,3},{3,2},{4,5},{5,4},{6,7},{7,6},{8,9},{9,8},{10,11... | collective-permute-start | bytes 2359304 | tf_op jit(solution)/shard_map/cond/branch_1_fun/ppermute | solution.py:1037
  357.5 16.8 %collective-permute-start.33 = (bf16[192,1536]{1,0:T(8,128)(2,1)}, bf16[192,1536]{1,0:T(8,128)(2,1)}, u32[]{:S(2)}, u32[]{:S(2)}) collective-permute-start(bf16[192,1536]{1,0:T(8,128)(2,1)} %get-tuple-element.557), channel_id=1, source_target_pairs={{0,4},{4,0},{1,5},{5,1},{2,6},{6,2},{3,7},{7,3},{8,12},{12,8},{9,1... | collective-permute-start | bytes 1769480 | tf_op jit(solution)/shard_map/cond/branch_1_fun/ppermute | solution.py:1037
  379.4 19.1 %collective-permute-start.38 = (bf16[640,256]{1,0:T(8,128)(2,1)}, bf16[640,256]{1,0:T(8,128)(2,1)}, u32[]{:S(2)}, u32[]{:S(2)}) collective-permute-start(bf16[640,256]{1,0:T(8,128)(2,1)} %get-tuple-element.577), channel_id=1, source_target_pairs={{0,6},{2,4},{4,2},{6,0},{1,7},{3,5},{5,3},{7,1},{8,14},{10,12},{12... | collective-permute-start | bytes 983048 | tf_op jit(solution)/shard_map/cond/branch_1_fun/ppermute | solution.py:1063
  380.6 17.9 %collective-permute-start.37 = (bf16[640,256]{1,0:T(8,128)(2,1)}, bf16[640,256]{1,0:T(8,128)(2,1)}, u32[]{:S(2)}, u32[]{:S(2)}) collective-permute-start(bf16[640,256]{1,0:T(8,128)(2,1)} %get-tuple-element.576), channel_id=1, source_target_pairs={{0,4},{4,0},{1,5},{5,1},{2,6},{6,2},{3,7},{7,3},{8,12},{12,8},{9,1... | collective-permute-start | bytes 983048 | tf_op jit(solution)/shard_map/cond/branch_1_fun/ppermute | solution.py:1037
  381.5 17.0 %collective-permute-start.36 = (bf16[640,256]{1,0:T(8,128)(2,1)}, bf16[640,256]{1,0:T(8,128)(2,1)}, u32[]{:S(2)}, u32[]{:S(2)}) collective-permute-start(bf16[640,256]{1,0:T(8,128)(2,1)} %get-tuple-element.575), channel_id=1, source_target_pairs={{0,2},{2,0},{1,3},{3,1},{4,6},{6,4},{5,7},{7,5},{8,10},{10,8},{9,1... | collective-permute-start | bytes 983048 | tf_op jit(solution)/shard_map/cond/branch_1_fun/ppermute | solution.py:1037
  400.4 20.0 %collective-permute-start.56 = (bf16[192,1152]{1,0:T(8,128)(2,1)S(1)}, bf16[192,1152]{1,0:T(8,128)(2,1)}, u32[]{:S(2)}, u32[]{:S(2)}) collective-permute-start(bf16[192,1152]{1,0:T(8,128)(2,1)S(1)} %constant_dynamic-slice_fusion.1), channel_id=1, source_target_pairs={{0,4},{4,0},{1,5},{5,1},{2,6},{6,2},{3,7},{7,3},{8,12},{12,8},{9,1... | collective-permute-start | bytes 1327112 | tf_op jit(solution)/shard_map/cond/branch_1_fun/ppermute | solution.py:1037
  403.2 17.3 %collective-permute-start.57 = (bf16[1280,256]{1,0:T(8,128)(2,1)}, bf16[1280,256]{1,0:T(8,128)(2,1)}, u32[]{:S(2)}, u32[]{:S(2)}) collective-permute-start(bf16[1280,256]{1,0:T(8,128)(2,1)} %far_parts.4), channel_id=1, source_target_pairs={{0,1},{1,0},{2,3},{3,2},{4,5},{5,4},{6,7},{7,6},{8,9},{9,8},{10,11... | collective-permute-start | bytes 1966088 | tf_op jit(solution)/shard_map/cond/branch_1_fun/ppermute | solution.py:1037
  404.0 11.8 %collective-permute-start.55 = (bf16[128,1536]{1,0:T(8,128)(2,1)}, bf16[128,1536]{1,0:T(8,128)(2,1)}, u32[]{:S(2)}, u32[]{:S(2)}) collective-permute-start(bf16[128,1536]{1,0:T(8,128)(2,1)} %get-tuple-element.1133), channel_id=1, source_target_pairs={{0,2},{2,0},{1,3},{3,1},{4,6},{6,4},{5,7},{7,5},{8,10},{10,8},{9,1... | collective-permute-start | bytes 1179656 | tf_op jit(solution)/shard_map/cond/branch_1_fun/ppermute | solution.py:1037
  405.0 15.4 %collective-permute-start.54 = (bf16[128,1536]{1,0:T(8,128)(2,1)S(1)}, bf16[128,1536]{1,0:T(8,128)(2,1)}, u32[]{:S(2)}, u32[]{:S(2)}) collective-permute-start(bf16[128,1536]{1,0:T(8,128)(2,1)S(1)} %get-tuple-element.1134), channel_id=1, source_target_pairs={{0,4},{4,0},{1,5},{5,1},{2,6},{6,2},{3,7},{7,3},{8,12},{12,8},{9,1... | collective-permute-start | bytes 1179656 | tf_op jit(solution)/shard_map/cond/branch_1_fun/ppermute | solution.py:1037
  424.9 19.8 %collective-permute-start.39 = (bf16[256,1536]{1,0:T(8,128)(2,1)}, bf16[256,1536]{1,0:T(8,128)(2,1)}, u32[]{:S(2)}, u32[]{:S(2)}) collective-permute-start(bf16[256,1536]{1,0:T(8,128)(2,1)} %get-tuple-element.613), channel_id=1, source_target_pairs={{0,2},{2,0},{1,3},{3,1},{4,6},{6,4},{5,7},{7,5},{8,10},{10,8},{9,1... | collective-permute-start | bytes 2359304 | tf_op jit(solution)/shard_map/cond/branch_1_fun/ppermute | solution.py:1037
  426.6 19.9 %collective-permute-start.40 = (bf16[256,1536]{1,0:T(8,128)(2,1)}, bf16[256,1536]{1,0:T(8,128)(2,1)}, u32[]{:S(2)}, u32[]{:S(2)}) collective-permute-start(bf16[256,1536]{1,0:T(8,128)(2,1)} %get-tuple-element.614), channel_id=1, source_target_pairs={{0,4},{4,0},{1,5},{5,1},{2,6},{6,2},{3,7},{7,3},{8,12},{12,8},{9,1... | collective-permute-start | bytes 2359304 | tf_op jit(solution)/shard_map/cond/branch_1_fun/ppermute | solution.py:1037
  447.5 7.3 %collective-permute-start.53 = (bf16[192,640]{1,0:T(8,128)(2,1)S(1)}, bf16[192,640]{1,0:T(8,128)(2,1)}, u32[]{:S(2)}, u32[]{:S(2)}) collective-permute-start(bf16[192,640]{1,0:T(8,128)(2,1)S(1)} %constant_dynamic-slice_fusion.2), channel_id=1, source_target_pairs={{0,4},{4,0},{1,5},{5,1},{2,6},{6,2},{3,7},{7,3},{8,12},{12,8},{9,1... | collective-permute-start | bytes 737288 | tf_op jit(solution)/shard_map/cond/branch_1_fun/ppermute | solution.py:1037
  (63 other events, 634.6 us)
Sparse Core Ops, SparseCore 0:
  36.9 43.8 all-gather.3
  82.4 88.2 all-gather.7
  172.3 68.4 all-gather.5
  242.9 83.8 reduce-scatter.3
  328.9 66.8 reduce-scatter.5
  400.0 39.7 reduce-scatter.7

commit v8 on v7

--- a/solution.py
+++ b/solution.py
@@ -1076,6 +1076,15 @@
     return came, swap(far_parts(came), "c")
 
 
+def sums_to_send(sides, corner, far):
+    rows = corner.shape[0]
+    near = sides[:rows], sides[rows:], corner
+    return [
+        (part.astype(F32) + far[(k + 1) * rows : (k + 2) * rows].astype(F32)).astype(BF16)
+        for k, part in enumerate(near)
+    ]
+
+
 def scatter_end(mine, others):
     mine = mine.astype(F32)
     for other in others:
@@ -1254,7 +1263,7 @@
     )
     far = swap(late[2][1], "c")
     sides = feed_forward(post[1:3], grads[1:3], ffn_full[1], [2], [sides_total], late[2][1:])
-    parts = sent_sums(sides[2][0], late[2][0], far)
+    parts = sums_to_send(sides[2][0], late[2][0], far)
 
     def behind(parts, post, grads, weights, own_total, act_0, act_1, both_1):
         others = diamond(*parts)

time: 475 us -> 474 us (level)
  other arithmetic: 5.39 us -> 10.5 us
  Pallas kernels: 237 us -> 232 us
    convert_element_type x0 -> x2, other arithmetic: none -> 5.12 us  [the longest x1 3.82 us: sums_to_send(): (part.astype(F32) + far[(k + 1) * rows:(k + 2) * rows].astype(F32)).astyp...]
  transfers between devices with their start and end apart: 79 -> 79, of which waited for: 32 -> 32; matrix products, arithmetic and copies ran while one was open for 2% -> 3% of each run, Pallas kernels for 49% -> 49%
where the time goes in v8:
time: 474 us; the launch traced here: 469 us
  Pallas kernels  232 us (49%)
  waiting for transfers between devices  124 us (26%)
  starting transfers between devices  61.3 us (13%)
  blocking collectives  16.6 us (4%)
  between operations  14.7 us (3%)
  other arithmetic  10.5 us (2%)
  local copies, waits for them, and re-layouts  9.7 us (2%)
    ppermute x65, waiting for transfers between devices, swap(): return lax.ppermute(values, axis, SWAP)  94.5 us
    pallas_call x5, Pallas kernels, feed_forward(): pl.pallas_call(body, grid=(rows // TILE,), in_specs=specs * 2 + [entire(w...  58.2 us
    ppermute x65, starting transfers between devices, swap(): return lax.ppermute(values, axis, SWAP)  42.6 us
    pallas_call x3, Pallas kernels, weight_grads(): pl.pallas_call(body, grid=(depth // tile,), in_specs=specs + [ANY] * len(...  39.8 us
    pallas_call x2, Pallas kernels, backward_attention(): pl.pallas_call(attend_backward, grid_spec=pltpu.PrefetchScalarGridSpec(nu...  31.6 us
    all_to_all x1, blocking collectives, plane_columns(): lax.all_to_all(payload, PLANE, split_axis=0, concat_axis=0, tiled=True)  16.6 us
    all_to_all x2, waiting for transfers between devices, plane_columns(): lax.all_to_all(payload, PLANE, split_axis=0, concat_axis=0, tiled=True)  15.8 us
    pallas_call x1, Pallas kernels, attention_call(): pl.pallas_call(body, grid_spec=pltpu.PrefetchScalarGridSpec(num_scalar_pr...  15.7 us
  transfers between devices with their start and end apart: 79, of which 32 were waited for; matrix products, arithmetic and copies ran while one was open for 3% of the time, Pallas kernels for 49%

profile of v8, /device:TPU:0, one launch (start us, length us, event | category | flops | bytes accessed | tf_op | source)
XLA Modules:
  0.0 468.8 jit_solution(17465518592850718470)
XLA Ops:
  9.2 27.5 %conditional.14 = (bf16[384,640]{1,0:T(8,128)(2,1)}, bf16[256,1536]{1,0:T(8,128)(2,1)}, bf16[256,1536]{1,0:T(8,128)(2,1)}, bf16[8,48,1536]{2,1,0:T(8,128)(2,1)}, bf16[8,48,1152]{2,1,0:T(8,128)(2,1)S(1)}) conditional(s32[]{:T(128)} %convert_element_type.79, () %tuple.140, (bf16[8,48,640]{2,1,0:T(8,128)(2,1)}, bf16[256,1536]{1,0:T(8,128)(2,1)}, ...), branch_computations={%region_0.0_spmd, %region_1.0_spmd} | conditional | bytes 7766168 | solution.py:1109
  9.2 2.9 collective-permute-start.1
  13.7 4.1 all-to-all-start
  17.8 3.1 pack_columns.2
  21.0 15.8 %all-to-all-done = bf16[8,48,640]{2,1,0:T(8,128)(2,1)} async-done(((bf16[8,48,640]{2,1,0:T(8,128)(2,1)}), bf16[8,48,640]{2,1,0:T(8,128)(2,1)}, u32[]{:S(2)}, u32[]{:S(2)}) %all-to-all-start) | async-done | bytes 491552 | tf_op jit(solution)/shard_map/cond/branch_1_fun/all_to_all | solution.py:1113
  36.8 28.7 %conditional.15 = (bf16[128,1536]{1,0:T(8,128)(2,1)}, bf16[128,1536]{1,0:T(8,128)(2,1)}, bf16[256,1536]{1,0:T(8,128)(2,1)}, bf16[256,1536]{1,0:T(8,128)(2,1)}, b...) conditional(s32[]{:T(128)} %convert_element_type.79, () %tuple.142, ...), branch_computations={%region_2.0_spmd, %region_3.0_spmd} | conditional | flops 33890 | bytes 19538502 | solution.py:1109
  36.9 4.4 all-to-all-start.1
  47.4 3.0 multiply_sine_fusion
  50.4 3.1 rotary_rows.1
  53.5 12.1 %collective-permute-done.45 = bf16[128,1536]{1,0:T(8,128)(2,1)} collective-permute-done((bf16[128,1536]{1,0:T(8,128)(2,1)}, bf16[128,1536]{1,0:T(8,128)(2,1)}, u32[]{:S(2)}, u32[]{:S(2)}) %collective-permute-start.45) | collective-permute-done | bytes 393248 | tf_op jit(solution)/shard_map/cond/branch_1_fun/ppermute | solution.py:1037
  67.7 16.6 %all_to_all.13 = bf16[8,48,1152]{2,1,0:T(8,128)(2,1)} all-to-all(bf16[8,48,1152]{2,1,0:T(8,128)(2,1)S(1)} %after.4), channel_id=1, replica_groups=mesh['dp'=4,'x'=2,'y'=2,'c'=2] {'x','y','c'}, dimensions={0} | all-to-all | bytes 1769472 | tf_op jit(solution)/shard_map/all_to_all | solution.py:1113
  84.5 3.4 turn.1
  89.0 30.2 %conditional.16 = (bf16[192,1536]{1,0:T(8,128)(2,1)}, bf16[192,1536]{1,0:T(8,128)(2,1)}, bf16[192,1536]{1,0:T(8,128)(2,1)}, bf16[192,1536]{1,0:T(8,128)(2,1)}, b...) conditional(s32[]{:T(128)} %convert_element_type.79, () %tuple.139, ...), branch_computations={%region_4.0_spmd, %region_5.0_spmd} | conditional | flops 2 | bytes 17826128 | solution.py:1109
  93.0 10.5 %norm_project.1 = (bf16[2048,1536]{1,0:T(8,128)(2,1)}, bf16[2048,320]{1,0:T(8,128)(2,1)}) custom-call(bf16[256,1536]{1,0:T(8,128)(2,1)S(1)} %get-tuple-element.409.refs_0_, bf16[256,1536]{1,0:T(8,128)(2,1)} %get-tuple-element.410.refs_1_, bf16[256,1536]{1,0:T(8,128)(2,1)} %get-tuple-element.411.refs_2_, bf16[256,1536]{1,0:T(8,128)(2,1)} %get-tuple-element.412.refs_3_, ...), custom_call_target="tpu_custom_call" | custom-call | flops 1 | bytes 1 | tf_op jit(solution)/shard_map/cond/branch_1_fun/norm_project/pallas_call | solution.py:438
  103.5 15.7 %attend_forward.1 = (bf16[2,1,256,192]{3,2,1,0:T(8,128)(2,1)}, bf16[2,1,256,192]{3,2,1,0:T(8,128)(2,1)}, bf16[2,1,256,192]{3,2,1,0:T(8,128)(2,1)}, bf16[2,1,256,...) custom-call(s32[1]{0:T(128)} %get-tuple-element.421.place_ref, ...), custom_call_target="tpu_custom_call" | custom-call | flops 1 | bytes 1 | tf_op jit(solution)/shard_map/cond/branch_1_fun/attend_forward/pallas_call | solution.py:256
  119.2 52.4 %conditional.17 = (f32[256,1536]{1,0:T(8,128)}, bf16[256,1536]{1,0:T(8,128)(2,1)}, bf16[256,1536]{1,0:T(8,128)(2,1)}, bf16[256,1536]{1,0:T(8,128)(2,1)}, bf16[25...) conditional(s32[]{:T(128)} %convert_element_type.79, () %tuple.138, ...), branch_computations={%region_6.0_spmd, %region_7.0_spmd} | conditional | flops 2 | bytes 45810620 | solution.py:1109
  122.8 5.2 %collective-permute-done.8.refs_3_ = bf16[384,256]{1,0:T(8,128)(2,1)S(1)} collective-permute-done((bf16[384,256]{1,0:T(8,128)(2,1)S(1)}, bf16[384,256]{1,0:T(8,128)(2,1)S(1)}, u32[]{:S(2)}, u32[]{:S(2)}) %collective-permute-start.8) | collective-permute-done | bytes 196640 | tf_op jit(solution)/shard_map/cond/branch_1_fun/ppermute | solution.py:1063
  139.3 5.5 %attend_out.1 = (f32[256,1536]{1,0:T(8,128)}, bf16[256,1536]{1,0:T(8,128)(2,1)}) custom-call(bf16[384,256]{1,0:T(8,128)(2,1)S(1)} %bitcast.100, bf16[384,256]{1,0:T(8,128)(2,1)S(1)} %copy-done.1, bf16[384,256]{1,0:T(8,128)(2,1)S(1)} %copy-done.5, bf16[384,256]{1,0:T(8,128)(2,1)S(1)} %copy-done.3, ...), custom_call_target="tpu_custom_call" | custom-call | flops 1 | bytes 1 | tf_op jit(solution)/shard_map/cond/branch_1_fun/attend_out/pallas_call | solution.py:697
  147.3 7.8 %collective-permute-done.17 = bf16[256,1536]{1,0:T(8,128)(2,1)} collective-permute-done((bf16[256,1536]{1,0:T(8,128)(2,1)}, bf16[256,1536]{1,0:T(8,128)(2,1)}, u32[]{:S(2)}, u32[]{:S(2)}) %collective-permute-start.17) | collective-permute-done | bytes 786464 | tf_op jit(solution)/shard_map/cond/branch_1_fun/ppermute | solution.py:1037
  156.0 15.0 %collective-permute-done.14 = bf16[256,1536]{1,0:T(8,128)(2,1)} collective-permute-done((bf16[256,1536]{1,0:T(8,128)(2,1)}, bf16[256,1536]{1,0:T(8,128)(2,1)}, u32[]{:S(2)}, u32[]{:S(2)}) %collective-permute-start.14) | collective-permute-done | bytes 786464 | tf_op jit(solution)/shard_map/cond/branch_1_fun/ppermute | solution.py:1037
  171.7 22.5 %conditional.18 = (bf16[256,1536]{1,0:T(8,128)(2,1)}, bf16[256,1536]{1,0:T(8,128)(2,1)}, bf16[256,1536]{1,0:T(8,128)(2,1)}, bf16[256,1536]{1,0:T(8,128)(2,1)}, b...) conditional(s32[]{:T(128)} %convert_element_type.79, () %tuple.146, ...), branch_computations={%region_8.0_spmd, %region_9.0_spmd} | conditional | flops 2 | bytes 12583138 | solution.py:1109
  171.7 2.6 halves.4
  176.9 12.8 %feed_forward.5 = (bf16[768,1024]{1,0:T(8,128)(2,1)}, bf16[768,512]{1,0:T(8,128)(2,1)}, bf16[256,1536]{1,0:T(8,128)(2,1)}, bf16[512,1536]{1,0:T(8,128)(2,1)}) custom-call(bf16[256,1536]{1,0:T(8,128)(2,1)} %get-tuple-element.454.refs_0_, bf16[256,1536]{1,0:T(8,128)(2,1)} %get-tuple-element.448.refs_0_.refs_1_, ...), custom_call_target="tpu_custom_call" | custom-call | flops 1 | bytes 1 | tf_op jit(solution)/shard_map/cond/branch_1_fun/feed_forward/pallas_call | solution.py:494
  189.7 3.2 collective-permute-done.21
  200.0 35.0 %conditional.19 = (bf16[1280,512]{1,0:T(8,128)(2,1)}, bf16[256,1536]{1,0:T(8,128)(2,1)}, bf16[1024,1536]{1,0:T(8,128)(2,1)}, bf16[1536,1536]{1,0:T(8,128)(2,1)},...) conditional(s32[]{:T(128)} %convert_element_type.79, () %tuple.149, (bf16[256,1536]{1,0:T(8,128)(2,1)S(1)}, ...), branch_computations={%region_10.0_spmd, %region_11.0_spmd} | conditional | flops 2 | bytes 17301690 | solution.py:1109
  202.0 17.9 %feed_forward.6 = (bf16[1280,1024]{1,0:T(8,128)(2,1)}, bf16[1280,512]{1,0:T(8,128)(2,1)}, bf16[256,1536]{1,0:T(8,128)(2,1)}, bf16[1024,1536]{1,0:T(8,128)(2,1)}) custom-call(bf16[256,1536]{1,0:T(8,128)(2,1)S(1)} %get-tuple-element.461.refs_0_.refs_3_, bf16[256,1536]{1,0:T(8,128)(2,1)} %get-tuple-element.462.refs_1_.refs_4_, ...), custom_call_target="tpu_custom_call" | custom-call | flops 1 | bytes 1 | tf_op jit(solution)/shard_map/cond/branch_1_fun/feed_forward/pallas_call | solution.py:494
  219.9 15.0 %weight_grads.3 = bf16[1536,1536]{1,0:T(8,128)(2,1)} custom-call(bf16[256,1536]{1,0:T(8,128)(2,1)} %get-tuple-element.475.refs_0_, bf16[256,1536]{1,0:T(8,128)(2,1)} %get-tuple-element.476.refs_1_, bf16[256,1536]{1,0:T(8,128)(2,1)} %get-tuple-element.477.refs_2_, bf16[256,1536]{1,0:T(8,128)(2,1)S(1)} %get-tuple-element.461.refs_0_.refs_3_, ...), custom_call_target="tpu_custom_call" | custom-call | flops 1 | bytes 1 | tf_op jit(solution)/shard_map/cond/branch_1_fun/weight_grads/pallas_call | solution.py:595
  235.0 2.2 halves.5
  237.3 3.5 all-gather.6.cloned.1.call-done.refs_4_
  240.8 19.4 %conditional.20 = (bf16[160,1536]{1,0:T(8,128)(2,1)}, bf16[160,1536]{1,0:T(8,128)(2,1)}, bf16[1280,768]{1,0:T(8,128)(2,1)}, bf16[1280,384]{1,0:T(8,128)(2,1)}, b...) conditional(s32[]{:T(128)} %convert_element_type.79, () %tuple.148, (bf16[160,1536]{1,0:T(8,128)(2,1)}, ...), branch_computations={%region_12.0_spmd, %region_13.0_spmd} | conditional | flops 393217 | bytes 8650814 | solution.py:1109
  243.8 15.0 %feed_forward.7 = (bf16[1280,768]{1,0:T(8,128)(2,1)}, bf16[1280,384]{1,0:T(8,128)(2,1)}, bf16[256,1536]{1,0:T(8,128)(2,1)}, bf16[1024,1536]{1,0:T(8,128)(2,1)S(1)}) custom-call(bf16[256,1536]{1,0:T(8,128)(2,1)S(1)} %get-tuple-element.487.refs_0_, bf16[256,1536]{1,0:T(8,128)(2,1)} %get-tuple-element.488.refs_1_, ...), custom_call_target="tpu_custom_call" | custom-call | flops 1 | bytes 1 | tf_op jit(solution)/shard_map/cond/branch_1_fun/feed_forward/pallas_call | solution.py:494
  260.2 8.4 %feed_forward.9 = (bf16[512,768]{1,0:T(8,128)(2,1)}, bf16[512,384]{1,0:T(8,128)(2,1)S(1)}, bf16[512,1536]{1,0:T(8,128)(2,1)}) custom-call(bf16[256,1536]{1,0:T(8,128)(2,1)} %get-tuple-element.809.refs_0_, bf16[256,1536]{1,0:T(8,128)(2,1)} %get-tuple-element.810.refs_1_, bf16[256,1536]{1,0:T(8,128)(2,1)} %get-tuple-element.811.refs_2_, ...), custom_call_target="tpu_custom_call" | custom-call | flops 1 | bytes 1 | tf_op jit(solution)/shard_map/feed_forward/pallas_call | solution.py:494
  268.7 3.8 add_convert_fusion.2
  272.5 37.9 %conditional.21 = (bf16[256,1536]{1,0:T(8,128)(2,1)}, bf16[256,1536]{1,0:T(8,128)(2,1)}, bf16[256,1536]{1,0:T(8,128)(2,1)}, bf16[256,1536]{1,0:T(8,128)(2,1)}, b...) conditional(s32[]{:T(128)} %convert_element_type.79, () %tuple.137, ...), branch_computations={%region_14.0_spmd, %region_15.0_spmd} | conditional | flops 3 | bytes 12976218 | solution.py:1109
  273.2 2.8 collective-permute-start.31
  276.0 4.1 feed_forward.8
  280.0 13.4 %project_back.1 = (bf16[256,1536]{1,0:T(8,128)(2,1)}, bf16[512,1536]{1,0:T(8,128)(2,1)}, bf16[256,1536]{1,0:T(8,128)(2,1)}, bf16[1024,1536]{1,0:T(8,128)(2,1)}) custom-call(bf16[768,512]{1,0:T(8,128)(2,1)} %get-tuple-element.532.refs_0_, bf16[1280,512]{1,0:T(8,128)(2,1)} %get-tuple-element.533.refs_1_, bf16[256,384]{1,0:T(8,128)(2,1)} %get-tuple-element.529.refs_19_.refs_2_, ...), custom_call_target="tpu_custom_call" | custom-call | flops 1 | bytes 1 | tf_op jit(solution)/shard_map/cond/branch_1_fun/project_back/pallas_call | solution.py:646
  293.4 13.8 %weight_grads.4 = bf16[1536,1152]{1,0:T(8,128)(2,1)} custom-call(bf16[256,1536]{1,0:T(8,128)(2,1)} %get-tuple-element.507.refs_0_, bf16[256,1536]{1,0:T(8,128)(2,1)} %get-tuple-element.512.refs_1_, bf16[256,1536]{1,0:T(8,128)(2,1)} %get-tuple-element.513.refs_2_, bf16[256,1536]{1,0:T(8,128)(2,1)} %get-tuple-element.514.refs_3_, ...), custom_call_target="tpu_custom_call" | custom-call | flops 1 | bytes 1 | tf_op jit(solution)/shard_map/cond/branch_1_fun/weight_grads/pallas_call | solution.py:595
  307.2 3.2 collective-permute-done.31
  311.2 8.1 %middle_back.1 = (f32[256,1536]{1,0:T(8,128)}, bf16[256,1536]{1,0:T(8,128)(2,1)}, bf16[2,192,256]{2,1,0:T(8,128)(2,1)S(1)}, bf16[2,192,256]{2,1,0:T(8,128)(2,1)S...) custom-call(bf16[256,1536]{1,0:T(8,128)(2,1)} %get-tuple-element.845.refs_0_, ...), custom_call_target="tpu_custom_call" | custom-call | flops 1 | bytes 1 | tf_op jit(solution)/shard_map/middle_back/pallas_call | solution.py:756
  319.9 2.9 collective-permute-start.64
  322.9 4.2 collective-permute-done.63.refs_2_
  327.1 3.6 collective-permute-done.62.refs_1_
  333.5 21.4 %conditional.22 = (bf16[256,1536]{1,0:T(8,128)(2,1)}, bf16[256,1536]{1,0:T(8,128)(2,1)}, bf16[256,1536]{1,0:T(8,128)(2,1)}, bf16[2,1,256,320]{3,2,1,0:T(8,128)(2...) conditional(s32[]{:T(128)} %convert_element_type.79, () %tuple.136, ...), branch_computations={%region_17.0_spmd, %region_18.0_spmd} | conditional | flops 9 | bytes 15335739 | solution.py:1109
  335.5 15.9 %attend_backward.2 = (bf16[2,1,256,320]{3,2,1,0:T(8,128)(2,1)}, bf16[2,1,256,320]{3,2,1,0:T(8,128)(2,1)}, bf16[2,1,320,256]{3,2,1,0:T(8,128)(2,1)S(1)}, bf16[2,1,320,256]{3,2,1,0:T(8,128)(2,1)}, f32[1,8,256]{2,1,0:T(8,128)S(1)}) custom-call(s32[1]{0:T(128)} %get-tuple-element.540.place_ref, bf16[2,2,2,1,256,320]{5,4,3,2,1,0:T(8,128)(2,1)} %bitcast.16.qkv_ref, ...), custom_call_target="tpu_custom_call" | custom-call | flops 1 | bytes 1 | tf_op jit(solution)/shard_map/cond/branch_1_fun/attend_backward/pallas_call | solution.py:320
  354.9 20.4 %conditional.23 = (bf16[256,1536]{1,0:T(8,128)(2,1)}, bf16[192,1536]{1,0:T(8,128)(2,1)}, bf16[256,1536]{1,0:T(8,128)(2,1)}, bf16[256,1536]{1,0:T(8,128)(2,1)}, b...) conditional(s32[]{:T(128)} %convert_element_type.79, () %tuple.154, ...), branch_computations={%region_19.0_spmd, %region_20.0_spmd} | conditional | flops 1 | bytes 11796713 | solution.py:1109
  356.9 15.7 %attend_backward.3 = (bf16[2,1,256,320]{3,2,1,0:T(8,128)(2,1)}, bf16[2,1,256,320]{3,2,1,0:T(8,128)(2,1)}, bf16[2,1,320,256]{3,2,1,0:T(8,128)(2,1)}, bf16[2,1,320,256]{3,2,1,0:T(8,128)(2,1)}, f32[1,8,256]{2,1,0:T(8,128)S(1)}) custom-call(s32[1]{0:T(128)} %get-tuple-element.560.place_ref, bf16[2,2,2,1,256,320]{5,4,3,2,1,0:T(8,128)(2,1)} %bitcast.27.qkv_ref, ...), custom_call_target="tpu_custom_call" | custom-call | flops 1 | bytes 1 | tf_op jit(solution)/shard_map/cond/branch_1_fun/attend_backward/pallas_call | solution.py:320
  372.7 2.6 collective-permute-done.32
  375.2 2.5 collective-permute-done.66
  377.7 19.2 %conditional.24 = (bf16[640,256]{1,0:T(8,128)(2,1)}, bf16[640,256]{1,0:T(8,128)(2,1)}, bf16[640,256]{1,0:T(8,128)(2,1)}, bf16[1536,640]{1,0:T(8,128)(2,1)S(1)}, ...) conditional(s32[]{:T(128)} %convert_element_type.79, () %tuple.135, ...), branch_computations={%region_21.0_spmd, %region_22.0_spmd} | conditional | flops 2 | bytes 8388842 | solution.py:1109
  381.2 4.7 %sent_sums.1 = (bf16[256,1536]{1,0:T(8,128)(2,1)}, bf16[256,1536]{1,0:T(8,128)(2,1)}, bf16[256,1536]{1,0:T(8,128)(2,1)}) custom-call(bf16[512,1536]{1,0:T(8,128)(2,1)} %get-tuple-element.600.sides_ref, bf16[256,1536]{1,0:T(8,128)(2,1)} %get-tuple-element.601.corner_ref, bf16[1024,1536]{1,0:T(8,128)(2,1)} %get-tuple-element.602.far_ref), custom_call_target="tpu_custom_call" | custom-call | flops 1 | bytes 1 | tf_op jit(solution)/shard_map/cond/branch_1_fun/sent_sums/pallas_call | solution.py:815
  385.9 11.0 %weight_grads.5 = bf16[1536,640]{1,0:T(8,128)(2,1)S(1)} custom-call(bf16[2048,1536]{1,0:T(8,128)(2,1)} %get-tuple-element.579.refs_0_, bf16[512,320]{1,0:T(8,128)(2,1)} %bitcast.102, bf16[512,320]{1,0:T(8,128)(2,1)S(1)} %bitcast.101, bf16[512,320]{1,0:T(8,128)(2,1)} %bitcast.104, bf16[512,320]{1,0:T(8,128)(2,1)} %bitcast.103, ...), custom_call_target="tpu_custom_call" | custom-call | flops 1 | bytes 1 | tf_op jit(solution)/shard_map/cond/branch_1_fun/weight_grads/pallas_call | solution.py:595
  398.8 20.1 %conditional.25 = (bf16[128,1536]{1,0:T(8,128)(2,1)}, bf16[128,1536]{1,0:T(8,128)(2,1)}, bf16[192,1152]{1,0:T(8,128)(2,1)}, bf16[1280,256]{1,0:T(8,128)(2,1)}, bf16[320,1536]{1,0:T(8,128)(2,1)S(1)}) conditional(s32[]{:T(128)} %convert_element_type.79, () %tuple.158, (bf16[256,1536]{1,0:T(8,128)(2,1)}, bf16[384,1152]{1,0:T(8,128)(2,1)S(1)}, ...), branch_computations={%region_24.0_spmd, %region_25.0_spmd} | conditional | flops 10 | bytes 13140292 | solution.py:1109
  405.3 8.6 %collective-permute-done.55 = bf16[128,1536]{1,0:T(8,128)(2,1)} collective-permute-done((bf16[128,1536]{1,0:T(8,128)(2,1)}, bf16[128,1536]{1,0:T(8,128)(2,1)}, u32[]{:S(2)}, u32[]{:S(2)}) %collective-permute-start.55) | collective-permute-done | bytes 393248 | tf_op jit(solution)/shard_map/cond/branch_1_fun/ppermute | solution.py:1037
  413.9 4.9 %collective-permute-done.54 = bf16[128,1536]{1,0:T(8,128)(2,1)} collective-permute-done((bf16[128,1536]{1,0:T(8,128)(2,1)S(1)}, bf16[128,1536]{1,0:T(8,128)(2,1)}, u32[]{:S(2)}, u32[]{:S(2)}) %collective-permute-start.54) | collective-permute-done | bytes 393248 | tf_op jit(solution)/shard_map/cond/branch_1_fun/ppermute | solution.py:1037
  418.9 3.3 corner_sum.1
  422.1 22.8 %conditional.26 = (bf16[256,1536]{1,0:T(8,128)(2,1)}, bf16[256,1536]{1,0:T(8,128)(2,1)}, f32[192,1728]{1,0:T(8,128)}, f32[192,1728]{1,0:T(8,128)}, f32[192,1728]{1,0:T(8,128)}, /*index=5*/f32[1,256,1536]{2,1,0:T(8,128)}) conditional(s32[]{:T(128)} %convert_element_type.79, () %tuple.157, (bf16[256,1536]{1,0:T(8,128)(2,1)}, ...), branch_computations={%region_26.0_spmd, %region_27.0_spmd} | conditional | flops 1 | bytes 32244056 | solution.py:1109
  425.7 3.8 unpack_columns.2
  429.5 7.2 %input_back.1 = f32[256,1536]{1,0:T(8,128)} custom-call(bf16[640,256]{1,0:T(8,128)(2,1)S(1)} %get-tuple-element.624.refs_0_, bf16[640,256]{1,0:T(8,128)(2,1)} %get-tuple-element.625.refs_1_, bf16[640,256]{1,0:T(8,128)(2,1)} %get-tuple-element.626.refs_2_, bf16[640,256]{1,0:T(8,128)(2,1)} %get-tuple-element.627.refs_3_, ...), custom_call_target="tpu_custom_call" | custom-call | flops 1 | bytes 1 | tf_op jit(solution)/shard_map/cond/branch_1_fun/input_back/pallas_call | solution.py:787
  436.8 6.3 %collective-permute-done.39 = bf16[256,1536]{1,0:T(8,128)(2,1)} collective-permute-done((bf16[256,1536]{1,0:T(8,128)(2,1)}, bf16[256,1536]{1,0:T(8,128)(2,1)}, u32[]{:S(2)}, u32[]{:S(2)}) %collective-permute-start.39) | collective-permute-done | bytes 786464 | tf_op jit(solution)/shard_map/cond/branch_1_fun/ppermute | solution.py:1037
  444.9 8.3 %conditional.27 = (bf16[192,640]{1,0:T(8,128)(2,1)}, bf16[1,256,1536]{2,1,0:T(8,128)(2,1)S(1)}) conditional(s32[]{:T(128)} %convert_element_type.79, () %tuple.134, (bf16[384,640]{1,0:T(8,128)(2,1)}, bf16[256,1536]{1,0:T(8,128)(2,1)}, bf16[1024,1536]{1,0:T(8,128)(2,1)}, bf16[256,1536]{1,0:T(8,128)(2,1)}, bf16[256,1536]{1,0:T(8,128)(2,1)}, ...), branch_computations={%region_29.0_spmd, %region_30.0_spmd} | conditional | flops 3538952 | bytes 6979734 | solution.py:1109
  446.6 2.3 fusion
  449.0 4.3 collective-permute-done.53
  453.2 2.4 unpack_columns.3
  (262 shorter events, 89.4 us)
Async XLA Ops:
  7.2 77.3 %all-gather.4.cloned.1.call-start = ((), (), s32[]{:S(2)}) async-start(), calls=%async_computation.6 | async-start | bytes 2457600 | tf_op jit(solution)/shard_map/all_gather | solution.py:1096
  9.2 27.5 %collective-permute-start.1 = (bf16[256,1536]{1,0:T(8,128)(2,1)}, bf16[256,1536]{1,0:T(8,128)(2,1)}, u32[]{:S(2)}, u32[]{:S(2)}) collective-permute-start(bf16[256,1536]{1,0:T(8,128)(2,1)} %get-tuple-element.394), channel_id=1, source_target_pairs={{0,4},{4,0},{1,5},{5,1},{2,6},{6,2},{3,7},{7,3},{8,12},{12,8},{9,1... | collective-permute-start | bytes 2359304 | tf_op jit(solution)/shard_map/cond/branch_1_fun/ppermute | solution.py:1037
  12.2 24.6 %collective-permute-start = (bf16[256,1536]{1,0:T(8,128)(2,1)}, bf16[256,1536]{1,0:T(8,128)(2,1)}, u32[]{:S(2)}, u32[]{:S(2)}) collective-permute-start(bf16[256,1536]{1,0:T(8,128)(2,1)} %get-tuple-element.394), channel_id=1, source_target_pairs={{0,2},{2,0},{1,3},{3,1},{4,6},{6,4},{5,7},{7,5},{8,10},{10,8},{9,1... | collective-permute-start | bytes 2359304 | tf_op jit(solution)/shard_map/cond/branch_1_fun/ppermute | solution.py:1037
  13.7 23.1 %all-to-all-start = ((bf16[8,48,640]{2,1,0:T(8,128)(2,1)}), bf16[8,48,640]{2,1,0:T(8,128)(2,1)}, u32[]{:S(2)}, u32[]{:S(2)}) async-start(bf16[8,48,640]{2,1,0:T(8,128)(2,1)} %get-tuple-element.393), calls=%async_computation | async-start | bytes 983040 | tf_op jit(solution)/shard_map/cond/branch_1_fun/all_to_all | solution.py:1113
  36.8 134.9 %all-gather.8.cloned.1.call-start = ((), (), s32[]{:S(2)}) async-start(), calls=%async_computation.8 | async-start | bytes 5898240 | tf_op jit(solution)/shard_map/all_gather | solution.py:1096
  36.9 28.7 %all-to-all-start.1 = ((bf16[8,48,1536]{2,1,0:T(8,128)(2,1)}), bf16[8,48,1536]{2,1,0:T(8,128)(2,1)}, u32[]{:S(2)}, u32[]{:S(2)}) async-start(bf16[8,48,1536]{2,1,0:T(8,128)(2,1)} %get-tuple-element.407), calls=%async_computation.1 | async-start | bytes 2359296 | tf_op jit(solution)/shard_map/cond/branch_1_fun/all_to_all | solution.py:1113
  41.3 24.3 %collective-permute-start.47 = (bf16[256,1536]{1,0:T(8,128)(2,1)S(1)}, bf16[256,1536]{1,0:T(8,128)(2,1)}, u32[]{:S(2)}, u32[]{:S(2)}) collective-permute-start(bf16[256,1536]{1,0:T(8,128)(2,1)S(1)} %copy-done.22), channel_id=1, source_target_pairs={{0,1},{1,0},{2,3},{3,2},{4,5},{5,4},{6,7},{7,6},{8,9},{9,8},{10,11... | collective-permute-start | bytes 2359304 | tf_op jit(solution)/shard_map/cond/branch_1_fun/ppermute | solution.py:1037
  41.7 23.9 %collective-permute-start.48 = (bf16[256,1536]{1,0:T(8,128)(2,1)}, bf16[256,1536]{1,0:T(8,128)(2,1)}, u32[]{:S(2)}, u32[]{:S(2)}) collective-permute-start(bf16[256,1536]{1,0:T(8,128)(2,1)} %get-tuple-element.400.refs_0_), channel_id=1, source_target_pairs={{0,1},{1,0},{2,3},{3,2},{4,5},{5,4},{6,7},{7,6},{8,9},{9,8},{10,11... | collective-permute-start | bytes 2359304 | tf_op jit(solution)/shard_map/cond/branch_1_fun/ppermute | solution.py:1037
  41.9 23.7 %collective-permute-start.49 = (bf16[256,1536]{1,0:T(8,128)(2,1)}, bf16[256,1536]{1,0:T(8,128)(2,1)}, u32[]{:S(2)}, u32[]{:S(2)}) collective-permute-start(bf16[256,1536]{1,0:T(8,128)(2,1)} %get-tuple-element.401.refs_1_), channel_id=1, source_target_pairs={{0,1},{1,0},{2,3},{3,2},{4,5},{5,4},{6,7},{7,6},{8,9},{9,8},{10,11... | collective-permute-start | bytes 2359304 | tf_op jit(solution)/shard_map/cond/branch_1_fun/ppermute | solution.py:1037
  44.2 21.4 %collective-permute-start.45 = (bf16[128,1536]{1,0:T(8,128)(2,1)}, bf16[128,1536]{1,0:T(8,128)(2,1)}, u32[]{:S(2)}, u32[]{:S(2)}) collective-permute-start(bf16[128,1536]{1,0:T(8,128)(2,1)} %get-tuple-element.402), channel_id=1, source_target_pairs={{0,4},{4,0},{1,5},{5,1},{2,6},{6,2},{3,7},{7,3},{8,12},{12,8},{9,1... | collective-permute-start | bytes 1179656 | tf_op jit(solution)/shard_map/cond/branch_1_fun/ppermute | solution.py:1037
  45.9 19.7 %collective-permute-start.46 = (bf16[128,1536]{1,0:T(8,128)(2,1)}, bf16[128,1536]{1,0:T(8,128)(2,1)}, u32[]{:S(2)}, u32[]{:S(2)}) collective-permute-start(bf16[128,1536]{1,0:T(8,128)(2,1)} %get-tuple-element.403), channel_id=1, source_target_pairs={{0,2},{2,0},{1,3},{3,1},{4,6},{6,4},{5,7},{7,5},{8,10},{10,8},{9,1... | collective-permute-start | bytes 1179656 | tf_op jit(solution)/shard_map/cond/branch_1_fun/ppermute | solution.py:1037
  65.6 175.1 %all-gather.6.cloned.1.call-start = ((), (), s32[]{:S(2)}) async-start(), calls=%async_computation.7 | async-start | bytes 4423680 | tf_op jit(solution)/shard_map/all_gather | solution.py:1096
  84.3 249.1 %reduce-scatter.4.cloned.1.call-start = ((), (), s32[]{:S(2)}) async-start(), calls=%async_computation.9 | async-start | bytes 5898240 | tf_op jit(solution)/shard_map/reduce_scatter | solution.py:1100
  89.0 30.1 %collective-permute-start.5 = (bf16[192,1536]{1,0:T(8,128)(2,1)S(1)}, bf16[192,1536]{1,0:T(8,128)(2,1)}, u32[]{:S(2)}, u32[]{:S(2)}) collective-permute-start(bf16[192,1536]{1,0:T(8,128)(2,1)S(1)} %get-tuple-element.408), channel_id=1, source_target_pairs={{0,1},{1,0},{2,3},{3,2},{4,5},{5,4},{6,7},{7,6},{8,9},{9,8},{10,11... | collective-permute-start | bytes 1769480 | tf_op jit(solution)/shard_map/cond/branch_1_fun/ppermute | solution.py:1037
  89.5 29.7 %collective-permute-start.4 = (bf16[192,1536]{1,0:T(8,128)(2,1)S(1)}, bf16[192,1536]{1,0:T(8,128)(2,1)}, u32[]{:S(2)}, u32[]{:S(2)}) collective-permute-start(bf16[192,1536]{1,0:T(8,128)(2,1)S(1)} %get-tuple-element.408), channel_id=1, source_target_pairs={{0,6},{2,4},{4,2},{6,0},{1,7},{3,5},{5,3},{7,1},{8,14},{10,12},{12... | collective-permute-start | bytes 1769480 | tf_op jit(solution)/shard_map/cond/branch_1_fun/ppermute | solution.py:1063
  90.3 28.9 %collective-permute-start.3 = (bf16[192,1536]{1,0:T(8,128)(2,1)S(1)}, bf16[192,1536]{1,0:T(8,128)(2,1)}, u32[]{:S(2)}, u32[]{:S(2)}) collective-permute-start(bf16[192,1536]{1,0:T(8,128)(2,1)S(1)} %get-tuple-element.408), channel_id=1, source_target_pairs={{0,4},{4,0},{1,5},{5,1},{2,6},{6,2},{3,7},{7,3},{8,12},{12,8},{9,1... | collective-permute-start | bytes 1769480 | tf_op jit(solution)/shard_map/cond/branch_1_fun/ppermute | solution.py:1037
  91.8 27.4 %collective-permute-start.2 = (bf16[192,1536]{1,0:T(8,128)(2,1)S(1)}, bf16[192,1536]{1,0:T(8,128)(2,1)}, u32[]{:S(2)}, u32[]{:S(2)}) collective-permute-start(bf16[192,1536]{1,0:T(8,128)(2,1)S(1)} %get-tuple-element.408), channel_id=1, source_target_pairs={{0,2},{2,0},{1,3},{3,1},{4,6},{6,4},{5,7},{7,5},{8,10},{10,8},{9,1... | collective-permute-start | bytes 1769480 | tf_op jit(solution)/shard_map/cond/branch_1_fun/ppermute | solution.py:1037
  119.2 8.8 %collective-permute-start.8 = (bf16[384,256]{1,0:T(8,128)(2,1)S(1)}, bf16[384,256]{1,0:T(8,128)(2,1)S(1)}, u32[]{:S(2)}, u32[]{:S(2)}) collective-permute-start(bf16[384,256]{1,0:T(8,128)(2,1)S(1)} %bitcast.112), channel_id=1, source_target_pairs={{0,6},{2,4},{4,2},{6,0},{1,7},{3,5},{5,3},{7,1},{8,14},{10,12},{12... | collective-permute-start | bytes 589832 | tf_op jit(solution)/shard_map/cond/branch_1_fun/ppermute | solution.py:1063
  120.2 9.7 %collective-permute-start.7 = (bf16[384,256]{1,0:T(8,128)(2,1)S(1)}, bf16[384,256]{1,0:T(8,128)(2,1)S(1)}, u32[]{:S(2)}, u32[]{:S(2)}) collective-permute-start(bf16[384,256]{1,0:T(8,128)(2,1)S(1)} %bitcast.113), channel_id=1, source_target_pairs={{0,4},{4,0},{1,5},{5,1},{2,6},{6,2},{3,7},{7,3},{8,12},{12,8},{9,1... | collective-permute-start | bytes 589832 | tf_op jit(solution)/shard_map/cond/branch_1_fun/ppermute | solution.py:1037
  121.6 8.9 %collective-permute-start.6 = (bf16[384,256]{1,0:T(8,128)(2,1)S(1)}, bf16[384,256]{1,0:T(8,128)(2,1)S(1)}, u32[]{:S(2)}, u32[]{:S(2)}) collective-permute-start(bf16[384,256]{1,0:T(8,128)(2,1)S(1)} %bitcast.114), channel_id=1, source_target_pairs={{0,2},{2,0},{1,3},{3,1},{4,6},{6,4},{5,7},{7,5},{8,10},{10,8},{9,1... | collective-permute-start | bytes 589832 | tf_op jit(solution)/shard_map/cond/branch_1_fun/ppermute | solution.py:1037
  122.8 13.3 %collective-permute-start.12 = (bf16[192,1536]{1,0:T(8,128)(2,1)}, bf16[192,1536]{1,0:T(8,128)(2,1)}, u32[]{:S(2)}, u32[]{:S(2)}) collective-permute-start(bf16[192,1536]{1,0:T(8,128)(2,1)} %get-tuple-element.441.refs_11_), channel_id=1, source_target_pairs={{0,1},{1,0},{2,3},{3,2},{4,5},{5,4},{6,7},{7,6},{8,9},{9,8},{10,11... | collective-permute-start | bytes 1769480 | tf_op jit(solution)/shard_map/cond/branch_1_fun/ppermute | solution.py:1037
  132.9 13.4 %collective-permute-start.18 = (bf16[256,1536]{1,0:T(8,128)(2,1)S(1)}, bf16[256,1536]{1,0:T(8,128)(2,1)}, u32[]{:S(2)}, u32[]{:S(2)}) collective-permute-start(bf16[256,1536]{1,0:T(8,128)(2,1)S(1)} %get-tuple-element.447), channel_id=1, source_target_pairs={{0,1},{1,0},{2,3},{3,2},{4,5},{5,4},{6,7},{7,6},{8,9},{9,8},{10,11... | collective-permute-start | bytes 2359304 | tf_op jit(solution)/shard_map/cond/branch_1_fun/ppermute | solution.py:1037
  134.4 20.7 %collective-permute-start.17 = (bf16[256,1536]{1,0:T(8,128)(2,1)}, bf16[256,1536]{1,0:T(8,128)(2,1)}, u32[]{:S(2)}, u32[]{:S(2)}) collective-permute-start(bf16[256,1536]{1,0:T(8,128)(2,1)} %after.3), channel_id=1, source_target_pairs={{0,4},{4,0},{1,5},{5,1},{2,6},{6,2},{3,7},{7,3},{8,12},{12,8},{9,1... | collective-permute-start | bytes 2359304 | tf_op jit(solution)/shard_map/cond/branch_1_fun/ppermute | solution.py:1037
  135.3 20.8 %collective-permute-start.16 = (bf16[256,1536]{1,0:T(8,128)(2,1)}, bf16[256,1536]{1,0:T(8,128)(2,1)}, u32[]{:S(2)}, u32[]{:S(2)}) collective-permute-start(bf16[256,1536]{1,0:T(8,128)(2,1)} %after.3), channel_id=1, source_target_pairs={{0,2},{2,0},{1,3},{3,1},{4,6},{6,4},{5,7},{7,5},{8,10},{10,8},{9,1... | collective-permute-start | bytes 2359304 | tf_op jit(solution)/shard_map/cond/branch_1_fun/ppermute | solution.py:1037
  144.8 11.2 %collective-permute-start.15 = (bf16[256,1536]{1,0:T(8,128)(2,1)}, bf16[256,1536]{1,0:T(8,128)(2,1)}, u32[]{:S(2)}, u32[]{:S(2)}) collective-permute-start(bf16[256,1536]{1,0:T(8,128)(2,1)} %get-tuple-element.1206), channel_id=1, source_target_pairs={{0,1},{1,0},{2,3},{3,2},{4,5},{5,4},{6,7},{7,6},{8,9},{9,8},{10,11... | collective-permute-start | bytes 2359304 | tf_op jit(solution)/shard_map/cond/branch_1_fun/ppermute | solution.py:1037
  145.0 26.1 %collective-permute-start.14 = (bf16[256,1536]{1,0:T(8,128)(2,1)}, bf16[256,1536]{1,0:T(8,128)(2,1)}, u32[]{:S(2)}, u32[]{:S(2)}) collective-permute-start(bf16[256,1536]{1,0:T(8,128)(2,1)} %get-tuple-element.1206), channel_id=1, source_target_pairs={{0,4},{4,0},{1,5},{5,1},{2,6},{6,2},{3,7},{7,3},{8,12},{12,8},{9,1... | collective-permute-start | bytes 2359304 | tf_op jit(solution)/shard_map/cond/branch_1_fun/ppermute | solution.py:1037
  146.3 25.3 %collective-permute-start.13 = (bf16[256,1536]{1,0:T(8,128)(2,1)}, bf16[256,1536]{1,0:T(8,128)(2,1)}, u32[]{:S(2)}, u32[]{:S(2)}) collective-permute-start(bf16[256,1536]{1,0:T(8,128)(2,1)} %get-tuple-element.1206), channel_id=1, source_target_pairs={{0,2},{2,0},{1,3},{3,1},{4,6},{6,4},{5,7},{7,5},{8,10},{10,8},{9,1... | collective-permute-start | bytes 2359304 | tf_op jit(solution)/shard_map/cond/branch_1_fun/ppermute | solution.py:1037
  155.1 16.5 %collective-permute-start.20 = (bf16[256,1536]{1,0:T(8,128)(2,1)}, bf16[256,1536]{1,0:T(8,128)(2,1)}, u32[]{:S(2)}, u32[]{:S(2)}) collective-permute-start(bf16[256,1536]{1,0:T(8,128)(2,1)} %collective-permute-done.17), channel_id=1, source_target_pairs={{0,1},{1,0},{2,3},{3,2},{4,5},{5,4},{6,7},{7,6},{8,9},{9,8},{10,11... | collective-permute-start | bytes 2359304 | tf_op jit(solution)/shard_map/cond/branch_1_fun/ppermute | solution.py:1037
  156.0 15.6 %collective-permute-start.19 = (bf16[256,1536]{1,0:T(8,128)(2,1)}, bf16[256,1536]{1,0:T(8,128)(2,1)}, u32[]{:S(2)}, u32[]{:S(2)}) collective-permute-start(bf16[256,1536]{1,0:T(8,128)(2,1)} %collective-permute-done.16), channel_id=1, source_target_pairs={{0,1},{1,0},{2,3},{3,2},{4,5},{5,4},{6,7},{7,6},{8,9},{9,8},{10,11... | collective-permute-start | bytes 2359304 | tf_op jit(solution)/shard_map/cond/branch_1_fun/ppermute | solution.py:1037
  174.3 18.7 %collective-permute-start.21 = (bf16[256,1536]{1,0:T(8,128)(2,1)}, bf16[256,1536]{1,0:T(8,128)(2,1)}, u32[]{:S(2)}, u32[]{:S(2)}) collective-permute-start(bf16[256,1536]{1,0:T(8,128)(2,1)} %get-tuple-element.452), channel_id=1, source_target_pairs={{0,4},{4,0},{1,5},{5,1},{2,6},{6,2},{3,7},{7,3},{8,12},{12,8},{9,1... | collective-permute-start | bytes 2359304 | tf_op jit(solution)/shard_map/cond/branch_1_fun/ppermute | solution.py:1037
  175.4 18.8 %collective-permute-start.22 = (bf16[256,1536]{1,0:T(8,128)(2,1)}, bf16[256,1536]{1,0:T(8,128)(2,1)}, u32[]{:S(2)}, u32[]{:S(2)}) collective-permute-start(bf16[256,1536]{1,0:T(8,128)(2,1)} %get-tuple-element.453), channel_id=1, source_target_pairs={{0,2},{2,0},{1,3},{3,1},{4,6},{6,4},{5,7},{7,5},{8,10},{10,8},{9,1... | collective-permute-start | bytes 2359304 | tf_op jit(solution)/shard_map/cond/branch_1_fun/ppermute | solution.py:1037
  176.4 17.8 %collective-permute-start.23 = (bf16[256,1536]{1,0:T(8,128)(2,1)}, bf16[256,1536]{1,0:T(8,128)(2,1)}, u32[]{:S(2)}, u32[]{:S(2)}) collective-permute-start(bf16[256,1536]{1,0:T(8,128)(2,1)} %get-tuple-element.448.refs_0_.refs_1_), channel_id=1, source_target_pairs={{0,1},{1,0},{2,3},{3,2},{4,5},{5,4},{6,7},{7,6},{8,9},{9,8},{10,11... | collective-permute-start | bytes 2359304 | tf_op jit(solution)/shard_map/cond/branch_1_fun/ppermute | solution.py:1037
  176.4 17.8 %collective-permute-start.24 = (bf16[256,1536]{1,0:T(8,128)(2,1)}, bf16[256,1536]{1,0:T(8,128)(2,1)}, u32[]{:S(2)}, u32[]{:S(2)}) collective-permute-start(bf16[256,1536]{1,0:T(8,128)(2,1)} %get-tuple-element.449.refs_1_.refs_2_), channel_id=1, source_target_pairs={{0,1},{1,0},{2,3},{3,2},{4,5},{5,4},{6,7},{7,6},{8,9},{9,8},{10,11... | collective-permute-start | bytes 2359304 | tf_op jit(solution)/shard_map/cond/branch_1_fun/ppermute | solution.py:1037
  200.0 34.9 %collective-permute-start.26 = (bf16[320,1536]{1,0:T(8,128)(2,1)}, bf16[320,1536]{1,0:T(8,128)(2,1)}, u32[]{:S(2)}, u32[]{:S(2)}) collective-permute-start(bf16[320,1536]{1,0:T(8,128)(2,1)} %get-tuple-element.484), channel_id=1, source_target_pairs={{0,4},{4,0},{1,5},{5,1},{2,6},{6,2},{3,7},{7,3},{8,12},{12,8},{9,1... | collective-permute-start | bytes 2949128 | tf_op jit(solution)/shard_map/cond/branch_1_fun/ppermute | solution.py:1037
  200.5 34.4 %collective-permute-start.25 = (bf16[320,1536]{1,0:T(8,128)(2,1)}, bf16[320,1536]{1,0:T(8,128)(2,1)}, u32[]{:S(2)}, u32[]{:S(2)}) collective-permute-start(bf16[320,1536]{1,0:T(8,128)(2,1)} %get-tuple-element.484), channel_id=1, source_target_pairs={{0,2},{2,0},{1,3},{3,1},{4,6},{6,4},{5,7},{7,5},{8,10},{10,8},{9,1... | collective-permute-start | bytes 2949128 | tf_op jit(solution)/shard_map/cond/branch_1_fun/ppermute | solution.py:1037
  235.0 162.0 %reduce-scatter.6.cloned.1.call-start = ((), (), s32[]{:S(2)}) async-start(), calls=%async_computation.10 | async-start | bytes 4423680 | tf_op jit(solution)/shard_map/reduce_scatter | solution.py:1100
  240.8 19.4 %collective-permute-start.27 = (bf16[160,1536]{1,0:T(8,128)(2,1)}, bf16[160,1536]{1,0:T(8,128)(2,1)}, u32[]{:S(2)}, u32[]{:S(2)}) collective-permute-start(bf16[160,1536]{1,0:T(8,128)(2,1)} %get-tuple-element.485), channel_id=1, source_target_pairs={{0,4},{4,0},{1,5},{5,1},{2,6},{6,2},{3,7},{7,3},{8,12},{12,8},{9,1... | collective-permute-start | bytes 1474568 | tf_op jit(solution)/shard_map/cond/branch_1_fun/ppermute | solution.py:1037
  242.3 17.8 %collective-permute-start.28 = (bf16[160,1536]{1,0:T(8,128)(2,1)}, bf16[160,1536]{1,0:T(8,128)(2,1)}, u32[]{:S(2)}, u32[]{:S(2)}) collective-permute-start(bf16[160,1536]{1,0:T(8,128)(2,1)} %get-tuple-element.486), channel_id=1, source_target_pairs={{0,2},{2,0},{1,3},{3,1},{4,6},{6,4},{5,7},{7,5},{8,10},{10,8},{9,1... | collective-permute-start | bytes 1474568 | tf_op jit(solution)/shard_map/cond/branch_1_fun/ppermute | solution.py:1037
  260.2 8.5 %collective-permute-start.61 = (bf16[1024,1536]{1,0:T(8,128)(2,1)S(1)}, bf16[1024,1536]{1,0:T(8,128)(2,1)S(1)}, u32[]{:S(2)}, u32[]{:S(2)}) collective-permute-start(bf16[1024,1536]{1,0:T(8,128)(2,1)S(1)} %get-tuple-element.836.refs_6_), channel_id=1, source_target_pairs={{0,1},{1,0},{2,3},{3,2},{4,5},{5,4},{6,7},{7,6},{8,9},{9,8},{10,11... | collective-permute-start | bytes 9437192 | tf_op jit(solution)/shard_map/ppermute | solution.py:1037
  272.5 34.7 %collective-permute-start.29 = (bf16[256,1536]{1,0:T(8,128)(2,1)}, bf16[256,1536]{1,0:T(8,128)(2,1)}, u32[]{:S(2)}, u32[]{:S(2)}) collective-permute-start(bf16[256,1536]{1,0:T(8,128)(2,1)} %get-tuple-element.504), channel_id=1, source_target_pairs={{0,2},{2,0},{1,3},{3,1},{4,6},{6,4},{5,7},{7,5},{8,10},{10,8},{9,1... | collective-permute-start | bytes 2359304 | tf_op jit(solution)/shard_map/cond/branch_1_fun/ppermute | solution.py:1037
  272.6 34.6 %collective-permute-start.30 = (bf16[256,1536]{1,0:T(8,128)(2,1)}, bf16[256,1536]{1,0:T(8,128)(2,1)}, u32[]{:S(2)}, u32[]{:S(2)}) collective-permute-start(bf16[256,1536]{1,0:T(8,128)(2,1)} %get-tuple-element.505), channel_id=1, source_target_pairs={{0,4},{4,0},{1,5},{5,1},{2,6},{6,2},{3,7},{7,3},{8,12},{12,8},{9,1... | collective-permute-start | bytes 2359304 | tf_op jit(solution)/shard_map/cond/branch_1_fun/ppermute | solution.py:1037
  273.2 37.2 %collective-permute-start.31 = (bf16[256,1536]{1,0:T(8,128)(2,1)}, bf16[256,1536]{1,0:T(8,128)(2,1)}, u32[]{:S(2)}, u32[]{:S(2)}) collective-permute-start(bf16[256,1536]{1,0:T(8,128)(2,1)} %get-tuple-element.506), channel_id=1, source_target_pairs={{0,6},{2,4},{4,2},{6,0},{1,7},{3,5},{5,3},{7,1},{8,14},{10,12},{12... | collective-permute-start | bytes 2359304 | tf_op jit(solution)/shard_map/cond/branch_1_fun/ppermute | solution.py:1063
  310.4 134.5 %reduce-scatter.8.cloned.1.call-start = ((), (), s32[]{:S(2)}) async-start(), calls=%async_computation.11 | async-start | bytes 2457600 | tf_op jit(solution)/shard_map/reduce_scatter | solution.py:1100
  310.9 64.3 %collective-permute-start.67 = (bf16[1024,1536]{1,0:T(8,128)(2,1)}, bf16[1024,1536]{1,0:T(8,128)(2,1)}, u32[]{:S(2)}, u32[]{:S(2)}) collective-permute-start(bf16[1024,1536]{1,0:T(8,128)(2,1)} %get-tuple-element.885), channel_id=1, source_target_pairs={{0,1},{1,0},{2,3},{3,2},{4,5},{5,4},{6,7},{7,6},{8,9},{9,8},{10,11... | collective-permute-start | bytes 9437192 | tf_op jit(solution)/shard_map/ppermute | solution.py:1037
  319.4 7.7 %collective-permute-start.63 = (bf16[384,256]{1,0:T(8,128)(2,1)S(1)}, bf16[384,256]{1,0:T(8,128)(2,1)S(1)}, u32[]{:S(2)}, u32[]{:S(2)}) collective-permute-start(bf16[384,256]{1,0:T(8,128)(2,1)S(1)} %bitcast.80), channel_id=1, source_target_pairs={{0,4},{4,0},{1,5},{5,1},{2,6},{6,2},{3,7},{7,3},{8,12},{12,8},{9,1... | collective-permute-start | bytes 589832 | tf_op jit(solution)/shard_map/ppermute | solution.py:1037
  319.6 11.2 %collective-permute-start.62 = (bf16[384,256]{1,0:T(8,128)(2,1)S(1)}, bf16[384,256]{1,0:T(8,128)(2,1)S(1)}, u32[]{:S(2)}, u32[]{:S(2)}) collective-permute-start(bf16[384,256]{1,0:T(8,128)(2,1)S(1)} %bitcast.79), channel_id=1, source_target_pairs={{0,2},{2,0},{1,3},{3,1},{4,6},{6,4},{5,7},{7,5},{8,10},{10,8},{9,1... | collective-permute-start | bytes 589832 | tf_op jit(solution)/shard_map/ppermute | solution.py:1037
  319.9 10.8 %collective-permute-start.64 = (bf16[384,256]{1,0:T(8,128)(2,1)S(1)}, bf16[384,256]{1,0:T(8,128)(2,1)S(1)}, u32[]{:S(2)}, u32[]{:S(2)}) collective-permute-start(bf16[384,256]{1,0:T(8,128)(2,1)S(1)} %bitcast.78), channel_id=1, source_target_pairs={{0,6},{2,4},{4,2},{6,0},{1,7},{3,5},{5,3},{7,1},{8,14},{10,12},{12... | collective-permute-start | bytes 589832 | tf_op jit(solution)/shard_map/ppermute | solution.py:1063
  333.5 20.0 %collective-permute-start.51 = (bf16[256,1536]{1,0:T(8,128)(2,1)}, bf16[256,1536]{1,0:T(8,128)(2,1)}, u32[]{:S(2)}, u32[]{:S(2)}) collective-permute-start(bf16[256,1536]{1,0:T(8,128)(2,1)} %get-tuple-element.539), channel_id=1, source_target_pairs={{0,4},{4,0},{1,5},{5,1},{2,6},{6,2},{3,7},{7,3},{8,12},{12,8},{9,1... | collective-permute-start | bytes 2359304 | tf_op jit(solution)/shard_map/cond/branch_1_fun/ppermute | solution.py:1037
  335.2 19.6 %collective-permute-start.50 = (bf16[256,1536]{1,0:T(8,128)(2,1)}, bf16[256,1536]{1,0:T(8,128)(2,1)}, u32[]{:S(2)}, u32[]{:S(2)}) collective-permute-start(bf16[256,1536]{1,0:T(8,128)(2,1)} %get-tuple-element.539), channel_id=1, source_target_pairs={{0,2},{2,0},{1,3},{3,1},{4,6},{6,4},{5,7},{7,5},{8,10},{10,8},{9,1... | collective-permute-start | bytes 2359304 | tf_op jit(solution)/shard_map/cond/branch_1_fun/ppermute | solution.py:1037
  335.5 19.3 %collective-permute-start.52 = (bf16[256,1536]{1,0:T(8,128)(2,1)}, bf16[256,1536]{1,0:T(8,128)(2,1)}, u32[]{:S(2)}, u32[]{:S(2)}) collective-permute-start(bf16[256,1536]{1,0:T(8,128)(2,1)} %get-tuple-element.539), channel_id=1, source_target_pairs={{0,1},{1,0},{2,3},{3,2},{4,5},{5,4},{6,7},{7,6},{8,9},{9,8},{10,11... | collective-permute-start | bytes 2359304 | tf_op jit(solution)/shard_map/cond/branch_1_fun/ppermute | solution.py:1037
  354.9 17.8 %collective-permute-start.34 = (bf16[256,1536]{1,0:T(8,128)(2,1)}, bf16[256,1536]{1,0:T(8,128)(2,1)}, u32[]{:S(2)}, u32[]{:S(2)}) collective-permute-start(bf16[256,1536]{1,0:T(8,128)(2,1)} %get-tuple-element.559), channel_id=1, source_target_pairs={{0,1},{1,0},{2,3},{3,2},{4,5},{5,4},{6,7},{7,6},{8,9},{9,8},{10,11... | collective-permute-start | bytes 2359304 | tf_op jit(solution)/shard_map/cond/branch_1_fun/ppermute | solution.py:1037
  354.9 20.3 %collective-permute-start.32 = (bf16[256,1536]{1,0:T(8,128)(2,1)}, bf16[256,1536]{1,0:T(8,128)(2,1)}, u32[]{:S(2)}, u32[]{:S(2)}) collective-permute-start(bf16[256,1536]{1,0:T(8,128)(2,1)} %get-tuple-element.557), channel_id=1, source_target_pairs={{0,2},{2,0},{1,3},{3,1},{4,6},{6,4},{5,7},{7,5},{8,10},{10,8},{9,1... | collective-permute-start | bytes 2359304 | tf_op jit(solution)/shard_map/cond/branch_1_fun/ppermute | solution.py:1037
  355.3 19.9 %collective-permute-start.35 = (bf16[256,1536]{1,0:T(8,128)(2,1)}, bf16[256,1536]{1,0:T(8,128)(2,1)}, u32[]{:S(2)}, u32[]{:S(2)}) collective-permute-start(bf16[256,1536]{1,0:T(8,128)(2,1)} %get-tuple-element.557), channel_id=1, source_target_pairs={{0,1},{1,0},{2,3},{3,2},{4,5},{5,4},{6,7},{7,6},{8,9},{9,8},{10,11... | collective-permute-start | bytes 2359304 | tf_op jit(solution)/shard_map/cond/branch_1_fun/ppermute | solution.py:1037
  355.5 17.2 %collective-permute-start.33 = (bf16[192,1536]{1,0:T(8,128)(2,1)}, bf16[192,1536]{1,0:T(8,128)(2,1)}, u32[]{:S(2)}, u32[]{:S(2)}) collective-permute-start(bf16[192,1536]{1,0:T(8,128)(2,1)} %get-tuple-element.558), channel_id=1, source_target_pairs={{0,4},{4,0},{1,5},{5,1},{2,6},{6,2},{3,7},{7,3},{8,12},{12,8},{9,1... | collective-permute-start | bytes 1769480 | tf_op jit(solution)/shard_map/cond/branch_1_fun/ppermute | solution.py:1037
  377.7 19.2 %collective-permute-start.38 = (bf16[640,256]{1,0:T(8,128)(2,1)}, bf16[640,256]{1,0:T(8,128)(2,1)}, u32[]{:S(2)}, u32[]{:S(2)}) collective-permute-start(bf16[640,256]{1,0:T(8,128)(2,1)} %get-tuple-element.578), channel_id=1, source_target_pairs={{0,6},{2,4},{4,2},{6,0},{1,7},{3,5},{5,3},{7,1},{8,14},{10,12},{12... | collective-permute-start | bytes 983048 | tf_op jit(solution)/shard_map/cond/branch_1_fun/ppermute | solution.py:1063
  378.9 18.0 %collective-permute-start.37 = (bf16[640,256]{1,0:T(8,128)(2,1)}, bf16[640,256]{1,0:T(8,128)(2,1)}, u32[]{:S(2)}, u32[]{:S(2)}) collective-permute-start(bf16[640,256]{1,0:T(8,128)(2,1)} %get-tuple-element.577), channel_id=1, source_target_pairs={{0,4},{4,0},{1,5},{5,1},{2,6},{6,2},{3,7},{7,3},{8,12},{12,8},{9,1... | collective-permute-start | bytes 983048 | tf_op jit(solution)/shard_map/cond/branch_1_fun/ppermute | solution.py:1037
  379.5 17.4 %collective-permute-start.36 = (bf16[640,256]{1,0:T(8,128)(2,1)}, bf16[640,256]{1,0:T(8,128)(2,1)}, u32[]{:S(2)}, u32[]{:S(2)}) collective-permute-start(bf16[640,256]{1,0:T(8,128)(2,1)} %get-tuple-element.576), channel_id=1, source_target_pairs={{0,2},{2,0},{1,3},{3,1},{4,6},{6,4},{5,7},{7,5},{8,10},{10,8},{9,1... | collective-permute-start | bytes 983048 | tf_op jit(solution)/shard_map/cond/branch_1_fun/ppermute | solution.py:1037
  398.8 20.0 %collective-permute-start.56 = (bf16[192,1152]{1,0:T(8,128)(2,1)S(1)}, bf16[192,1152]{1,0:T(8,128)(2,1)}, u32[]{:S(2)}, u32[]{:S(2)}) collective-permute-start(bf16[192,1152]{1,0:T(8,128)(2,1)S(1)} %constant_dynamic-slice_fusion.1), channel_id=1, source_target_pairs={{0,4},{4,0},{1,5},{5,1},{2,6},{6,2},{3,7},{7,3},{8,12},{12,8},{9,1... | collective-permute-start | bytes 1327112 | tf_op jit(solution)/shard_map/cond/branch_1_fun/ppermute | solution.py:1037
  401.3 17.6 %collective-permute-start.57 = (bf16[1280,256]{1,0:T(8,128)(2,1)}, bf16[1280,256]{1,0:T(8,128)(2,1)}, u32[]{:S(2)}, u32[]{:S(2)}) collective-permute-start(bf16[1280,256]{1,0:T(8,128)(2,1)} %far_parts.4), channel_id=1, source_target_pairs={{0,1},{1,0},{2,3},{3,2},{4,5},{5,4},{6,7},{7,6},{8,9},{9,8},{10,11... | collective-permute-start | bytes 1966088 | tf_op jit(solution)/shard_map/cond/branch_1_fun/ppermute | solution.py:1037
  402.1 11.8 %collective-permute-start.55 = (bf16[128,1536]{1,0:T(8,128)(2,1)}, bf16[128,1536]{1,0:T(8,128)(2,1)}, u32[]{:S(2)}, u32[]{:S(2)}) collective-permute-start(bf16[128,1536]{1,0:T(8,128)(2,1)} %get-tuple-element.1128), channel_id=1, source_target_pairs={{0,2},{2,0},{1,3},{3,1},{4,6},{6,4},{5,7},{7,5},{8,10},{10,8},{9,1... | collective-permute-start | bytes 1179656 | tf_op jit(solution)/shard_map/cond/branch_1_fun/ppermute | solution.py:1037
  403.5 15.4 %collective-permute-start.54 = (bf16[128,1536]{1,0:T(8,128)(2,1)S(1)}, bf16[128,1536]{1,0:T(8,128)(2,1)}, u32[]{:S(2)}, u32[]{:S(2)}) collective-permute-start(bf16[128,1536]{1,0:T(8,128)(2,1)S(1)} %get-tuple-element.1129), channel_id=1, source_target_pairs={{0,4},{4,0},{1,5},{5,1},{2,6},{6,2},{3,7},{7,3},{8,12},{12,8},{9,1... | collective-permute-start | bytes 1179656 | tf_op jit(solution)/shard_map/cond/branch_1_fun/ppermute | solution.py:1037
  423.3 19.8 %collective-permute-start.39 = (bf16[256,1536]{1,0:T(8,128)(2,1)}, bf16[256,1536]{1,0:T(8,128)(2,1)}, u32[]{:S(2)}, u32[]{:S(2)}) collective-permute-start(bf16[256,1536]{1,0:T(8,128)(2,1)} %get-tuple-element.614), channel_id=1, source_target_pairs={{0,2},{2,0},{1,3},{3,1},{4,6},{6,4},{5,7},{7,5},{8,10},{10,8},{9,1... | collective-permute-start | bytes 2359304 | tf_op jit(solution)/shard_map/cond/branch_1_fun/ppermute | solution.py:1037
  425.0 19.9 %collective-permute-start.40 = (bf16[256,1536]{1,0:T(8,128)(2,1)}, bf16[256,1536]{1,0:T(8,128)(2,1)}, u32[]{:S(2)}, u32[]{:S(2)}) collective-permute-start(bf16[256,1536]{1,0:T(8,128)(2,1)} %get-tuple-element.615), channel_id=1, source_target_pairs={{0,4},{4,0},{1,5},{5,1},{2,6},{6,2},{3,7},{7,3},{8,12},{12,8},{9,1... | collective-permute-start | bytes 2359304 | tf_op jit(solution)/shard_map/cond/branch_1_fun/ppermute | solution.py:1037
  445.9 7.3 %collective-permute-start.53 = (bf16[192,640]{1,0:T(8,128)(2,1)S(1)}, bf16[192,640]{1,0:T(8,128)(2,1)}, u32[]{:S(2)}, u32[]{:S(2)}) collective-permute-start(bf16[192,640]{1,0:T(8,128)(2,1)S(1)} %constant_dynamic-slice_fusion.2), channel_id=1, source_target_pairs={{0,4},{4,0},{1,5},{5,1},{2,6},{6,2},{3,7},{7,3},{8,12},{12,8},{9,1... | collective-permute-start | bytes 737288 | tf_op jit(solution)/shard_map/cond/branch_1_fun/ppermute | solution.py:1037
  (63 other events, 587.2 us)
Sparse Core Ops, SparseCore 0:
  36.9 43.8 all-gather.3
  82.4 88.2 all-gather.7
  172.3 68.4 all-gather.5
  242.9 83.8 reduce-scatter.3
  328.9 66.8 reduce-scatter.5
  398.4 41.3 reduce-scatter.7

commit v9 on v8

--- a/solution.py
+++ b/solution.py
@@ -845,6 +845,26 @@
     )(for_y, for_x, by_x, by_y)
 
 
+def rows_from(parts, layouts):
+    def body(*refs):
+        for out, layout in zip(refs[len(parts) :], layouts):
+            at = 0
+            for part, first, last in layout:
+                out[at : at + last - first] = refs[part][first:last]
+                at += last - first
+
+    sizes = [sum(last - first for _, first, last in layout) for layout in layouts]
+    return pl.pallas_call(
+        body,
+        out_shape=[
+            jax.ShapeDtypeStruct((size, parts[0].shape[1]), parts[0].dtype) for size in sizes
+        ],
+        name="rows_from",
+        cost_estimate=cost(0),
+        compiler_params=pltpu.CompilerParams(vmem_limit_bytes=60 << 20),
+    )(*parts)
+
+
 def halves(sides):
     count = len(sides)
     rows, width = sides[0][0].shape[0] // 2, sides[0][0].shape[1]
@@ -931,13 +951,19 @@
     )(weight)
 
 
-def pack_columns(weights, layouts, gains=()):
+def pack_columns(weights, layouts, gains=(), rows_in=None, cuts=()):
     rows = weights[0].shape[0]
     count = len(weights)
     spans = [w.shape[1] // 8 for w in weights]
 
     def body(*refs):
-        outs = refs[count + len(gains) :]
+        extra = rows_in is not None
+        outs = refs[count + len(gains) + extra :]
+        for out, parts in zip(outs[len(layouts) :], cuts):
+            at = 0
+            for first, last in parts:
+                out[at : at + last - first] = refs[count + len(gains)][first:last]
+                at += last - first
         columns = None
         if gains:
             lane = lax.broadcasted_iota(jnp.int32, (rows, GAIN_LANES), 1)
@@ -973,10 +999,16 @@
         out_shape=[
             jax.ShapeDtypeStruct((8, rows, sum(lanes(e) for e in layout)), BF16)
             for layout in layouts
+        ]
+        + [
+            jax.ShapeDtypeStruct(
+                (sum(last - first for first, last in parts), rows_in.shape[1]), rows_in.dtype
+            )
+            for parts in cuts
         ],
         name="pack_columns",
         compiler_params=pltpu.CompilerParams(vmem_limit_bytes=60 << 20),
-    )(*weights, *gains)
+    )(*weights, *gains, *([] if rows_in is None else [rows_in]))
 
 
 def unpack_columns(x, sums, others, outputs, dtype=F32):
@@ -1148,17 +1180,25 @@
     own_upstream = upstream.reshape(own_rows, model_width)
     cut = 512
     rest = -(wide - cut) % 128
-    (first_payload,) = pack_columns(
+    half, quarter = own_rows // 2, own_rows // 4
+    first_payload, early_y, early_x, late_y, late_x = pack_columns(
         [query_weight, key_weight, value_weight, output_weight],
         [
             [(0, 0, query_cols), (1, 0, kv_cols), (2, 0, kv_cols), None, (3, 0, query_cols)]
             + [GAIN_LANES]
         ],
         gain_rows,
-    )
-
-
-    def start(payload, own_hidden, weights):
+        own_hidden,
+        [
+            [(0, 3 * quarter)],
+            [(half, own_rows), (quarter, half)],
+            [(3 * quarter, own_rows)],
+            [(0, quarter)],
+        ],
+    )
+
+
+    def start(payload, early_y, early_x, weights):
         payloads = pack_columns(
             weights,
             [
@@ -1166,23 +1206,33 @@
                 [(0, cut, wide), rest, (1, cut, wide), rest, (2, cut, wide), rest],
             ],
         )
-        return plane_columns(payload), sides_come(own_hidden), payloads
-
-    first_block, hidden_sides, payloads = together(
-        start, first_payload, own_hidden, [gate_weight, up_weight, down_weight]
+        return plane_columns(payload), (swap(early_y, "y"), swap(early_x, "x")), payloads
+
+    first_block, early, payloads = together(
+        start, first_payload, early_y, early_x, [gate_weight, up_weight, down_weight]
     )
     first_full = line_gather(first_block)
     out_first = qkv_cols + GAIN_LANES
 
-    def hidden_corner(own_hidden, hidden_sides, payload):
-        come = corners_come(hidden_sides), across([own_hidden, *hidden_sides])
-        return *come, rotary_rows(4 * tokens), plane_columns(payload)
-
-    corner, far, (cosine, sine), early_block = together(
-        hidden_corner, own_hidden, hidden_sides, payloads[0]
-    )
-    (corner,) = joined(*corner, 1)
-    late_block = plane_columns(after(payloads[1], early_block, corner))
+    def hidden_rest(own_hidden, early, late_y, late_x, payload):
+        by_x, by_y = rows_from(early, [[(0, 0, half)], [(1, 0, half)]])
+        corner = swap(by_x, "x"), swap(by_y, "y")
+        late = swap(late_y, "y"), swap(late_x, "x")
+        own = swap(own_hidden, "c")
+        return corner, late, own, rotary_rows(4 * tokens), plane_columns(payload)
+
+    corner, late, hidden_far, (cosine, sine), early_block = together(
+        hidden_rest, own_hidden, early, late_y, late_x, payloads[0]
+    )
+    hidden_near = rows_from(
+        [*early, *late, *corner],
+        [
+            [(0, 0, 3 * quarter), (2, 0, quarter)],
+            [(3, 0, quarter), (1, half, 3 * quarter), (1, 0, half)],
+            [(4, 0, half), (5, 0, half)],
+        ],
+    )
+    late_block = plane_columns(after(payloads[1], early_block, hidden_near[2]))
     qkv_rows, gain_turned, out_rows, head_scale = turn(
         first_full,
         [(0, qkv_cols), (qkv_cols, qkv_cols + 16), (out_first, out_first + query_cols)],
@@ -1190,7 +1240,7 @@
         rows,
     )
     ffn_full = [line_gather(block) for block in (early_block, late_block)]
-    hidden = [own_hidden, *hidden_sides, corner, *far, swap(corner, "c")]
+    hidden = [own_hidden, *hidden_near, hidden_far, *across(hidden_near)]
 
     def attend(hidden, gain_turned, first_full, out_rows, head_scale, cosine, sine):
         out_near, out_first = plane_near(out_rows)

time: 474 us -> 472 us (level)
    pallas_call x0 -> x2, Pallas kernels: none -> 5.24 us  [rows_from(): pl.pallas_call(body, out_shape=[jax.ShapeDtypeStruct((size, parts[0].shap...]
    ppermute x65 -> x67, waiting for transfers between devices: 94.5 us -> 99.1 us  [swap(): return lax.ppermute(values, axis, SWAP)]
    ppermute x65 -> x67, starting transfers between devices: 42.6 us -> 42.4 us  [swap(): return lax.ppermute(values, axis, SWAP)]
  transfers between devices with their start and end apart: 79 -> 81, of which waited for: 32 -> 33; matrix products, arithmetic and copies ran while one was open for 3% -> 3% of each run, Pallas kernels for 49% -> 49%
where the time goes in v9:
time: 472 us; the launch traced here: 466 us
  Pallas kernels  234 us (50%)
  waiting for transfers between devices  120 us (25%)
  starting transfers between devices  60.4 us (13%)
  blocking collectives  16.6 us (4%)
  between operations  14.9 us (3%)
  other arithmetic  10.5 us (2%)
  local copies, waits for them, and re-layouts  9.31 us (2%)
    ppermute x67, waiting for transfers between devices, swap(): return lax.ppermute(values, axis, SWAP)  99.1 us
    pallas_call x5, Pallas kernels, feed_forward(): pl.pallas_call(body, grid=(rows // TILE,), in_specs=specs * 2 + [entire(w...  58.2 us
    ppermute x67, starting transfers between devices, swap(): return lax.ppermute(values, axis, SWAP)  42.4 us
    pallas_call x3, Pallas kernels, weight_grads(): pl.pallas_call(body, grid=(depth // tile,), in_specs=specs + [ANY] * len(...  39.7 us
    pallas_call x2, Pallas kernels, backward_attention(): pl.pallas_call(attend_backward, grid_spec=pltpu.PrefetchScalarGridSpec(nu...  31.6 us
    all_to_all x1, blocking collectives, plane_columns(): lax.all_to_all(payload, PLANE, split_axis=0, concat_axis=0, tiled=True)  16.6 us
    pallas_call x1, Pallas kernels, attention_call(): pl.pallas_call(body, grid_spec=pltpu.PrefetchScalarGridSpec(num_scalar_pr...  15.8 us
    pallas_call x1, Pallas kernels, project_back(): pl.pallas_call(body, grid=(rows_of(lefts[0]) // TILE,), in_specs=specs +...  13.4 us
  transfers between devices with their start and end apart: 81, of which 33 were waited for; matrix products, arithmetic and copies ran while one was open for 3% of the time, Pallas kernels for 49%

profile of v9, /device:TPU:0, one launch (start us, length us, event | category | flops | bytes accessed | tf_op | source)
XLA Modules:
  0.0 466.4 jit_solution(17596119516346571247)
XLA Ops:
  7.2 2.5 pack_columns.3
  9.7 23.2 %conditional.14 = (bf16[384,640]{1,0:T(8,128)(2,1)}, bf16[192,1536]{1,0:T(8,128)(2,1)}, bf16[192,1536]{1,0:T(8,128)(2,1)}, bf16[8,48,1536]{2,1,0:T(8,128)(2,1)}, bf16[8,48,1152]{2,1,0:T(8,128)(2,1)S(1)}) conditional(s32[]{:T(128)} %convert_element_type.79, () %tuple.140, (bf16[8,48,640]{2,1,0:T(8,128)(2,1)}, bf16[192,1536]{1,0:T(8,128)(2,1)S(1)}, ...), branch_computations={%region_0.0_spmd, %region_1.0_spmd} | conditional | bytes 6193304 | solution.py:1141
  9.7 3.0 collective-permute-start
  14.1 4.1 all-to-all-start
  18.3 3.1 pack_columns.2
  21.4 11.4 %all-to-all-done = bf16[8,48,640]{2,1,0:T(8,128)(2,1)} async-done(((bf16[8,48,640]{2,1,0:T(8,128)(2,1)}), bf16[8,48,640]{2,1,0:T(8,128)(2,1)}, u32[]{:S(2)}, u32[]{:S(2)}) %all-to-all-start) | async-done | bytes 491552 | tf_op jit(solution)/shard_map/cond/branch_1_fun/all_to_all | solution.py:1145
  33.0 32.8 %conditional.15 = (bf16[128,1536]{1,0:T(8,128)(2,1)}, bf16[128,1536]{1,0:T(8,128)(2,1)}, bf16[64,1536]{1,0:T(8,128)(2,1)}, bf16[64,1536]{1,0:T(8,128)(2,1)}, bf1...) conditional(s32[]{:T(128)} %convert_element_type.79, () %tuple.142, ...), branch_computations={%region_2.0_spmd, %region_3.0_spmd} | conditional | flops 33890 | bytes 11674154 | solution.py:1141
  33.0 4.3 all-to-all-start.1
  43.8 3.0 multiply_sine_fusion
  46.9 3.1 rotary_rows.1
  49.9 7.8 %collective-permute-done.47 = bf16[64,1536]{1,0:T(8,128)(2,1)} collective-permute-done((bf16[64,1536]{1,0:T(8,128)(2,1)S(1)}, bf16[64,1536]{1,0:T(8,128)(2,1)}, u32[]{:S(2)}, u32[]{:S(2)}) %collective-permute-start.47) | collective-permute-done | bytes 196640 | tf_op jit(solution)/shard_map/cond/branch_1_fun/ppermute | solution.py:1069
  57.8 8.0 %collective-permute-done.45 = bf16[128,1536]{1,0:T(8,128)(2,1)} collective-permute-done((bf16[128,1536]{1,0:T(8,128)(2,1)}, bf16[128,1536]{1,0:T(8,128)(2,1)}, u32[]{:S(2)}, u32[]{:S(2)}) %collective-permute-start.45) | collective-permute-done | bytes 393248 | tf_op jit(solution)/shard_map/cond/branch_1_fun/ppermute | solution.py:1069
  65.8 3.0 rows_from.3
  68.9 16.6 %all_to_all.13 = bf16[8,48,1152]{2,1,0:T(8,128)(2,1)} all-to-all(bf16[8,48,1152]{2,1,0:T(8,128)(2,1)S(1)} %after.4), channel_id=1, replica_groups=mesh['dp'=4,'x'=2,'y'=2,'c'=2] {'x','y','c'}, dimensions={0} | all-to-all | bytes 1769472 | tf_op jit(solution)/shard_map/all_to_all | solution.py:1145
  86.2 3.6 turn.1
  90.9 30.4 %conditional.16 = (bf16[192,1536]{1,0:T(8,128)(2,1)}, bf16[192,1536]{1,0:T(8,128)(2,1)}, bf16[192,1536]{1,0:T(8,128)(2,1)}, bf16[192,1536]{1,0:T(8,128)(2,1)}, b...) conditional(s32[]{:T(128)} %convert_element_type.79, () %tuple.139, ...), branch_computations={%region_4.0_spmd, %region_5.0_spmd} | conditional | flops 2 | bytes 17826128 | solution.py:1141
  94.8 10.6 %norm_project.1 = (bf16[2048,1536]{1,0:T(8,128)(2,1)}, bf16[2048,320]{1,0:T(8,128)(2,1)}) custom-call(bf16[256,1536]{1,0:T(8,128)(2,1)S(1)} %get-tuple-element.418.refs_0_, bf16[256,1536]{1,0:T(8,128)(2,1)} %get-tuple-element.419.refs_1_, bf16[256,1536]{1,0:T(8,128)(2,1)} %get-tuple-element.420.refs_2_, bf16[256,1536]{1,0:T(8,128)(2,1)} %get-tuple-element.421.refs_3_, ...), custom_call_target="tpu_custom_call" | custom-call | flops 1 | bytes 1 | tf_op jit(solution)/shard_map/cond/branch_1_fun/norm_project/pallas_call | solution.py:438
  105.4 15.8 %attend_forward.1 = (bf16[2,1,256,192]{3,2,1,0:T(8,128)(2,1)}, bf16[2,1,256,192]{3,2,1,0:T(8,128)(2,1)}, bf16[2,1,256,192]{3,2,1,0:T(8,128)(2,1)}, bf16[2,1,256,...) custom-call(s32[1]{0:T(128)} %get-tuple-element.430.place_ref, ...), custom_call_target="tpu_custom_call" | custom-call | flops 1 | bytes 1 | tf_op jit(solution)/shard_map/cond/branch_1_fun/attend_forward/pallas_call | solution.py:256
  121.3 52.2 %conditional.17 = (f32[256,1536]{1,0:T(8,128)}, bf16[256,1536]{1,0:T(8,128)(2,1)}, bf16[256,1536]{1,0:T(8,128)(2,1)}, bf16[256,1536]{1,0:T(8,128)(2,1)}, bf16[25...) conditional(s32[]{:T(128)} %convert_element_type.79, () %tuple.138, ...), branch_computations={%region_6.0_spmd, %region_7.0_spmd} | conditional | flops 2 | bytes 45810620 | solution.py:1141
  124.9 5.3 %collective-permute-done.8.refs_3_ = bf16[384,256]{1,0:T(8,128)(2,1)S(1)} collective-permute-done((bf16[384,256]{1,0:T(8,128)(2,1)S(1)}, bf16[384,256]{1,0:T(8,128)(2,1)S(1)}, u32[]{:S(2)}, u32[]{:S(2)}) %collective-permute-start.8) | collective-permute-done | bytes 196640 | tf_op jit(solution)/shard_map/cond/branch_1_fun/ppermute | solution.py:1095
  141.2 5.5 %attend_out.1 = (f32[256,1536]{1,0:T(8,128)}, bf16[256,1536]{1,0:T(8,128)(2,1)}) custom-call(bf16[384,256]{1,0:T(8,128)(2,1)S(1)} %bitcast.100, bf16[384,256]{1,0:T(8,128)(2,1)S(1)} %copy-done.1, bf16[384,256]{1,0:T(8,128)(2,1)S(1)} %copy-done.5, bf16[384,256]{1,0:T(8,128)(2,1)S(1)} %copy-done.3, ...), custom_call_target="tpu_custom_call" | custom-call | flops 1 | bytes 1 | tf_op jit(solution)/shard_map/cond/branch_1_fun/attend_out/pallas_call | solution.py:697
  149.4 7.8 %collective-permute-done.17 = bf16[256,1536]{1,0:T(8,128)(2,1)} collective-permute-done((bf16[256,1536]{1,0:T(8,128)(2,1)}, bf16[256,1536]{1,0:T(8,128)(2,1)}, u32[]{:S(2)}, u32[]{:S(2)}) %collective-permute-start.17) | collective-permute-done | bytes 786464 | tf_op jit(solution)/shard_map/cond/branch_1_fun/ppermute | solution.py:1069
  157.9 15.2 %collective-permute-done.14 = bf16[256,1536]{1,0:T(8,128)(2,1)} collective-permute-done((bf16[256,1536]{1,0:T(8,128)(2,1)}, bf16[256,1536]{1,0:T(8,128)(2,1)}, u32[]{:S(2)}, u32[]{:S(2)}) %collective-permute-start.14) | collective-permute-done | bytes 786464 | tf_op jit(solution)/shard_map/cond/branch_1_fun/ppermute | solution.py:1069
  173.6 22.3 %conditional.18 = (bf16[256,1536]{1,0:T(8,128)(2,1)}, bf16[256,1536]{1,0:T(8,128)(2,1)}, bf16[256,1536]{1,0:T(8,128)(2,1)}, bf16[256,1536]{1,0:T(8,128)(2,1)}, b...) conditional(s32[]{:T(128)} %convert_element_type.79, () %tuple.146, ...), branch_computations={%region_8.0_spmd, %region_9.0_spmd} | conditional | flops 2 | bytes 12583138 | solution.py:1141
  173.6 2.7 halves.2
  178.9 12.2 %feed_forward.5 = (bf16[768,1024]{1,0:T(8,128)(2,1)}, bf16[768,512]{1,0:T(8,128)(2,1)}, bf16[256,1536]{1,0:T(8,128)(2,1)}, bf16[512,1536]{1,0:T(8,128)(2,1)}) custom-call(bf16[256,1536]{1,0:T(8,128)(2,1)} %get-tuple-element.463.refs_0_, bf16[256,1536]{1,0:T(8,128)(2,1)} %get-tuple-element.457.refs_0_.refs_1_, ...), custom_call_target="tpu_custom_call" | custom-call | flops 1 | bytes 1 | tf_op jit(solution)/shard_map/cond/branch_1_fun/feed_forward/pallas_call | solution.py:494
  191.1 3.7 collective-permute-done.21
  201.7 34.2 %conditional.19 = (bf16[1280,512]{1,0:T(8,128)(2,1)}, bf16[256,1536]{1,0:T(8,128)(2,1)}, bf16[1024,1536]{1,0:T(8,128)(2,1)}, bf16[1536,1536]{1,0:T(8,128)(2,1)},...) conditional(s32[]{:T(128)} %convert_element_type.79, () %tuple.149, (bf16[256,1536]{1,0:T(8,128)(2,1)S(1)}, ...), branch_computations={%region_10.0_spmd, %region_11.0_spmd} | conditional | flops 2 | bytes 17301690 | solution.py:1141
  203.2 17.6 %feed_forward.6 = (bf16[1280,1024]{1,0:T(8,128)(2,1)}, bf16[1280,512]{1,0:T(8,128)(2,1)}, bf16[256,1536]{1,0:T(8,128)(2,1)}, bf16[1024,1536]{1,0:T(8,128)(2,1)}) custom-call(bf16[256,1536]{1,0:T(8,128)(2,1)S(1)} %get-tuple-element.470.refs_0_.refs_3_, bf16[256,1536]{1,0:T(8,128)(2,1)} %get-tuple-element.471.refs_1_.refs_4_, ...), custom_call_target="tpu_custom_call" | custom-call | flops 1 | bytes 1 | tf_op jit(solution)/shard_map/cond/branch_1_fun/feed_forward/pallas_call | solution.py:494
  220.9 15.0 %weight_grads.3 = bf16[1536,1536]{1,0:T(8,128)(2,1)} custom-call(bf16[256,1536]{1,0:T(8,128)(2,1)} %get-tuple-element.484.refs_0_, bf16[256,1536]{1,0:T(8,128)(2,1)} %get-tuple-element.485.refs_1_, bf16[256,1536]{1,0:T(8,128)(2,1)} %get-tuple-element.486.refs_2_, bf16[256,1536]{1,0:T(8,128)(2,1)S(1)} %get-tuple-element.470.refs_0_.refs_3_, ...), custom_call_target="tpu_custom_call" | custom-call | flops 1 | bytes 1 | tf_op jit(solution)/shard_map/cond/branch_1_fun/weight_grads/pallas_call | solution.py:595
  238.2 19.8 %conditional.20 = (bf16[160,1536]{1,0:T(8,128)(2,1)}, bf16[160,1536]{1,0:T(8,128)(2,1)}, bf16[1280,768]{1,0:T(8,128)(2,1)}, bf16[1280,384]{1,0:T(8,128)(2,1)}, b...) conditional(s32[]{:T(128)} %convert_element_type.79, () %tuple.148, (bf16[160,1536]{1,0:T(8,128)(2,1)}, ...), branch_computations={%region_12.0_spmd, %region_13.0_spmd} | conditional | flops 393217 | bytes 8650814 | solution.py:1141
  240.9 15.8 %feed_forward.7 = (bf16[1280,768]{1,0:T(8,128)(2,1)}, bf16[1280,384]{1,0:T(8,128)(2,1)}, bf16[256,1536]{1,0:T(8,128)(2,1)}, bf16[1024,1536]{1,0:T(8,128)(2,1)S(1)}) custom-call(bf16[256,1536]{1,0:T(8,128)(2,1)S(1)} %get-tuple-element.496.refs_0_, bf16[256,1536]{1,0:T(8,128)(2,1)} %get-tuple-element.497.refs_1_, ...), custom_call_target="tpu_custom_call" | custom-call | flops 1 | bytes 1 | tf_op jit(solution)/shard_map/cond/branch_1_fun/feed_forward/pallas_call | solution.py:494
  258.1 8.5 %feed_forward.9 = (bf16[512,768]{1,0:T(8,128)(2,1)}, bf16[512,384]{1,0:T(8,128)(2,1)S(1)}, bf16[512,1536]{1,0:T(8,128)(2,1)}) custom-call(bf16[256,1536]{1,0:T(8,128)(2,1)} %get-tuple-element.834.refs_0_, bf16[256,1536]{1,0:T(8,128)(2,1)} %get-tuple-element.835.refs_1_, bf16[256,1536]{1,0:T(8,128)(2,1)} %get-tuple-element.836.refs_2_, ...), custom_call_target="tpu_custom_call" | custom-call | flops 1 | bytes 1 | tf_op jit(solution)/shard_map/feed_forward/pallas_call | solution.py:494
  266.6 3.8 add_convert_fusion.2
  270.4 37.8 %conditional.21 = (bf16[256,1536]{1,0:T(8,128)(2,1)}, bf16[256,1536]{1,0:T(8,128)(2,1)}, bf16[256,1536]{1,0:T(8,128)(2,1)}, bf16[256,1536]{1,0:T(8,128)(2,1)}, b...) conditional(s32[]{:T(128)} %convert_element_type.79, () %tuple.137, ...), branch_computations={%region_14.0_spmd, %region_15.0_spmd} | conditional | flops 3 | bytes 12976218 | solution.py:1141
  271.0 3.0 collective-permute-start.31
  273.9 4.1 feed_forward.8
  278.0 13.4 %project_back.1 = (bf16[256,1536]{1,0:T(8,128)(2,1)}, bf16[512,1536]{1,0:T(8,128)(2,1)}, bf16[256,1536]{1,0:T(8,128)(2,1)}, bf16[1024,1536]{1,0:T(8,128)(2,1)}) custom-call(bf16[768,512]{1,0:T(8,128)(2,1)} %get-tuple-element.541.refs_0_, bf16[1280,512]{1,0:T(8,128)(2,1)} %get-tuple-element.542.refs_1_, bf16[256,384]{1,0:T(8,128)(2,1)} %get-tuple-element.538.refs_19_.refs_2_, ...), custom_call_target="tpu_custom_call" | custom-call | flops 1 | bytes 1 | tf_op jit(solution)/shard_map/cond/branch_1_fun/project_back/pallas_call | solution.py:646
  291.3 13.7 %weight_grads.4 = bf16[1536,1152]{1,0:T(8,128)(2,1)} custom-call(bf16[256,1536]{1,0:T(8,128)(2,1)} %get-tuple-element.516.refs_0_, bf16[256,1536]{1,0:T(8,128)(2,1)} %get-tuple-element.521.refs_1_, bf16[256,1536]{1,0:T(8,128)(2,1)} %get-tuple-element.522.refs_2_, bf16[256,1536]{1,0:T(8,128)(2,1)} %get-tuple-element.523.refs_3_, ...), custom_call_target="tpu_custom_call" | custom-call | flops 1 | bytes 1 | tf_op jit(solution)/shard_map/cond/branch_1_fun/weight_grads/pallas_call | solution.py:595
  305.1 3.2 collective-permute-done.31
  309.0 8.2 %middle_back.1 = (f32[256,1536]{1,0:T(8,128)}, bf16[256,1536]{1,0:T(8,128)(2,1)}, bf16[2,192,256]{2,1,0:T(8,128)(2,1)S(1)}, bf16[2,192,256]{2,1,0:T(8,128)(2,1)S...) custom-call(bf16[256,1536]{1,0:T(8,128)(2,1)} %get-tuple-element.870.refs_0_, ...), custom_call_target="tpu_custom_call" | custom-call | flops 1 | bytes 1 | tf_op jit(solution)/shard_map/middle_back/pallas_call | solution.py:756
  318.0 2.7 collective-permute-start.66
  320.7 4.3 collective-permute-done.65.refs_2_
  325.0 3.4 collective-permute-done.64.refs_1_
  331.1 21.3 %conditional.22 = (bf16[256,1536]{1,0:T(8,128)(2,1)}, bf16[256,1536]{1,0:T(8,128)(2,1)}, bf16[256,1536]{1,0:T(8,128)(2,1)}, bf16[2,1,256,320]{3,2,1,0:T(8,128)(2...) conditional(s32[]{:T(128)} %convert_element_type.79, () %tuple.136, ...), branch_computations={%region_17.0_spmd, %region_18.0_spmd} | conditional | flops 9 | bytes 15335739 | solution.py:1141
  333.3 15.8 %attend_backward.2 = (bf16[2,1,256,320]{3,2,1,0:T(8,128)(2,1)}, bf16[2,1,256,320]{3,2,1,0:T(8,128)(2,1)}, bf16[2,1,320,256]{3,2,1,0:T(8,128)(2,1)S(1)}, bf16[2,1,320,256]{3,2,1,0:T(8,128)(2,1)}, f32[1,8,256]{2,1,0:T(8,128)S(1)}) custom-call(s32[1]{0:T(128)} %get-tuple-element.549.place_ref, bf16[2,2,2,1,256,320]{5,4,3,2,1,0:T(8,128)(2,1)} %bitcast.16.qkv_ref, ...), custom_call_target="tpu_custom_call" | custom-call | flops 1 | bytes 1 | tf_op jit(solution)/shard_map/cond/branch_1_fun/attend_backward/pallas_call | solution.py:320
  352.4 20.4 %conditional.23 = (bf16[256,1536]{1,0:T(8,128)(2,1)}, bf16[192,1536]{1,0:T(8,128)(2,1)}, bf16[256,1536]{1,0:T(8,128)(2,1)}, bf16[256,1536]{1,0:T(8,128)(2,1)}, b...) conditional(s32[]{:T(128)} %convert_element_type.79, () %tuple.154, ...), branch_computations={%region_19.0_spmd, %region_20.0_spmd} | conditional | flops 1 | bytes 11796713 | solution.py:1141
  354.5 15.8 %attend_backward.3 = (bf16[2,1,256,320]{3,2,1,0:T(8,128)(2,1)}, bf16[2,1,256,320]{3,2,1,0:T(8,128)(2,1)}, bf16[2,1,320,256]{3,2,1,0:T(8,128)(2,1)}, bf16[2,1,320,256]{3,2,1,0:T(8,128)(2,1)}, f32[1,8,256]{2,1,0:T(8,128)S(1)}) custom-call(s32[1]{0:T(128)} %get-tuple-element.569.place_ref, bf16[2,2,2,1,256,320]{5,4,3,2,1,0:T(8,128)(2,1)} %bitcast.27.qkv_ref, ...), custom_call_target="tpu_custom_call" | custom-call | flops 1 | bytes 1 | tf_op jit(solution)/shard_map/cond/branch_1_fun/attend_backward/pallas_call | solution.py:320
  370.3 2.5 collective-permute-done.32
  372.8 2.5 collective-permute-done.68
  375.3 19.2 %conditional.24 = (bf16[640,256]{1,0:T(8,128)(2,1)}, bf16[640,256]{1,0:T(8,128)(2,1)}, bf16[640,256]{1,0:T(8,128)(2,1)}, bf16[1536,640]{1,0:T(8,128)(2,1)S(1)}, ...) conditional(s32[]{:T(128)} %convert_element_type.79, () %tuple.135, ...), branch_computations={%region_21.0_spmd, %region_22.0_spmd} | conditional | flops 2 | bytes 8388842 | solution.py:1141
  378.8 4.7 %sent_sums.1 = (bf16[256,1536]{1,0:T(8,128)(2,1)}, bf16[256,1536]{1,0:T(8,128)(2,1)}, bf16[256,1536]{1,0:T(8,128)(2,1)}) custom-call(bf16[512,1536]{1,0:T(8,128)(2,1)} %get-tuple-element.609.sides_ref, bf16[256,1536]{1,0:T(8,128)(2,1)} %get-tuple-element.610.corner_ref, bf16[1024,1536]{1,0:T(8,128)(2,1)} %get-tuple-element.611.far_ref), custom_call_target="tpu_custom_call" | custom-call | flops 1 | bytes 1 | tf_op jit(solution)/shard_map/cond/branch_1_fun/sent_sums/pallas_call | solution.py:815
  383.5 10.9 %weight_grads.5 = bf16[1536,640]{1,0:T(8,128)(2,1)S(1)} custom-call(bf16[2048,1536]{1,0:T(8,128)(2,1)} %get-tuple-element.588.refs_0_, bf16[512,320]{1,0:T(8,128)(2,1)} %bitcast.102, bf16[512,320]{1,0:T(8,128)(2,1)S(1)} %bitcast.101, bf16[512,320]{1,0:T(8,128)(2,1)} %bitcast.104, bf16[512,320]{1,0:T(8,128)(2,1)} %bitcast.103, ...), custom_call_target="tpu_custom_call" | custom-call | flops 1 | bytes 1 | tf_op jit(solution)/shard_map/cond/branch_1_fun/weight_grads/pallas_call | solution.py:595
  396.3 20.1 %conditional.25 = (bf16[128,1536]{1,0:T(8,128)(2,1)}, bf16[128,1536]{1,0:T(8,128)(2,1)}, bf16[192,1152]{1,0:T(8,128)(2,1)}, bf16[1280,256]{1,0:T(8,128)(2,1)}, bf16[320,1536]{1,0:T(8,128)(2,1)S(1)}) conditional(s32[]{:T(128)} %convert_element_type.79, () %tuple.158, (bf16[256,1536]{1,0:T(8,128)(2,1)}, bf16[384,1152]{1,0:T(8,128)(2,1)S(1)}, ...), branch_computations={%region_24.0_spmd, %region_25.0_spmd} | conditional | flops 10 | bytes 13140292 | solution.py:1141
  403.0 8.5 %collective-permute-done.55 = bf16[128,1536]{1,0:T(8,128)(2,1)} collective-permute-done((bf16[128,1536]{1,0:T(8,128)(2,1)}, bf16[128,1536]{1,0:T(8,128)(2,1)}, u32[]{:S(2)}, u32[]{:S(2)}) %collective-permute-start.55) | collective-permute-done | bytes 393248 | tf_op jit(solution)/shard_map/cond/branch_1_fun/ppermute | solution.py:1069
  411.5 4.9 %collective-permute-done.54 = bf16[128,1536]{1,0:T(8,128)(2,1)} collective-permute-done((bf16[128,1536]{1,0:T(8,128)(2,1)S(1)}, bf16[128,1536]{1,0:T(8,128)(2,1)}, u32[]{:S(2)}, u32[]{:S(2)}) %collective-permute-start.54) | collective-permute-done | bytes 393248 | tf_op jit(solution)/shard_map/cond/branch_1_fun/ppermute | solution.py:1069
  416.4 3.3 corner_sum.1
  419.7 22.8 %conditional.26 = (bf16[256,1536]{1,0:T(8,128)(2,1)}, bf16[256,1536]{1,0:T(8,128)(2,1)}, f32[192,1728]{1,0:T(8,128)}, f32[192,1728]{1,0:T(8,128)}, f32[192,1728]{1,0:T(8,128)}, /*index=5*/f32[1,256,1536]{2,1,0:T(8,128)}) conditional(s32[]{:T(128)} %convert_element_type.79, () %tuple.157, (bf16[256,1536]{1,0:T(8,128)(2,1)}, ...), branch_computations={%region_26.0_spmd, %region_27.0_spmd} | conditional | flops 1 | bytes 32244056 | solution.py:1141
  423.0 3.8 unpack_columns.2
  426.8 7.2 %input_back.1 = f32[256,1536]{1,0:T(8,128)} custom-call(bf16[640,256]{1,0:T(8,128)(2,1)S(1)} %get-tuple-element.633.refs_0_, bf16[640,256]{1,0:T(8,128)(2,1)} %get-tuple-element.634.refs_1_, bf16[640,256]{1,0:T(8,128)(2,1)} %get-tuple-element.635.refs_2_, bf16[640,256]{1,0:T(8,128)(2,1)} %get-tuple-element.636.refs_3_, ...), custom_call_target="tpu_custom_call" | custom-call | flops 1 | bytes 1 | tf_op jit(solution)/shard_map/cond/branch_1_fun/input_back/pallas_call | solution.py:787
  434.1 6.6 %collective-permute-done.39 = bf16[256,1536]{1,0:T(8,128)(2,1)} collective-permute-done((bf16[256,1536]{1,0:T(8,128)(2,1)}, bf16[256,1536]{1,0:T(8,128)(2,1)}, u32[]{:S(2)}, u32[]{:S(2)}) %collective-permute-start.39) | collective-permute-done | bytes 786464 | tf_op jit(solution)/shard_map/cond/branch_1_fun/ppermute | solution.py:1069
  442.5 8.3 %conditional.27 = (bf16[192,640]{1,0:T(8,128)(2,1)}, bf16[1,256,1536]{2,1,0:T(8,128)(2,1)S(1)}) conditional(s32[]{:T(128)} %convert_element_type.79, () %tuple.134, (bf16[384,640]{1,0:T(8,128)(2,1)}, bf16[256,1536]{1,0:T(8,128)(2,1)}, bf16[1024,1536]{1,0:T(8,128)(2,1)}, bf16[256,1536]{1,0:T(8,128)(2,1)}, bf16[256,1536]{1,0:T(8,128)(2,1)}, ...), branch_computations={%region_29.0_spmd, %region_30.0_spmd} | conditional | flops 3538952 | bytes 6979734 | solution.py:1141
  446.3 4.5 collective-permute-done.53
  450.8 2.4 unpack_columns.3
  (264 shorter events, 88.8 us)
Async XLA Ops:
  7.2 79.0 %all-gather.4.cloned.1.call-start = ((), (), s32[]{:S(2)}) async-start(), calls=%async_computation.6 | async-start | bytes 2457600 | tf_op jit(solution)/shard_map/all_gather | solution.py:1128
  9.7 23.2 %collective-permute-start = (bf16[192,1536]{1,0:T(8,128)(2,1)S(1)}, bf16[192,1536]{1,0:T(8,128)(2,1)}, u32[]{:S(2)}, u32[]{:S(2)}) collective-permute-start(bf16[192,1536]{1,0:T(8,128)(2,1)S(1)} %get-tuple-element.400), channel_id=1, source_target_pairs={{0,2},{2,0},{1,3},{3,1},{4,6},{6,4},{5,7},{7,5},{8,10},{10,8},{9,1... | collective-permute-start | bytes 1769480 | tf_op jit(solution)/shard_map/cond/branch_1_fun/ppermute | solution.py:1069
  12.7 20.2 %collective-permute-start.1 = (bf16[192,1536]{1,0:T(8,128)(2,1)S(1)}, bf16[192,1536]{1,0:T(8,128)(2,1)}, u32[]{:S(2)}, u32[]{:S(2)}) collective-permute-start(bf16[192,1536]{1,0:T(8,128)(2,1)S(1)} %get-tuple-element.401), channel_id=1, source_target_pairs={{0,4},{4,0},{1,5},{5,1},{2,6},{6,2},{3,7},{7,3},{8,12},{12,8},{9,1... | collective-permute-start | bytes 1769480 | tf_op jit(solution)/shard_map/cond/branch_1_fun/ppermute | solution.py:1069
  14.1 18.7 %all-to-all-start = ((bf16[8,48,640]{2,1,0:T(8,128)(2,1)}), bf16[8,48,640]{2,1,0:T(8,128)(2,1)}, u32[]{:S(2)}, u32[]{:S(2)}) async-start(bf16[8,48,640]{2,1,0:T(8,128)(2,1)} %get-tuple-element.399), calls=%async_computation | async-start | bytes 983040 | tf_op jit(solution)/shard_map/cond/branch_1_fun/all_to_all | solution.py:1145
  32.9 140.7 %all-gather.8.cloned.1.call-start = ((), (), s32[]{:S(2)}) async-start(), calls=%async_computation.8 | async-start | bytes 5898240 | tf_op jit(solution)/shard_map/all_gather | solution.py:1128
  33.0 32.8 %all-to-all-start.1 = ((bf16[8,48,1536]{2,1,0:T(8,128)(2,1)}), bf16[8,48,1536]{2,1,0:T(8,128)(2,1)}, u32[]{:S(2)}, u32[]{:S(2)}) async-start(bf16[8,48,1536]{2,1,0:T(8,128)(2,1)} %get-tuple-element.416), calls=%async_computation.1 | async-start | bytes 2359296 | tf_op jit(solution)/shard_map/cond/branch_1_fun/all_to_all | solution.py:1145
  37.2 28.5 %collective-permute-start.49 = (bf16[256,1536]{1,0:T(8,128)(2,1)S(1)}, bf16[256,1536]{1,0:T(8,128)(2,1)}, u32[]{:S(2)}, u32[]{:S(2)}) collective-permute-start(bf16[256,1536]{1,0:T(8,128)(2,1)S(1)} %get-tuple-element.413), channel_id=1, source_target_pairs={{0,1},{1,0},{2,3},{3,2},{4,5},{5,4},{6,7},{7,6},{8,9},{9,8},{10,11... | collective-permute-start | bytes 2359304 | tf_op jit(solution)/shard_map/cond/branch_1_fun/ppermute | solution.py:1069
  37.6 20.2 %collective-permute-start.47 = (bf16[64,1536]{1,0:T(8,128)(2,1)S(1)}, bf16[64,1536]{1,0:T(8,128)(2,1)}, u32[]{:S(2)}, u32[]{:S(2)}) collective-permute-start(bf16[64,1536]{1,0:T(8,128)(2,1)S(1)} %get-tuple-element.411), channel_id=1, source_target_pairs={{0,2},{2,0},{1,3},{3,1},{4,6},{6,4},{5,7},{7,5},{8,10},{10,8},{9,1... | collective-permute-start | bytes 589832 | tf_op jit(solution)/shard_map/cond/branch_1_fun/ppermute | solution.py:1069
  39.3 18.5 %collective-permute-start.48 = (bf16[64,1536]{1,0:T(8,128)(2,1)S(1)}, bf16[64,1536]{1,0:T(8,128)(2,1)}, u32[]{:S(2)}, u32[]{:S(2)}) collective-permute-start(bf16[64,1536]{1,0:T(8,128)(2,1)S(1)} %get-tuple-element.412), channel_id=1, source_target_pairs={{0,4},{4,0},{1,5},{5,1},{2,6},{6,2},{3,7},{7,3},{8,12},{12,8},{9,1... | collective-permute-start | bytes 589832 | tf_op jit(solution)/shard_map/cond/branch_1_fun/ppermute | solution.py:1069
  43.0 22.8 %collective-permute-start.45 = (bf16[128,1536]{1,0:T(8,128)(2,1)}, bf16[128,1536]{1,0:T(8,128)(2,1)}, u32[]{:S(2)}, u32[]{:S(2)}) collective-permute-start(bf16[128,1536]{1,0:T(8,128)(2,1)} %get-tuple-element.409), channel_id=1, source_target_pairs={{0,4},{4,0},{1,5},{5,1},{2,6},{6,2},{3,7},{7,3},{8,12},{12,8},{9,1... | collective-permute-start | bytes 1179656 | tf_op jit(solution)/shard_map/cond/branch_1_fun/ppermute | solution.py:1069
  43.6 22.2 %collective-permute-start.46 = (bf16[128,1536]{1,0:T(8,128)(2,1)}, bf16[128,1536]{1,0:T(8,128)(2,1)}, u32[]{:S(2)}, u32[]{:S(2)}) collective-permute-start(bf16[128,1536]{1,0:T(8,128)(2,1)} %get-tuple-element.410), channel_id=1, source_target_pairs={{0,2},{2,0},{1,3},{3,1},{4,6},{6,4},{5,7},{7,5},{8,10},{10,8},{9,1... | collective-permute-start | bytes 1179656 | tf_op jit(solution)/shard_map/cond/branch_1_fun/ppermute | solution.py:1069
  65.8 172.4 %all-gather.6.cloned.1.call-start = ((), (), s32[]{:S(2)}) async-start(), calls=%async_computation.7 | async-start | bytes 4423680 | tf_op jit(solution)/shard_map/all_gather | solution.py:1128
  85.5 245.7 %reduce-scatter.4.cloned.1.call-start = ((), (), s32[]{:S(2)}) async-start(), calls=%async_computation.9 | async-start | bytes 5898240 | tf_op jit(solution)/shard_map/reduce_scatter | solution.py:1132
  90.9 30.4 %collective-permute-start.5 = (bf16[192,1536]{1,0:T(8,128)(2,1)S(1)}, bf16[192,1536]{1,0:T(8,128)(2,1)}, u32[]{:S(2)}, u32[]{:S(2)}) collective-permute-start(bf16[192,1536]{1,0:T(8,128)(2,1)S(1)} %get-tuple-element.417), channel_id=1, source_target_pairs={{0,1},{1,0},{2,3},{3,2},{4,5},{5,4},{6,7},{7,6},{8,9},{9,8},{10,11... | collective-permute-start | bytes 1769480 | tf_op jit(solution)/shard_map/cond/branch_1_fun/ppermute | solution.py:1069
  91.3 29.9 %collective-permute-start.4 = (bf16[192,1536]{1,0:T(8,128)(2,1)S(1)}, bf16[192,1536]{1,0:T(8,128)(2,1)}, u32[]{:S(2)}, u32[]{:S(2)}) collective-permute-start(bf16[192,1536]{1,0:T(8,128)(2,1)S(1)} %get-tuple-element.417), channel_id=1, source_target_pairs={{0,6},{2,4},{4,2},{6,0},{1,7},{3,5},{5,3},{7,1},{8,14},{10,12},{12... | collective-permute-start | bytes 1769480 | tf_op jit(solution)/shard_map/cond/branch_1_fun/ppermute | solution.py:1095
  92.2 29.1 %collective-permute-start.3 = (bf16[192,1536]{1,0:T(8,128)(2,1)S(1)}, bf16[192,1536]{1,0:T(8,128)(2,1)}, u32[]{:S(2)}, u32[]{:S(2)}) collective-permute-start(bf16[192,1536]{1,0:T(8,128)(2,1)S(1)} %get-tuple-element.417), channel_id=1, source_target_pairs={{0,4},{4,0},{1,5},{5,1},{2,6},{6,2},{3,7},{7,3},{8,12},{12,8},{9,1... | collective-permute-start | bytes 1769480 | tf_op jit(solution)/shard_map/cond/branch_1_fun/ppermute | solution.py:1069
  93.5 27.8 %collective-permute-start.2 = (bf16[192,1536]{1,0:T(8,128)(2,1)S(1)}, bf16[192,1536]{1,0:T(8,128)(2,1)}, u32[]{:S(2)}, u32[]{:S(2)}) collective-permute-start(bf16[192,1536]{1,0:T(8,128)(2,1)S(1)} %get-tuple-element.417), channel_id=1, source_target_pairs={{0,2},{2,0},{1,3},{3,1},{4,6},{6,4},{5,7},{7,5},{8,10},{10,8},{9,1... | collective-permute-start | bytes 1769480 | tf_op jit(solution)/shard_map/cond/branch_1_fun/ppermute | solution.py:1069
  121.3 8.8 %collective-permute-start.8 = (bf16[384,256]{1,0:T(8,128)(2,1)S(1)}, bf16[384,256]{1,0:T(8,128)(2,1)S(1)}, u32[]{:S(2)}, u32[]{:S(2)}) collective-permute-start(bf16[384,256]{1,0:T(8,128)(2,1)S(1)} %bitcast.112), channel_id=1, source_target_pairs={{0,6},{2,4},{4,2},{6,0},{1,7},{3,5},{5,3},{7,1},{8,14},{10,12},{12... | collective-permute-start | bytes 589832 | tf_op jit(solution)/shard_map/cond/branch_1_fun/ppermute | solution.py:1095
  122.3 9.6 %collective-permute-start.7 = (bf16[384,256]{1,0:T(8,128)(2,1)S(1)}, bf16[384,256]{1,0:T(8,128)(2,1)S(1)}, u32[]{:S(2)}, u32[]{:S(2)}) collective-permute-start(bf16[384,256]{1,0:T(8,128)(2,1)S(1)} %bitcast.113), channel_id=1, source_target_pairs={{0,4},{4,0},{1,5},{5,1},{2,6},{6,2},{3,7},{7,3},{8,12},{12,8},{9,1... | collective-permute-start | bytes 589832 | tf_op jit(solution)/shard_map/cond/branch_1_fun/ppermute | solution.py:1069
  123.6 9.0 %collective-permute-start.6 = (bf16[384,256]{1,0:T(8,128)(2,1)S(1)}, bf16[384,256]{1,0:T(8,128)(2,1)S(1)}, u32[]{:S(2)}, u32[]{:S(2)}) collective-permute-start(bf16[384,256]{1,0:T(8,128)(2,1)S(1)} %bitcast.114), channel_id=1, source_target_pairs={{0,2},{2,0},{1,3},{3,1},{4,6},{6,4},{5,7},{7,5},{8,10},{10,8},{9,1... | collective-permute-start | bytes 589832 | tf_op jit(solution)/shard_map/cond/branch_1_fun/ppermute | solution.py:1069
  124.9 13.1 %collective-permute-start.12 = (bf16[192,1536]{1,0:T(8,128)(2,1)}, bf16[192,1536]{1,0:T(8,128)(2,1)}, u32[]{:S(2)}, u32[]{:S(2)}) collective-permute-start(bf16[192,1536]{1,0:T(8,128)(2,1)} %get-tuple-element.450.refs_11_), channel_id=1, source_target_pairs={{0,1},{1,0},{2,3},{3,2},{4,5},{5,4},{6,7},{7,6},{8,9},{9,8},{10,11... | collective-permute-start | bytes 1769480 | tf_op jit(solution)/shard_map/cond/branch_1_fun/ppermute | solution.py:1069
  135.1 13.1 %collective-permute-start.18 = (bf16[256,1536]{1,0:T(8,128)(2,1)S(1)}, bf16[256,1536]{1,0:T(8,128)(2,1)}, u32[]{:S(2)}, u32[]{:S(2)}) collective-permute-start(bf16[256,1536]{1,0:T(8,128)(2,1)S(1)} %get-tuple-element.456), channel_id=1, source_target_pairs={{0,1},{1,0},{2,3},{3,2},{4,5},{5,4},{6,7},{7,6},{8,9},{9,8},{10,11... | collective-permute-start | bytes 2359304 | tf_op jit(solution)/shard_map/cond/branch_1_fun/ppermute | solution.py:1069
  136.5 20.7 %collective-permute-start.17 = (bf16[256,1536]{1,0:T(8,128)(2,1)}, bf16[256,1536]{1,0:T(8,128)(2,1)}, u32[]{:S(2)}, u32[]{:S(2)}) collective-permute-start(bf16[256,1536]{1,0:T(8,128)(2,1)} %after.3), channel_id=1, source_target_pairs={{0,4},{4,0},{1,5},{5,1},{2,6},{6,2},{3,7},{7,3},{8,12},{12,8},{9,1... | collective-permute-start | bytes 2359304 | tf_op jit(solution)/shard_map/cond/branch_1_fun/ppermute | solution.py:1069
  137.2 20.8 %collective-permute-start.16 = (bf16[256,1536]{1,0:T(8,128)(2,1)}, bf16[256,1536]{1,0:T(8,128)(2,1)}, u32[]{:S(2)}, u32[]{:S(2)}) collective-permute-start(bf16[256,1536]{1,0:T(8,128)(2,1)} %after.3), channel_id=1, source_target_pairs={{0,2},{2,0},{1,3},{3,1},{4,6},{6,4},{5,7},{7,5},{8,10},{10,8},{9,1... | collective-permute-start | bytes 2359304 | tf_op jit(solution)/shard_map/cond/branch_1_fun/ppermute | solution.py:1069
  146.7 11.2 %collective-permute-start.15 = (bf16[256,1536]{1,0:T(8,128)(2,1)}, bf16[256,1536]{1,0:T(8,128)(2,1)}, u32[]{:S(2)}, u32[]{:S(2)}) collective-permute-start(bf16[256,1536]{1,0:T(8,128)(2,1)} %get-tuple-element.1231), channel_id=1, source_target_pairs={{0,1},{1,0},{2,3},{3,2},{4,5},{5,4},{6,7},{7,6},{8,9},{9,8},{10,11... | collective-permute-start | bytes 2359304 | tf_op jit(solution)/shard_map/cond/branch_1_fun/ppermute | solution.py:1069
  146.9 26.3 %collective-permute-start.14 = (bf16[256,1536]{1,0:T(8,128)(2,1)}, bf16[256,1536]{1,0:T(8,128)(2,1)}, u32[]{:S(2)}, u32[]{:S(2)}) collective-permute-start(bf16[256,1536]{1,0:T(8,128)(2,1)} %get-tuple-element.1231), channel_id=1, source_target_pairs={{0,4},{4,0},{1,5},{5,1},{2,6},{6,2},{3,7},{7,3},{8,12},{12,8},{9,1... | collective-permute-start | bytes 2359304 | tf_op jit(solution)/shard_map/cond/branch_1_fun/ppermute | solution.py:1069
  148.2 25.3 %collective-permute-start.13 = (bf16[256,1536]{1,0:T(8,128)(2,1)}, bf16[256,1536]{1,0:T(8,128)(2,1)}, u32[]{:S(2)}, u32[]{:S(2)}) collective-permute-start(bf16[256,1536]{1,0:T(8,128)(2,1)} %get-tuple-element.1231), channel_id=1, source_target_pairs={{0,2},{2,0},{1,3},{3,1},{4,6},{6,4},{5,7},{7,5},{8,10},{10,8},{9,1... | collective-permute-start | bytes 2359304 | tf_op jit(solution)/shard_map/cond/branch_1_fun/ppermute | solution.py:1069
  157.2 16.3 %collective-permute-start.20 = (bf16[256,1536]{1,0:T(8,128)(2,1)}, bf16[256,1536]{1,0:T(8,128)(2,1)}, u32[]{:S(2)}, u32[]{:S(2)}) collective-permute-start(bf16[256,1536]{1,0:T(8,128)(2,1)} %collective-permute-done.17), channel_id=1, source_target_pairs={{0,1},{1,0},{2,3},{3,2},{4,5},{5,4},{6,7},{7,6},{8,9},{9,8},{10,11... | collective-permute-start | bytes 2359304 | tf_op jit(solution)/shard_map/cond/branch_1_fun/ppermute | solution.py:1069
  157.9 15.6 %collective-permute-start.19 = (bf16[256,1536]{1,0:T(8,128)(2,1)}, bf16[256,1536]{1,0:T(8,128)(2,1)}, u32[]{:S(2)}, u32[]{:S(2)}) collective-permute-start(bf16[256,1536]{1,0:T(8,128)(2,1)} %collective-permute-done.16), channel_id=1, source_target_pairs={{0,1},{1,0},{2,3},{3,2},{4,5},{5,4},{6,7},{7,6},{8,9},{9,8},{10,11... | collective-permute-start | bytes 2359304 | tf_op jit(solution)/shard_map/cond/branch_1_fun/ppermute | solution.py:1069
  176.3 18.6 %collective-permute-start.21 = (bf16[256,1536]{1,0:T(8,128)(2,1)}, bf16[256,1536]{1,0:T(8,128)(2,1)}, u32[]{:S(2)}, u32[]{:S(2)}) collective-permute-start(bf16[256,1536]{1,0:T(8,128)(2,1)} %get-tuple-element.461), channel_id=1, source_target_pairs={{0,4},{4,0},{1,5},{5,1},{2,6},{6,2},{3,7},{7,3},{8,12},{12,8},{9,1... | collective-permute-start | bytes 2359304 | tf_op jit(solution)/shard_map/cond/branch_1_fun/ppermute | solution.py:1069
  177.6 18.2 %collective-permute-start.22 = (bf16[256,1536]{1,0:T(8,128)(2,1)}, bf16[256,1536]{1,0:T(8,128)(2,1)}, u32[]{:S(2)}, u32[]{:S(2)}) collective-permute-start(bf16[256,1536]{1,0:T(8,128)(2,1)} %get-tuple-element.462), channel_id=1, source_target_pairs={{0,2},{2,0},{1,3},{3,1},{4,6},{6,4},{5,7},{7,5},{8,10},{10,8},{9,1... | collective-permute-start | bytes 2359304 | tf_op jit(solution)/shard_map/cond/branch_1_fun/ppermute | solution.py:1069
  178.4 17.4 %collective-permute-start.23 = (bf16[256,1536]{1,0:T(8,128)(2,1)}, bf16[256,1536]{1,0:T(8,128)(2,1)}, u32[]{:S(2)}, u32[]{:S(2)}) collective-permute-start(bf16[256,1536]{1,0:T(8,128)(2,1)} %get-tuple-element.457.refs_0_.refs_1_), channel_id=1, source_target_pairs={{0,1},{1,0},{2,3},{3,2},{4,5},{5,4},{6,7},{7,6},{8,9},{9,8},{10,11... | collective-permute-start | bytes 2359304 | tf_op jit(solution)/shard_map/cond/branch_1_fun/ppermute | solution.py:1069
  178.4 17.4 %collective-permute-start.24 = (bf16[256,1536]{1,0:T(8,128)(2,1)}, bf16[256,1536]{1,0:T(8,128)(2,1)}, u32[]{:S(2)}, u32[]{:S(2)}) collective-permute-start(bf16[256,1536]{1,0:T(8,128)(2,1)} %get-tuple-element.458.refs_1_.refs_2_), channel_id=1, source_target_pairs={{0,1},{1,0},{2,3},{3,2},{4,5},{5,4},{6,7},{7,6},{8,9},{9,8},{10,11... | collective-permute-start | bytes 2359304 | tf_op jit(solution)/shard_map/cond/branch_1_fun/ppermute | solution.py:1069
  201.7 34.1 %collective-permute-start.26 = (bf16[320,1536]{1,0:T(8,128)(2,1)}, bf16[320,1536]{1,0:T(8,128)(2,1)}, u32[]{:S(2)}, u32[]{:S(2)}) collective-permute-start(bf16[320,1536]{1,0:T(8,128)(2,1)} %get-tuple-element.493), channel_id=1, source_target_pairs={{0,4},{4,0},{1,5},{5,1},{2,6},{6,2},{3,7},{7,3},{8,12},{12,8},{9,1... | collective-permute-start | bytes 2949128 | tf_op jit(solution)/shard_map/cond/branch_1_fun/ppermute | solution.py:1069
  202.5 33.4 %collective-permute-start.25 = (bf16[320,1536]{1,0:T(8,128)(2,1)}, bf16[320,1536]{1,0:T(8,128)(2,1)}, u32[]{:S(2)}, u32[]{:S(2)}) collective-permute-start(bf16[320,1536]{1,0:T(8,128)(2,1)} %get-tuple-element.493), channel_id=1, source_target_pairs={{0,2},{2,0},{1,3},{3,1},{4,6},{6,4},{5,7},{7,5},{8,10},{10,8},{9,1... | collective-permute-start | bytes 2949128 | tf_op jit(solution)/shard_map/cond/branch_1_fun/ppermute | solution.py:1069
  235.9 158.6 %reduce-scatter.6.cloned.1.call-start = ((), (), s32[]{:S(2)}) async-start(), calls=%async_computation.10 | async-start | bytes 4423680 | tf_op jit(solution)/shard_map/reduce_scatter | solution.py:1132
  238.2 19.8 %collective-permute-start.27 = (bf16[160,1536]{1,0:T(8,128)(2,1)}, bf16[160,1536]{1,0:T(8,128)(2,1)}, u32[]{:S(2)}, u32[]{:S(2)}) collective-permute-start(bf16[160,1536]{1,0:T(8,128)(2,1)} %get-tuple-element.494), channel_id=1, source_target_pairs={{0,4},{4,0},{1,5},{5,1},{2,6},{6,2},{3,7},{7,3},{8,12},{12,8},{9,1... | collective-permute-start | bytes 1474568 | tf_op jit(solution)/shard_map/cond/branch_1_fun/ppermute | solution.py:1069
  239.6 18.4 %collective-permute-start.28 = (bf16[160,1536]{1,0:T(8,128)(2,1)}, bf16[160,1536]{1,0:T(8,128)(2,1)}, u32[]{:S(2)}, u32[]{:S(2)}) collective-permute-start(bf16[160,1536]{1,0:T(8,128)(2,1)} %get-tuple-element.495), channel_id=1, source_target_pairs={{0,2},{2,0},{1,3},{3,1},{4,6},{6,4},{5,7},{7,5},{8,10},{10,8},{9,1... | collective-permute-start | bytes 1474568 | tf_op jit(solution)/shard_map/cond/branch_1_fun/ppermute | solution.py:1069
  258.0 8.6 %collective-permute-start.63 = (bf16[1024,1536]{1,0:T(8,128)(2,1)S(1)}, bf16[1024,1536]{1,0:T(8,128)(2,1)S(1)}, u32[]{:S(2)}, u32[]{:S(2)}) collective-permute-start(bf16[1024,1536]{1,0:T(8,128)(2,1)S(1)} %get-tuple-element.861.refs_6_), channel_id=1, source_target_pairs={{0,1},{1,0},{2,3},{3,2},{4,5},{5,4},{6,7},{7,6},{8,9},{9,8},{10,11... | collective-permute-start | bytes 9437192 | tf_op jit(solution)/shard_map/ppermute | solution.py:1069
  270.4 34.6 %collective-permute-start.29 = (bf16[256,1536]{1,0:T(8,128)(2,1)}, bf16[256,1536]{1,0:T(8,128)(2,1)}, u32[]{:S(2)}, u32[]{:S(2)}) collective-permute-start(bf16[256,1536]{1,0:T(8,128)(2,1)} %get-tuple-element.513), channel_id=1, source_target_pairs={{0,2},{2,0},{1,3},{3,1},{4,6},{6,4},{5,7},{7,5},{8,10},{10,8},{9,1... | collective-permute-start | bytes 2359304 | tf_op jit(solution)/shard_map/cond/branch_1_fun/ppermute | solution.py:1069
  270.9 34.2 %collective-permute-start.30 = (bf16[256,1536]{1,0:T(8,128)(2,1)}, bf16[256,1536]{1,0:T(8,128)(2,1)}, u32[]{:S(2)}, u32[]{:S(2)}) collective-permute-start(bf16[256,1536]{1,0:T(8,128)(2,1)} %get-tuple-element.514), channel_id=1, source_target_pairs={{0,4},{4,0},{1,5},{5,1},{2,6},{6,2},{3,7},{7,3},{8,12},{12,8},{9,1... | collective-permute-start | bytes 2359304 | tf_op jit(solution)/shard_map/cond/branch_1_fun/ppermute | solution.py:1069
  271.0 37.3 %collective-permute-start.31 = (bf16[256,1536]{1,0:T(8,128)(2,1)}, bf16[256,1536]{1,0:T(8,128)(2,1)}, u32[]{:S(2)}, u32[]{:S(2)}) collective-permute-start(bf16[256,1536]{1,0:T(8,128)(2,1)} %get-tuple-element.515), channel_id=1, source_target_pairs={{0,6},{2,4},{4,2},{6,0},{1,7},{3,5},{5,3},{7,1},{8,14},{10,12},{12... | collective-permute-start | bytes 2359304 | tf_op jit(solution)/shard_map/cond/branch_1_fun/ppermute | solution.py:1095
  308.3 134.2 %reduce-scatter.8.cloned.1.call-start = ((), (), s32[]{:S(2)}) async-start(), calls=%async_computation.11 | async-start | bytes 2457600 | tf_op jit(solution)/shard_map/reduce_scatter | solution.py:1132
  308.5 64.3 %collective-permute-start.69 = (bf16[1024,1536]{1,0:T(8,128)(2,1)}, bf16[1024,1536]{1,0:T(8,128)(2,1)}, u32[]{:S(2)}, u32[]{:S(2)}) collective-permute-start(bf16[1024,1536]{1,0:T(8,128)(2,1)} %get-tuple-element.910), channel_id=1, source_target_pairs={{0,1},{1,0},{2,3},{3,2},{4,5},{5,4},{6,7},{7,6},{8,9},{9,8},{10,11... | collective-permute-start | bytes 9437192 | tf_op jit(solution)/shard_map/ppermute | solution.py:1069
  317.2 7.8 %collective-permute-start.65 = (bf16[384,256]{1,0:T(8,128)(2,1)S(1)}, bf16[384,256]{1,0:T(8,128)(2,1)S(1)}, u32[]{:S(2)}, u32[]{:S(2)}) collective-permute-start(bf16[384,256]{1,0:T(8,128)(2,1)S(1)} %bitcast.80), channel_id=1, source_target_pairs={{0,4},{4,0},{1,5},{5,1},{2,6},{6,2},{3,7},{7,3},{8,12},{12,8},{9,1... | collective-permute-start | bytes 589832 | tf_op jit(solution)/shard_map/ppermute | solution.py:1069
  317.6 10.8 %collective-permute-start.64 = (bf16[384,256]{1,0:T(8,128)(2,1)S(1)}, bf16[384,256]{1,0:T(8,128)(2,1)S(1)}, u32[]{:S(2)}, u32[]{:S(2)}) collective-permute-start(bf16[384,256]{1,0:T(8,128)(2,1)S(1)} %bitcast.79), channel_id=1, source_target_pairs={{0,2},{2,0},{1,3},{3,1},{4,6},{6,4},{5,7},{7,5},{8,10},{10,8},{9,1... | collective-permute-start | bytes 589832 | tf_op jit(solution)/shard_map/ppermute | solution.py:1069
  318.0 10.4 %collective-permute-start.66 = (bf16[384,256]{1,0:T(8,128)(2,1)S(1)}, bf16[384,256]{1,0:T(8,128)(2,1)S(1)}, u32[]{:S(2)}, u32[]{:S(2)}) collective-permute-start(bf16[384,256]{1,0:T(8,128)(2,1)S(1)} %bitcast.78), channel_id=1, source_target_pairs={{0,6},{2,4},{4,2},{6,0},{1,7},{3,5},{5,3},{7,1},{8,14},{10,12},{12... | collective-permute-start | bytes 589832 | tf_op jit(solution)/shard_map/ppermute | solution.py:1095
  331.2 20.0 %collective-permute-start.51 = (bf16[256,1536]{1,0:T(8,128)(2,1)}, bf16[256,1536]{1,0:T(8,128)(2,1)}, u32[]{:S(2)}, u32[]{:S(2)}) collective-permute-start(bf16[256,1536]{1,0:T(8,128)(2,1)} %get-tuple-element.548), channel_id=1, source_target_pairs={{0,4},{4,0},{1,5},{5,1},{2,6},{6,2},{3,7},{7,3},{8,12},{12,8},{9,1... | collective-permute-start | bytes 2359304 | tf_op jit(solution)/shard_map/cond/branch_1_fun/ppermute | solution.py:1069
  332.8 19.6 %collective-permute-start.50 = (bf16[256,1536]{1,0:T(8,128)(2,1)}, bf16[256,1536]{1,0:T(8,128)(2,1)}, u32[]{:S(2)}, u32[]{:S(2)}) collective-permute-start(bf16[256,1536]{1,0:T(8,128)(2,1)} %get-tuple-element.548), channel_id=1, source_target_pairs={{0,2},{2,0},{1,3},{3,1},{4,6},{6,4},{5,7},{7,5},{8,10},{10,8},{9,1... | collective-permute-start | bytes 2359304 | tf_op jit(solution)/shard_map/cond/branch_1_fun/ppermute | solution.py:1069
  333.3 19.2 %collective-permute-start.52 = (bf16[256,1536]{1,0:T(8,128)(2,1)}, bf16[256,1536]{1,0:T(8,128)(2,1)}, u32[]{:S(2)}, u32[]{:S(2)}) collective-permute-start(bf16[256,1536]{1,0:T(8,128)(2,1)} %get-tuple-element.548), channel_id=1, source_target_pairs={{0,1},{1,0},{2,3},{3,2},{4,5},{5,4},{6,7},{7,6},{8,9},{9,8},{10,11... | collective-permute-start | bytes 2359304 | tf_op jit(solution)/shard_map/cond/branch_1_fun/ppermute | solution.py:1069
  352.5 17.9 %collective-permute-start.34 = (bf16[256,1536]{1,0:T(8,128)(2,1)}, bf16[256,1536]{1,0:T(8,128)(2,1)}, u32[]{:S(2)}, u32[]{:S(2)}) collective-permute-start(bf16[256,1536]{1,0:T(8,128)(2,1)} %get-tuple-element.568), channel_id=1, source_target_pairs={{0,1},{1,0},{2,3},{3,2},{4,5},{5,4},{6,7},{7,6},{8,9},{9,8},{10,11... | collective-permute-start | bytes 2359304 | tf_op jit(solution)/shard_map/cond/branch_1_fun/ppermute | solution.py:1069
  352.5 20.3 %collective-permute-start.32 = (bf16[256,1536]{1,0:T(8,128)(2,1)}, bf16[256,1536]{1,0:T(8,128)(2,1)}, u32[]{:S(2)}, u32[]{:S(2)}) collective-permute-start(bf16[256,1536]{1,0:T(8,128)(2,1)} %get-tuple-element.566), channel_id=1, source_target_pairs={{0,2},{2,0},{1,3},{3,1},{4,6},{6,4},{5,7},{7,5},{8,10},{10,8},{9,1... | collective-permute-start | bytes 2359304 | tf_op jit(solution)/shard_map/cond/branch_1_fun/ppermute | solution.py:1069
  353.1 19.7 %collective-permute-start.35 = (bf16[256,1536]{1,0:T(8,128)(2,1)}, bf16[256,1536]{1,0:T(8,128)(2,1)}, u32[]{:S(2)}, u32[]{:S(2)}) collective-permute-start(bf16[256,1536]{1,0:T(8,128)(2,1)} %get-tuple-element.566), channel_id=1, source_target_pairs={{0,1},{1,0},{2,3},{3,2},{4,5},{5,4},{6,7},{7,6},{8,9},{9,8},{10,11... | collective-permute-start | bytes 2359304 | tf_op jit(solution)/shard_map/cond/branch_1_fun/ppermute | solution.py:1069
  353.2 17.1 %collective-permute-start.33 = (bf16[192,1536]{1,0:T(8,128)(2,1)}, bf16[192,1536]{1,0:T(8,128)(2,1)}, u32[]{:S(2)}, u32[]{:S(2)}) collective-permute-start(bf16[192,1536]{1,0:T(8,128)(2,1)} %get-tuple-element.567), channel_id=1, source_target_pairs={{0,4},{4,0},{1,5},{5,1},{2,6},{6,2},{3,7},{7,3},{8,12},{12,8},{9,1... | collective-permute-start | bytes 1769480 | tf_op jit(solution)/shard_map/cond/branch_1_fun/ppermute | solution.py:1069
  375.3 19.1 %collective-permute-start.38 = (bf16[640,256]{1,0:T(8,128)(2,1)}, bf16[640,256]{1,0:T(8,128)(2,1)}, u32[]{:S(2)}, u32[]{:S(2)}) collective-permute-start(bf16[640,256]{1,0:T(8,128)(2,1)} %get-tuple-element.587), channel_id=1, source_target_pairs={{0,6},{2,4},{4,2},{6,0},{1,7},{3,5},{5,3},{7,1},{8,14},{10,12},{12... | collective-permute-start | bytes 983048 | tf_op jit(solution)/shard_map/cond/branch_1_fun/ppermute | solution.py:1095
  376.5 18.0 %collective-permute-start.37 = (bf16[640,256]{1,0:T(8,128)(2,1)}, bf16[640,256]{1,0:T(8,128)(2,1)}, u32[]{:S(2)}, u32[]{:S(2)}) collective-permute-start(bf16[640,256]{1,0:T(8,128)(2,1)} %get-tuple-element.586), channel_id=1, source_target_pairs={{0,4},{4,0},{1,5},{5,1},{2,6},{6,2},{3,7},{7,3},{8,12},{12,8},{9,1... | collective-permute-start | bytes 983048 | tf_op jit(solution)/shard_map/cond/branch_1_fun/ppermute | solution.py:1069
  377.2 17.2 %collective-permute-start.36 = (bf16[640,256]{1,0:T(8,128)(2,1)}, bf16[640,256]{1,0:T(8,128)(2,1)}, u32[]{:S(2)}, u32[]{:S(2)}) collective-permute-start(bf16[640,256]{1,0:T(8,128)(2,1)} %get-tuple-element.585), channel_id=1, source_target_pairs={{0,2},{2,0},{1,3},{3,1},{4,6},{6,4},{5,7},{7,5},{8,10},{10,8},{9,1... | collective-permute-start | bytes 983048 | tf_op jit(solution)/shard_map/cond/branch_1_fun/ppermute | solution.py:1069
  396.4 20.0 %collective-permute-start.56 = (bf16[192,1152]{1,0:T(8,128)(2,1)S(1)}, bf16[192,1152]{1,0:T(8,128)(2,1)}, u32[]{:S(2)}, u32[]{:S(2)}) collective-permute-start(bf16[192,1152]{1,0:T(8,128)(2,1)S(1)} %constant_dynamic-slice_fusion.1), channel_id=1, source_target_pairs={{0,4},{4,0},{1,5},{5,1},{2,6},{6,2},{3,7},{7,3},{8,12},{12,8},{9,1... | collective-permute-start | bytes 1327112 | tf_op jit(solution)/shard_map/cond/branch_1_fun/ppermute | solution.py:1069
  398.9 17.5 %collective-permute-start.57 = (bf16[1280,256]{1,0:T(8,128)(2,1)}, bf16[1280,256]{1,0:T(8,128)(2,1)}, u32[]{:S(2)}, u32[]{:S(2)}) collective-permute-start(bf16[1280,256]{1,0:T(8,128)(2,1)} %far_parts.4), channel_id=1, source_target_pairs={{0,1},{1,0},{2,3},{3,2},{4,5},{5,4},{6,7},{7,6},{8,9},{9,8},{10,11... | collective-permute-start | bytes 1966088 | tf_op jit(solution)/shard_map/cond/branch_1_fun/ppermute | solution.py:1069
  399.7 11.8 %collective-permute-start.55 = (bf16[128,1536]{1,0:T(8,128)(2,1)}, bf16[128,1536]{1,0:T(8,128)(2,1)}, u32[]{:S(2)}, u32[]{:S(2)}) collective-permute-start(bf16[128,1536]{1,0:T(8,128)(2,1)} %get-tuple-element.1153), channel_id=1, source_target_pairs={{0,2},{2,0},{1,3},{3,1},{4,6},{6,4},{5,7},{7,5},{8,10},{10,8},{9,1... | collective-permute-start | bytes 1179656 | tf_op jit(solution)/shard_map/cond/branch_1_fun/ppermute | solution.py:1069
  400.9 15.5 %collective-permute-start.54 = (bf16[128,1536]{1,0:T(8,128)(2,1)S(1)}, bf16[128,1536]{1,0:T(8,128)(2,1)}, u32[]{:S(2)}, u32[]{:S(2)}) collective-permute-start(bf16[128,1536]{1,0:T(8,128)(2,1)S(1)} %get-tuple-element.1154), channel_id=1, source_target_pairs={{0,4},{4,0},{1,5},{5,1},{2,6},{6,2},{3,7},{7,3},{8,12},{12,8},{9,1... | collective-permute-start | bytes 1179656 | tf_op jit(solution)/shard_map/cond/branch_1_fun/ppermute | solution.py:1069
  420.8 19.8 %collective-permute-start.39 = (bf16[256,1536]{1,0:T(8,128)(2,1)}, bf16[256,1536]{1,0:T(8,128)(2,1)}, u32[]{:S(2)}, u32[]{:S(2)}) collective-permute-start(bf16[256,1536]{1,0:T(8,128)(2,1)} %get-tuple-element.623), channel_id=1, source_target_pairs={{0,2},{2,0},{1,3},{3,1},{4,6},{6,4},{5,7},{7,5},{8,10},{10,8},{9,1... | collective-permute-start | bytes 2359304 | tf_op jit(solution)/shard_map/cond/branch_1_fun/ppermute | solution.py:1069
  422.6 19.9 %collective-permute-start.40 = (bf16[256,1536]{1,0:T(8,128)(2,1)}, bf16[256,1536]{1,0:T(8,128)(2,1)}, u32[]{:S(2)}, u32[]{:S(2)}) collective-permute-start(bf16[256,1536]{1,0:T(8,128)(2,1)} %get-tuple-element.624), channel_id=1, source_target_pairs={{0,4},{4,0},{1,5},{5,1},{2,6},{6,2},{3,7},{7,3},{8,12},{12,8},{9,1... | collective-permute-start | bytes 2359304 | tf_op jit(solution)/shard_map/cond/branch_1_fun/ppermute | solution.py:1069
  443.5 7.3 %collective-permute-start.53 = (bf16[192,640]{1,0:T(8,128)(2,1)S(1)}, bf16[192,640]{1,0:T(8,128)(2,1)}, u32[]{:S(2)}, u32[]{:S(2)}) collective-permute-start(bf16[192,640]{1,0:T(8,128)(2,1)S(1)} %constant_dynamic-slice_fusion.2), channel_id=1, source_target_pairs={{0,4},{4,0},{1,5},{5,1},{2,6},{6,2},{3,7},{7,3},{8,12},{12,8},{9,1... | collective-permute-start | bytes 737288 | tf_op jit(solution)/shard_map/cond/branch_1_fun/ppermute | solution.py:1069
  (64 other events, 591.0 us)
Sparse Core Ops, SparseCore 0:
  33.0 43.8 all-gather.3
  78.5 88.2 all-gather.7
  168.3 68.4 all-gather.5
  239.0 83.8 reduce-scatter.3
  325.0 66.8 reduce-scatter.5
  396.0 41.3 reduce-scatter.7

commit v10 on v9

--- a/solution.py
+++ b/solution.py
@@ -1279,12 +1279,11 @@
     out_weights = [*out_weights[0], out_weights[1], *out_far]
 
     def first_blocks(post, grads, weight):
-        corners = corners_come(post[1:], grads[1:])
+        corner, grad_corner = swap(post[2], "y"), swap(grads[1], "x")
         far = across(post[1:])
-        return corners, far, feed_forward(post, grads, weight, [1, 2])
-
-    corners, far, early = together(first_blocks, post, grads, ffn_full[0])
-    corner, grad_corner = joined(*corners, 2)
+        return corner, grad_corner, far, feed_forward(post, grads, weight, [1, 2])
+
+    corner, grad_corner, far, early = together(first_blocks, post, grads, ffn_full[0])
     post = [*post, corner, *post_far, *far, swap(corner, "c")]
     grads = [*grads, grad_corner, *grad_far, swap(grad_corner, "c")]
 

time: 472 us -> 471 us (level)
  Pallas kernels: 234 us -> 229 us
  waiting for transfers between devices: 120 us -> 125 us
  transfers between devices with their start and end apart: 81 -> 81, of which waited for: 33 -> 34; matrix products, arithmetic and copies ran while one was open for 3% -> 3% of each run, Pallas kernels for 49% -> 48%
where the time goes in v10:
time: 471 us; the launch traced here: 465 us
  Pallas kernels  229 us (49%)
  waiting for transfers between devices  125 us (27%)
  starting transfers between devices  61 us (13%)
  blocking collectives  16.6 us (4%)
  between operations  14.6 us (3%)
  other arithmetic  10.5 us (2%)
  local copies, waits for them, and re-layouts  8.18 us (2%)
    ppermute x67, waiting for transfers between devices, swap(): return lax.ppermute(values, axis, SWAP)  102 us
    pallas_call x5, Pallas kernels, feed_forward(): pl.pallas_call(body, grid=(rows // TILE,), in_specs=specs * 2 + [entire(w...  58.7 us
    ppermute x67, starting transfers between devices, swap(): return lax.ppermute(values, axis, SWAP)  42.2 us
    pallas_call x3, Pallas kernels, weight_grads(): pl.pallas_call(body, grid=(depth // tile,), in_specs=specs + [ANY] * len(...  39.8 us
    pallas_call x2, Pallas kernels, backward_attention(): pl.pallas_call(attend_backward, grid_spec=pltpu.PrefetchScalarGridSpec(nu...  31.5 us
    all_to_all x1, blocking collectives, plane_columns(): lax.all_to_all(payload, PLANE, split_axis=0, concat_axis=0, tiled=True)  16.6 us
    pallas_call x1, Pallas kernels, attention_call(): pl.pallas_call(body, grid_spec=pltpu.PrefetchScalarGridSpec(num_scalar_pr...  15.6 us
    pallas_call x1, Pallas kernels, project_back(): pl.pallas_call(body, grid=(rows_of(lefts[0]) // TILE,), in_specs=specs +...  13.3 us
  transfers between devices with their start and end apart: 81, of which 34 were waited for; matrix products, arithmetic and copies ran while one was open for 3% of the time, Pallas kernels for 48%

profile of v10, /device:TPU:0, one launch (start us, length us, event | category | flops | bytes accessed | tf_op | source)
XLA Modules:
  0.0 465.3 jit_solution(15084584522960342836)
XLA Ops:
  7.2 2.5 pack_columns.3
  9.7 23.2 %conditional.14 = (bf16[384,640]{1,0:T(8,128)(2,1)}, bf16[192,1536]{1,0:T(8,128)(2,1)}, bf16[192,1536]{1,0:T(8,128)(2,1)}, bf16[8,48,1536]{2,1,0:T(8,128)(2,1)}, bf16[8,48,1152]{2,1,0:T(8,128)(2,1)S(1)}) conditional(s32[]{:T(128)} %convert_element_type.79, () %tuple.140, (bf16[8,48,640]{2,1,0:T(8,128)(2,1)}, bf16[192,1536]{1,0:T(8,128)(2,1)S(1)}, ...), branch_computations={%region_0.0_spmd, %region_1.0_spmd} | conditional | bytes 6193304 | solution.py:1141
  9.7 3.0 collective-permute-start
  14.1 4.1 all-to-all-start
  18.3 3.1 pack_columns.2
  21.4 11.5 %all-to-all-done = bf16[8,48,640]{2,1,0:T(8,128)(2,1)} async-done(((bf16[8,48,640]{2,1,0:T(8,128)(2,1)}), bf16[8,48,640]{2,1,0:T(8,128)(2,1)}, u32[]{:S(2)}, u32[]{:S(2)}) %all-to-all-start) | async-done | bytes 491552 | tf_op jit(solution)/shard_map/cond/branch_1_fun/all_to_all | solution.py:1145
  33.0 32.8 %conditional.15 = (bf16[128,1536]{1,0:T(8,128)(2,1)}, bf16[128,1536]{1,0:T(8,128)(2,1)}, bf16[64,1536]{1,0:T(8,128)(2,1)}, bf16[64,1536]{1,0:T(8,128)(2,1)}, bf1...) conditional(s32[]{:T(128)} %convert_element_type.79, () %tuple.142, ...), branch_computations={%region_2.0_spmd, %region_3.0_spmd} | conditional | flops 33890 | bytes 11674154 | solution.py:1141
  33.0 4.3 all-to-all-start.1
  43.9 3.0 multiply_sine_fusion
  46.9 3.0 rotary_rows.1
  50.0 7.8 %collective-permute-done.47 = bf16[64,1536]{1,0:T(8,128)(2,1)} collective-permute-done((bf16[64,1536]{1,0:T(8,128)(2,1)S(1)}, bf16[64,1536]{1,0:T(8,128)(2,1)}, u32[]{:S(2)}, u32[]{:S(2)}) %collective-permute-start.47) | collective-permute-done | bytes 196640 | tf_op jit(solution)/shard_map/cond/branch_1_fun/ppermute | solution.py:1069
  57.8 8.0 %collective-permute-done.45 = bf16[128,1536]{1,0:T(8,128)(2,1)} collective-permute-done((bf16[128,1536]{1,0:T(8,128)(2,1)}, bf16[128,1536]{1,0:T(8,128)(2,1)}, u32[]{:S(2)}, u32[]{:S(2)}) %collective-permute-start.45) | collective-permute-done | bytes 393248 | tf_op jit(solution)/shard_map/cond/branch_1_fun/ppermute | solution.py:1069
  65.8 3.1 rows_from.3
  68.9 16.6 %all_to_all.13 = bf16[8,48,1152]{2,1,0:T(8,128)(2,1)} all-to-all(bf16[8,48,1152]{2,1,0:T(8,128)(2,1)S(1)} %after.4), channel_id=1, replica_groups=mesh['dp'=4,'x'=2,'y'=2,'c'=2] {'x','y','c'}, dimensions={0} | all-to-all | bytes 1769472 | tf_op jit(solution)/shard_map/all_to_all | solution.py:1145
  86.2 3.6 turn.1
  90.9 30.1 %conditional.16 = (bf16[192,1536]{1,0:T(8,128)(2,1)}, bf16[192,1536]{1,0:T(8,128)(2,1)}, bf16[192,1536]{1,0:T(8,128)(2,1)}, bf16[192,1536]{1,0:T(8,128)(2,1)}, b...) conditional(s32[]{:T(128)} %convert_element_type.79, () %tuple.139, ...), branch_computations={%region_4.0_spmd, %region_5.0_spmd} | conditional | flops 2 | bytes 17826128 | solution.py:1141
  94.8 10.5 %norm_project.1 = (bf16[2048,1536]{1,0:T(8,128)(2,1)}, bf16[2048,320]{1,0:T(8,128)(2,1)}) custom-call(bf16[256,1536]{1,0:T(8,128)(2,1)S(1)} %get-tuple-element.418.refs_0_, bf16[256,1536]{1,0:T(8,128)(2,1)} %get-tuple-element.419.refs_1_, bf16[256,1536]{1,0:T(8,128)(2,1)} %get-tuple-element.420.refs_2_, bf16[256,1536]{1,0:T(8,128)(2,1)} %get-tuple-element.421.refs_3_, ...), custom_call_target="tpu_custom_call" | custom-call | flops 1 | bytes 1 | tf_op jit(solution)/shard_map/cond/branch_1_fun/norm_project/pallas_call | solution.py:438
  105.4 15.6 %attend_forward.1 = (bf16[2,1,256,192]{3,2,1,0:T(8,128)(2,1)}, bf16[2,1,256,192]{3,2,1,0:T(8,128)(2,1)}, bf16[2,1,256,192]{3,2,1,0:T(8,128)(2,1)}, bf16[2,1,256,...) custom-call(s32[1]{0:T(128)} %get-tuple-element.430.place_ref, ...), custom_call_target="tpu_custom_call" | custom-call | flops 1 | bytes 1 | tf_op jit(solution)/shard_map/cond/branch_1_fun/attend_forward/pallas_call | solution.py:256
  121.1 52.2 %conditional.17 = (f32[256,1536]{1,0:T(8,128)}, bf16[256,1536]{1,0:T(8,128)(2,1)}, bf16[256,1536]{1,0:T(8,128)(2,1)}, bf16[256,1536]{1,0:T(8,128)(2,1)}, bf16[25...) conditional(s32[]{:T(128)} %convert_element_type.79, () %tuple.138, ...), branch_computations={%region_6.0_spmd, %region_7.0_spmd} | conditional | flops 2 | bytes 45810620 | solution.py:1141
  124.6 5.3 %collective-permute-done.8.refs_3_ = bf16[384,256]{1,0:T(8,128)(2,1)S(1)} collective-permute-done((bf16[384,256]{1,0:T(8,128)(2,1)S(1)}, bf16[384,256]{1,0:T(8,128)(2,1)S(1)}, u32[]{:S(2)}, u32[]{:S(2)}) %collective-permute-start.8) | collective-permute-done | bytes 196640 | tf_op jit(solution)/shard_map/cond/branch_1_fun/ppermute | solution.py:1095
  141.0 5.5 %attend_out.1 = (f32[256,1536]{1,0:T(8,128)}, bf16[256,1536]{1,0:T(8,128)(2,1)}) custom-call(bf16[384,256]{1,0:T(8,128)(2,1)S(1)} %bitcast.100, bf16[384,256]{1,0:T(8,128)(2,1)S(1)} %copy-done.1, bf16[384,256]{1,0:T(8,128)(2,1)S(1)} %copy-done.5, bf16[384,256]{1,0:T(8,128)(2,1)S(1)} %copy-done.3, ...), custom_call_target="tpu_custom_call" | custom-call | flops 1 | bytes 1 | tf_op jit(solution)/shard_map/cond/branch_1_fun/attend_out/pallas_call | solution.py:697
  149.2 7.8 %collective-permute-done.17 = bf16[256,1536]{1,0:T(8,128)(2,1)} collective-permute-done((bf16[256,1536]{1,0:T(8,128)(2,1)}, bf16[256,1536]{1,0:T(8,128)(2,1)}, u32[]{:S(2)}, u32[]{:S(2)}) %collective-permute-start.17) | collective-permute-done | bytes 786464 | tf_op jit(solution)/shard_map/cond/branch_1_fun/ppermute | solution.py:1069
  157.7 15.2 %collective-permute-done.14 = bf16[256,1536]{1,0:T(8,128)(2,1)} collective-permute-done((bf16[256,1536]{1,0:T(8,128)(2,1)}, bf16[256,1536]{1,0:T(8,128)(2,1)}, u32[]{:S(2)}, u32[]{:S(2)}) %collective-permute-start.14) | collective-permute-done | bytes 786464 | tf_op jit(solution)/shard_map/cond/branch_1_fun/ppermute | solution.py:1069
  173.3 21.7 %conditional.18 = (bf16[256,1536]{1,0:T(8,128)(2,1)}, bf16[256,1536]{1,0:T(8,128)(2,1)}, bf16[256,1536]{1,0:T(8,128)(2,1)}, bf16[256,1536]{1,0:T(8,128)(2,1)}, b...) conditional(s32[]{:T(128)} %convert_element_type.79, () %tuple.146, ...), branch_computations={%region_8.0_spmd, %region_9.0_spmd} | conditional | flops 1 | bytes 12583137 | solution.py:1141
  176.0 12.2 %feed_forward.5 = (bf16[768,1024]{1,0:T(8,128)(2,1)}, bf16[768,512]{1,0:T(8,128)(2,1)S(1)}, bf16[256,1536]{1,0:T(8,128)(2,1)}, bf16[512,1536]{1,0:T(8,128)(2,1)}) custom-call(bf16[256,1536]{1,0:T(8,128)(2,1)} %get-tuple-element.460.refs_0_, bf16[256,1536]{1,0:T(8,128)(2,1)} %get-tuple-element.459.refs_1_, bf16[256,1536]{1,0:T(8,128)(2,1)} %get-tuple-element.457.refs_2_, ...), custom_call_target="tpu_custom_call" | custom-call | flops 1 | bytes 1 | tf_op jit(solution)/shard_map/cond/branch_1_fun/feed_forward/pallas_call | solution.py:494
  188.2 3.8 collective-permute-done.22
  192.0 3.0 collective-permute-done.21
  198.7 34.7 %conditional.19 = (bf16[1280,512]{1,0:T(8,128)(2,1)}, bf16[256,1536]{1,0:T(8,128)(2,1)}, bf16[1024,1536]{1,0:T(8,128)(2,1)}, bf16[1536,1536]{1,0:T(8,128)(2,1)},...) conditional(s32[]{:T(128)} %convert_element_type.79, () %tuple.149, (bf16[256,1536]{1,0:T(8,128)(2,1)}, ...), branch_computations={%region_10.0_spmd, %region_11.0_spmd} | conditional | flops 2 | bytes 14155934 | solution.py:1141
  200.1 18.2 %feed_forward.6 = (bf16[1280,1024]{1,0:T(8,128)(2,1)}, bf16[1280,512]{1,0:T(8,128)(2,1)}, bf16[256,1536]{1,0:T(8,128)(2,1)}, bf16[1024,1536]{1,0:T(8,128)(2,1)}) custom-call(bf16[256,1536]{1,0:T(8,128)(2,1)} %get-tuple-element.468.refs_0_.refs_3_, bf16[256,1536]{1,0:T(8,128)(2,1)} %get-tuple-element.469.refs_1_.refs_4_, ...), custom_call_target="tpu_custom_call" | custom-call | flops 1 | bytes 1 | tf_op jit(solution)/shard_map/cond/branch_1_fun/feed_forward/pallas_call | solution.py:494
  218.3 15.0 %weight_grads.3 = bf16[1536,1536]{1,0:T(8,128)(2,1)} custom-call(bf16[256,1536]{1,0:T(8,128)(2,1)} %get-tuple-element.482.refs_0_, bf16[256,1536]{1,0:T(8,128)(2,1)} %get-tuple-element.483.refs_1_, bf16[256,1536]{1,0:T(8,128)(2,1)} %get-tuple-element.484.refs_2_, bf16[256,1536]{1,0:T(8,128)(2,1)} %get-tuple-element.468.refs_0_.refs_3_, ...), custom_call_target="tpu_custom_call" | custom-call | flops 1 | bytes 1 | tf_op jit(solution)/shard_map/cond/branch_1_fun/weight_grads/pallas_call | solution.py:595
  236.8 20.1 %conditional.20 = (bf16[160,1536]{1,0:T(8,128)(2,1)}, bf16[160,1536]{1,0:T(8,128)(2,1)}, bf16[1280,768]{1,0:T(8,128)(2,1)}, bf16[1280,384]{1,0:T(8,128)(2,1)}, b...) conditional(s32[]{:T(128)} %convert_element_type.79, () %tuple.148, (bf16[160,1536]{1,0:T(8,128)(2,1)S(1)}, ...), branch_computations={%region_12.0_spmd, %region_13.0_spmd} | conditional | flops 393217 | bytes 8650814 | solution.py:1141
  239.8 15.8 %feed_forward.7 = (bf16[1280,768]{1,0:T(8,128)(2,1)}, bf16[1280,384]{1,0:T(8,128)(2,1)}, bf16[256,1536]{1,0:T(8,128)(2,1)}, bf16[1024,1536]{1,0:T(8,128)(2,1)S(1)}) custom-call(bf16[256,1536]{1,0:T(8,128)(2,1)} %get-tuple-element.494.refs_0_, bf16[256,1536]{1,0:T(8,128)(2,1)} %get-tuple-element.495.refs_1_, bf16[256,1536]{1,0:T(8,128)(2,1)} %get-tuple-element.496.refs_2_, ...), custom_call_target="tpu_custom_call" | custom-call | flops 1 | bytes 1 | tf_op jit(solution)/shard_map/cond/branch_1_fun/feed_forward/pallas_call | solution.py:494
  257.0 8.5 %feed_forward.9 = (bf16[512,768]{1,0:T(8,128)(2,1)}, bf16[512,384]{1,0:T(8,128)(2,1)S(1)}, bf16[512,1536]{1,0:T(8,128)(2,1)}) custom-call(bf16[256,1536]{1,0:T(8,128)(2,1)} %get-tuple-element.830.refs_0_, bf16[256,1536]{1,0:T(8,128)(2,1)} %get-tuple-element.831.refs_1_, bf16[256,1536]{1,0:T(8,128)(2,1)} %get-tuple-element.832.refs_2_, ...), custom_call_target="tpu_custom_call" | custom-call | flops 1 | bytes 1 | tf_op jit(solution)/shard_map/feed_forward/pallas_call | solution.py:494
  265.5 3.8 add_convert_fusion.2
  269.4 37.8 %conditional.21 = (bf16[256,1536]{1,0:T(8,128)(2,1)}, bf16[256,1536]{1,0:T(8,128)(2,1)}, bf16[256,1536]{1,0:T(8,128)(2,1)}, bf16[256,1536]{1,0:T(8,128)(2,1)}, b...) conditional(s32[]{:T(128)} %convert_element_type.79, () %tuple.137, ...), branch_computations={%region_14.0_spmd, %region_15.0_spmd} | conditional | flops 3 | bytes 12976218 | solution.py:1141
  269.6 3.2 collective-permute-start.31
  272.9 4.1 feed_forward.8
  276.9 13.3 %project_back.1 = (bf16[256,1536]{1,0:T(8,128)(2,1)}, bf16[512,1536]{1,0:T(8,128)(2,1)}, bf16[256,1536]{1,0:T(8,128)(2,1)}, bf16[1024,1536]{1,0:T(8,128)(2,1)}) custom-call(bf16[768,512]{1,0:T(8,128)(2,1)} %get-tuple-element.539.refs_0_, bf16[1280,512]{1,0:T(8,128)(2,1)} %get-tuple-element.540.refs_1_, bf16[256,384]{1,0:T(8,128)(2,1)} %get-tuple-element.536.refs_19_.refs_2_, ...), custom_call_target="tpu_custom_call" | custom-call | flops 1 | bytes 1 | tf_op jit(solution)/shard_map/cond/branch_1_fun/project_back/pallas_call | solution.py:646
  290.2 13.7 %weight_grads.4 = bf16[1536,1152]{1,0:T(8,128)(2,1)} custom-call(bf16[256,1536]{1,0:T(8,128)(2,1)} %get-tuple-element.514.refs_0_, bf16[256,1536]{1,0:T(8,128)(2,1)} %get-tuple-element.519.refs_1_, bf16[256,1536]{1,0:T(8,128)(2,1)} %get-tuple-element.520.refs_2_, bf16[256,1536]{1,0:T(8,128)(2,1)} %get-tuple-element.521.refs_3_, ...), custom_call_target="tpu_custom_call" | custom-call | flops 1 | bytes 1 | tf_op jit(solution)/shard_map/cond/branch_1_fun/weight_grads/pallas_call | solution.py:595
  304.0 3.2 collective-permute-done.31
  308.0 8.1 %middle_back.1 = (f32[256,1536]{1,0:T(8,128)}, bf16[256,1536]{1,0:T(8,128)(2,1)}, bf16[2,192,256]{2,1,0:T(8,128)(2,1)S(1)}, bf16[2,192,256]{2,1,0:T(8,128)(2,1)S...) custom-call(bf16[256,1536]{1,0:T(8,128)(2,1)} %get-tuple-element.864.refs_0_, ...), custom_call_target="tpu_custom_call" | custom-call | flops 1 | bytes 1 | tf_op jit(solution)/shard_map/middle_back/pallas_call | solution.py:756
  316.7 2.9 collective-permute-start.66
  319.6 4.2 collective-permute-done.65.refs_2_
  323.9 3.6 collective-permute-done.64.refs_1_
  330.2 21.4 %conditional.22 = (bf16[256,1536]{1,0:T(8,128)(2,1)}, bf16[256,1536]{1,0:T(8,128)(2,1)}, bf16[256,1536]{1,0:T(8,128)(2,1)}, bf16[2,1,256,320]{3,2,1,0:T(8,128)(2...) conditional(s32[]{:T(128)} %convert_element_type.79, () %tuple.136, ...), branch_computations={%region_17.0_spmd, %region_18.0_spmd} | conditional | flops 9 | bytes 15335739 | solution.py:1141
  332.3 15.8 %attend_backward.2 = (bf16[2,1,256,320]{3,2,1,0:T(8,128)(2,1)}, bf16[2,1,256,320]{3,2,1,0:T(8,128)(2,1)}, bf16[2,1,320,256]{3,2,1,0:T(8,128)(2,1)S(1)}, bf16[2,1,320,256]{3,2,1,0:T(8,128)(2,1)}, f32[1,8,256]{2,1,0:T(8,128)S(1)}) custom-call(s32[1]{0:T(128)} %get-tuple-element.547.place_ref, bf16[2,2,2,1,256,320]{5,4,3,2,1,0:T(8,128)(2,1)} %bitcast.16.qkv_ref, ...), custom_call_target="tpu_custom_call" | custom-call | flops 1 | bytes 1 | tf_op jit(solution)/shard_map/cond/branch_1_fun/attend_backward/pallas_call | solution.py:320
  351.6 20.4 %conditional.23 = (bf16[256,1536]{1,0:T(8,128)(2,1)}, bf16[192,1536]{1,0:T(8,128)(2,1)}, bf16[256,1536]{1,0:T(8,128)(2,1)}, bf16[256,1536]{1,0:T(8,128)(2,1)}, b...) conditional(s32[]{:T(128)} %convert_element_type.79, () %tuple.154, ...), branch_computations={%region_19.0_spmd, %region_20.0_spmd} | conditional | flops 1 | bytes 11796713 | solution.py:1141
  353.7 15.7 %attend_backward.3 = (bf16[2,1,256,320]{3,2,1,0:T(8,128)(2,1)}, bf16[2,1,256,320]{3,2,1,0:T(8,128)(2,1)}, bf16[2,1,320,256]{3,2,1,0:T(8,128)(2,1)}, bf16[2,1,320,256]{3,2,1,0:T(8,128)(2,1)}, f32[1,8,256]{2,1,0:T(8,128)S(1)}) custom-call(s32[1]{0:T(128)} %get-tuple-element.567.place_ref, bf16[2,2,2,1,256,320]{5,4,3,2,1,0:T(8,128)(2,1)} %bitcast.27.qkv_ref, ...), custom_call_target="tpu_custom_call" | custom-call | flops 1 | bytes 1 | tf_op jit(solution)/shard_map/cond/branch_1_fun/attend_backward/pallas_call | solution.py:320
  369.3 2.6 collective-permute-done.32
  372.0 2.5 collective-permute-done.68
  374.5 19.2 %conditional.24 = (bf16[640,256]{1,0:T(8,128)(2,1)}, bf16[640,256]{1,0:T(8,128)(2,1)}, bf16[640,256]{1,0:T(8,128)(2,1)}, bf16[1536,640]{1,0:T(8,128)(2,1)S(1)}, ...) conditional(s32[]{:T(128)} %convert_element_type.79, () %tuple.135, ...), branch_computations={%region_21.0_spmd, %region_22.0_spmd} | conditional | flops 2 | bytes 8388842 | solution.py:1141
  378.0 4.7 %sent_sums.1 = (bf16[256,1536]{1,0:T(8,128)(2,1)}, bf16[256,1536]{1,0:T(8,128)(2,1)}, bf16[256,1536]{1,0:T(8,128)(2,1)}) custom-call(bf16[512,1536]{1,0:T(8,128)(2,1)} %get-tuple-element.607.sides_ref, bf16[256,1536]{1,0:T(8,128)(2,1)} %get-tuple-element.608.corner_ref, bf16[1024,1536]{1,0:T(8,128)(2,1)} %get-tuple-element.609.far_ref), custom_call_target="tpu_custom_call" | custom-call | flops 1 | bytes 1 | tf_op jit(solution)/shard_map/cond/branch_1_fun/sent_sums/pallas_call | solution.py:815
  382.6 11.0 %weight_grads.5 = bf16[1536,640]{1,0:T(8,128)(2,1)S(1)} custom-call(bf16[2048,1536]{1,0:T(8,128)(2,1)} %get-tuple-element.586.refs_0_, bf16[512,320]{1,0:T(8,128)(2,1)} %bitcast.102, bf16[512,320]{1,0:T(8,128)(2,1)S(1)} %bitcast.101, bf16[512,320]{1,0:T(8,128)(2,1)} %bitcast.104, bf16[512,320]{1,0:T(8,128)(2,1)} %bitcast.103, ...), custom_call_target="tpu_custom_call" | custom-call | flops 1 | bytes 1 | tf_op jit(solution)/shard_map/cond/branch_1_fun/weight_grads/pallas_call | solution.py:595
  395.6 20.0 %conditional.25 = (bf16[128,1536]{1,0:T(8,128)(2,1)}, bf16[128,1536]{1,0:T(8,128)(2,1)}, bf16[192,1152]{1,0:T(8,128)(2,1)}, bf16[1280,256]{1,0:T(8,128)(2,1)}, bf16[320,1536]{1,0:T(8,128)(2,1)S(1)}) conditional(s32[]{:T(128)} %convert_element_type.79, () %tuple.158, (bf16[256,1536]{1,0:T(8,128)(2,1)}, bf16[384,1152]{1,0:T(8,128)(2,1)S(1)}, ...), branch_computations={%region_24.0_spmd, %region_25.0_spmd} | conditional | flops 10 | bytes 13140292 | solution.py:1141
  402.1 8.6 %collective-permute-done.55 = bf16[128,1536]{1,0:T(8,128)(2,1)} collective-permute-done((bf16[128,1536]{1,0:T(8,128)(2,1)}, bf16[128,1536]{1,0:T(8,128)(2,1)}, u32[]{:S(2)}, u32[]{:S(2)}) %collective-permute-start.55) | collective-permute-done | bytes 393248 | tf_op jit(solution)/shard_map/cond/branch_1_fun/ppermute | solution.py:1069
  410.7 4.8 %collective-permute-done.54 = bf16[128,1536]{1,0:T(8,128)(2,1)} collective-permute-done((bf16[128,1536]{1,0:T(8,128)(2,1)S(1)}, bf16[128,1536]{1,0:T(8,128)(2,1)}, u32[]{:S(2)}, u32[]{:S(2)}) %collective-permute-start.54) | collective-permute-done | bytes 393248 | tf_op jit(solution)/shard_map/cond/branch_1_fun/ppermute | solution.py:1069
  415.6 3.2 corner_sum.1
  418.8 22.8 %conditional.26 = (bf16[256,1536]{1,0:T(8,128)(2,1)}, bf16[256,1536]{1,0:T(8,128)(2,1)}, f32[192,1728]{1,0:T(8,128)}, f32[192,1728]{1,0:T(8,128)}, f32[192,1728]{1,0:T(8,128)}, /*index=5*/f32[1,256,1536]{2,1,0:T(8,128)}) conditional(s32[]{:T(128)} %convert_element_type.79, () %tuple.157, (bf16[256,1536]{1,0:T(8,128)(2,1)}, ...), branch_computations={%region_26.0_spmd, %region_27.0_spmd} | conditional | flops 1 | bytes 32244056 | solution.py:1141
  422.2 3.8 unpack_columns.2
  426.0 7.2 %input_back.1 = f32[256,1536]{1,0:T(8,128)} custom-call(bf16[640,256]{1,0:T(8,128)(2,1)S(1)} %get-tuple-element.631.refs_0_, bf16[640,256]{1,0:T(8,128)(2,1)} %get-tuple-element.632.refs_1_, bf16[640,256]{1,0:T(8,128)(2,1)} %get-tuple-element.633.refs_2_, bf16[640,256]{1,0:T(8,128)(2,1)} %get-tuple-element.634.refs_3_, ...), custom_call_target="tpu_custom_call" | custom-call | flops 1 | bytes 1 | tf_op jit(solution)/shard_map/cond/branch_1_fun/input_back/pallas_call | solution.py:787
  433.3 6.5 %collective-permute-done.39 = bf16[256,1536]{1,0:T(8,128)(2,1)} collective-permute-done((bf16[256,1536]{1,0:T(8,128)(2,1)}, bf16[256,1536]{1,0:T(8,128)(2,1)}, u32[]{:S(2)}, u32[]{:S(2)}) %collective-permute-start.39) | collective-permute-done | bytes 786464 | tf_op jit(solution)/shard_map/cond/branch_1_fun/ppermute | solution.py:1069
  441.6 8.3 %conditional.27 = (bf16[192,640]{1,0:T(8,128)(2,1)}, bf16[1,256,1536]{2,1,0:T(8,128)(2,1)S(1)}) conditional(s32[]{:T(128)} %convert_element_type.79, () %tuple.134, (bf16[384,640]{1,0:T(8,128)(2,1)}, bf16[256,1536]{1,0:T(8,128)(2,1)}, bf16[1024,1536]{1,0:T(8,128)(2,1)}, bf16[256,1536]{1,0:T(8,128)(2,1)}, bf16[256,1536]{1,0:T(8,128)(2,1)}, ...), branch_computations={%region_29.0_spmd, %region_30.0_spmd} | conditional | flops 3538952 | bytes 6979734 | solution.py:1141
  445.5 4.4 collective-permute-done.53
  449.9 2.4 unpack_columns.3
  (256 shorter events, 86.7 us)
Async XLA Ops:
  7.2 79.0 %all-gather.4.cloned.1.call-start = ((), (), s32[]{:S(2)}) async-start(), calls=%async_computation.6 | async-start | bytes 2457600 | tf_op jit(solution)/shard_map/all_gather | solution.py:1128
  9.7 23.2 %collective-permute-start = (bf16[192,1536]{1,0:T(8,128)(2,1)S(1)}, bf16[192,1536]{1,0:T(8,128)(2,1)}, u32[]{:S(2)}, u32[]{:S(2)}) collective-permute-start(bf16[192,1536]{1,0:T(8,128)(2,1)S(1)} %get-tuple-element.400), channel_id=1, source_target_pairs={{0,2},{2,0},{1,3},{3,1},{4,6},{6,4},{5,7},{7,5},{8,10},{10,8},{9,1... | collective-permute-start | bytes 1769480 | tf_op jit(solution)/shard_map/cond/branch_1_fun/ppermute | solution.py:1069
  12.7 20.2 %collective-permute-start.1 = (bf16[192,1536]{1,0:T(8,128)(2,1)S(1)}, bf16[192,1536]{1,0:T(8,128)(2,1)}, u32[]{:S(2)}, u32[]{:S(2)}) collective-permute-start(bf16[192,1536]{1,0:T(8,128)(2,1)S(1)} %get-tuple-element.401), channel_id=1, source_target_pairs={{0,4},{4,0},{1,5},{5,1},{2,6},{6,2},{3,7},{7,3},{8,12},{12,8},{9,1... | collective-permute-start | bytes 1769480 | tf_op jit(solution)/shard_map/cond/branch_1_fun/ppermute | solution.py:1069
  14.1 18.7 %all-to-all-start = ((bf16[8,48,640]{2,1,0:T(8,128)(2,1)}), bf16[8,48,640]{2,1,0:T(8,128)(2,1)}, u32[]{:S(2)}, u32[]{:S(2)}) async-start(bf16[8,48,640]{2,1,0:T(8,128)(2,1)} %get-tuple-element.399), calls=%async_computation | async-start | bytes 983040 | tf_op jit(solution)/shard_map/cond/branch_1_fun/all_to_all | solution.py:1145
  32.9 140.4 %all-gather.8.cloned.1.call-start = ((), (), s32[]{:S(2)}) async-start(), calls=%async_computation.8 | async-start | bytes 5898240 | tf_op jit(solution)/shard_map/all_gather | solution.py:1128
  33.0 32.8 %all-to-all-start.1 = ((bf16[8,48,1536]{2,1,0:T(8,128)(2,1)}), bf16[8,48,1536]{2,1,0:T(8,128)(2,1)}, u32[]{:S(2)}, u32[]{:S(2)}) async-start(bf16[8,48,1536]{2,1,0:T(8,128)(2,1)} %get-tuple-element.416), calls=%async_computation.1 | async-start | bytes 2359296 | tf_op jit(solution)/shard_map/cond/branch_1_fun/all_to_all | solution.py:1145
  37.2 28.5 %collective-permute-start.49 = (bf16[256,1536]{1,0:T(8,128)(2,1)S(1)}, bf16[256,1536]{1,0:T(8,128)(2,1)}, u32[]{:S(2)}, u32[]{:S(2)}) collective-permute-start(bf16[256,1536]{1,0:T(8,128)(2,1)S(1)} %get-tuple-element.413), channel_id=1, source_target_pairs={{0,1},{1,0},{2,3},{3,2},{4,5},{5,4},{6,7},{7,6},{8,9},{9,8},{10,11... | collective-permute-start | bytes 2359304 | tf_op jit(solution)/shard_map/cond/branch_1_fun/ppermute | solution.py:1069
  37.6 20.2 %collective-permute-start.47 = (bf16[64,1536]{1,0:T(8,128)(2,1)S(1)}, bf16[64,1536]{1,0:T(8,128)(2,1)}, u32[]{:S(2)}, u32[]{:S(2)}) collective-permute-start(bf16[64,1536]{1,0:T(8,128)(2,1)S(1)} %get-tuple-element.411), channel_id=1, source_target_pairs={{0,2},{2,0},{1,3},{3,1},{4,6},{6,4},{5,7},{7,5},{8,10},{10,8},{9,1... | collective-permute-start | bytes 589832 | tf_op jit(solution)/shard_map/cond/branch_1_fun/ppermute | solution.py:1069
  39.3 18.5 %collective-permute-start.48 = (bf16[64,1536]{1,0:T(8,128)(2,1)S(1)}, bf16[64,1536]{1,0:T(8,128)(2,1)}, u32[]{:S(2)}, u32[]{:S(2)}) collective-permute-start(bf16[64,1536]{1,0:T(8,128)(2,1)S(1)} %get-tuple-element.412), channel_id=1, source_target_pairs={{0,4},{4,0},{1,5},{5,1},{2,6},{6,2},{3,7},{7,3},{8,12},{12,8},{9,1... | collective-permute-start | bytes 589832 | tf_op jit(solution)/shard_map/cond/branch_1_fun/ppermute | solution.py:1069
  43.0 22.7 %collective-permute-start.45 = (bf16[128,1536]{1,0:T(8,128)(2,1)}, bf16[128,1536]{1,0:T(8,128)(2,1)}, u32[]{:S(2)}, u32[]{:S(2)}) collective-permute-start(bf16[128,1536]{1,0:T(8,128)(2,1)} %get-tuple-element.409), channel_id=1, source_target_pairs={{0,4},{4,0},{1,5},{5,1},{2,6},{6,2},{3,7},{7,3},{8,12},{12,8},{9,1... | collective-permute-start | bytes 1179656 | tf_op jit(solution)/shard_map/cond/branch_1_fun/ppermute | solution.py:1069
  43.6 22.2 %collective-permute-start.46 = (bf16[128,1536]{1,0:T(8,128)(2,1)}, bf16[128,1536]{1,0:T(8,128)(2,1)}, u32[]{:S(2)}, u32[]{:S(2)}) collective-permute-start(bf16[128,1536]{1,0:T(8,128)(2,1)} %get-tuple-element.410), channel_id=1, source_target_pairs={{0,2},{2,0},{1,3},{3,1},{4,6},{6,4},{5,7},{7,5},{8,10},{10,8},{9,1... | collective-permute-start | bytes 1179656 | tf_op jit(solution)/shard_map/cond/branch_1_fun/ppermute | solution.py:1069
  65.8 171.0 %all-gather.6.cloned.1.call-start = ((), (), s32[]{:S(2)}) async-start(), calls=%async_computation.7 | async-start | bytes 4423680 | tf_op jit(solution)/shard_map/all_gather | solution.py:1128
  85.5 244.7 %reduce-scatter.4.cloned.1.call-start = ((), (), s32[]{:S(2)}) async-start(), calls=%async_computation.9 | async-start | bytes 5898240 | tf_op jit(solution)/shard_map/reduce_scatter | solution.py:1132
  90.9 30.1 %collective-permute-start.5 = (bf16[192,1536]{1,0:T(8,128)(2,1)S(1)}, bf16[192,1536]{1,0:T(8,128)(2,1)}, u32[]{:S(2)}, u32[]{:S(2)}) collective-permute-start(bf16[192,1536]{1,0:T(8,128)(2,1)S(1)} %get-tuple-element.417), channel_id=1, source_target_pairs={{0,1},{1,0},{2,3},{3,2},{4,5},{5,4},{6,7},{7,6},{8,9},{9,8},{10,11... | collective-permute-start | bytes 1769480 | tf_op jit(solution)/shard_map/cond/branch_1_fun/ppermute | solution.py:1069
  91.3 29.7 %collective-permute-start.4 = (bf16[192,1536]{1,0:T(8,128)(2,1)S(1)}, bf16[192,1536]{1,0:T(8,128)(2,1)}, u32[]{:S(2)}, u32[]{:S(2)}) collective-permute-start(bf16[192,1536]{1,0:T(8,128)(2,1)S(1)} %get-tuple-element.417), channel_id=1, source_target_pairs={{0,6},{2,4},{4,2},{6,0},{1,7},{3,5},{5,3},{7,1},{8,14},{10,12},{12... | collective-permute-start | bytes 1769480 | tf_op jit(solution)/shard_map/cond/branch_1_fun/ppermute | solution.py:1095
  92.2 28.8 %collective-permute-start.3 = (bf16[192,1536]{1,0:T(8,128)(2,1)S(1)}, bf16[192,1536]{1,0:T(8,128)(2,1)}, u32[]{:S(2)}, u32[]{:S(2)}) collective-permute-start(bf16[192,1536]{1,0:T(8,128)(2,1)S(1)} %get-tuple-element.417), channel_id=1, source_target_pairs={{0,4},{4,0},{1,5},{5,1},{2,6},{6,2},{3,7},{7,3},{8,12},{12,8},{9,1... | collective-permute-start | bytes 1769480 | tf_op jit(solution)/shard_map/cond/branch_1_fun/ppermute | solution.py:1069
  93.5 27.5 %collective-permute-start.2 = (bf16[192,1536]{1,0:T(8,128)(2,1)S(1)}, bf16[192,1536]{1,0:T(8,128)(2,1)}, u32[]{:S(2)}, u32[]{:S(2)}) collective-permute-start(bf16[192,1536]{1,0:T(8,128)(2,1)S(1)} %get-tuple-element.417), channel_id=1, source_target_pairs={{0,2},{2,0},{1,3},{3,1},{4,6},{6,4},{5,7},{7,5},{8,10},{10,8},{9,1... | collective-permute-start | bytes 1769480 | tf_op jit(solution)/shard_map/cond/branch_1_fun/ppermute | solution.py:1069
  121.1 8.8 %collective-permute-start.8 = (bf16[384,256]{1,0:T(8,128)(2,1)S(1)}, bf16[384,256]{1,0:T(8,128)(2,1)S(1)}, u32[]{:S(2)}, u32[]{:S(2)}) collective-permute-start(bf16[384,256]{1,0:T(8,128)(2,1)S(1)} %bitcast.112), channel_id=1, source_target_pairs={{0,6},{2,4},{4,2},{6,0},{1,7},{3,5},{5,3},{7,1},{8,14},{10,12},{12... | collective-permute-start | bytes 589832 | tf_op jit(solution)/shard_map/cond/branch_1_fun/ppermute | solution.py:1095
  122.0 9.6 %collective-permute-start.7 = (bf16[384,256]{1,0:T(8,128)(2,1)S(1)}, bf16[384,256]{1,0:T(8,128)(2,1)S(1)}, u32[]{:S(2)}, u32[]{:S(2)}) collective-permute-start(bf16[384,256]{1,0:T(8,128)(2,1)S(1)} %bitcast.113), channel_id=1, source_target_pairs={{0,4},{4,0},{1,5},{5,1},{2,6},{6,2},{3,7},{7,3},{8,12},{12,8},{9,1... | collective-permute-start | bytes 589832 | tf_op jit(solution)/shard_map/cond/branch_1_fun/ppermute | solution.py:1069
  123.3 9.0 %collective-permute-start.6 = (bf16[384,256]{1,0:T(8,128)(2,1)S(1)}, bf16[384,256]{1,0:T(8,128)(2,1)S(1)}, u32[]{:S(2)}, u32[]{:S(2)}) collective-permute-start(bf16[384,256]{1,0:T(8,128)(2,1)S(1)} %bitcast.114), channel_id=1, source_target_pairs={{0,2},{2,0},{1,3},{3,1},{4,6},{6,4},{5,7},{7,5},{8,10},{10,8},{9,1... | collective-permute-start | bytes 589832 | tf_op jit(solution)/shard_map/cond/branch_1_fun/ppermute | solution.py:1069
  124.6 13.1 %collective-permute-start.12 = (bf16[192,1536]{1,0:T(8,128)(2,1)}, bf16[192,1536]{1,0:T(8,128)(2,1)}, u32[]{:S(2)}, u32[]{:S(2)}) collective-permute-start(bf16[192,1536]{1,0:T(8,128)(2,1)} %get-tuple-element.450.refs_11_), channel_id=1, source_target_pairs={{0,1},{1,0},{2,3},{3,2},{4,5},{5,4},{6,7},{7,6},{8,9},{9,8},{10,11... | collective-permute-start | bytes 1769480 | tf_op jit(solution)/shard_map/cond/branch_1_fun/ppermute | solution.py:1069
  134.8 13.1 %collective-permute-start.18 = (bf16[256,1536]{1,0:T(8,128)(2,1)S(1)}, bf16[256,1536]{1,0:T(8,128)(2,1)}, u32[]{:S(2)}, u32[]{:S(2)}) collective-permute-start(bf16[256,1536]{1,0:T(8,128)(2,1)S(1)} %get-tuple-element.456), channel_id=1, source_target_pairs={{0,1},{1,0},{2,3},{3,2},{4,5},{5,4},{6,7},{7,6},{8,9},{9,8},{10,11... | collective-permute-start | bytes 2359304 | tf_op jit(solution)/shard_map/cond/branch_1_fun/ppermute | solution.py:1069
  136.3 20.7 %collective-permute-start.17 = (bf16[256,1536]{1,0:T(8,128)(2,1)}, bf16[256,1536]{1,0:T(8,128)(2,1)}, u32[]{:S(2)}, u32[]{:S(2)}) collective-permute-start(bf16[256,1536]{1,0:T(8,128)(2,1)} %after.3), channel_id=1, source_target_pairs={{0,4},{4,0},{1,5},{5,1},{2,6},{6,2},{3,7},{7,3},{8,12},{12,8},{9,1... | collective-permute-start | bytes 2359304 | tf_op jit(solution)/shard_map/cond/branch_1_fun/ppermute | solution.py:1069
  136.9 20.8 %collective-permute-start.16 = (bf16[256,1536]{1,0:T(8,128)(2,1)}, bf16[256,1536]{1,0:T(8,128)(2,1)}, u32[]{:S(2)}, u32[]{:S(2)}) collective-permute-start(bf16[256,1536]{1,0:T(8,128)(2,1)} %after.3), channel_id=1, source_target_pairs={{0,2},{2,0},{1,3},{3,1},{4,6},{6,4},{5,7},{7,5},{8,10},{10,8},{9,1... | collective-permute-start | bytes 2359304 | tf_op jit(solution)/shard_map/cond/branch_1_fun/ppermute | solution.py:1069
  146.5 11.2 %collective-permute-start.15 = (bf16[256,1536]{1,0:T(8,128)(2,1)}, bf16[256,1536]{1,0:T(8,128)(2,1)}, u32[]{:S(2)}, u32[]{:S(2)}) collective-permute-start(bf16[256,1536]{1,0:T(8,128)(2,1)} %get-tuple-element.1225), channel_id=1, source_target_pairs={{0,1},{1,0},{2,3},{3,2},{4,5},{5,4},{6,7},{7,6},{8,9},{9,8},{10,11... | collective-permute-start | bytes 2359304 | tf_op jit(solution)/shard_map/cond/branch_1_fun/ppermute | solution.py:1069
  146.6 26.3 %collective-permute-start.14 = (bf16[256,1536]{1,0:T(8,128)(2,1)}, bf16[256,1536]{1,0:T(8,128)(2,1)}, u32[]{:S(2)}, u32[]{:S(2)}) collective-permute-start(bf16[256,1536]{1,0:T(8,128)(2,1)} %get-tuple-element.1225), channel_id=1, source_target_pairs={{0,4},{4,0},{1,5},{5,1},{2,6},{6,2},{3,7},{7,3},{8,12},{12,8},{9,1... | collective-permute-start | bytes 2359304 | tf_op jit(solution)/shard_map/cond/branch_1_fun/ppermute | solution.py:1069
  147.9 25.3 %collective-permute-start.13 = (bf16[256,1536]{1,0:T(8,128)(2,1)}, bf16[256,1536]{1,0:T(8,128)(2,1)}, u32[]{:S(2)}, u32[]{:S(2)}) collective-permute-start(bf16[256,1536]{1,0:T(8,128)(2,1)} %get-tuple-element.1225), channel_id=1, source_target_pairs={{0,2},{2,0},{1,3},{3,1},{4,6},{6,4},{5,7},{7,5},{8,10},{10,8},{9,1... | collective-permute-start | bytes 2359304 | tf_op jit(solution)/shard_map/cond/branch_1_fun/ppermute | solution.py:1069
  157.0 16.3 %collective-permute-start.20 = (bf16[256,1536]{1,0:T(8,128)(2,1)}, bf16[256,1536]{1,0:T(8,128)(2,1)}, u32[]{:S(2)}, u32[]{:S(2)}) collective-permute-start(bf16[256,1536]{1,0:T(8,128)(2,1)} %collective-permute-done.17), channel_id=1, source_target_pairs={{0,1},{1,0},{2,3},{3,2},{4,5},{5,4},{6,7},{7,6},{8,9},{9,8},{10,11... | collective-permute-start | bytes 2359304 | tf_op jit(solution)/shard_map/cond/branch_1_fun/ppermute | solution.py:1069
  157.7 15.6 %collective-permute-start.19 = (bf16[256,1536]{1,0:T(8,128)(2,1)}, bf16[256,1536]{1,0:T(8,128)(2,1)}, u32[]{:S(2)}, u32[]{:S(2)}) collective-permute-start(bf16[256,1536]{1,0:T(8,128)(2,1)} %collective-permute-done.16), channel_id=1, source_target_pairs={{0,1},{1,0},{2,3},{3,2},{4,5},{5,4},{6,7},{7,6},{8,9},{9,8},{10,11... | collective-permute-start | bytes 2359304 | tf_op jit(solution)/shard_map/cond/branch_1_fun/ppermute | solution.py:1069
  173.3 18.7 %collective-permute-start.22 = (bf16[256,1536]{1,0:T(8,128)(2,1)}, bf16[256,1536]{1,0:T(8,128)(2,1)}, u32[]{:S(2)}, u32[]{:S(2)}) collective-permute-start(bf16[256,1536]{1,0:T(8,128)(2,1)} %get-tuple-element.458.refs_4_), channel_id=1, source_target_pairs={{0,4},{4,0},{1,5},{5,1},{2,6},{6,2},{3,7},{7,3},{8,12},{12,8},{9,1... | collective-permute-start | bytes 2359304 | tf_op jit(solution)/shard_map/cond/branch_1_fun/ppermute | solution.py:1069
  174.8 17.2 %collective-permute-start.23 = (bf16[256,1536]{1,0:T(8,128)(2,1)}, bf16[256,1536]{1,0:T(8,128)(2,1)}, u32[]{:S(2)}, u32[]{:S(2)}) collective-permute-start(bf16[256,1536]{1,0:T(8,128)(2,1)} %get-tuple-element.459.refs_1_), channel_id=1, source_target_pairs={{0,1},{1,0},{2,3},{3,2},{4,5},{5,4},{6,7},{7,6},{8,9},{9,8},{10,11... | collective-permute-start | bytes 2359304 | tf_op jit(solution)/shard_map/cond/branch_1_fun/ppermute | solution.py:1069
  174.8 17.2 %collective-permute-start.24 = (bf16[256,1536]{1,0:T(8,128)(2,1)}, bf16[256,1536]{1,0:T(8,128)(2,1)}, u32[]{:S(2)}, u32[]{:S(2)}) collective-permute-start(bf16[256,1536]{1,0:T(8,128)(2,1)} %get-tuple-element.457.refs_2_), channel_id=1, source_target_pairs={{0,1},{1,0},{2,3},{3,2},{4,5},{5,4},{6,7},{7,6},{8,9},{9,8},{10,11... | collective-permute-start | bytes 2359304 | tf_op jit(solution)/shard_map/cond/branch_1_fun/ppermute | solution.py:1069
  175.3 19.8 %collective-permute-start.21 = (bf16[256,1536]{1,0:T(8,128)(2,1)}, bf16[256,1536]{1,0:T(8,128)(2,1)}, u32[]{:S(2)}, u32[]{:S(2)}) collective-permute-start(bf16[256,1536]{1,0:T(8,128)(2,1)} %get-tuple-element.457.refs_2_), channel_id=1, source_target_pairs={{0,2},{2,0},{1,3},{3,1},{4,6},{6,4},{5,7},{7,5},{8,10},{10,8},{9,1... | collective-permute-start | bytes 2359304 | tf_op jit(solution)/shard_map/cond/branch_1_fun/ppermute | solution.py:1069
  198.7 34.7 %collective-permute-start.26 = (bf16[320,1536]{1,0:T(8,128)(2,1)}, bf16[320,1536]{1,0:T(8,128)(2,1)}, u32[]{:S(2)}, u32[]{:S(2)}) collective-permute-start(bf16[320,1536]{1,0:T(8,128)(2,1)} %get-tuple-element.491), channel_id=1, source_target_pairs={{0,4},{4,0},{1,5},{5,1},{2,6},{6,2},{3,7},{7,3},{8,12},{12,8},{9,1... | collective-permute-start | bytes 2949128 | tf_op jit(solution)/shard_map/cond/branch_1_fun/ppermute | solution.py:1069
  199.3 34.1 %collective-permute-start.25 = (bf16[320,1536]{1,0:T(8,128)(2,1)}, bf16[320,1536]{1,0:T(8,128)(2,1)}, u32[]{:S(2)}, u32[]{:S(2)}) collective-permute-start(bf16[320,1536]{1,0:T(8,128)(2,1)} %get-tuple-element.491), channel_id=1, source_target_pairs={{0,2},{2,0},{1,3},{3,1},{4,6},{6,4},{5,7},{7,5},{8,10},{10,8},{9,1... | collective-permute-start | bytes 2949128 | tf_op jit(solution)/shard_map/cond/branch_1_fun/ppermute | solution.py:1069
  233.4 160.3 %reduce-scatter.6.cloned.1.call-start = ((), (), s32[]{:S(2)}) async-start(), calls=%async_computation.10 | async-start | bytes 4423680 | tf_op jit(solution)/shard_map/reduce_scatter | solution.py:1132
  236.8 20.1 %collective-permute-start.27 = (bf16[160,1536]{1,0:T(8,128)(2,1)S(1)}, bf16[160,1536]{1,0:T(8,128)(2,1)}, u32[]{:S(2)}, u32[]{:S(2)}) collective-permute-start(bf16[160,1536]{1,0:T(8,128)(2,1)S(1)} %get-tuple-element.492), channel_id=1, source_target_pairs={{0,4},{4,0},{1,5},{5,1},{2,6},{6,2},{3,7},{7,3},{8,12},{12,8},{9,1... | collective-permute-start | bytes 1474568 | tf_op jit(solution)/shard_map/cond/branch_1_fun/ppermute | solution.py:1069
  238.3 18.6 %collective-permute-start.28 = (bf16[160,1536]{1,0:T(8,128)(2,1)S(1)}, bf16[160,1536]{1,0:T(8,128)(2,1)}, u32[]{:S(2)}, u32[]{:S(2)}) collective-permute-start(bf16[160,1536]{1,0:T(8,128)(2,1)S(1)} %get-tuple-element.493), channel_id=1, source_target_pairs={{0,2},{2,0},{1,3},{3,1},{4,6},{6,4},{5,7},{7,5},{8,10},{10,8},{9,1... | collective-permute-start | bytes 1474568 | tf_op jit(solution)/shard_map/cond/branch_1_fun/ppermute | solution.py:1069
  256.9 8.6 %collective-permute-start.63 = (bf16[1024,1536]{1,0:T(8,128)(2,1)S(1)}, bf16[1024,1536]{1,0:T(8,128)(2,1)S(1)}, u32[]{:S(2)}, u32[]{:S(2)}) collective-permute-start(bf16[1024,1536]{1,0:T(8,128)(2,1)S(1)} %get-tuple-element.855.refs_6_), channel_id=1, source_target_pairs={{0,1},{1,0},{2,3},{3,2},{4,5},{5,4},{6,7},{7,6},{8,9},{9,8},{10,11... | collective-permute-start | bytes 9437192 | tf_op jit(solution)/shard_map/ppermute | solution.py:1069
  269.4 34.6 %collective-permute-start.29 = (bf16[256,1536]{1,0:T(8,128)(2,1)}, bf16[256,1536]{1,0:T(8,128)(2,1)}, u32[]{:S(2)}, u32[]{:S(2)}) collective-permute-start(bf16[256,1536]{1,0:T(8,128)(2,1)} %get-tuple-element.511), channel_id=1, source_target_pairs={{0,2},{2,0},{1,3},{3,1},{4,6},{6,4},{5,7},{7,5},{8,10},{10,8},{9,1... | collective-permute-start | bytes 2359304 | tf_op jit(solution)/shard_map/cond/branch_1_fun/ppermute | solution.py:1069
  269.4 34.6 %collective-permute-start.30 = (bf16[256,1536]{1,0:T(8,128)(2,1)}, bf16[256,1536]{1,0:T(8,128)(2,1)}, u32[]{:S(2)}, u32[]{:S(2)}) collective-permute-start(bf16[256,1536]{1,0:T(8,128)(2,1)} %get-tuple-element.512), channel_id=1, source_target_pairs={{0,4},{4,0},{1,5},{5,1},{2,6},{6,2},{3,7},{7,3},{8,12},{12,8},{9,1... | collective-permute-start | bytes 2359304 | tf_op jit(solution)/shard_map/cond/branch_1_fun/ppermute | solution.py:1069
  269.6 37.5 %collective-permute-start.31 = (bf16[256,1536]{1,0:T(8,128)(2,1)}, bf16[256,1536]{1,0:T(8,128)(2,1)}, u32[]{:S(2)}, u32[]{:S(2)}) collective-permute-start(bf16[256,1536]{1,0:T(8,128)(2,1)} %get-tuple-element.513), channel_id=1, source_target_pairs={{0,6},{2,4},{4,2},{6,0},{1,7},{3,5},{5,3},{7,1},{8,14},{10,12},{12... | collective-permute-start | bytes 2359304 | tf_op jit(solution)/shard_map/cond/branch_1_fun/ppermute | solution.py:1095
  307.2 134.4 %reduce-scatter.8.cloned.1.call-start = ((), (), s32[]{:S(2)}) async-start(), calls=%async_computation.11 | async-start | bytes 2457600 | tf_op jit(solution)/shard_map/reduce_scatter | solution.py:1132
  307.7 64.3 %collective-permute-start.69 = (bf16[1024,1536]{1,0:T(8,128)(2,1)}, bf16[1024,1536]{1,0:T(8,128)(2,1)}, u32[]{:S(2)}, u32[]{:S(2)}) collective-permute-start(bf16[1024,1536]{1,0:T(8,128)(2,1)} %get-tuple-element.904), channel_id=1, source_target_pairs={{0,1},{1,0},{2,3},{3,2},{4,5},{5,4},{6,7},{7,6},{8,9},{9,8},{10,11... | collective-permute-start | bytes 9437192 | tf_op jit(solution)/shard_map/ppermute | solution.py:1069
  316.1 7.7 %collective-permute-start.65 = (bf16[384,256]{1,0:T(8,128)(2,1)S(1)}, bf16[384,256]{1,0:T(8,128)(2,1)S(1)}, u32[]{:S(2)}, u32[]{:S(2)}) collective-permute-start(bf16[384,256]{1,0:T(8,128)(2,1)S(1)} %bitcast.80), channel_id=1, source_target_pairs={{0,4},{4,0},{1,5},{5,1},{2,6},{6,2},{3,7},{7,3},{8,12},{12,8},{9,1... | collective-permute-start | bytes 589832 | tf_op jit(solution)/shard_map/ppermute | solution.py:1069
  316.4 11.1 %collective-permute-start.64 = (bf16[384,256]{1,0:T(8,128)(2,1)S(1)}, bf16[384,256]{1,0:T(8,128)(2,1)S(1)}, u32[]{:S(2)}, u32[]{:S(2)}) collective-permute-start(bf16[384,256]{1,0:T(8,128)(2,1)S(1)} %bitcast.79), channel_id=1, source_target_pairs={{0,2},{2,0},{1,3},{3,1},{4,6},{6,4},{5,7},{7,5},{8,10},{10,8},{9,1... | collective-permute-start | bytes 589832 | tf_op jit(solution)/shard_map/ppermute | solution.py:1069
  316.7 10.8 %collective-permute-start.66 = (bf16[384,256]{1,0:T(8,128)(2,1)S(1)}, bf16[384,256]{1,0:T(8,128)(2,1)S(1)}, u32[]{:S(2)}, u32[]{:S(2)}) collective-permute-start(bf16[384,256]{1,0:T(8,128)(2,1)S(1)} %bitcast.78), channel_id=1, source_target_pairs={{0,6},{2,4},{4,2},{6,0},{1,7},{3,5},{5,3},{7,1},{8,14},{10,12},{12... | collective-permute-start | bytes 589832 | tf_op jit(solution)/shard_map/ppermute | solution.py:1095
  330.2 20.0 %collective-permute-start.51 = (bf16[256,1536]{1,0:T(8,128)(2,1)}, bf16[256,1536]{1,0:T(8,128)(2,1)}, u32[]{:S(2)}, u32[]{:S(2)}) collective-permute-start(bf16[256,1536]{1,0:T(8,128)(2,1)} %get-tuple-element.546), channel_id=1, source_target_pairs={{0,4},{4,0},{1,5},{5,1},{2,6},{6,2},{3,7},{7,3},{8,12},{12,8},{9,1... | collective-permute-start | bytes 2359304 | tf_op jit(solution)/shard_map/cond/branch_1_fun/ppermute | solution.py:1069
  331.9 19.6 %collective-permute-start.50 = (bf16[256,1536]{1,0:T(8,128)(2,1)}, bf16[256,1536]{1,0:T(8,128)(2,1)}, u32[]{:S(2)}, u32[]{:S(2)}) collective-permute-start(bf16[256,1536]{1,0:T(8,128)(2,1)} %get-tuple-element.546), channel_id=1, source_target_pairs={{0,2},{2,0},{1,3},{3,1},{4,6},{6,4},{5,7},{7,5},{8,10},{10,8},{9,1... | collective-permute-start | bytes 2359304 | tf_op jit(solution)/shard_map/cond/branch_1_fun/ppermute | solution.py:1069
  332.3 19.3 %collective-permute-start.52 = (bf16[256,1536]{1,0:T(8,128)(2,1)}, bf16[256,1536]{1,0:T(8,128)(2,1)}, u32[]{:S(2)}, u32[]{:S(2)}) collective-permute-start(bf16[256,1536]{1,0:T(8,128)(2,1)} %get-tuple-element.546), channel_id=1, source_target_pairs={{0,1},{1,0},{2,3},{3,2},{4,5},{5,4},{6,7},{7,6},{8,9},{9,8},{10,11... | collective-permute-start | bytes 2359304 | tf_op jit(solution)/shard_map/cond/branch_1_fun/ppermute | solution.py:1069
  351.6 17.7 %collective-permute-start.34 = (bf16[256,1536]{1,0:T(8,128)(2,1)}, bf16[256,1536]{1,0:T(8,128)(2,1)}, u32[]{:S(2)}, u32[]{:S(2)}) collective-permute-start(bf16[256,1536]{1,0:T(8,128)(2,1)} %get-tuple-element.566), channel_id=1, source_target_pairs={{0,1},{1,0},{2,3},{3,2},{4,5},{5,4},{6,7},{7,6},{8,9},{9,8},{10,11... | collective-permute-start | bytes 2359304 | tf_op jit(solution)/shard_map/cond/branch_1_fun/ppermute | solution.py:1069
  351.7 20.3 %collective-permute-start.32 = (bf16[256,1536]{1,0:T(8,128)(2,1)}, bf16[256,1536]{1,0:T(8,128)(2,1)}, u32[]{:S(2)}, u32[]{:S(2)}) collective-permute-start(bf16[256,1536]{1,0:T(8,128)(2,1)} %get-tuple-element.564), channel_id=1, source_target_pairs={{0,2},{2,0},{1,3},{3,1},{4,6},{6,4},{5,7},{7,5},{8,10},{10,8},{9,1... | collective-permute-start | bytes 2359304 | tf_op jit(solution)/shard_map/cond/branch_1_fun/ppermute | solution.py:1069
  352.1 19.9 %collective-permute-start.35 = (bf16[256,1536]{1,0:T(8,128)(2,1)}, bf16[256,1536]{1,0:T(8,128)(2,1)}, u32[]{:S(2)}, u32[]{:S(2)}) collective-permute-start(bf16[256,1536]{1,0:T(8,128)(2,1)} %get-tuple-element.564), channel_id=1, source_target_pairs={{0,1},{1,0},{2,3},{3,2},{4,5},{5,4},{6,7},{7,6},{8,9},{9,8},{10,11... | collective-permute-start | bytes 2359304 | tf_op jit(solution)/shard_map/cond/branch_1_fun/ppermute | solution.py:1069
  352.3 17.1 %collective-permute-start.33 = (bf16[192,1536]{1,0:T(8,128)(2,1)}, bf16[192,1536]{1,0:T(8,128)(2,1)}, u32[]{:S(2)}, u32[]{:S(2)}) collective-permute-start(bf16[192,1536]{1,0:T(8,128)(2,1)} %get-tuple-element.565), channel_id=1, source_target_pairs={{0,4},{4,0},{1,5},{5,1},{2,6},{6,2},{3,7},{7,3},{8,12},{12,8},{9,1... | collective-permute-start | bytes 1769480 | tf_op jit(solution)/shard_map/cond/branch_1_fun/ppermute | solution.py:1069
  374.5 19.2 %collective-permute-start.38 = (bf16[640,256]{1,0:T(8,128)(2,1)}, bf16[640,256]{1,0:T(8,128)(2,1)}, u32[]{:S(2)}, u32[]{:S(2)}) collective-permute-start(bf16[640,256]{1,0:T(8,128)(2,1)} %get-tuple-element.585), channel_id=1, source_target_pairs={{0,6},{2,4},{4,2},{6,0},{1,7},{3,5},{5,3},{7,1},{8,14},{10,12},{12... | collective-permute-start | bytes 983048 | tf_op jit(solution)/shard_map/cond/branch_1_fun/ppermute | solution.py:1095
  375.6 18.1 %collective-permute-start.37 = (bf16[640,256]{1,0:T(8,128)(2,1)}, bf16[640,256]{1,0:T(8,128)(2,1)}, u32[]{:S(2)}, u32[]{:S(2)}) collective-permute-start(bf16[640,256]{1,0:T(8,128)(2,1)} %get-tuple-element.584), channel_id=1, source_target_pairs={{0,4},{4,0},{1,5},{5,1},{2,6},{6,2},{3,7},{7,3},{8,12},{12,8},{9,1... | collective-permute-start | bytes 983048 | tf_op jit(solution)/shard_map/cond/branch_1_fun/ppermute | solution.py:1069
  376.3 17.4 %collective-permute-start.36 = (bf16[640,256]{1,0:T(8,128)(2,1)}, bf16[640,256]{1,0:T(8,128)(2,1)}, u32[]{:S(2)}, u32[]{:S(2)}) collective-permute-start(bf16[640,256]{1,0:T(8,128)(2,1)} %get-tuple-element.583), channel_id=1, source_target_pairs={{0,2},{2,0},{1,3},{3,1},{4,6},{6,4},{5,7},{7,5},{8,10},{10,8},{9,1... | collective-permute-start | bytes 983048 | tf_op jit(solution)/shard_map/cond/branch_1_fun/ppermute | solution.py:1069
  395.6 19.9 %collective-permute-start.56 = (bf16[192,1152]{1,0:T(8,128)(2,1)S(1)}, bf16[192,1152]{1,0:T(8,128)(2,1)}, u32[]{:S(2)}, u32[]{:S(2)}) collective-permute-start(bf16[192,1152]{1,0:T(8,128)(2,1)S(1)} %constant_dynamic-slice_fusion.1), channel_id=1, source_target_pairs={{0,4},{4,0},{1,5},{5,1},{2,6},{6,2},{3,7},{7,3},{8,12},{12,8},{9,1... | collective-permute-start | bytes 1327112 | tf_op jit(solution)/shard_map/cond/branch_1_fun/ppermute | solution.py:1069
  398.0 17.5 %collective-permute-start.57 = (bf16[1280,256]{1,0:T(8,128)(2,1)}, bf16[1280,256]{1,0:T(8,128)(2,1)}, u32[]{:S(2)}, u32[]{:S(2)}) collective-permute-start(bf16[1280,256]{1,0:T(8,128)(2,1)} %far_parts.4), channel_id=1, source_target_pairs={{0,1},{1,0},{2,3},{3,2},{4,5},{5,4},{6,7},{7,6},{8,9},{9,8},{10,11... | collective-permute-start | bytes 1966088 | tf_op jit(solution)/shard_map/cond/branch_1_fun/ppermute | solution.py:1069
  398.8 11.8 %collective-permute-start.55 = (bf16[128,1536]{1,0:T(8,128)(2,1)}, bf16[128,1536]{1,0:T(8,128)(2,1)}, u32[]{:S(2)}, u32[]{:S(2)}) collective-permute-start(bf16[128,1536]{1,0:T(8,128)(2,1)} %get-tuple-element.1147), channel_id=1, source_target_pairs={{0,2},{2,0},{1,3},{3,1},{4,6},{6,4},{5,7},{7,5},{8,10},{10,8},{9,1... | collective-permute-start | bytes 1179656 | tf_op jit(solution)/shard_map/cond/branch_1_fun/ppermute | solution.py:1069
  400.2 15.3 %collective-permute-start.54 = (bf16[128,1536]{1,0:T(8,128)(2,1)S(1)}, bf16[128,1536]{1,0:T(8,128)(2,1)}, u32[]{:S(2)}, u32[]{:S(2)}) collective-permute-start(bf16[128,1536]{1,0:T(8,128)(2,1)S(1)} %get-tuple-element.1148), channel_id=1, source_target_pairs={{0,4},{4,0},{1,5},{5,1},{2,6},{6,2},{3,7},{7,3},{8,12},{12,8},{9,1... | collective-permute-start | bytes 1179656 | tf_op jit(solution)/shard_map/cond/branch_1_fun/ppermute | solution.py:1069
  419.9 19.8 %collective-permute-start.39 = (bf16[256,1536]{1,0:T(8,128)(2,1)}, bf16[256,1536]{1,0:T(8,128)(2,1)}, u32[]{:S(2)}, u32[]{:S(2)}) collective-permute-start(bf16[256,1536]{1,0:T(8,128)(2,1)} %get-tuple-element.621), channel_id=1, source_target_pairs={{0,2},{2,0},{1,3},{3,1},{4,6},{6,4},{5,7},{7,5},{8,10},{10,8},{9,1... | collective-permute-start | bytes 2359304 | tf_op jit(solution)/shard_map/cond/branch_1_fun/ppermute | solution.py:1069
  421.7 19.9 %collective-permute-start.40 = (bf16[256,1536]{1,0:T(8,128)(2,1)}, bf16[256,1536]{1,0:T(8,128)(2,1)}, u32[]{:S(2)}, u32[]{:S(2)}) collective-permute-start(bf16[256,1536]{1,0:T(8,128)(2,1)} %get-tuple-element.622), channel_id=1, source_target_pairs={{0,4},{4,0},{1,5},{5,1},{2,6},{6,2},{3,7},{7,3},{8,12},{12,8},{9,1... | collective-permute-start | bytes 2359304 | tf_op jit(solution)/shard_map/cond/branch_1_fun/ppermute | solution.py:1069
  442.6 7.3 %collective-permute-start.53 = (bf16[192,640]{1,0:T(8,128)(2,1)S(1)}, bf16[192,640]{1,0:T(8,128)(2,1)}, u32[]{:S(2)}, u32[]{:S(2)}) collective-permute-start(bf16[192,640]{1,0:T(8,128)(2,1)S(1)} %constant_dynamic-slice_fusion.2), channel_id=1, source_target_pairs={{0,4},{4,0},{1,5},{5,1},{2,6},{6,2},{3,7},{7,3},{8,12},{12,8},{9,1... | collective-permute-start | bytes 737288 | tf_op jit(solution)/shard_map/cond/branch_1_fun/ppermute | solution.py:1069
  (61 other events, 532.4 us)
Sparse Core Ops, SparseCore 0:
  33.0 43.8 all-gather.3
  78.5 88.2 all-gather.7
  168.3 68.4 all-gather.5
  239.0 83.8 reduce-scatter.3
  325.0 66.8 reduce-scatter.5
  395.2 40.6 reduce-scatter.7
